TPU v7x, 32 devices: a whole 2x2x4 slice. The times are simulated.
32 devices in a mesh: depth: 4 (over z), row: 2 (over core), col: 4 (over y, x).
Axes of the slice: x: 2, y: 2, z: 4, core: 2. Of those that a mesh axis runs over, the one named last changes fastest.
Arguments:
- phase: float32 [4, 128, 512], P('depth', 'row', 'col'), may hold values from -1.8 to 1.8
- tilt: int32 [2, 2], replicated, may hold values from -6 to 6
- intensity: float32 [2, 128, 512], P(None, 'row', 'col'), may hold values from 0.3 to 1.5
Outputs:
- grad_phase: float32 [4, 128, 512], P('depth', 'row', 'col')
- exit_waves: float32 [2, 4, 2, 128, 512], P(None, 'depth', None, 'row', 'col')
Inputs may be any that keep to these rules, and one draw needn't show every extreme that they name: `tilt`: whole numbers of phase cycles across the field.
All inputs are finite; a program needn't handle non-finite values.
Results may differ from a plain program's by a relative error of at most 0.0003.
Values sent between devices are 32-bit elements; how exact they have to be, the bound alone decides.
No kernel may reach another device: no remote copies, remote signals or barrier semaphores. Data moves between devices by JAX's collectives and lax.ppermute only.
A program may use at most 64 MiB of HBM per device.

v0:
```python
import math

import jax
import jax.numpy as jnp
from jax import lax
from jax.sharding import PartitionSpec as P

HALO = 32
FRESNEL = 64


def extended_2(cells, sides, width):
    for axis, dim in sides:
        count = lax.axis_size(axis)
        ends = count - 1
        head = lax.slice_in_dim(cells, 0, width, axis=dim)
        tail = lax.slice_in_dim(cells, cells.shape[dim] - width, cells.shape[dim], axis=dim)
        cells = jnp.concatenate(
            [
                lax.ppermute(tail, axis, [(i, (i + 1) % count) for i in range(ends)]),
                cells,
                lax.ppermute(head, axis, [((i + 1) % count, i) for i in range(ends)]),
            ],
            axis=dim,
        )
    return cells


def from_behind(value, axis, steps):
    count = lax.axis_size(axis)
    leading, last = (max(0, -steps), min(count, count - steps))
    return lax.ppermute(value, axis, [(source, source + steps) for source in range(leading, last)])


def band_matrix(block_size, margin, fresnel, adjoint):
    shape_full = (block_size, block_size + 2 * margin)
    out_idx = lax.broadcasted_iota(jnp.int32, shape_full, 0)
    in_idx = lax.broadcasted_iota(jnp.int32, shape_full, 1)
    offset = (out_idx + margin - in_idx).astype(jnp.float32)
    inside = jnp.abs(offset) <= margin
    taper_dist = jnp.maximum(jnp.abs(offset) - 0.5 * margin, 0.0)
    profile = jnp.cos(jnp.pi * taper_dist / (margin + 2.0))
    weight = profile * profile / math.sqrt(fresnel)
    phase_angle = jnp.pi * offset * offset / fresnel
    real_part = jnp.where(inside, jnp.cos(phase_angle) * weight, 0.0)
    imag_part = jnp.where(inside, jnp.sin(phase_angle) * weight, 0.0)
    if adjoint:
        imag_part = -imag_part
    upper = jnp.stack([real_part, -imag_part])
    lower = jnp.stack([imag_part, real_part])
    return jnp.stack([upper, lower])


def along_rows(extended, matrix):
    pieces = [jnp.einsum("pqij,gqjc->gpic", matrix, extended, precision=lax.Precision.HIGHEST)]
    return jnp.concatenate(pieces, axis=2)


def along_cols(extended, matrix, margin):
    block_size = matrix.shape[2]
    extent = extended.shape[3] - 2 * margin
    pieces = []
    for block_start in range(0, extent, block_size):
        window = extended[:, :, :, block_start : block_start + block_size + 2 * margin]
        pieces.append(
            jnp.einsum("pqij,gqrj->gpri", matrix, window, precision=lax.Precision.HIGHEST)
        )
    return jnp.concatenate(pieces, axis=3)


def propagate(current, row_matrix, col_matrix):
    with_rows = extended_2(current, (("row", 2),), HALO)
    row_done = along_rows(with_rows, row_matrix)
    with_cols = extended_2(row_done, (("col", 3),), HALO)
    return along_cols(with_cols, col_matrix, HALO)


def transmit(screen, current, adjoint):
    screen_re = screen[0][None]
    screen_im = screen[1][None]
    if adjoint:
        screen_im = -screen_im
    real_part = screen_re * current[:, 0] - screen_im * current[:, 1]
    imag_part = screen_re * current[:, 1] + screen_im * current[:, 0]
    return jnp.stack([real_part, imag_part], axis=1)


def store_item(store, current, first_item, slice_index, active):
    begin = (first_item, jnp.int32(slice_index), jnp.int32(0), jnp.int32(0), jnp.int32(0))
    sizes_now = (current.shape[0], 1) + current.shape[1:]
    previous = lax.dynamic_slice(store, begin, sizes_now)
    fresh = jnp.where(active, current[:, None], previous)
    return lax.dynamic_update_slice(store, fresh, begin)


def body(phase, tilt, intensity):
    slices, tile_r, tile_c = phase.shape
    batch_size = tilt.shape[0]
    sections = lax.axis_size("depth")
    section_index = lax.axis_index("depth")
    group_size = 1
    groups = batch_size // group_size
    tick_count = sections + groups - 1
    block_r = 64
    block_c = 128
    fwd_rows = band_matrix(block_r, HALO, FRESNEL, False)
    fwd_cols = band_matrix(block_c, HALO, FRESNEL, False)
    adj_rows = band_matrix(block_r, HALO, FRESNEL, True)
    adj_cols = band_matrix(block_c, HALO, FRESNEL, True)
    row_pos = (
        lax.axis_index("row") * tile_r + lax.broadcasted_iota(jnp.int32, (tile_r, tile_c), 0)
    ).astype(jnp.float32)
    col_pos = (
        lax.axis_index("col") * tile_c + lax.broadcasted_iota(jnp.int32, (tile_r, tile_c), 1)
    ).astype(jnp.float32)
    height = float(tile_r * lax.axis_size("row"))
    width_all = float(tile_c * lax.axis_size("col"))
    tilt_f = tilt.astype(jnp.float32)
    phase_angle = (
        2.0
        * jnp.pi
        * (
            tilt_f[:, 0, None, None] * row_pos / height
            + tilt_f[:, 1, None, None] * col_pos / width_all
        )
    )
    incident = jnp.stack([jnp.cos(phase_angle), jnp.sin(phase_angle)], axis=1)
    screens = jnp.stack([jnp.cos(phase), jnp.sin(phase)], axis=1)

    def forward_tick(tick_now, carry):
        incoming, entering, leaving = carry
        group_index = tick_now - section_index
        active = (group_index >= 0) & (group_index < groups)
        first_item = jnp.clip(group_index, 0, groups - 1) * group_size
        current = jnp.where(
            section_index == 0,
            lax.dynamic_slice_in_dim(incident, first_item, group_size, 0),
            incoming,
        )
        entering = store_item(entering, current, first_item, 0, active)
        current = propagate(transmit(screens[0], current, False), fwd_rows, fwd_cols)
        leaving = store_item(leaving, current, first_item, 0, active)
        incoming = from_behind(current, "depth", 1)
        return (incoming, entering, leaving)

    store_zero = jnp.zeros((batch_size, slices, 2, tile_r, tile_c), jnp.float32)
    start_wave = jnp.zeros((group_size, 2, tile_r, tile_c), jnp.float32)
    _, entering, leaving = lax.fori_loop(
        0, tick_count, forward_tick, (start_wave, store_zero, store_zero)
    )
    final_wave = leaving[:, slices - 1]
    misfit = final_wave[:, 0] * final_wave[:, 0] + final_wave[:, 1] * final_wave[:, 1] - intensity
    seed_adjoint = 2.0 * misfit[:, None] * final_wave

    def backward_tick(tick_now, carry):
        incoming, gradient = carry
        group_index = tick_now - (sections - 1 - section_index)
        active = (group_index >= 0) & (group_index < groups)
        first_item = jnp.clip(group_index, 0, groups - 1) * group_size
        adjoint_wave = jnp.where(
            section_index == sections - 1,
            lax.dynamic_slice_in_dim(seed_adjoint, first_item, group_size, 0),
            incoming,
        )
        for slice_index in reversed(range(slices)):
            pulled = propagate(adjoint_wave, adj_rows, adj_cols)
            arrived = lax.dynamic_slice_in_dim(entering[:, slice_index], first_item, group_size, 0)
            moved = transmit(screens[slice_index], arrived, False)
            contribution = jnp.sum(pulled[:, 1] * moved[:, 0] - pulled[:, 0] * moved[:, 1], axis=0)
            gradient = gradient.at[slice_index].add(jnp.where(active, contribution, 0.0))
            adjoint_wave = transmit(screens[slice_index], pulled, True)
        incoming = from_behind(adjoint_wave, "depth", -1)
        return (incoming, gradient)

    grad_zero = jnp.zeros((slices, tile_r, tile_c), jnp.float32)
    _, gradient = lax.fori_loop(0, tick_count, backward_tick, (start_wave, grad_zero))
    return (gradient, leaving)


def solution(mesh):
    placed = (P("depth", "row", "col"), P(), P(None, "row", "col"))
    return jax.shard_map(
        body,
        mesh=mesh,
        in_specs=placed,
        out_specs=(P("depth", "row", "col"), P(None, "depth", None, "row", "col")),
        check_vma=False,
    )
```

profile of v0, /device:TPU:0, one launch (start us, length us, event | category | flops | bytes accessed | tf_op | source)
XLA Modules:
  0.0 216.9 jit_solution(5021720865077658081)
XLA Ops:
  4.1 104.6 %while.38 = (s32[]{:T(128)}, f32[1,2,64,128]{3,2,1,0:T(8,128)S(1)}, f32[2,1,2,64,128]{4,3,2,1,0:T(8,128)S(1)}, f32[2,1,2,64,128]{4,3,2,1,0:T(8,128)S(1)}, f32[1,...) while((s32[]{:T(128)}, f32[1,2,64,128]{3,2,1,0:T(8,128)S(1)}, ...), condition=%wide.region_1.2_spmd, body=%wide.region_0.1_spmd.sunk | while | flops 126091272 | bytes 2490761 | solution.py:148
  4.2 1.3 collective-permute-start
  5.5 3.0 %collective-permute-start.1 = (f32[1,2,32,128]{3,2,1,0:T(8,128)S(1)}, f32[1,2,32,128]{3,2,1,0:T(8,128)S(1)}, u32[]{:S(2)}, u32[]{:S(2)}) collective-permute-start(f32[1,2,32,128]{3,2,1,0:T(8,128)S(1)} %get-tuple-element.749), channel_id=1, source_target_pairs={{0,4},{1,5},{2,6},{3,7},{8,12},{9,13},{10,14},{11,15},{16,20},{17,... | collective-permute-start | bytes 98312 | tf_op jit(solution)/shard_map/while/body/eval_jaxpr/ppermute | solution.py:20
  9.7 1.3 collective-permute-start.2
  11.0 5.5 %collective-permute-start.3 = (f32[1,2,64,32]{3,2,1,0:T(8,128)S(1)}, f32[1,2,64,32]{3,2,1,0:T(8,128)S(1)}, u32[]{:S(2)}, u32[]{:S(2)}) collective-permute-start(f32[1,2,64,32]{3,2,1,0:T(8,128)S(1)} %get-tuple-element.751), channel_id=1, source_target_pairs={{0,1},{1,2},{2,3},{4,5},{5,6},{6,7},{8,9},{9,10},{10,11},{12,13},{... | collective-permute-start | bytes 49160 | tf_op jit(solution)/shard_map/while/body/eval_jaxpr/ppermute | solution.py:20
  18.8 4.0 %collective-permute-start.4 = (f32[1,2,64,128]{3,2,1,0:T(8,128)S(1)}, f32[1,2,64,128]{3,2,1,0:T(8,128)S(1)}, u32[]{:S(2)}, u32[]{:S(2)}) collective-permute-start(f32[1,2,64,128]{3,2,1,0:T(8,128)S(1)} %bitcast.121), channel_id=1, source_target_pairs={{0,8},{8,16},{16,24},{1,9},{9,17},{17,25},{2,10},{10,18},{18,26},{... | collective-permute-start | bytes 196616 | tf_op jit(solution)/shard_map/while/body/eval_jaxpr/ppermute | solution.py:32
  22.8 1.9 collective-permute-done.4
  24.7 1.3 collective-permute-start
  26.0 3.0 %collective-permute-start.1 = (f32[1,2,32,128]{3,2,1,0:T(8,128)S(1)}, f32[1,2,32,128]{3,2,1,0:T(8,128)S(1)}, u32[]{:S(2)}, u32[]{:S(2)}) collective-permute-start(f32[1,2,32,128]{3,2,1,0:T(8,128)S(1)} %get-tuple-element.749), channel_id=1, source_target_pairs={{0,4},{1,5},{2,6},{3,7},{8,12},{9,13},{10,14},{11,15},{16,20},{17,... | collective-permute-start | bytes 98312 | tf_op jit(solution)/shard_map/while/body/eval_jaxpr/ppermute | solution.py:20
  30.3 1.3 collective-permute-start.2
  31.6 4.9 %collective-permute-start.3 = (f32[1,2,64,32]{3,2,1,0:T(8,128)S(1)}, f32[1,2,64,32]{3,2,1,0:T(8,128)S(1)}, u32[]{:S(2)}, u32[]{:S(2)}) collective-permute-start(f32[1,2,64,32]{3,2,1,0:T(8,128)S(1)} %get-tuple-element.751), channel_id=1, source_target_pairs={{0,1},{1,2},{2,3},{4,5},{5,6},{6,7},{8,9},{9,10},{10,11},{12,13},{... | collective-permute-start | bytes 49160 | tf_op jit(solution)/shard_map/while/body/eval_jaxpr/ppermute | solution.py:20
  38.8 4.3 %collective-permute-start.4 = (f32[1,2,64,128]{3,2,1,0:T(8,128)S(1)}, f32[1,2,64,128]{3,2,1,0:T(8,128)S(1)}, u32[]{:S(2)}, u32[]{:S(2)}) collective-permute-start(f32[1,2,64,128]{3,2,1,0:T(8,128)S(1)} %bitcast.121), channel_id=1, source_target_pairs={{0,8},{8,16},{16,24},{1,9},{9,17},{17,25},{2,10},{10,18},{18,26},{... | collective-permute-start | bytes 196616 | tf_op jit(solution)/shard_map/while/body/eval_jaxpr/ppermute | solution.py:32
  43.1 1.9 collective-permute-done.4
  45.1 1.3 collective-permute-start
  46.4 3.0 %collective-permute-start.1 = (f32[1,2,32,128]{3,2,1,0:T(8,128)S(1)}, f32[1,2,32,128]{3,2,1,0:T(8,128)S(1)}, u32[]{:S(2)}, u32[]{:S(2)}) collective-permute-start(f32[1,2,32,128]{3,2,1,0:T(8,128)S(1)} %get-tuple-element.749), channel_id=1, source_target_pairs={{0,4},{1,5},{2,6},{3,7},{8,12},{9,13},{10,14},{11,15},{16,20},{17,... | collective-permute-start | bytes 98312 | tf_op jit(solution)/shard_map/while/body/eval_jaxpr/ppermute | solution.py:20
  50.6 1.3 collective-permute-start.2
  51.9 5.8 %collective-permute-start.3 = (f32[1,2,64,32]{3,2,1,0:T(8,128)S(1)}, f32[1,2,64,32]{3,2,1,0:T(8,128)S(1)}, u32[]{:S(2)}, u32[]{:S(2)}) collective-permute-start(f32[1,2,64,32]{3,2,1,0:T(8,128)S(1)} %get-tuple-element.751), channel_id=1, source_target_pairs={{0,1},{1,2},{2,3},{4,5},{5,6},{6,7},{8,9},{9,10},{10,11},{12,13},{... | collective-permute-start | bytes 49160 | tf_op jit(solution)/shard_map/while/body/eval_jaxpr/ppermute | solution.py:20
  60.0 4.3 %collective-permute-start.4 = (f32[1,2,64,128]{3,2,1,0:T(8,128)S(1)}, f32[1,2,64,128]{3,2,1,0:T(8,128)S(1)}, u32[]{:S(2)}, u32[]{:S(2)}) collective-permute-start(f32[1,2,64,128]{3,2,1,0:T(8,128)S(1)} %bitcast.121), channel_id=1, source_target_pairs={{0,8},{8,16},{16,24},{1,9},{9,17},{17,25},{2,10},{10,18},{18,26},{... | collective-permute-start | bytes 196616 | tf_op jit(solution)/shard_map/while/body/eval_jaxpr/ppermute | solution.py:32
  64.3 1.9 collective-permute-done.4
  66.2 1.3 collective-permute-start
  67.5 3.0 %collective-permute-start.1 = (f32[1,2,32,128]{3,2,1,0:T(8,128)S(1)}, f32[1,2,32,128]{3,2,1,0:T(8,128)S(1)}, u32[]{:S(2)}, u32[]{:S(2)}) collective-permute-start(f32[1,2,32,128]{3,2,1,0:T(8,128)S(1)} %get-tuple-element.749), channel_id=1, source_target_pairs={{0,4},{1,5},{2,6},{3,7},{8,12},{9,13},{10,14},{11,15},{16,20},{17,... | collective-permute-start | bytes 98312 | tf_op jit(solution)/shard_map/while/body/eval_jaxpr/ppermute | solution.py:20
  71.8 1.3 collective-permute-start.2
  73.1 5.9 %collective-permute-start.3 = (f32[1,2,64,32]{3,2,1,0:T(8,128)S(1)}, f32[1,2,64,32]{3,2,1,0:T(8,128)S(1)}, u32[]{:S(2)}, u32[]{:S(2)}) collective-permute-start(f32[1,2,64,32]{3,2,1,0:T(8,128)S(1)} %get-tuple-element.751), channel_id=1, source_target_pairs={{0,1},{1,2},{2,3},{4,5},{5,6},{6,7},{8,9},{9,10},{10,11},{12,13},{... | collective-permute-start | bytes 49160 | tf_op jit(solution)/shard_map/while/body/eval_jaxpr/ppermute | solution.py:20
  81.3 4.3 %collective-permute-start.4 = (f32[1,2,64,128]{3,2,1,0:T(8,128)S(1)}, f32[1,2,64,128]{3,2,1,0:T(8,128)S(1)}, u32[]{:S(2)}, u32[]{:S(2)}) collective-permute-start(f32[1,2,64,128]{3,2,1,0:T(8,128)S(1)} %bitcast.121), channel_id=1, source_target_pairs={{0,8},{8,16},{16,24},{1,9},{9,17},{17,25},{2,10},{10,18},{18,26},{... | collective-permute-start | bytes 196616 | tf_op jit(solution)/shard_map/while/body/eval_jaxpr/ppermute | solution.py:32
  85.6 1.9 collective-permute-done.4
  87.5 1.3 collective-permute-start
  88.8 3.0 %collective-permute-start.1 = (f32[1,2,32,128]{3,2,1,0:T(8,128)S(1)}, f32[1,2,32,128]{3,2,1,0:T(8,128)S(1)}, u32[]{:S(2)}, u32[]{:S(2)}) collective-permute-start(f32[1,2,32,128]{3,2,1,0:T(8,128)S(1)} %get-tuple-element.749), channel_id=1, source_target_pairs={{0,4},{1,5},{2,6},{3,7},{8,12},{9,13},{10,14},{11,15},{16,20},{17,... | collective-permute-start | bytes 98312 | tf_op jit(solution)/shard_map/while/body/eval_jaxpr/ppermute | solution.py:20
  93.0 1.3 collective-permute-start.2
  94.3 5.9 %collective-permute-start.3 = (f32[1,2,64,32]{3,2,1,0:T(8,128)S(1)}, f32[1,2,64,32]{3,2,1,0:T(8,128)S(1)}, u32[]{:S(2)}, u32[]{:S(2)}) collective-permute-start(f32[1,2,64,32]{3,2,1,0:T(8,128)S(1)} %get-tuple-element.751), channel_id=1, source_target_pairs={{0,1},{1,2},{2,3},{4,5},{5,6},{6,7},{8,9},{9,10},{10,11},{12,13},{... | collective-permute-start | bytes 49160 | tf_op jit(solution)/shard_map/while/body/eval_jaxpr/ppermute | solution.py:20
  102.5 4.3 %collective-permute-start.4 = (f32[1,2,64,128]{3,2,1,0:T(8,128)S(1)}, f32[1,2,64,128]{3,2,1,0:T(8,128)S(1)}, u32[]{:S(2)}, u32[]{:S(2)}) collective-permute-start(f32[1,2,64,128]{3,2,1,0:T(8,128)S(1)} %bitcast.121), channel_id=1, source_target_pairs={{0,8},{8,16},{16,24},{1,9},{9,17},{17,25},{2,10},{10,18},{18,26},{... | collective-permute-start | bytes 196616 | tf_op jit(solution)/shard_map/while/body/eval_jaxpr/ppermute | solution.py:32
  106.8 1.9 collective-permute-done.4
  109.5 106.7 %while.39 = (s32[]{:T(128)}, f32[1,2,64,128]{3,2,1,0:T(8,128)S(1)}, f32[1,64,128]{2,1,0:T(8,128)S(1)}, f32[1,2,64,128]{3,2,1,0:T(8,128)S(1)}, pred[]{:T(512)}, /...) while((s32[]{:T(128)}, f32[1,2,64,128]{3,2,1,0:T(8,128)S(1)}, ...), condition=%wide.region_3.4_spmd.clone, body=%wide.region_2.3_spmd.clone.sunk | while | flops 126124032 | bytes 2654618 | solution.py:176
  109.6 1.3 collective-permute-start.5
  110.9 3.0 %collective-permute-start.6 = (f32[1,2,32,128]{3,2,1,0:T(8,128)S(1)}, f32[1,2,32,128]{3,2,1,0:T(8,128)S(1)}, u32[]{:S(2)}, u32[]{:S(2)}) collective-permute-start(f32[1,2,32,128]{3,2,1,0:T(8,128)S(1)} %get-tuple-element.767), channel_id=1, source_target_pairs={{0,4},{1,5},{2,6},{3,7},{8,12},{9,13},{10,14},{11,15},{16,20},{17,... | collective-permute-start | bytes 98312 | tf_op jit(solution)/shard_map/while/body/eval_jaxpr/ppermute | solution.py:20
  115.1 1.3 collective-permute-start.7
  116.4 5.9 %collective-permute-start.8 = (f32[1,2,64,32]{3,2,1,0:T(8,128)S(1)}, f32[1,2,64,32]{3,2,1,0:T(8,128)S(1)}, u32[]{:S(2)}, u32[]{:S(2)}) collective-permute-start(f32[1,2,64,32]{3,2,1,0:T(8,128)S(1)} %get-tuple-element.769), channel_id=1, source_target_pairs={{0,1},{1,2},{2,3},{4,5},{5,6},{6,7},{8,9},{9,10},{10,11},{12,13},{... | collective-permute-start | bytes 49160 | tf_op jit(solution)/shard_map/while/body/eval_jaxpr/ppermute | solution.py:20
  124.7 1.3 collective-permute-start.9
  126.0 5.2 %collective-permute-done.9 = f32[1,2,64,128]{3,2,1,0:T(8,128)S(1)} collective-permute-done((f32[1,2,64,128]{3,2,1,0:T(8,128)S(1)}, f32[1,2,64,128]{3,2,1,0:T(8,128)S(1)}, u32[]{:S(2)}, u32[]{:S(2)}) %collective-permute-start.9) | collective-permute-done | bytes 65568 | tf_op jit(solution)/shard_map/while/body/eval_jaxpr/ppermute | solution.py:32
  131.2 1.3 collective-permute-start.5
  132.5 3.0 %collective-permute-start.6 = (f32[1,2,32,128]{3,2,1,0:T(8,128)S(1)}, f32[1,2,32,128]{3,2,1,0:T(8,128)S(1)}, u32[]{:S(2)}, u32[]{:S(2)}) collective-permute-start(f32[1,2,32,128]{3,2,1,0:T(8,128)S(1)} %get-tuple-element.767), channel_id=1, source_target_pairs={{0,4},{1,5},{2,6},{3,7},{8,12},{9,13},{10,14},{11,15},{16,20},{17,... | collective-permute-start | bytes 98312 | tf_op jit(solution)/shard_map/while/body/eval_jaxpr/ppermute | solution.py:20
  136.7 1.3 collective-permute-start.7
  138.0 5.9 %collective-permute-start.8 = (f32[1,2,64,32]{3,2,1,0:T(8,128)S(1)}, f32[1,2,64,32]{3,2,1,0:T(8,128)S(1)}, u32[]{:S(2)}, u32[]{:S(2)}) collective-permute-start(f32[1,2,64,32]{3,2,1,0:T(8,128)S(1)} %get-tuple-element.769), channel_id=1, source_target_pairs={{0,1},{1,2},{2,3},{4,5},{5,6},{6,7},{8,9},{9,10},{10,11},{12,13},{... | collective-permute-start | bytes 49160 | tf_op jit(solution)/shard_map/while/body/eval_jaxpr/ppermute | solution.py:20
  144.6 1.2 collective-permute-done.8
  146.3 1.3 collective-permute-start.9
  147.6 4.8 %collective-permute-done.9 = f32[1,2,64,128]{3,2,1,0:T(8,128)S(1)} collective-permute-done((f32[1,2,64,128]{3,2,1,0:T(8,128)S(1)}, f32[1,2,64,128]{3,2,1,0:T(8,128)S(1)}, u32[]{:S(2)}, u32[]{:S(2)}) %collective-permute-start.9) | collective-permute-done | bytes 65568 | tf_op jit(solution)/shard_map/while/body/eval_jaxpr/ppermute | solution.py:32
  152.5 1.3 collective-permute-start.5
  153.8 3.0 %collective-permute-start.6 = (f32[1,2,32,128]{3,2,1,0:T(8,128)S(1)}, f32[1,2,32,128]{3,2,1,0:T(8,128)S(1)}, u32[]{:S(2)}, u32[]{:S(2)}) collective-permute-start(f32[1,2,32,128]{3,2,1,0:T(8,128)S(1)} %get-tuple-element.767), channel_id=1, source_target_pairs={{0,4},{1,5},{2,6},{3,7},{8,12},{9,13},{10,14},{11,15},{16,20},{17,... | collective-permute-start | bytes 98312 | tf_op jit(solution)/shard_map/while/body/eval_jaxpr/ppermute | solution.py:20
  158.0 1.3 collective-permute-start.7
  159.3 5.9 %collective-permute-start.8 = (f32[1,2,64,32]{3,2,1,0:T(8,128)S(1)}, f32[1,2,64,32]{3,2,1,0:T(8,128)S(1)}, u32[]{:S(2)}, u32[]{:S(2)}) collective-permute-start(f32[1,2,64,32]{3,2,1,0:T(8,128)S(1)} %get-tuple-element.769), channel_id=1, source_target_pairs={{0,1},{1,2},{2,3},{4,5},{5,6},{6,7},{8,9},{9,10},{10,11},{12,13},{... | collective-permute-start | bytes 49160 | tf_op jit(solution)/shard_map/while/body/eval_jaxpr/ppermute | solution.py:20
  165.9 1.2 collective-permute-done.8
  167.6 1.3 collective-permute-start.9
  168.9 4.8 %collective-permute-done.9 = f32[1,2,64,128]{3,2,1,0:T(8,128)S(1)} collective-permute-done((f32[1,2,64,128]{3,2,1,0:T(8,128)S(1)}, f32[1,2,64,128]{3,2,1,0:T(8,128)S(1)}, u32[]{:S(2)}, u32[]{:S(2)}) %collective-permute-start.9) | collective-permute-done | bytes 65568 | tf_op jit(solution)/shard_map/while/body/eval_jaxpr/ppermute | solution.py:32
  173.7 1.3 collective-permute-start.5
  175.0 3.0 %collective-permute-start.6 = (f32[1,2,32,128]{3,2,1,0:T(8,128)S(1)}, f32[1,2,32,128]{3,2,1,0:T(8,128)S(1)}, u32[]{:S(2)}, u32[]{:S(2)}) collective-permute-start(f32[1,2,32,128]{3,2,1,0:T(8,128)S(1)} %get-tuple-element.767), channel_id=1, source_target_pairs={{0,4},{1,5},{2,6},{3,7},{8,12},{9,13},{10,14},{11,15},{16,20},{17,... | collective-permute-start | bytes 98312 | tf_op jit(solution)/shard_map/while/body/eval_jaxpr/ppermute | solution.py:20
  179.3 1.3 collective-permute-start.7
  180.6 5.9 %collective-permute-start.8 = (f32[1,2,64,32]{3,2,1,0:T(8,128)S(1)}, f32[1,2,64,32]{3,2,1,0:T(8,128)S(1)}, u32[]{:S(2)}, u32[]{:S(2)}) collective-permute-start(f32[1,2,64,32]{3,2,1,0:T(8,128)S(1)} %get-tuple-element.769), channel_id=1, source_target_pairs={{0,1},{1,2},{2,3},{4,5},{5,6},{6,7},{8,9},{9,10},{10,11},{12,13},{... | collective-permute-start | bytes 49160 | tf_op jit(solution)/shard_map/while/body/eval_jaxpr/ppermute | solution.py:20
  188.8 1.3 collective-permute-start.9
  190.2 4.8 %collective-permute-done.9 = f32[1,2,64,128]{3,2,1,0:T(8,128)S(1)} collective-permute-done((f32[1,2,64,128]{3,2,1,0:T(8,128)S(1)}, f32[1,2,64,128]{3,2,1,0:T(8,128)S(1)}, u32[]{:S(2)}, u32[]{:S(2)}) %collective-permute-start.9) | collective-permute-done | bytes 65568 | tf_op jit(solution)/shard_map/while/body/eval_jaxpr/ppermute | solution.py:32
  195.0 1.3 collective-permute-start.5
  196.3 3.0 %collective-permute-start.6 = (f32[1,2,32,128]{3,2,1,0:T(8,128)S(1)}, f32[1,2,32,128]{3,2,1,0:T(8,128)S(1)}, u32[]{:S(2)}, u32[]{:S(2)}) collective-permute-start(f32[1,2,32,128]{3,2,1,0:T(8,128)S(1)} %get-tuple-element.767), channel_id=1, source_target_pairs={{0,4},{1,5},{2,6},{3,7},{8,12},{9,13},{10,14},{11,15},{16,20},{17,... | collective-permute-start | bytes 98312 | tf_op jit(solution)/shard_map/while/body/eval_jaxpr/ppermute | solution.py:20
  200.5 1.3 collective-permute-start.7
  201.8 5.9 %collective-permute-start.8 = (f32[1,2,64,32]{3,2,1,0:T(8,128)S(1)}, f32[1,2,64,32]{3,2,1,0:T(8,128)S(1)}, u32[]{:S(2)}, u32[]{:S(2)}) collective-permute-start(f32[1,2,64,32]{3,2,1,0:T(8,128)S(1)} %get-tuple-element.769), channel_id=1, source_target_pairs={{0,1},{1,2},{2,3},{4,5},{5,6},{6,7},{8,9},{9,10},{10,11},{12,13},{... | collective-permute-start | bytes 49160 | tf_op jit(solution)/shard_map/while/body/eval_jaxpr/ppermute | solution.py:20
  210.1 1.3 collective-permute-start.9
  211.4 4.8 %collective-permute-done.9 = f32[1,2,64,128]{3,2,1,0:T(8,128)S(1)} collective-permute-done((f32[1,2,64,128]{3,2,1,0:T(8,128)S(1)}, f32[1,2,64,128]{3,2,1,0:T(8,128)S(1)}, u32[]{:S(2)}, u32[]{:S(2)}) %collective-permute-start.9) | collective-permute-done | bytes 65568 | tf_op jit(solution)/shard_map/while/body/eval_jaxpr/ppermute | solution.py:32
  (147 shorter events, 37.7 us)
Async XLA Ops:
  1.9 0.7 copy-start.4
  3.1 0.8 copy-start.2
  4.1 104.7 %copy-start.3 = (f32[2,64,128]{2,1,0:T(8,128)S(1)}, f32[2,64,128]{2,1,0:T(8,128)}, u32[]{:S(2)}) copy-start(f32[2,64,128]{2,1,0:T(8,128)} %param.11) | copy-start | bytes 196612
  4.2 4.3 %collective-permute-start = (f32[1,2,32,128]{3,2,1,0:T(8,128)S(1)}, f32[1,2,32,128]{3,2,1,0:T(8,128)S(1)}, u32[]{:S(2)}, u32[]{:S(2)}) collective-permute-start(f32[1,2,32,128]{3,2,1,0:T(8,128)S(1)} %get-tuple-element.748), channel_id=1, source_target_pairs={{4,0},{5,1},{6,2},{7,3},{12,8},{13,9},{14,10},{15,11},{20,16},{21,... | collective-permute-start | bytes 98312 | tf_op jit(solution)/shard_map/while/body/eval_jaxpr/ppermute | solution.py:22
  5.5 3.9 %collective-permute-start.1 = (f32[1,2,32,128]{3,2,1,0:T(8,128)S(1)}, f32[1,2,32,128]{3,2,1,0:T(8,128)S(1)}, u32[]{:S(2)}, u32[]{:S(2)}) collective-permute-start(f32[1,2,32,128]{3,2,1,0:T(8,128)S(1)} %get-tuple-element.749), channel_id=1, source_target_pairs={{0,4},{1,5},{2,6},{3,7},{8,12},{9,13},{10,14},{11,15},{16,20},{17,... | collective-permute-start | bytes 98312 | tf_op jit(solution)/shard_map/while/body/eval_jaxpr/ppermute | solution.py:20
  9.7 7.4 %collective-permute-start.2 = (f32[1,2,64,32]{3,2,1,0:T(8,128)S(1)}, f32[1,2,64,32]{3,2,1,0:T(8,128)S(1)}, u32[]{:S(2)}, u32[]{:S(2)}) collective-permute-start(f32[1,2,64,32]{3,2,1,0:T(8,128)S(1)} %get-tuple-element.750), channel_id=1, source_target_pairs={{1,0},{2,1},{3,2},{5,4},{6,5},{7,6},{9,8},{10,9},{11,10},{13,12},{... | collective-permute-start | bytes 49160 | tf_op jit(solution)/shard_map/while/body/eval_jaxpr/ppermute | solution.py:22
  11.0 7.4 %collective-permute-start.3 = (f32[1,2,64,32]{3,2,1,0:T(8,128)S(1)}, f32[1,2,64,32]{3,2,1,0:T(8,128)S(1)}, u32[]{:S(2)}, u32[]{:S(2)}) collective-permute-start(f32[1,2,64,32]{3,2,1,0:T(8,128)S(1)} %get-tuple-element.751), channel_id=1, source_target_pairs={{0,1},{1,2},{2,3},{4,5},{5,6},{6,7},{8,9},{9,10},{10,11},{12,13},{... | collective-permute-start | bytes 49160 | tf_op jit(solution)/shard_map/while/body/eval_jaxpr/ppermute | solution.py:20
  18.8 5.9 %collective-permute-start.4 = (f32[1,2,64,128]{3,2,1,0:T(8,128)S(1)}, f32[1,2,64,128]{3,2,1,0:T(8,128)S(1)}, u32[]{:S(2)}, u32[]{:S(2)}) collective-permute-start(f32[1,2,64,128]{3,2,1,0:T(8,128)S(1)} %bitcast.121), channel_id=1, source_target_pairs={{0,8},{8,16},{16,24},{1,9},{9,17},{17,25},{2,10},{10,18},{18,26},{... | collective-permute-start | bytes 196616 | tf_op jit(solution)/shard_map/while/body/eval_jaxpr/ppermute | solution.py:32
  24.7 4.3 %collective-permute-start = (f32[1,2,32,128]{3,2,1,0:T(8,128)S(1)}, f32[1,2,32,128]{3,2,1,0:T(8,128)S(1)}, u32[]{:S(2)}, u32[]{:S(2)}) collective-permute-start(f32[1,2,32,128]{3,2,1,0:T(8,128)S(1)} %get-tuple-element.748), channel_id=1, source_target_pairs={{4,0},{5,1},{6,2},{7,3},{12,8},{13,9},{14,10},{15,11},{20,16},{21,... | collective-permute-start | bytes 98312 | tf_op jit(solution)/shard_map/while/body/eval_jaxpr/ppermute | solution.py:22
  26.0 3.9 %collective-permute-start.1 = (f32[1,2,32,128]{3,2,1,0:T(8,128)S(1)}, f32[1,2,32,128]{3,2,1,0:T(8,128)S(1)}, u32[]{:S(2)}, u32[]{:S(2)}) collective-permute-start(f32[1,2,32,128]{3,2,1,0:T(8,128)S(1)} %get-tuple-element.749), channel_id=1, source_target_pairs={{0,4},{1,5},{2,6},{3,7},{8,12},{9,13},{10,14},{11,15},{16,20},{17,... | collective-permute-start | bytes 98312 | tf_op jit(solution)/shard_map/while/body/eval_jaxpr/ppermute | solution.py:20
  30.3 6.9 %collective-permute-start.2 = (f32[1,2,64,32]{3,2,1,0:T(8,128)S(1)}, f32[1,2,64,32]{3,2,1,0:T(8,128)S(1)}, u32[]{:S(2)}, u32[]{:S(2)}) collective-permute-start(f32[1,2,64,32]{3,2,1,0:T(8,128)S(1)} %get-tuple-element.750), channel_id=1, source_target_pairs={{1,0},{2,1},{3,2},{5,4},{6,5},{7,6},{9,8},{10,9},{11,10},{13,12},{... | collective-permute-start | bytes 49160 | tf_op jit(solution)/shard_map/while/body/eval_jaxpr/ppermute | solution.py:22
  31.6 6.8 %collective-permute-start.3 = (f32[1,2,64,32]{3,2,1,0:T(8,128)S(1)}, f32[1,2,64,32]{3,2,1,0:T(8,128)S(1)}, u32[]{:S(2)}, u32[]{:S(2)}) collective-permute-start(f32[1,2,64,32]{3,2,1,0:T(8,128)S(1)} %get-tuple-element.751), channel_id=1, source_target_pairs={{0,1},{1,2},{2,3},{4,5},{5,6},{6,7},{8,9},{9,10},{10,11},{12,13},{... | collective-permute-start | bytes 49160 | tf_op jit(solution)/shard_map/while/body/eval_jaxpr/ppermute | solution.py:20
  38.8 6.2 %collective-permute-start.4 = (f32[1,2,64,128]{3,2,1,0:T(8,128)S(1)}, f32[1,2,64,128]{3,2,1,0:T(8,128)S(1)}, u32[]{:S(2)}, u32[]{:S(2)}) collective-permute-start(f32[1,2,64,128]{3,2,1,0:T(8,128)S(1)} %bitcast.121), channel_id=1, source_target_pairs={{0,8},{8,16},{16,24},{1,9},{9,17},{17,25},{2,10},{10,18},{18,26},{... | collective-permute-start | bytes 196616 | tf_op jit(solution)/shard_map/while/body/eval_jaxpr/ppermute | solution.py:32
  45.1 4.3 %collective-permute-start = (f32[1,2,32,128]{3,2,1,0:T(8,128)S(1)}, f32[1,2,32,128]{3,2,1,0:T(8,128)S(1)}, u32[]{:S(2)}, u32[]{:S(2)}) collective-permute-start(f32[1,2,32,128]{3,2,1,0:T(8,128)S(1)} %get-tuple-element.748), channel_id=1, source_target_pairs={{4,0},{5,1},{6,2},{7,3},{12,8},{13,9},{14,10},{15,11},{20,16},{21,... | collective-permute-start | bytes 98312 | tf_op jit(solution)/shard_map/while/body/eval_jaxpr/ppermute | solution.py:22
  46.4 3.9 %collective-permute-start.1 = (f32[1,2,32,128]{3,2,1,0:T(8,128)S(1)}, f32[1,2,32,128]{3,2,1,0:T(8,128)S(1)}, u32[]{:S(2)}, u32[]{:S(2)}) collective-permute-start(f32[1,2,32,128]{3,2,1,0:T(8,128)S(1)} %get-tuple-element.749), channel_id=1, source_target_pairs={{0,4},{1,5},{2,6},{3,7},{8,12},{9,13},{10,14},{11,15},{16,20},{17,... | collective-permute-start | bytes 98312 | tf_op jit(solution)/shard_map/while/body/eval_jaxpr/ppermute | solution.py:20
  50.6 7.8 %collective-permute-start.2 = (f32[1,2,64,32]{3,2,1,0:T(8,128)S(1)}, f32[1,2,64,32]{3,2,1,0:T(8,128)S(1)}, u32[]{:S(2)}, u32[]{:S(2)}) collective-permute-start(f32[1,2,64,32]{3,2,1,0:T(8,128)S(1)} %get-tuple-element.750), channel_id=1, source_target_pairs={{1,0},{2,1},{3,2},{5,4},{6,5},{7,6},{9,8},{10,9},{11,10},{13,12},{... | collective-permute-start | bytes 49160 | tf_op jit(solution)/shard_map/while/body/eval_jaxpr/ppermute | solution.py:22
  51.9 7.7 %collective-permute-start.3 = (f32[1,2,64,32]{3,2,1,0:T(8,128)S(1)}, f32[1,2,64,32]{3,2,1,0:T(8,128)S(1)}, u32[]{:S(2)}, u32[]{:S(2)}) collective-permute-start(f32[1,2,64,32]{3,2,1,0:T(8,128)S(1)} %get-tuple-element.751), channel_id=1, source_target_pairs={{0,1},{1,2},{2,3},{4,5},{5,6},{6,7},{8,9},{9,10},{10,11},{12,13},{... | collective-permute-start | bytes 49160 | tf_op jit(solution)/shard_map/while/body/eval_jaxpr/ppermute | solution.py:20
  60.0 6.2 %collective-permute-start.4 = (f32[1,2,64,128]{3,2,1,0:T(8,128)S(1)}, f32[1,2,64,128]{3,2,1,0:T(8,128)S(1)}, u32[]{:S(2)}, u32[]{:S(2)}) collective-permute-start(f32[1,2,64,128]{3,2,1,0:T(8,128)S(1)} %bitcast.121), channel_id=1, source_target_pairs={{0,8},{8,16},{16,24},{1,9},{9,17},{17,25},{2,10},{10,18},{18,26},{... | collective-permute-start | bytes 196616 | tf_op jit(solution)/shard_map/while/body/eval_jaxpr/ppermute | solution.py:32
  66.2 4.3 %collective-permute-start = (f32[1,2,32,128]{3,2,1,0:T(8,128)S(1)}, f32[1,2,32,128]{3,2,1,0:T(8,128)S(1)}, u32[]{:S(2)}, u32[]{:S(2)}) collective-permute-start(f32[1,2,32,128]{3,2,1,0:T(8,128)S(1)} %get-tuple-element.748), channel_id=1, source_target_pairs={{4,0},{5,1},{6,2},{7,3},{12,8},{13,9},{14,10},{15,11},{20,16},{21,... | collective-permute-start | bytes 98312 | tf_op jit(solution)/shard_map/while/body/eval_jaxpr/ppermute | solution.py:22
  67.5 3.9 %collective-permute-start.1 = (f32[1,2,32,128]{3,2,1,0:T(8,128)S(1)}, f32[1,2,32,128]{3,2,1,0:T(8,128)S(1)}, u32[]{:S(2)}, u32[]{:S(2)}) collective-permute-start(f32[1,2,32,128]{3,2,1,0:T(8,128)S(1)} %get-tuple-element.749), channel_id=1, source_target_pairs={{0,4},{1,5},{2,6},{3,7},{8,12},{9,13},{10,14},{11,15},{16,20},{17,... | collective-permute-start | bytes 98312 | tf_op jit(solution)/shard_map/while/body/eval_jaxpr/ppermute | solution.py:20
  71.8 7.8 %collective-permute-start.2 = (f32[1,2,64,32]{3,2,1,0:T(8,128)S(1)}, f32[1,2,64,32]{3,2,1,0:T(8,128)S(1)}, u32[]{:S(2)}, u32[]{:S(2)}) collective-permute-start(f32[1,2,64,32]{3,2,1,0:T(8,128)S(1)} %get-tuple-element.750), channel_id=1, source_target_pairs={{1,0},{2,1},{3,2},{5,4},{6,5},{7,6},{9,8},{10,9},{11,10},{13,12},{... | collective-permute-start | bytes 49160 | tf_op jit(solution)/shard_map/while/body/eval_jaxpr/ppermute | solution.py:22
  73.1 7.8 %collective-permute-start.3 = (f32[1,2,64,32]{3,2,1,0:T(8,128)S(1)}, f32[1,2,64,32]{3,2,1,0:T(8,128)S(1)}, u32[]{:S(2)}, u32[]{:S(2)}) collective-permute-start(f32[1,2,64,32]{3,2,1,0:T(8,128)S(1)} %get-tuple-element.751), channel_id=1, source_target_pairs={{0,1},{1,2},{2,3},{4,5},{5,6},{6,7},{8,9},{9,10},{10,11},{12,13},{... | collective-permute-start | bytes 49160 | tf_op jit(solution)/shard_map/while/body/eval_jaxpr/ppermute | solution.py:20
  81.3 6.2 %collective-permute-start.4 = (f32[1,2,64,128]{3,2,1,0:T(8,128)S(1)}, f32[1,2,64,128]{3,2,1,0:T(8,128)S(1)}, u32[]{:S(2)}, u32[]{:S(2)}) collective-permute-start(f32[1,2,64,128]{3,2,1,0:T(8,128)S(1)} %bitcast.121), channel_id=1, source_target_pairs={{0,8},{8,16},{16,24},{1,9},{9,17},{17,25},{2,10},{10,18},{18,26},{... | collective-permute-start | bytes 196616 | tf_op jit(solution)/shard_map/while/body/eval_jaxpr/ppermute | solution.py:32
  87.5 4.3 %collective-permute-start = (f32[1,2,32,128]{3,2,1,0:T(8,128)S(1)}, f32[1,2,32,128]{3,2,1,0:T(8,128)S(1)}, u32[]{:S(2)}, u32[]{:S(2)}) collective-permute-start(f32[1,2,32,128]{3,2,1,0:T(8,128)S(1)} %get-tuple-element.748), channel_id=1, source_target_pairs={{4,0},{5,1},{6,2},{7,3},{12,8},{13,9},{14,10},{15,11},{20,16},{21,... | collective-permute-start | bytes 98312 | tf_op jit(solution)/shard_map/while/body/eval_jaxpr/ppermute | solution.py:22
  88.8 3.9 %collective-permute-start.1 = (f32[1,2,32,128]{3,2,1,0:T(8,128)S(1)}, f32[1,2,32,128]{3,2,1,0:T(8,128)S(1)}, u32[]{:S(2)}, u32[]{:S(2)}) collective-permute-start(f32[1,2,32,128]{3,2,1,0:T(8,128)S(1)} %get-tuple-element.749), channel_id=1, source_target_pairs={{0,4},{1,5},{2,6},{3,7},{8,12},{9,13},{10,14},{11,15},{16,20},{17,... | collective-permute-start | bytes 98312 | tf_op jit(solution)/shard_map/while/body/eval_jaxpr/ppermute | solution.py:20
  93.0 7.8 %collective-permute-start.2 = (f32[1,2,64,32]{3,2,1,0:T(8,128)S(1)}, f32[1,2,64,32]{3,2,1,0:T(8,128)S(1)}, u32[]{:S(2)}, u32[]{:S(2)}) collective-permute-start(f32[1,2,64,32]{3,2,1,0:T(8,128)S(1)} %get-tuple-element.750), channel_id=1, source_target_pairs={{1,0},{2,1},{3,2},{5,4},{6,5},{7,6},{9,8},{10,9},{11,10},{13,12},{... | collective-permute-start | bytes 49160 | tf_op jit(solution)/shard_map/while/body/eval_jaxpr/ppermute | solution.py:22
  94.3 7.8 %collective-permute-start.3 = (f32[1,2,64,32]{3,2,1,0:T(8,128)S(1)}, f32[1,2,64,32]{3,2,1,0:T(8,128)S(1)}, u32[]{:S(2)}, u32[]{:S(2)}) collective-permute-start(f32[1,2,64,32]{3,2,1,0:T(8,128)S(1)} %get-tuple-element.751), channel_id=1, source_target_pairs={{0,1},{1,2},{2,3},{4,5},{5,6},{6,7},{8,9},{9,10},{10,11},{12,13},{... | collective-permute-start | bytes 49160 | tf_op jit(solution)/shard_map/while/body/eval_jaxpr/ppermute | solution.py:20
  102.5 6.2 %collective-permute-start.4 = (f32[1,2,64,128]{3,2,1,0:T(8,128)S(1)}, f32[1,2,64,128]{3,2,1,0:T(8,128)S(1)}, u32[]{:S(2)}, u32[]{:S(2)}) collective-permute-start(f32[1,2,64,128]{3,2,1,0:T(8,128)S(1)} %bitcast.121), channel_id=1, source_target_pairs={{0,8},{8,16},{16,24},{1,9},{9,17},{17,25},{2,10},{10,18},{18,26},{... | collective-permute-start | bytes 196616 | tf_op jit(solution)/shard_map/while/body/eval_jaxpr/ppermute | solution.py:32
  108.7 0.7 copy-start
  109.6 4.3 %collective-permute-start.5 = (f32[1,2,32,128]{3,2,1,0:T(8,128)S(1)}, f32[1,2,32,128]{3,2,1,0:T(8,128)S(1)}, u32[]{:S(2)}, u32[]{:S(2)}) collective-permute-start(f32[1,2,32,128]{3,2,1,0:T(8,128)S(1)} %get-tuple-element.766), channel_id=1, source_target_pairs={{4,0},{5,1},{6,2},{7,3},{12,8},{13,9},{14,10},{15,11},{20,16},{21,... | collective-permute-start | bytes 98312 | tf_op jit(solution)/shard_map/while/body/eval_jaxpr/ppermute | solution.py:22
  110.9 3.9 %collective-permute-start.6 = (f32[1,2,32,128]{3,2,1,0:T(8,128)S(1)}, f32[1,2,32,128]{3,2,1,0:T(8,128)S(1)}, u32[]{:S(2)}, u32[]{:S(2)}) collective-permute-start(f32[1,2,32,128]{3,2,1,0:T(8,128)S(1)} %get-tuple-element.767), channel_id=1, source_target_pairs={{0,4},{1,5},{2,6},{3,7},{8,12},{9,13},{10,14},{11,15},{16,20},{17,... | collective-permute-start | bytes 98312 | tf_op jit(solution)/shard_map/while/body/eval_jaxpr/ppermute | solution.py:20
  115.1 7.8 %collective-permute-start.7 = (f32[1,2,64,32]{3,2,1,0:T(8,128)S(1)}, f32[1,2,64,32]{3,2,1,0:T(8,128)S(1)}, u32[]{:S(2)}, u32[]{:S(2)}) collective-permute-start(f32[1,2,64,32]{3,2,1,0:T(8,128)S(1)} %get-tuple-element.768), channel_id=1, source_target_pairs={{1,0},{2,1},{3,2},{5,4},{6,5},{7,6},{9,8},{10,9},{11,10},{13,12},{... | collective-permute-start | bytes 49160 | tf_op jit(solution)/shard_map/while/body/eval_jaxpr/ppermute | solution.py:22
  116.4 7.8 %collective-permute-start.8 = (f32[1,2,64,32]{3,2,1,0:T(8,128)S(1)}, f32[1,2,64,32]{3,2,1,0:T(8,128)S(1)}, u32[]{:S(2)}, u32[]{:S(2)}) collective-permute-start(f32[1,2,64,32]{3,2,1,0:T(8,128)S(1)} %get-tuple-element.769), channel_id=1, source_target_pairs={{0,1},{1,2},{2,3},{4,5},{5,6},{6,7},{8,9},{9,10},{10,11},{12,13},{... | collective-permute-start | bytes 49160 | tf_op jit(solution)/shard_map/while/body/eval_jaxpr/ppermute | solution.py:20
  124.7 6.5 %collective-permute-start.9 = (f32[1,2,64,128]{3,2,1,0:T(8,128)S(1)}, f32[1,2,64,128]{3,2,1,0:T(8,128)S(1)}, u32[]{:S(2)}, u32[]{:S(2)}) collective-permute-start(f32[1,2,64,128]{3,2,1,0:T(8,128)S(1)} %pad_maximum_fusion.17), channel_id=1, source_target_pairs={{8,0},{16,8},{24,16},{9,1},{17,9},{25,17},{10,2},{18,10},{26,18},{... | collective-permute-start | bytes 196616 | tf_op jit(solution)/shard_map/while/body/eval_jaxpr/ppermute | solution.py:32
  131.2 4.3 %collective-permute-start.5 = (f32[1,2,32,128]{3,2,1,0:T(8,128)S(1)}, f32[1,2,32,128]{3,2,1,0:T(8,128)S(1)}, u32[]{:S(2)}, u32[]{:S(2)}) collective-permute-start(f32[1,2,32,128]{3,2,1,0:T(8,128)S(1)} %get-tuple-element.766), channel_id=1, source_target_pairs={{4,0},{5,1},{6,2},{7,3},{12,8},{13,9},{14,10},{15,11},{20,16},{21,... | collective-permute-start | bytes 98312 | tf_op jit(solution)/shard_map/while/body/eval_jaxpr/ppermute | solution.py:22
  132.5 3.9 %collective-permute-start.6 = (f32[1,2,32,128]{3,2,1,0:T(8,128)S(1)}, f32[1,2,32,128]{3,2,1,0:T(8,128)S(1)}, u32[]{:S(2)}, u32[]{:S(2)}) collective-permute-start(f32[1,2,32,128]{3,2,1,0:T(8,128)S(1)} %get-tuple-element.767), channel_id=1, source_target_pairs={{0,4},{1,5},{2,6},{3,7},{8,12},{9,13},{10,14},{11,15},{16,20},{17,... | collective-permute-start | bytes 98312 | tf_op jit(solution)/shard_map/while/body/eval_jaxpr/ppermute | solution.py:20
  136.7 7.8 %collective-permute-start.7 = (f32[1,2,64,32]{3,2,1,0:T(8,128)S(1)}, f32[1,2,64,32]{3,2,1,0:T(8,128)S(1)}, u32[]{:S(2)}, u32[]{:S(2)}) collective-permute-start(f32[1,2,64,32]{3,2,1,0:T(8,128)S(1)} %get-tuple-element.768), channel_id=1, source_target_pairs={{1,0},{2,1},{3,2},{5,4},{6,5},{7,6},{9,8},{10,9},{11,10},{13,12},{... | collective-permute-start | bytes 49160 | tf_op jit(solution)/shard_map/while/body/eval_jaxpr/ppermute | solution.py:22
  138.0 7.8 %collective-permute-start.8 = (f32[1,2,64,32]{3,2,1,0:T(8,128)S(1)}, f32[1,2,64,32]{3,2,1,0:T(8,128)S(1)}, u32[]{:S(2)}, u32[]{:S(2)}) collective-permute-start(f32[1,2,64,32]{3,2,1,0:T(8,128)S(1)} %get-tuple-element.769), channel_id=1, source_target_pairs={{0,1},{1,2},{2,3},{4,5},{5,6},{6,7},{8,9},{9,10},{10,11},{12,13},{... | collective-permute-start | bytes 49160 | tf_op jit(solution)/shard_map/while/body/eval_jaxpr/ppermute | solution.py:20
  146.3 6.2 %collective-permute-start.9 = (f32[1,2,64,128]{3,2,1,0:T(8,128)S(1)}, f32[1,2,64,128]{3,2,1,0:T(8,128)S(1)}, u32[]{:S(2)}, u32[]{:S(2)}) collective-permute-start(f32[1,2,64,128]{3,2,1,0:T(8,128)S(1)} %pad_maximum_fusion.17), channel_id=1, source_target_pairs={{8,0},{16,8},{24,16},{9,1},{17,9},{25,17},{10,2},{18,10},{26,18},{... | collective-permute-start | bytes 196616 | tf_op jit(solution)/shard_map/while/body/eval_jaxpr/ppermute | solution.py:32
  152.5 4.3 %collective-permute-start.5 = (f32[1,2,32,128]{3,2,1,0:T(8,128)S(1)}, f32[1,2,32,128]{3,2,1,0:T(8,128)S(1)}, u32[]{:S(2)}, u32[]{:S(2)}) collective-permute-start(f32[1,2,32,128]{3,2,1,0:T(8,128)S(1)} %get-tuple-element.766), channel_id=1, source_target_pairs={{4,0},{5,1},{6,2},{7,3},{12,8},{13,9},{14,10},{15,11},{20,16},{21,... | collective-permute-start | bytes 98312 | tf_op jit(solution)/shard_map/while/body/eval_jaxpr/ppermute | solution.py:22
  153.8 3.9 %collective-permute-start.6 = (f32[1,2,32,128]{3,2,1,0:T(8,128)S(1)}, f32[1,2,32,128]{3,2,1,0:T(8,128)S(1)}, u32[]{:S(2)}, u32[]{:S(2)}) collective-permute-start(f32[1,2,32,128]{3,2,1,0:T(8,128)S(1)} %get-tuple-element.767), channel_id=1, source_target_pairs={{0,4},{1,5},{2,6},{3,7},{8,12},{9,13},{10,14},{11,15},{16,20},{17,... | collective-permute-start | bytes 98312 | tf_op jit(solution)/shard_map/while/body/eval_jaxpr/ppermute | solution.py:20
  158.0 7.8 %collective-permute-start.7 = (f32[1,2,64,32]{3,2,1,0:T(8,128)S(1)}, f32[1,2,64,32]{3,2,1,0:T(8,128)S(1)}, u32[]{:S(2)}, u32[]{:S(2)}) collective-permute-start(f32[1,2,64,32]{3,2,1,0:T(8,128)S(1)} %get-tuple-element.768), channel_id=1, source_target_pairs={{1,0},{2,1},{3,2},{5,4},{6,5},{7,6},{9,8},{10,9},{11,10},{13,12},{... | collective-permute-start | bytes 49160 | tf_op jit(solution)/shard_map/while/body/eval_jaxpr/ppermute | solution.py:22
  159.3 7.8 %collective-permute-start.8 = (f32[1,2,64,32]{3,2,1,0:T(8,128)S(1)}, f32[1,2,64,32]{3,2,1,0:T(8,128)S(1)}, u32[]{:S(2)}, u32[]{:S(2)}) collective-permute-start(f32[1,2,64,32]{3,2,1,0:T(8,128)S(1)} %get-tuple-element.769), channel_id=1, source_target_pairs={{0,1},{1,2},{2,3},{4,5},{5,6},{6,7},{8,9},{9,10},{10,11},{12,13},{... | collective-permute-start | bytes 49160 | tf_op jit(solution)/shard_map/while/body/eval_jaxpr/ppermute | solution.py:20
  167.6 6.2 %collective-permute-start.9 = (f32[1,2,64,128]{3,2,1,0:T(8,128)S(1)}, f32[1,2,64,128]{3,2,1,0:T(8,128)S(1)}, u32[]{:S(2)}, u32[]{:S(2)}) collective-permute-start(f32[1,2,64,128]{3,2,1,0:T(8,128)S(1)} %pad_maximum_fusion.17), channel_id=1, source_target_pairs={{8,0},{16,8},{24,16},{9,1},{17,9},{25,17},{10,2},{18,10},{26,18},{... | collective-permute-start | bytes 196616 | tf_op jit(solution)/shard_map/while/body/eval_jaxpr/ppermute | solution.py:32
  173.7 4.3 %collective-permute-start.5 = (f32[1,2,32,128]{3,2,1,0:T(8,128)S(1)}, f32[1,2,32,128]{3,2,1,0:T(8,128)S(1)}, u32[]{:S(2)}, u32[]{:S(2)}) collective-permute-start(f32[1,2,32,128]{3,2,1,0:T(8,128)S(1)} %get-tuple-element.766), channel_id=1, source_target_pairs={{4,0},{5,1},{6,2},{7,3},{12,8},{13,9},{14,10},{15,11},{20,16},{21,... | collective-permute-start | bytes 98312 | tf_op jit(solution)/shard_map/while/body/eval_jaxpr/ppermute | solution.py:22
  175.0 3.9 %collective-permute-start.6 = (f32[1,2,32,128]{3,2,1,0:T(8,128)S(1)}, f32[1,2,32,128]{3,2,1,0:T(8,128)S(1)}, u32[]{:S(2)}, u32[]{:S(2)}) collective-permute-start(f32[1,2,32,128]{3,2,1,0:T(8,128)S(1)} %get-tuple-element.767), channel_id=1, source_target_pairs={{0,4},{1,5},{2,6},{3,7},{8,12},{9,13},{10,14},{11,15},{16,20},{17,... | collective-permute-start | bytes 98312 | tf_op jit(solution)/shard_map/while/body/eval_jaxpr/ppermute | solution.py:20
  179.3 7.8 %collective-permute-start.7 = (f32[1,2,64,32]{3,2,1,0:T(8,128)S(1)}, f32[1,2,64,32]{3,2,1,0:T(8,128)S(1)}, u32[]{:S(2)}, u32[]{:S(2)}) collective-permute-start(f32[1,2,64,32]{3,2,1,0:T(8,128)S(1)} %get-tuple-element.768), channel_id=1, source_target_pairs={{1,0},{2,1},{3,2},{5,4},{6,5},{7,6},{9,8},{10,9},{11,10},{13,12},{... | collective-permute-start | bytes 49160 | tf_op jit(solution)/shard_map/while/body/eval_jaxpr/ppermute | solution.py:22
  180.6 7.8 %collective-permute-start.8 = (f32[1,2,64,32]{3,2,1,0:T(8,128)S(1)}, f32[1,2,64,32]{3,2,1,0:T(8,128)S(1)}, u32[]{:S(2)}, u32[]{:S(2)}) collective-permute-start(f32[1,2,64,32]{3,2,1,0:T(8,128)S(1)} %get-tuple-element.769), channel_id=1, source_target_pairs={{0,1},{1,2},{2,3},{4,5},{5,6},{6,7},{8,9},{9,10},{10,11},{12,13},{... | collective-permute-start | bytes 49160 | tf_op jit(solution)/shard_map/while/body/eval_jaxpr/ppermute | solution.py:20
  188.8 6.2 %collective-permute-start.9 = (f32[1,2,64,128]{3,2,1,0:T(8,128)S(1)}, f32[1,2,64,128]{3,2,1,0:T(8,128)S(1)}, u32[]{:S(2)}, u32[]{:S(2)}) collective-permute-start(f32[1,2,64,128]{3,2,1,0:T(8,128)S(1)} %pad_maximum_fusion.17), channel_id=1, source_target_pairs={{8,0},{16,8},{24,16},{9,1},{17,9},{25,17},{10,2},{18,10},{26,18},{... | collective-permute-start | bytes 196616 | tf_op jit(solution)/shard_map/while/body/eval_jaxpr/ppermute | solution.py:32
  195.0 4.3 %collective-permute-start.5 = (f32[1,2,32,128]{3,2,1,0:T(8,128)S(1)}, f32[1,2,32,128]{3,2,1,0:T(8,128)S(1)}, u32[]{:S(2)}, u32[]{:S(2)}) collective-permute-start(f32[1,2,32,128]{3,2,1,0:T(8,128)S(1)} %get-tuple-element.766), channel_id=1, source_target_pairs={{4,0},{5,1},{6,2},{7,3},{12,8},{13,9},{14,10},{15,11},{20,16},{21,... | collective-permute-start | bytes 98312 | tf_op jit(solution)/shard_map/while/body/eval_jaxpr/ppermute | solution.py:22
  196.3 3.9 %collective-permute-start.6 = (f32[1,2,32,128]{3,2,1,0:T(8,128)S(1)}, f32[1,2,32,128]{3,2,1,0:T(8,128)S(1)}, u32[]{:S(2)}, u32[]{:S(2)}) collective-permute-start(f32[1,2,32,128]{3,2,1,0:T(8,128)S(1)} %get-tuple-element.767), channel_id=1, source_target_pairs={{0,4},{1,5},{2,6},{3,7},{8,12},{9,13},{10,14},{11,15},{16,20},{17,... | collective-permute-start | bytes 98312 | tf_op jit(solution)/shard_map/while/body/eval_jaxpr/ppermute | solution.py:20
  200.5 7.8 %collective-permute-start.7 = (f32[1,2,64,32]{3,2,1,0:T(8,128)S(1)}, f32[1,2,64,32]{3,2,1,0:T(8,128)S(1)}, u32[]{:S(2)}, u32[]{:S(2)}) collective-permute-start(f32[1,2,64,32]{3,2,1,0:T(8,128)S(1)} %get-tuple-element.768), channel_id=1, source_target_pairs={{1,0},{2,1},{3,2},{5,4},{6,5},{7,6},{9,8},{10,9},{11,10},{13,12},{... | collective-permute-start | bytes 49160 | tf_op jit(solution)/shard_map/while/body/eval_jaxpr/ppermute | solution.py:22
  201.8 7.8 %collective-permute-start.8 = (f32[1,2,64,32]{3,2,1,0:T(8,128)S(1)}, f32[1,2,64,32]{3,2,1,0:T(8,128)S(1)}, u32[]{:S(2)}, u32[]{:S(2)}) collective-permute-start(f32[1,2,64,32]{3,2,1,0:T(8,128)S(1)} %get-tuple-element.769), channel_id=1, source_target_pairs={{0,1},{1,2},{2,3},{4,5},{5,6},{6,7},{8,9},{9,10},{10,11},{12,13},{... | collective-permute-start | bytes 49160 | tf_op jit(solution)/shard_map/while/body/eval_jaxpr/ppermute | solution.py:20
  210.1 6.2 %collective-permute-start.9 = (f32[1,2,64,128]{3,2,1,0:T(8,128)S(1)}, f32[1,2,64,128]{3,2,1,0:T(8,128)S(1)}, u32[]{:S(2)}, u32[]{:S(2)}) collective-permute-start(f32[1,2,64,128]{3,2,1,0:T(8,128)S(1)} %pad_maximum_fusion.17), channel_id=1, source_target_pairs={{8,0},{16,8},{24,16},{9,1},{17,9},{25,17},{10,2},{18,10},{26,18},{... | collective-permute-start | bytes 196616 | tf_op jit(solution)/shard_map/while/body/eval_jaxpr/ppermute | solution.py:32
  216.3 0.6 copy-start.1
where the time goes:
time: 221 us; the launch traced here: 217 us
  starting transfers between devices  141 us (64%)
  waiting for transfers between devices  60.9 us (28%)
  matrix products  7.06 us (3%)
  local copies, waits for them, and re-layouts  3.87 us (2%)
    ppermute x20, starting transfers between devices, extended_2(): lax.ppermute(tail, axis, [(i, (i + 1) % count) for i in range(ends)])  87.6 us
    ppermute x10, waiting for transfers between devices, from_behind(): lax.ppermute(value, axis, [(source, source + steps) for source in range(l...  33.9 us
    ppermute x10, starting transfers between devices, from_behind(): lax.ppermute(value, axis, [(source, source + steps) for source in range(l...  27.5 us
    ppermute x20, starting transfers between devices, extended_2(): lax.ppermute(head, axis, [((i + 1) % count, i) for i in range(ends)])  25.8 us
    ppermute x20, waiting for transfers between devices, extended_2(): lax.ppermute(tail, axis, [(i, (i + 1) % count) for i in range(ends)])  20.5 us
    ppermute x20, waiting for transfers between devices, extended_2(): lax.ppermute(head, axis, [((i + 1) % count, i) for i in range(ends)])  6.47 us
  transfers between devices with their start and end apart: 50, of which 40 were waited for; matrix products, arithmetic and copies ran while one was open for 0% of the time, Pallas kernels for 0%

commit v1 on v0

--- a/solution.py
+++ b/solution.py
@@ -1,12 +1,282 @@
+import functools
 import math
 
 import jax
 import jax.numpy as jnp
+import numpy as np
 from jax import lax
+from jax.experimental import pallas as pl
+from jax.experimental.pallas import tpu as pltpu
 from jax.sharding import PartitionSpec as P
 
 HALO = 32
 FRESNEL = 64
+LANES = 128
+GATHER_BUDGET = 4 * 2**20
+SIN = (
+    0.9999999980536763,
+    -0.1666666530009577,
+    0.008333305907073658,
+    -0.00019838908256358006,
+    2.745822627876341e-06,
+    -2.3043562782810933e-08,
+)
+COS = (
+    0.9999999961345007,
+    -0.4999999301617528,
+    0.04166646215023687,
+    -0.0013886696163545999,
+    2.4695045482778703e-05,
+    -2.5154931690000354e-07,
+)
+
+
+def horner(coefficients, square):
+    total = jnp.full_like(square, coefficients[-1])
+    for coefficient in coefficients[-2::-1]:
+        total = total * square + coefficient
+    return total
+
+
+def cos_sin(angle):
+    square = angle * angle
+    return horner(COS, square), horner(SIN, square) * angle
+
+
+def turn(fraction):
+    half_cos, half_sin = cos_sin(fraction * math.pi)
+    return half_cos * half_cos - half_sin * half_sin, 2.0 * half_cos * half_sin
+
+
+def halves(value):
+    high = value.astype(jnp.bfloat16)
+    return high, (value - high.astype(jnp.float32)).astype(jnp.bfloat16)
+
+
+def np_halves(matrix):
+    high = matrix.astype(jnp.bfloat16)
+    return high, (matrix - high.astype(np.float64)).astype(jnp.bfloat16)
+
+
+def np_taps():
+    offset = np.arange(-HALO, HALO + 1, dtype=np.float64)
+    taper = np.maximum(np.abs(offset) - 0.5 * HALO, 0.0)
+    weight = np.cos(np.pi * taper / (HALO + 2.0)) ** 2 / math.sqrt(FRESNEL)
+    return weight * np.exp(1j * np.pi * offset * offset / FRESNEL)
+
+
+def np_band(out_pos, in_pos):
+    offset = out_pos[:, None] - in_pos[None, :]
+    inside = np.abs(offset) <= HALO
+    return np.where(inside, np_taps()[np.clip(offset, -HALO, HALO) + HALO], 0.0)
+
+
+def row_constant(height):
+    band = np_band(np.arange(height), np.arange(height))
+    whole = np.block([[band.real, -band.imag], [band.imag, band.real]])
+    high, low = np_halves(whole)
+    return np.concatenate([high, high, low], axis=1)
+
+
+def col_constant():
+    lane = np.arange(LANES)
+    edge_pos = np.where(lane < LANES // 2, lane + LANES, lane - LANES)
+    parts = []
+    for position in (lane, edge_pos):
+        band = np_band(lane, position).T
+        parts.append(np.block([[band.real, band.imag], [-band.imag, band.real]]))
+    high, low = np_halves(np.concatenate(parts, axis=0))
+    return np.concatenate([high, high, low], axis=0)
+
+
+def wave_kernel(
+    sections, tilt_ref, phase_ref, intensity_ref, row_ref, col_ref, grad_ref, exit_ref,
+    cos_ref, sin_ref, u_high, u_low, a_high, a_low, v_ref, moved_ref,
+):
+    items, height, width = v_ref.shape[0], v_ref.shape[2], v_ref.shape[3]
+    slices, tile_r, tile_c = grad_ref.shape
+    rows, cols = height // tile_r, width // tile_c
+    count = sections * slices
+    blocks = width // LANES
+    half = LANES // 2
+    first = lax.axis_index("depth") * slices
+    own_row = pl.multiple_of(lax.axis_index("row") * tile_r, tile_r)
+    own_col = pl.multiple_of(lax.axis_index("col") * tile_c, tile_c)
+    own = (pl.ds(own_row, tile_r), pl.ds(own_col, tile_c))
+
+    def store_u(item, row, col, real, imag):
+        for part, value in enumerate((real, imag)):
+            high, low = halves(value)
+            where = (item, pl.ds(part * height + row, value.shape[0]), pl.ds(col, value.shape[1]))
+            u_high[where] = high
+            u_low[where] = low
+
+    def keep_moved(slice_index):
+        @pl.when((slice_index >= first) & (slice_index < first + slices))
+        def _():
+            cos, sin = cos_ref[(slice_index,) + own], sin_ref[(slice_index,) + own]
+            for item in range(items):
+                real, imag = v_ref[(item, 0) + own], v_ref[(item, 1) + own]
+                moved_ref[slice_index - first, item, 0] = cos * real - sin * imag
+                moved_ref[slice_index - first, item, 1] = cos * imag + sin * real
+
+    def transmit(slice_index):
+        for item in range(items):
+            for block in range(blocks):
+                where = (slice(None), pl.ds(block * LANES, LANES))
+                cos, sin = cos_ref[(slice_index,) + where], sin_ref[(slice_index,) + where]
+                real, imag = v_ref[(item, 0) + where], v_ref[(item, 1) + where]
+                store_u(item, 0, block * LANES, cos * real - sin * imag, cos * imag + sin * real)
+
+    def propagate():
+        for item in range(items):
+            for start in range(0, width, 2 * LANES):
+                where = (item, slice(None), pl.ds(start, 2 * LANES))
+                high, low = u_high[where], u_low[where]
+                done = jnp.dot(
+                    row_ref[...],
+                    jnp.concatenate([high, low, high], axis=0),
+                    preferred_element_type=jnp.float32,
+                )
+                for part in range(2):
+                    for sub in range(2):
+                        block = start // LANES + sub
+                        value = done[part * height : (part + 1) * height, sub * LANES : (sub + 1) * LANES]
+                        for target, piece in zip((a_high, a_low), halves(value)):
+                            target[item, block, :, pl.ds(part * LANES, LANES)] = piece
+                            if block > 0:
+                                target[item, block - 1, :, pl.ds((2 + part) * LANES, half)] = piece[:, :half]
+                            if block < blocks - 1:
+                                target[item, block + 1, :, pl.ds((2 + part) * LANES + half, half)] = piece[:, half:]
+        for item in range(items):
+            high = a_high[item].reshape(blocks * height, 4 * LANES)
+            low = a_low[item].reshape(blocks * height, 4 * LANES)
+            done = jnp.dot(
+                jnp.concatenate([high, low, high], axis=1),
+                col_ref[...],
+                preferred_element_type=jnp.float32,
+            )
+            for block in range(blocks):
+                for part in range(2):
+                    v_ref[item, part, :, pl.ds(block * LANES, LANES)] = done[
+                        block * height : (block + 1) * height, part * LANES : (part + 1) * LANES
+                    ]
+
+    for target in (a_high, a_low):
+        for item in range(items):
+            for part in range(2):
+                target[item, 0, :, pl.ds((2 + part) * LANES + half, half)] = jnp.zeros((height, half), jnp.bfloat16)
+                target[item, blocks - 1, :, pl.ds((2 + part) * LANES, half)] = jnp.zeros((height, half), jnp.bfloat16)
+
+    def screens(slice_index, carry):
+        section, inner = slice_index // slices, slice_index % slices
+        for row in range(rows):
+            for col in range(cols):
+                cos, sin = cos_sin(phase_ref[section * (rows * cols) + row * cols + col, inner])
+                where = (slice_index, pl.ds(row * tile_r, tile_r), pl.ds(col * tile_c, tile_c))
+                cos_ref[where] = cos
+                sin_ref[where] = sin
+        return carry
+
+    lax.fori_loop(0, count, screens, 0)
+
+    def cycles(number, position, extent):
+        fraction = (number * position).astype(jnp.float32) / extent
+        return turn(fraction - jnp.round(fraction))
+
+    for item in range(items):
+        row_cos, row_sin = cycles(
+            tilt_ref[item, 0], lax.broadcasted_iota(jnp.int32, (height, LANES), 0), float(height)
+        )
+        for block in range(blocks):
+            col_cos, col_sin = cycles(
+                tilt_ref[item, 1],
+                lax.broadcasted_iota(jnp.int32, (8, LANES), 1) + block * LANES,
+                float(width),
+            )
+            col_cos, col_sin = col_cos[:1], col_sin[:1]
+            where = (slice(None), pl.ds(block * LANES, LANES))
+            v_ref[(item, 0) + where] = row_cos * col_cos - row_sin * col_sin
+            v_ref[(item, 1) + where] = row_sin * col_cos + row_cos * col_sin
+    transmit(0)
+    keep_moved(0)
+
+    def step(tick, carry):
+        propagate()
+
+        @pl.when((tick >= first) & (tick < first + slices))
+        def _():
+            for item in range(items):
+                for part in range(2):
+                    exit_ref[item, tick - first, part] = v_ref[(item, part) + own]
+
+        @pl.when(tick == count - 1)
+        def _():
+            for item in range(items):
+                for row in range(rows):
+                    for col in range(cols):
+                        where = (pl.ds(row * tile_r, tile_r), pl.ds(col * tile_c, tile_c))
+                        real, imag = v_ref[(item, 0) + where], v_ref[(item, 1) + where]
+                        misfit = 2.0 * (real * real + imag * imag - intensity_ref[row * cols + col, item])
+                        store_u(item, row * tile_r, col * tile_c, misfit * real, -misfit * imag)
+
+        back = 2 * count - 1 - tick
+
+        @pl.when((tick >= count) & (back < first + slices))
+        def _():
+            total = jnp.zeros((tile_r, tile_c), jnp.float32)
+            for item in range(items):
+                real, imag = v_ref[(item, 0) + own], v_ref[(item, 1) + own]
+                total = total - (
+                    imag * moved_ref[back - first, item, 0] + real * moved_ref[back - first, item, 1]
+                )
+            grad_ref[back - first] = total
+
+        @pl.when((tick != count - 1) & (back > first))
+        def _():
+            transmit(jnp.where(tick < count, tick + 1, back))
+
+        @pl.when(tick < count - 1)
+        def _():
+            keep_moved(tick + 1)
+
+        return carry
+
+    lax.fori_loop(0, 2 * count - first, step, 0)
+
+
+def whole_field_body(sections, phase, tilt, intensity):
+    slices, tile_r, tile_c = phase.shape
+    items = tilt.shape[0]
+    height = tile_r * lax.axis_size("row")
+    width = tile_c * lax.axis_size("col")
+    count = sections * slices
+    blocks = width // LANES
+    all_phase = lax.all_gather(phase, ("depth", "row", "col"))
+    all_intensity = lax.all_gather(intensity, ("row", "col"))
+    vmem = pl.BlockSpec(memory_space=pltpu.VMEM)
+    field = (items, 2, height, width)
+    gradient, leaving = pl.pallas_call(
+        functools.partial(wave_kernel, sections),
+        out_shape=(
+            jax.ShapeDtypeStruct(phase.shape, jnp.float32),
+            jax.ShapeDtypeStruct((items, slices, 2, tile_r, tile_c), jnp.float32),
+        ),
+        in_specs=[pl.BlockSpec(memory_space=pltpu.SMEM), vmem, vmem, vmem, vmem],
+        out_specs=(vmem, vmem),
+        scratch_shapes=[
+            pltpu.VMEM((count, height, width), jnp.float32),
+            pltpu.VMEM((count, height, width), jnp.float32),
+            pltpu.VMEM((items, 2 * height, width), jnp.bfloat16),
+            pltpu.VMEM((items, 2 * height, width), jnp.bfloat16),
+            pltpu.VMEM((items, blocks, height, 4 * LANES), jnp.bfloat16),
+            pltpu.VMEM((items, blocks, height, 4 * LANES), jnp.bfloat16),
+            pltpu.VMEM(field, jnp.float32),
+            pltpu.VMEM((slices, items, 2, tile_r, tile_c), jnp.float32),
+        ],
+        compiler_params=pltpu.CompilerParams(vmem_limit_bytes=40 * 2**20),
+    )(tilt, all_phase, all_intensity, jnp.asarray(row_constant(height)), jnp.asarray(col_constant()))
+    return gradient, leaving
 
 
 def extended_2(cells, sides, width):
@@ -93,7 +363,7 @@
     return lax.dynamic_update_slice(store, fresh, begin)
 
 
-def body(phase, tilt, intensity):
+def staged_body(phase, tilt, intensity):
     slices, tile_r, tile_c = phase.shape
     batch_size = tilt.shape[0]
     sections = lax.axis_size("depth")
@@ -177,12 +447,33 @@
     return (gradient, leaving)
 
 
+def fits_whole(phase_shape, batch, mesh):
+    slices, height, width = phase_shape
+    rows, cols = mesh.shape["row"], mesh.shape["col"]
+    bytes_all = 4 * height * width * (slices + batch)
+    return (
+        bytes_all <= GATHER_BUDGET
+        and height == LANES
+        and (height // rows) % 16 == 0
+        and (width // cols) % LANES == 0
+        and width % (2 * LANES) == 0
+    )
+
+
 def solution(mesh):
     placed = (P("depth", "row", "col"), P(), P(None, "row", "col"))
-    return jax.shard_map(
-        body,
-        mesh=mesh,
-        in_specs=placed,
-        out_specs=(P("depth", "row", "col"), P(None, "depth", None, "row", "col")),
-        check_vma=False,
-    )
+
+    def run(phase, tilt, intensity):
+        if fits_whole(phase.shape, tilt.shape[0], mesh):
+            body = functools.partial(whole_field_body, mesh.shape["depth"])
+        else:
+            body = staged_body
+        return jax.shard_map(
+            body,
+            mesh=mesh,
+            in_specs=placed,
+            out_specs=(P("depth", "row", "col"), P(None, "depth", None, "row", "col")),
+            check_vma=False,
+        )(phase, tilt, intensity)
+
+    return run

time: 221 us -> 97 us (0.44); the launches traced: 217 us -> 96.8 us
  starting transfers between devices: 141 us -> 0.04 us
  waiting for transfers between devices: 60.9 us -> 34 us
  blocking collectives: 0 us -> 26.3 us
  Pallas kernels: 0 us -> 19.3 us
  between operations: 0.82 us -> 14 us
  matrix products: 7.06 us -> 0 us
    ppermute x50 -> x0, starting transfers between devices: 141 us -> none  [the longest x20 87.6 us: extended_2(): lax.ppermute(tail, axis, [(i, (i + 1) % count) for i in range(ends)])]
    ppermute x50 -> x0, waiting for transfers between devices: 60.9 us -> none  [the longest x10 33.9 us: from_behind(): lax.ppermute(value, axis, [(source, source + steps) for source in range(l...]
    all_gather x0 -> x1, waiting for transfers between devices: none -> 33.3 us  [whole_field_body(): all_phase = lax.all_gather(phase, ('depth', 'row', 'col'))]
    all_gather x0 -> x1, blocking collectives: none -> 26.3 us  [whole_field_body(): all_intensity = lax.all_gather(intensity, ('row', 'col'))]
    pallas_call x0 -> x1, Pallas kernels: none -> 19.3 us  [whole_field_body(): pl.pallas_call(functools.partial(wave_kernel, sections), out_shape=(jax.S...]
    dot_general x20 -> x0, matrix products: 7.06 us -> none  [the longest x10 4.42 us: along_cols(): jnp.einsum('pqij,gqrj->gpri', matrix, window, precision=lax.Precision.HIG...]
  transfers between devices with their start and end apart: 50 -> 1, of which waited for: 40 -> 1; matrix products, arithmetic and copies ran while one was open for 0% -> 0% of each run, Pallas kernels for 0% -> 0%
where the time goes in v1:
time: 97 us; the launch traced here: 96.8 us
  waiting for transfers between devices  34 us (35%)
  blocking collectives  26.3 us (27%)
  Pallas kernels  19.3 us (20%)
  between operations  14 us (14%)
  local copies, waits for them, and re-layouts  3.04 us (3%)
    all_gather x1, waiting for transfers between devices, whole_field_body(): all_phase = lax.all_gather(phase, ('depth', 'row', 'col'))  33.3 us
    all_gather x1, blocking collectives, whole_field_body(): all_intensity = lax.all_gather(intensity, ('row', 'col'))  26.3 us
    pallas_call x1, Pallas kernels, whole_field_body(): pl.pallas_call(functools.partial(wave_kernel, sections), out_shape=(jax.S...  19.3 us
    unnamed x8, local copies, waits for them, and re-layouts  3.04 us
  transfers between devices with their start and end apart: 1, of which 1 were waited for; matrix products, arithmetic and copies ran while one was open for 0% of the time, Pallas kernels for 0%

profile of v1, /device:TPU:0, one launch (start us, length us, event | category | flops | bytes accessed | tf_op | source)
XLA Modules:
  0.0 96.8 jit_solution(8509859070758729018)
XLA Ops:
  7.2 0.0 copy-start.2
  7.2 0.0 all-gather.4.cloned.1.call-start
  7.2 0.7 all-gather.4.cloned.1.call-update
  7.9 26.3 %all-gather.1 = f32[16,64,128]{2,1,0:T(8,128)S(1)} all-gather(f32[2,64,128]{2,1,0:T(8,128)} %param.7), channel_id=3, replica_groups=mesh['depth'=4,'row'=2,'col'=4] {'row','col'}, dimensions={0}, use_global_device_ids=true | all-gather | bytes 589824 | tf_op jit(solution)/shard_map/all_gather | solution.py:256
  34.2 33.3 %all-gather.4.cloned.1.call-done = f32[32,64,128]{2,1,0:T(8,128)} async-done(((f32[1,64,128]{2,1,0:T(8,128)}), f32[32,64,128]{2,1,0:T(8,128)}) %all-gather.4.cloned.1.call-update) | async-done | bytes 1048592 | tf_op jit(solution)/shard_map/all_gather | solution.py:255
  67.6 0.0 copy-start.3
  67.6 0.0 copy-done.2
  67.6 0.7 copy-done.3
  68.3 0.0 copy-start
  68.3 1.2 %copy-done = f32[32,64,128]{2,1,0:T(8,128)S(1)} copy-done((f32[32,64,128]{2,1,0:T(8,128)S(1)}, f32[32,64,128]{2,1,0:T(8,128)}, u32[]{:S(2)}) %copy-start) | copy-done | bytes 1048600
  69.5 0.0 copy-start.1
  69.5 1.1 %copy-done.1 = bf16[1536,256]{1,0:T(8,128)(2,1)S(1)} copy-done((bf16[1536,256]{1,0:T(8,128)(2,1)S(1)}, bf16[1536,256]{1,0:T(8,128)(2,1)}, u32[]{:S(2)}) %copy-start.1) | copy-done | bytes 786456
  70.6 19.3 %shard_map.68 = (f32[1,64,128]{2,1,0:T(8,128)}, f32[2,1,2,64,128]{4,3,2,1,0:T(8,128)}) custom-call(s32[2,2]{1,0:T(2,128)S(1)} %copy-done.3, f32[32,1,64,128]{3,2,1,0:T(8,128)S(1)} %bitcast.3, f32[8,2,64,128]{3,2,1,0:T(8,128)S(1)} %bitcast.2, bf16[256,768]{1,0:T(8,128)(2,1)S(1)} %copy-done.2, bf16[1536,256]{1,0:T(8,128)(2,1)S(1)} %copy-done.1), custom_call_target="tpu_custom_call" | custom-call | tf_op jit(solution)/shard_map/pallas_call | solution.py:259
Async XLA Ops:
  7.2 60.4 %copy-start.2 = (bf16[256,768]{1,0:T(8,128)(2,1)S(1)}, bf16[256,768]{1,0:T(8,128)(2,1)}, u32[]{:S(2)}) copy-start(bf16[256,768]{1,0:T(8,128)(2,1)} %constant.4.clone.row_ref) | copy-start | bytes 1179652
  7.2 60.4 %all-gather.4.cloned.1.call-start = ((), (), s32[]{:S(2)}) async-start(), calls=%async_computation | async-start | bytes 1081344 | tf_op jit(solution)/shard_map/all_gather | solution.py:255
  67.6 0.7 copy-start.3
  68.3 1.2 %copy-start = (f32[32,64,128]{2,1,0:T(8,128)S(1)}, f32[32,64,128]{2,1,0:T(8,128)}, u32[]{:S(2)}) copy-start(f32[32,64,128]{2,1,0:T(8,128)} %all-gather.4.cloned.1.call-done) | copy-start | bytes 3145732
  69.5 1.1 %copy-start.1 = (bf16[1536,256]{1,0:T(8,128)(2,1)S(1)}, bf16[1536,256]{1,0:T(8,128)(2,1)}, u32[]{:S(2)}) copy-start(bf16[1536,256]{1,0:T(8,128)(2,1)} %constant.5.clone.col_ref) | copy-start | bytes 2359300
Sparse Core Ops, SparseCore 0:
  11.0 56.5 all-gather.3

commit v2 on v1

--- a/solution.py
+++ b/solution.py
@@ -1,4 +1,3 @@
-import functools
 import math
 
 import jax
@@ -75,7 +74,7 @@
     band = np_band(np.arange(height), np.arange(height))
     whole = np.block([[band.real, -band.imag], [band.imag, band.real]])
     high, low = np_halves(whole)
-    return np.concatenate([high, high, low], axis=1)
+    return np.concatenate([high, low], axis=1)
 
 
 def col_constant():
@@ -86,94 +85,93 @@
         band = np_band(lane, position).T
         parts.append(np.block([[band.real, band.imag], [-band.imag, band.real]]))
     high, low = np_halves(np.concatenate(parts, axis=0))
-    return np.concatenate([high, high, low], axis=0)
+    return np.concatenate([high, low], axis=0)
 
 
 def wave_kernel(
-    sections, tilt_ref, phase_ref, intensity_ref, row_ref, col_ref, grad_ref, exit_ref,
+    tilt_ref, near_ref, far_ref, row_ref, col_ref, mine_ref, theirs_ref,
     cos_ref, sin_ref, u_high, u_low, a_high, a_low, v_ref, moved_ref,
 ):
-    items, height, width = v_ref.shape[0], v_ref.shape[2], v_ref.shape[3]
-    slices, tile_r, tile_c = grad_ref.shape
-    rows, cols = height // tile_r, width // tile_c
-    count = sections * slices
+    count, height, width = cos_ref.shape
+    slices, _, tile_r, tile_c = mine_ref.shape
+    cols = width // tile_c
     blocks = width // LANES
     half = LANES // 2
+    core = lax.axis_index("row")
     first = lax.axis_index("depth") * slices
-    own_row = pl.multiple_of(lax.axis_index("row") * tile_r, tile_r)
-    own_col = pl.multiple_of(lax.axis_index("col") * tile_c, tile_c)
-    own = (pl.ds(own_row, tile_r), pl.ds(own_col, tile_c))
-
-    def store_u(item, row, col, real, imag):
+    near_row = pl.multiple_of(core * tile_r, tile_r)
+    far_row = pl.multiple_of((1 - core) * tile_r, tile_r)
+    own_col = pl.ds(pl.multiple_of(lax.axis_index("col") * tile_c, tile_c), tile_c)
+    sides = ((near_ref, near_row), (far_ref, far_row))
+
+    def store_u(row, col, real, imag):
         for part, value in enumerate((real, imag)):
             high, low = halves(value)
-            where = (item, pl.ds(part * height + row, value.shape[0]), pl.ds(col, value.shape[1]))
+            where = (pl.ds(part * height + row, value.shape[0]), pl.ds(col, value.shape[1]))
             u_high[where] = high
             u_low[where] = low
 
+    def turned(slice_index, where):
+        cos, sin = cos_ref[(slice_index,) + where], sin_ref[(slice_index,) + where]
+        real, imag = v_ref[(0,) + where], v_ref[(1,) + where]
+        return cos * real - sin * imag, cos * imag + sin * real
+
     def keep_moved(slice_index):
         @pl.when((slice_index >= first) & (slice_index < first + slices))
         def _():
-            cos, sin = cos_ref[(slice_index,) + own], sin_ref[(slice_index,) + own]
-            for item in range(items):
-                real, imag = v_ref[(item, 0) + own], v_ref[(item, 1) + own]
-                moved_ref[slice_index - first, item, 0] = cos * real - sin * imag
-                moved_ref[slice_index - first, item, 1] = cos * imag + sin * real
+            real, imag = turned(slice_index, (slice(None), own_col))
+            moved_ref[slice_index - first, 0] = real
+            moved_ref[slice_index - first, 1] = imag
 
     def transmit(slice_index):
-        for item in range(items):
-            for block in range(blocks):
-                where = (slice(None), pl.ds(block * LANES, LANES))
-                cos, sin = cos_ref[(slice_index,) + where], sin_ref[(slice_index,) + where]
-                real, imag = v_ref[(item, 0) + where], v_ref[(item, 1) + where]
-                store_u(item, 0, block * LANES, cos * real - sin * imag, cos * imag + sin * real)
+        for block in range(blocks):
+            where = (slice(None), pl.ds(block * LANES, LANES))
+            store_u(0, block * LANES, *turned(slice_index, where))
 
     def propagate():
-        for item in range(items):
-            for start in range(0, width, 2 * LANES):
-                where = (item, slice(None), pl.ds(start, 2 * LANES))
-                high, low = u_high[where], u_low[where]
-                done = jnp.dot(
-                    row_ref[...],
-                    jnp.concatenate([high, low, high], axis=0),
-                    preferred_element_type=jnp.float32,
-                )
-                for part in range(2):
-                    for sub in range(2):
-                        block = start // LANES + sub
-                        value = done[part * height : (part + 1) * height, sub * LANES : (sub + 1) * LANES]
-                        for target, piece in zip((a_high, a_low), halves(value)):
-                            target[item, block, :, pl.ds(part * LANES, LANES)] = piece
-                            if block > 0:
-                                target[item, block - 1, :, pl.ds((2 + part) * LANES, half)] = piece[:, :half]
-                            if block < blocks - 1:
-                                target[item, block + 1, :, pl.ds((2 + part) * LANES + half, half)] = piece[:, half:]
-        for item in range(items):
-            high = a_high[item].reshape(blocks * height, 4 * LANES)
-            low = a_low[item].reshape(blocks * height, 4 * LANES)
+        matrix = jnp.concatenate([row_ref[:, : 2 * height], row_ref[...]], axis=1)
+        for start in range(0, width, 2 * LANES):
+            where = (slice(None), pl.ds(start, 2 * LANES))
+            high, low = u_high[where], u_low[where]
             done = jnp.dot(
-                jnp.concatenate([high, low, high], axis=1),
-                col_ref[...],
+                matrix,
+                jnp.concatenate([high, low, high], axis=0),
                 preferred_element_type=jnp.float32,
             )
-            for block in range(blocks):
-                for part in range(2):
-                    v_ref[item, part, :, pl.ds(block * LANES, LANES)] = done[
-                        block * height : (block + 1) * height, part * LANES : (part + 1) * LANES
-                    ]
+            for part in range(2):
+                for sub in range(2):
+                    block = start // LANES + sub
+                    value = done[part * height : (part + 1) * height, sub * LANES : (sub + 1) * LANES]
+                    for target, piece in zip((a_high, a_low), halves(value)):
+                        target[block, :, pl.ds(part * LANES, LANES)] = piece
+                        if block > 0:
+                            target[block - 1, :, pl.ds((2 + part) * LANES, half)] = piece[:, :half]
+                        if block < blocks - 1:
+                            target[block + 1, :, pl.ds((2 + part) * LANES + half, half)] = piece[:, half:]
+        high = a_high[...].reshape(blocks * height, 4 * LANES)
+        low = a_low[...].reshape(blocks * height, 4 * LANES)
+        done = jnp.dot(
+            jnp.concatenate([high, low, high], axis=1),
+            jnp.concatenate([col_ref[: 4 * LANES], col_ref[...]], axis=0),
+            preferred_element_type=jnp.float32,
+        )
+        for block in range(blocks):
+            for part in range(2):
+                v_ref[part, :, pl.ds(block * LANES, LANES)] = done[
+                    block * height : (block + 1) * height, part * LANES : (part + 1) * LANES
+                ]
 
     for target in (a_high, a_low):
-        for item in range(items):
-            for part in range(2):
-                target[item, 0, :, pl.ds((2 + part) * LANES + half, half)] = jnp.zeros((height, half), jnp.bfloat16)
-                target[item, blocks - 1, :, pl.ds((2 + part) * LANES, half)] = jnp.zeros((height, half), jnp.bfloat16)
+        for part in range(2):
+            target[0, :, pl.ds((2 + part) * LANES + half, half)] = jnp.zeros((height, half), jnp.bfloat16)
+            target[blocks - 1, :, pl.ds((2 + part) * LANES, half)] = jnp.zeros((height, half), jnp.bfloat16)
 
     def screens(slice_index, carry):
         section, inner = slice_index // slices, slice_index % slices
-        for row in range(rows):
+        for side_ref, row in sides:
             for col in range(cols):
-                cos, sin = cos_sin(phase_ref[section * (rows * cols) + row * cols + col, inner])
-                where = (slice_index, pl.ds(row * tile_r, tile_r), pl.ds(col * tile_c, tile_c))
+                cos, sin = cos_sin(side_ref[(section * cols + col) * slices + inner])
+                where = (slice_index, pl.ds(row, tile_r), pl.ds(col * tile_c, tile_c))
                 cos_ref[where] = cos
                 sin_ref[where] = sin
         return carry
@@ -184,20 +182,19 @@
         fraction = (number * position).astype(jnp.float32) / extent
         return turn(fraction - jnp.round(fraction))
 
-    for item in range(items):
-        row_cos, row_sin = cycles(
-            tilt_ref[item, 0], lax.broadcasted_iota(jnp.int32, (height, LANES), 0), float(height)
-        )
-        for block in range(blocks):
-            col_cos, col_sin = cycles(
-                tilt_ref[item, 1],
-                lax.broadcasted_iota(jnp.int32, (8, LANES), 1) + block * LANES,
-                float(width),
-            )
-            col_cos, col_sin = col_cos[:1], col_sin[:1]
-            where = (slice(None), pl.ds(block * LANES, LANES))
-            v_ref[(item, 0) + where] = row_cos * col_cos - row_sin * col_sin
-            v_ref[(item, 1) + where] = row_sin * col_cos + row_cos * col_sin
+    row_cos, row_sin = cycles(
+        tilt_ref[core, 0], lax.broadcasted_iota(jnp.int32, (height, LANES), 0), float(height)
+    )
+    for block in range(blocks):
+        col_cos, col_sin = cycles(
+            tilt_ref[core, 1],
+            lax.broadcasted_iota(jnp.int32, (8, LANES), 1) + block * LANES,
+            float(width),
+        )
+        col_cos, col_sin = col_cos[:1], col_sin[:1]
+        where = (slice(None), pl.ds(block * LANES, LANES))
+        v_ref[(0,) + where] = row_cos * col_cos - row_sin * col_sin
+        v_ref[(1,) + where] = row_sin * col_cos + row_cos * col_sin
     transmit(0)
     keep_moved(0)
 
@@ -206,31 +203,30 @@
 
         @pl.when((tick >= first) & (tick < first + slices))
         def _():
-            for item in range(items):
+            for target, row in ((mine_ref, near_row), (theirs_ref, far_row)):
                 for part in range(2):
-                    exit_ref[item, tick - first, part] = v_ref[(item, part) + own]
+                    target[tick - first, part] = v_ref[part, pl.ds(row, tile_r), own_col]
 
         @pl.when(tick == count - 1)
         def _():
-            for item in range(items):
-                for row in range(rows):
-                    for col in range(cols):
-                        where = (pl.ds(row * tile_r, tile_r), pl.ds(col * tile_c, tile_c))
-                        real, imag = v_ref[(item, 0) + where], v_ref[(item, 1) + where]
-                        misfit = 2.0 * (real * real + imag * imag - intensity_ref[row * cols + col, item])
-                        store_u(item, row * tile_r, col * tile_c, misfit * real, -misfit * imag)
+            for side_ref, row in sides:
+                for col in range(cols):
+                    where = (pl.ds(row, tile_r), pl.ds(col * tile_c, tile_c))
+                    real, imag = v_ref[(0,) + where], v_ref[(1,) + where]
+                    misfit = 2.0 * (real * real + imag * imag - side_ref[count * cols + col])
+                    store_u(row, col * tile_c, misfit * real, -misfit * imag)
 
         back = 2 * count - 1 - tick
 
         @pl.when((tick >= count) & (back < first + slices))
         def _():
-            total = jnp.zeros((tile_r, tile_c), jnp.float32)
-            for item in range(items):
-                real, imag = v_ref[(item, 0) + own], v_ref[(item, 1) + own]
-                total = total - (
-                    imag * moved_ref[back - first, item, 0] + real * moved_ref[back - first, item, 1]
+            for target, row in ((mine_ref, near_row), (theirs_ref, far_row)):
+                where = (pl.ds(row, tile_r), own_col)
+                here = (pl.ds(row, tile_r), slice(None))
+                real, imag = v_ref[(0,) + where], v_ref[(1,) + where]
+                target[back - first, 2] = -(
+                    imag * moved_ref[(back - first, 0) + here] + real * moved_ref[(back - first, 1) + here]
                 )
-            grad_ref[back - first] = total
 
         @pl.when((tick != count - 1) & (back > first))
         def _():
@@ -245,37 +241,54 @@
     lax.fori_loop(0, 2 * count - first, step, 0)
 
 
-def whole_field_body(sections, phase, tilt, intensity):
+def spread(shard, axis):
+    size = lax.axis_size(axis)
+    return lax.all_to_all(jnp.broadcast_to(shard[None], (size,) + shard.shape), axis, 0, 0)
+
+
+def swap_cores(value):
+    return lax.ppermute(value, "row", [(0, 1), (1, 0)])
+
+
+def whole_field_body(phase, tilt, intensity):
     slices, tile_r, tile_c = phase.shape
-    items = tilt.shape[0]
+    sections, cols = lax.axis_size("depth"), lax.axis_size("col")
+    core = lax.axis_index("row")
     height = tile_r * lax.axis_size("row")
-    width = tile_c * lax.axis_size("col")
+    width = tile_c * cols
     count = sections * slices
     blocks = width // LANES
-    all_phase = lax.all_gather(phase, ("depth", "row", "col"))
-    all_intensity = lax.all_gather(intensity, ("row", "col"))
+    plane = spread(jnp.concatenate([phase, intensity], axis=0), "col")
+    near_phase = spread(plane[:, :slices], "depth").reshape(count * cols, tile_r, tile_c)
+
+    def packed(item):
+        chosen = lax.dynamic_index_in_dim(plane, slices + item, 1, keepdims=False)
+        return jnp.concatenate([near_phase, chosen], axis=0)
+
+    near, far = packed(core), swap_cores(packed(1 - core))
     vmem = pl.BlockSpec(memory_space=pltpu.VMEM)
-    field = (items, 2, height, width)
-    gradient, leaving = pl.pallas_call(
-        functools.partial(wave_kernel, sections),
-        out_shape=(
-            jax.ShapeDtypeStruct(phase.shape, jnp.float32),
-            jax.ShapeDtypeStruct((items, slices, 2, tile_r, tile_c), jnp.float32),
-        ),
+    result = jax.ShapeDtypeStruct((slices, 3, tile_r, tile_c), jnp.float32)
+    mine, theirs = pl.pallas_call(
+        wave_kernel,
+        out_shape=(result, result),
         in_specs=[pl.BlockSpec(memory_space=pltpu.SMEM), vmem, vmem, vmem, vmem],
         out_specs=(vmem, vmem),
         scratch_shapes=[
             pltpu.VMEM((count, height, width), jnp.float32),
             pltpu.VMEM((count, height, width), jnp.float32),
-            pltpu.VMEM((items, 2 * height, width), jnp.bfloat16),
-            pltpu.VMEM((items, 2 * height, width), jnp.bfloat16),
-            pltpu.VMEM((items, blocks, height, 4 * LANES), jnp.bfloat16),
-            pltpu.VMEM((items, blocks, height, 4 * LANES), jnp.bfloat16),
-            pltpu.VMEM(field, jnp.float32),
-            pltpu.VMEM((slices, items, 2, tile_r, tile_c), jnp.float32),
+            pltpu.VMEM((2 * height, width), jnp.bfloat16),
+            pltpu.VMEM((2 * height, width), jnp.bfloat16),
+            pltpu.VMEM((blocks, height, 4 * LANES), jnp.bfloat16),
+            pltpu.VMEM((blocks, height, 4 * LANES), jnp.bfloat16),
+            pltpu.VMEM((2, height, width), jnp.float32),
+            pltpu.VMEM((slices, 2, height, tile_c), jnp.float32),
         ],
-        compiler_params=pltpu.CompilerParams(vmem_limit_bytes=40 * 2**20),
-    )(tilt, all_phase, all_intensity, jnp.asarray(row_constant(height)), jnp.asarray(col_constant()))
+        compiler_params=pltpu.CompilerParams(vmem_limit_bytes=24 * 2**20),
+    )(tilt, near, far, jnp.asarray(row_constant(height)), jnp.asarray(col_constant()))
+    received = swap_cores(theirs)
+    gradient = mine[:, 2] + received[:, 2]
+    waves = (mine[:, :2], received[:, :2])
+    leaving = jnp.stack([jnp.where(core == 0, waves[0], waves[1]), jnp.where(core == 0, waves[1], waves[0])])
     return gradient, leaving
 
 
@@ -453,6 +466,7 @@
     bytes_all = 4 * height * width * (slices + batch)
     return (
         bytes_all <= GATHER_BUDGET
+        and batch == rows == 2
         and height == LANES
         and (height // rows) % 16 == 0
         and (width // cols) % LANES == 0
@@ -465,7 +479,7 @@
 
     def run(phase, tilt, intensity):
         if fits_whole(phase.shape, tilt.shape[0], mesh):
-            body = functools.partial(whole_field_body, mesh.shape["depth"])
+            body = whole_field_body
         else:
             body = staged_body
         return jax.shard_map(

time: 97 us -> 48.8 us (0.50)
  waiting for transfers between devices: 34 us -> 9.86 us
  between operations: 14 us -> 0.69 us
  blocking collectives: 26.3 us -> 18 us
  Pallas kernels: 19.3 us -> 11.4 us
  starting transfers between devices: 0.04 us -> 5.43 us
  other arithmetic: 0 us -> 2.25 us
  local copies, waits for them, and re-layouts: 3.04 us -> 0.87 us
    all_gather x1 -> x0, waiting for transfers between devices: 33.3 us -> none  [whole_field_body(): all_phase = lax.all_gather(phase, ('depth', 'row', 'col'))]
    all_gather x1 -> x0, blocking collectives: 26.3 us -> none  [whole_field_body(): all_intensity = lax.all_gather(intensity, ('row', 'col'))]
    all_to_all x0 -> x1, blocking collectives: none -> 18 us  [spread(): lax.all_to_all(jnp.broadcast_to(shard[None], (size,) + shard.shape), axis...]
    pallas_call x1, Pallas kernels: 19.3 us -> 11.4 us  [whole_field_body(): pl.pallas_call(wave_kernel, out_shape=(result, result), in_specs=[pl.Bloc...]
    all_to_all x0 -> x1, waiting for transfers between devices: none -> 6.61 us  [spread(): lax.all_to_all(jnp.broadcast_to(shard[None], (size,) + shard.shape), axis...]
    all_to_all x0 -> x1, starting transfers between devices: none -> 5.16 us  [spread(): lax.all_to_all(jnp.broadcast_to(shard[None], (size,) + shard.shape), axis...]
    ppermute x0 -> x2, waiting for transfers between devices: none -> 3.25 us  [swap_cores(): return lax.ppermute(value, 'row', [(0, 1), (1, 0)])]
    unnamed x8 -> x6, local copies, waits for them, and re-layouts: 3.04 us -> 0.01 us
  transfers between devices with their start and end apart: 1 -> 3, of which waited for: 1 -> 3; matrix products, arithmetic and copies ran while one was open for 0% -> 0% of each run, Pallas kernels for 0% -> 0%
where the time goes in v2:
time: 48.8 us; the launch traced here: 48.5 us
  blocking collectives  18 us (37%)
  Pallas kernels  11.4 us (23%)
  waiting for transfers between devices  9.86 us (20%)
  starting transfers between devices  5.43 us (11%)
  other arithmetic  2.25 us (5%)
  local copies, waits for them, and re-layouts  0.87 us (2%)
  between operations  0.69 us (1%)
    all_to_all x1, blocking collectives, spread(): lax.all_to_all(jnp.broadcast_to(shard[None], (size,) + shard.shape), axis...  18 us
    pallas_call x1, Pallas kernels, whole_field_body(): pl.pallas_call(wave_kernel, out_shape=(result, result), in_specs=[pl.Bloc...  11.4 us
    all_to_all x1, waiting for transfers between devices, spread(): lax.all_to_all(jnp.broadcast_to(shard[None], (size,) + shard.shape), axis...  6.61 us
    all_to_all x1, starting transfers between devices, spread(): lax.all_to_all(jnp.broadcast_to(shard[None], (size,) + shard.shape), axis...  5.16 us
    ppermute x2, waiting for transfers between devices, swap_cores(): return lax.ppermute(value, 'row', [(0, 1), (1, 0)])  3.25 us
  transfers between devices with their start and end apart: 3, of which 3 were waited for; matrix products, arithmetic and copies ran while one was open for 0% of the time, Pallas kernels for 0%

profile of v2, /device:TPU:0, one launch (start us, length us, event | category | flops | bytes accessed | tf_op | source)
XLA Modules:
  0.0 48.5 jit_solution(13700725489271784237)
XLA Ops:
  0.6 0.8 %pad_maximum_fusion.3 = f32[3,64,128]{2,1,0:T(8,128)S(1)} fusion(f32[2,64,128]{2,1,0:T(8,128)} %param.7, f32[1,64,128]{2,1,0:T(8,128)} %param.5), kind=kLoop, calls=%fused_computation.6 | loop fusion | flops 24576 | bytes 196608 | tf_op jit(solution)/shard_map/concatenate | solution.py:261
  1.5 0.8 %broadcast_in_dim.6 = f32[4,3,64,128]{3,2,1,0:T(8,128)} broadcast(f32[3,64,128]{2,1,0:T(8,128)S(1)} %pad_maximum_fusion.3), dimensions={1,2,3} | broadcast | bytes 491520 | tf_op jit(solution)/shard_map/broadcast_in_dim | solution.py:246
  2.3 5.2 %all-to-all-start = ((f32[4,3,64,128]{3,2,1,0:T(8,128)}), f32[4,3,64,128]{3,2,1,0:T(8,128)S(1)}, u32[]{:S(2)}, u32[]{:S(2)}) async-start(f32[4,3,64,128]{3,2,1,0:T(8,128)} %broadcast_in_dim.6), calls=%async_computation | async-start | bytes 786432 | tf_op jit(solution)/shard_map/all_to_all | solution.py:246
  7.4 6.6 %all-to-all-done = f32[4,3,64,128]{3,2,1,0:T(8,128)S(1)} async-done(((f32[4,3,64,128]{3,2,1,0:T(8,128)}), f32[4,3,64,128]{3,2,1,0:T(8,128)S(1)}, u32[]{:S(2)}, u32[]{:S(2)}) %all-to-all-start) | async-done | bytes 393248 | tf_op jit(solution)/shard_map/all_to_all | solution.py:246
  14.1 18.0 %all_to_all.10 = f32[4,4,1,64,128]{4,3,1,2,0:T(8,128)S(1)} all-to-all(f32[4,4,1,64,128]{4,3,1,2,0:T(8,128)S(1)} %broadcast_in_dim.16), channel_id=1, replica_groups=mesh['depth'=4,'row'=2,'col'=4] {'depth'}, dimensions={0} | all-to-all | bytes 1048576 | tf_op jit(solution)/shard_map/all_to_all | solution.py:246
  32.1 0.0 copy-start
  32.1 0.0 copy-start.1
  32.1 0.1 pad_maximum_fusion
  32.3 0.0 copy-start.2
  32.3 0.1 collective-permute-start
  32.3 2.1 %collective-permute-done.far_ref = f32[20,64,128]{2,1,0:T(8,128)S(1)} collective-permute-done((f32[20,64,128]{2,1,0:T(8,128)S(1)}, f32[20,64,128]{2,1,0:T(8,128)S(1)}, u32[]{:S(2)}, u32[]{:S(2)}) %collective-permute-start) | collective-permute-done | bytes 655392 | tf_op jit(solution)/shard_map/ppermute | solution.py:250
  34.4 0.0 copy-done
  34.4 0.0 copy-done.1
  34.4 0.0 copy-done.2
  34.4 11.4 %shard_map.68 = (f32[1,3,64,128]{3,2,1,0:T(8,128)S(1)}, f32[1,3,64,128]{3,2,1,0:T(8,128)S(1)}) custom-call(s32[2,2]{1,0:T(2,128)S(1)} %copy-done.2, f32[20,64,128]{2,1,0:T(8,128)S(1)} %get-tuple-element.7.near_ref, f32[20,64,128]{2,1,0:T(8,128)S(1)} %collective-permute-done.far_ref, bf16[256,512]{1,0:T(8,128)(2,1)S(1)} %copy-done.1, ...), custom_call_target="tpu_custom_call" | custom-call | tf_op jit(solution)/shard_map/pallas_call | solution.py:271
  45.9 0.2 collective-permute-start.1
  46.0 1.2 %collective-permute-done.1 = f32[1,3,64,128]{3,2,1,0:T(8,128)S(1)} collective-permute-done((f32[1,3,64,128]{3,2,1,0:T(8,128)S(1)}, f32[1,3,64,128]{3,2,1,0:T(8,128)S(1)}, u32[]{:S(2)}, u32[]{:S(2)}) %collective-permute-start.1) | collective-permute-done | bytes 98336 | tf_op jit(solution)/shard_map/ppermute | solution.py:250
  47.2 0.7 %pad_maximum_fusion.2 = f32[2,1,2,64,128]{4,3,2,1,0:T(8,128)} fusion(f32[1,1,2,64,128]{4,3,2,1,0:T(8,128)S(1)} %get-tuple-element.12, f32[1,1,2,64,128]{4,3,2,1,0:T(8,128)S(1)} %get-tuple-element.11), kind=kLoop, calls=%fused_computation.3 | loop fusion | flops 32768 | bytes 262144 | tf_op jit(solution)/shard_map/stack | solution.py:291
  47.9 0.6 %fusion = f32[1,64,128]{2,1,0:T(8,128)} fusion(f32[1,3,64,128]{3,2,1,0:T(8,128)S(1)} %collective-permute-done.1, f32[1,3,64,128]{3,2,1,0:T(8,128)S(1)} %get-tuple-element.4), kind=kLoop, calls=%fused_computation.10 | loop fusion | flops 8192 | bytes 98304 | tf_op jit(solution)/shard_map/add | solution.py:289
  (3 shorter events, 0.1 us)
Async XLA Ops:
  2.3 11.8 %all-to-all-start = ((f32[4,3,64,128]{3,2,1,0:T(8,128)}), f32[4,3,64,128]{3,2,1,0:T(8,128)S(1)}, u32[]{:S(2)}, u32[]{:S(2)}) async-start(f32[4,3,64,128]{3,2,1,0:T(8,128)} %broadcast_in_dim.6), calls=%async_computation | async-start | bytes 786432 | tf_op jit(solution)/shard_map/all_to_all | solution.py:246
  32.1 2.3 %copy-start = (bf16[1024,256]{1,0:T(8,128)(2,1)S(1)}, bf16[1024,256]{1,0:T(8,128)(2,1)}, u32[]{:S(2)}) copy-start(bf16[1024,256]{1,0:T(8,128)(2,1)} %constant.27.clone.col_ref) | copy-start | bytes 1572868
  32.1 2.3 %copy-start.1 = (bf16[256,512]{1,0:T(8,128)(2,1)S(1)}, bf16[256,512]{1,0:T(8,128)(2,1)}, u32[]{:S(2)}) copy-start(bf16[256,512]{1,0:T(8,128)(2,1)} %constant.26.clone.row_ref) | copy-start | bytes 786436
  32.3 2.2 %copy-start.2 = (s32[2,2]{1,0:T(2,128)S(1)}, s32[2,2]{1,0:T(2,128)}, u32[]{:S(2)}) copy-start(s32[2,2]{1,0:T(2,128)} %tilt_ref.1) | copy-start | bytes 52
  32.3 2.2 %collective-permute-start = (f32[20,64,128]{2,1,0:T(8,128)S(1)}, f32[20,64,128]{2,1,0:T(8,128)S(1)}, u32[]{:S(2)}, u32[]{:S(2)}) collective-permute-start(f32[20,64,128]{2,1,0:T(8,128)S(1)} %get-tuple-element.6), channel_id=1, source_target_pairs={{0,4},{4,0},{1,5},{5,1},{2,6},{6,2},{3,7},{7,3},{8,12},{12,8},{9,1... | collective-permute-start | bytes 1966088 | tf_op jit(solution)/shard_map/ppermute | solution.py:250
  45.9 1.4 %collective-permute-start.1 = (f32[1,3,64,128]{3,2,1,0:T(8,128)S(1)}, f32[1,3,64,128]{3,2,1,0:T(8,128)S(1)}, u32[]{:S(2)}, u32[]{:S(2)}) collective-permute-start(f32[1,3,64,128]{3,2,1,0:T(8,128)S(1)} %get-tuple-element.5), channel_id=1, source_target_pairs={{0,4},{4,0},{1,5},{5,1},{2,6},{6,2},{3,7},{7,3},{8,12},{12,8},{9,1... | collective-permute-start | bytes 294920 | tf_op jit(solution)/shard_map/ppermute | solution.py:250

commit v3 on v2

--- a/solution.py
+++ b/solution.py
@@ -103,6 +103,7 @@
     far_row = pl.multiple_of((1 - core) * tile_r, tile_r)
     own_col = pl.ds(pl.multiple_of(lax.axis_index("col") * tile_c, tile_c), tile_c)
     sides = ((near_ref, near_row), (far_ref, far_row))
+    own_section, own_place = lax.axis_index("depth"), lax.axis_index("col")
 
     def store_u(row, col, real, imag):
         for part, value in enumerate((real, imag)):
@@ -167,10 +168,10 @@
             target[blocks - 1, :, pl.ds((2 + part) * LANES, half)] = jnp.zeros((height, half), jnp.bfloat16)
 
     def screens(slice_index, carry):
-        section, inner = slice_index // slices, slice_index % slices
+        held = ((slice_index // slices) ^ own_section) * slices + slice_index % slices
         for side_ref, row in sides:
             for col in range(cols):
-                cos, sin = cos_sin(side_ref[(section * cols + col) * slices + inner])
+                cos, sin = cos_sin(side_ref[(col ^ own_place) * count + held])
                 where = (slice_index, pl.ds(row, tile_r), pl.ds(col * tile_c, tile_c))
                 cos_ref[where] = cos
                 sin_ref[where] = sin
@@ -213,7 +214,7 @@
                 for col in range(cols):
                     where = (pl.ds(row, tile_r), pl.ds(col * tile_c, tile_c))
                     real, imag = v_ref[(0,) + where], v_ref[(1,) + where]
-                    misfit = 2.0 * (real * real + imag * imag - side_ref[count * cols + col])
+                    misfit = 2.0 * (real * real + imag * imag - side_ref[count * cols + (col ^ own_place)])
                     store_u(row, col * tile_c, misfit * real, -misfit * imag)
 
         back = 2 * count - 1 - tick
@@ -243,7 +244,10 @@
 
 def spread(shard, axis):
     size = lax.axis_size(axis)
-    return lax.all_to_all(jnp.broadcast_to(shard[None], (size,) + shard.shape), axis, 0, 0)
+    pieces = [shard]
+    for bits in range(1, size):
+        pieces.append(lax.ppermute(shard, axis, [(i, i ^ bits) for i in range(size)]))
+    return jnp.stack(pieces)
 
 
 def swap_cores(value):
@@ -258,11 +262,12 @@
     width = tile_c * cols
     count = sections * slices
     blocks = width // LANES
-    plane = spread(jnp.concatenate([phase, intensity], axis=0), "col")
-    near_phase = spread(plane[:, :slices], "depth").reshape(count * cols, tile_r, tile_c)
+    column = spread(phase, "depth").reshape(count, tile_r, tile_c)
+    near_intensity = spread(intensity, "col")
+    near_phase = spread(column, "col").reshape(cols * count, tile_r, tile_c)
 
     def packed(item):
-        chosen = lax.dynamic_index_in_dim(plane, slices + item, 1, keepdims=False)
+        chosen = lax.dynamic_index_in_dim(near_intensity, item, 1, keepdims=False)
         return jnp.concatenate([near_phase, chosen], axis=0)
 
     near, far = packed(core), swap_cores(packed(1 - core))
@@ -462,11 +467,13 @@
 
 def fits_whole(phase_shape, batch, mesh):
     slices, height, width = phase_shape
-    rows, cols = mesh.shape["row"], mesh.shape["col"]
+    rows, cols, sections = mesh.shape["row"], mesh.shape["col"], mesh.shape["depth"]
     bytes_all = 4 * height * width * (slices + batch)
     return (
         bytes_all <= GATHER_BUDGET
         and batch == rows == 2
+        and cols & (cols - 1) == 0
+        and sections & (sections - 1) == 0
         and height == LANES
         and (height // rows) % 16 == 0
         and (width // cols) % LANES == 0

time: 48.8 us -> 37.1 us (0.76)
  blocking collectives: 18 us -> 0 us
  starting transfers between devices: 5.43 us -> 13 us
  local copies, waits for them, and re-layouts: 0.87 us -> 0.05 us
    all_to_all x1 -> x0, blocking collectives: 18 us -> none  [spread(): lax.all_to_all(jnp.broadcast_to(shard[None], (size,) + shard.shape), axis...]
    ppermute x0 -> x9, starting transfers between devices: none -> 12.7 us  [spread(): lax.ppermute(shard, axis, [(i, i ^ bits) for i in range(size)])]
    all_to_all x1 -> x0, waiting for transfers between devices: 6.61 us -> none  [spread(): lax.all_to_all(jnp.broadcast_to(shard[None], (size,) + shard.shape), axis...]
    ppermute x0 -> x9, waiting for transfers between devices: none -> 6.24 us  [spread(): lax.ppermute(shard, axis, [(i, i ^ bits) for i in range(size)])]
    all_to_all x1 -> x0, starting transfers between devices: 5.16 us -> none  [spread(): lax.all_to_all(jnp.broadcast_to(shard[None], (size,) + shard.shape), axis...]
    another operation x0 -> x3, other arithmetic: none -> 0.87 us  [spread(): return jnp.stack(pieces)]
    concatenate x1 -> x0, other arithmetic: 0.85 us -> none  [whole_field_body(): plane = spread(jnp.concatenate([phase, intensity], axis=0), 'col')]
    broadcast_in_dim x2 -> x0, local copies, waits for them, and re-layouts: 0.83 us -> none  [spread(): jnp.broadcast_to(shard[None], (size,) + shard.shape)]
  transfers between devices with their start and end apart: 3 -> 11, of which waited for: 3 -> 6; matrix products, arithmetic and copies ran while one was open for 0% -> 2% of each run, Pallas kernels for 0% -> 0%
where the time goes in v3:
time: 37.1 us; the launch traced here: 37 us
  starting transfers between devices  13 us (35%)
  Pallas kernels  11.4 us (31%)
  waiting for transfers between devices  9.5 us (26%)
  other arithmetic  2.27 us (6%)
  between operations  0.72 us (2%)
    ppermute x9, starting transfers between devices, spread(): lax.ppermute(shard, axis, [(i, i ^ bits) for i in range(size)])  12.7 us
    pallas_call x1, Pallas kernels, whole_field_body(): pl.pallas_call(wave_kernel, out_shape=(result, result), in_specs=[pl.Bloc...  11.4 us
    ppermute x9, waiting for transfers between devices, spread(): lax.ppermute(shard, axis, [(i, i ^ bits) for i in range(size)])  6.24 us
    ppermute x2, waiting for transfers between devices, swap_cores(): return lax.ppermute(value, 'row', [(0, 1), (1, 0)])  3.25 us
    another operation x3, other arithmetic, spread(): return jnp.stack(pieces)  0.87 us
  transfers between devices with their start and end apart: 11, of which 6 were waited for; matrix products, arithmetic and copies ran while one was open for 2% of the time, Pallas kernels for 0%

profile of v3, /device:TPU:0, one launch (start us, length us, event | category | flops | bytes accessed | tf_op | source)
XLA Modules:
  0.0 37.0 jit_solution(7200266623638452584)
XLA Ops:
  0.6 3.1 %collective-permute-start = (f32[1,64,128]{2,1,0:T(8,128)}, f32[1,64,128]{2,1,0:T(8,128)S(1)}, u32[]{:S(2)}, u32[]{:S(2)}) collective-permute-start(f32[1,64,128]{2,1,0:T(8,128)} %param.5), channel_id=1, source_target_pairs={{0,8},{8,0},{16,24},{24,16},{1,9},{9,1},{17,25},{25,17},{2,10},{10... | collective-permute-start | bytes 98312 | tf_op jit(solution)/shard_map/ppermute | solution.py:249
  3.7 2.5 %collective-permute-start.2 = (f32[1,64,128]{2,1,0:T(8,128)}, f32[1,64,128]{2,1,0:T(8,128)S(1)}, u32[]{:S(2)}, u32[]{:S(2)}) collective-permute-start(f32[1,64,128]{2,1,0:T(8,128)} %param.5), channel_id=1, source_target_pairs={{0,24},{8,16},{16,8},{24,0},{1,25},{9,17},{17,9},{25,1},{2,26},{10... | collective-permute-start | bytes 98312 | tf_op jit(solution)/shard_map/ppermute | solution.py:249
  6.2 0.1 collective-permute-start.1
  6.3 1.5 %collective-permute-start.6 = (f32[2,64,128]{2,1,0:T(8,128)}, f32[2,64,128]{2,1,0:T(8,128)S(1)}, u32[]{:S(2)}, u32[]{:S(2)}) collective-permute-start(f32[2,64,128]{2,1,0:T(8,128)} %param.7), channel_id=1, source_target_pairs={{0,1},{1,0},{2,3},{3,2},{4,5},{5,4},{6,7},{7,6},{8,9},{9,8},{10,11... | collective-permute-start | bytes 196616 | tf_op jit(solution)/shard_map/ppermute | solution.py:249
  7.8 1.5 %collective-permute-start.8 = (f32[2,64,128]{2,1,0:T(8,128)}, f32[2,64,128]{2,1,0:T(8,128)S(1)}, u32[]{:S(2)}, u32[]{:S(2)}) collective-permute-start(f32[2,64,128]{2,1,0:T(8,128)} %param.7), channel_id=1, source_target_pairs={{0,3},{1,2},{2,1},{3,0},{4,7},{5,6},{6,5},{7,4},{8,11},{9,10},{10,... | collective-permute-start | bytes 196616 | tf_op jit(solution)/shard_map/ppermute | solution.py:249
  9.3 0.0 collective-permute-done
  9.3 0.5 %collective-permute-start.7 = (f32[2,64,128]{2,1,0:T(8,128)}, f32[2,64,128]{2,1,0:T(8,128)S(1)}, u32[]{:S(2)}, u32[]{:S(2)}) collective-permute-start(f32[2,64,128]{2,1,0:T(8,128)} %param.7), channel_id=1, source_target_pairs={{0,2},{1,3},{2,0},{3,1},{4,6},{5,7},{6,4},{7,5},{8,10},{9,11},{10,... | collective-permute-start | bytes 196616 | tf_op jit(solution)/shard_map/ppermute | solution.py:249
  9.8 0.3 collective-permute-done.2
  10.1 1.5 %collective-permute-done.1 = f32[1,64,128]{2,1,0:T(8,128)S(1)} collective-permute-done((f32[1,64,128]{2,1,0:T(8,128)}, f32[1,64,128]{2,1,0:T(8,128)S(1)}, u32[]{:S(2)}, u32[]{:S(2)}) %collective-permute-start.1) | collective-permute-done | bytes 32800 | tf_op jit(solution)/shard_map/ppermute | solution.py:249
  11.6 0.0 copy-start.3
  11.6 0.8 %fusion.1 = (f32[1,4,64,128]{3,2,1,0:T(8,128)S(1)}, f32[4,64,128]{2,1,0:T(8,128)S(1)}) fusion(f32[1,1,64,128]{3,2,1,0:T(8,128)S(1)} %bitcast.36, f32[1,1,64,128]{3,2,1,0:T(8,128)S(1)} %bitcast.37, f32[1,1,64,128]{3,2,1,0:T(8,128)S(1)} %bitcast.35, f32[1,1,64,128]{3,2,1,0:T(8,128)} %bitcast.34), kind=kLoop, calls=%fused_computation.9 | loop fusion | flops 98304 | bytes 393216 | tf_op jit(solution)/shard_map/stack;reshape | solution.py:250
  12.4 2.5 %collective-permute-start.5 = (f32[4,64,128]{2,1,0:T(8,128)S(1)}, f32[4,64,128]{2,1,0:T(8,128)S(1)}, u32[]{:S(2)}, u32[]{:S(2)}) collective-permute-start(f32[4,64,128]{2,1,0:T(8,128)S(1)} %get-tuple-element.13), channel_id=1, source_target_pairs={{0,3},{1,2},{2,1},{3,0},{4,7},{5,6},{6,5},{7,4},{8,11},{9,10},{10,... | collective-permute-start | bytes 393224 | tf_op jit(solution)/shard_map/ppermute | solution.py:249
  14.9 0.5 %collective-permute-start.4 = (f32[4,64,128]{2,1,0:T(8,128)S(1)}, f32[4,64,128]{2,1,0:T(8,128)S(1)}, u32[]{:S(2)}, u32[]{:S(2)}) collective-permute-start(f32[4,64,128]{2,1,0:T(8,128)S(1)} %get-tuple-element.13), channel_id=1, source_target_pairs={{0,2},{1,3},{2,0},{3,1},{4,6},{5,7},{6,4},{7,5},{8,10},{9,11},{10,... | collective-permute-start | bytes 393224 | tf_op jit(solution)/shard_map/ppermute | solution.py:249
  15.4 0.0 collective-permute-done.6
  15.4 0.5 %collective-permute-start.3 = (f32[4,64,128]{2,1,0:T(8,128)S(1)}, f32[4,64,128]{2,1,0:T(8,128)S(1)}, u32[]{:S(2)}, u32[]{:S(2)}) collective-permute-start(f32[4,64,128]{2,1,0:T(8,128)S(1)} %get-tuple-element.13), channel_id=1, source_target_pairs={{0,1},{1,0},{2,3},{3,2},{4,5},{5,4},{6,7},{7,6},{8,9},{9,8},{10,11... | collective-permute-start | bytes 393224 | tf_op jit(solution)/shard_map/ppermute | solution.py:249
  15.9 0.0 collective-permute-done.8
  15.9 0.0 collective-permute-done.7
  15.9 0.0 copy-done.3
  16.0 3.7 %collective-permute-done.5 = f32[4,64,128]{2,1,0:T(8,128)S(1)} collective-permute-done((f32[4,64,128]{2,1,0:T(8,128)S(1)}, f32[4,64,128]{2,1,0:T(8,128)S(1)}, u32[]{:S(2)}, u32[]{:S(2)}) %collective-permute-start.5) | collective-permute-done | bytes 131104 | tf_op jit(solution)/shard_map/ppermute | solution.py:249
  19.7 0.8 %collective-permute-done.4 = f32[4,64,128]{2,1,0:T(8,128)S(1)} collective-permute-done((f32[4,64,128]{2,1,0:T(8,128)S(1)}, f32[4,64,128]{2,1,0:T(8,128)S(1)}, u32[]{:S(2)}, u32[]{:S(2)}) %collective-permute-start.4) | collective-permute-done | bytes 131104 | tf_op jit(solution)/shard_map/ppermute | solution.py:249
  20.5 0.0 collective-permute-done.3
  20.5 0.0 copy-start
  20.5 0.0 copy-start.1
  20.6 0.1 pad_maximum_fusion
  20.7 0.0 copy-start.2
  20.7 0.1 collective-permute-start.9
  20.8 2.1 %collective-permute-done.9.far_ref = f32[20,64,128]{2,1,0:T(8,128)S(1)} collective-permute-done((f32[20,64,128]{2,1,0:T(8,128)S(1)}, f32[20,64,128]{2,1,0:T(8,128)S(1)}, u32[]{:S(2)}, u32[]{:S(2)}) %collective-permute-start.9) | collective-permute-done | bytes 655392 | tf_op jit(solution)/shard_map/ppermute | solution.py:254
  22.8 0.0 copy-done
  22.8 0.0 copy-done.1
  22.8 0.0 copy-done.2
  22.9 11.4 %shard_map.68 = (f32[1,3,64,128]{3,2,1,0:T(8,128)S(1)}, f32[1,3,64,128]{3,2,1,0:T(8,128)S(1)}) custom-call(s32[2,2]{1,0:T(2,128)S(1)} %copy-done.2, f32[20,64,128]{2,1,0:T(8,128)S(1)} %get-tuple-element.7.near_ref, f32[20,64,128]{2,1,0:T(8,128)S(1)} %collective-permute-done.9.far_ref, bf16[256,512]{1,0:T(8,128)(2,1)S(1)} %copy-done.1, ...), custom_call_target="tpu_custom_call" | custom-call | tf_op jit(solution)/shard_map/pallas_call | solution.py:276
  34.3 0.2 collective-permute-start.10
  34.5 1.2 %collective-permute-done.10 = f32[1,3,64,128]{3,2,1,0:T(8,128)S(1)} collective-permute-done((f32[1,3,64,128]{3,2,1,0:T(8,128)S(1)}, f32[1,3,64,128]{3,2,1,0:T(8,128)S(1)}, u32[]{:S(2)}, u32[]{:S(2)}) %collective-permute-start.10) | collective-permute-done | bytes 98336 | tf_op jit(solution)/shard_map/ppermute | solution.py:254
  35.7 0.7 %pad_maximum_fusion.5 = f32[2,1,2,64,128]{4,3,2,1,0:T(8,128)} fusion(f32[1,1,2,64,128]{4,3,2,1,0:T(8,128)S(1)} %get-tuple-element.11, f32[1,1,2,64,128]{4,3,2,1,0:T(8,128)S(1)} %get-tuple-element.10), kind=kLoop, calls=%fused_computation.5 | loop fusion | flops 32768 | bytes 262144 | tf_op jit(solution)/shard_map/stack | solution.py:296
  36.4 0.6 %fusion.2 = f32[1,64,128]{2,1,0:T(8,128)} fusion(f32[1,3,64,128]{3,2,1,0:T(8,128)S(1)} %collective-permute-done.10, f32[1,3,64,128]{3,2,1,0:T(8,128)S(1)} %get-tuple-element.4), kind=kLoop, calls=%fused_computation.13 | loop fusion | flops 8192 | bytes 98304 | tf_op jit(solution)/shard_map/add | solution.py:294
  (4 shorter events, 0.1 us)
Async XLA Ops:
  0.6 8.7 %collective-permute-start = (f32[1,64,128]{2,1,0:T(8,128)}, f32[1,64,128]{2,1,0:T(8,128)S(1)}, u32[]{:S(2)}, u32[]{:S(2)}) collective-permute-start(f32[1,64,128]{2,1,0:T(8,128)} %param.5), channel_id=1, source_target_pairs={{0,8},{8,0},{16,24},{24,16},{1,9},{9,1},{17,25},{25,17},{2,10},{10... | collective-permute-start | bytes 98312 | tf_op jit(solution)/shard_map/ppermute | solution.py:249
  3.7 6.4 %collective-permute-start.2 = (f32[1,64,128]{2,1,0:T(8,128)}, f32[1,64,128]{2,1,0:T(8,128)S(1)}, u32[]{:S(2)}, u32[]{:S(2)}) collective-permute-start(f32[1,64,128]{2,1,0:T(8,128)} %param.5), channel_id=1, source_target_pairs={{0,24},{8,16},{16,8},{24,0},{1,25},{9,17},{17,9},{25,1},{2,26},{10... | collective-permute-start | bytes 98312 | tf_op jit(solution)/shard_map/ppermute | solution.py:249
  6.2 5.4 %collective-permute-start.1 = (f32[1,64,128]{2,1,0:T(8,128)}, f32[1,64,128]{2,1,0:T(8,128)S(1)}, u32[]{:S(2)}, u32[]{:S(2)}) collective-permute-start(f32[1,64,128]{2,1,0:T(8,128)} %param.5), channel_id=1, source_target_pairs={{0,16},{8,24},{16,0},{24,8},{1,17},{9,25},{17,1},{25,9},{2,18},{10... | collective-permute-start | bytes 98312 | tf_op jit(solution)/shard_map/ppermute | solution.py:249
  6.3 9.1 %collective-permute-start.6 = (f32[2,64,128]{2,1,0:T(8,128)}, f32[2,64,128]{2,1,0:T(8,128)S(1)}, u32[]{:S(2)}, u32[]{:S(2)}) collective-permute-start(f32[2,64,128]{2,1,0:T(8,128)} %param.7), channel_id=1, source_target_pairs={{0,1},{1,0},{2,3},{3,2},{4,5},{5,4},{6,7},{7,6},{8,9},{9,8},{10,11... | collective-permute-start | bytes 196616 | tf_op jit(solution)/shard_map/ppermute | solution.py:249
  7.8 8.1 %collective-permute-start.8 = (f32[2,64,128]{2,1,0:T(8,128)}, f32[2,64,128]{2,1,0:T(8,128)S(1)}, u32[]{:S(2)}, u32[]{:S(2)}) collective-permute-start(f32[2,64,128]{2,1,0:T(8,128)} %param.7), channel_id=1, source_target_pairs={{0,3},{1,2},{2,1},{3,0},{4,7},{5,6},{6,5},{7,4},{8,11},{9,10},{10,... | collective-permute-start | bytes 196616 | tf_op jit(solution)/shard_map/ppermute | solution.py:249
  9.3 6.7 %collective-permute-start.7 = (f32[2,64,128]{2,1,0:T(8,128)}, f32[2,64,128]{2,1,0:T(8,128)S(1)}, u32[]{:S(2)}, u32[]{:S(2)}) collective-permute-start(f32[2,64,128]{2,1,0:T(8,128)} %param.7), channel_id=1, source_target_pairs={{0,2},{1,3},{2,0},{3,1},{4,6},{5,7},{6,4},{7,5},{8,10},{9,11},{10,... | collective-permute-start | bytes 196616 | tf_op jit(solution)/shard_map/ppermute | solution.py:249
  11.6 4.4 %copy-start.3 = (f32[2,64,128]{2,1,0:T(8,128)S(1)}, f32[2,64,128]{2,1,0:T(8,128)}, u32[]{:S(2)}) copy-start(f32[2,64,128]{2,1,0:T(8,128)} %param.7) | copy-start | bytes 196612
  12.4 7.3 %collective-permute-start.5 = (f32[4,64,128]{2,1,0:T(8,128)S(1)}, f32[4,64,128]{2,1,0:T(8,128)S(1)}, u32[]{:S(2)}, u32[]{:S(2)}) collective-permute-start(f32[4,64,128]{2,1,0:T(8,128)S(1)} %get-tuple-element.13), channel_id=1, source_target_pairs={{0,3},{1,2},{2,1},{3,0},{4,7},{5,6},{6,5},{7,4},{8,11},{9,10},{10,... | collective-permute-start | bytes 393224 | tf_op jit(solution)/shard_map/ppermute | solution.py:249
  14.9 5.6 %collective-permute-start.4 = (f32[4,64,128]{2,1,0:T(8,128)S(1)}, f32[4,64,128]{2,1,0:T(8,128)S(1)}, u32[]{:S(2)}, u32[]{:S(2)}) collective-permute-start(f32[4,64,128]{2,1,0:T(8,128)S(1)} %get-tuple-element.13), channel_id=1, source_target_pairs={{0,2},{1,3},{2,0},{3,1},{4,6},{5,7},{6,4},{7,5},{8,10},{9,11},{10,... | collective-permute-start | bytes 393224 | tf_op jit(solution)/shard_map/ppermute | solution.py:249
  15.4 5.1 %collective-permute-start.3 = (f32[4,64,128]{2,1,0:T(8,128)S(1)}, f32[4,64,128]{2,1,0:T(8,128)S(1)}, u32[]{:S(2)}, u32[]{:S(2)}) collective-permute-start(f32[4,64,128]{2,1,0:T(8,128)S(1)} %get-tuple-element.13), channel_id=1, source_target_pairs={{0,1},{1,0},{2,3},{3,2},{4,5},{5,4},{6,7},{7,6},{8,9},{9,8},{10,11... | collective-permute-start | bytes 393224 | tf_op jit(solution)/shard_map/ppermute | solution.py:249
  20.5 2.3 %copy-start = (bf16[1024,256]{1,0:T(8,128)(2,1)S(1)}, bf16[1024,256]{1,0:T(8,128)(2,1)}, u32[]{:S(2)}) copy-start(bf16[1024,256]{1,0:T(8,128)(2,1)} %constant.24.clone.col_ref) | copy-start | bytes 1572868
  20.5 2.3 %copy-start.1 = (bf16[256,512]{1,0:T(8,128)(2,1)S(1)}, bf16[256,512]{1,0:T(8,128)(2,1)}, u32[]{:S(2)}) copy-start(bf16[256,512]{1,0:T(8,128)(2,1)} %constant.23.clone.row_ref) | copy-start | bytes 786436
  20.7 2.2 %copy-start.2 = (s32[2,2]{1,0:T(2,128)S(1)}, s32[2,2]{1,0:T(2,128)}, u32[]{:S(2)}) copy-start(s32[2,2]{1,0:T(2,128)} %tilt_ref.1) | copy-start | bytes 52
  20.7 2.2 %collective-permute-start.9 = (f32[20,64,128]{2,1,0:T(8,128)S(1)}, f32[20,64,128]{2,1,0:T(8,128)S(1)}, u32[]{:S(2)}, u32[]{:S(2)}) collective-permute-start(f32[20,64,128]{2,1,0:T(8,128)S(1)} %get-tuple-element.6), channel_id=1, source_target_pairs={{0,4},{4,0},{1,5},{5,1},{2,6},{6,2},{3,7},{7,3},{8,12},{12,8},{9,1... | collective-permute-start | bytes 1966088 | tf_op jit(solution)/shard_map/ppermute | solution.py:254
  34.3 1.4 %collective-permute-start.10 = (f32[1,3,64,128]{3,2,1,0:T(8,128)S(1)}, f32[1,3,64,128]{3,2,1,0:T(8,128)S(1)}, u32[]{:S(2)}, u32[]{:S(2)}) collective-permute-start(f32[1,3,64,128]{3,2,1,0:T(8,128)S(1)} %get-tuple-element.5), channel_id=1, source_target_pairs={{0,4},{4,0},{1,5},{5,1},{2,6},{6,2},{3,7},{7,3},{8,12},{12,8},{9,1... | collective-permute-start | bytes 294920 | tf_op jit(solution)/shard_map/ppermute | solution.py:254

commit v4 on v2

--- a/solution.py
+++ b/solution.py
@@ -88,95 +88,90 @@
     return np.concatenate([high, low], axis=0)
 
 
-def wave_kernel(
-    tilt_ref, near_ref, far_ref, row_ref, col_ref, mine_ref, theirs_ref,
-    cos_ref, sin_ref, u_high, u_low, a_high, a_low, v_ref, moved_ref,
-):
-    count, height, width = cos_ref.shape
-    slices, _, tile_r, tile_c = mine_ref.shape
-    cols = width // tile_c
+def advance(slice_index, cos_ref, sin_ref, row_ref, col_ref, v_ref, a_high, a_low):
+    _, height, width = v_ref.shape
     blocks = width // LANES
     half = LANES // 2
-    core = lax.axis_index("row")
-    first = lax.axis_index("depth") * slices
-    near_row = pl.multiple_of(core * tile_r, tile_r)
-    far_row = pl.multiple_of((1 - core) * tile_r, tile_r)
-    own_col = pl.ds(pl.multiple_of(lax.axis_index("col") * tile_c, tile_c), tile_c)
-    sides = ((near_ref, near_row), (far_ref, far_row))
-
-    def store_u(row, col, real, imag):
-        for part, value in enumerate((real, imag)):
-            high, low = halves(value)
-            where = (pl.ds(part * height + row, value.shape[0]), pl.ds(col, value.shape[1]))
-            u_high[where] = high
-            u_low[where] = low
-
-    def turned(slice_index, where):
+    matrix = jnp.concatenate([row_ref[:, : 2 * height], row_ref[...]], axis=1)
+    for start in range(0, width, 2 * LANES):
+        where = (slice(None), pl.ds(start, 2 * LANES))
         cos, sin = cos_ref[(slice_index,) + where], sin_ref[(slice_index,) + where]
         real, imag = v_ref[(0,) + where], v_ref[(1,) + where]
-        return cos * real - sin * imag, cos * imag + sin * real
-
-    def keep_moved(slice_index):
-        @pl.when((slice_index >= first) & (slice_index < first + slices))
-        def _():
-            real, imag = turned(slice_index, (slice(None), own_col))
-            moved_ref[slice_index - first, 0] = real
-            moved_ref[slice_index - first, 1] = imag
-
-    def transmit(slice_index):
-        for block in range(blocks):
-            where = (slice(None), pl.ds(block * LANES, LANES))
-            store_u(0, block * LANES, *turned(slice_index, where))
-
-    def propagate():
-        matrix = jnp.concatenate([row_ref[:, : 2 * height], row_ref[...]], axis=1)
-        for start in range(0, width, 2 * LANES):
-            where = (slice(None), pl.ds(start, 2 * LANES))
-            high, low = u_high[where], u_low[where]
-            done = jnp.dot(
-                matrix,
-                jnp.concatenate([high, low, high], axis=0),
-                preferred_element_type=jnp.float32,
-            )
-            for part in range(2):
-                for sub in range(2):
-                    block = start // LANES + sub
-                    value = done[part * height : (part + 1) * height, sub * LANES : (sub + 1) * LANES]
-                    for target, piece in zip((a_high, a_low), halves(value)):
-                        target[block, :, pl.ds(part * LANES, LANES)] = piece
-                        if block > 0:
-                            target[block - 1, :, pl.ds((2 + part) * LANES, half)] = piece[:, :half]
-                        if block < blocks - 1:
-                            target[block + 1, :, pl.ds((2 + part) * LANES + half, half)] = piece[:, half:]
-        high = a_high[...].reshape(blocks * height, 4 * LANES)
-        low = a_low[...].reshape(blocks * height, 4 * LANES)
+        high, low = halves(jnp.concatenate([cos * real - sin * imag, cos * imag + sin * real], axis=0))
         done = jnp.dot(
-            jnp.concatenate([high, low, high], axis=1),
-            jnp.concatenate([col_ref[: 4 * LANES], col_ref[...]], axis=0),
-            preferred_element_type=jnp.float32,
-        )
-        for block in range(blocks):
-            for part in range(2):
-                v_ref[part, :, pl.ds(block * LANES, LANES)] = done[
-                    block * height : (block + 1) * height, part * LANES : (part + 1) * LANES
-                ]
-
+            matrix, jnp.concatenate([high, low, high], axis=0), preferred_element_type=jnp.float32
+        )
+        for part in range(2):
+            for sub in range(2):
+                block = start // LANES + sub
+                value = done[part * height : (part + 1) * height, sub * LANES : (sub + 1) * LANES]
+                for target, piece in zip((a_high, a_low), halves(value)):
+                    target[block, :, pl.ds(part * LANES, LANES)] = piece
+                    if block > 0:
+                        target[block - 1, :, pl.ds((2 + part) * LANES, half)] = piece[:, :half]
+                    if block < blocks - 1:
+                        target[block + 1, :, pl.ds((2 + part) * LANES + half, half)] = piece[:, half:]
+    high = a_high[...].reshape(blocks * height, 4 * LANES)
+    low = a_low[...].reshape(blocks * height, 4 * LANES)
+    done = jnp.dot(
+        jnp.concatenate([high, low, high], axis=1),
+        jnp.concatenate([col_ref[: 4 * LANES], col_ref[...]], axis=0),
+        preferred_element_type=jnp.float32,
+    )
+    for block in range(blocks):
+        for part in range(2):
+            v_ref[part, :, pl.ds(block * LANES, LANES)] = done[
+                block * height : (block + 1) * height, part * LANES : (part + 1) * LANES
+            ]
+
+
+def clear_ends(a_high, a_low):
+    blocks, height, _ = a_high.shape
+    half = LANES // 2
     for target in (a_high, a_low):
         for part in range(2):
             target[0, :, pl.ds((2 + part) * LANES + half, half)] = jnp.zeros((height, half), jnp.bfloat16)
             target[blocks - 1, :, pl.ds((2 + part) * LANES, half)] = jnp.zeros((height, half), jnp.bfloat16)
 
-    def screens(slice_index, carry):
-        section, inner = slice_index // slices, slice_index % slices
-        for side_ref, row in sides:
-            for col in range(cols):
-                cos, sin = cos_sin(side_ref[(section * cols + col) * slices + inner])
-                where = (slice_index, pl.ds(row, tile_r), pl.ds(col * tile_c, tile_c))
-                cos_ref[where] = cos
-                sin_ref[where] = sin
+
+def places(tile_r, tile_c):
+    core = lax.axis_index("row")
+    near = pl.ds(pl.multiple_of(core * tile_r, tile_r), tile_r)
+    far = pl.ds(pl.multiple_of((1 - core) * tile_r, tile_r), tile_r)
+    own_col = pl.ds(pl.multiple_of(lax.axis_index("col") * tile_c, tile_c), tile_c)
+    return near, far, own_col
+
+
+def wave_kernel(
+    tilt_ref, near_own, far_own, near_rest, far_rest, row_ref, col_ref,
+    mine_ref, theirs_ref, cos_ref, sin_ref, v_ref, moved_ref, a_high, a_low,
+):
+    slices, _, tile_r, tile_c = mine_ref.shape
+    _, height, width = v_ref.shape
+    cols = width // tile_c
+    count = cos_ref.shape[0] - 1
+    core, own_section, own_place = lax.axis_index("row"), lax.axis_index("depth"), lax.axis_index("col")
+    first = own_section * slices
+    near, far, own_col = places(tile_r, tile_c)
+    clear_ends(a_high, a_low)
+
+    def screens(col, carry):
+        held = col ^ own_place
+        own_cells = pl.ds(pl.multiple_of(col * tile_c, tile_c), tile_c)
+        for bits in range(count // slices):
+            for inner in range(slices):
+                slice_index = (bits ^ own_section) * slices + inner
+                sources = (near_own, far_own) if bits == 0 else (near_rest, far_rest)
+                place = inner if bits == 0 else (bits - 1) * slices + inner
+                for source, row in zip(sources, (near, far)):
+                    cos, sin = cos_sin(source[held, place])
+                    cos_ref[slice_index, row, own_cells] = cos
+                    sin_ref[slice_index, row, own_cells] = sin
         return carry
 
-    lax.fori_loop(0, count, screens, 0)
+    lax.fori_loop(0, cols, screens, 0)
+    cos_ref[count] = jnp.ones((height, width), jnp.float32)
+    sin_ref[count] = jnp.zeros((height, width), jnp.float32)
 
     def cycles(number, position, extent):
         fraction = (number * position).astype(jnp.float32) / extent
@@ -185,65 +180,74 @@
     row_cos, row_sin = cycles(
         tilt_ref[core, 0], lax.broadcasted_iota(jnp.int32, (height, LANES), 0), float(height)
     )
-    for block in range(blocks):
+    for start in range(0, width, LANES):
         col_cos, col_sin = cycles(
-            tilt_ref[core, 1],
-            lax.broadcasted_iota(jnp.int32, (8, LANES), 1) + block * LANES,
-            float(width),
+            tilt_ref[core, 1], lax.broadcasted_iota(jnp.int32, (8, LANES), 1) + start, float(width)
         )
         col_cos, col_sin = col_cos[:1], col_sin[:1]
-        where = (slice(None), pl.ds(block * LANES, LANES))
-        v_ref[(0,) + where] = row_cos * col_cos - row_sin * col_sin
-        v_ref[(1,) + where] = row_sin * col_cos + row_cos * col_sin
-    transmit(0)
-    keep_moved(0)
+        v_ref[0, :, pl.ds(start, LANES)] = row_cos * col_cos - row_sin * col_sin
+        v_ref[1, :, pl.ds(start, LANES)] = row_sin * col_cos + row_cos * col_sin
 
     def step(tick, carry):
-        propagate()
-
-        @pl.when((tick >= first) & (tick < first + slices))
+        own = (tick >= first) & (tick < first + slices)
+        behind = 2 * count - tick
+
+        @pl.when(own)
         def _():
-            for target, row in ((mine_ref, near_row), (theirs_ref, far_row)):
+            cos, sin = cos_ref[tick, :, own_col], sin_ref[tick, :, own_col]
+            real, imag = v_ref[0, :, own_col], v_ref[1, :, own_col]
+            moved_ref[tick - first, 0] = cos * real - sin * imag
+            moved_ref[tick - first, 1] = cos * imag + sin * real
+
+        @pl.when(tick == count)
+        def _():
+            for row, measured in ((near, near_own), (far, far_own)):
+                for col in range(cols):
+                    where = (row, pl.ds(col * tile_c, tile_c))
+                    place = slices + core if measured is near_own else slices
+                    real, imag = v_ref[(0,) + where], v_ref[(1,) + where]
+                    misfit = 2.0 * (real * real + imag * imag - measured[col ^ own_place, place])
+                    v_ref[(0,) + where] = misfit * real
+                    v_ref[(1,) + where] = -misfit * imag
+
+        passed = jnp.where(tick < count, tick, jnp.minimum(behind, count))
+        advance(passed, cos_ref, sin_ref, row_ref, col_ref, v_ref, a_high, a_low)
+
+        @pl.when(own)
+        def _():
+            for target, row in ((mine_ref, near), (theirs_ref, far)):
                 for part in range(2):
-                    target[tick - first, part] = v_ref[part, pl.ds(row, tile_r), own_col]
-
-        @pl.when(tick == count - 1)
+                    target[tick - first, part] = v_ref[part, row, own_col]
+
+        @pl.when((tick >= count) & (behind - 1 < first + slices))
         def _():
-            for side_ref, row in sides:
-                for col in range(cols):
-                    where = (pl.ds(row, tile_r), pl.ds(col * tile_c, tile_c))
-                    real, imag = v_ref[(0,) + where], v_ref[(1,) + where]
-                    misfit = 2.0 * (real * real + imag * imag - side_ref[count * cols + col])
-                    store_u(row, col * tile_c, misfit * real, -misfit * imag)
-
-        back = 2 * count - 1 - tick
-
-        @pl.when((tick >= count) & (back < first + slices))
-        def _():
-            for target, row in ((mine_ref, near_row), (theirs_ref, far_row)):
-                where = (pl.ds(row, tile_r), own_col)
-                here = (pl.ds(row, tile_r), slice(None))
-                real, imag = v_ref[(0,) + where], v_ref[(1,) + where]
-                target[back - first, 2] = -(
-                    imag * moved_ref[(back - first, 0) + here] + real * moved_ref[(back - first, 1) + here]
-                )
-
-        @pl.when((tick != count - 1) & (back > first))
-        def _():
-            transmit(jnp.where(tick < count, tick + 1, back))
-
-        @pl.when(tick < count - 1)
-        def _():
-            keep_moved(tick + 1)
+            for target, row in ((mine_ref, near), (theirs_ref, far)):
+                real, imag = v_ref[0, row, own_col], v_ref[1, row, own_col]
+                moved = moved_ref[behind - 1 - first, 0, row], moved_ref[behind - 1 - first, 1, row]
+                target[behind - 1 - first, 2] = -(imag * moved[0] + real * moved[1])
 
         return carry
 
     lax.fori_loop(0, 2 * count - first, step, 0)
+
+
+def finish_kernel(mine_ref, received_ref, grad_ref, exit_ref, total_ref, sems):
+    core = lax.axis_index("row")
+    copies = []
+    for source, item in ((mine_ref, core), (received_ref, 1 - core)):
+        copies.append(pltpu.make_async_copy(source.at[:, pl.ds(0, 2)], exit_ref.at[item], sems.at[len(copies)]))
+    for copy in copies:
+        copy.start()
+    total_ref[...] = mine_ref[:, 2] + received_ref[:, 2]
+    copies.append(pltpu.make_async_copy(total_ref, grad_ref, sems.at[2]))
+    copies[2].start()
+    for copy in copies:
+        copy.wait()
 
 
 def spread(shard, axis):
     size = lax.axis_size(axis)
-    return lax.all_to_all(jnp.broadcast_to(shard[None], (size,) + shard.shape), axis, 0, 0)
+    return [lax.ppermute(shard, axis, [(i, i ^ bits) for i in range(size)]) for bits in range(1, size)]
 
 
 def swap_cores(value):
@@ -258,38 +262,47 @@
     width = tile_c * cols
     count = sections * slices
     blocks = width // LANES
-    plane = spread(jnp.concatenate([phase, intensity], axis=0), "col")
-    near_phase = spread(plane[:, :slices], "depth").reshape(count * cols, tile_r, tile_c)
-
-    def packed(item):
-        chosen = lax.dynamic_index_in_dim(plane, slices + item, 1, keepdims=False)
-        return jnp.concatenate([near_phase, chosen], axis=0)
-
-    near, far = packed(core), swap_cores(packed(1 - core))
     vmem = pl.BlockSpec(memory_space=pltpu.VMEM)
+    smem = pl.BlockSpec(memory_space=pltpu.SMEM)
     result = jax.ShapeDtypeStruct((slices, 3, tile_r, tile_c), jnp.float32)
+
+    other_depths = jnp.concatenate(spread(phase, "depth"), axis=0)
+    packet = jnp.concatenate([phase, intensity], axis=0)
+    near_own = jnp.stack([packet] + spread(packet, "col"))
+    arriving = spread(other_depths, "col")
+    arriving[0], near_own = lax.optimization_barrier((arriving[0], near_own))
+    near_rest = jnp.stack([other_depths] + arriving)
+    wanted = lax.dynamic_slice_in_dim(near_own, slices + 1 - core, 1, 1)
+    far_own = swap_cores(jnp.concatenate([near_own[:, :slices], wanted], axis=1))
+    far_rest = swap_cores(near_rest)
+
+    halves_scratch = [pltpu.VMEM((blocks, height, 4 * LANES), jnp.bfloat16)] * 2
+    screen_scratch = [pltpu.VMEM((count + 1, height, width), jnp.float32)] * 2
     mine, theirs = pl.pallas_call(
         wave_kernel,
         out_shape=(result, result),
-        in_specs=[pl.BlockSpec(memory_space=pltpu.SMEM), vmem, vmem, vmem, vmem],
+        in_specs=[smem] + [vmem] * 6,
         out_specs=(vmem, vmem),
-        scratch_shapes=[
-            pltpu.VMEM((count, height, width), jnp.float32),
-            pltpu.VMEM((count, height, width), jnp.float32),
-            pltpu.VMEM((2 * height, width), jnp.bfloat16),
-            pltpu.VMEM((2 * height, width), jnp.bfloat16),
-            pltpu.VMEM((blocks, height, 4 * LANES), jnp.bfloat16),
-            pltpu.VMEM((blocks, height, 4 * LANES), jnp.bfloat16),
-            pltpu.VMEM((2, height, width), jnp.float32),
-            pltpu.VMEM((slices, 2, height, tile_c), jnp.float32),
-        ],
+        scratch_shapes=screen_scratch
+        + [pltpu.VMEM((2, height, width), jnp.float32), pltpu.VMEM((slices, 2, height, tile_c), jnp.float32)]
+        + halves_scratch,
         compiler_params=pltpu.CompilerParams(vmem_limit_bytes=24 * 2**20),
-    )(tilt, near, far, jnp.asarray(row_constant(height)), jnp.asarray(col_constant()))
-    received = swap_cores(theirs)
-    gradient = mine[:, 2] + received[:, 2]
-    waves = (mine[:, :2], received[:, :2])
-    leaving = jnp.stack([jnp.where(core == 0, waves[0], waves[1]), jnp.where(core == 0, waves[1], waves[0])])
-    return gradient, leaving
+    )(
+        tilt, near_own, far_own, near_rest, far_rest,
+        jnp.asarray(row_constant(height)), jnp.asarray(col_constant()),
+    )
+    hbm = pl.BlockSpec(memory_space=pl.ANY)
+    return pl.pallas_call(
+        finish_kernel,
+        out_shape=(
+            jax.ShapeDtypeStruct(phase.shape, jnp.float32),
+            jax.ShapeDtypeStruct((2, slices, 2, tile_r, tile_c), jnp.float32),
+        ),
+        in_specs=[vmem, vmem],
+        out_specs=(hbm, hbm),
+        scratch_shapes=[pltpu.VMEM(phase.shape, jnp.float32), pltpu.SemaphoreType.DMA((3,))],
+        compiler_params=pltpu.CompilerParams(vmem_limit_bytes=4 * 2**20),
+    )(mine, swap_cores(theirs))
 
 
 def extended_2(cells, sides, width):
@@ -462,11 +475,13 @@
 
 def fits_whole(phase_shape, batch, mesh):
     slices, height, width = phase_shape
-    rows, cols = mesh.shape["row"], mesh.shape["col"]
+    rows, cols, sections = mesh.shape["row"], mesh.shape["col"], mesh.shape["depth"]
     bytes_all = 4 * height * width * (slices + batch)
     return (
         bytes_all <= GATHER_BUDGET
         and batch == rows == 2
+        and cols & (cols - 1) == 0
+        and sections & (sections - 1) == 0
         and height == LANES
         and (height // rows) % 16 == 0
         and (width // cols) % LANES == 0

time: 48.8 us -> 34.9 us (0.72)
  blocking collectives: 18 us -> 0 us
  starting transfers between devices: 5.43 us -> 13.5 us
  other arithmetic: 2.25 us -> 0.08 us
  waiting for transfers between devices: 9.86 us -> 8.19 us
    all_to_all x1 -> x0, blocking collectives: 18 us -> none  [spread(): lax.all_to_all(jnp.broadcast_to(shard[None], (size,) + shard.shape), axis...]
    ppermute x0 -> x9, starting transfers between devices: none -> 12.7 us  [spread(): lax.ppermute(shard, axis, [(i, i ^ bits) for i in range(size)])]
    all_to_all x1 -> x0, waiting for transfers between devices: 6.61 us -> none  [spread(): lax.all_to_all(jnp.broadcast_to(shard[None], (size,) + shard.shape), axis...]
    ppermute x0 -> x9, waiting for transfers between devices: none -> 5.57 us  [spread(): lax.ppermute(shard, axis, [(i, i ^ bits) for i in range(size)])]
    all_to_all x1 -> x0, starting transfers between devices: 5.16 us -> none  [spread(): lax.all_to_all(jnp.broadcast_to(shard[None], (size,) + shard.shape), axis...]
    concatenate x2 -> x1, other arithmetic: 0.95 us -> 0.02 us  [whole_field_body(): jnp.concatenate([near_own[:, :slices], wanted], axis=1)]
    unnamed x6 -> x11, local copies, waits for them, and re-layouts: 0.01 us -> 0.86 us
    broadcast_in_dim x2 -> x0, local copies, waits for them, and re-layouts: 0.83 us -> none  [spread(): jnp.broadcast_to(shard[None], (size,) + shard.shape)]
  transfers between devices with their start and end apart: 3 -> 12, of which waited for: 3 -> 5; matrix products, arithmetic and copies ran while one was open for 0% -> 3% of each run, Pallas kernels for 0% -> 0%
where the time goes in v4:
time: 34.9 us; the launch traced here: 34.8 us
  starting transfers between devices  13.5 us (39%)
  Pallas kernels  11.3 us (32%)
  waiting for transfers between devices  8.19 us (23%)
  local copies, waits for them, and re-layouts  0.89 us (3%)
  between operations  0.73 us (2%)
    ppermute x9, starting transfers between devices, spread(): lax.ppermute(shard, axis, [(i, i ^ bits) for i in range(size)])  12.7 us
    pallas_call x1, Pallas kernels, whole_field_body(): pl.pallas_call(wave_kernel, out_shape=(result, result), in_specs=[smem] +...  10.6 us
    ppermute x9, waiting for transfers between devices, spread(): lax.ppermute(shard, axis, [(i, i ^ bits) for i in range(size)])  5.57 us
    ppermute x3, waiting for transfers between devices, swap_cores(): return lax.ppermute(value, 'row', [(0, 1), (1, 0)])  2.62 us
    unnamed x11, local copies, waits for them, and re-layouts  0.86 us
    ppermute x3, starting transfers between devices, swap_cores(): return lax.ppermute(value, 'row', [(0, 1), (1, 0)])  0.82 us
  transfers between devices with their start and end apart: 12, of which 5 were waited for; matrix products, arithmetic and copies ran while one was open for 3% of the time, Pallas kernels for 0%

profile of v4, /device:TPU:0, one launch (start us, length us, event | category | flops | bytes accessed | tf_op | source)
XLA Modules:
  0.0 34.8 jit_solution(10521438661138211012)
XLA Ops:
  0.6 0.0 copy-start.3
  0.6 4.1 %collective-permute-start.1 = (f32[1,64,128]{2,1,0:T(8,128)}, f32[1,64,128]{2,1,0:T(8,128)S(1)}, u32[]{:S(2)}, u32[]{:S(2)}) collective-permute-start(f32[1,64,128]{2,1,0:T(8,128)} %param.5), channel_id=1, source_target_pairs={{0,16},{8,24},{16,0},{24,8},{1,17},{9,25},{17,1},{25,9},{2,18},{10... | collective-permute-start | bytes 98312 | tf_op jit(solution)/shard_map/ppermute | solution.py:250
  4.7 1.6 %collective-permute-start = (f32[1,64,128]{2,1,0:T(8,128)}, f32[1,64,128]{2,1,0:T(8,128)S(1)}, u32[]{:S(2)}, u32[]{:S(2)}) collective-permute-start(f32[1,64,128]{2,1,0:T(8,128)} %param.5), channel_id=1, source_target_pairs={{0,8},{8,0},{16,24},{24,16},{1,9},{9,1},{17,25},{25,17},{2,10},{10... | collective-permute-start | bytes 98312 | tf_op jit(solution)/shard_map/ppermute | solution.py:250
  6.3 0.0 collective-permute-start.2
  6.3 0.8 %constant_dynamic-update-slice_fusion.4 = f32[3,64,128]{2,1,0:T(8,128)S(1)} fusion(f32[1,64,128]{2,1,0:T(8,128)} %param.5), kind=kLoop, calls=%fused_computation.7 | loop fusion | bytes 65536
  7.1 0.0 copy-done.3
  7.2 2.7 %collective-permute-start.6 = (f32[3,64,128]{2,1,0:T(8,128)S(1)}, f32[3,64,128]{2,1,0:T(8,128)S(1)}, u32[]{:S(2)}, u32[]{:S(2)}) collective-permute-start(f32[3,64,128]{2,1,0:T(8,128)S(1)} %constant_dynamic-update-slice_fusion.3), channel_id=1, source_target_pairs={{0,3},{1,2},{2,1},{3,0},{4,7},{5,6},{6,5},{7,4},{8,11},{9,10},{10,... | collective-permute-start | bytes 294920 | tf_op jit(solution)/shard_map/ppermute | solution.py:250
  9.9 0.5 %collective-permute-start.5 = (f32[3,64,128]{2,1,0:T(8,128)S(1)}, f32[3,64,128]{2,1,0:T(8,128)S(1)}, u32[]{:S(2)}, u32[]{:S(2)}) collective-permute-start(f32[3,64,128]{2,1,0:T(8,128)S(1)} %constant_dynamic-update-slice_fusion.3), channel_id=1, source_target_pairs={{0,2},{1,3},{2,0},{3,1},{4,6},{5,7},{6,4},{7,5},{8,10},{9,11},{10,... | collective-permute-start | bytes 294920 | tf_op jit(solution)/shard_map/ppermute | solution.py:250
  10.4 0.0 collective-permute-done
  10.4 0.3 %collective-permute-start.4 = (f32[3,64,128]{2,1,0:T(8,128)S(1)}, f32[3,64,128]{2,1,0:T(8,128)S(1)}, u32[]{:S(2)}, u32[]{:S(2)}) collective-permute-start(f32[3,64,128]{2,1,0:T(8,128)S(1)} %constant_dynamic-update-slice_fusion.3), channel_id=1, source_target_pairs={{0,1},{1,0},{2,3},{3,2},{4,5},{5,4},{6,7},{7,6},{8,9},{9,8},{10,11... | collective-permute-start | bytes 294920 | tf_op jit(solution)/shard_map/ppermute | solution.py:250
  10.7 0.0 collective-permute-done.1
  10.7 1.5 %collective-permute-done.2 = f32[1,64,128]{2,1,0:T(8,128)S(1)} collective-permute-done((f32[1,64,128]{2,1,0:T(8,128)}, f32[1,64,128]{2,1,0:T(8,128)S(1)}, u32[]{:S(2)}, u32[]{:S(2)}) %collective-permute-start.2) | collective-permute-done | bytes 32800 | tf_op jit(solution)/shard_map/ppermute | solution.py:250
  12.2 2.4 %collective-permute-start.9 = (f32[3,64,128]{2,1,0:T(8,128)S(1)}, f32[3,64,128]{2,1,0:T(8,128)S(1)}, u32[]{:S(2)}, u32[]{:S(2)}) collective-permute-start(f32[3,64,128]{2,1,0:T(8,128)S(1)} %constant_dynamic-update-slice_fusion), channel_id=1, source_target_pairs={{0,3},{1,2},{2,1},{3,0},{4,7},{5,6},{6,5},{7,4},{8,11},{9,10},{10,... | collective-permute-start | bytes 294920 | tf_op jit(solution)/shard_map/ppermute | solution.py:250
  14.7 0.5 %collective-permute-start.8 = (f32[3,64,128]{2,1,0:T(8,128)S(1)}, f32[3,64,128]{2,1,0:T(8,128)S(1)}, u32[]{:S(2)}, u32[]{:S(2)}) collective-permute-start(f32[3,64,128]{2,1,0:T(8,128)S(1)} %constant_dynamic-update-slice_fusion), channel_id=1, source_target_pairs={{0,2},{1,3},{2,0},{3,1},{4,6},{5,7},{6,4},{7,5},{8,10},{9,11},{10,... | collective-permute-start | bytes 294920 | tf_op jit(solution)/shard_map/ppermute | solution.py:250
  15.2 0.0 collective-permute-done.6
  15.2 0.5 %collective-permute-start.3 = (f32[3,64,128]{2,1,0:T(8,128)S(1)}, f32[3,64,128]{2,1,0:T(8,128)S(1)}, u32[]{:S(2)}, u32[]{:S(2)}) collective-permute-start(f32[3,64,128]{2,1,0:T(8,128)S(1)} %constant_dynamic-update-slice_fusion), channel_id=1, source_target_pairs={{0,1},{1,0},{2,3},{3,2},{4,5},{5,4},{6,7},{7,6},{8,9},{9,8},{10,11... | collective-permute-start | bytes 294920 | tf_op jit(solution)/shard_map/ppermute | solution.py:250
  15.7 0.0 collective-permute-done.5
  15.7 0.2 collective-permute-done.4
  16.0 3.8 %collective-permute-done.3 = f32[3,64,128]{2,1,0:T(8,128)S(1)} collective-permute-done((f32[3,64,128]{2,1,0:T(8,128)S(1)}, f32[3,64,128]{2,1,0:T(8,128)S(1)}, u32[]{:S(2)}, u32[]{:S(2)}) %collective-permute-start.3) | collective-permute-done | bytes 98336 | tf_op jit(solution)/shard_map/ppermute | solution.py:250
  19.8 0.0 collective-permute-done.9
  19.8 0.0 collective-permute-done.8
  19.9 0.0 copy-start
  19.9 0.1 collective-permute-start.10
  20.0 0.0 copy-start.1
  20.0 0.0 copy-start.2
  20.0 0.6 %collective-permute-start.7 = (f32[4,2,64,128]{3,2,1,0:T(8,128)S(1)}, f32[4,2,64,128]{3,2,1,0:T(8,128)S(1)}, u32[]{:S(2)}, u32[]{:S(2)}) collective-permute-start(f32[4,2,64,128]{3,2,1,0:T(8,128)S(1)} %pad_maximum_fusion.2), channel_id=1, source_target_pairs={{0,4},{4,0},{1,5},{5,1},{2,6},{6,2},{3,7},{7,3},{8,12},{12,8},{9,1... | collective-permute-start | bytes 786440 | tf_op jit(solution)/shard_map/ppermute | solution.py:254
  20.6 1.4 %collective-permute-done.7.far_own = f32[4,2,64,128]{3,2,1,0:T(8,128)S(1)} collective-permute-done((f32[4,2,64,128]{3,2,1,0:T(8,128)S(1)}, f32[4,2,64,128]{3,2,1,0:T(8,128)S(1)}, u32[]{:S(2)}, u32[]{:S(2)}) %collective-permute-start.7) | collective-permute-done | bytes 262176 | tf_op jit(solution)/shard_map/ppermute | solution.py:254
  22.0 0.0 collective-permute-done.10.far_rest
  22.0 0.0 copy-done
  22.0 0.0 copy-done.1
  22.0 0.0 copy-done.2
  22.1 10.6 %shard_map.68 = (f32[1,3,64,128]{3,2,1,0:T(8,128)S(1)}, f32[1,3,64,128]{3,2,1,0:T(8,128)S(1)}) custom-call(s32[2,2]{1,0:T(2,128)S(1)} %copy-done.2, f32[4,3,64,128]{3,2,1,0:T(8,128)S(1)} %pad_maximum_fusion.near_own, f32[4,2,64,128]{3,2,1,0:T(8,128)S(1)} %collective-permute-done.7.far_own, f32[4,3,64,128]{3,2,1,0:T(8,128)S(1)} %pad_maximum_fusion.1.near_rest, ...), custom_call_target="tpu_custom_call" | custom-call | tf_op jit(solution)/shard_map/pallas_call | solution.py:281
  32.7 0.2 collective-permute-start.11
  32.9 1.2 %collective-permute-done.11.received_ref = f32[1,3,64,128]{3,2,1,0:T(8,128)S(1)} collective-permute-done((f32[1,3,64,128]{3,2,1,0:T(8,128)S(1)}, f32[1,3,64,128]{3,2,1,0:T(8,128)S(1)}, u32[]{:S(2)}, u32[]{:S(2)}) %collective-permute-start.11) | collective-permute-done | bytes 98336 | tf_op jit(solution)/shard_map/ppermute | solution.py:254
  34.1 0.7 %shard_map.69 = (f32[1,64,128]{2,1,0:T(8,128)}, f32[2,1,2,64,128]{4,3,2,1,0:T(8,128)}) custom-call(f32[1,3,64,128]{3,2,1,0:T(8,128)S(1)} %get-tuple-element.8.mine_ref, f32[1,3,64,128]{3,2,1,0:T(8,128)S(1)} %collective-permute-done.11.received_ref), custom_call_target="tpu_custom_call" | custom-call | tf_op jit(solution)/shard_map/pallas_call | solution.py:295
  (8 shorter events, 0.1 us)
Async XLA Ops:
  0.6 6.5 %copy-start.3 = (f32[2,64,128]{2,1,0:T(8,128)S(1)}, f32[2,64,128]{2,1,0:T(8,128)}, u32[]{:S(2)}) copy-start(f32[2,64,128]{2,1,0:T(8,128)} %param.7) | copy-start | bytes 196612
  0.6 10.1 %collective-permute-start.1 = (f32[1,64,128]{2,1,0:T(8,128)}, f32[1,64,128]{2,1,0:T(8,128)S(1)}, u32[]{:S(2)}, u32[]{:S(2)}) collective-permute-start(f32[1,64,128]{2,1,0:T(8,128)} %param.5), channel_id=1, source_target_pairs={{0,16},{8,24},{16,0},{24,8},{1,17},{9,25},{17,1},{25,9},{2,18},{10... | collective-permute-start | bytes 98312 | tf_op jit(solution)/shard_map/ppermute | solution.py:250
  4.7 5.6 %collective-permute-start = (f32[1,64,128]{2,1,0:T(8,128)}, f32[1,64,128]{2,1,0:T(8,128)S(1)}, u32[]{:S(2)}, u32[]{:S(2)}) collective-permute-start(f32[1,64,128]{2,1,0:T(8,128)} %param.5), channel_id=1, source_target_pairs={{0,8},{8,0},{16,24},{24,16},{1,9},{9,1},{17,25},{25,17},{2,10},{10... | collective-permute-start | bytes 98312 | tf_op jit(solution)/shard_map/ppermute | solution.py:250
  6.3 5.9 %collective-permute-start.2 = (f32[1,64,128]{2,1,0:T(8,128)}, f32[1,64,128]{2,1,0:T(8,128)S(1)}, u32[]{:S(2)}, u32[]{:S(2)}) collective-permute-start(f32[1,64,128]{2,1,0:T(8,128)} %param.5), channel_id=1, source_target_pairs={{0,24},{8,16},{16,8},{24,0},{1,25},{9,17},{17,9},{25,1},{2,26},{10... | collective-permute-start | bytes 98312 | tf_op jit(solution)/shard_map/ppermute | solution.py:250
  7.2 8.0 %collective-permute-start.6 = (f32[3,64,128]{2,1,0:T(8,128)S(1)}, f32[3,64,128]{2,1,0:T(8,128)S(1)}, u32[]{:S(2)}, u32[]{:S(2)}) collective-permute-start(f32[3,64,128]{2,1,0:T(8,128)S(1)} %constant_dynamic-update-slice_fusion.3), channel_id=1, source_target_pairs={{0,3},{1,2},{2,1},{3,0},{4,7},{5,6},{6,5},{7,4},{8,11},{9,10},{10,... | collective-permute-start | bytes 294920 | tf_op jit(solution)/shard_map/ppermute | solution.py:250
  9.9 5.9 %collective-permute-start.5 = (f32[3,64,128]{2,1,0:T(8,128)S(1)}, f32[3,64,128]{2,1,0:T(8,128)S(1)}, u32[]{:S(2)}, u32[]{:S(2)}) collective-permute-start(f32[3,64,128]{2,1,0:T(8,128)S(1)} %constant_dynamic-update-slice_fusion.3), channel_id=1, source_target_pairs={{0,2},{1,3},{2,0},{3,1},{4,6},{5,7},{6,4},{7,5},{8,10},{9,11},{10,... | collective-permute-start | bytes 294920 | tf_op jit(solution)/shard_map/ppermute | solution.py:250
  10.4 5.6 %collective-permute-start.4 = (f32[3,64,128]{2,1,0:T(8,128)S(1)}, f32[3,64,128]{2,1,0:T(8,128)S(1)}, u32[]{:S(2)}, u32[]{:S(2)}) collective-permute-start(f32[3,64,128]{2,1,0:T(8,128)S(1)} %constant_dynamic-update-slice_fusion.3), channel_id=1, source_target_pairs={{0,1},{1,0},{2,3},{3,2},{4,5},{5,4},{6,7},{7,6},{8,9},{9,8},{10,11... | collective-permute-start | bytes 294920 | tf_op jit(solution)/shard_map/ppermute | solution.py:250
  12.2 7.6 %collective-permute-start.9 = (f32[3,64,128]{2,1,0:T(8,128)S(1)}, f32[3,64,128]{2,1,0:T(8,128)S(1)}, u32[]{:S(2)}, u32[]{:S(2)}) collective-permute-start(f32[3,64,128]{2,1,0:T(8,128)S(1)} %constant_dynamic-update-slice_fusion), channel_id=1, source_target_pairs={{0,3},{1,2},{2,1},{3,0},{4,7},{5,6},{6,5},{7,4},{8,11},{9,10},{10,... | collective-permute-start | bytes 294920 | tf_op jit(solution)/shard_map/ppermute | solution.py:250
  14.7 5.1 %collective-permute-start.8 = (f32[3,64,128]{2,1,0:T(8,128)S(1)}, f32[3,64,128]{2,1,0:T(8,128)S(1)}, u32[]{:S(2)}, u32[]{:S(2)}) collective-permute-start(f32[3,64,128]{2,1,0:T(8,128)S(1)} %constant_dynamic-update-slice_fusion), channel_id=1, source_target_pairs={{0,2},{1,3},{2,0},{3,1},{4,6},{5,7},{6,4},{7,5},{8,10},{9,11},{10,... | collective-permute-start | bytes 294920 | tf_op jit(solution)/shard_map/ppermute | solution.py:250
  15.2 4.6 %collective-permute-start.3 = (f32[3,64,128]{2,1,0:T(8,128)S(1)}, f32[3,64,128]{2,1,0:T(8,128)S(1)}, u32[]{:S(2)}, u32[]{:S(2)}) collective-permute-start(f32[3,64,128]{2,1,0:T(8,128)S(1)} %constant_dynamic-update-slice_fusion), channel_id=1, source_target_pairs={{0,1},{1,0},{2,3},{3,2},{4,5},{5,4},{6,7},{7,6},{8,9},{9,8},{10,11... | collective-permute-start | bytes 294920 | tf_op jit(solution)/shard_map/ppermute | solution.py:250
  19.9 2.2 %copy-start = (bf16[1024,256]{1,0:T(8,128)(2,1)S(1)}, bf16[1024,256]{1,0:T(8,128)(2,1)}, u32[]{:S(2)}) copy-start(bf16[1024,256]{1,0:T(8,128)(2,1)} %constant.18.clone.col_ref) | copy-start | bytes 1572868
  19.9 2.2 %collective-permute-start.10 = (f32[4,3,64,128]{3,2,1,0:T(8,128)S(1)}, f32[4,3,64,128]{3,2,1,0:T(8,128)S(1)}, u32[]{:S(2)}, u32[]{:S(2)}) collective-permute-start(f32[4,3,64,128]{3,2,1,0:T(8,128)S(1)} %pad_maximum_fusion.1.near_rest), channel_id=1, source_target_pairs={{0,4},{4,0},{1,5},{5,1},{2,6},{6,2},{3,7},{7,3},{8,12},{12,8},{9,1... | collective-permute-start | bytes 1179656 | tf_op jit(solution)/shard_map/ppermute | solution.py:254
  20.0 2.1 %copy-start.1 = (bf16[256,512]{1,0:T(8,128)(2,1)S(1)}, bf16[256,512]{1,0:T(8,128)(2,1)}, u32[]{:S(2)}) copy-start(bf16[256,512]{1,0:T(8,128)(2,1)} %constant.17.clone.row_ref) | copy-start | bytes 786436
  20.0 2.1 %copy-start.2 = (s32[2,2]{1,0:T(2,128)S(1)}, s32[2,2]{1,0:T(2,128)}, u32[]{:S(2)}) copy-start(s32[2,2]{1,0:T(2,128)} %tilt_ref.1) | copy-start | bytes 52
  20.0 2.0 %collective-permute-start.7 = (f32[4,2,64,128]{3,2,1,0:T(8,128)S(1)}, f32[4,2,64,128]{3,2,1,0:T(8,128)S(1)}, u32[]{:S(2)}, u32[]{:S(2)}) collective-permute-start(f32[4,2,64,128]{3,2,1,0:T(8,128)S(1)} %pad_maximum_fusion.2), channel_id=1, source_target_pairs={{0,4},{4,0},{1,5},{5,1},{2,6},{6,2},{3,7},{7,3},{8,12},{12,8},{9,1... | collective-permute-start | bytes 786440 | tf_op jit(solution)/shard_map/ppermute | solution.py:254
  32.7 1.4 %collective-permute-start.11 = (f32[1,3,64,128]{3,2,1,0:T(8,128)S(1)}, f32[1,3,64,128]{3,2,1,0:T(8,128)S(1)}, u32[]{:S(2)}, u32[]{:S(2)}) collective-permute-start(f32[1,3,64,128]{3,2,1,0:T(8,128)S(1)} %get-tuple-element.9), channel_id=1, source_target_pairs={{0,4},{4,0},{1,5},{5,1},{2,6},{6,2},{3,7},{7,3},{8,12},{12,8},{9,1... | collective-permute-start | bytes 294920 | tf_op jit(solution)/shard_map/ppermute | solution.py:254

commit v5 on v0

--- a/solution.py
+++ b/solution.py
@@ -2,11 +2,384 @@
 
 import jax
 import jax.numpy as jnp
+import numpy as np
 from jax import lax
+from jax.experimental import pallas as pl
+from jax.experimental.pallas import tpu as pltpu
 from jax.sharding import PartitionSpec as P
 
 HALO = 32
 FRESNEL = 64
+LANES = 128
+GATHER_BUDGET = 4 * 2**20
+SIN = (
+    0.9999999980536763,
+    -0.1666666530009577,
+    0.008333305907073658,
+    -0.00019838908256358006,
+    2.745822627876341e-06,
+    -2.3043562782810933e-08,
+)
+COS = (
+    0.9999999961345007,
+    -0.4999999301617528,
+    0.04166646215023687,
+    -0.0013886696163545999,
+    2.4695045482778703e-05,
+    -2.5154931690000354e-07,
+)
+
+
+def horner(coefficients, square):
+    total = jnp.full_like(square, coefficients[-1])
+    for coefficient in coefficients[-2::-1]:
+        total = total * square + coefficient
+    return total
+
+
+def cos_sin(angle):
+    square = angle * angle
+    return horner(COS, square), horner(SIN, square) * angle
+
+
+def turn(fraction):
+    half_cos, half_sin = cos_sin(fraction * math.pi)
+    return half_cos * half_cos - half_sin * half_sin, 2.0 * half_cos * half_sin
+
+
+def halves(value):
+    high = value.astype(jnp.bfloat16)
+    return high, (value - high.astype(jnp.float32)).astype(jnp.bfloat16)
+
+
+def np_halves(matrix):
+    high = matrix.astype(jnp.bfloat16)
+    return high, (matrix - high.astype(np.float64)).astype(jnp.bfloat16)
+
+
+def np_taps():
+    offset = np.arange(-HALO, HALO + 1, dtype=np.float64)
+    taper = np.maximum(np.abs(offset) - 0.5 * HALO, 0.0)
+    weight = np.cos(np.pi * taper / (HALO + 2.0)) ** 2 / math.sqrt(FRESNEL)
+    return weight * np.exp(1j * np.pi * offset * offset / FRESNEL)
+
+
+def np_band(out_pos, in_pos):
+    offset = out_pos[:, None] - in_pos[None, :]
+    inside = np.abs(offset) <= HALO
+    return np.where(inside, np_taps()[np.clip(offset, -HALO, HALO) + HALO], 0.0)
+
+
+def row_constant(height):
+    matrices = []
+    for core in range(2):
+        pos = (np.arange(height) + core * (height // 2)) % height
+        band = np_band(pos, pos)
+        whole = np.block([[band.real, -band.imag], [band.imag, band.real]])
+        matrices.append(np.concatenate(np_halves(whole), axis=1))
+    return np.stack(matrices)
+
+
+def col_constant():
+    lane = np.arange(LANES)
+    edge_pos = np.where(lane < LANES // 2, lane + LANES, lane - LANES)
+    parts = []
+    for position in (lane, edge_pos):
+        band = np_band(lane, position).T
+        parts.append(np.block([[band.real, band.imag], [-band.imag, band.real]]))
+    high, low = np_halves(np.concatenate(parts, axis=0))
+    return np.concatenate([high, low], axis=0)
+
+
+def both_rows(near_ref, far_ref, where):
+    return jnp.concatenate([near_ref[where], far_ref[where]], axis=0)
+
+
+def block_turned(slice_index, block, screens, v_ref):
+    near_cos, near_sin, far_cos, far_sin = screens
+    cos = both_rows(near_cos, far_cos, (slice_index, block))
+    sin = both_rows(near_sin, far_sin, (slice_index, block))
+    real, imag = v_ref[block, 0], v_ref[block, 1]
+    return cos * real - sin * imag, cos * imag + sin * real
+
+
+def row_product(row_matrix, columns):
+    high, low = halves(columns)
+    whole = row_matrix.shape[0]
+    return jnp.dot(
+        jnp.concatenate([row_matrix[:, :whole], row_matrix], axis=1),
+        jnp.concatenate([high, low, high], axis=0),
+        preferred_element_type=jnp.float32,
+    )
+
+
+def col_product(high, low, col_high, col_low):
+    return jnp.dot(
+        jnp.concatenate([high, low, high], axis=1),
+        jnp.concatenate([col_high, col_high, col_low], axis=0),
+        preferred_element_type=jnp.float32,
+    )
+
+
+def advance(slice_index, start, size, screens, row_matrix, col_ref, v_ref, a_high, a_low):
+    height = v_ref.shape[2]
+    half = LANES // 2
+    own, edge = pl.ds(0, 2 * LANES), pl.ds(2 * LANES, 2 * LANES)
+    low_own, low_edge = pl.ds(4 * LANES, 2 * LANES), pl.ds(6 * LANES, 2 * LANES)
+    chunks = [range(place, min(place + 2, size)) for place in range(0, size, 2)]
+    for chunk in chunks:
+        columns = jnp.concatenate(
+            [jnp.concatenate(block_turned(slice_index, start + place, screens, v_ref), axis=0) for place in chunk],
+            axis=1,
+        )
+        done = row_product(row_matrix, columns)
+        for sub, place in enumerate(chunk):
+            for part in range(2):
+                value = done[part * height : (part + 1) * height, sub * LANES : (sub + 1) * LANES]
+                for target, piece in zip((a_high, a_low), halves(value)):
+                    target[place, :, pl.ds(part * LANES, LANES)] = piece
+                    if place > 0:
+                        target[place - 1, :, pl.ds((2 + part) * LANES, half)] = piece[:, :half]
+                    if place < size - 1:
+                        target[place + 1, :, pl.ds((2 + part) * LANES + half, half)] = piece[:, half:]
+    parts = []
+    for chunk in chunks:
+        cells = pl.ds(chunk[0], len(chunk))
+        rows = len(chunk) * height
+        parts.append(
+            col_product(
+                a_high[cells, :, own].reshape(rows, 2 * LANES),
+                a_low[cells, :, own].reshape(rows, 2 * LANES),
+                col_ref[own],
+                col_ref[low_own],
+            )
+        )
+    cells, rows = pl.ds(0, size), size * height
+    edges = col_product(
+        a_high[cells, :, edge].reshape(rows, 2 * LANES),
+        a_low[cells, :, edge].reshape(rows, 2 * LANES),
+        col_ref[edge],
+        col_ref[low_edge],
+    )
+    for chunk, done in zip(chunks, parts):
+        for sub, place in enumerate(chunk):
+            total = done[sub * height : (sub + 1) * height] + edges[place * height : (place + 1) * height]
+            for part in range(2):
+                v_ref[start + place, part] = total[:, part * LANES : (part + 1) * LANES]
+
+
+def clear_edge(a_ref, place, right):
+    half = LANES // 2
+    for part in range(2):
+        begin = (2 + part) * LANES + (0 if right else half)
+        a_ref[place, :, pl.ds(begin, half)] = jnp.zeros((a_ref.shape[1], half), a_ref.dtype)
+
+
+def prepare_kernel(tilt_ref, near_phase, wave_ref, cos_ref, sin_ref):
+    blocks, _, height, _ = wave_ref.shape
+    count = cos_ref.shape[0] - 1
+    core, own_section, own_place = lax.axis_index("row"), lax.axis_index("depth"), lax.axis_index("col")
+
+    def screens(col, carry):
+        held = col ^ own_place
+        for bits in range(count):
+            cos_ref[bits ^ own_section, col], sin_ref[bits ^ own_section, col] = cos_sin(near_phase[held, bits])
+        return carry
+
+    lax.fori_loop(0, blocks, screens, 0)
+    cos_ref[count] = jnp.ones(cos_ref.shape[1:], jnp.float32)
+    sin_ref[count] = jnp.zeros(cos_ref.shape[1:], jnp.float32)
+
+    def cycles(number, position, extent):
+        fraction = (number * position).astype(jnp.float32) / extent
+        return turn(fraction - jnp.round(fraction))
+
+    row = lax.broadcasted_iota(jnp.int32, (height, LANES), 0) + core * (height // 2)
+    row = jnp.where(row >= height, row - height, row)
+    row_cos, row_sin = cycles(tilt_ref[core, 0], row, float(height))
+    for block in range(blocks):
+        col_cos, col_sin = cycles(
+            tilt_ref[core, 1],
+            lax.broadcasted_iota(jnp.int32, (8, LANES), 1) + block * LANES,
+            float(blocks * LANES),
+        )
+        col_cos, col_sin = col_cos[:1], col_sin[:1]
+        wave_ref[block, 0] = row_cos * col_cos - row_sin * col_sin
+        wave_ref[block, 1] = row_sin * col_cos + row_cos * col_sin
+
+
+def wave_kernel(
+    wave_ref, near_cos, near_sin, near_measured, far_measured, far_phase, row_ref, col_ref,
+    mine_ref, theirs_ref, far_cos, far_sin, v_ref, moved_ref, a_high, a_low,
+):
+    blocks, _, height, _ = v_ref.shape
+    count = near_cos.shape[0] - 1
+    core, own_section, own_place = lax.axis_index("row"), lax.axis_index("depth"), lax.axis_index("col")
+    near, far = pl.ds(0, height // 2), pl.ds(height // 2, height // 2)
+    screens = (near_cos, near_sin, far_cos, far_sin)
+    row_matrix = row_ref.at[core]
+    window = min(3, blocks)
+    window_start = jnp.clip(own_place - 1, 0, blocks - window)
+
+    def far_screens(slice_index):
+        for col in range(blocks):
+            angle = far_phase[col ^ own_place, slice_index ^ own_section]
+            far_cos[slice_index, col], far_sin[slice_index, col] = cos_sin(angle)
+
+    for target in (a_high, a_low):
+        clear_edge(target, 0, False)
+        clear_edge(target, blocks - 1, True)
+    far_cos[count] = jnp.ones(far_cos.shape[1:], jnp.float32)
+    far_sin[count] = jnp.zeros(far_cos.shape[1:], jnp.float32)
+    v_ref[...] = wave_ref[...]
+    far_screens(0)
+
+    def forward(tick, carry):
+        @pl.when(tick == own_section)
+        def _():
+            moved_ref[0], moved_ref[1] = block_turned(tick, own_place, screens, v_ref)
+
+        advance(tick, 0, blocks, screens, row_matrix[...], col_ref, v_ref, a_high, a_low)
+        far_screens(jnp.minimum(tick + 1, count - 1))
+
+        @pl.when(tick == own_section)
+        def _():
+            for target, row in ((mine_ref, near), (theirs_ref, far)):
+                for part in range(2):
+                    target[0, part] = v_ref[own_place, part, row]
+
+        return carry
+
+    lax.fori_loop(0, count, forward, 0)
+
+    for target in (a_high, a_low):
+        clear_edge(target, window - 1, True)
+    for place in range(window):
+        block = window_start + place
+        held = block ^ own_place
+        for row, measured in ((near, near_measured[held, core]), (far, far_measured[held, 0])):
+            real, imag = v_ref[block, 0, row], v_ref[block, 1, row]
+            misfit = 2.0 * (real * real + imag * imag - measured)
+            v_ref[block, 0, row] = misfit * real
+            v_ref[block, 1, row] = -misfit * imag
+
+    def backward(tick, carry):
+        advance(count - tick, window_start, window, screens, row_matrix[...], col_ref, v_ref, a_high, a_low)
+        return carry
+
+    lax.fori_loop(0, count - 1 - own_section, backward, 0)
+
+    left, right = jnp.maximum(own_place - 1, 0), jnp.minimum(own_place + 1, blocks - 1)
+    lane = lax.broadcasted_iota(jnp.int32, (2 * height, LANES), 1)
+    has_left, has_right = own_place > 0, own_place < blocks - 1
+    behind = own_section + 1
+    own_cells = jnp.concatenate(block_turned(behind, own_place, screens, v_ref), axis=0)
+    left_cells = jnp.concatenate(block_turned(behind, left, screens, v_ref), axis=0)
+    right_cells = jnp.concatenate(block_turned(behind, right, screens, v_ref), axis=0)
+    edge_cells = jnp.where(
+        lane < LANES // 2, jnp.where(has_right, right_cells, 0.0), jnp.where(has_left, left_cells, 0.0)
+    )
+    done = row_product(row_matrix[...], jnp.concatenate([own_cells, edge_cells], axis=1))
+    quarters = [
+        done[part * height : (part + 1) * height, sub * LANES : (sub + 1) * LANES]
+        for sub in range(2)
+        for part in range(2)
+    ]
+    high, low = halves(jnp.concatenate(quarters, axis=1))
+    pulled = col_product(high, low, col_ref[: 4 * LANES], col_ref[4 * LANES :])
+    gradient = -(pulled[:, LANES:] * moved_ref[0] + pulled[:, :LANES] * moved_ref[1])
+    mine_ref[0, 2] = gradient[: height // 2]
+    theirs_ref[0, 2] = gradient[height // 2 :]
+
+
+def copy_kernel(from_ref, to_ref):
+    to_ref[...] = from_ref[...]
+
+
+def finish_kernel(mine_ref, received_ref, grad_ref, exit_ref, total_ref, sems):
+    core = lax.axis_index("row")
+    copies = []
+    for source, item in ((mine_ref, core), (received_ref, 1 - core)):
+        copies.append(pltpu.make_async_copy(source.at[:, pl.ds(0, 2)], exit_ref.at[item], sems.at[len(copies)]))
+    for copy in copies:
+        copy.start()
+    total_ref[...] = mine_ref[:, 2] + received_ref[:, 2]
+    copies.append(pltpu.make_async_copy(total_ref, grad_ref, sems.at[2]))
+    copies[2].start()
+    for copy in copies:
+        copy.wait()
+
+
+def spread(shard, axis):
+    size = lax.axis_size(axis)
+    return [lax.ppermute(shard, axis, [(i, i ^ bits) for i in range(size)]) for bits in range(1, size)]
+
+
+def swap_cores(value):
+    return lax.ppermute(value, "row", [(0, 1), (1, 0)])
+
+
+def whole_field_body(phase, tilt, intensity):
+    _, tile_r, tile_c = phase.shape
+    count, blocks = lax.axis_size("depth"), lax.axis_size("col")
+    core = lax.axis_index("row")
+    height = 2 * tile_r
+    vmem = pl.BlockSpec(memory_space=pltpu.VMEM)
+    smem = pl.BlockSpec(memory_space=pltpu.SMEM)
+    hbm = pl.BlockSpec(memory_space=pl.ANY)
+
+    def array(*shape):
+        return jax.ShapeDtypeStruct(shape, jnp.float32)
+
+    def params(mebibytes):
+        return pltpu.CompilerParams(vmem_limit_bytes=mebibytes * 2**20)
+
+    own_phase = pl.pallas_call(
+        copy_kernel,
+        out_shape=array(*phase.shape),
+        in_specs=[vmem],
+        out_specs=vmem,
+        compiler_params=params(1),
+    )(phase)
+    column = jnp.concatenate([own_phase] + spread(phase, "depth"), axis=0)
+    near_measured = jnp.stack([intensity] + spread(intensity, "col"))
+    far_measured = swap_cores(lax.dynamic_slice_in_dim(near_measured, 1 - core, 1, 1))
+    arriving = spread(column, "col")
+    arriving[0], far_measured = lax.optimization_barrier((arriving[0], far_measured))
+    near_phase = jnp.stack([column] + arriving)
+    far_phase = swap_cores(near_phase)
+
+    half_screens = (count + 1, blocks, tile_r, tile_c)
+    field = (blocks, 2, height, tile_c)
+    wave, near_cos, near_sin = pl.pallas_call(
+        prepare_kernel,
+        out_shape=(array(*field), array(*half_screens), array(*half_screens)),
+        in_specs=[smem, vmem],
+        out_specs=(vmem,) * 3,
+        compiler_params=params(8),
+        cost_estimate=pl.CostEstimate(flops=5 * 10**8, bytes_accessed=2**20, transcendentals=0),
+    )(tilt, near_phase)
+    mine, theirs = pl.pallas_call(
+        wave_kernel,
+        out_shape=(array(1, 3, tile_r, tile_c),) * 2,
+        in_specs=[vmem] * 8,
+        out_specs=(vmem,) * 2,
+        scratch_shapes=[pltpu.VMEM(half_screens, jnp.float32)] * 2
+        + [pltpu.VMEM(field, jnp.float32), pltpu.VMEM((2, height, tile_c), jnp.float32)]
+        + [pltpu.VMEM((blocks, height, 4 * LANES), jnp.bfloat16)] * 2,
+        compiler_params=params(24),
+    )(
+        wave, near_cos, near_sin, near_measured, far_measured, far_phase,
+        jnp.asarray(row_constant(height)), jnp.asarray(col_constant()),
+    )
+    return pl.pallas_call(
+        finish_kernel,
+        out_shape=(array(*phase.shape), array(2, 1, 2, tile_r, tile_c)),
+        in_specs=[vmem, vmem],
+        out_specs=(hbm, hbm),
+        scratch_shapes=[pltpu.VMEM(phase.shape, jnp.float32), pltpu.SemaphoreType.DMA((3,))],
+        compiler_params=params(4),
+    )(mine, swap_cores(theirs))
 
 
 def extended_2(cells, sides, width):
@@ -93,7 +466,7 @@
     return lax.dynamic_update_slice(store, fresh, begin)
 
 
-def body(phase, tilt, intensity):
+def staged_body(phase, tilt, intensity):
     slices, tile_r, tile_c = phase.shape
     batch_size = tilt.shape[0]
     sections = lax.axis_size("depth")
@@ -177,12 +550,37 @@
     return (gradient, leaving)
 
 
+def fits_whole(phase_shape, batch, mesh):
+    slices, height, width = phase_shape
+    rows, cols, sections = mesh.shape["row"], mesh.shape["col"], mesh.shape["depth"]
+    return (
+        4 * height * width * (slices + batch) <= GATHER_BUDGET
+        and batch == rows == 2
+        and slices == sections
+        and sections & (sections - 1) == 0
+        and cols & (cols - 1) == 0
+        and height == LANES
+        and width == cols * LANES
+        and cols > 1
+        and sections > 1
+        and sections * HALO <= LANES
+    )
+
+
 def solution(mesh):
     placed = (P("depth", "row", "col"), P(), P(None, "row", "col"))
-    return jax.shard_map(
-        body,
-        mesh=mesh,
-        in_specs=placed,
-        out_specs=(P("depth", "row", "col"), P(None, "depth", None, "row", "col")),
-        check_vma=False,
-    )
+
+    def run(phase, tilt, intensity):
+        if fits_whole(phase.shape, tilt.shape[0], mesh):
+            body = whole_field_body
+        else:
+            body = staged_body
+        return jax.shard_map(
+            body,
+            mesh=mesh,
+            in_specs=placed,
+            out_specs=(P("depth", "row", "col"), P(None, "depth", None, "row", "col")),
+            check_vma=False,
+        )(phase, tilt, intensity)
+
+    return run

time: 221 us -> 36.7 us (0.17); the launches traced: 217 us -> 36.4 us
  starting transfers between devices: 141 us -> 14.1 us
  waiting for transfers between devices: 60.9 us -> 9.29 us
  Pallas kernels: 0 us -> 10.1 us
  matrix products: 7.06 us -> 0 us
    ppermute x50 -> x12, starting transfers between devices: 141 us -> 14.1 us  [the longest x9 13.7 us: spread(): lax.ppermute(shard, axis, [(i, i ^ bits) for i in range(size)])]
    ppermute x50 -> x12, waiting for transfers between devices: 60.9 us -> 9.29 us  [the longest x9 7.88 us: spread(): lax.ppermute(shard, axis, [(i, i ^ bits) for i in range(size)])]
    pallas_call x0 -> x4, Pallas kernels: none -> 10.1 us  [the longest x1 8.28 us: whole_field_body(): pl.pallas_call(wave_kernel, out_shape=(array(1, 3, tile_r, tile_c),) * 2,...]
    dot_general x20 -> x0, matrix products: 7.06 us -> none  [the longest x10 4.42 us: along_cols(): jnp.einsum('pqij,gqrj->gpri', matrix, window, precision=lax.Precision.HIG...]
  transfers between devices with their start and end apart: 50 -> 12, of which waited for: 40 -> 6; matrix products, arithmetic and copies ran while one was open for 0% -> 0% of each run, Pallas kernels for 0% -> 3%
where the time goes in v5:
time: 36.7 us; the launch traced here: 36.4 us
  starting transfers between devices  14.1 us (38%)
  Pallas kernels  10.1 us (28%)
  waiting for transfers between devices  9.29 us (25%)
  local copies, waits for them, and re-layouts  2.15 us (6%)
  between operations  0.72 us (2%)
    ppermute x9, starting transfers between devices, spread(): lax.ppermute(shard, axis, [(i, i ^ bits) for i in range(size)])  13.7 us
    pallas_call x1, Pallas kernels, whole_field_body(): pl.pallas_call(wave_kernel, out_shape=(array(1, 3, tile_r, tile_c),) * 2,...  8.28 us
    ppermute x9, waiting for transfers between devices, spread(): lax.ppermute(shard, axis, [(i, i ^ bits) for i in range(size)])  7.88 us
    unnamed x10, local copies, waits for them, and re-layouts  2.13 us
    ppermute x3, waiting for transfers between devices, swap_cores(): return lax.ppermute(value, 'row', [(0, 1), (1, 0)])  1.41 us
    pallas_call x1, Pallas kernels, whole_field_body(): pl.pallas_call(prepare_kernel, out_shape=(array(*field), array(*half_scre...  1.12 us
  transfers between devices with their start and end apart: 12, of which 6 were waited for; matrix products, arithmetic and copies ran while one was open for 0% of the time, Pallas kernels for 3%

profile of v5, /device:TPU:0, one launch (start us, length us, event | category | flops | bytes accessed | tf_op | source)
XLA Modules:
  0.0 36.4 jit_solution(8576227203810470018)
XLA Ops:
  0.6 3.1 %collective-permute-start = (f32[1,64,128]{2,1,0:T(8,128)}, f32[1,64,128]{2,1,0:T(8,128)S(1)}, u32[]{:S(2)}, u32[]{:S(2)}) collective-permute-start(f32[1,64,128]{2,1,0:T(8,128)} %from_ref.1), channel_id=1, source_target_pairs={{0,8},{8,0},{16,24},{24,16},{1,9},{9,1},{17,25},{25,17},{2,10},{10... | collective-permute-start | bytes 98312 | tf_op jit(solution)/shard_map/ppermute | solution.py:315
  3.7 2.5 %collective-permute-start.2 = (f32[1,64,128]{2,1,0:T(8,128)}, f32[1,64,128]{2,1,0:T(8,128)S(1)}, u32[]{:S(2)}, u32[]{:S(2)}) collective-permute-start(f32[1,64,128]{2,1,0:T(8,128)} %from_ref.1), channel_id=1, source_target_pairs={{0,24},{8,16},{16,8},{24,0},{1,25},{9,17},{17,9},{25,1},{2,26},{10... | collective-permute-start | bytes 98312 | tf_op jit(solution)/shard_map/ppermute | solution.py:315
  6.2 0.1 collective-permute-start.1
  6.3 1.5 %collective-permute-start.4 = (f32[2,64,128]{2,1,0:T(8,128)}, f32[2,64,128]{2,1,0:T(8,128)S(1)}, u32[]{:S(2)}, u32[]{:S(2)}) collective-permute-start(f32[2,64,128]{2,1,0:T(8,128)} %param.7), channel_id=1, source_target_pairs={{0,1},{1,0},{2,3},{3,2},{4,5},{5,4},{6,7},{7,6},{8,9},{9,8},{10,11... | collective-permute-start | bytes 196616 | tf_op jit(solution)/shard_map/ppermute | solution.py:315
  7.8 1.5 %collective-permute-start.6 = (f32[2,64,128]{2,1,0:T(8,128)}, f32[2,64,128]{2,1,0:T(8,128)S(1)}, u32[]{:S(2)}, u32[]{:S(2)}) collective-permute-start(f32[2,64,128]{2,1,0:T(8,128)} %param.7), channel_id=1, source_target_pairs={{0,3},{1,2},{2,1},{3,0},{4,7},{5,6},{6,5},{7,4},{8,11},{9,10},{10,... | collective-permute-start | bytes 196616 | tf_op jit(solution)/shard_map/ppermute | solution.py:315
  9.3 0.0 copy-start.2
  9.3 0.8 %copy-done.2 = f32[1,64,128]{2,1,0:T(8,128)S(1)} copy-done((f32[1,64,128]{2,1,0:T(8,128)S(1)}, f32[1,64,128]{2,1,0:T(8,128)}, u32[]{:S(2)}) %copy-start.2) | copy-done | bytes 32792
  10.1 0.0 copy-start.4
  10.1 0.0 collective-permute-done
  10.1 0.8 %copy-done.4 = f32[2,64,128]{2,1,0:T(8,128)S(1)} copy-done((f32[2,64,128]{2,1,0:T(8,128)S(1)}, f32[2,64,128]{2,1,0:T(8,128)}, u32[]{:S(2)}) %copy-start.4) | copy-done | bytes 65560
  10.9 0.5 %collective-permute-start.5 = (f32[2,64,128]{2,1,0:T(8,128)S(1)}, f32[2,64,128]{2,1,0:T(8,128)S(1)}, u32[]{:S(2)}, u32[]{:S(2)}) collective-permute-start(f32[2,64,128]{2,1,0:T(8,128)S(1)} %copy-done.4), channel_id=1, source_target_pairs={{0,2},{1,3},{2,0},{3,1},{4,6},{5,7},{6,4},{7,5},{8,10},{9,11},{10,... | collective-permute-start | bytes 196616 | tf_op jit(solution)/shard_map/ppermute | solution.py:315
  11.4 0.0 collective-permute-done.2
  11.4 0.2 collective-permute-done.1
  11.6 1.6 %collective-permute-start.3 = (f32[4,64,128]{2,1,0:T(8,128)S(1)}, f32[4,64,128]{2,1,0:T(8,128)S(1)}, u32[]{:S(2)}, u32[]{:S(2)}) collective-permute-start(f32[4,64,128]{2,1,0:T(8,128)S(1)} %get-tuple-element.17), channel_id=1, source_target_pairs={{0,1},{1,0},{2,3},{3,2},{4,5},{5,4},{6,7},{7,6},{8,9},{9,8},{10,11... | collective-permute-start | bytes 393224 | tf_op jit(solution)/shard_map/ppermute | solution.py:315
  13.1 0.0 collective-permute-done.4
  13.2 0.1 collective-permute-done.6
  13.3 1.9 %collective-permute-done.5 = f32[2,64,128]{2,1,0:T(8,128)S(1)} collective-permute-done((f32[2,64,128]{2,1,0:T(8,128)S(1)}, f32[2,64,128]{2,1,0:T(8,128)S(1)}, u32[]{:S(2)}, u32[]{:S(2)}) %collective-permute-start.5) | collective-permute-done | bytes 65568 | tf_op jit(solution)/shard_map/ppermute | solution.py:315
  15.2 0.1 collective-permute-start.7
  15.3 0.7 %collective-permute-start.8 = (f32[4,64,128]{2,1,0:T(8,128)S(1)}, f32[4,64,128]{2,1,0:T(8,128)S(1)}, u32[]{:S(2)}, u32[]{:S(2)}) collective-permute-start(f32[4,64,128]{2,1,0:T(8,128)S(1)} %get-tuple-element.17), channel_id=1, source_target_pairs={{0,2},{1,3},{2,0},{3,1},{4,6},{5,7},{6,4},{7,5},{8,10},{9,11},{10,... | collective-permute-start | bytes 393224 | tf_op jit(solution)/shard_map/ppermute | solution.py:315
  16.0 2.4 %collective-permute-start.9 = (f32[4,64,128]{2,1,0:T(8,128)S(1)}, f32[4,64,128]{2,1,0:T(8,128)S(1)}, u32[]{:S(2)}, u32[]{:S(2)}) collective-permute-start(f32[4,64,128]{2,1,0:T(8,128)S(1)} %get-tuple-element.17), channel_id=1, source_target_pairs={{0,3},{1,2},{2,1},{3,0},{4,7},{5,6},{6,5},{7,4},{8,11},{9,10},{10,... | collective-permute-start | bytes 393224 | tf_op jit(solution)/shard_map/ppermute | solution.py:315
  18.3 0.0 collective-permute-done.3
  18.3 0.0 collective-permute-done.7.far_measured
  18.3 5.7 %collective-permute-done.8 = f32[4,64,128]{2,1,0:T(8,128)S(1)} collective-permute-done((f32[4,64,128]{2,1,0:T(8,128)S(1)}, f32[4,64,128]{2,1,0:T(8,128)S(1)}, u32[]{:S(2)}, u32[]{:S(2)}) %collective-permute-start.8) | collective-permute-done | bytes 131104 | tf_op jit(solution)/shard_map/ppermute | solution.py:315
  24.0 0.0 collective-permute-done.9
  24.0 0.0 copy-start.3
  24.1 0.0 copy-start
  24.1 0.0 copy-start.1
  24.1 0.1 collective-permute-start.10
  24.2 0.5 %copy-done.3 = s32[2,2]{1,0:T(2,128)S(1)} copy-done((s32[2,2]{1,0:T(2,128)S(1)}, s32[2,2]{1,0:T(2,128)}, u32[]{:S(2)}) %copy-start.3) | copy-done | bytes 40
  24.7 1.1 %shard_map.69 = (f32[4,2,128,128]{3,2,1,0:T(8,128)S(1)}, f32[5,4,64,128]{3,2,1,0:T(8,128)S(1)}, f32[5,4,64,128]{3,2,1,0:T(8,128)S(1)}) custom-call(s32[2,2]{1,0:T(2,128)S(1)} %copy-done.3, f32[4,4,64,128]{3,2,1,0:T(8,128)S(1)} %pad_maximum_fusion.near_phase), custom_call_target="tpu_custom_call" | custom-call | flops 500000000 | bytes 1048576 | tf_op jit(solution)/shard_map/pallas_call | solution.py:354
  25.8 0.2 collective-permute-done.10.far_phase
  26.1 0.0 copy-done
  26.1 0.0 copy-done.1
  26.1 8.3 %shard_map.70 = (f32[1,3,64,128]{3,2,1,0:T(8,128)S(1)}, f32[1,3,64,128]{3,2,1,0:T(8,128)S(1)}) custom-call(f32[4,2,128,128]{3,2,1,0:T(8,128)S(1)} %get-tuple-element.10.wave_ref, f32[5,4,64,128]{3,2,1,0:T(8,128)S(1)} %get-tuple-element.11.near_cos, f32[5,4,64,128]{3,2,1,0:T(8,128)S(1)} %get-tuple-element.12.near_sin, ...), custom_call_target="tpu_custom_call" | custom-call | tf_op jit(solution)/shard_map/pallas_call | solution.py:362
  34.4 0.2 collective-permute-start.11
  34.6 1.2 %collective-permute-done.11.received_ref = f32[1,3,64,128]{3,2,1,0:T(8,128)S(1)} collective-permute-done((f32[1,3,64,128]{3,2,1,0:T(8,128)S(1)}, f32[1,3,64,128]{3,2,1,0:T(8,128)S(1)}, u32[]{:S(2)}, u32[]{:S(2)}) %collective-permute-start.11) | collective-permute-done | bytes 98336 | tf_op jit(solution)/shard_map/ppermute | solution.py:319
  35.7 0.7 %shard_map.71 = (f32[1,64,128]{2,1,0:T(8,128)}, f32[2,1,2,64,128]{4,3,2,1,0:T(8,128)}) custom-call(f32[1,3,64,128]{3,2,1,0:T(8,128)S(1)} %get-tuple-element.14.mine_ref, f32[1,3,64,128]{3,2,1,0:T(8,128)S(1)} %collective-permute-done.11.received_ref), custom_call_target="tpu_custom_call" | custom-call | tf_op jit(solution)/shard_map/pallas_call | solution.py:375
  (5 shorter events, 0.1 us)
Async XLA Ops:
  0.6 9.4 %collective-permute-start = (f32[1,64,128]{2,1,0:T(8,128)}, f32[1,64,128]{2,1,0:T(8,128)S(1)}, u32[]{:S(2)}, u32[]{:S(2)}) collective-permute-start(f32[1,64,128]{2,1,0:T(8,128)} %from_ref.1), channel_id=1, source_target_pairs={{0,8},{8,0},{16,24},{24,16},{1,9},{9,1},{17,25},{25,17},{2,10},{10... | collective-permute-start | bytes 98312 | tf_op jit(solution)/shard_map/ppermute | solution.py:315
  3.7 7.7 %collective-permute-start.2 = (f32[1,64,128]{2,1,0:T(8,128)}, f32[1,64,128]{2,1,0:T(8,128)S(1)}, u32[]{:S(2)}, u32[]{:S(2)}) collective-permute-start(f32[1,64,128]{2,1,0:T(8,128)} %from_ref.1), channel_id=1, source_target_pairs={{0,24},{8,16},{16,8},{24,0},{1,25},{9,17},{17,9},{25,1},{2,26},{10... | collective-permute-start | bytes 98312 | tf_op jit(solution)/shard_map/ppermute | solution.py:315
  6.2 5.4 %collective-permute-start.1 = (f32[1,64,128]{2,1,0:T(8,128)}, f32[1,64,128]{2,1,0:T(8,128)S(1)}, u32[]{:S(2)}, u32[]{:S(2)}) collective-permute-start(f32[1,64,128]{2,1,0:T(8,128)} %from_ref.1), channel_id=1, source_target_pairs={{0,16},{8,24},{16,0},{24,8},{1,17},{9,25},{17,1},{25,9},{2,18},{10... | collective-permute-start | bytes 98312 | tf_op jit(solution)/shard_map/ppermute | solution.py:315
  6.3 6.8 %collective-permute-start.4 = (f32[2,64,128]{2,1,0:T(8,128)}, f32[2,64,128]{2,1,0:T(8,128)S(1)}, u32[]{:S(2)}, u32[]{:S(2)}) collective-permute-start(f32[2,64,128]{2,1,0:T(8,128)} %param.7), channel_id=1, source_target_pairs={{0,1},{1,0},{2,3},{3,2},{4,5},{5,4},{6,7},{7,6},{8,9},{9,8},{10,11... | collective-permute-start | bytes 196616 | tf_op jit(solution)/shard_map/ppermute | solution.py:315
  7.8 5.5 %collective-permute-start.6 = (f32[2,64,128]{2,1,0:T(8,128)}, f32[2,64,128]{2,1,0:T(8,128)S(1)}, u32[]{:S(2)}, u32[]{:S(2)}) collective-permute-start(f32[2,64,128]{2,1,0:T(8,128)} %param.7), channel_id=1, source_target_pairs={{0,3},{1,2},{2,1},{3,0},{4,7},{5,6},{6,5},{7,4},{8,11},{9,10},{10,... | collective-permute-start | bytes 196616 | tf_op jit(solution)/shard_map/ppermute | solution.py:315
  9.3 0.8 %copy-start.2 = (f32[1,64,128]{2,1,0:T(8,128)S(1)}, f32[1,64,128]{2,1,0:T(8,128)}, u32[]{:S(2)}) copy-start(f32[1,64,128]{2,1,0:T(8,128)} %from_ref.1) | copy-start | bytes 98308
  10.1 0.8 %copy-start.4 = (f32[2,64,128]{2,1,0:T(8,128)S(1)}, f32[2,64,128]{2,1,0:T(8,128)}, u32[]{:S(2)}) copy-start(f32[2,64,128]{2,1,0:T(8,128)} %param.7) | copy-start | bytes 196612
  10.9 4.3 %collective-permute-start.5 = (f32[2,64,128]{2,1,0:T(8,128)S(1)}, f32[2,64,128]{2,1,0:T(8,128)S(1)}, u32[]{:S(2)}, u32[]{:S(2)}) collective-permute-start(f32[2,64,128]{2,1,0:T(8,128)S(1)} %copy-done.4), channel_id=1, source_target_pairs={{0,2},{1,3},{2,0},{3,1},{4,6},{5,7},{6,4},{7,5},{8,10},{9,11},{10,... | collective-permute-start | bytes 196616 | tf_op jit(solution)/shard_map/ppermute | solution.py:315
  11.6 6.7 %collective-permute-start.3 = (f32[4,64,128]{2,1,0:T(8,128)S(1)}, f32[4,64,128]{2,1,0:T(8,128)S(1)}, u32[]{:S(2)}, u32[]{:S(2)}) collective-permute-start(f32[4,64,128]{2,1,0:T(8,128)S(1)} %get-tuple-element.17), channel_id=1, source_target_pairs={{0,1},{1,0},{2,3},{3,2},{4,5},{5,4},{6,7},{7,6},{8,9},{9,8},{10,11... | collective-permute-start | bytes 393224 | tf_op jit(solution)/shard_map/ppermute | solution.py:315
  15.2 3.1 %collective-permute-start.7 = (f32[4,1,64,128]{3,2,1,0:T(8,128)S(1)}, f32[4,1,64,128]{3,2,1,0:T(8,128)S(1)}, u32[]{:S(2)}, u32[]{:S(2)}) collective-permute-start(f32[4,1,64,128]{3,2,1,0:T(8,128)S(1)} %constant_dynamic-slice_fusion), channel_id=1, source_target_pairs={{0,4},{4,0},{1,5},{5,1},{2,6},{6,2},{3,7},{7,3},{8,12},{12,8},{9,1... | collective-permute-start | bytes 393224 | tf_op jit(solution)/shard_map/ppermute | solution.py:319
  15.3 8.7 %collective-permute-start.8 = (f32[4,64,128]{2,1,0:T(8,128)S(1)}, f32[4,64,128]{2,1,0:T(8,128)S(1)}, u32[]{:S(2)}, u32[]{:S(2)}) collective-permute-start(f32[4,64,128]{2,1,0:T(8,128)S(1)} %get-tuple-element.17), channel_id=1, source_target_pairs={{0,2},{1,3},{2,0},{3,1},{4,6},{5,7},{6,4},{7,5},{8,10},{9,11},{10,... | collective-permute-start | bytes 393224 | tf_op jit(solution)/shard_map/ppermute | solution.py:315
  16.0 8.1 %collective-permute-start.9 = (f32[4,64,128]{2,1,0:T(8,128)S(1)}, f32[4,64,128]{2,1,0:T(8,128)S(1)}, u32[]{:S(2)}, u32[]{:S(2)}) collective-permute-start(f32[4,64,128]{2,1,0:T(8,128)S(1)} %get-tuple-element.17), channel_id=1, source_target_pairs={{0,3},{1,2},{2,1},{3,0},{4,7},{5,6},{6,5},{7,4},{8,11},{9,10},{10,... | collective-permute-start | bytes 393224 | tf_op jit(solution)/shard_map/ppermute | solution.py:315
  24.0 0.7 %copy-start.3 = (s32[2,2]{1,0:T(2,128)S(1)}, s32[2,2]{1,0:T(2,128)}, u32[]{:S(2)}) copy-start(s32[2,2]{1,0:T(2,128)} %tilt_ref.1) | copy-start | bytes 52
  24.1 2.0 %copy-start = (bf16[1024,256]{1,0:T(8,128)(2,1)S(1)}, bf16[1024,256]{1,0:T(8,128)(2,1)}, u32[]{:S(2)}) copy-start(bf16[1024,256]{1,0:T(8,128)(2,1)} %constant.18.clone.col_ref) | copy-start | bytes 1572868
  24.1 2.0 %copy-start.1 = (bf16[2,256,512]{2,1,0:T(8,128)(2,1)S(1)}, bf16[2,256,512]{2,1,0:T(8,128)(2,1)}, u32[]{:S(2)}) copy-start(bf16[2,256,512]{2,1,0:T(8,128)(2,1)} %constant.17.clone.row_ref) | copy-start | bytes 1572868
  24.1 2.0 %collective-permute-start.10 = (f32[4,4,64,128]{3,2,1,0:T(8,128)S(1)}, f32[4,4,64,128]{3,2,1,0:T(8,128)S(1)}, u32[]{:S(2)}, u32[]{:S(2)}) collective-permute-start(f32[4,4,64,128]{3,2,1,0:T(8,128)S(1)} %pad_maximum_fusion.near_phase), channel_id=1, source_target_pairs={{0,4},{4,0},{1,5},{5,1},{2,6},{6,2},{3,7},{7,3},{8,12},{12,8},{9,1... | collective-permute-start | bytes 1572872 | tf_op jit(solution)/shard_map/ppermute | solution.py:319
  34.4 1.4 %collective-permute-start.11 = (f32[1,3,64,128]{3,2,1,0:T(8,128)S(1)}, f32[1,3,64,128]{3,2,1,0:T(8,128)S(1)}, u32[]{:S(2)}, u32[]{:S(2)}) collective-permute-start(f32[1,3,64,128]{3,2,1,0:T(8,128)S(1)} %get-tuple-element.15), channel_id=1, source_target_pairs={{0,4},{4,0},{1,5},{5,1},{2,6},{6,2},{3,7},{7,3},{8,12},{12,8},{9,1... | collective-permute-start | bytes 294920 | tf_op jit(solution)/shard_map/ppermute | solution.py:319

commit v6 on v5

--- a/solution.py
+++ b/solution.py
@@ -175,7 +175,7 @@
         a_ref[place, :, pl.ds(begin, half)] = jnp.zeros((a_ref.shape[1], half), a_ref.dtype)
 
 
-def prepare_kernel(tilt_ref, near_phase, wave_ref, cos_ref, sin_ref):
+def prepare_kernel(tilt_ref, near_phase, all_measured, wave_ref, cos_ref, sin_ref, measured_ref):
     blocks, _, height, _ = wave_ref.shape
     count = cos_ref.shape[0] - 1
     core, own_section, own_place = lax.axis_index("row"), lax.axis_index("depth"), lax.axis_index("col")
@@ -184,6 +184,7 @@
         held = col ^ own_place
         for bits in range(count):
             cos_ref[bits ^ own_section, col], sin_ref[bits ^ own_section, col] = cos_sin(near_phase[held, bits])
+        measured_ref[col] = all_measured[held].reshape(height, LANES)
         return carry
 
     lax.fori_loop(0, blocks, screens, 0)
@@ -209,7 +210,7 @@
 
 
 def wave_kernel(
-    wave_ref, near_cos, near_sin, near_measured, far_measured, far_phase, row_ref, col_ref,
+    wave_ref, near_cos, near_sin, measured_ref, far_phase, row_ref, col_ref,
     mine_ref, theirs_ref, far_cos, far_sin, v_ref, moved_ref, a_high, a_low,
 ):
     blocks, _, height, _ = v_ref.shape
@@ -256,12 +257,10 @@
         clear_edge(target, window - 1, True)
     for place in range(window):
         block = window_start + place
-        held = block ^ own_place
-        for row, measured in ((near, near_measured[held, core]), (far, far_measured[held, 0])):
-            real, imag = v_ref[block, 0, row], v_ref[block, 1, row]
-            misfit = 2.0 * (real * real + imag * imag - measured)
-            v_ref[block, 0, row] = misfit * real
-            v_ref[block, 1, row] = -misfit * imag
+        real, imag = v_ref[block, 0], v_ref[block, 1]
+        misfit = 2.0 * (real * real + imag * imag - measured_ref[block])
+        v_ref[block, 0] = misfit * real
+        v_ref[block, 1] = -misfit * imag
 
     def backward(tick, carry):
         advance(count - tick, window_start, window, screens, row_matrix[...], col_ref, v_ref, a_high, a_low)
@@ -342,34 +341,33 @@
         compiler_params=params(1),
     )(phase)
     column = jnp.concatenate([own_phase] + spread(phase, "depth"), axis=0)
-    near_measured = jnp.stack([intensity] + spread(intensity, "col"))
-    far_measured = swap_cores(lax.dynamic_slice_in_dim(near_measured, 1 - core, 1, 1))
-    arriving = spread(column, "col")
-    arriving[0], far_measured = lax.optimization_barrier((arriving[0], far_measured))
-    near_phase = jnp.stack([column] + arriving)
+    own_tilt = [lax.dynamic_index_in_dim(both, core, 0, False) for both in (intensity, swap_cores(intensity))]
+    tile_measured = jnp.stack(own_tilt)
+    near_phase = jnp.stack([column] + spread(column, "col"))
+    all_measured = jnp.stack([tile_measured] + spread(tile_measured, "col"))
     far_phase = swap_cores(near_phase)
 
     half_screens = (count + 1, blocks, tile_r, tile_c)
     field = (blocks, 2, height, tile_c)
-    wave, near_cos, near_sin = pl.pallas_call(
+    wave, near_cos, near_sin, measured = pl.pallas_call(
         prepare_kernel,
-        out_shape=(array(*field), array(*half_screens), array(*half_screens)),
-        in_specs=[smem, vmem],
-        out_specs=(vmem,) * 3,
+        out_shape=(array(*field), array(*half_screens), array(*half_screens), array(blocks, height, tile_c)),
+        in_specs=[smem, vmem, vmem],
+        out_specs=(vmem,) * 4,
         compiler_params=params(8),
-        cost_estimate=pl.CostEstimate(flops=5 * 10**8, bytes_accessed=2**20, transcendentals=0),
-    )(tilt, near_phase)
+        cost_estimate=pl.CostEstimate(flops=4 * 10**9, bytes_accessed=2**20, transcendentals=0),
+    )(tilt, near_phase, all_measured)
     mine, theirs = pl.pallas_call(
         wave_kernel,
         out_shape=(array(1, 3, tile_r, tile_c),) * 2,
-        in_specs=[vmem] * 8,
+        in_specs=[vmem] * 7,
         out_specs=(vmem,) * 2,
         scratch_shapes=[pltpu.VMEM(half_screens, jnp.float32)] * 2
         + [pltpu.VMEM(field, jnp.float32), pltpu.VMEM((2, height, tile_c), jnp.float32)]
         + [pltpu.VMEM((blocks, height, 4 * LANES), jnp.bfloat16)] * 2,
         compiler_params=params(24),
     )(
-        wave, near_cos, near_sin, near_measured, far_measured, far_phase,
+        wave, near_cos, near_sin, measured, far_phase,
         jnp.asarray(row_constant(height)), jnp.asarray(col_constant()),
     )
     return pl.pallas_call(

time: 36.7 us -> 36.5 us (level)
  local copies, waits for them, and re-layouts: 2.15 us -> 1.52 us
  starting transfers between devices: 14.1 us -> 14.7 us
    unnamed x10 -> x8, local copies, waits for them, and re-layouts: 2.13 us -> 0.75 us
    ppermute x9, starting transfers between devices: 13.7 us -> 14.6 us  [spread(): lax.ppermute(shard, axis, [(i, i ^ bits) for i in range(size)])]
    dynamic_slice x1 -> x2, local copies, waits for them, and re-layouts: 0.02 us -> 0.78 us  [whole_field_body(): lax.dynamic_index_in_dim(both, core, 0, False)]
  transfers between devices with their start and end apart: 12 -> 12, of which waited for: 6 -> 6; matrix products, arithmetic and copies ran while one was open for 0% -> 2% of each run, Pallas kernels for 3% -> 3%
where the time goes in v6:
time: 36.5 us; the launch traced here: 36.3 us
  starting transfers between devices  14.7 us (40%)
  Pallas kernels  10.1 us (28%)
  waiting for transfers between devices  9.15 us (25%)
  local copies, waits for them, and re-layouts  1.52 us (4%)
  between operations  0.72 us (2%)
    ppermute x9, starting transfers between devices, spread(): lax.ppermute(shard, axis, [(i, i ^ bits) for i in range(size)])  14.6 us
    pallas_call x1, Pallas kernels, whole_field_body(): pl.pallas_call(wave_kernel, out_shape=(array(1, 3, tile_r, tile_c),) * 2,...  8.29 us
    ppermute x9, waiting for transfers between devices, spread(): lax.ppermute(shard, axis, [(i, i ^ bits) for i in range(size)])  7.86 us
    ppermute x3, waiting for transfers between devices, swap_cores(): return lax.ppermute(value, 'row', [(0, 1), (1, 0)])  1.29 us
    pallas_call x1, Pallas kernels, whole_field_body(): pl.pallas_call(prepare_kernel, out_shape=(array(*field), array(*half_scre...  1.13 us
    dynamic_slice x2, local copies, waits for them, and re-layouts, whole_field_body(): lax.dynamic_index_in_dim(both, core, 0, False)  0.78 us
    unnamed x8, local copies, waits for them, and re-layouts  0.75 us
  transfers between devices with their start and end apart: 12, of which 6 were waited for; matrix products, arithmetic and copies ran while one was open for 2% of the time, Pallas kernels for 3%

profile of v6, /device:TPU:0, one launch (start us, length us, event | category | flops | bytes accessed | tf_op | source)
XLA Modules:
  0.0 36.3 jit_solution(9062030295366376675)
XLA Ops:
  0.6 3.1 %collective-permute-start = (f32[1,64,128]{2,1,0:T(8,128)}, f32[1,64,128]{2,1,0:T(8,128)S(1)}, u32[]{:S(2)}, u32[]{:S(2)}) collective-permute-start(f32[1,64,128]{2,1,0:T(8,128)} %from_ref.1), channel_id=1, source_target_pairs={{0,8},{8,0},{16,24},{24,16},{1,9},{9,1},{17,25},{25,17},{2,10},{10... | collective-permute-start | bytes 98312 | tf_op jit(solution)/shard_map/ppermute | solution.py:314
  3.7 2.6 %collective-permute-start.1 = (f32[1,64,128]{2,1,0:T(8,128)}, f32[1,64,128]{2,1,0:T(8,128)S(1)}, u32[]{:S(2)}, u32[]{:S(2)}) collective-permute-start(f32[1,64,128]{2,1,0:T(8,128)} %from_ref.1), channel_id=1, source_target_pairs={{0,16},{8,24},{16,0},{24,8},{1,17},{9,25},{17,1},{25,9},{2,18},{10... | collective-permute-start | bytes 98312 | tf_op jit(solution)/shard_map/ppermute | solution.py:314
  6.3 0.0 collective-permute-start.2
  6.3 0.0 collective-permute-start.6
  6.3 0.0 copy-start.2
  6.3 0.8 %constant_dynamic-slice_fusion.1 = f32[1,64,128]{2,1,0:T(8,128)S(1)} fusion(f32[2,64,128]{2,1,0:T(8,128)} %param.7, s32[]{:T(128)S(6)} %select_n.5), kind=kLoop, calls=%fused_computation.5 | loop fusion | bytes 65540 | tf_op jit(solution)/shard_map/jit(dynamic_index_in_dim)/dynamic_slice | solution.py:344
  7.1 0.0 copy-done.2
  7.1 0.0 collective-permute-done
  7.1 2.2 %collective-permute-done.1 = f32[1,64,128]{2,1,0:T(8,128)S(1)} collective-permute-done((f32[1,64,128]{2,1,0:T(8,128)}, f32[1,64,128]{2,1,0:T(8,128)S(1)}, u32[]{:S(2)}, u32[]{:S(2)}) %collective-permute-start.1) | collective-permute-done | bytes 32800 | tf_op jit(solution)/shard_map/ppermute | solution.py:314
  9.3 2.9 %collective-permute-done.2 = f32[1,64,128]{2,1,0:T(8,128)S(1)} collective-permute-done((f32[1,64,128]{2,1,0:T(8,128)}, f32[1,64,128]{2,1,0:T(8,128)S(1)}, u32[]{:S(2)}, u32[]{:S(2)}) %collective-permute-start.2) | collective-permute-done | bytes 32800 | tf_op jit(solution)/shard_map/ppermute | solution.py:314
  12.3 1.6 %collective-permute-start.3 = (f32[4,64,128]{2,1,0:T(8,128)S(1)}, f32[4,64,128]{2,1,0:T(8,128)S(1)}, u32[]{:S(2)}, u32[]{:S(2)}) collective-permute-start(f32[4,64,128]{2,1,0:T(8,128)S(1)} %get-tuple-element.15), channel_id=1, source_target_pairs={{0,1},{1,0},{2,3},{3,2},{4,5},{5,4},{6,7},{7,6},{8,9},{9,8},{10,11... | collective-permute-start | bytes 393224 | tf_op jit(solution)/shard_map/ppermute | solution.py:314
  13.8 1.5 %collective-permute-start.4 = (f32[4,64,128]{2,1,0:T(8,128)S(1)}, f32[4,64,128]{2,1,0:T(8,128)S(1)}, u32[]{:S(2)}, u32[]{:S(2)}) collective-permute-start(f32[4,64,128]{2,1,0:T(8,128)S(1)} %get-tuple-element.15), channel_id=1, source_target_pairs={{0,2},{1,3},{2,0},{3,1},{4,6},{5,7},{6,4},{7,5},{8,10},{9,11},{10,... | collective-permute-start | bytes 393224 | tf_op jit(solution)/shard_map/ppermute | solution.py:314
  15.3 0.5 %collective-permute-start.5 = (f32[4,64,128]{2,1,0:T(8,128)S(1)}, f32[4,64,128]{2,1,0:T(8,128)S(1)}, u32[]{:S(2)}, u32[]{:S(2)}) collective-permute-start(f32[4,64,128]{2,1,0:T(8,128)S(1)} %get-tuple-element.15), channel_id=1, source_target_pairs={{0,3},{1,2},{2,1},{3,0},{4,7},{5,6},{6,5},{7,4},{8,11},{9,10},{10,... | collective-permute-start | bytes 393224 | tf_op jit(solution)/shard_map/ppermute | solution.py:314
  15.8 0.0 collective-permute-done.6
  15.8 1.6 %collective-permute-start.7 = (f32[2,64,128]{2,1,0:T(8,128)S(1)}, f32[2,64,128]{2,1,0:T(8,128)S(1)}, u32[]{:S(2)}, u32[]{:S(2)}) collective-permute-start(f32[2,64,128]{2,1,0:T(8,128)S(1)} %get-tuple-element.17), channel_id=1, source_target_pairs={{0,1},{1,0},{2,3},{3,2},{4,5},{5,4},{6,7},{7,6},{8,9},{9,8},{10,11... | collective-permute-start | bytes 196616 | tf_op jit(solution)/shard_map/ppermute | solution.py:314
  17.4 1.5 %collective-permute-start.8 = (f32[2,64,128]{2,1,0:T(8,128)S(1)}, f32[2,64,128]{2,1,0:T(8,128)S(1)}, u32[]{:S(2)}, u32[]{:S(2)}) collective-permute-start(f32[2,64,128]{2,1,0:T(8,128)S(1)} %get-tuple-element.17), channel_id=1, source_target_pairs={{0,2},{1,3},{2,0},{3,1},{4,6},{5,7},{6,4},{7,5},{8,10},{9,11},{10,... | collective-permute-start | bytes 196616 | tf_op jit(solution)/shard_map/ppermute | solution.py:314
  18.9 0.0 collective-permute-done.3
  18.9 2.3 %collective-permute-start.9 = (f32[2,64,128]{2,1,0:T(8,128)S(1)}, f32[2,64,128]{2,1,0:T(8,128)S(1)}, u32[]{:S(2)}, u32[]{:S(2)}) collective-permute-start(f32[2,64,128]{2,1,0:T(8,128)S(1)} %get-tuple-element.17), channel_id=1, source_target_pairs={{0,3},{1,2},{2,1},{3,0},{4,7},{5,6},{6,5},{7,4},{8,11},{9,10},{10,... | collective-permute-start | bytes 196616 | tf_op jit(solution)/shard_map/ppermute | solution.py:314
  21.2 1.1 %collective-permute-done.4 = f32[4,64,128]{2,1,0:T(8,128)S(1)} collective-permute-done((f32[4,64,128]{2,1,0:T(8,128)S(1)}, f32[4,64,128]{2,1,0:T(8,128)S(1)}, u32[]{:S(2)}, u32[]{:S(2)}) %collective-permute-start.4) | collective-permute-done | bytes 131104 | tf_op jit(solution)/shard_map/ppermute | solution.py:314
  22.2 0.0 collective-permute-done.5
  22.3 0.1 collective-permute-start.10
  22.4 0.0 collective-permute-done.7
  22.4 0.6 %collective-permute-done.8 = f32[2,64,128]{2,1,0:T(8,128)S(1)} collective-permute-done((f32[2,64,128]{2,1,0:T(8,128)S(1)}, f32[2,64,128]{2,1,0:T(8,128)S(1)}, u32[]{:S(2)}, u32[]{:S(2)}) %collective-permute-start.8) | collective-permute-done | bytes 65568 | tf_op jit(solution)/shard_map/ppermute | solution.py:314
  22.9 1.1 %collective-permute-done.9 = f32[2,64,128]{2,1,0:T(8,128)S(1)} collective-permute-done((f32[2,64,128]{2,1,0:T(8,128)S(1)}, f32[2,64,128]{2,1,0:T(8,128)S(1)}, u32[]{:S(2)}, u32[]{:S(2)}) %collective-permute-start.9) | collective-permute-done | bytes 65568 | tf_op jit(solution)/shard_map/ppermute | solution.py:314
  24.1 0.0 copy-start.3
  24.1 0.7 %copy-done.3 = s32[2,2]{1,0:T(2,128)S(1)} copy-done((s32[2,2]{1,0:T(2,128)S(1)}, s32[2,2]{1,0:T(2,128)}, u32[]{:S(2)}) %copy-start.3) | copy-done | bytes 40
  24.8 0.0 copy-start
  24.8 0.0 copy-start.1
  24.8 1.1 %shard_map.69 = (f32[4,2,128,128]{3,2,1,0:T(8,128)S(1)}, f32[5,4,64,128]{3,2,1,0:T(8,128)S(1)}, f32[5,4,64,128]{3,2,1,0:T(8,128)S(1)}, f32[4,128,128]{2,1,0:T(8,128)S(1)}) custom-call(s32[2,2]{1,0:T(2,128)S(1)} %copy-done.3, f32[4,4,64,128]{3,2,1,0:T(8,128)S(1)} %pad_maximum_fusion.near_phase, f32[4,2,64,128]{3,2,1,0:T(8,128)S(1)} %pad_maximum_fusion.1.all_measured), custom_call_target="tpu_custom_call" | custom-call | flops 4000000000 | bytes 1048576 | tf_op jit(solution)/shard_map/pallas_call | solution.py:352
  25.9 0.0 collective-permute-done.10.far_phase
  25.9 0.0 copy-done
  25.9 0.0 copy-done.1
  26.0 8.3 %shard_map.70 = (f32[1,3,64,128]{3,2,1,0:T(8,128)S(1)}, f32[1,3,64,128]{3,2,1,0:T(8,128)S(1)}) custom-call(f32[4,2,128,128]{3,2,1,0:T(8,128)S(1)} %get-tuple-element.8.wave_ref, f32[5,4,64,128]{3,2,1,0:T(8,128)S(1)} %get-tuple-element.9.near_cos, f32[5,4,64,128]{3,2,1,0:T(8,128)S(1)} %get-tuple-element.10.near_sin, ...), custom_call_target="tpu_custom_call" | custom-call | tf_op jit(solution)/shard_map/pallas_call | solution.py:360
  34.2 0.1 collective-permute-start.11
  34.3 1.3 %collective-permute-done.11.received_ref = f32[1,3,64,128]{3,2,1,0:T(8,128)S(1)} collective-permute-done((f32[1,3,64,128]{3,2,1,0:T(8,128)S(1)}, f32[1,3,64,128]{3,2,1,0:T(8,128)S(1)}, u32[]{:S(2)}, u32[]{:S(2)}) %collective-permute-start.11) | collective-permute-done | bytes 98336 | tf_op jit(solution)/shard_map/ppermute | solution.py:318
  35.6 0.7 %shard_map.71 = (f32[1,64,128]{2,1,0:T(8,128)}, f32[2,1,2,64,128]{4,3,2,1,0:T(8,128)}) custom-call(f32[1,3,64,128]{3,2,1,0:T(8,128)S(1)} %get-tuple-element.12.mine_ref, f32[1,3,64,128]{3,2,1,0:T(8,128)S(1)} %collective-permute-done.11.received_ref), custom_call_target="tpu_custom_call" | custom-call | tf_op jit(solution)/shard_map/pallas_call | solution.py:373
  (6 shorter events, 0.1 us)
Async XLA Ops:
  0.6 6.5 %collective-permute-start = (f32[1,64,128]{2,1,0:T(8,128)}, f32[1,64,128]{2,1,0:T(8,128)S(1)}, u32[]{:S(2)}, u32[]{:S(2)}) collective-permute-start(f32[1,64,128]{2,1,0:T(8,128)} %from_ref.1), channel_id=1, source_target_pairs={{0,8},{8,0},{16,24},{24,16},{1,9},{9,1},{17,25},{25,17},{2,10},{10... | collective-permute-start | bytes 98312 | tf_op jit(solution)/shard_map/ppermute | solution.py:314
  3.7 5.6 %collective-permute-start.1 = (f32[1,64,128]{2,1,0:T(8,128)}, f32[1,64,128]{2,1,0:T(8,128)S(1)}, u32[]{:S(2)}, u32[]{:S(2)}) collective-permute-start(f32[1,64,128]{2,1,0:T(8,128)} %from_ref.1), channel_id=1, source_target_pairs={{0,16},{8,24},{16,0},{24,8},{1,17},{9,25},{17,1},{25,9},{2,18},{10... | collective-permute-start | bytes 98312 | tf_op jit(solution)/shard_map/ppermute | solution.py:314
  6.3 5.9 %collective-permute-start.2 = (f32[1,64,128]{2,1,0:T(8,128)}, f32[1,64,128]{2,1,0:T(8,128)S(1)}, u32[]{:S(2)}, u32[]{:S(2)}) collective-permute-start(f32[1,64,128]{2,1,0:T(8,128)} %from_ref.1), channel_id=1, source_target_pairs={{0,24},{8,16},{16,8},{24,0},{1,25},{9,17},{17,9},{25,1},{2,26},{10... | collective-permute-start | bytes 98312 | tf_op jit(solution)/shard_map/ppermute | solution.py:314
  6.3 9.5 %collective-permute-start.6 = (f32[2,64,128]{2,1,0:T(8,128)}, f32[2,64,128]{2,1,0:T(8,128)S(1)}, u32[]{:S(2)}, u32[]{:S(2)}) collective-permute-start(f32[2,64,128]{2,1,0:T(8,128)} %param.7), channel_id=1, source_target_pairs={{0,4},{4,0},{1,5},{5,1},{2,6},{6,2},{3,7},{7,3},{8,12},{12,8},{9,1... | collective-permute-start | bytes 196616 | tf_op jit(solution)/shard_map/ppermute | solution.py:318
  6.3 0.8 %copy-start.2 = (f32[1,64,128]{2,1,0:T(8,128)S(1)}, f32[1,64,128]{2,1,0:T(8,128)}, u32[]{:S(2)}) copy-start(f32[1,64,128]{2,1,0:T(8,128)} %from_ref.1) | copy-start | bytes 98308
  12.3 6.7 %collective-permute-start.3 = (f32[4,64,128]{2,1,0:T(8,128)S(1)}, f32[4,64,128]{2,1,0:T(8,128)S(1)}, u32[]{:S(2)}, u32[]{:S(2)}) collective-permute-start(f32[4,64,128]{2,1,0:T(8,128)S(1)} %get-tuple-element.15), channel_id=1, source_target_pairs={{0,1},{1,0},{2,3},{3,2},{4,5},{5,4},{6,7},{7,6},{8,9},{9,8},{10,11... | collective-permute-start | bytes 393224 | tf_op jit(solution)/shard_map/ppermute | solution.py:314
  13.8 8.4 %collective-permute-start.4 = (f32[4,64,128]{2,1,0:T(8,128)S(1)}, f32[4,64,128]{2,1,0:T(8,128)S(1)}, u32[]{:S(2)}, u32[]{:S(2)}) collective-permute-start(f32[4,64,128]{2,1,0:T(8,128)S(1)} %get-tuple-element.15), channel_id=1, source_target_pairs={{0,2},{1,3},{2,0},{3,1},{4,6},{5,7},{6,4},{7,5},{8,10},{9,11},{10,... | collective-permute-start | bytes 393224 | tf_op jit(solution)/shard_map/ppermute | solution.py:314
  15.3 6.9 %collective-permute-start.5 = (f32[4,64,128]{2,1,0:T(8,128)S(1)}, f32[4,64,128]{2,1,0:T(8,128)S(1)}, u32[]{:S(2)}, u32[]{:S(2)}) collective-permute-start(f32[4,64,128]{2,1,0:T(8,128)S(1)} %get-tuple-element.15), channel_id=1, source_target_pairs={{0,3},{1,2},{2,1},{3,0},{4,7},{5,6},{6,5},{7,4},{8,11},{9,10},{10,... | collective-permute-start | bytes 393224 | tf_op jit(solution)/shard_map/ppermute | solution.py:314
  15.8 6.5 %collective-permute-start.7 = (f32[2,64,128]{2,1,0:T(8,128)S(1)}, f32[2,64,128]{2,1,0:T(8,128)S(1)}, u32[]{:S(2)}, u32[]{:S(2)}) collective-permute-start(f32[2,64,128]{2,1,0:T(8,128)S(1)} %get-tuple-element.17), channel_id=1, source_target_pairs={{0,1},{1,0},{2,3},{3,2},{4,5},{5,4},{6,7},{7,6},{8,9},{9,8},{10,11... | collective-permute-start | bytes 196616 | tf_op jit(solution)/shard_map/ppermute | solution.py:314
  17.4 5.6 %collective-permute-start.8 = (f32[2,64,128]{2,1,0:T(8,128)S(1)}, f32[2,64,128]{2,1,0:T(8,128)S(1)}, u32[]{:S(2)}, u32[]{:S(2)}) collective-permute-start(f32[2,64,128]{2,1,0:T(8,128)S(1)} %get-tuple-element.17), channel_id=1, source_target_pairs={{0,2},{1,3},{2,0},{3,1},{4,6},{5,7},{6,4},{7,5},{8,10},{9,11},{10,... | collective-permute-start | bytes 196616 | tf_op jit(solution)/shard_map/ppermute | solution.py:314
  18.9 5.2 %collective-permute-start.9 = (f32[2,64,128]{2,1,0:T(8,128)S(1)}, f32[2,64,128]{2,1,0:T(8,128)S(1)}, u32[]{:S(2)}, u32[]{:S(2)}) collective-permute-start(f32[2,64,128]{2,1,0:T(8,128)S(1)} %get-tuple-element.17), channel_id=1, source_target_pairs={{0,3},{1,2},{2,1},{3,0},{4,7},{5,6},{6,5},{7,4},{8,11},{9,10},{10,... | collective-permute-start | bytes 196616 | tf_op jit(solution)/shard_map/ppermute | solution.py:314
  22.3 3.6 %collective-permute-start.10 = (f32[4,4,64,128]{3,2,1,0:T(8,128)S(1)}, f32[4,4,64,128]{3,2,1,0:T(8,128)S(1)}, u32[]{:S(2)}, u32[]{:S(2)}) collective-permute-start(f32[4,4,64,128]{3,2,1,0:T(8,128)S(1)} %pad_maximum_fusion.near_phase), channel_id=1, source_target_pairs={{0,4},{4,0},{1,5},{5,1},{2,6},{6,2},{3,7},{7,3},{8,12},{12,8},{9,1... | collective-permute-start | bytes 1572872 | tf_op jit(solution)/shard_map/ppermute | solution.py:318
  24.1 0.7 %copy-start.3 = (s32[2,2]{1,0:T(2,128)S(1)}, s32[2,2]{1,0:T(2,128)}, u32[]{:S(2)}) copy-start(s32[2,2]{1,0:T(2,128)} %tilt_ref.1) | copy-start | bytes 52
  24.8 1.2 %copy-start = (bf16[2,256,512]{2,1,0:T(8,128)(2,1)S(1)}, bf16[2,256,512]{2,1,0:T(8,128)(2,1)}, u32[]{:S(2)}) copy-start(bf16[2,256,512]{2,1,0:T(8,128)(2,1)} %constant.18.clone.row_ref) | copy-start | bytes 1572868
  24.8 1.2 %copy-start.1 = (bf16[1024,256]{1,0:T(8,128)(2,1)S(1)}, bf16[1024,256]{1,0:T(8,128)(2,1)}, u32[]{:S(2)}) copy-start(bf16[1024,256]{1,0:T(8,128)(2,1)} %constant.19.clone.col_ref) | copy-start | bytes 1572868
  34.2 1.4 %collective-permute-start.11 = (f32[1,3,64,128]{3,2,1,0:T(8,128)S(1)}, f32[1,3,64,128]{3,2,1,0:T(8,128)S(1)}, u32[]{:S(2)}, u32[]{:S(2)}) collective-permute-start(f32[1,3,64,128]{3,2,1,0:T(8,128)S(1)} %get-tuple-element.13), channel_id=1, source_target_pairs={{0,4},{4,0},{1,5},{5,1},{2,6},{6,2},{3,7},{7,3},{8,12},{12,8},{9,1... | collective-permute-start | bytes 294920 | tf_op jit(solution)/shard_map/ppermute | solution.py:318

commit v7 on v5

--- a/solution.py
+++ b/solution.py
@@ -175,7 +175,7 @@
         a_ref[place, :, pl.ds(begin, half)] = jnp.zeros((a_ref.shape[1], half), a_ref.dtype)
 
 
-def prepare_kernel(tilt_ref, near_phase, wave_ref, cos_ref, sin_ref):
+def prepare_kernel(tilt_ref, near_own, near_rest, wave_ref, cos_ref, sin_ref):
     blocks, _, height, _ = wave_ref.shape
     count = cos_ref.shape[0] - 1
     core, own_section, own_place = lax.axis_index("row"), lax.axis_index("depth"), lax.axis_index("col")
@@ -183,7 +183,8 @@
     def screens(col, carry):
         held = col ^ own_place
         for bits in range(count):
-            cos_ref[bits ^ own_section, col], sin_ref[bits ^ own_section, col] = cos_sin(near_phase[held, bits])
+            angle = near_own[held, 0] if bits == 0 else near_rest[held, bits - 1]
+            cos_ref[bits ^ own_section, col], sin_ref[bits ^ own_section, col] = cos_sin(angle)
         return carry
 
     lax.fori_loop(0, blocks, screens, 0)
@@ -209,7 +210,7 @@
 
 
 def wave_kernel(
-    wave_ref, near_cos, near_sin, near_measured, far_measured, far_phase, row_ref, col_ref,
+    wave_ref, near_cos, near_sin, near_own, far_own, far_rest, row_ref, col_ref,
     mine_ref, theirs_ref, far_cos, far_sin, v_ref, moved_ref, a_high, a_low,
 ):
     blocks, _, height, _ = v_ref.shape
@@ -222,8 +223,10 @@
     window_start = jnp.clip(own_place - 1, 0, blocks - window)
 
     def far_screens(slice_index):
+        bits = slice_index ^ own_section
         for col in range(blocks):
-            angle = far_phase[col ^ own_place, slice_index ^ own_section]
+            held = col ^ own_place
+            angle = jnp.where(bits == 0, far_own[held, 0], far_rest[held, jnp.maximum(bits - 1, 0)])
             far_cos[slice_index, col], far_sin[slice_index, col] = cos_sin(angle)
 
     for target in (a_high, a_low):
@@ -257,7 +260,7 @@
     for place in range(window):
         block = window_start + place
         held = block ^ own_place
-        for row, measured in ((near, near_measured[held, core]), (far, far_measured[held, 0])):
+        for row, measured in ((near, near_own[held, 1 + core]), (far, far_own[held, 1])):
             real, imag = v_ref[block, 0, row], v_ref[block, 1, row]
             misfit = 2.0 * (real * real + imag * imag - measured)
             v_ref[block, 0, row] = misfit * real
@@ -290,10 +293,6 @@
     gradient = -(pulled[:, LANES:] * moved_ref[0] + pulled[:, :LANES] * moved_ref[1])
     mine_ref[0, 2] = gradient[: height // 2]
     theirs_ref[0, 2] = gradient[height // 2 :]
-
-
-def copy_kernel(from_ref, to_ref):
-    to_ref[...] = from_ref[...]
 
 
 def finish_kernel(mine_ref, received_ref, grad_ref, exit_ref, total_ref, sems):
@@ -310,9 +309,14 @@
         copy.wait()
 
 
-def spread(shard, axis):
+def spread(shard, axis, reach=None):
     size = lax.axis_size(axis)
-    return [lax.ppermute(shard, axis, [(i, i ^ bits) for i in range(size)]) for bits in range(1, size)]
+    reach = size if reach is None else reach
+    pieces = []
+    for bits in range(1, size):
+        pairs = [(i, i ^ bits) for i in range(size) if abs(i - (i ^ bits)) <= reach]
+        pieces.append(lax.ppermute(shard, axis, pairs) if pairs else jnp.zeros_like(shard))
+    return pieces
 
 
 def swap_cores(value):
@@ -334,31 +338,38 @@
     def params(mebibytes):
         return pltpu.CompilerParams(vmem_limit_bytes=mebibytes * 2**20)
 
-    own_phase = pl.pallas_call(
-        copy_kernel,
-        out_shape=array(*phase.shape),
-        in_specs=[vmem],
-        out_specs=vmem,
-        compiler_params=params(1),
-    )(phase)
-    column = jnp.concatenate([own_phase] + spread(phase, "depth"), axis=0)
-    near_measured = jnp.stack([intensity] + spread(intensity, "col"))
-    far_measured = swap_cores(lax.dynamic_slice_in_dim(near_measured, 1 - core, 1, 1))
-    arriving = spread(column, "col")
-    arriving[0], far_measured = lax.optimization_barrier((arriving[0], far_measured))
-    near_phase = jnp.stack([column] + arriving)
-    far_phase = swap_cores(near_phase)
+    other_depths = spread(phase, "depth")
+    other_depths[0], measured, slab = lax.optimization_barrier((other_depths[0], intensity, phase))
+    other_depths = jnp.concatenate(other_depths, axis=0)
+    packet = jnp.concatenate([slab, measured], axis=0)
+    near_own = [packet]
+    for bits in range(1, blocks):
+        pairs = [(i, i ^ bits) for i in range(blocks)]
+        close = [(i, j) for i, j in pairs if abs(i - j) <= 1]
+        if close:
+            near_own.append(lax.ppermute(packet, "col", close))
+        else:
+            further = [(i, j) for i, j in pairs if abs(i - j) <= 2]
+            arrived = lax.ppermute(slab, "col", further) if further else jnp.zeros_like(slab)
+            near_own.append(jnp.concatenate([arrived, jnp.zeros_like(measured)], axis=0))
+    near_own = jnp.stack(near_own)
+    arriving = spread(other_depths, "col", 2)
+    arriving[0], near_own = lax.optimization_barrier((arriving[0], near_own))
+    near_rest = jnp.stack([other_depths] + arriving)
+    wanted = lax.dynamic_slice_in_dim(near_own, 2 - core, 1, 1)
+    far_own = swap_cores(jnp.concatenate([near_own[:, :1], wanted], axis=1))
+    far_rest = swap_cores(near_rest)
 
     half_screens = (count + 1, blocks, tile_r, tile_c)
     field = (blocks, 2, height, tile_c)
     wave, near_cos, near_sin = pl.pallas_call(
         prepare_kernel,
         out_shape=(array(*field), array(*half_screens), array(*half_screens)),
-        in_specs=[smem, vmem],
+        in_specs=[smem, vmem, vmem],
         out_specs=(vmem,) * 3,
         compiler_params=params(8),
         cost_estimate=pl.CostEstimate(flops=5 * 10**8, bytes_accessed=2**20, transcendentals=0),
-    )(tilt, near_phase)
+    )(tilt, near_own, near_rest)
     mine, theirs = pl.pallas_call(
         wave_kernel,
         out_shape=(array(1, 3, tile_r, tile_c),) * 2,
@@ -369,7 +380,7 @@
         + [pltpu.VMEM((blocks, height, 4 * LANES), jnp.bfloat16)] * 2,
         compiler_params=params(24),
     )(
-        wave, near_cos, near_sin, near_measured, far_measured, far_phase,
+        wave, near_cos, near_sin, near_own, far_own, far_rest,
         jnp.asarray(row_constant(height)), jnp.asarray(col_constant()),
     )
     return pl.pallas_call(

time: 36.7 us -> 33.9 us (0.924)
  waiting for transfers between devices: 9.29 us -> 5.18 us
  starting transfers between devices: 14.1 us -> 16.7 us
  local copies, waits for them, and re-layouts: 2.15 us -> 0.93 us
    ppermute x9, waiting for transfers between devices: 7.88 us -> 3.92 us  [the longest x6 3.91 us: spread(): lax.ppermute(shard, axis, pairs)]
    ppermute x9, starting transfers between devices: 13.7 us -> 15.7 us  [the longest x6 10.2 us: spread(): lax.ppermute(shard, axis, pairs)]
    unnamed x10 -> x11, local copies, waits for them, and re-layouts: 2.13 us -> 0.89 us
    ppermute x3, starting transfers between devices: 0.34 us -> 0.97 us  [swap_cores(): return lax.ppermute(value, 'row', [(0, 1), (1, 0)])]
  transfers between devices with their start and end apart: 12 -> 12, of which waited for: 6 -> 3; matrix products, arithmetic and copies ran while one was open for 0% -> 3% of each run, Pallas kernels for 3% -> 3%
where the time goes in v7:
time: 33.9 us; the launch traced here: 33.7 us
  starting transfers between devices  16.7 us (49%)
  Pallas kernels  10.1 us (30%)
  waiting for transfers between devices  5.18 us (15%)
  local copies, waits for them, and re-layouts  0.93 us (3%)
  between operations  0.77 us (2%)
    ppermute x6, starting transfers between devices, spread(): lax.ppermute(shard, axis, pairs)  10.2 us
    pallas_call x1, Pallas kernels, whole_field_body(): pl.pallas_call(wave_kernel, out_shape=(array(1, 3, tile_r, tile_c),) * 2,...  8.29 us
    ppermute x2, starting transfers between devices, whole_field_body(): near_own.append(lax.ppermute(packet, 'col', close))  3.94 us
    ppermute x6, waiting for transfers between devices, spread(): lax.ppermute(shard, axis, pairs)  3.91 us
    ppermute x1, starting transfers between devices, whole_field_body(): lax.ppermute(slab, 'col', further)  1.52 us
    ppermute x3, waiting for transfers between devices, swap_cores(): return lax.ppermute(value, 'row', [(0, 1), (1, 0)])  1.26 us
    pallas_call x1, Pallas kernels, whole_field_body(): pl.pallas_call(prepare_kernel, out_shape=(array(*field), array(*half_scre...  1.13 us
    ppermute x3, starting transfers between devices, swap_cores(): return lax.ppermute(value, 'row', [(0, 1), (1, 0)])  0.97 us
  transfers between devices with their start and end apart: 12, of which 3 were waited for; matrix products, arithmetic and copies ran while one was open for 3% of the time, Pallas kernels for 3%

profile of v7, /device:TPU:0, one launch (start us, length us, event | category | flops | bytes accessed | tf_op | source)
XLA Modules:
  0.0 33.7 jit_solution(13988128814374805904)
XLA Ops:
  0.6 0.0 copy-start.3
  0.6 3.1 %collective-permute-start = (f32[1,64,128]{2,1,0:T(8,128)}, f32[1,64,128]{2,1,0:T(8,128)S(1)}, u32[]{:S(2)}, u32[]{:S(2)}) collective-permute-start(f32[1,64,128]{2,1,0:T(8,128)} %param.5), channel_id=1, source_target_pairs={{0,8},{8,0},{16,24},{24,16},{1,9},{9,1},{17,25},{25,17},{2,10},{10... | collective-permute-start | bytes 98312 | tf_op jit(solution)/shard_map/ppermute | solution.py:318
  3.7 2.5 %collective-permute-start.2 = (f32[1,64,128]{2,1,0:T(8,128)}, f32[1,64,128]{2,1,0:T(8,128)S(1)}, u32[]{:S(2)}, u32[]{:S(2)}) collective-permute-start(f32[1,64,128]{2,1,0:T(8,128)} %param.5), channel_id=1, source_target_pairs={{0,24},{8,16},{16,8},{24,0},{1,25},{9,17},{17,9},{25,1},{2,26},{10... | collective-permute-start | bytes 98312 | tf_op jit(solution)/shard_map/ppermute | solution.py:318
  6.2 0.1 collective-permute-start.1
  6.3 0.0 collective-permute-done
  6.3 1.5 %collective-permute-start.5 = (f32[1,64,128]{2,1,0:T(8,128)}, f32[1,64,128]{2,1,0:T(8,128)S(1)}, u32[]{:S(2)}, u32[]{:S(2)}) collective-permute-start(f32[1,64,128]{2,1,0:T(8,128)} %param.5), channel_id=1, source_target_pairs={{0,2},{1,3},{2,0},{3,1},{4,6},{5,7},{6,4},{7,5},{8,10},{9,11},{10,... | collective-permute-start | bytes 98312 | tf_op jit(solution)/shard_map/ppermute | solution.py:353
  7.8 0.8 %constant_dynamic-update-slice_fusion.4 = f32[3,64,128]{2,1,0:T(8,128)S(1)} fusion(f32[1,64,128]{2,1,0:T(8,128)} %param.5), kind=kLoop, calls=%fused_computation.8 | loop fusion | bytes 65536
  8.6 0.0 copy-done.3
  8.7 0.7 %collective-permute-start.6 = (f32[3,64,128]{2,1,0:T(8,128)S(1)}, f32[3,64,128]{2,1,0:T(8,128)S(1)}, u32[]{:S(2)}, u32[]{:S(2)}) collective-permute-start(f32[3,64,128]{2,1,0:T(8,128)S(1)} %constant_dynamic-update-slice_fusion.3), channel_id=1, source_target_pairs={{1,2},{2,1},{5,6},{6,5},{9,10},{10,9},{13,14},{14,13},{17,18},{18,... | collective-permute-start | bytes 294920 | tf_op jit(solution)/shard_map/ppermute | solution.py:350
  9.3 3.3 %collective-permute-start.4 = (f32[3,64,128]{2,1,0:T(8,128)S(1)}, f32[3,64,128]{2,1,0:T(8,128)S(1)}, u32[]{:S(2)}, u32[]{:S(2)}) collective-permute-start(f32[3,64,128]{2,1,0:T(8,128)S(1)} %constant_dynamic-update-slice_fusion.3), channel_id=1, source_target_pairs={{0,1},{1,0},{2,3},{3,2},{4,5},{5,4},{6,7},{7,6},{8,9},{9,8},{10,11... | collective-permute-start | bytes 294920 | tf_op jit(solution)/shard_map/ppermute | solution.py:350
  12.6 0.0 collective-permute-done.1
  12.6 0.0 collective-permute-done.2
  12.6 0.7 %collective-permute-start.8 = (f32[3,64,128]{2,1,0:T(8,128)S(1)}, f32[3,64,128]{2,1,0:T(8,128)S(1)}, u32[]{:S(2)}, u32[]{:S(2)}) collective-permute-start(f32[3,64,128]{2,1,0:T(8,128)S(1)} %constant_dynamic-update-slice_fusion), channel_id=1, source_target_pairs={{1,2},{2,1},{5,6},{6,5},{9,10},{10,9},{13,14},{14,13},{17,18},{18,... | collective-permute-start | bytes 294920 | tf_op jit(solution)/shard_map/ppermute | solution.py:318
  13.3 3.2 %collective-permute-start.7 = (f32[3,64,128]{2,1,0:T(8,128)S(1)}, f32[3,64,128]{2,1,0:T(8,128)S(1)}, u32[]{:S(2)}, u32[]{:S(2)}) collective-permute-start(f32[3,64,128]{2,1,0:T(8,128)S(1)} %constant_dynamic-update-slice_fusion), channel_id=1, source_target_pairs={{0,2},{1,3},{2,0},{3,1},{4,6},{5,7},{6,4},{7,5},{8,10},{9,11},{10,... | collective-permute-start | bytes 294920 | tf_op jit(solution)/shard_map/ppermute | solution.py:318
  16.5 0.0 collective-permute-done.5
  16.5 0.7 %collective-permute-start.3 = (f32[3,64,128]{2,1,0:T(8,128)S(1)}, f32[3,64,128]{2,1,0:T(8,128)S(1)}, u32[]{:S(2)}, u32[]{:S(2)}) collective-permute-start(f32[3,64,128]{2,1,0:T(8,128)S(1)} %constant_dynamic-update-slice_fusion), channel_id=1, source_target_pairs={{0,1},{1,0},{2,3},{3,2},{4,5},{5,4},{6,7},{7,6},{8,9},{9,8},{10,11... | collective-permute-start | bytes 294920 | tf_op jit(solution)/shard_map/ppermute | solution.py:318
  17.2 0.0 collective-permute-done.6
  17.2 0.0 collective-permute-done.4
  17.3 3.9 %collective-permute-done.3 = f32[3,64,128]{2,1,0:T(8,128)S(1)} collective-permute-done((f32[3,64,128]{2,1,0:T(8,128)S(1)}, f32[3,64,128]{2,1,0:T(8,128)S(1)}, u32[]{:S(2)}, u32[]{:S(2)}) %collective-permute-start.3) | collective-permute-done | bytes 98336 | tf_op jit(solution)/shard_map/ppermute | solution.py:318
  21.2 0.0 collective-permute-done.8
  21.2 0.0 collective-permute-done.7
  21.2 0.1 collective-permute-start.10
  21.3 0.0 copy-start.2
  21.3 0.0 copy-start
  21.4 0.0 copy-start.1
  21.4 0.6 %collective-permute-start.9 = (f32[4,2,64,128]{3,2,1,0:T(8,128)S(1)}, f32[4,2,64,128]{3,2,1,0:T(8,128)S(1)}, u32[]{:S(2)}, u32[]{:S(2)}) collective-permute-start(f32[4,2,64,128]{3,2,1,0:T(8,128)S(1)} %pad_maximum_fusion.2), channel_id=1, source_target_pairs={{0,4},{4,0},{1,5},{5,1},{2,6},{6,2},{3,7},{7,3},{8,12},{12,8},{9,1... | collective-permute-start | bytes 786440 | tf_op jit(solution)/shard_map/ppermute | solution.py:323
  21.9 0.1 copy-done.2
  22.0 1.1 %shard_map.68 = (f32[4,2,128,128]{3,2,1,0:T(8,128)S(1)}, f32[5,4,64,128]{3,2,1,0:T(8,128)S(1)}, f32[5,4,64,128]{3,2,1,0:T(8,128)S(1)}) custom-call(s32[2,2]{1,0:T(2,128)S(1)} %copy-done.2, f32[4,3,64,128]{3,2,1,0:T(8,128)S(1)} %pad_maximum_fusion.near_own, f32[4,3,64,128]{3,2,1,0:T(8,128)S(1)} %pad_maximum_fusion.1.near_rest), custom_call_target="tpu_custom_call" | custom-call | flops 500000000 | bytes 1048576 | tf_op jit(solution)/shard_map/pallas_call | solution.py:365
  23.1 0.2 collective-permute-done.9.far_own
  23.4 0.0 collective-permute-done.10.far_rest
  23.4 0.0 copy-done
  23.4 0.0 copy-done.1
  23.4 8.3 %shard_map.69 = (f32[1,3,64,128]{3,2,1,0:T(8,128)S(1)}, f32[1,3,64,128]{3,2,1,0:T(8,128)S(1)}) custom-call(f32[4,2,128,128]{3,2,1,0:T(8,128)S(1)} %get-tuple-element.17.wave_ref, f32[5,4,64,128]{3,2,1,0:T(8,128)S(1)} %get-tuple-element.18.near_cos, f32[5,4,64,128]{3,2,1,0:T(8,128)S(1)} %get-tuple-element.19.near_sin, ...), custom_call_target="tpu_custom_call" | custom-call | tf_op jit(solution)/shard_map/pallas_call | solution.py:373
  31.7 0.3 %collective-permute-start.11 = (f32[1,3,64,128]{3,2,1,0:T(8,128)S(1)}, f32[1,3,64,128]{3,2,1,0:T(8,128)S(1)}, u32[]{:S(2)}, u32[]{:S(2)}) collective-permute-start(f32[1,3,64,128]{3,2,1,0:T(8,128)S(1)} %get-tuple-element.21), channel_id=1, source_target_pairs={{0,4},{4,0},{1,5},{5,1},{2,6},{6,2},{3,7},{7,3},{8,12},{12,8},{9,1... | collective-permute-start | bytes 294920 | tf_op jit(solution)/shard_map/ppermute | solution.py:323
  32.0 1.0 %collective-permute-done.11.received_ref = f32[1,3,64,128]{3,2,1,0:T(8,128)S(1)} collective-permute-done((f32[1,3,64,128]{3,2,1,0:T(8,128)S(1)}, f32[1,3,64,128]{3,2,1,0:T(8,128)S(1)}, u32[]{:S(2)}, u32[]{:S(2)}) %collective-permute-start.11) | collective-permute-done | bytes 98336 | tf_op jit(solution)/shard_map/ppermute | solution.py:323
  33.0 0.7 %shard_map.70 = (f32[1,64,128]{2,1,0:T(8,128)}, f32[2,1,2,64,128]{4,3,2,1,0:T(8,128)}) custom-call(f32[1,3,64,128]{3,2,1,0:T(8,128)S(1)} %get-tuple-element.20.mine_ref, f32[1,3,64,128]{3,2,1,0:T(8,128)S(1)} %collective-permute-done.11.received_ref), custom_call_target="tpu_custom_call" | custom-call | tf_op jit(solution)/shard_map/pallas_call | solution.py:386
  (9 shorter events, 0.1 us)
Async XLA Ops:
  0.6 8.0 %copy-start.3 = (f32[2,64,128]{2,1,0:T(8,128)S(1)}, f32[2,64,128]{2,1,0:T(8,128)}, u32[]{:S(2)}) copy-start(f32[2,64,128]{2,1,0:T(8,128)} %param.7) | copy-start | bytes 196612
  0.6 5.7 %collective-permute-start = (f32[1,64,128]{2,1,0:T(8,128)}, f32[1,64,128]{2,1,0:T(8,128)S(1)}, u32[]{:S(2)}, u32[]{:S(2)}) collective-permute-start(f32[1,64,128]{2,1,0:T(8,128)} %param.5), channel_id=1, source_target_pairs={{0,8},{8,0},{16,24},{24,16},{1,9},{9,1},{17,25},{25,17},{2,10},{10... | collective-permute-start | bytes 98312 | tf_op jit(solution)/shard_map/ppermute | solution.py:318
  3.7 8.9 %collective-permute-start.2 = (f32[1,64,128]{2,1,0:T(8,128)}, f32[1,64,128]{2,1,0:T(8,128)S(1)}, u32[]{:S(2)}, u32[]{:S(2)}) collective-permute-start(f32[1,64,128]{2,1,0:T(8,128)} %param.5), channel_id=1, source_target_pairs={{0,24},{8,16},{16,8},{24,0},{1,25},{9,17},{17,9},{25,1},{2,26},{10... | collective-permute-start | bytes 98312 | tf_op jit(solution)/shard_map/ppermute | solution.py:318
  6.2 6.4 %collective-permute-start.1 = (f32[1,64,128]{2,1,0:T(8,128)}, f32[1,64,128]{2,1,0:T(8,128)S(1)}, u32[]{:S(2)}, u32[]{:S(2)}) collective-permute-start(f32[1,64,128]{2,1,0:T(8,128)} %param.5), channel_id=1, source_target_pairs={{0,16},{8,24},{16,0},{24,8},{1,17},{9,25},{17,1},{25,9},{2,18},{10... | collective-permute-start | bytes 98312 | tf_op jit(solution)/shard_map/ppermute | solution.py:318
  6.3 10.2 %collective-permute-start.5 = (f32[1,64,128]{2,1,0:T(8,128)}, f32[1,64,128]{2,1,0:T(8,128)S(1)}, u32[]{:S(2)}, u32[]{:S(2)}) collective-permute-start(f32[1,64,128]{2,1,0:T(8,128)} %param.5), channel_id=1, source_target_pairs={{0,2},{1,3},{2,0},{3,1},{4,6},{5,7},{6,4},{7,5},{8,10},{9,11},{10,... | collective-permute-start | bytes 98312 | tf_op jit(solution)/shard_map/ppermute | solution.py:353
  8.7 8.6 %collective-permute-start.6 = (f32[3,64,128]{2,1,0:T(8,128)S(1)}, f32[3,64,128]{2,1,0:T(8,128)S(1)}, u32[]{:S(2)}, u32[]{:S(2)}) collective-permute-start(f32[3,64,128]{2,1,0:T(8,128)S(1)} %constant_dynamic-update-slice_fusion.3), channel_id=1, source_target_pairs={{1,2},{2,1},{5,6},{6,5},{9,10},{10,9},{13,14},{14,13},{17,18},{18,... | collective-permute-start | bytes 294920 | tf_op jit(solution)/shard_map/ppermute | solution.py:350
  9.3 7.9 %collective-permute-start.4 = (f32[3,64,128]{2,1,0:T(8,128)S(1)}, f32[3,64,128]{2,1,0:T(8,128)S(1)}, u32[]{:S(2)}, u32[]{:S(2)}) collective-permute-start(f32[3,64,128]{2,1,0:T(8,128)S(1)} %constant_dynamic-update-slice_fusion.3), channel_id=1, source_target_pairs={{0,1},{1,0},{2,3},{3,2},{4,5},{5,4},{6,7},{7,6},{8,9},{9,8},{10,11... | collective-permute-start | bytes 294920 | tf_op jit(solution)/shard_map/ppermute | solution.py:350
  12.6 8.5 %collective-permute-start.8 = (f32[3,64,128]{2,1,0:T(8,128)S(1)}, f32[3,64,128]{2,1,0:T(8,128)S(1)}, u32[]{:S(2)}, u32[]{:S(2)}) collective-permute-start(f32[3,64,128]{2,1,0:T(8,128)S(1)} %constant_dynamic-update-slice_fusion), channel_id=1, source_target_pairs={{1,2},{2,1},{5,6},{6,5},{9,10},{10,9},{13,14},{14,13},{17,18},{18,... | collective-permute-start | bytes 294920 | tf_op jit(solution)/shard_map/ppermute | solution.py:318
  13.3 7.8 %collective-permute-start.7 = (f32[3,64,128]{2,1,0:T(8,128)S(1)}, f32[3,64,128]{2,1,0:T(8,128)S(1)}, u32[]{:S(2)}, u32[]{:S(2)}) collective-permute-start(f32[3,64,128]{2,1,0:T(8,128)S(1)} %constant_dynamic-update-slice_fusion), channel_id=1, source_target_pairs={{0,2},{1,3},{2,0},{3,1},{4,6},{5,7},{6,4},{7,5},{8,10},{9,11},{10,... | collective-permute-start | bytes 294920 | tf_op jit(solution)/shard_map/ppermute | solution.py:318
  16.5 4.6 %collective-permute-start.3 = (f32[3,64,128]{2,1,0:T(8,128)S(1)}, f32[3,64,128]{2,1,0:T(8,128)S(1)}, u32[]{:S(2)}, u32[]{:S(2)}) collective-permute-start(f32[3,64,128]{2,1,0:T(8,128)S(1)} %constant_dynamic-update-slice_fusion), channel_id=1, source_target_pairs={{0,1},{1,0},{2,3},{3,2},{4,5},{5,4},{6,7},{7,6},{8,9},{9,8},{10,11... | collective-permute-start | bytes 294920 | tf_op jit(solution)/shard_map/ppermute | solution.py:318
  21.2 2.2 %collective-permute-start.10 = (f32[4,3,64,128]{3,2,1,0:T(8,128)S(1)}, f32[4,3,64,128]{3,2,1,0:T(8,128)S(1)}, u32[]{:S(2)}, u32[]{:S(2)}) collective-permute-start(f32[4,3,64,128]{3,2,1,0:T(8,128)S(1)} %pad_maximum_fusion.1.near_rest), channel_id=1, source_target_pairs={{0,4},{4,0},{1,5},{5,1},{2,6},{6,2},{3,7},{7,3},{8,12},{12,8},{9,1... | collective-permute-start | bytes 1179656 | tf_op jit(solution)/shard_map/ppermute | solution.py:323
  21.3 0.7 %copy-start.2 = (s32[2,2]{1,0:T(2,128)S(1)}, s32[2,2]{1,0:T(2,128)}, u32[]{:S(2)}) copy-start(s32[2,2]{1,0:T(2,128)} %tilt_ref.1) | copy-start | bytes 52
  21.3 2.0 %copy-start = (bf16[1024,256]{1,0:T(8,128)(2,1)S(1)}, bf16[1024,256]{1,0:T(8,128)(2,1)}, u32[]{:S(2)}) copy-start(bf16[1024,256]{1,0:T(8,128)(2,1)} %constant.20.clone.col_ref) | copy-start | bytes 1572868
  21.4 2.0 %copy-start.1 = (bf16[2,256,512]{2,1,0:T(8,128)(2,1)S(1)}, bf16[2,256,512]{2,1,0:T(8,128)(2,1)}, u32[]{:S(2)}) copy-start(bf16[2,256,512]{2,1,0:T(8,128)(2,1)} %constant.19.clone.row_ref) | copy-start | bytes 1572868
  21.4 2.0 %collective-permute-start.9 = (f32[4,2,64,128]{3,2,1,0:T(8,128)S(1)}, f32[4,2,64,128]{3,2,1,0:T(8,128)S(1)}, u32[]{:S(2)}, u32[]{:S(2)}) collective-permute-start(f32[4,2,64,128]{3,2,1,0:T(8,128)S(1)} %pad_maximum_fusion.2), channel_id=1, source_target_pairs={{0,4},{4,0},{1,5},{5,1},{2,6},{6,2},{3,7},{7,3},{8,12},{12,8},{9,1... | collective-permute-start | bytes 786440 | tf_op jit(solution)/shard_map/ppermute | solution.py:323
  31.7 1.4 %collective-permute-start.11 = (f32[1,3,64,128]{3,2,1,0:T(8,128)S(1)}, f32[1,3,64,128]{3,2,1,0:T(8,128)S(1)}, u32[]{:S(2)}, u32[]{:S(2)}) collective-permute-start(f32[1,3,64,128]{3,2,1,0:T(8,128)S(1)} %get-tuple-element.21), channel_id=1, source_target_pairs={{0,4},{4,0},{1,5},{5,1},{2,6},{6,2},{3,7},{7,3},{8,12},{12,8},{9,1... | collective-permute-start | bytes 294920 | tf_op jit(solution)/shard_map/ppermute | solution.py:323

commit v8 on v7

--- a/solution.py
+++ b/solution.py
@@ -309,14 +309,13 @@
         copy.wait()
 
 
-def spread(shard, axis, reach=None):
+def spread(shard, axis):
     size = lax.axis_size(axis)
-    reach = size if reach is None else reach
-    pieces = []
-    for bits in range(1, size):
-        pairs = [(i, i ^ bits) for i in range(size) if abs(i - (i ^ bits)) <= reach]
-        pieces.append(lax.ppermute(shard, axis, pairs) if pairs else jnp.zeros_like(shard))
-    return pieces
+    return [lax.ppermute(shard, axis, [(i, i ^ bits) for i in range(size)]) for bits in range(1, size)]
+
+
+def exchange(value, bits):
+    return lax.ppermute(value, "col", [(i, i ^ bits) for i in range(4)])
 
 
 def swap_cores(value):
@@ -340,22 +339,15 @@
 
     other_depths = spread(phase, "depth")
     other_depths[0], measured, slab = lax.optimization_barrier((other_depths[0], intensity, phase))
+    packet = jnp.concatenate([slab, measured], axis=0)
+    packet_x, packet_y = exchange(packet, 1), exchange(packet, 2)
+    other_depths[-1], packet_x = lax.optimization_barrier((other_depths[-1], packet_x))
     other_depths = jnp.concatenate(other_depths, axis=0)
-    packet = jnp.concatenate([slab, measured], axis=0)
-    near_own = [packet]
-    for bits in range(1, blocks):
-        pairs = [(i, i ^ bits) for i in range(blocks)]
-        close = [(i, j) for i, j in pairs if abs(i - j) <= 1]
-        if close:
-            near_own.append(lax.ppermute(packet, "col", close))
-        else:
-            further = [(i, j) for i, j in pairs if abs(i - j) <= 2]
-            arrived = lax.ppermute(slab, "col", further) if further else jnp.zeros_like(slab)
-            near_own.append(jnp.concatenate([arrived, jnp.zeros_like(measured)], axis=0))
-    near_own = jnp.stack(near_own)
-    arriving = spread(other_depths, "col", 2)
-    arriving[0], near_own = lax.optimization_barrier((arriving[0], near_own))
-    near_rest = jnp.stack([other_depths] + arriving)
+    near_own = jnp.stack([packet, packet_x, packet_y, exchange(packet_y, 1)])
+    rest_x, rest_y = exchange(other_depths, 1), exchange(other_depths, 2)
+    rest_corner = exchange(rest_x, 2)
+    rest_x, near_own = lax.optimization_barrier((rest_x, near_own))
+    near_rest = jnp.stack([other_depths, rest_x, rest_y, rest_corner])
     wanted = lax.dynamic_slice_in_dim(near_own, 2 - core, 1, 1)
     far_own = swap_cores(jnp.concatenate([near_own[:, :1], wanted], axis=1))
     far_rest = swap_cores(near_rest)
@@ -569,10 +561,9 @@
         and batch == rows == 2
         and slices == sections
         and sections & (sections - 1) == 0
-        and cols & (cols - 1) == 0
+        and cols == 4
         and height == LANES
         and width == cols * LANES
-        and cols > 1
         and sections > 1
         and sections * HALO <= LANES
     )

time: 33.9 us -> 35.3 us (1.041)
  waiting for transfers between devices: 5.18 us -> 10.5 us
  starting transfers between devices: 16.7 us -> 12.8 us
    ppermute x9, waiting for transfers between devices: 3.92 us -> 9.28 us  [the longest x6 7.9 us: exchange(): return lax.ppermute(value, 'col', [(i, i ^ bits) for i in range(4)])]
    ppermute x9, starting transfers between devices: 15.7 us -> 11.8 us  [the longest x6 6.11 us: exchange(): return lax.ppermute(value, 'col', [(i, i ^ bits) for i in range(4)])]
  transfers between devices with their start and end apart: 12 -> 12, of which waited for: 3 -> 8; matrix products, arithmetic and copies ran while one was open for 3% -> 2% of each run, Pallas kernels for 3% -> 3%
where the time goes in v8:
time: 35.3 us; the launch traced here: 35.1 us
  starting transfers between devices  12.8 us (36%)
  waiting for transfers between devices  10.5 us (30%)
  Pallas kernels  10.1 us (29%)
  local copies, waits for them, and re-layouts  0.91 us (3%)
  between operations  0.73 us (2%)
    pallas_call x1, Pallas kernels, whole_field_body(): pl.pallas_call(wave_kernel, out_shape=(array(1, 3, tile_r, tile_c),) * 2,...  8.3 us
    ppermute x6, waiting for transfers between devices, exchange(): return lax.ppermute(value, 'col', [(i, i ^ bits) for i in range(4)])  7.9 us
    ppermute x6, starting transfers between devices, exchange(): return lax.ppermute(value, 'col', [(i, i ^ bits) for i in range(4)])  6.11 us
    ppermute x3, starting transfers between devices, spread(): lax.ppermute(shard, axis, [(i, i ^ bits) for i in range(size)])  5.68 us
    ppermute x3, waiting for transfers between devices, spread(): lax.ppermute(shard, axis, [(i, i ^ bits) for i in range(size)])  1.38 us
    ppermute x3, waiting for transfers between devices, swap_cores(): return lax.ppermute(value, 'row', [(0, 1), (1, 0)])  1.26 us
    pallas_call x1, Pallas kernels, whole_field_body(): pl.pallas_call(prepare_kernel, out_shape=(array(*field), array(*half_scre...  1.13 us
    ppermute x3, starting transfers between devices, swap_cores(): return lax.ppermute(value, 'row', [(0, 1), (1, 0)])  0.97 us
  transfers between devices with their start and end apart: 12, of which 8 were waited for; matrix products, arithmetic and copies ran while one was open for 2% of the time, Pallas kernels for 3%

profile of v8, /device:TPU:0, one launch (start us, length us, event | category | flops | bytes accessed | tf_op | source)
XLA Modules:
  0.0 35.1 jit_solution(13151990612464078420)
XLA Ops:
  0.6 0.0 copy-start.3
  0.6 3.1 %collective-permute-start = (f32[1,64,128]{2,1,0:T(8,128)}, f32[1,64,128]{2,1,0:T(8,128)S(1)}, u32[]{:S(2)}, u32[]{:S(2)}) collective-permute-start(f32[1,64,128]{2,1,0:T(8,128)} %param.5), channel_id=1, source_target_pairs={{0,8},{8,0},{16,24},{24,16},{1,9},{9,1},{17,25},{25,17},{2,10},{10... | collective-permute-start | bytes 98312 | tf_op jit(solution)/shard_map/ppermute | solution.py:314
  3.7 2.5 %collective-permute-start.2 = (f32[1,64,128]{2,1,0:T(8,128)}, f32[1,64,128]{2,1,0:T(8,128)S(1)}, u32[]{:S(2)}, u32[]{:S(2)}) collective-permute-start(f32[1,64,128]{2,1,0:T(8,128)} %param.5), channel_id=1, source_target_pairs={{0,24},{8,16},{16,8},{24,0},{1,25},{9,17},{17,9},{25,1},{2,26},{10... | collective-permute-start | bytes 98312 | tf_op jit(solution)/shard_map/ppermute | solution.py:314
  6.2 0.1 collective-permute-start.1
  6.3 0.0 collective-permute-done
  6.3 0.8 %constant_dynamic-update-slice_fusion.1 = f32[3,64,128]{2,1,0:T(8,128)S(1)} fusion(f32[1,64,128]{2,1,0:T(8,128)} %param.5), kind=kLoop, calls=%fused_computation.4 | loop fusion | bytes 65536
  7.1 0.0 copy-done.3
  7.1 1.6 %collective-permute-start.5 = (f32[3,64,128]{2,1,0:T(8,128)S(1)}, f32[3,64,128]{2,1,0:T(8,128)S(1)}, u32[]{:S(2)}, u32[]{:S(2)}) collective-permute-start(f32[3,64,128]{2,1,0:T(8,128)S(1)} %constant_dynamic-update-slice_fusion), channel_id=1, source_target_pairs={{0,2},{1,3},{2,0},{3,1},{4,6},{5,7},{6,4},{7,5},{8,10},{9,11},{10,... | collective-permute-start | bytes 294920 | tf_op jit(solution)/shard_map/ppermute | solution.py:318
  8.7 1.5 %collective-permute-start.3 = (f32[3,64,128]{2,1,0:T(8,128)S(1)}, f32[3,64,128]{2,1,0:T(8,128)S(1)}, u32[]{:S(2)}, u32[]{:S(2)}) collective-permute-start(f32[3,64,128]{2,1,0:T(8,128)S(1)} %constant_dynamic-update-slice_fusion), channel_id=1, source_target_pairs={{0,1},{1,0},{2,3},{3,2},{4,5},{5,4},{6,7},{7,6},{8,9},{9,8},{10,11... | collective-permute-start | bytes 294920 | tf_op jit(solution)/shard_map/ppermute | solution.py:318
  10.2 1.4 %collective-permute-done.1 = f32[1,64,128]{2,1,0:T(8,128)S(1)} collective-permute-done((f32[1,64,128]{2,1,0:T(8,128)}, f32[1,64,128]{2,1,0:T(8,128)S(1)}, u32[]{:S(2)}, u32[]{:S(2)}) %collective-permute-start.1) | collective-permute-done | bytes 32800 | tf_op jit(solution)/shard_map/ppermute | solution.py:314
  11.6 0.0 collective-permute-done.2
  11.6 1.7 %collective-permute-done.3 = f32[3,64,128]{2,1,0:T(8,128)S(1)} collective-permute-done((f32[3,64,128]{2,1,0:T(8,128)S(1)}, f32[3,64,128]{2,1,0:T(8,128)S(1)}, u32[]{:S(2)}, u32[]{:S(2)}) %collective-permute-start.3) | collective-permute-done | bytes 98336 | tf_op jit(solution)/shard_map/ppermute | solution.py:318
  13.3 1.5 %collective-permute-start.4 = (f32[3,64,128]{2,1,0:T(8,128)S(1)}, f32[3,64,128]{2,1,0:T(8,128)S(1)}, u32[]{:S(2)}, u32[]{:S(2)}) collective-permute-start(f32[3,64,128]{2,1,0:T(8,128)S(1)} %constant_dynamic-update-slice_fusion.2), channel_id=1, source_target_pairs={{0,1},{1,0},{2,3},{3,2},{4,5},{5,4},{6,7},{7,6},{8,9},{9,8},{10,11... | collective-permute-start | bytes 294920 | tf_op jit(solution)/shard_map/ppermute | solution.py:318
  14.8 0.0 collective-permute-done.5
  14.8 0.5 %collective-permute-start.6 = (f32[3,64,128]{2,1,0:T(8,128)S(1)}, f32[3,64,128]{2,1,0:T(8,128)S(1)}, u32[]{:S(2)}, u32[]{:S(2)}) collective-permute-start(f32[3,64,128]{2,1,0:T(8,128)S(1)} %collective-permute-done.5), channel_id=1, source_target_pairs={{0,1},{1,0},{2,3},{3,2},{4,5},{5,4},{6,7},{7,6},{8,9},{9,8},{10,11... | collective-permute-start | bytes 294920 | tf_op jit(solution)/shard_map/ppermute | solution.py:318
  15.4 0.5 %collective-permute-start.7 = (f32[3,64,128]{2,1,0:T(8,128)S(1)}, f32[3,64,128]{2,1,0:T(8,128)S(1)}, u32[]{:S(2)}, u32[]{:S(2)}) collective-permute-start(f32[3,64,128]{2,1,0:T(8,128)S(1)} %constant_dynamic-update-slice_fusion.2), channel_id=1, source_target_pairs={{0,2},{1,3},{2,0},{3,1},{4,6},{5,7},{6,4},{7,5},{8,10},{9,11},{10,... | collective-permute-start | bytes 294920 | tf_op jit(solution)/shard_map/ppermute | solution.py:318
  15.9 2.1 %collective-permute-done.4 = f32[3,64,128]{2,1,0:T(8,128)S(1)} collective-permute-done((f32[3,64,128]{2,1,0:T(8,128)S(1)}, f32[3,64,128]{2,1,0:T(8,128)S(1)}, u32[]{:S(2)}, u32[]{:S(2)}) %collective-permute-start.4) | collective-permute-done | bytes 98336 | tf_op jit(solution)/shard_map/ppermute | solution.py:318
  18.0 0.5 %collective-permute-start.8 = (f32[3,64,128]{2,1,0:T(8,128)S(1)}, f32[3,64,128]{2,1,0:T(8,128)S(1)}, u32[]{:S(2)}, u32[]{:S(2)}) collective-permute-start(f32[3,64,128]{2,1,0:T(8,128)S(1)} %collective-permute-done.4), channel_id=1, source_target_pairs={{0,2},{1,3},{2,0},{3,1},{4,6},{5,7},{6,4},{7,5},{8,10},{9,11},{10,... | collective-permute-start | bytes 294920 | tf_op jit(solution)/shard_map/ppermute | solution.py:318
  18.5 1.0 %collective-permute-done.6 = f32[3,64,128]{2,1,0:T(8,128)S(1)} collective-permute-done((f32[3,64,128]{2,1,0:T(8,128)S(1)}, f32[3,64,128]{2,1,0:T(8,128)S(1)}, u32[]{:S(2)}, u32[]{:S(2)}) %collective-permute-start.6) | collective-permute-done | bytes 98336 | tf_op jit(solution)/shard_map/ppermute | solution.py:318
  19.5 0.5 %collective-permute-done.7 = f32[3,64,128]{2,1,0:T(8,128)S(1)} collective-permute-done((f32[3,64,128]{2,1,0:T(8,128)S(1)}, f32[3,64,128]{2,1,0:T(8,128)S(1)}, u32[]{:S(2)}, u32[]{:S(2)}) %collective-permute-start.7) | collective-permute-done | bytes 98336 | tf_op jit(solution)/shard_map/ppermute | solution.py:318
  20.0 2.6 %collective-permute-done.8 = f32[3,64,128]{2,1,0:T(8,128)S(1)} collective-permute-done((f32[3,64,128]{2,1,0:T(8,128)S(1)}, f32[3,64,128]{2,1,0:T(8,128)S(1)}, u32[]{:S(2)}, u32[]{:S(2)}) %collective-permute-start.8) | collective-permute-done | bytes 98336 | tf_op jit(solution)/shard_map/ppermute | solution.py:318
  22.6 0.1 collective-permute-start.10
  22.7 0.0 copy-start.2
  22.7 0.0 copy-start
  22.8 0.0 copy-start.1
  22.8 0.6 %collective-permute-start.9 = (f32[4,2,64,128]{3,2,1,0:T(8,128)S(1)}, f32[4,2,64,128]{3,2,1,0:T(8,128)S(1)}, u32[]{:S(2)}, u32[]{:S(2)}) collective-permute-start(f32[4,2,64,128]{3,2,1,0:T(8,128)S(1)} %pad_maximum_fusion.2), channel_id=1, source_target_pairs={{0,4},{4,0},{1,5},{5,1},{2,6},{6,2},{3,7},{7,3},{8,12},{12,8},{9,1... | collective-permute-start | bytes 786440 | tf_op jit(solution)/shard_map/ppermute | solution.py:322
  23.3 0.1 copy-done.2
  23.4 1.1 %shard_map.68 = (f32[4,2,128,128]{3,2,1,0:T(8,128)S(1)}, f32[5,4,64,128]{3,2,1,0:T(8,128)S(1)}, f32[5,4,64,128]{3,2,1,0:T(8,128)S(1)}) custom-call(s32[2,2]{1,0:T(2,128)S(1)} %copy-done.2, f32[4,3,64,128]{3,2,1,0:T(8,128)S(1)} %pad_maximum_fusion.near_own, f32[4,3,64,128]{3,2,1,0:T(8,128)S(1)} %pad_maximum_fusion.1.near_rest), custom_call_target="tpu_custom_call" | custom-call | flops 500000000 | bytes 1048576 | tf_op jit(solution)/shard_map/pallas_call | solution.py:357
  24.5 0.2 collective-permute-done.9.far_own
  24.8 0.0 collective-permute-done.10.far_rest
  24.8 0.0 copy-done
  24.8 0.0 copy-done.1
  24.8 8.3 %shard_map.69 = (f32[1,3,64,128]{3,2,1,0:T(8,128)S(1)}, f32[1,3,64,128]{3,2,1,0:T(8,128)S(1)}) custom-call(f32[4,2,128,128]{3,2,1,0:T(8,128)S(1)} %get-tuple-element.21.wave_ref, f32[5,4,64,128]{3,2,1,0:T(8,128)S(1)} %get-tuple-element.22.near_cos, f32[5,4,64,128]{3,2,1,0:T(8,128)S(1)} %get-tuple-element.23.near_sin, ...), custom_call_target="tpu_custom_call" | custom-call | tf_op jit(solution)/shard_map/pallas_call | solution.py:365
  33.1 0.3 collective-permute-start.11
  33.4 1.0 %collective-permute-done.11.received_ref = f32[1,3,64,128]{3,2,1,0:T(8,128)S(1)} collective-permute-done((f32[1,3,64,128]{3,2,1,0:T(8,128)S(1)}, f32[1,3,64,128]{3,2,1,0:T(8,128)S(1)}, u32[]{:S(2)}, u32[]{:S(2)}) %collective-permute-start.11) | collective-permute-done | bytes 98336 | tf_op jit(solution)/shard_map/ppermute | solution.py:322
  34.4 0.7 %shard_map.70 = (f32[1,64,128]{2,1,0:T(8,128)}, f32[2,1,2,64,128]{4,3,2,1,0:T(8,128)}) custom-call(f32[1,3,64,128]{3,2,1,0:T(8,128)S(1)} %get-tuple-element.24.mine_ref, f32[1,3,64,128]{3,2,1,0:T(8,128)S(1)} %collective-permute-done.11.received_ref), custom_call_target="tpu_custom_call" | custom-call | tf_op jit(solution)/shard_map/pallas_call | solution.py:378
  (8 shorter events, 0.1 us)
Async XLA Ops:
  0.6 6.5 %copy-start.3 = (f32[2,64,128]{2,1,0:T(8,128)S(1)}, f32[2,64,128]{2,1,0:T(8,128)}, u32[]{:S(2)}) copy-start(f32[2,64,128]{2,1,0:T(8,128)} %param.7) | copy-start | bytes 196612
  0.6 5.7 %collective-permute-start = (f32[1,64,128]{2,1,0:T(8,128)}, f32[1,64,128]{2,1,0:T(8,128)S(1)}, u32[]{:S(2)}, u32[]{:S(2)}) collective-permute-start(f32[1,64,128]{2,1,0:T(8,128)} %param.5), channel_id=1, source_target_pairs={{0,8},{8,0},{16,24},{24,16},{1,9},{9,1},{17,25},{25,17},{2,10},{10... | collective-permute-start | bytes 98312 | tf_op jit(solution)/shard_map/ppermute | solution.py:314
  3.7 7.9 %collective-permute-start.2 = (f32[1,64,128]{2,1,0:T(8,128)}, f32[1,64,128]{2,1,0:T(8,128)S(1)}, u32[]{:S(2)}, u32[]{:S(2)}) collective-permute-start(f32[1,64,128]{2,1,0:T(8,128)} %param.5), channel_id=1, source_target_pairs={{0,24},{8,16},{16,8},{24,0},{1,25},{9,17},{17,9},{25,1},{2,26},{10... | collective-permute-start | bytes 98312 | tf_op jit(solution)/shard_map/ppermute | solution.py:314
  6.2 5.4 %collective-permute-start.1 = (f32[1,64,128]{2,1,0:T(8,128)}, f32[1,64,128]{2,1,0:T(8,128)S(1)}, u32[]{:S(2)}, u32[]{:S(2)}) collective-permute-start(f32[1,64,128]{2,1,0:T(8,128)} %param.5), channel_id=1, source_target_pairs={{0,16},{8,24},{16,0},{24,8},{1,17},{9,25},{17,1},{25,9},{2,18},{10... | collective-permute-start | bytes 98312 | tf_op jit(solution)/shard_map/ppermute | solution.py:314
  7.1 7.7 %collective-permute-start.5 = (f32[3,64,128]{2,1,0:T(8,128)S(1)}, f32[3,64,128]{2,1,0:T(8,128)S(1)}, u32[]{:S(2)}, u32[]{:S(2)}) collective-permute-start(f32[3,64,128]{2,1,0:T(8,128)S(1)} %constant_dynamic-update-slice_fusion), channel_id=1, source_target_pairs={{0,2},{1,3},{2,0},{3,1},{4,6},{5,7},{6,4},{7,5},{8,10},{9,11},{10,... | collective-permute-start | bytes 294920 | tf_op jit(solution)/shard_map/ppermute | solution.py:318
  8.7 4.6 %collective-permute-start.3 = (f32[3,64,128]{2,1,0:T(8,128)S(1)}, f32[3,64,128]{2,1,0:T(8,128)S(1)}, u32[]{:S(2)}, u32[]{:S(2)}) collective-permute-start(f32[3,64,128]{2,1,0:T(8,128)S(1)} %constant_dynamic-update-slice_fusion), channel_id=1, source_target_pairs={{0,1},{1,0},{2,3},{3,2},{4,5},{5,4},{6,7},{7,6},{8,9},{9,8},{10,11... | collective-permute-start | bytes 294920 | tf_op jit(solution)/shard_map/ppermute | solution.py:318
  13.3 4.6 %collective-permute-start.4 = (f32[3,64,128]{2,1,0:T(8,128)S(1)}, f32[3,64,128]{2,1,0:T(8,128)S(1)}, u32[]{:S(2)}, u32[]{:S(2)}) collective-permute-start(f32[3,64,128]{2,1,0:T(8,128)S(1)} %constant_dynamic-update-slice_fusion.2), channel_id=1, source_target_pairs={{0,1},{1,0},{2,3},{3,2},{4,5},{5,4},{6,7},{7,6},{8,9},{9,8},{10,11... | collective-permute-start | bytes 294920 | tf_op jit(solution)/shard_map/ppermute | solution.py:318
  14.8 4.6 %collective-permute-start.6 = (f32[3,64,128]{2,1,0:T(8,128)S(1)}, f32[3,64,128]{2,1,0:T(8,128)S(1)}, u32[]{:S(2)}, u32[]{:S(2)}) collective-permute-start(f32[3,64,128]{2,1,0:T(8,128)S(1)} %collective-permute-done.5), channel_id=1, source_target_pairs={{0,1},{1,0},{2,3},{3,2},{4,5},{5,4},{6,7},{7,6},{8,9},{9,8},{10,11... | collective-permute-start | bytes 294920 | tf_op jit(solution)/shard_map/ppermute | solution.py:318
  15.4 4.6 %collective-permute-start.7 = (f32[3,64,128]{2,1,0:T(8,128)S(1)}, f32[3,64,128]{2,1,0:T(8,128)S(1)}, u32[]{:S(2)}, u32[]{:S(2)}) collective-permute-start(f32[3,64,128]{2,1,0:T(8,128)S(1)} %constant_dynamic-update-slice_fusion.2), channel_id=1, source_target_pairs={{0,2},{1,3},{2,0},{3,1},{4,6},{5,7},{6,4},{7,5},{8,10},{9,11},{10,... | collective-permute-start | bytes 294920 | tf_op jit(solution)/shard_map/ppermute | solution.py:318
  18.0 4.6 %collective-permute-start.8 = (f32[3,64,128]{2,1,0:T(8,128)S(1)}, f32[3,64,128]{2,1,0:T(8,128)S(1)}, u32[]{:S(2)}, u32[]{:S(2)}) collective-permute-start(f32[3,64,128]{2,1,0:T(8,128)S(1)} %collective-permute-done.4), channel_id=1, source_target_pairs={{0,2},{1,3},{2,0},{3,1},{4,6},{5,7},{6,4},{7,5},{8,10},{9,11},{10,... | collective-permute-start | bytes 294920 | tf_op jit(solution)/shard_map/ppermute | solution.py:318
  22.6 2.2 %collective-permute-start.10 = (f32[4,3,64,128]{3,2,1,0:T(8,128)S(1)}, f32[4,3,64,128]{3,2,1,0:T(8,128)S(1)}, u32[]{:S(2)}, u32[]{:S(2)}) collective-permute-start(f32[4,3,64,128]{3,2,1,0:T(8,128)S(1)} %pad_maximum_fusion.1.near_rest), channel_id=1, source_target_pairs={{0,4},{4,0},{1,5},{5,1},{2,6},{6,2},{3,7},{7,3},{8,12},{12,8},{9,1... | collective-permute-start | bytes 1179656 | tf_op jit(solution)/shard_map/ppermute | solution.py:322
  22.7 0.7 %copy-start.2 = (s32[2,2]{1,0:T(2,128)S(1)}, s32[2,2]{1,0:T(2,128)}, u32[]{:S(2)}) copy-start(s32[2,2]{1,0:T(2,128)} %tilt_ref.1) | copy-start | bytes 52
  22.7 2.0 %copy-start = (bf16[1024,256]{1,0:T(8,128)(2,1)S(1)}, bf16[1024,256]{1,0:T(8,128)(2,1)}, u32[]{:S(2)}) copy-start(bf16[1024,256]{1,0:T(8,128)(2,1)} %constant.18.clone.col_ref) | copy-start | bytes 1572868
  22.8 2.0 %copy-start.1 = (bf16[2,256,512]{2,1,0:T(8,128)(2,1)S(1)}, bf16[2,256,512]{2,1,0:T(8,128)(2,1)}, u32[]{:S(2)}) copy-start(bf16[2,256,512]{2,1,0:T(8,128)(2,1)} %constant.17.clone.row_ref) | copy-start | bytes 1572868
  22.8 2.0 %collective-permute-start.9 = (f32[4,2,64,128]{3,2,1,0:T(8,128)S(1)}, f32[4,2,64,128]{3,2,1,0:T(8,128)S(1)}, u32[]{:S(2)}, u32[]{:S(2)}) collective-permute-start(f32[4,2,64,128]{3,2,1,0:T(8,128)S(1)} %pad_maximum_fusion.2), channel_id=1, source_target_pairs={{0,4},{4,0},{1,5},{5,1},{2,6},{6,2},{3,7},{7,3},{8,12},{12,8},{9,1... | collective-permute-start | bytes 786440 | tf_op jit(solution)/shard_map/ppermute | solution.py:322
  33.1 1.4 %collective-permute-start.11 = (f32[1,3,64,128]{3,2,1,0:T(8,128)S(1)}, f32[1,3,64,128]{3,2,1,0:T(8,128)S(1)}, u32[]{:S(2)}, u32[]{:S(2)}) collective-permute-start(f32[1,3,64,128]{3,2,1,0:T(8,128)S(1)} %get-tuple-element.25), channel_id=1, source_target_pairs={{0,4},{4,0},{1,5},{5,1},{2,6},{6,2},{3,7},{7,3},{8,12},{12,8},{9,1... | collective-permute-start | bytes 294920 | tf_op jit(solution)/shard_map/ppermute | solution.py:322

commit v9 on v7

--- a/solution.py
+++ b/solution.py
@@ -95,11 +95,11 @@
     return jnp.concatenate([near_ref[where], far_ref[where]], axis=0)
 
 
-def block_turned(slice_index, block, screens, v_ref):
+def block_turned(slice_index, block, screens, wave_ref, place):
     near_cos, near_sin, far_cos, far_sin = screens
     cos = both_rows(near_cos, far_cos, (slice_index, block))
     sin = both_rows(near_sin, far_sin, (slice_index, block))
-    real, imag = v_ref[block, 0], v_ref[block, 1]
+    real, imag = wave_ref[place, 0], wave_ref[place, 1]
     return cos * real - sin * imag, cos * imag + sin * real
 
 
@@ -121,15 +121,18 @@
     )
 
 
-def advance(slice_index, start, size, screens, row_matrix, col_ref, v_ref, a_high, a_low):
-    height = v_ref.shape[2]
+def advance(slice_index, start, size, screens, row_matrix, col_ref, from_ref, to_ref, a_high, a_low):
+    height = from_ref.shape[2]
     half = LANES // 2
     own, edge = pl.ds(0, 2 * LANES), pl.ds(2 * LANES, 2 * LANES)
     low_own, low_edge = pl.ds(4 * LANES, 2 * LANES), pl.ds(6 * LANES, 2 * LANES)
     chunks = [range(place, min(place + 2, size)) for place in range(0, size, 2)]
     for chunk in chunks:
         columns = jnp.concatenate(
-            [jnp.concatenate(block_turned(slice_index, start + place, screens, v_ref), axis=0) for place in chunk],
+            [
+                jnp.concatenate(block_turned(slice_index, start + place, screens, from_ref, place), axis=0)
+                for place in chunk
+            ],
             axis=1,
         )
         done = row_product(row_matrix, columns)
@@ -154,18 +157,18 @@
                 col_ref[low_own],
             )
         )
-    cells, rows = pl.ds(0, size), size * height
-    edges = col_product(
-        a_high[cells, :, edge].reshape(rows, 2 * LANES),
-        a_low[cells, :, edge].reshape(rows, 2 * LANES),
-        col_ref[edge],
-        col_ref[low_edge],
-    )
     for chunk, done in zip(chunks, parts):
+        cells = pl.ds(chunk[0], len(chunk))
+        rows = len(chunk) * height
+        total = done + col_product(
+            a_high[cells, :, edge].reshape(rows, 2 * LANES),
+            a_low[cells, :, edge].reshape(rows, 2 * LANES),
+            col_ref[edge],
+            col_ref[low_edge],
+        )
         for sub, place in enumerate(chunk):
-            total = done[sub * height : (sub + 1) * height] + edges[place * height : (place + 1) * height]
             for part in range(2):
-                v_ref[start + place, part] = total[:, part * LANES : (part + 1) * LANES]
+                to_ref[place, part] = total[sub * height : (sub + 1) * height, part * LANES : (part + 1) * LANES]
 
 
 def clear_edge(a_ref, place, right):
@@ -211,16 +214,20 @@
 
 def wave_kernel(
     wave_ref, near_cos, near_sin, near_own, far_own, far_rest, row_ref, col_ref,
-    mine_ref, theirs_ref, far_cos, far_sin, v_ref, moved_ref, a_high, a_low,
+    mine_ref, theirs_ref, far_cos, far_sin, even_ref, odd_ref, moved_ref, left_ref, grad_ref,
+    even_high, even_low, odd_high, odd_low,
 ):
-    blocks, _, height, _ = v_ref.shape
+    blocks, _, height, _ = wave_ref.shape
     count = near_cos.shape[0] - 1
     core, own_section, own_place = lax.axis_index("row"), lax.axis_index("depth"), lax.axis_index("col")
     near, far = pl.ds(0, height // 2), pl.ds(height // 2, height // 2)
     screens = (near_cos, near_sin, far_cos, far_sin)
-    row_matrix = row_ref.at[core]
+    row_matrix = row_ref[core]
     window = min(3, blocks)
     window_start = jnp.clip(own_place - 1, 0, blocks - window)
+    own_in_window = own_place - window_start
+    waves = (even_ref, odd_ref)
+    sums = ((even_high, even_low), (odd_high, odd_low))
 
     def far_screens(slice_index):
         bits = slice_index ^ own_section
@@ -229,60 +236,57 @@
             angle = jnp.where(bits == 0, far_own[held, 0], far_rest[held, jnp.maximum(bits - 1, 0)])
             far_cos[slice_index, col], far_sin[slice_index, col] = cos_sin(angle)
 
-    for target in (a_high, a_low):
-        clear_edge(target, 0, False)
-        clear_edge(target, blocks - 1, True)
+    for pair in sums:
+        for target in pair:
+            clear_edge(target, 0, False)
+            clear_edge(target, blocks - 1, True)
     far_cos[count] = jnp.ones(far_cos.shape[1:], jnp.float32)
     far_sin[count] = jnp.zeros(far_cos.shape[1:], jnp.float32)
-    v_ref[...] = wave_ref[...]
     far_screens(0)
 
-    def forward(tick, carry):
-        @pl.when(tick == own_section)
-        def _():
-            moved_ref[0], moved_ref[1] = block_turned(tick, own_place, screens, v_ref)
-
-        advance(tick, 0, blocks, screens, row_matrix[...], col_ref, v_ref, a_high, a_low)
-        far_screens(jnp.minimum(tick + 1, count - 1))
-
-        @pl.when(tick == own_section)
-        def _():
-            for target, row in ((mine_ref, near), (theirs_ref, far)):
-                for part in range(2):
-                    target[0, part] = v_ref[own_place, part, row]
-
-        return carry
-
-    lax.fori_loop(0, count, forward, 0)
-
-    for target in (a_high, a_low):
-        clear_edge(target, window - 1, True)
+    for tick in range(count):
+        source, target = wave_ref if tick == 0 else waves[tick % 2], waves[(tick + 1) % 2]
+        moved_ref[tick, 0], moved_ref[tick, 1] = block_turned(tick, own_place, screens, source, own_place)
+        advance(tick, 0, blocks, screens, row_matrix, col_ref, source, target, *sums[tick % 2])
+        if tick + 1 < count:
+            far_screens(tick + 1)
+        left_ref[tick] = target[own_place]
+
+    last = waves[count % 2]
+    source = waves[(count + 1) % 2]
+    for pair in sums:
+        for target in pair:
+            clear_edge(target, window - 1, True)
     for place in range(window):
         block = window_start + place
         held = block ^ own_place
-        for row, measured in ((near, near_own[held, 1 + core]), (far, far_own[held, 1])):
-            real, imag = v_ref[block, 0, row], v_ref[block, 1, row]
-            misfit = 2.0 * (real * real + imag * imag - measured)
-            v_ref[block, 0, row] = misfit * real
-            v_ref[block, 1, row] = -misfit * imag
-
-    def backward(tick, carry):
-        advance(count - tick, window_start, window, screens, row_matrix[...], col_ref, v_ref, a_high, a_low)
-        return carry
-
-    lax.fori_loop(0, count - 1 - own_section, backward, 0)
-
+        measured = jnp.concatenate([near_own[held, 1 + core], far_own[held, 1]], axis=0)
+        real, imag = last[block, 0], last[block, 1]
+        misfit = 2.0 * (real * real + imag * imag - measured)
+        source[place, 0] = misfit * real
+        source[place, 1] = -misfit * imag
+
+    for tick in range(count - 1):
+        source, target = waves[(count + 1 + tick) % 2], waves[(count + tick) % 2]
+        advance(
+            count - tick, window_start, window, screens, row_matrix, col_ref, source, target, *sums[tick % 2]
+        )
+        arrived = count - 1 - tick
+        pulled = target[own_in_window, 0], target[own_in_window, 1]
+        grad_ref[arrived] = -(pulled[1] * moved_ref[arrived, 0] + pulled[0] * moved_ref[arrived, 1])
+
+    source = waves[(2 * count) % 2]
     left, right = jnp.maximum(own_place - 1, 0), jnp.minimum(own_place + 1, blocks - 1)
     lane = lax.broadcasted_iota(jnp.int32, (2 * height, LANES), 1)
     has_left, has_right = own_place > 0, own_place < blocks - 1
-    behind = own_section + 1
-    own_cells = jnp.concatenate(block_turned(behind, own_place, screens, v_ref), axis=0)
-    left_cells = jnp.concatenate(block_turned(behind, left, screens, v_ref), axis=0)
-    right_cells = jnp.concatenate(block_turned(behind, right, screens, v_ref), axis=0)
+
+    def cells(block):
+        return jnp.concatenate(block_turned(1, block, screens, source, block - window_start), axis=0)
+
     edge_cells = jnp.where(
-        lane < LANES // 2, jnp.where(has_right, right_cells, 0.0), jnp.where(has_left, left_cells, 0.0)
+        lane < LANES // 2, jnp.where(has_right, cells(right), 0.0), jnp.where(has_left, cells(left), 0.0)
     )
-    done = row_product(row_matrix[...], jnp.concatenate([own_cells, edge_cells], axis=1))
+    done = row_product(row_matrix, jnp.concatenate([cells(own_place), edge_cells], axis=1))
     quarters = [
         done[part * height : (part + 1) * height, sub * LANES : (sub + 1) * LANES]
         for sub in range(2)
@@ -290,9 +294,12 @@
     ]
     high, low = halves(jnp.concatenate(quarters, axis=1))
     pulled = col_product(high, low, col_ref[: 4 * LANES], col_ref[4 * LANES :])
-    gradient = -(pulled[:, LANES:] * moved_ref[0] + pulled[:, :LANES] * moved_ref[1])
-    mine_ref[0, 2] = gradient[: height // 2]
-    theirs_ref[0, 2] = gradient[height // 2 :]
+    grad_ref[0] = -(pulled[:, LANES:] * moved_ref[0, 0] + pulled[:, :LANES] * moved_ref[0, 1])
+
+    for target, row in ((mine_ref, near), (theirs_ref, far)):
+        for part in range(2):
+            target[0, part] = left_ref[own_section, part, row]
+        target[0, 2] = grad_ref[own_section, row]
 
 
 def finish_kernel(mine_ref, received_ref, grad_ref, exit_ref, total_ref, sems):
@@ -376,8 +383,10 @@
         in_specs=[vmem] * 8,
         out_specs=(vmem,) * 2,
         scratch_shapes=[pltpu.VMEM(half_screens, jnp.float32)] * 2
-        + [pltpu.VMEM(field, jnp.float32), pltpu.VMEM((2, height, tile_c), jnp.float32)]
-        + [pltpu.VMEM((blocks, height, 4 * LANES), jnp.bfloat16)] * 2,
+        + [pltpu.VMEM(field, jnp.float32)] * 2
+        + [pltpu.VMEM((count, 2, height, tile_c), jnp.float32)] * 2
+        + [pltpu.VMEM((count, height, tile_c), jnp.float32)]
+        + [pltpu.VMEM((blocks, height, 4 * LANES), jnp.bfloat16)] * 4,
         compiler_params=params(24),
     )(
         wave, near_cos, near_sin, near_own, far_own, far_rest,

time: 33.9 us -> 33.7 us (level)
  no operation moved by 1% of the time
where the time goes in v9:
time: 33.7 us; the launch traced here: 33.4 us
  starting transfers between devices  16.6 us (49%)
  Pallas kernels  9.84 us (29%)
  waiting for transfers between devices  5.18 us (15%)
  local copies, waits for them, and re-layouts  0.93 us (3%)
  between operations  0.77 us (2%)
    ppermute x6, starting transfers between devices, spread(): lax.ppermute(shard, axis, pairs)  10.2 us
    pallas_call x1, Pallas kernels, whole_field_body(): pl.pallas_call(wave_kernel, out_shape=(array(1, 3, tile_r, tile_c),) * 2,...  8.03 us
    ppermute x2, starting transfers between devices, whole_field_body(): near_own.append(lax.ppermute(packet, 'col', close))  3.94 us
    ppermute x6, waiting for transfers between devices, spread(): lax.ppermute(shard, axis, pairs)  3.91 us
    ppermute x1, starting transfers between devices, whole_field_body(): lax.ppermute(slab, 'col', further)  1.52 us
    ppermute x3, waiting for transfers between devices, swap_cores(): return lax.ppermute(value, 'row', [(0, 1), (1, 0)])  1.26 us
    pallas_call x1, Pallas kernels, whole_field_body(): pl.pallas_call(prepare_kernel, out_shape=(array(*field), array(*half_scre...  1.13 us
    ppermute x3, starting transfers between devices, swap_cores(): return lax.ppermute(value, 'row', [(0, 1), (1, 0)])  0.97 us
  transfers between devices with their start and end apart: 12, of which 3 were waited for; matrix products, arithmetic and copies ran while one was open for 3% of the time, Pallas kernels for 3%

profile of v9, /device:TPU:0, one launch (start us, length us, event | category | flops | bytes accessed | tf_op | source)
XLA Modules:
  0.0 33.4 jit_solution(15476100625610121990)
XLA Ops:
  0.6 0.0 copy-start.3
  0.6 3.1 %collective-permute-start = (f32[1,64,128]{2,1,0:T(8,128)}, f32[1,64,128]{2,1,0:T(8,128)S(1)}, u32[]{:S(2)}, u32[]{:S(2)}) collective-permute-start(f32[1,64,128]{2,1,0:T(8,128)} %param.5), channel_id=1, source_target_pairs={{0,8},{8,0},{16,24},{24,16},{1,9},{9,1},{17,25},{25,17},{2,10},{10... | collective-permute-start | bytes 98312 | tf_op jit(solution)/shard_map/ppermute | solution.py:325
  3.7 2.5 %collective-permute-start.2 = (f32[1,64,128]{2,1,0:T(8,128)}, f32[1,64,128]{2,1,0:T(8,128)S(1)}, u32[]{:S(2)}, u32[]{:S(2)}) collective-permute-start(f32[1,64,128]{2,1,0:T(8,128)} %param.5), channel_id=1, source_target_pairs={{0,24},{8,16},{16,8},{24,0},{1,25},{9,17},{17,9},{25,1},{2,26},{10... | collective-permute-start | bytes 98312 | tf_op jit(solution)/shard_map/ppermute | solution.py:325
  6.2 0.1 collective-permute-start.1
  6.3 0.0 collective-permute-done
  6.3 1.5 %collective-permute-start.5 = (f32[1,64,128]{2,1,0:T(8,128)}, f32[1,64,128]{2,1,0:T(8,128)S(1)}, u32[]{:S(2)}, u32[]{:S(2)}) collective-permute-start(f32[1,64,128]{2,1,0:T(8,128)} %param.5), channel_id=1, source_target_pairs={{0,2},{1,3},{2,0},{3,1},{4,6},{5,7},{6,4},{7,5},{8,10},{9,11},{10,... | collective-permute-start | bytes 98312 | tf_op jit(solution)/shard_map/ppermute | solution.py:360
  7.8 0.8 %constant_dynamic-update-slice_fusion.4 = f32[3,64,128]{2,1,0:T(8,128)S(1)} fusion(f32[1,64,128]{2,1,0:T(8,128)} %param.5), kind=kLoop, calls=%fused_computation.8 | loop fusion | bytes 65536
  8.6 0.0 copy-done.3
  8.7 0.7 %collective-permute-start.6 = (f32[3,64,128]{2,1,0:T(8,128)S(1)}, f32[3,64,128]{2,1,0:T(8,128)S(1)}, u32[]{:S(2)}, u32[]{:S(2)}) collective-permute-start(f32[3,64,128]{2,1,0:T(8,128)S(1)} %constant_dynamic-update-slice_fusion.3), channel_id=1, source_target_pairs={{1,2},{2,1},{5,6},{6,5},{9,10},{10,9},{13,14},{14,13},{17,18},{18,... | collective-permute-start | bytes 294920 | tf_op jit(solution)/shard_map/ppermute | solution.py:357
  9.3 3.3 %collective-permute-start.4 = (f32[3,64,128]{2,1,0:T(8,128)S(1)}, f32[3,64,128]{2,1,0:T(8,128)S(1)}, u32[]{:S(2)}, u32[]{:S(2)}) collective-permute-start(f32[3,64,128]{2,1,0:T(8,128)S(1)} %constant_dynamic-update-slice_fusion.3), channel_id=1, source_target_pairs={{0,1},{1,0},{2,3},{3,2},{4,5},{5,4},{6,7},{7,6},{8,9},{9,8},{10,11... | collective-permute-start | bytes 294920 | tf_op jit(solution)/shard_map/ppermute | solution.py:357
  12.6 0.0 collective-permute-done.1
  12.6 0.0 collective-permute-done.2
  12.6 0.7 %collective-permute-start.8 = (f32[3,64,128]{2,1,0:T(8,128)S(1)}, f32[3,64,128]{2,1,0:T(8,128)S(1)}, u32[]{:S(2)}, u32[]{:S(2)}) collective-permute-start(f32[3,64,128]{2,1,0:T(8,128)S(1)} %constant_dynamic-update-slice_fusion), channel_id=1, source_target_pairs={{1,2},{2,1},{5,6},{6,5},{9,10},{10,9},{13,14},{14,13},{17,18},{18,... | collective-permute-start | bytes 294920 | tf_op jit(solution)/shard_map/ppermute | solution.py:325
  13.3 3.2 %collective-permute-start.7 = (f32[3,64,128]{2,1,0:T(8,128)S(1)}, f32[3,64,128]{2,1,0:T(8,128)S(1)}, u32[]{:S(2)}, u32[]{:S(2)}) collective-permute-start(f32[3,64,128]{2,1,0:T(8,128)S(1)} %constant_dynamic-update-slice_fusion), channel_id=1, source_target_pairs={{0,2},{1,3},{2,0},{3,1},{4,6},{5,7},{6,4},{7,5},{8,10},{9,11},{10,... | collective-permute-start | bytes 294920 | tf_op jit(solution)/shard_map/ppermute | solution.py:325
  16.5 0.0 collective-permute-done.5
  16.5 0.7 %collective-permute-start.3 = (f32[3,64,128]{2,1,0:T(8,128)S(1)}, f32[3,64,128]{2,1,0:T(8,128)S(1)}, u32[]{:S(2)}, u32[]{:S(2)}) collective-permute-start(f32[3,64,128]{2,1,0:T(8,128)S(1)} %constant_dynamic-update-slice_fusion), channel_id=1, source_target_pairs={{0,1},{1,0},{2,3},{3,2},{4,5},{5,4},{6,7},{7,6},{8,9},{9,8},{10,11... | collective-permute-start | bytes 294920 | tf_op jit(solution)/shard_map/ppermute | solution.py:325
  17.2 0.0 collective-permute-done.6
  17.2 0.0 collective-permute-done.4
  17.3 3.9 %collective-permute-done.3 = f32[3,64,128]{2,1,0:T(8,128)S(1)} collective-permute-done((f32[3,64,128]{2,1,0:T(8,128)S(1)}, f32[3,64,128]{2,1,0:T(8,128)S(1)}, u32[]{:S(2)}, u32[]{:S(2)}) %collective-permute-start.3) | collective-permute-done | bytes 98336 | tf_op jit(solution)/shard_map/ppermute | solution.py:325
  21.2 0.0 collective-permute-done.8
  21.2 0.0 collective-permute-done.7
  21.2 0.1 collective-permute-start.10
  21.3 0.0 copy-start.2
  21.3 0.0 copy-start
  21.4 0.0 copy-start.1
  21.4 0.6 %collective-permute-start.9 = (f32[4,2,64,128]{3,2,1,0:T(8,128)S(1)}, f32[4,2,64,128]{3,2,1,0:T(8,128)S(1)}, u32[]{:S(2)}, u32[]{:S(2)}) collective-permute-start(f32[4,2,64,128]{3,2,1,0:T(8,128)S(1)} %pad_maximum_fusion.2), channel_id=1, source_target_pairs={{0,4},{4,0},{1,5},{5,1},{2,6},{6,2},{3,7},{7,3},{8,12},{12,8},{9,1... | collective-permute-start | bytes 786440 | tf_op jit(solution)/shard_map/ppermute | solution.py:330
  21.9 0.1 copy-done.2
  22.0 1.1 %shard_map.68 = (f32[4,2,128,128]{3,2,1,0:T(8,128)S(1)}, f32[5,4,64,128]{3,2,1,0:T(8,128)S(1)}, f32[5,4,64,128]{3,2,1,0:T(8,128)S(1)}) custom-call(s32[2,2]{1,0:T(2,128)S(1)} %copy-done.2, f32[4,3,64,128]{3,2,1,0:T(8,128)S(1)} %pad_maximum_fusion.near_own, f32[4,3,64,128]{3,2,1,0:T(8,128)S(1)} %pad_maximum_fusion.1.near_rest), custom_call_target="tpu_custom_call" | custom-call | flops 500000000 | bytes 1048576 | tf_op jit(solution)/shard_map/pallas_call | solution.py:372
  23.1 0.2 collective-permute-done.9.far_own
  23.4 0.0 collective-permute-done.10.far_rest
  23.4 0.0 copy-done
  23.4 0.0 copy-done.1
  23.4 8.0 %shard_map.69 = (f32[1,3,64,128]{3,2,1,0:T(8,128)S(1)}, f32[1,3,64,128]{3,2,1,0:T(8,128)S(1)}) custom-call(f32[4,2,128,128]{3,2,1,0:T(8,128)S(1)} %get-tuple-element.17.wave_ref, f32[5,4,64,128]{3,2,1,0:T(8,128)S(1)} %get-tuple-element.18.near_cos, f32[5,4,64,128]{3,2,1,0:T(8,128)S(1)} %get-tuple-element.19.near_sin, ...), custom_call_target="tpu_custom_call" | custom-call | tf_op jit(solution)/shard_map/pallas_call | solution.py:380
  31.4 0.3 %collective-permute-start.11 = (f32[1,3,64,128]{3,2,1,0:T(8,128)S(1)}, f32[1,3,64,128]{3,2,1,0:T(8,128)S(1)}, u32[]{:S(2)}, u32[]{:S(2)}) collective-permute-start(f32[1,3,64,128]{3,2,1,0:T(8,128)S(1)} %get-tuple-element.21), channel_id=1, source_target_pairs={{0,4},{4,0},{1,5},{5,1},{2,6},{6,2},{3,7},{7,3},{8,12},{12,8},{9,1... | collective-permute-start | bytes 294920 | tf_op jit(solution)/shard_map/ppermute | solution.py:330
  31.7 1.0 %collective-permute-done.11.received_ref = f32[1,3,64,128]{3,2,1,0:T(8,128)S(1)} collective-permute-done((f32[1,3,64,128]{3,2,1,0:T(8,128)S(1)}, f32[1,3,64,128]{3,2,1,0:T(8,128)S(1)}, u32[]{:S(2)}, u32[]{:S(2)}) %collective-permute-start.11) | collective-permute-done | bytes 98336 | tf_op jit(solution)/shard_map/ppermute | solution.py:330
  32.8 0.7 %shard_map.70 = (f32[1,64,128]{2,1,0:T(8,128)}, f32[2,1,2,64,128]{4,3,2,1,0:T(8,128)}) custom-call(f32[1,3,64,128]{3,2,1,0:T(8,128)S(1)} %get-tuple-element.20.mine_ref, f32[1,3,64,128]{3,2,1,0:T(8,128)S(1)} %collective-permute-done.11.received_ref), custom_call_target="tpu_custom_call" | custom-call | tf_op jit(solution)/shard_map/pallas_call | solution.py:395
  (9 shorter events, 0.1 us)
Async XLA Ops:
  0.6 8.0 %copy-start.3 = (f32[2,64,128]{2,1,0:T(8,128)S(1)}, f32[2,64,128]{2,1,0:T(8,128)}, u32[]{:S(2)}) copy-start(f32[2,64,128]{2,1,0:T(8,128)} %param.7) | copy-start | bytes 196612
  0.6 5.7 %collective-permute-start = (f32[1,64,128]{2,1,0:T(8,128)}, f32[1,64,128]{2,1,0:T(8,128)S(1)}, u32[]{:S(2)}, u32[]{:S(2)}) collective-permute-start(f32[1,64,128]{2,1,0:T(8,128)} %param.5), channel_id=1, source_target_pairs={{0,8},{8,0},{16,24},{24,16},{1,9},{9,1},{17,25},{25,17},{2,10},{10... | collective-permute-start | bytes 98312 | tf_op jit(solution)/shard_map/ppermute | solution.py:325
  3.7 8.9 %collective-permute-start.2 = (f32[1,64,128]{2,1,0:T(8,128)}, f32[1,64,128]{2,1,0:T(8,128)S(1)}, u32[]{:S(2)}, u32[]{:S(2)}) collective-permute-start(f32[1,64,128]{2,1,0:T(8,128)} %param.5), channel_id=1, source_target_pairs={{0,24},{8,16},{16,8},{24,0},{1,25},{9,17},{17,9},{25,1},{2,26},{10... | collective-permute-start | bytes 98312 | tf_op jit(solution)/shard_map/ppermute | solution.py:325
  6.2 6.4 %collective-permute-start.1 = (f32[1,64,128]{2,1,0:T(8,128)}, f32[1,64,128]{2,1,0:T(8,128)S(1)}, u32[]{:S(2)}, u32[]{:S(2)}) collective-permute-start(f32[1,64,128]{2,1,0:T(8,128)} %param.5), channel_id=1, source_target_pairs={{0,16},{8,24},{16,0},{24,8},{1,17},{9,25},{17,1},{25,9},{2,18},{10... | collective-permute-start | bytes 98312 | tf_op jit(solution)/shard_map/ppermute | solution.py:325
  6.3 10.2 %collective-permute-start.5 = (f32[1,64,128]{2,1,0:T(8,128)}, f32[1,64,128]{2,1,0:T(8,128)S(1)}, u32[]{:S(2)}, u32[]{:S(2)}) collective-permute-start(f32[1,64,128]{2,1,0:T(8,128)} %param.5), channel_id=1, source_target_pairs={{0,2},{1,3},{2,0},{3,1},{4,6},{5,7},{6,4},{7,5},{8,10},{9,11},{10,... | collective-permute-start | bytes 98312 | tf_op jit(solution)/shard_map/ppermute | solution.py:360
  8.7 8.6 %collective-permute-start.6 = (f32[3,64,128]{2,1,0:T(8,128)S(1)}, f32[3,64,128]{2,1,0:T(8,128)S(1)}, u32[]{:S(2)}, u32[]{:S(2)}) collective-permute-start(f32[3,64,128]{2,1,0:T(8,128)S(1)} %constant_dynamic-update-slice_fusion.3), channel_id=1, source_target_pairs={{1,2},{2,1},{5,6},{6,5},{9,10},{10,9},{13,14},{14,13},{17,18},{18,... | collective-permute-start | bytes 294920 | tf_op jit(solution)/shard_map/ppermute | solution.py:357
  9.3 7.9 %collective-permute-start.4 = (f32[3,64,128]{2,1,0:T(8,128)S(1)}, f32[3,64,128]{2,1,0:T(8,128)S(1)}, u32[]{:S(2)}, u32[]{:S(2)}) collective-permute-start(f32[3,64,128]{2,1,0:T(8,128)S(1)} %constant_dynamic-update-slice_fusion.3), channel_id=1, source_target_pairs={{0,1},{1,0},{2,3},{3,2},{4,5},{5,4},{6,7},{7,6},{8,9},{9,8},{10,11... | collective-permute-start | bytes 294920 | tf_op jit(solution)/shard_map/ppermute | solution.py:357
  12.6 8.5 %collective-permute-start.8 = (f32[3,64,128]{2,1,0:T(8,128)S(1)}, f32[3,64,128]{2,1,0:T(8,128)S(1)}, u32[]{:S(2)}, u32[]{:S(2)}) collective-permute-start(f32[3,64,128]{2,1,0:T(8,128)S(1)} %constant_dynamic-update-slice_fusion), channel_id=1, source_target_pairs={{1,2},{2,1},{5,6},{6,5},{9,10},{10,9},{13,14},{14,13},{17,18},{18,... | collective-permute-start | bytes 294920 | tf_op jit(solution)/shard_map/ppermute | solution.py:325
  13.3 7.8 %collective-permute-start.7 = (f32[3,64,128]{2,1,0:T(8,128)S(1)}, f32[3,64,128]{2,1,0:T(8,128)S(1)}, u32[]{:S(2)}, u32[]{:S(2)}) collective-permute-start(f32[3,64,128]{2,1,0:T(8,128)S(1)} %constant_dynamic-update-slice_fusion), channel_id=1, source_target_pairs={{0,2},{1,3},{2,0},{3,1},{4,6},{5,7},{6,4},{7,5},{8,10},{9,11},{10,... | collective-permute-start | bytes 294920 | tf_op jit(solution)/shard_map/ppermute | solution.py:325
  16.5 4.6 %collective-permute-start.3 = (f32[3,64,128]{2,1,0:T(8,128)S(1)}, f32[3,64,128]{2,1,0:T(8,128)S(1)}, u32[]{:S(2)}, u32[]{:S(2)}) collective-permute-start(f32[3,64,128]{2,1,0:T(8,128)S(1)} %constant_dynamic-update-slice_fusion), channel_id=1, source_target_pairs={{0,1},{1,0},{2,3},{3,2},{4,5},{5,4},{6,7},{7,6},{8,9},{9,8},{10,11... | collective-permute-start | bytes 294920 | tf_op jit(solution)/shard_map/ppermute | solution.py:325
  21.2 2.2 %collective-permute-start.10 = (f32[4,3,64,128]{3,2,1,0:T(8,128)S(1)}, f32[4,3,64,128]{3,2,1,0:T(8,128)S(1)}, u32[]{:S(2)}, u32[]{:S(2)}) collective-permute-start(f32[4,3,64,128]{3,2,1,0:T(8,128)S(1)} %pad_maximum_fusion.1.near_rest), channel_id=1, source_target_pairs={{0,4},{4,0},{1,5},{5,1},{2,6},{6,2},{3,7},{7,3},{8,12},{12,8},{9,1... | collective-permute-start | bytes 1179656 | tf_op jit(solution)/shard_map/ppermute | solution.py:330
  21.3 0.7 %copy-start.2 = (s32[2,2]{1,0:T(2,128)S(1)}, s32[2,2]{1,0:T(2,128)}, u32[]{:S(2)}) copy-start(s32[2,2]{1,0:T(2,128)} %tilt_ref.1) | copy-start | bytes 52
  21.3 2.0 %copy-start = (bf16[1024,256]{1,0:T(8,128)(2,1)S(1)}, bf16[1024,256]{1,0:T(8,128)(2,1)}, u32[]{:S(2)}) copy-start(bf16[1024,256]{1,0:T(8,128)(2,1)} %constant.20.clone.col_ref) | copy-start | bytes 1572868
  21.4 2.0 %copy-start.1 = (bf16[2,256,512]{2,1,0:T(8,128)(2,1)S(1)}, bf16[2,256,512]{2,1,0:T(8,128)(2,1)}, u32[]{:S(2)}) copy-start(bf16[2,256,512]{2,1,0:T(8,128)(2,1)} %constant.19.clone.row_ref) | copy-start | bytes 1572868
  21.4 2.0 %collective-permute-start.9 = (f32[4,2,64,128]{3,2,1,0:T(8,128)S(1)}, f32[4,2,64,128]{3,2,1,0:T(8,128)S(1)}, u32[]{:S(2)}, u32[]{:S(2)}) collective-permute-start(f32[4,2,64,128]{3,2,1,0:T(8,128)S(1)} %pad_maximum_fusion.2), channel_id=1, source_target_pairs={{0,4},{4,0},{1,5},{5,1},{2,6},{6,2},{3,7},{7,3},{8,12},{12,8},{9,1... | collective-permute-start | bytes 786440 | tf_op jit(solution)/shard_map/ppermute | solution.py:330
  31.4 1.4 %collective-permute-start.11 = (f32[1,3,64,128]{3,2,1,0:T(8,128)S(1)}, f32[1,3,64,128]{3,2,1,0:T(8,128)S(1)}, u32[]{:S(2)}, u32[]{:S(2)}) collective-permute-start(f32[1,3,64,128]{3,2,1,0:T(8,128)S(1)} %get-tuple-element.21), channel_id=1, source_target_pairs={{0,4},{4,0},{1,5},{5,1},{2,6},{6,2},{3,7},{7,3},{8,12},{12,8},{9,1... | collective-permute-start | bytes 294920 | tf_op jit(solution)/shard_map/ppermute | solution.py:330

commit v10 on v9

--- a/solution.py
+++ b/solution.py
@@ -124,51 +124,30 @@
 def advance(slice_index, start, size, screens, row_matrix, col_ref, from_ref, to_ref, a_high, a_low):
     height = from_ref.shape[2]
     half = LANES // 2
-    own, edge = pl.ds(0, 2 * LANES), pl.ds(2 * LANES, 2 * LANES)
-    low_own, low_edge = pl.ds(4 * LANES, 2 * LANES), pl.ds(6 * LANES, 2 * LANES)
-    chunks = [range(place, min(place + 2, size)) for place in range(0, size, 2)]
-    for chunk in chunks:
-        columns = jnp.concatenate(
-            [
-                jnp.concatenate(block_turned(slice_index, start + place, screens, from_ref, place), axis=0)
-                for place in chunk
-            ],
-            axis=1,
-        )
-        done = row_product(row_matrix, columns)
-        for sub, place in enumerate(chunk):
-            for part in range(2):
-                value = done[part * height : (part + 1) * height, sub * LANES : (sub + 1) * LANES]
-                for target, piece in zip((a_high, a_low), halves(value)):
-                    target[place, :, pl.ds(part * LANES, LANES)] = piece
-                    if place > 0:
-                        target[place - 1, :, pl.ds((2 + part) * LANES, half)] = piece[:, :half]
-                    if place < size - 1:
-                        target[place + 1, :, pl.ds((2 + part) * LANES + half, half)] = piece[:, half:]
-    parts = []
-    for chunk in chunks:
-        cells = pl.ds(chunk[0], len(chunk))
-        rows = len(chunk) * height
-        parts.append(
-            col_product(
-                a_high[cells, :, own].reshape(rows, 2 * LANES),
-                a_low[cells, :, own].reshape(rows, 2 * LANES),
-                col_ref[own],
-                col_ref[low_own],
-            )
-        )
-    for chunk, done in zip(chunks, parts):
-        cells = pl.ds(chunk[0], len(chunk))
-        rows = len(chunk) * height
-        total = done + col_product(
-            a_high[cells, :, edge].reshape(rows, 2 * LANES),
-            a_low[cells, :, edge].reshape(rows, 2 * LANES),
-            col_ref[edge],
-            col_ref[low_edge],
-        )
-        for sub, place in enumerate(chunk):
-            for part in range(2):
-                to_ref[place, part] = total[sub * height : (sub + 1) * height, part * LANES : (part + 1) * LANES]
+    columns = [
+        jnp.concatenate(block_turned(slice_index, start + place, screens, from_ref, place), axis=0)
+        for place in range(size)
+    ]
+    done = row_product(row_matrix, jnp.concatenate(columns, axis=1))
+    for place in range(size):
+        for part in range(2):
+            value = done[part * height : (part + 1) * height, place * LANES : (place + 1) * LANES]
+            for target, piece in zip((a_high, a_low), halves(value)):
+                target[place, :, pl.ds(part * LANES, LANES)] = piece
+                if place > 0:
+                    target[place - 1, :, pl.ds((2 + part) * LANES, half)] = piece[:, :half]
+                if place < size - 1:
+                    target[place + 1, :, pl.ds((2 + part) * LANES + half, half)] = piece[:, half:]
+    cells, rows = pl.ds(0, size), size * height
+    total = col_product(
+        a_high[cells].reshape(rows, 4 * LANES),
+        a_low[cells].reshape(rows, 4 * LANES),
+        col_ref[: 4 * LANES],
+        col_ref[4 * LANES :],
+    )
+    for place in range(size):
+        for part in range(2):
+            to_ref[place, part] = total[place * height : (place + 1) * height, part * LANES : (part + 1) * LANES]
 
 
 def clear_edge(a_ref, place, right):

time: 33.7 us -> 35.6 us (1.056)
  Pallas kernels: 9.84 us -> 11.8 us
    pallas_call x1, Pallas kernels: 8.03 us -> 9.99 us  [whole_field_body(): pl.pallas_call(wave_kernel, out_shape=(array(1, 3, tile_r, tile_c),) * 2,...]
where the time goes in v10:
time: 35.6 us; the launch traced here: 35.4 us
  starting transfers between devices  16.7 us (47%)
  Pallas kernels  11.8 us (33%)
  waiting for transfers between devices  5.18 us (15%)
  local copies, waits for them, and re-layouts  0.93 us (3%)
  between operations  0.77 us (2%)
    ppermute x6, starting transfers between devices, spread(): lax.ppermute(shard, axis, pairs)  10.2 us
    pallas_call x1, Pallas kernels, whole_field_body(): pl.pallas_call(wave_kernel, out_shape=(array(1, 3, tile_r, tile_c),) * 2,...  9.99 us
    ppermute x2, starting transfers between devices, whole_field_body(): near_own.append(lax.ppermute(packet, 'col', close))  3.94 us
    ppermute x6, waiting for transfers between devices, spread(): lax.ppermute(shard, axis, pairs)  3.91 us
    ppermute x1, starting transfers between devices, whole_field_body(): lax.ppermute(slab, 'col', further)  1.52 us
    ppermute x3, waiting for transfers between devices, swap_cores(): return lax.ppermute(value, 'row', [(0, 1), (1, 0)])  1.26 us
    pallas_call x1, Pallas kernels, whole_field_body(): pl.pallas_call(prepare_kernel, out_shape=(array(*field), array(*half_scre...  1.13 us
    ppermute x3, starting transfers between devices, swap_cores(): return lax.ppermute(value, 'row', [(0, 1), (1, 0)])  0.97 us
  transfers between devices with their start and end apart: 12, of which 3 were waited for; matrix products, arithmetic and copies ran while one was open for 3% of the time, Pallas kernels for 3%

profile of v10, /device:TPU:0, one launch (start us, length us, event | category | flops | bytes accessed | tf_op | source)
XLA Modules:
  0.0 35.4 jit_solution(10019819974929329515)
XLA Ops:
  0.6 0.0 copy-start.3
  0.6 3.1 %collective-permute-start = (f32[1,64,128]{2,1,0:T(8,128)}, f32[1,64,128]{2,1,0:T(8,128)S(1)}, u32[]{:S(2)}, u32[]{:S(2)}) collective-permute-start(f32[1,64,128]{2,1,0:T(8,128)} %param.5), channel_id=1, source_target_pairs={{0,8},{8,0},{16,24},{24,16},{1,9},{9,1},{17,25},{25,17},{2,10},{10... | collective-permute-start | bytes 98312 | tf_op jit(solution)/shard_map/ppermute | solution.py:304
  3.7 2.5 %collective-permute-start.2 = (f32[1,64,128]{2,1,0:T(8,128)}, f32[1,64,128]{2,1,0:T(8,128)S(1)}, u32[]{:S(2)}, u32[]{:S(2)}) collective-permute-start(f32[1,64,128]{2,1,0:T(8,128)} %param.5), channel_id=1, source_target_pairs={{0,24},{8,16},{16,8},{24,0},{1,25},{9,17},{17,9},{25,1},{2,26},{10... | collective-permute-start | bytes 98312 | tf_op jit(solution)/shard_map/ppermute | solution.py:304
  6.2 0.1 collective-permute-start.1
  6.3 0.0 collective-permute-done
  6.3 1.5 %collective-permute-start.5 = (f32[1,64,128]{2,1,0:T(8,128)}, f32[1,64,128]{2,1,0:T(8,128)S(1)}, u32[]{:S(2)}, u32[]{:S(2)}) collective-permute-start(f32[1,64,128]{2,1,0:T(8,128)} %param.5), channel_id=1, source_target_pairs={{0,2},{1,3},{2,0},{3,1},{4,6},{5,7},{6,4},{7,5},{8,10},{9,11},{10,... | collective-permute-start | bytes 98312 | tf_op jit(solution)/shard_map/ppermute | solution.py:339
  7.8 0.8 %constant_dynamic-update-slice_fusion.4 = f32[3,64,128]{2,1,0:T(8,128)S(1)} fusion(f32[1,64,128]{2,1,0:T(8,128)} %param.5), kind=kLoop, calls=%fused_computation.8 | loop fusion | bytes 65536
  8.6 0.0 copy-done.3
  8.7 0.7 %collective-permute-start.6 = (f32[3,64,128]{2,1,0:T(8,128)S(1)}, f32[3,64,128]{2,1,0:T(8,128)S(1)}, u32[]{:S(2)}, u32[]{:S(2)}) collective-permute-start(f32[3,64,128]{2,1,0:T(8,128)S(1)} %constant_dynamic-update-slice_fusion.3), channel_id=1, source_target_pairs={{1,2},{2,1},{5,6},{6,5},{9,10},{10,9},{13,14},{14,13},{17,18},{18,... | collective-permute-start | bytes 294920 | tf_op jit(solution)/shard_map/ppermute | solution.py:336
  9.3 3.3 %collective-permute-start.4 = (f32[3,64,128]{2,1,0:T(8,128)S(1)}, f32[3,64,128]{2,1,0:T(8,128)S(1)}, u32[]{:S(2)}, u32[]{:S(2)}) collective-permute-start(f32[3,64,128]{2,1,0:T(8,128)S(1)} %constant_dynamic-update-slice_fusion.3), channel_id=1, source_target_pairs={{0,1},{1,0},{2,3},{3,2},{4,5},{5,4},{6,7},{7,6},{8,9},{9,8},{10,11... | collective-permute-start | bytes 294920 | tf_op jit(solution)/shard_map/ppermute | solution.py:336
  12.6 0.0 collective-permute-done.1
  12.6 0.0 collective-permute-done.2
  12.6 0.7 %collective-permute-start.8 = (f32[3,64,128]{2,1,0:T(8,128)S(1)}, f32[3,64,128]{2,1,0:T(8,128)S(1)}, u32[]{:S(2)}, u32[]{:S(2)}) collective-permute-start(f32[3,64,128]{2,1,0:T(8,128)S(1)} %constant_dynamic-update-slice_fusion), channel_id=1, source_target_pairs={{1,2},{2,1},{5,6},{6,5},{9,10},{10,9},{13,14},{14,13},{17,18},{18,... | collective-permute-start | bytes 294920 | tf_op jit(solution)/shard_map/ppermute | solution.py:304
  13.3 3.2 %collective-permute-start.7 = (f32[3,64,128]{2,1,0:T(8,128)S(1)}, f32[3,64,128]{2,1,0:T(8,128)S(1)}, u32[]{:S(2)}, u32[]{:S(2)}) collective-permute-start(f32[3,64,128]{2,1,0:T(8,128)S(1)} %constant_dynamic-update-slice_fusion), channel_id=1, source_target_pairs={{0,2},{1,3},{2,0},{3,1},{4,6},{5,7},{6,4},{7,5},{8,10},{9,11},{10,... | collective-permute-start | bytes 294920 | tf_op jit(solution)/shard_map/ppermute | solution.py:304
  16.5 0.0 collective-permute-done.5
  16.5 0.7 %collective-permute-start.3 = (f32[3,64,128]{2,1,0:T(8,128)S(1)}, f32[3,64,128]{2,1,0:T(8,128)S(1)}, u32[]{:S(2)}, u32[]{:S(2)}) collective-permute-start(f32[3,64,128]{2,1,0:T(8,128)S(1)} %constant_dynamic-update-slice_fusion), channel_id=1, source_target_pairs={{0,1},{1,0},{2,3},{3,2},{4,5},{5,4},{6,7},{7,6},{8,9},{9,8},{10,11... | collective-permute-start | bytes 294920 | tf_op jit(solution)/shard_map/ppermute | solution.py:304
  17.2 0.0 collective-permute-done.6
  17.2 0.0 collective-permute-done.4
  17.3 3.9 %collective-permute-done.3 = f32[3,64,128]{2,1,0:T(8,128)S(1)} collective-permute-done((f32[3,64,128]{2,1,0:T(8,128)S(1)}, f32[3,64,128]{2,1,0:T(8,128)S(1)}, u32[]{:S(2)}, u32[]{:S(2)}) %collective-permute-start.3) | collective-permute-done | bytes 98336 | tf_op jit(solution)/shard_map/ppermute | solution.py:304
  21.2 0.0 collective-permute-done.8
  21.2 0.0 collective-permute-done.7
  21.2 0.1 collective-permute-start.10
  21.3 0.0 copy-start.2
  21.3 0.0 copy-start
  21.4 0.0 copy-start.1
  21.4 0.6 %collective-permute-start.9 = (f32[4,2,64,128]{3,2,1,0:T(8,128)S(1)}, f32[4,2,64,128]{3,2,1,0:T(8,128)S(1)}, u32[]{:S(2)}, u32[]{:S(2)}) collective-permute-start(f32[4,2,64,128]{3,2,1,0:T(8,128)S(1)} %pad_maximum_fusion.2), channel_id=1, source_target_pairs={{0,4},{4,0},{1,5},{5,1},{2,6},{6,2},{3,7},{7,3},{8,12},{12,8},{9,1... | collective-permute-start | bytes 786440 | tf_op jit(solution)/shard_map/ppermute | solution.py:309
  21.9 0.1 copy-done.2
  22.0 1.1 %shard_map.68 = (f32[4,2,128,128]{3,2,1,0:T(8,128)S(1)}, f32[5,4,64,128]{3,2,1,0:T(8,128)S(1)}, f32[5,4,64,128]{3,2,1,0:T(8,128)S(1)}) custom-call(s32[2,2]{1,0:T(2,128)S(1)} %copy-done.2, f32[4,3,64,128]{3,2,1,0:T(8,128)S(1)} %pad_maximum_fusion.near_own, f32[4,3,64,128]{3,2,1,0:T(8,128)S(1)} %pad_maximum_fusion.1.near_rest), custom_call_target="tpu_custom_call" | custom-call | flops 500000000 | bytes 1048576 | tf_op jit(solution)/shard_map/pallas_call | solution.py:351
  23.1 0.2 collective-permute-done.9.far_own
  23.4 0.0 collective-permute-done.10.far_rest
  23.4 0.0 copy-done
  23.4 0.0 copy-done.1
  23.4 10.0 %shard_map.69 = (f32[1,3,64,128]{3,2,1,0:T(8,128)S(1)}, f32[1,3,64,128]{3,2,1,0:T(8,128)S(1)}) custom-call(f32[4,2,128,128]{3,2,1,0:T(8,128)S(1)} %get-tuple-element.17.wave_ref, f32[5,4,64,128]{3,2,1,0:T(8,128)S(1)} %get-tuple-element.18.near_cos, f32[5,4,64,128]{3,2,1,0:T(8,128)S(1)} %get-tuple-element.19.near_sin, ...), custom_call_target="tpu_custom_call" | custom-call | tf_op jit(solution)/shard_map/pallas_call | solution.py:359
  33.4 0.3 collective-permute-start.11
  33.7 1.0 %collective-permute-done.11.received_ref = f32[1,3,64,128]{3,2,1,0:T(8,128)S(1)} collective-permute-done((f32[1,3,64,128]{3,2,1,0:T(8,128)S(1)}, f32[1,3,64,128]{3,2,1,0:T(8,128)S(1)}, u32[]{:S(2)}, u32[]{:S(2)}) %collective-permute-start.11) | collective-permute-done | bytes 98336 | tf_op jit(solution)/shard_map/ppermute | solution.py:309
  34.7 0.7 %shard_map.70 = (f32[1,64,128]{2,1,0:T(8,128)}, f32[2,1,2,64,128]{4,3,2,1,0:T(8,128)}) custom-call(f32[1,3,64,128]{3,2,1,0:T(8,128)S(1)} %get-tuple-element.20.mine_ref, f32[1,3,64,128]{3,2,1,0:T(8,128)S(1)} %collective-permute-done.11.received_ref), custom_call_target="tpu_custom_call" | custom-call | tf_op jit(solution)/shard_map/pallas_call | solution.py:374
  (9 shorter events, 0.1 us)
Async XLA Ops:
  0.6 8.0 %copy-start.3 = (f32[2,64,128]{2,1,0:T(8,128)S(1)}, f32[2,64,128]{2,1,0:T(8,128)}, u32[]{:S(2)}) copy-start(f32[2,64,128]{2,1,0:T(8,128)} %param.7) | copy-start | bytes 196612
  0.6 5.7 %collective-permute-start = (f32[1,64,128]{2,1,0:T(8,128)}, f32[1,64,128]{2,1,0:T(8,128)S(1)}, u32[]{:S(2)}, u32[]{:S(2)}) collective-permute-start(f32[1,64,128]{2,1,0:T(8,128)} %param.5), channel_id=1, source_target_pairs={{0,8},{8,0},{16,24},{24,16},{1,9},{9,1},{17,25},{25,17},{2,10},{10... | collective-permute-start | bytes 98312 | tf_op jit(solution)/shard_map/ppermute | solution.py:304
  3.7 8.9 %collective-permute-start.2 = (f32[1,64,128]{2,1,0:T(8,128)}, f32[1,64,128]{2,1,0:T(8,128)S(1)}, u32[]{:S(2)}, u32[]{:S(2)}) collective-permute-start(f32[1,64,128]{2,1,0:T(8,128)} %param.5), channel_id=1, source_target_pairs={{0,24},{8,16},{16,8},{24,0},{1,25},{9,17},{17,9},{25,1},{2,26},{10... | collective-permute-start | bytes 98312 | tf_op jit(solution)/shard_map/ppermute | solution.py:304
  6.2 6.4 %collective-permute-start.1 = (f32[1,64,128]{2,1,0:T(8,128)}, f32[1,64,128]{2,1,0:T(8,128)S(1)}, u32[]{:S(2)}, u32[]{:S(2)}) collective-permute-start(f32[1,64,128]{2,1,0:T(8,128)} %param.5), channel_id=1, source_target_pairs={{0,16},{8,24},{16,0},{24,8},{1,17},{9,25},{17,1},{25,9},{2,18},{10... | collective-permute-start | bytes 98312 | tf_op jit(solution)/shard_map/ppermute | solution.py:304
  6.3 10.2 %collective-permute-start.5 = (f32[1,64,128]{2,1,0:T(8,128)}, f32[1,64,128]{2,1,0:T(8,128)S(1)}, u32[]{:S(2)}, u32[]{:S(2)}) collective-permute-start(f32[1,64,128]{2,1,0:T(8,128)} %param.5), channel_id=1, source_target_pairs={{0,2},{1,3},{2,0},{3,1},{4,6},{5,7},{6,4},{7,5},{8,10},{9,11},{10,... | collective-permute-start | bytes 98312 | tf_op jit(solution)/shard_map/ppermute | solution.py:339
  8.7 8.6 %collective-permute-start.6 = (f32[3,64,128]{2,1,0:T(8,128)S(1)}, f32[3,64,128]{2,1,0:T(8,128)S(1)}, u32[]{:S(2)}, u32[]{:S(2)}) collective-permute-start(f32[3,64,128]{2,1,0:T(8,128)S(1)} %constant_dynamic-update-slice_fusion.3), channel_id=1, source_target_pairs={{1,2},{2,1},{5,6},{6,5},{9,10},{10,9},{13,14},{14,13},{17,18},{18,... | collective-permute-start | bytes 294920 | tf_op jit(solution)/shard_map/ppermute | solution.py:336
  9.3 7.9 %collective-permute-start.4 = (f32[3,64,128]{2,1,0:T(8,128)S(1)}, f32[3,64,128]{2,1,0:T(8,128)S(1)}, u32[]{:S(2)}, u32[]{:S(2)}) collective-permute-start(f32[3,64,128]{2,1,0:T(8,128)S(1)} %constant_dynamic-update-slice_fusion.3), channel_id=1, source_target_pairs={{0,1},{1,0},{2,3},{3,2},{4,5},{5,4},{6,7},{7,6},{8,9},{9,8},{10,11... | collective-permute-start | bytes 294920 | tf_op jit(solution)/shard_map/ppermute | solution.py:336
  12.6 8.5 %collective-permute-start.8 = (f32[3,64,128]{2,1,0:T(8,128)S(1)}, f32[3,64,128]{2,1,0:T(8,128)S(1)}, u32[]{:S(2)}, u32[]{:S(2)}) collective-permute-start(f32[3,64,128]{2,1,0:T(8,128)S(1)} %constant_dynamic-update-slice_fusion), channel_id=1, source_target_pairs={{1,2},{2,1},{5,6},{6,5},{9,10},{10,9},{13,14},{14,13},{17,18},{18,... | collective-permute-start | bytes 294920 | tf_op jit(solution)/shard_map/ppermute | solution.py:304
  13.3 7.8 %collective-permute-start.7 = (f32[3,64,128]{2,1,0:T(8,128)S(1)}, f32[3,64,128]{2,1,0:T(8,128)S(1)}, u32[]{:S(2)}, u32[]{:S(2)}) collective-permute-start(f32[3,64,128]{2,1,0:T(8,128)S(1)} %constant_dynamic-update-slice_fusion), channel_id=1, source_target_pairs={{0,2},{1,3},{2,0},{3,1},{4,6},{5,7},{6,4},{7,5},{8,10},{9,11},{10,... | collective-permute-start | bytes 294920 | tf_op jit(solution)/shard_map/ppermute | solution.py:304
  16.5 4.6 %collective-permute-start.3 = (f32[3,64,128]{2,1,0:T(8,128)S(1)}, f32[3,64,128]{2,1,0:T(8,128)S(1)}, u32[]{:S(2)}, u32[]{:S(2)}) collective-permute-start(f32[3,64,128]{2,1,0:T(8,128)S(1)} %constant_dynamic-update-slice_fusion), channel_id=1, source_target_pairs={{0,1},{1,0},{2,3},{3,2},{4,5},{5,4},{6,7},{7,6},{8,9},{9,8},{10,11... | collective-permute-start | bytes 294920 | tf_op jit(solution)/shard_map/ppermute | solution.py:304
  21.2 2.2 %collective-permute-start.10 = (f32[4,3,64,128]{3,2,1,0:T(8,128)S(1)}, f32[4,3,64,128]{3,2,1,0:T(8,128)S(1)}, u32[]{:S(2)}, u32[]{:S(2)}) collective-permute-start(f32[4,3,64,128]{3,2,1,0:T(8,128)S(1)} %pad_maximum_fusion.1.near_rest), channel_id=1, source_target_pairs={{0,4},{4,0},{1,5},{5,1},{2,6},{6,2},{3,7},{7,3},{8,12},{12,8},{9,1... | collective-permute-start | bytes 1179656 | tf_op jit(solution)/shard_map/ppermute | solution.py:309
  21.3 0.7 %copy-start.2 = (s32[2,2]{1,0:T(2,128)S(1)}, s32[2,2]{1,0:T(2,128)}, u32[]{:S(2)}) copy-start(s32[2,2]{1,0:T(2,128)} %tilt_ref.1) | copy-start | bytes 52
  21.3 2.0 %copy-start = (bf16[1024,256]{1,0:T(8,128)(2,1)S(1)}, bf16[1024,256]{1,0:T(8,128)(2,1)}, u32[]{:S(2)}) copy-start(bf16[1024,256]{1,0:T(8,128)(2,1)} %constant.20.clone.col_ref) | copy-start | bytes 1572868
  21.4 2.0 %copy-start.1 = (bf16[2,256,512]{2,1,0:T(8,128)(2,1)S(1)}, bf16[2,256,512]{2,1,0:T(8,128)(2,1)}, u32[]{:S(2)}) copy-start(bf16[2,256,512]{2,1,0:T(8,128)(2,1)} %constant.19.clone.row_ref) | copy-start | bytes 1572868
  21.4 2.0 %collective-permute-start.9 = (f32[4,2,64,128]{3,2,1,0:T(8,128)S(1)}, f32[4,2,64,128]{3,2,1,0:T(8,128)S(1)}, u32[]{:S(2)}, u32[]{:S(2)}) collective-permute-start(f32[4,2,64,128]{3,2,1,0:T(8,128)S(1)} %pad_maximum_fusion.2), channel_id=1, source_target_pairs={{0,4},{4,0},{1,5},{5,1},{2,6},{6,2},{3,7},{7,3},{8,12},{12,8},{9,1... | collective-permute-start | bytes 786440 | tf_op jit(solution)/shard_map/ppermute | solution.py:309
  33.4 1.4 %collective-permute-start.11 = (f32[1,3,64,128]{3,2,1,0:T(8,128)S(1)}, f32[1,3,64,128]{3,2,1,0:T(8,128)S(1)}, u32[]{:S(2)}, u32[]{:S(2)}) collective-permute-start(f32[1,3,64,128]{3,2,1,0:T(8,128)S(1)} %get-tuple-element.21), channel_id=1, source_target_pairs={{0,4},{4,0},{1,5},{5,1},{2,6},{6,2},{3,7},{7,3},{8,12},{12,8},{9,1... | collective-permute-start | bytes 294920 | tf_op jit(solution)/shard_map/ppermute | solution.py:309

commit v11 on v9

--- a/solution.py
+++ b/solution.py
@@ -87,8 +87,7 @@
     for position in (lane, edge_pos):
         band = np_band(lane, position).T
         parts.append(np.block([[band.real, band.imag], [-band.imag, band.real]]))
-    high, low = np_halves(np.concatenate(parts, axis=0))
-    return np.concatenate([high, low], axis=0)
+    return np.concatenate(np_halves(np.concatenate(parts, axis=0)), axis=1)
 
 
 def both_rows(near_ref, far_ref, where):
@@ -105,27 +104,23 @@
 
 def row_product(row_matrix, columns):
     high, low = halves(columns)
-    whole = row_matrix.shape[0]
-    return jnp.dot(
-        jnp.concatenate([row_matrix[:, :whole], row_matrix], axis=1),
-        jnp.concatenate([high, low, high], axis=0),
-        preferred_element_type=jnp.float32,
+    whole, width = columns.shape
+    wide = jnp.dot(
+        row_matrix[:, :whole], jnp.concatenate([high, low], axis=1), preferred_element_type=jnp.float32
     )
-
-
-def col_product(high, low, col_high, col_low):
-    return jnp.dot(
-        jnp.concatenate([high, low, high], axis=1),
-        jnp.concatenate([col_high, col_high, col_low], axis=0),
-        preferred_element_type=jnp.float32,
-    )
+    rest = jnp.dot(row_matrix[:, whole:], high, preferred_element_type=jnp.float32)
+    return wide[:, :width] + wide[:, width:] + rest
+
+
+def col_product(high, low, col_ref):
+    wide = jnp.dot(high, col_ref[...], preferred_element_type=jnp.float32)
+    rest = jnp.dot(low, col_ref[:, : 2 * LANES], preferred_element_type=jnp.float32)
+    return wide[:, : 2 * LANES] + wide[:, 2 * LANES :] + rest
 
 
 def advance(slice_index, start, size, screens, row_matrix, col_ref, from_ref, to_ref, a_high, a_low):
     height = from_ref.shape[2]
     half = LANES // 2
-    own, edge = pl.ds(0, 2 * LANES), pl.ds(2 * LANES, 2 * LANES)
-    low_own, low_edge = pl.ds(4 * LANES, 2 * LANES), pl.ds(6 * LANES, 2 * LANES)
     chunks = [range(place, min(place + 2, size)) for place in range(0, size, 2)]
     for chunk in chunks:
         columns = jnp.concatenate(
@@ -145,26 +140,11 @@
                         target[place - 1, :, pl.ds((2 + part) * LANES, half)] = piece[:, :half]
                     if place < size - 1:
                         target[place + 1, :, pl.ds((2 + part) * LANES + half, half)] = piece[:, half:]
-    parts = []
     for chunk in chunks:
         cells = pl.ds(chunk[0], len(chunk))
         rows = len(chunk) * height
-        parts.append(
-            col_product(
-                a_high[cells, :, own].reshape(rows, 2 * LANES),
-                a_low[cells, :, own].reshape(rows, 2 * LANES),
-                col_ref[own],
-                col_ref[low_own],
-            )
-        )
-    for chunk, done in zip(chunks, parts):
-        cells = pl.ds(chunk[0], len(chunk))
-        rows = len(chunk) * height
-        total = done + col_product(
-            a_high[cells, :, edge].reshape(rows, 2 * LANES),
-            a_low[cells, :, edge].reshape(rows, 2 * LANES),
-            col_ref[edge],
-            col_ref[low_edge],
+        total = col_product(
+            a_high[cells].reshape(rows, 4 * LANES), a_low[cells].reshape(rows, 4 * LANES), col_ref
         )
         for sub, place in enumerate(chunk):
             for part in range(2):
@@ -293,7 +273,7 @@
         for part in range(2)
     ]
     high, low = halves(jnp.concatenate(quarters, axis=1))
-    pulled = col_product(high, low, col_ref[: 4 * LANES], col_ref[4 * LANES :])
+    pulled = col_product(high, low, col_ref)
     grad_ref[0] = -(pulled[:, LANES:] * moved_ref[0, 0] + pulled[:, :LANES] * moved_ref[0, 1])
 
     for target, row in ((mine_ref, near), (theirs_ref, far)):

time: 33.7 us -> 33.2 us (0.985)
  Pallas kernels: 9.84 us -> 9.4 us
    pallas_call x1, Pallas kernels: 8.03 us -> 7.58 us  [whole_field_body(): pl.pallas_call(wave_kernel, out_shape=(array(1, 3, tile_r, tile_c),) * 2,...]
where the time goes in v11:
time: 33.2 us; the launch traced here: 33 us
  starting transfers between devices  16.7 us (50%)
  Pallas kernels  9.4 us (28%)
  waiting for transfers between devices  5.18 us (16%)
  local copies, waits for them, and re-layouts  0.93 us (3%)
  between operations  0.77 us (2%)
    ppermute x6, starting transfers between devices, spread(): lax.ppermute(shard, axis, pairs)  10.2 us
    pallas_call x1, Pallas kernels, whole_field_body(): pl.pallas_call(wave_kernel, out_shape=(array(1, 3, tile_r, tile_c),) * 2,...  7.58 us
    ppermute x2, starting transfers between devices, whole_field_body(): near_own.append(lax.ppermute(packet, 'col', close))  3.94 us
    ppermute x6, waiting for transfers between devices, spread(): lax.ppermute(shard, axis, pairs)  3.91 us
    ppermute x1, starting transfers between devices, whole_field_body(): lax.ppermute(slab, 'col', further)  1.52 us
    ppermute x3, waiting for transfers between devices, swap_cores(): return lax.ppermute(value, 'row', [(0, 1), (1, 0)])  1.26 us
    pallas_call x1, Pallas kernels, whole_field_body(): pl.pallas_call(prepare_kernel, out_shape=(array(*field), array(*half_scre...  1.13 us
    ppermute x3, starting transfers between devices, swap_cores(): return lax.ppermute(value, 'row', [(0, 1), (1, 0)])  0.97 us
  transfers between devices with their start and end apart: 12, of which 3 were waited for; matrix products, arithmetic and copies ran while one was open for 3% of the time, Pallas kernels for 3%

profile of v11, /device:TPU:0, one launch (start us, length us, event | category | flops | bytes accessed | tf_op | source)
XLA Modules:
  0.0 33.0 jit_solution(16152945829344009341)
XLA Ops:
  0.6 0.0 copy-start.3
  0.6 3.1 %collective-permute-start = (f32[1,64,128]{2,1,0:T(8,128)}, f32[1,64,128]{2,1,0:T(8,128)S(1)}, u32[]{:S(2)}, u32[]{:S(2)}) collective-permute-start(f32[1,64,128]{2,1,0:T(8,128)} %param.5), channel_id=1, source_target_pairs={{0,8},{8,0},{16,24},{24,16},{1,9},{9,1},{17,25},{25,17},{2,10},{10... | collective-permute-start | bytes 98312 | tf_op jit(solution)/shard_map/ppermute | solution.py:305
  3.7 2.5 %collective-permute-start.2 = (f32[1,64,128]{2,1,0:T(8,128)}, f32[1,64,128]{2,1,0:T(8,128)S(1)}, u32[]{:S(2)}, u32[]{:S(2)}) collective-permute-start(f32[1,64,128]{2,1,0:T(8,128)} %param.5), channel_id=1, source_target_pairs={{0,24},{8,16},{16,8},{24,0},{1,25},{9,17},{17,9},{25,1},{2,26},{10... | collective-permute-start | bytes 98312 | tf_op jit(solution)/shard_map/ppermute | solution.py:305
  6.2 0.1 collective-permute-start.1
  6.3 0.0 collective-permute-done
  6.3 1.5 %collective-permute-start.5 = (f32[1,64,128]{2,1,0:T(8,128)}, f32[1,64,128]{2,1,0:T(8,128)S(1)}, u32[]{:S(2)}, u32[]{:S(2)}) collective-permute-start(f32[1,64,128]{2,1,0:T(8,128)} %param.5), channel_id=1, source_target_pairs={{0,2},{1,3},{2,0},{3,1},{4,6},{5,7},{6,4},{7,5},{8,10},{9,11},{10,... | collective-permute-start | bytes 98312 | tf_op jit(solution)/shard_map/ppermute | solution.py:340
  7.8 0.8 %constant_dynamic-update-slice_fusion.4 = f32[3,64,128]{2,1,0:T(8,128)S(1)} fusion(f32[1,64,128]{2,1,0:T(8,128)} %param.5), kind=kLoop, calls=%fused_computation.8 | loop fusion | bytes 65536
  8.6 0.0 copy-done.3
  8.7 0.7 %collective-permute-start.6 = (f32[3,64,128]{2,1,0:T(8,128)S(1)}, f32[3,64,128]{2,1,0:T(8,128)S(1)}, u32[]{:S(2)}, u32[]{:S(2)}) collective-permute-start(f32[3,64,128]{2,1,0:T(8,128)S(1)} %constant_dynamic-update-slice_fusion.3), channel_id=1, source_target_pairs={{1,2},{2,1},{5,6},{6,5},{9,10},{10,9},{13,14},{14,13},{17,18},{18,... | collective-permute-start | bytes 294920 | tf_op jit(solution)/shard_map/ppermute | solution.py:337
  9.3 3.3 %collective-permute-start.4 = (f32[3,64,128]{2,1,0:T(8,128)S(1)}, f32[3,64,128]{2,1,0:T(8,128)S(1)}, u32[]{:S(2)}, u32[]{:S(2)}) collective-permute-start(f32[3,64,128]{2,1,0:T(8,128)S(1)} %constant_dynamic-update-slice_fusion.3), channel_id=1, source_target_pairs={{0,1},{1,0},{2,3},{3,2},{4,5},{5,4},{6,7},{7,6},{8,9},{9,8},{10,11... | collective-permute-start | bytes 294920 | tf_op jit(solution)/shard_map/ppermute | solution.py:337
  12.6 0.0 collective-permute-done.1
  12.6 0.0 collective-permute-done.2
  12.6 0.7 %collective-permute-start.8 = (f32[3,64,128]{2,1,0:T(8,128)S(1)}, f32[3,64,128]{2,1,0:T(8,128)S(1)}, u32[]{:S(2)}, u32[]{:S(2)}) collective-permute-start(f32[3,64,128]{2,1,0:T(8,128)S(1)} %constant_dynamic-update-slice_fusion), channel_id=1, source_target_pairs={{1,2},{2,1},{5,6},{6,5},{9,10},{10,9},{13,14},{14,13},{17,18},{18,... | collective-permute-start | bytes 294920 | tf_op jit(solution)/shard_map/ppermute | solution.py:305
  13.3 3.2 %collective-permute-start.7 = (f32[3,64,128]{2,1,0:T(8,128)S(1)}, f32[3,64,128]{2,1,0:T(8,128)S(1)}, u32[]{:S(2)}, u32[]{:S(2)}) collective-permute-start(f32[3,64,128]{2,1,0:T(8,128)S(1)} %constant_dynamic-update-slice_fusion), channel_id=1, source_target_pairs={{0,2},{1,3},{2,0},{3,1},{4,6},{5,7},{6,4},{7,5},{8,10},{9,11},{10,... | collective-permute-start | bytes 294920 | tf_op jit(solution)/shard_map/ppermute | solution.py:305
  16.5 0.0 collective-permute-done.5
  16.5 0.7 %collective-permute-start.3 = (f32[3,64,128]{2,1,0:T(8,128)S(1)}, f32[3,64,128]{2,1,0:T(8,128)S(1)}, u32[]{:S(2)}, u32[]{:S(2)}) collective-permute-start(f32[3,64,128]{2,1,0:T(8,128)S(1)} %constant_dynamic-update-slice_fusion), channel_id=1, source_target_pairs={{0,1},{1,0},{2,3},{3,2},{4,5},{5,4},{6,7},{7,6},{8,9},{9,8},{10,11... | collective-permute-start | bytes 294920 | tf_op jit(solution)/shard_map/ppermute | solution.py:305
  17.2 0.0 collective-permute-done.6
  17.2 0.0 collective-permute-done.4
  17.3 3.9 %collective-permute-done.3 = f32[3,64,128]{2,1,0:T(8,128)S(1)} collective-permute-done((f32[3,64,128]{2,1,0:T(8,128)S(1)}, f32[3,64,128]{2,1,0:T(8,128)S(1)}, u32[]{:S(2)}, u32[]{:S(2)}) %collective-permute-start.3) | collective-permute-done | bytes 98336 | tf_op jit(solution)/shard_map/ppermute | solution.py:305
  21.2 0.0 collective-permute-done.8
  21.2 0.0 collective-permute-done.7
  21.2 0.1 collective-permute-start.10
  21.3 0.0 copy-start.2
  21.3 0.0 copy-start
  21.4 0.0 copy-start.1
  21.4 0.6 %collective-permute-start.9 = (f32[4,2,64,128]{3,2,1,0:T(8,128)S(1)}, f32[4,2,64,128]{3,2,1,0:T(8,128)S(1)}, u32[]{:S(2)}, u32[]{:S(2)}) collective-permute-start(f32[4,2,64,128]{3,2,1,0:T(8,128)S(1)} %pad_maximum_fusion.2), channel_id=1, source_target_pairs={{0,4},{4,0},{1,5},{5,1},{2,6},{6,2},{3,7},{7,3},{8,12},{12,8},{9,1... | collective-permute-start | bytes 786440 | tf_op jit(solution)/shard_map/ppermute | solution.py:310
  21.9 0.1 copy-done.2
  22.0 1.1 %shard_map.68 = (f32[4,2,128,128]{3,2,1,0:T(8,128)S(1)}, f32[5,4,64,128]{3,2,1,0:T(8,128)S(1)}, f32[5,4,64,128]{3,2,1,0:T(8,128)S(1)}) custom-call(s32[2,2]{1,0:T(2,128)S(1)} %copy-done.2, f32[4,3,64,128]{3,2,1,0:T(8,128)S(1)} %pad_maximum_fusion.near_own, f32[4,3,64,128]{3,2,1,0:T(8,128)S(1)} %pad_maximum_fusion.1.near_rest), custom_call_target="tpu_custom_call" | custom-call | flops 500000000 | bytes 1048576 | tf_op jit(solution)/shard_map/pallas_call | solution.py:352
  23.1 0.2 collective-permute-done.9.far_own
  23.4 0.0 collective-permute-done.10.far_rest
  23.4 0.0 copy-done
  23.4 0.0 copy-done.1
  23.4 7.6 %shard_map.69 = (f32[1,3,64,128]{3,2,1,0:T(8,128)S(1)}, f32[1,3,64,128]{3,2,1,0:T(8,128)S(1)}) custom-call(f32[4,2,128,128]{3,2,1,0:T(8,128)S(1)} %get-tuple-element.17.wave_ref, f32[5,4,64,128]{3,2,1,0:T(8,128)S(1)} %get-tuple-element.18.near_cos, f32[5,4,64,128]{3,2,1,0:T(8,128)S(1)} %get-tuple-element.19.near_sin, ...), custom_call_target="tpu_custom_call" | custom-call | tf_op jit(solution)/shard_map/pallas_call | solution.py:360
  30.9 0.3 %collective-permute-start.11 = (f32[1,3,64,128]{3,2,1,0:T(8,128)S(1)}, f32[1,3,64,128]{3,2,1,0:T(8,128)S(1)}, u32[]{:S(2)}, u32[]{:S(2)}) collective-permute-start(f32[1,3,64,128]{3,2,1,0:T(8,128)S(1)} %get-tuple-element.21), channel_id=1, source_target_pairs={{0,4},{4,0},{1,5},{5,1},{2,6},{6,2},{3,7},{7,3},{8,12},{12,8},{9,1... | collective-permute-start | bytes 294920 | tf_op jit(solution)/shard_map/ppermute | solution.py:310
  31.3 1.0 %collective-permute-done.11.received_ref = f32[1,3,64,128]{3,2,1,0:T(8,128)S(1)} collective-permute-done((f32[1,3,64,128]{3,2,1,0:T(8,128)S(1)}, f32[1,3,64,128]{3,2,1,0:T(8,128)S(1)}, u32[]{:S(2)}, u32[]{:S(2)}) %collective-permute-start.11) | collective-permute-done | bytes 98336 | tf_op jit(solution)/shard_map/ppermute | solution.py:310
  32.3 0.7 %shard_map.70 = (f32[1,64,128]{2,1,0:T(8,128)}, f32[2,1,2,64,128]{4,3,2,1,0:T(8,128)}) custom-call(f32[1,3,64,128]{3,2,1,0:T(8,128)S(1)} %get-tuple-element.20.mine_ref, f32[1,3,64,128]{3,2,1,0:T(8,128)S(1)} %collective-permute-done.11.received_ref), custom_call_target="tpu_custom_call" | custom-call | tf_op jit(solution)/shard_map/pallas_call | solution.py:375
  (9 shorter events, 0.1 us)
Async XLA Ops:
  0.6 8.0 %copy-start.3 = (f32[2,64,128]{2,1,0:T(8,128)S(1)}, f32[2,64,128]{2,1,0:T(8,128)}, u32[]{:S(2)}) copy-start(f32[2,64,128]{2,1,0:T(8,128)} %param.7) | copy-start | bytes 196612
  0.6 5.7 %collective-permute-start = (f32[1,64,128]{2,1,0:T(8,128)}, f32[1,64,128]{2,1,0:T(8,128)S(1)}, u32[]{:S(2)}, u32[]{:S(2)}) collective-permute-start(f32[1,64,128]{2,1,0:T(8,128)} %param.5), channel_id=1, source_target_pairs={{0,8},{8,0},{16,24},{24,16},{1,9},{9,1},{17,25},{25,17},{2,10},{10... | collective-permute-start | bytes 98312 | tf_op jit(solution)/shard_map/ppermute | solution.py:305
  3.7 8.9 %collective-permute-start.2 = (f32[1,64,128]{2,1,0:T(8,128)}, f32[1,64,128]{2,1,0:T(8,128)S(1)}, u32[]{:S(2)}, u32[]{:S(2)}) collective-permute-start(f32[1,64,128]{2,1,0:T(8,128)} %param.5), channel_id=1, source_target_pairs={{0,24},{8,16},{16,8},{24,0},{1,25},{9,17},{17,9},{25,1},{2,26},{10... | collective-permute-start | bytes 98312 | tf_op jit(solution)/shard_map/ppermute | solution.py:305
  6.2 6.4 %collective-permute-start.1 = (f32[1,64,128]{2,1,0:T(8,128)}, f32[1,64,128]{2,1,0:T(8,128)S(1)}, u32[]{:S(2)}, u32[]{:S(2)}) collective-permute-start(f32[1,64,128]{2,1,0:T(8,128)} %param.5), channel_id=1, source_target_pairs={{0,16},{8,24},{16,0},{24,8},{1,17},{9,25},{17,1},{25,9},{2,18},{10... | collective-permute-start | bytes 98312 | tf_op jit(solution)/shard_map/ppermute | solution.py:305
  6.3 10.2 %collective-permute-start.5 = (f32[1,64,128]{2,1,0:T(8,128)}, f32[1,64,128]{2,1,0:T(8,128)S(1)}, u32[]{:S(2)}, u32[]{:S(2)}) collective-permute-start(f32[1,64,128]{2,1,0:T(8,128)} %param.5), channel_id=1, source_target_pairs={{0,2},{1,3},{2,0},{3,1},{4,6},{5,7},{6,4},{7,5},{8,10},{9,11},{10,... | collective-permute-start | bytes 98312 | tf_op jit(solution)/shard_map/ppermute | solution.py:340
  8.7 8.6 %collective-permute-start.6 = (f32[3,64,128]{2,1,0:T(8,128)S(1)}, f32[3,64,128]{2,1,0:T(8,128)S(1)}, u32[]{:S(2)}, u32[]{:S(2)}) collective-permute-start(f32[3,64,128]{2,1,0:T(8,128)S(1)} %constant_dynamic-update-slice_fusion.3), channel_id=1, source_target_pairs={{1,2},{2,1},{5,6},{6,5},{9,10},{10,9},{13,14},{14,13},{17,18},{18,... | collective-permute-start | bytes 294920 | tf_op jit(solution)/shard_map/ppermute | solution.py:337
  9.3 7.9 %collective-permute-start.4 = (f32[3,64,128]{2,1,0:T(8,128)S(1)}, f32[3,64,128]{2,1,0:T(8,128)S(1)}, u32[]{:S(2)}, u32[]{:S(2)}) collective-permute-start(f32[3,64,128]{2,1,0:T(8,128)S(1)} %constant_dynamic-update-slice_fusion.3), channel_id=1, source_target_pairs={{0,1},{1,0},{2,3},{3,2},{4,5},{5,4},{6,7},{7,6},{8,9},{9,8},{10,11... | collective-permute-start | bytes 294920 | tf_op jit(solution)/shard_map/ppermute | solution.py:337
  12.6 8.5 %collective-permute-start.8 = (f32[3,64,128]{2,1,0:T(8,128)S(1)}, f32[3,64,128]{2,1,0:T(8,128)S(1)}, u32[]{:S(2)}, u32[]{:S(2)}) collective-permute-start(f32[3,64,128]{2,1,0:T(8,128)S(1)} %constant_dynamic-update-slice_fusion), channel_id=1, source_target_pairs={{1,2},{2,1},{5,6},{6,5},{9,10},{10,9},{13,14},{14,13},{17,18},{18,... | collective-permute-start | bytes 294920 | tf_op jit(solution)/shard_map/ppermute | solution.py:305
  13.3 7.8 %collective-permute-start.7 = (f32[3,64,128]{2,1,0:T(8,128)S(1)}, f32[3,64,128]{2,1,0:T(8,128)S(1)}, u32[]{:S(2)}, u32[]{:S(2)}) collective-permute-start(f32[3,64,128]{2,1,0:T(8,128)S(1)} %constant_dynamic-update-slice_fusion), channel_id=1, source_target_pairs={{0,2},{1,3},{2,0},{3,1},{4,6},{5,7},{6,4},{7,5},{8,10},{9,11},{10,... | collective-permute-start | bytes 294920 | tf_op jit(solution)/shard_map/ppermute | solution.py:305
  16.5 4.6 %collective-permute-start.3 = (f32[3,64,128]{2,1,0:T(8,128)S(1)}, f32[3,64,128]{2,1,0:T(8,128)S(1)}, u32[]{:S(2)}, u32[]{:S(2)}) collective-permute-start(f32[3,64,128]{2,1,0:T(8,128)S(1)} %constant_dynamic-update-slice_fusion), channel_id=1, source_target_pairs={{0,1},{1,0},{2,3},{3,2},{4,5},{5,4},{6,7},{7,6},{8,9},{9,8},{10,11... | collective-permute-start | bytes 294920 | tf_op jit(solution)/shard_map/ppermute | solution.py:305
  21.2 2.2 %collective-permute-start.10 = (f32[4,3,64,128]{3,2,1,0:T(8,128)S(1)}, f32[4,3,64,128]{3,2,1,0:T(8,128)S(1)}, u32[]{:S(2)}, u32[]{:S(2)}) collective-permute-start(f32[4,3,64,128]{3,2,1,0:T(8,128)S(1)} %pad_maximum_fusion.1.near_rest), channel_id=1, source_target_pairs={{0,4},{4,0},{1,5},{5,1},{2,6},{6,2},{3,7},{7,3},{8,12},{12,8},{9,1... | collective-permute-start | bytes 1179656 | tf_op jit(solution)/shard_map/ppermute | solution.py:310
  21.3 0.7 %copy-start.2 = (s32[2,2]{1,0:T(2,128)S(1)}, s32[2,2]{1,0:T(2,128)}, u32[]{:S(2)}) copy-start(s32[2,2]{1,0:T(2,128)} %tilt_ref.1) | copy-start | bytes 52
  21.3 2.0 %copy-start = (bf16[512,512]{1,0:T(8,128)(2,1)S(1)}, bf16[512,512]{1,0:T(8,128)(2,1)}, u32[]{:S(2)}) copy-start(bf16[512,512]{1,0:T(8,128)(2,1)} %constant.20.clone.col_ref) | copy-start | bytes 1572868
  21.4 2.0 %copy-start.1 = (bf16[2,256,512]{2,1,0:T(8,128)(2,1)S(1)}, bf16[2,256,512]{2,1,0:T(8,128)(2,1)}, u32[]{:S(2)}) copy-start(bf16[2,256,512]{2,1,0:T(8,128)(2,1)} %constant.19.clone.row_ref) | copy-start | bytes 1572868
  21.4 2.0 %collective-permute-start.9 = (f32[4,2,64,128]{3,2,1,0:T(8,128)S(1)}, f32[4,2,64,128]{3,2,1,0:T(8,128)S(1)}, u32[]{:S(2)}, u32[]{:S(2)}) collective-permute-start(f32[4,2,64,128]{3,2,1,0:T(8,128)S(1)} %pad_maximum_fusion.2), channel_id=1, source_target_pairs={{0,4},{4,0},{1,5},{5,1},{2,6},{6,2},{3,7},{7,3},{8,12},{12,8},{9,1... | collective-permute-start | bytes 786440 | tf_op jit(solution)/shard_map/ppermute | solution.py:310
  30.9 1.4 %collective-permute-start.11 = (f32[1,3,64,128]{3,2,1,0:T(8,128)S(1)}, f32[1,3,64,128]{3,2,1,0:T(8,128)S(1)}, u32[]{:S(2)}, u32[]{:S(2)}) collective-permute-start(f32[1,3,64,128]{3,2,1,0:T(8,128)S(1)} %get-tuple-element.21), channel_id=1, source_target_pairs={{0,4},{4,0},{1,5},{5,1},{2,6},{6,2},{3,7},{7,3},{8,12},{12,8},{9,1... | collective-permute-start | bytes 294920 | tf_op jit(solution)/shard_map/ppermute | solution.py:310

commit v12 on v11

--- a/solution.py
+++ b/solution.py
@@ -82,7 +82,8 @@
 
 def col_constant():
     lane = np.arange(LANES)
-    edge_pos = np.where(lane < LANES // 2, lane + LANES, lane - LANES)
+    turned = np.where((lane >= HALO) & (lane < LANES - HALO), lane ^ (LANES // 2), lane)
+    edge_pos = np.where(turned < LANES // 2, turned + LANES, turned - LANES)
     parts = []
     for position in (lane, edge_pos):
         band = np_band(lane, position).T
@@ -114,13 +115,18 @@
 
 def col_product(high, low, col_ref):
     wide = jnp.dot(high, col_ref[...], preferred_element_type=jnp.float32)
-    rest = jnp.dot(low, col_ref[:, : 2 * LANES], preferred_element_type=jnp.float32)
+    rest = jnp.dot(low, col_ref[: 2 * LANES, : 2 * LANES], preferred_element_type=jnp.float32)
     return wide[:, : 2 * LANES] + wide[:, 2 * LANES :] + rest
+
+
+def three_parts(value):
+    high = value.astype(jnp.bfloat16)
+    rest = value - high.astype(jnp.float32)
+    return high, rest.astype(jnp.bfloat16), pltpu.roll(rest, LANES // 2, 1).astype(jnp.bfloat16)
 
 
 def advance(slice_index, start, size, screens, row_matrix, col_ref, from_ref, to_ref, a_high, a_low):
     height = from_ref.shape[2]
-    half = LANES // 2
     chunks = [range(place, min(place + 2, size)) for place in range(0, size, 2)]
     for chunk in chunks:
         columns = jnp.concatenate(
@@ -134,17 +140,22 @@
         for sub, place in enumerate(chunk):
             for part in range(2):
                 value = done[part * height : (part + 1) * height, sub * LANES : (sub + 1) * LANES]
-                for target, piece in zip((a_high, a_low), halves(value)):
-                    target[place, :, pl.ds(part * LANES, LANES)] = piece
-                    if place > 0:
-                        target[place - 1, :, pl.ds((2 + part) * LANES, half)] = piece[:, :half]
-                    if place < size - 1:
-                        target[place + 1, :, pl.ds((2 + part) * LANES + half, half)] = piece[:, half:]
+                high, low, turned = three_parts(value)
+                cells = pl.ds(part * LANES, LANES)
+                a_high[place, :, cells] = high
+                a_low[place, :, cells] = low
+                edge = (2 + part) * LANES
+                if place > 0:
+                    a_high[place - 1, :, pl.ds(edge, HALO)] = high[:, :HALO]
+                    a_high[place - 1, :, pl.ds(edge + 2 * HALO, HALO)] = turned[:, 2 * HALO : 3 * HALO]
+                if place < size - 1:
+                    a_high[place + 1, :, pl.ds(edge + 3 * HALO, HALO)] = high[:, 3 * HALO :]
+                    a_high[place + 1, :, pl.ds(edge + HALO, HALO)] = turned[:, HALO : 2 * HALO]
     for chunk in chunks:
         cells = pl.ds(chunk[0], len(chunk))
         rows = len(chunk) * height
         total = col_product(
-            a_high[cells].reshape(rows, 4 * LANES), a_low[cells].reshape(rows, 4 * LANES), col_ref
+            a_high[cells].reshape(rows, 4 * LANES), a_low[cells].reshape(rows, 2 * LANES), col_ref
         )
         for sub, place in enumerate(chunk):
             for part in range(2):
@@ -152,10 +163,9 @@
 
 
 def clear_edge(a_ref, place, right):
-    half = LANES // 2
     for part in range(2):
-        begin = (2 + part) * LANES + (0 if right else half)
-        a_ref[place, :, pl.ds(begin, half)] = jnp.zeros((a_ref.shape[1], half), a_ref.dtype)
+        for begin in (0, 2 * HALO) if right else (HALO, 3 * HALO):
+            a_ref[place, :, pl.ds((2 + part) * LANES + begin, HALO)] = jnp.zeros((a_ref.shape[1], HALO), a_ref.dtype)
 
 
 def prepare_kernel(tilt_ref, near_own, near_rest, wave_ref, cos_ref, sin_ref):
@@ -216,10 +226,9 @@
             angle = jnp.where(bits == 0, far_own[held, 0], far_rest[held, jnp.maximum(bits - 1, 0)])
             far_cos[slice_index, col], far_sin[slice_index, col] = cos_sin(angle)
 
-    for pair in sums:
-        for target in pair:
-            clear_edge(target, 0, False)
-            clear_edge(target, blocks - 1, True)
+    for target, _ in sums:
+        clear_edge(target, 0, False)
+        clear_edge(target, blocks - 1, True)
     far_cos[count] = jnp.ones(far_cos.shape[1:], jnp.float32)
     far_sin[count] = jnp.zeros(far_cos.shape[1:], jnp.float32)
     far_screens(0)
@@ -234,9 +243,8 @@
 
     last = waves[count % 2]
     source = waves[(count + 1) % 2]
-    for pair in sums:
-        for target in pair:
-            clear_edge(target, window - 1, True)
+    for target, _ in sums:
+        clear_edge(target, window - 1, True)
     for place in range(window):
         block = window_start + place
         held = block ^ own_place
@@ -267,13 +275,18 @@
         lane < LANES // 2, jnp.where(has_right, cells(right), 0.0), jnp.where(has_left, cells(left), 0.0)
     )
     done = row_product(row_matrix, jnp.concatenate([cells(own_place), edge_cells], axis=1))
-    quarters = [
-        done[part * height : (part + 1) * height, sub * LANES : (sub + 1) * LANES]
-        for sub in range(2)
-        for part in range(2)
-    ]
-    high, low = halves(jnp.concatenate(quarters, axis=1))
-    pulled = col_product(high, low, col_ref)
+    lane = lax.broadcasted_iota(jnp.int32, (height, LANES), 1)
+    between = (lane >= HALO) & (lane < LANES - HALO)
+    highs, lows, edges = [], [], []
+    for part in range(2):
+        high, low, _ = three_parts(done[part * height : (part + 1) * height, :LANES])
+        highs.append(high)
+        lows.append(low)
+        value = done[part * height : (part + 1) * height, LANES:]
+        whole_high = value.astype(jnp.bfloat16).astype(jnp.float32)
+        edge = jnp.where(between, pltpu.roll(value - whole_high, LANES // 2, 1), whole_high)
+        edges.append(edge.astype(jnp.bfloat16))
+    pulled = col_product(jnp.concatenate(highs + edges, axis=1), jnp.concatenate(lows, axis=1), col_ref)
     grad_ref[0] = -(pulled[:, LANES:] * moved_ref[0, 0] + pulled[:, :LANES] * moved_ref[0, 1])
 
     for target, row in ((mine_ref, near), (theirs_ref, far)):
@@ -366,7 +379,7 @@
         + [pltpu.VMEM(field, jnp.float32)] * 2
         + [pltpu.VMEM((count, 2, height, tile_c), jnp.float32)] * 2
         + [pltpu.VMEM((count, height, tile_c), jnp.float32)]
-        + [pltpu.VMEM((blocks, height, 4 * LANES), jnp.bfloat16)] * 4,
+        + [pltpu.VMEM((blocks, height, parts * LANES), jnp.bfloat16) for parts in (4, 2, 4, 2)],
         compiler_params=params(24),
     )(
         wave, near_cos, near_sin, near_own, far_own, far_rest,

time: 33.2 us -> 33.2 us (level)
  no operation moved by 1% of the time
where the time goes in v12:
time: 33.2 us; the launch traced here: 33 us
  starting transfers between devices  16.7 us (50%)
  Pallas kernels  9.35 us (28%)
  waiting for transfers between devices  5.17 us (16%)
  local copies, waits for them, and re-layouts  0.93 us (3%)
  between operations  0.77 us (2%)
    ppermute x6, starting transfers between devices, spread(): lax.ppermute(shard, axis, pairs)  10.2 us
    pallas_call x1, Pallas kernels, whole_field_body(): pl.pallas_call(wave_kernel, out_shape=(array(1, 3, tile_r, tile_c),) * 2,...  7.54 us
    ppermute x2, starting transfers between devices, whole_field_body(): near_own.append(lax.ppermute(packet, 'col', close))  3.94 us
    ppermute x6, waiting for transfers between devices, spread(): lax.ppermute(shard, axis, pairs)  3.91 us
    ppermute x1, starting transfers between devices, whole_field_body(): lax.ppermute(slab, 'col', further)  1.52 us
    ppermute x3, waiting for transfers between devices, swap_cores(): return lax.ppermute(value, 'row', [(0, 1), (1, 0)])  1.25 us
    pallas_call x1, Pallas kernels, whole_field_body(): pl.pallas_call(prepare_kernel, out_shape=(array(*field), array(*half_scre...  1.13 us
    ppermute x3, starting transfers between devices, swap_cores(): return lax.ppermute(value, 'row', [(0, 1), (1, 0)])  0.98 us
  transfers between devices with their start and end apart: 12, of which 3 were waited for; matrix products, arithmetic and copies ran while one was open for 3% of the time, Pallas kernels for 3%

profile of v12, /device:TPU:0, one launch (start us, length us, event | category | flops | bytes accessed | tf_op | source)
XLA Modules:
  0.0 33.0 jit_solution(3675249588585712277)
XLA Ops:
  0.6 0.0 copy-start.3
  0.6 3.1 %collective-permute-start = (f32[1,64,128]{2,1,0:T(8,128)}, f32[1,64,128]{2,1,0:T(8,128)S(1)}, u32[]{:S(2)}, u32[]{:S(2)}) collective-permute-start(f32[1,64,128]{2,1,0:T(8,128)} %param.5), channel_id=1, source_target_pairs={{0,8},{8,0},{16,24},{24,16},{1,9},{9,1},{17,25},{25,17},{2,10},{10... | collective-permute-start | bytes 98312 | tf_op jit(solution)/shard_map/ppermute | solution.py:318
  3.7 2.5 %collective-permute-start.2 = (f32[1,64,128]{2,1,0:T(8,128)}, f32[1,64,128]{2,1,0:T(8,128)S(1)}, u32[]{:S(2)}, u32[]{:S(2)}) collective-permute-start(f32[1,64,128]{2,1,0:T(8,128)} %param.5), channel_id=1, source_target_pairs={{0,24},{8,16},{16,8},{24,0},{1,25},{9,17},{17,9},{25,1},{2,26},{10... | collective-permute-start | bytes 98312 | tf_op jit(solution)/shard_map/ppermute | solution.py:318
  6.2 0.1 collective-permute-start.1
  6.3 0.0 collective-permute-done
  6.3 1.5 %collective-permute-start.5 = (f32[1,64,128]{2,1,0:T(8,128)}, f32[1,64,128]{2,1,0:T(8,128)S(1)}, u32[]{:S(2)}, u32[]{:S(2)}) collective-permute-start(f32[1,64,128]{2,1,0:T(8,128)} %param.5), channel_id=1, source_target_pairs={{0,2},{1,3},{2,0},{3,1},{4,6},{5,7},{6,4},{7,5},{8,10},{9,11},{10,... | collective-permute-start | bytes 98312 | tf_op jit(solution)/shard_map/ppermute | solution.py:353
  7.8 0.8 %constant_dynamic-update-slice_fusion.4 = f32[3,64,128]{2,1,0:T(8,128)S(1)} fusion(f32[1,64,128]{2,1,0:T(8,128)} %param.5), kind=kLoop, calls=%fused_computation.8 | loop fusion | bytes 65536
  8.6 0.0 copy-done.3
  8.7 0.7 %collective-permute-start.6 = (f32[3,64,128]{2,1,0:T(8,128)S(1)}, f32[3,64,128]{2,1,0:T(8,128)S(1)}, u32[]{:S(2)}, u32[]{:S(2)}) collective-permute-start(f32[3,64,128]{2,1,0:T(8,128)S(1)} %constant_dynamic-update-slice_fusion.3), channel_id=1, source_target_pairs={{1,2},{2,1},{5,6},{6,5},{9,10},{10,9},{13,14},{14,13},{17,18},{18,... | collective-permute-start | bytes 294920 | tf_op jit(solution)/shard_map/ppermute | solution.py:350
  9.3 3.3 %collective-permute-start.4 = (f32[3,64,128]{2,1,0:T(8,128)S(1)}, f32[3,64,128]{2,1,0:T(8,128)S(1)}, u32[]{:S(2)}, u32[]{:S(2)}) collective-permute-start(f32[3,64,128]{2,1,0:T(8,128)S(1)} %constant_dynamic-update-slice_fusion.3), channel_id=1, source_target_pairs={{0,1},{1,0},{2,3},{3,2},{4,5},{5,4},{6,7},{7,6},{8,9},{9,8},{10,11... | collective-permute-start | bytes 294920 | tf_op jit(solution)/shard_map/ppermute | solution.py:350
  12.6 0.0 collective-permute-done.1
  12.6 0.0 collective-permute-done.2
  12.6 0.7 %collective-permute-start.8 = (f32[3,64,128]{2,1,0:T(8,128)S(1)}, f32[3,64,128]{2,1,0:T(8,128)S(1)}, u32[]{:S(2)}, u32[]{:S(2)}) collective-permute-start(f32[3,64,128]{2,1,0:T(8,128)S(1)} %constant_dynamic-update-slice_fusion), channel_id=1, source_target_pairs={{1,2},{2,1},{5,6},{6,5},{9,10},{10,9},{13,14},{14,13},{17,18},{18,... | collective-permute-start | bytes 294920 | tf_op jit(solution)/shard_map/ppermute | solution.py:318
  13.3 3.2 %collective-permute-start.7 = (f32[3,64,128]{2,1,0:T(8,128)S(1)}, f32[3,64,128]{2,1,0:T(8,128)S(1)}, u32[]{:S(2)}, u32[]{:S(2)}) collective-permute-start(f32[3,64,128]{2,1,0:T(8,128)S(1)} %constant_dynamic-update-slice_fusion), channel_id=1, source_target_pairs={{0,2},{1,3},{2,0},{3,1},{4,6},{5,7},{6,4},{7,5},{8,10},{9,11},{10,... | collective-permute-start | bytes 294920 | tf_op jit(solution)/shard_map/ppermute | solution.py:318
  16.5 0.0 collective-permute-done.5
  16.5 0.7 %collective-permute-start.3 = (f32[3,64,128]{2,1,0:T(8,128)S(1)}, f32[3,64,128]{2,1,0:T(8,128)S(1)}, u32[]{:S(2)}, u32[]{:S(2)}) collective-permute-start(f32[3,64,128]{2,1,0:T(8,128)S(1)} %constant_dynamic-update-slice_fusion), channel_id=1, source_target_pairs={{0,1},{1,0},{2,3},{3,2},{4,5},{5,4},{6,7},{7,6},{8,9},{9,8},{10,11... | collective-permute-start | bytes 294920 | tf_op jit(solution)/shard_map/ppermute | solution.py:318
  17.2 0.0 collective-permute-done.6
  17.2 0.0 collective-permute-done.4
  17.3 3.9 %collective-permute-done.3 = f32[3,64,128]{2,1,0:T(8,128)S(1)} collective-permute-done((f32[3,64,128]{2,1,0:T(8,128)S(1)}, f32[3,64,128]{2,1,0:T(8,128)S(1)}, u32[]{:S(2)}, u32[]{:S(2)}) %collective-permute-start.3) | collective-permute-done | bytes 98336 | tf_op jit(solution)/shard_map/ppermute | solution.py:318
  21.2 0.0 collective-permute-done.8
  21.2 0.0 collective-permute-done.7
  21.2 0.1 collective-permute-start.10
  21.3 0.0 copy-start.2
  21.3 0.0 copy-start
  21.4 0.0 copy-start.1
  21.4 0.6 %collective-permute-start.9 = (f32[4,2,64,128]{3,2,1,0:T(8,128)S(1)}, f32[4,2,64,128]{3,2,1,0:T(8,128)S(1)}, u32[]{:S(2)}, u32[]{:S(2)}) collective-permute-start(f32[4,2,64,128]{3,2,1,0:T(8,128)S(1)} %pad_maximum_fusion.2), channel_id=1, source_target_pairs={{0,4},{4,0},{1,5},{5,1},{2,6},{6,2},{3,7},{7,3},{8,12},{12,8},{9,1... | collective-permute-start | bytes 786440 | tf_op jit(solution)/shard_map/ppermute | solution.py:323
  21.9 0.1 copy-done.2
  22.0 1.1 %shard_map.68 = (f32[4,2,128,128]{3,2,1,0:T(8,128)S(1)}, f32[5,4,64,128]{3,2,1,0:T(8,128)S(1)}, f32[5,4,64,128]{3,2,1,0:T(8,128)S(1)}) custom-call(s32[2,2]{1,0:T(2,128)S(1)} %copy-done.2, f32[4,3,64,128]{3,2,1,0:T(8,128)S(1)} %pad_maximum_fusion.near_own, f32[4,3,64,128]{3,2,1,0:T(8,128)S(1)} %pad_maximum_fusion.1.near_rest), custom_call_target="tpu_custom_call" | custom-call | flops 500000000 | bytes 1048576 | tf_op jit(solution)/shard_map/pallas_call | solution.py:365
  23.1 0.2 collective-permute-done.9.far_own
  23.4 0.0 collective-permute-done.10.far_rest
  23.4 0.0 copy-done
  23.4 0.0 copy-done.1
  23.4 7.5 %shard_map.69 = (f32[1,3,64,128]{3,2,1,0:T(8,128)S(1)}, f32[1,3,64,128]{3,2,1,0:T(8,128)S(1)}) custom-call(f32[4,2,128,128]{3,2,1,0:T(8,128)S(1)} %get-tuple-element.17.wave_ref, f32[5,4,64,128]{3,2,1,0:T(8,128)S(1)} %get-tuple-element.18.near_cos, f32[5,4,64,128]{3,2,1,0:T(8,128)S(1)} %get-tuple-element.19.near_sin, ...), custom_call_target="tpu_custom_call" | custom-call | tf_op jit(solution)/shard_map/pallas_call | solution.py:373
  30.9 0.4 %collective-permute-start.11 = (f32[1,3,64,128]{3,2,1,0:T(8,128)S(1)}, f32[1,3,64,128]{3,2,1,0:T(8,128)S(1)}, u32[]{:S(2)}, u32[]{:S(2)}) collective-permute-start(f32[1,3,64,128]{3,2,1,0:T(8,128)S(1)} %get-tuple-element.21), channel_id=1, source_target_pairs={{0,4},{4,0},{1,5},{5,1},{2,6},{6,2},{3,7},{7,3},{8,12},{12,8},{9,1... | collective-permute-start | bytes 294920 | tf_op jit(solution)/shard_map/ppermute | solution.py:323
  31.3 1.0 %collective-permute-done.11.received_ref = f32[1,3,64,128]{3,2,1,0:T(8,128)S(1)} collective-permute-done((f32[1,3,64,128]{3,2,1,0:T(8,128)S(1)}, f32[1,3,64,128]{3,2,1,0:T(8,128)S(1)}, u32[]{:S(2)}, u32[]{:S(2)}) %collective-permute-start.11) | collective-permute-done | bytes 98336 | tf_op jit(solution)/shard_map/ppermute | solution.py:323
  32.3 0.7 %shard_map.70 = (f32[1,64,128]{2,1,0:T(8,128)}, f32[2,1,2,64,128]{4,3,2,1,0:T(8,128)}) custom-call(f32[1,3,64,128]{3,2,1,0:T(8,128)S(1)} %get-tuple-element.20.mine_ref, f32[1,3,64,128]{3,2,1,0:T(8,128)S(1)} %collective-permute-done.11.received_ref), custom_call_target="tpu_custom_call" | custom-call | tf_op jit(solution)/shard_map/pallas_call | solution.py:388
  (9 shorter events, 0.1 us)
Async XLA Ops:
  0.6 8.0 %copy-start.3 = (f32[2,64,128]{2,1,0:T(8,128)S(1)}, f32[2,64,128]{2,1,0:T(8,128)}, u32[]{:S(2)}) copy-start(f32[2,64,128]{2,1,0:T(8,128)} %param.7) | copy-start | bytes 196612
  0.6 5.7 %collective-permute-start = (f32[1,64,128]{2,1,0:T(8,128)}, f32[1,64,128]{2,1,0:T(8,128)S(1)}, u32[]{:S(2)}, u32[]{:S(2)}) collective-permute-start(f32[1,64,128]{2,1,0:T(8,128)} %param.5), channel_id=1, source_target_pairs={{0,8},{8,0},{16,24},{24,16},{1,9},{9,1},{17,25},{25,17},{2,10},{10... | collective-permute-start | bytes 98312 | tf_op jit(solution)/shard_map/ppermute | solution.py:318
  3.7 8.9 %collective-permute-start.2 = (f32[1,64,128]{2,1,0:T(8,128)}, f32[1,64,128]{2,1,0:T(8,128)S(1)}, u32[]{:S(2)}, u32[]{:S(2)}) collective-permute-start(f32[1,64,128]{2,1,0:T(8,128)} %param.5), channel_id=1, source_target_pairs={{0,24},{8,16},{16,8},{24,0},{1,25},{9,17},{17,9},{25,1},{2,26},{10... | collective-permute-start | bytes 98312 | tf_op jit(solution)/shard_map/ppermute | solution.py:318
  6.2 6.4 %collective-permute-start.1 = (f32[1,64,128]{2,1,0:T(8,128)}, f32[1,64,128]{2,1,0:T(8,128)S(1)}, u32[]{:S(2)}, u32[]{:S(2)}) collective-permute-start(f32[1,64,128]{2,1,0:T(8,128)} %param.5), channel_id=1, source_target_pairs={{0,16},{8,24},{16,0},{24,8},{1,17},{9,25},{17,1},{25,9},{2,18},{10... | collective-permute-start | bytes 98312 | tf_op jit(solution)/shard_map/ppermute | solution.py:318
  6.3 10.2 %collective-permute-start.5 = (f32[1,64,128]{2,1,0:T(8,128)}, f32[1,64,128]{2,1,0:T(8,128)S(1)}, u32[]{:S(2)}, u32[]{:S(2)}) collective-permute-start(f32[1,64,128]{2,1,0:T(8,128)} %param.5), channel_id=1, source_target_pairs={{0,2},{1,3},{2,0},{3,1},{4,6},{5,7},{6,4},{7,5},{8,10},{9,11},{10,... | collective-permute-start | bytes 98312 | tf_op jit(solution)/shard_map/ppermute | solution.py:353
  8.7 8.6 %collective-permute-start.6 = (f32[3,64,128]{2,1,0:T(8,128)S(1)}, f32[3,64,128]{2,1,0:T(8,128)S(1)}, u32[]{:S(2)}, u32[]{:S(2)}) collective-permute-start(f32[3,64,128]{2,1,0:T(8,128)S(1)} %constant_dynamic-update-slice_fusion.3), channel_id=1, source_target_pairs={{1,2},{2,1},{5,6},{6,5},{9,10},{10,9},{13,14},{14,13},{17,18},{18,... | collective-permute-start | bytes 294920 | tf_op jit(solution)/shard_map/ppermute | solution.py:350
  9.3 7.9 %collective-permute-start.4 = (f32[3,64,128]{2,1,0:T(8,128)S(1)}, f32[3,64,128]{2,1,0:T(8,128)S(1)}, u32[]{:S(2)}, u32[]{:S(2)}) collective-permute-start(f32[3,64,128]{2,1,0:T(8,128)S(1)} %constant_dynamic-update-slice_fusion.3), channel_id=1, source_target_pairs={{0,1},{1,0},{2,3},{3,2},{4,5},{5,4},{6,7},{7,6},{8,9},{9,8},{10,11... | collective-permute-start | bytes 294920 | tf_op jit(solution)/shard_map/ppermute | solution.py:350
  12.6 8.5 %collective-permute-start.8 = (f32[3,64,128]{2,1,0:T(8,128)S(1)}, f32[3,64,128]{2,1,0:T(8,128)S(1)}, u32[]{:S(2)}, u32[]{:S(2)}) collective-permute-start(f32[3,64,128]{2,1,0:T(8,128)S(1)} %constant_dynamic-update-slice_fusion), channel_id=1, source_target_pairs={{1,2},{2,1},{5,6},{6,5},{9,10},{10,9},{13,14},{14,13},{17,18},{18,... | collective-permute-start | bytes 294920 | tf_op jit(solution)/shard_map/ppermute | solution.py:318
  13.3 7.8 %collective-permute-start.7 = (f32[3,64,128]{2,1,0:T(8,128)S(1)}, f32[3,64,128]{2,1,0:T(8,128)S(1)}, u32[]{:S(2)}, u32[]{:S(2)}) collective-permute-start(f32[3,64,128]{2,1,0:T(8,128)S(1)} %constant_dynamic-update-slice_fusion), channel_id=1, source_target_pairs={{0,2},{1,3},{2,0},{3,1},{4,6},{5,7},{6,4},{7,5},{8,10},{9,11},{10,... | collective-permute-start | bytes 294920 | tf_op jit(solution)/shard_map/ppermute | solution.py:318
  16.5 4.6 %collective-permute-start.3 = (f32[3,64,128]{2,1,0:T(8,128)S(1)}, f32[3,64,128]{2,1,0:T(8,128)S(1)}, u32[]{:S(2)}, u32[]{:S(2)}) collective-permute-start(f32[3,64,128]{2,1,0:T(8,128)S(1)} %constant_dynamic-update-slice_fusion), channel_id=1, source_target_pairs={{0,1},{1,0},{2,3},{3,2},{4,5},{5,4},{6,7},{7,6},{8,9},{9,8},{10,11... | collective-permute-start | bytes 294920 | tf_op jit(solution)/shard_map/ppermute | solution.py:318
  21.2 2.2 %collective-permute-start.10 = (f32[4,3,64,128]{3,2,1,0:T(8,128)S(1)}, f32[4,3,64,128]{3,2,1,0:T(8,128)S(1)}, u32[]{:S(2)}, u32[]{:S(2)}) collective-permute-start(f32[4,3,64,128]{3,2,1,0:T(8,128)S(1)} %pad_maximum_fusion.1.near_rest), channel_id=1, source_target_pairs={{0,4},{4,0},{1,5},{5,1},{2,6},{6,2},{3,7},{7,3},{8,12},{12,8},{9,1... | collective-permute-start | bytes 1179656 | tf_op jit(solution)/shard_map/ppermute | solution.py:323
  21.3 0.7 %copy-start.2 = (s32[2,2]{1,0:T(2,128)S(1)}, s32[2,2]{1,0:T(2,128)}, u32[]{:S(2)}) copy-start(s32[2,2]{1,0:T(2,128)} %tilt_ref.1) | copy-start | bytes 52
  21.3 2.0 %copy-start = (bf16[512,512]{1,0:T(8,128)(2,1)S(1)}, bf16[512,512]{1,0:T(8,128)(2,1)}, u32[]{:S(2)}) copy-start(bf16[512,512]{1,0:T(8,128)(2,1)} %constant.20.clone.col_ref) | copy-start | bytes 1572868
  21.4 2.0 %copy-start.1 = (bf16[2,256,512]{2,1,0:T(8,128)(2,1)S(1)}, bf16[2,256,512]{2,1,0:T(8,128)(2,1)}, u32[]{:S(2)}) copy-start(bf16[2,256,512]{2,1,0:T(8,128)(2,1)} %constant.19.clone.row_ref) | copy-start | bytes 1572868
  21.4 2.0 %collective-permute-start.9 = (f32[4,2,64,128]{3,2,1,0:T(8,128)S(1)}, f32[4,2,64,128]{3,2,1,0:T(8,128)S(1)}, u32[]{:S(2)}, u32[]{:S(2)}) collective-permute-start(f32[4,2,64,128]{3,2,1,0:T(8,128)S(1)} %pad_maximum_fusion.2), channel_id=1, source_target_pairs={{0,4},{4,0},{1,5},{5,1},{2,6},{6,2},{3,7},{7,3},{8,12},{12,8},{9,1... | collective-permute-start | bytes 786440 | tf_op jit(solution)/shard_map/ppermute | solution.py:323
  30.9 1.4 %collective-permute-start.11 = (f32[1,3,64,128]{3,2,1,0:T(8,128)S(1)}, f32[1,3,64,128]{3,2,1,0:T(8,128)S(1)}, u32[]{:S(2)}, u32[]{:S(2)}) collective-permute-start(f32[1,3,64,128]{3,2,1,0:T(8,128)S(1)} %get-tuple-element.21), channel_id=1, source_target_pairs={{0,4},{4,0},{1,5},{5,1},{2,6},{6,2},{3,7},{7,3},{8,12},{12,8},{9,1... | collective-permute-start | bytes 294920 | tf_op jit(solution)/shard_map/ppermute | solution.py:323

commit v13 on v12

--- a/solution.py
+++ b/solution.py
@@ -95,11 +95,11 @@
     return jnp.concatenate([near_ref[where], far_ref[where]], axis=0)
 
 
-def block_turned(slice_index, block, screens, wave_ref, place):
+def turned(slice_index, block, screens, wave):
     near_cos, near_sin, far_cos, far_sin = screens
     cos = both_rows(near_cos, far_cos, (slice_index, block))
     sin = both_rows(near_sin, far_sin, (slice_index, block))
-    real, imag = wave_ref[place, 0], wave_ref[place, 1]
+    real, imag = wave
     return cos * real - sin * imag, cos * imag + sin * real
 
 
@@ -125,47 +125,57 @@
     return high, rest.astype(jnp.bfloat16), pltpu.roll(rest, LANES // 2, 1).astype(jnp.bfloat16)
 
 
-def advance(slice_index, start, size, screens, row_matrix, col_ref, from_ref, to_ref, a_high, a_low):
-    height = from_ref.shape[2]
+def advance(slice_index, start, waves, screens, row_matrix, col_ref, edge_ref):
+    size, height = len(waves), waves[0][0].shape[0]
     chunks = [range(place, min(place + 2, size)) for place in range(0, size, 2)]
+    highs, lows = [], []
     for chunk in chunks:
-        columns = jnp.concatenate(
-            [
-                jnp.concatenate(block_turned(slice_index, start + place, screens, from_ref, place), axis=0)
-                for place in chunk
-            ],
-            axis=1,
-        )
-        done = row_product(row_matrix, columns)
+        columns = [
+            jnp.concatenate(turned(slice_index, start + place, screens, waves[place]), axis=0) for place in chunk
+        ]
+        done = row_product(row_matrix, jnp.concatenate(columns, axis=1))
         for sub, place in enumerate(chunk):
+            own_high, own_low = [], []
             for part in range(2):
                 value = done[part * height : (part + 1) * height, sub * LANES : (sub + 1) * LANES]
-                high, low, turned = three_parts(value)
-                cells = pl.ds(part * LANES, LANES)
-                a_high[place, :, cells] = high
-                a_low[place, :, cells] = low
-                edge = (2 + part) * LANES
+                high, low, swung = three_parts(value)
+                own_high.append(high)
+                own_low.append(low)
+                edge = part * LANES
                 if place > 0:
-                    a_high[place - 1, :, pl.ds(edge, HALO)] = high[:, :HALO]
-                    a_high[place - 1, :, pl.ds(edge + 2 * HALO, HALO)] = turned[:, 2 * HALO : 3 * HALO]
+                    edge_ref[place - 1, :, pl.ds(edge, HALO)] = high[:, :HALO]
+                    edge_ref[place - 1, :, pl.ds(edge + 2 * HALO, HALO)] = swung[:, 2 * HALO : 3 * HALO]
                 if place < size - 1:
-                    a_high[place + 1, :, pl.ds(edge + 3 * HALO, HALO)] = high[:, 3 * HALO :]
-                    a_high[place + 1, :, pl.ds(edge + HALO, HALO)] = turned[:, HALO : 2 * HALO]
+                    edge_ref[place + 1, :, pl.ds(edge + 3 * HALO, HALO)] = high[:, 3 * HALO :]
+                    edge_ref[place + 1, :, pl.ds(edge + HALO, HALO)] = swung[:, HALO : 2 * HALO]
+            highs.append(jnp.concatenate(own_high, axis=1))
+            lows.append(jnp.concatenate(own_low, axis=1))
+    results = []
     for chunk in chunks:
-        cells = pl.ds(chunk[0], len(chunk))
         rows = len(chunk) * height
+        edges = edge_ref[pl.ds(chunk[0], len(chunk))].reshape(rows, 2 * LANES)
+        own = jnp.concatenate([highs[place] for place in chunk], axis=0)
         total = col_product(
-            a_high[cells].reshape(rows, 4 * LANES), a_low[cells].reshape(rows, 2 * LANES), col_ref
+            jnp.concatenate([own, edges], axis=1),
+            jnp.concatenate([lows[place] for place in chunk], axis=0),
+            col_ref,
         )
-        for sub, place in enumerate(chunk):
-            for part in range(2):
-                to_ref[place, part] = total[sub * height : (sub + 1) * height, part * LANES : (part + 1) * LANES]
-
-
-def clear_edge(a_ref, place, right):
+        for sub in range(len(chunk)):
+            block = total[sub * height : (sub + 1) * height]
+            results.append((block[:, :LANES], block[:, LANES:]))
+    return results
+
+
+def clear_edge(edge_ref, place, right):
     for part in range(2):
         for begin in (0, 2 * HALO) if right else (HALO, 3 * HALO):
-            a_ref[place, :, pl.ds((2 + part) * LANES + begin, HALO)] = jnp.zeros((a_ref.shape[1], HALO), a_ref.dtype)
+            cells = pl.ds(part * LANES + begin, HALO)
+            edge_ref[place, :, cells] = jnp.zeros((edge_ref.shape[1], HALO), edge_ref.dtype)
+
+
+def keep(wave_ref, waves):
+    for place, wave in enumerate(waves):
+        wave_ref[place, 0], wave_ref[place, 1] = wave
 
 
 def prepare_kernel(tilt_ref, near_own, near_rest, wave_ref, cos_ref, sin_ref):
@@ -204,8 +214,7 @@
 
 def wave_kernel(
     wave_ref, near_cos, near_sin, near_own, far_own, far_rest, row_ref, col_ref,
-    mine_ref, theirs_ref, far_cos, far_sin, even_ref, odd_ref, moved_ref, left_ref, grad_ref,
-    even_high, even_low, odd_high, odd_low,
+    mine_ref, theirs_ref, far_cos, far_sin, kept_ref, moved_ref, left_ref, grad_ref, even_edge, odd_edge,
 ):
     blocks, _, height, _ = wave_ref.shape
     count = near_cos.shape[0] - 1
@@ -216,8 +225,7 @@
     window = min(3, blocks)
     window_start = jnp.clip(own_place - 1, 0, blocks - window)
     own_in_window = own_place - window_start
-    waves = (even_ref, odd_ref)
-    sums = ((even_high, even_low), (odd_high, odd_low))
+    edges = (even_edge, odd_edge)
 
     def far_screens(slice_index):
         bits = slice_index ^ own_section
@@ -226,50 +234,48 @@
             angle = jnp.where(bits == 0, far_own[held, 0], far_rest[held, jnp.maximum(bits - 1, 0)])
             far_cos[slice_index, col], far_sin[slice_index, col] = cos_sin(angle)
 
-    for target, _ in sums:
-        clear_edge(target, 0, False)
-        clear_edge(target, blocks - 1, True)
+    for edge_ref in edges:
+        clear_edge(edge_ref, 0, False)
+        clear_edge(edge_ref, blocks - 1, True)
     far_cos[count] = jnp.ones(far_cos.shape[1:], jnp.float32)
     far_sin[count] = jnp.zeros(far_cos.shape[1:], jnp.float32)
     far_screens(0)
 
+    waves = [(wave_ref[place, 0], wave_ref[place, 1]) for place in range(blocks)]
     for tick in range(count):
-        source, target = wave_ref if tick == 0 else waves[tick % 2], waves[(tick + 1) % 2]
-        moved_ref[tick, 0], moved_ref[tick, 1] = block_turned(tick, own_place, screens, source, own_place)
-        advance(tick, 0, blocks, screens, row_matrix, col_ref, source, target, *sums[tick % 2])
+        entering = (wave_ref if tick == 0 else kept_ref)[own_place]
+        moved_ref[tick, 0], moved_ref[tick, 1] = turned(tick, own_place, screens, (entering[0], entering[1]))
+        waves = advance(tick, 0, waves, screens, row_matrix, col_ref, edges[tick % 2])
         if tick + 1 < count:
             far_screens(tick + 1)
-        left_ref[tick] = target[own_place]
-
-    last = waves[count % 2]
-    source = waves[(count + 1) % 2]
-    for target, _ in sums:
-        clear_edge(target, window - 1, True)
+        keep(kept_ref, waves)
+        left_ref[tick] = kept_ref[own_place]
+
+    for edge_ref in edges:
+        clear_edge(edge_ref, window - 1, True)
+    waves = []
     for place in range(window):
         block = window_start + place
         held = block ^ own_place
         measured = jnp.concatenate([near_own[held, 1 + core], far_own[held, 1]], axis=0)
-        real, imag = last[block, 0], last[block, 1]
+        real, imag = kept_ref[block, 0], kept_ref[block, 1]
         misfit = 2.0 * (real * real + imag * imag - measured)
-        source[place, 0] = misfit * real
-        source[place, 1] = -misfit * imag
+        waves.append((misfit * real, -misfit * imag))
 
     for tick in range(count - 1):
-        source, target = waves[(count + 1 + tick) % 2], waves[(count + tick) % 2]
-        advance(
-            count - tick, window_start, window, screens, row_matrix, col_ref, source, target, *sums[tick % 2]
-        )
+        waves = advance(count - tick, window_start, waves, screens, row_matrix, col_ref, edges[tick % 2])
+        keep(kept_ref, waves)
         arrived = count - 1 - tick
-        pulled = target[own_in_window, 0], target[own_in_window, 1]
+        pulled = kept_ref[own_in_window]
         grad_ref[arrived] = -(pulled[1] * moved_ref[arrived, 0] + pulled[0] * moved_ref[arrived, 1])
 
-    source = waves[(2 * count) % 2]
     left, right = jnp.maximum(own_place - 1, 0), jnp.minimum(own_place + 1, blocks - 1)
     lane = lax.broadcasted_iota(jnp.int32, (2 * height, LANES), 1)
     has_left, has_right = own_place > 0, own_place < blocks - 1
 
     def cells(block):
-        return jnp.concatenate(block_turned(1, block, screens, source, block - window_start), axis=0)
+        wave = kept_ref[block - window_start]
+        return jnp.concatenate(turned(1, block, screens, (wave[0], wave[1])), axis=0)
 
     edge_cells = jnp.where(
         lane < LANES // 2, jnp.where(has_right, cells(right), 0.0), jnp.where(has_left, cells(left), 0.0)
@@ -376,10 +382,10 @@
         in_specs=[vmem] * 8,
         out_specs=(vmem,) * 2,
         scratch_shapes=[pltpu.VMEM(half_screens, jnp.float32)] * 2
-        + [pltpu.VMEM(field, jnp.float32)] * 2
+        + [pltpu.VMEM(field, jnp.float32)]
         + [pltpu.VMEM((count, 2, height, tile_c), jnp.float32)] * 2
         + [pltpu.VMEM((count, height, tile_c), jnp.float32)]
-        + [pltpu.VMEM((blocks, height, parts * LANES), jnp.bfloat16) for parts in (4, 2, 4, 2)],
+        + [pltpu.VMEM((blocks, height, 2 * LANES), jnp.bfloat16)] * 2,
         compiler_params=params(24),
     )(
         wave, near_cos, near_sin, near_own, far_own, far_rest,

time: 33.2 us -> 32.9 us (level)
  no operation moved by 1% of the time
where the time goes in v13:
time: 32.9 us; the launch traced here: 32.7 us
  starting transfers between devices  16.7 us (51%)
  Pallas kernels  9.12 us (28%)
  waiting for transfers between devices  5.17 us (16%)
  local copies, waits for them, and re-layouts  0.93 us (3%)
  between operations  0.77 us (2%)
    ppermute x6, starting transfers between devices, spread(): lax.ppermute(shard, axis, pairs)  10.2 us
    pallas_call x1, Pallas kernels, whole_field_body(): pl.pallas_call(wave_kernel, out_shape=(array(1, 3, tile_r, tile_c),) * 2,...  7.3 us
    ppermute x2, starting transfers between devices, whole_field_body(): near_own.append(lax.ppermute(packet, 'col', close))  3.94 us
    ppermute x6, waiting for transfers between devices, spread(): lax.ppermute(shard, axis, pairs)  3.91 us
    ppermute x1, starting transfers between devices, whole_field_body(): lax.ppermute(slab, 'col', further)  1.52 us
    ppermute x3, waiting for transfers between devices, swap_cores(): return lax.ppermute(value, 'row', [(0, 1), (1, 0)])  1.25 us
    pallas_call x1, Pallas kernels, whole_field_body(): pl.pallas_call(prepare_kernel, out_shape=(array(*field), array(*half_scre...  1.13 us
    ppermute x3, starting transfers between devices, swap_cores(): return lax.ppermute(value, 'row', [(0, 1), (1, 0)])  0.98 us
  transfers between devices with their start and end apart: 12, of which 3 were waited for; matrix products, arithmetic and copies ran while one was open for 3% of the time, Pallas kernels for 3%

profile of v13, /device:TPU:0, one launch (start us, length us, event | category | flops | bytes accessed | tf_op | source)
XLA Modules:
  0.0 32.7 jit_solution(8698528560181177060)
XLA Ops:
  0.6 0.0 copy-start.3
  0.6 3.1 %collective-permute-start = (f32[1,64,128]{2,1,0:T(8,128)}, f32[1,64,128]{2,1,0:T(8,128)S(1)}, u32[]{:S(2)}, u32[]{:S(2)}) collective-permute-start(f32[1,64,128]{2,1,0:T(8,128)} %param.5), channel_id=1, source_target_pairs={{0,8},{8,0},{16,24},{24,16},{1,9},{9,1},{17,25},{25,17},{2,10},{10... | collective-permute-start | bytes 98312 | tf_op jit(solution)/shard_map/ppermute | solution.py:324
  3.7 2.5 %collective-permute-start.2 = (f32[1,64,128]{2,1,0:T(8,128)}, f32[1,64,128]{2,1,0:T(8,128)S(1)}, u32[]{:S(2)}, u32[]{:S(2)}) collective-permute-start(f32[1,64,128]{2,1,0:T(8,128)} %param.5), channel_id=1, source_target_pairs={{0,24},{8,16},{16,8},{24,0},{1,25},{9,17},{17,9},{25,1},{2,26},{10... | collective-permute-start | bytes 98312 | tf_op jit(solution)/shard_map/ppermute | solution.py:324
  6.2 0.1 collective-permute-start.1
  6.3 0.0 collective-permute-done
  6.3 1.5 %collective-permute-start.5 = (f32[1,64,128]{2,1,0:T(8,128)}, f32[1,64,128]{2,1,0:T(8,128)S(1)}, u32[]{:S(2)}, u32[]{:S(2)}) collective-permute-start(f32[1,64,128]{2,1,0:T(8,128)} %param.5), channel_id=1, source_target_pairs={{0,2},{1,3},{2,0},{3,1},{4,6},{5,7},{6,4},{7,5},{8,10},{9,11},{10,... | collective-permute-start | bytes 98312 | tf_op jit(solution)/shard_map/ppermute | solution.py:359
  7.8 0.8 %constant_dynamic-update-slice_fusion.4 = f32[3,64,128]{2,1,0:T(8,128)S(1)} fusion(f32[1,64,128]{2,1,0:T(8,128)} %param.5), kind=kLoop, calls=%fused_computation.8 | loop fusion | bytes 65536
  8.6 0.0 copy-done.3
  8.7 0.7 %collective-permute-start.6 = (f32[3,64,128]{2,1,0:T(8,128)S(1)}, f32[3,64,128]{2,1,0:T(8,128)S(1)}, u32[]{:S(2)}, u32[]{:S(2)}) collective-permute-start(f32[3,64,128]{2,1,0:T(8,128)S(1)} %constant_dynamic-update-slice_fusion.3), channel_id=1, source_target_pairs={{1,2},{2,1},{5,6},{6,5},{9,10},{10,9},{13,14},{14,13},{17,18},{18,... | collective-permute-start | bytes 294920 | tf_op jit(solution)/shard_map/ppermute | solution.py:356
  9.3 3.3 %collective-permute-start.4 = (f32[3,64,128]{2,1,0:T(8,128)S(1)}, f32[3,64,128]{2,1,0:T(8,128)S(1)}, u32[]{:S(2)}, u32[]{:S(2)}) collective-permute-start(f32[3,64,128]{2,1,0:T(8,128)S(1)} %constant_dynamic-update-slice_fusion.3), channel_id=1, source_target_pairs={{0,1},{1,0},{2,3},{3,2},{4,5},{5,4},{6,7},{7,6},{8,9},{9,8},{10,11... | collective-permute-start | bytes 294920 | tf_op jit(solution)/shard_map/ppermute | solution.py:356
  12.6 0.0 collective-permute-done.1
  12.6 0.0 collective-permute-done.2
  12.6 0.7 %collective-permute-start.8 = (f32[3,64,128]{2,1,0:T(8,128)S(1)}, f32[3,64,128]{2,1,0:T(8,128)S(1)}, u32[]{:S(2)}, u32[]{:S(2)}) collective-permute-start(f32[3,64,128]{2,1,0:T(8,128)S(1)} %constant_dynamic-update-slice_fusion), channel_id=1, source_target_pairs={{1,2},{2,1},{5,6},{6,5},{9,10},{10,9},{13,14},{14,13},{17,18},{18,... | collective-permute-start | bytes 294920 | tf_op jit(solution)/shard_map/ppermute | solution.py:324
  13.3 3.2 %collective-permute-start.7 = (f32[3,64,128]{2,1,0:T(8,128)S(1)}, f32[3,64,128]{2,1,0:T(8,128)S(1)}, u32[]{:S(2)}, u32[]{:S(2)}) collective-permute-start(f32[3,64,128]{2,1,0:T(8,128)S(1)} %constant_dynamic-update-slice_fusion), channel_id=1, source_target_pairs={{0,2},{1,3},{2,0},{3,1},{4,6},{5,7},{6,4},{7,5},{8,10},{9,11},{10,... | collective-permute-start | bytes 294920 | tf_op jit(solution)/shard_map/ppermute | solution.py:324
  16.5 0.0 collective-permute-done.5
  16.5 0.7 %collective-permute-start.3 = (f32[3,64,128]{2,1,0:T(8,128)S(1)}, f32[3,64,128]{2,1,0:T(8,128)S(1)}, u32[]{:S(2)}, u32[]{:S(2)}) collective-permute-start(f32[3,64,128]{2,1,0:T(8,128)S(1)} %constant_dynamic-update-slice_fusion), channel_id=1, source_target_pairs={{0,1},{1,0},{2,3},{3,2},{4,5},{5,4},{6,7},{7,6},{8,9},{9,8},{10,11... | collective-permute-start | bytes 294920 | tf_op jit(solution)/shard_map/ppermute | solution.py:324
  17.2 0.0 collective-permute-done.6
  17.2 0.0 collective-permute-done.4
  17.3 3.9 %collective-permute-done.3 = f32[3,64,128]{2,1,0:T(8,128)S(1)} collective-permute-done((f32[3,64,128]{2,1,0:T(8,128)S(1)}, f32[3,64,128]{2,1,0:T(8,128)S(1)}, u32[]{:S(2)}, u32[]{:S(2)}) %collective-permute-start.3) | collective-permute-done | bytes 98336 | tf_op jit(solution)/shard_map/ppermute | solution.py:324
  21.2 0.0 collective-permute-done.8
  21.2 0.0 collective-permute-done.7
  21.2 0.1 collective-permute-start.10
  21.3 0.0 copy-start.2
  21.3 0.0 copy-start
  21.4 0.0 copy-start.1
  21.4 0.6 %collective-permute-start.9 = (f32[4,2,64,128]{3,2,1,0:T(8,128)S(1)}, f32[4,2,64,128]{3,2,1,0:T(8,128)S(1)}, u32[]{:S(2)}, u32[]{:S(2)}) collective-permute-start(f32[4,2,64,128]{3,2,1,0:T(8,128)S(1)} %pad_maximum_fusion.2), channel_id=1, source_target_pairs={{0,4},{4,0},{1,5},{5,1},{2,6},{6,2},{3,7},{7,3},{8,12},{12,8},{9,1... | collective-permute-start | bytes 786440 | tf_op jit(solution)/shard_map/ppermute | solution.py:329
  21.9 0.1 copy-done.2
  22.0 1.1 %shard_map.68 = (f32[4,2,128,128]{3,2,1,0:T(8,128)S(1)}, f32[5,4,64,128]{3,2,1,0:T(8,128)S(1)}, f32[5,4,64,128]{3,2,1,0:T(8,128)S(1)}) custom-call(s32[2,2]{1,0:T(2,128)S(1)} %copy-done.2, f32[4,3,64,128]{3,2,1,0:T(8,128)S(1)} %pad_maximum_fusion.near_own, f32[4,3,64,128]{3,2,1,0:T(8,128)S(1)} %pad_maximum_fusion.1.near_rest), custom_call_target="tpu_custom_call" | custom-call | flops 500000000 | bytes 1048576 | tf_op jit(solution)/shard_map/pallas_call | solution.py:371
  23.1 0.2 collective-permute-done.9.far_own
  23.4 0.0 collective-permute-done.10.far_rest
  23.4 0.0 copy-done
  23.4 0.0 copy-done.1
  23.4 7.3 %shard_map.69 = (f32[1,3,64,128]{3,2,1,0:T(8,128)S(1)}, f32[1,3,64,128]{3,2,1,0:T(8,128)S(1)}) custom-call(f32[4,2,128,128]{3,2,1,0:T(8,128)S(1)} %get-tuple-element.17.wave_ref, f32[5,4,64,128]{3,2,1,0:T(8,128)S(1)} %get-tuple-element.18.near_cos, f32[5,4,64,128]{3,2,1,0:T(8,128)S(1)} %get-tuple-element.19.near_sin, ...), custom_call_target="tpu_custom_call" | custom-call | tf_op jit(solution)/shard_map/pallas_call | solution.py:379
  30.7 0.4 %collective-permute-start.11 = (f32[1,3,64,128]{3,2,1,0:T(8,128)S(1)}, f32[1,3,64,128]{3,2,1,0:T(8,128)S(1)}, u32[]{:S(2)}, u32[]{:S(2)}) collective-permute-start(f32[1,3,64,128]{3,2,1,0:T(8,128)S(1)} %get-tuple-element.21), channel_id=1, source_target_pairs={{0,4},{4,0},{1,5},{5,1},{2,6},{6,2},{3,7},{7,3},{8,12},{12,8},{9,1... | collective-permute-start | bytes 294920 | tf_op jit(solution)/shard_map/ppermute | solution.py:329
  31.0 1.0 %collective-permute-done.11.received_ref = f32[1,3,64,128]{3,2,1,0:T(8,128)S(1)} collective-permute-done((f32[1,3,64,128]{3,2,1,0:T(8,128)S(1)}, f32[1,3,64,128]{3,2,1,0:T(8,128)S(1)}, u32[]{:S(2)}, u32[]{:S(2)}) %collective-permute-start.11) | collective-permute-done | bytes 98336 | tf_op jit(solution)/shard_map/ppermute | solution.py:329
  32.0 0.7 %shard_map.70 = (f32[1,64,128]{2,1,0:T(8,128)}, f32[2,1,2,64,128]{4,3,2,1,0:T(8,128)}) custom-call(f32[1,3,64,128]{3,2,1,0:T(8,128)S(1)} %get-tuple-element.20.mine_ref, f32[1,3,64,128]{3,2,1,0:T(8,128)S(1)} %collective-permute-done.11.received_ref), custom_call_target="tpu_custom_call" | custom-call | tf_op jit(solution)/shard_map/pallas_call | solution.py:394
  (9 shorter events, 0.1 us)
Async XLA Ops:
  0.6 8.0 %copy-start.3 = (f32[2,64,128]{2,1,0:T(8,128)S(1)}, f32[2,64,128]{2,1,0:T(8,128)}, u32[]{:S(2)}) copy-start(f32[2,64,128]{2,1,0:T(8,128)} %param.7) | copy-start | bytes 196612
  0.6 5.7 %collective-permute-start = (f32[1,64,128]{2,1,0:T(8,128)}, f32[1,64,128]{2,1,0:T(8,128)S(1)}, u32[]{:S(2)}, u32[]{:S(2)}) collective-permute-start(f32[1,64,128]{2,1,0:T(8,128)} %param.5), channel_id=1, source_target_pairs={{0,8},{8,0},{16,24},{24,16},{1,9},{9,1},{17,25},{25,17},{2,10},{10... | collective-permute-start | bytes 98312 | tf_op jit(solution)/shard_map/ppermute | solution.py:324
  3.7 8.9 %collective-permute-start.2 = (f32[1,64,128]{2,1,0:T(8,128)}, f32[1,64,128]{2,1,0:T(8,128)S(1)}, u32[]{:S(2)}, u32[]{:S(2)}) collective-permute-start(f32[1,64,128]{2,1,0:T(8,128)} %param.5), channel_id=1, source_target_pairs={{0,24},{8,16},{16,8},{24,0},{1,25},{9,17},{17,9},{25,1},{2,26},{10... | collective-permute-start | bytes 98312 | tf_op jit(solution)/shard_map/ppermute | solution.py:324
  6.2 6.4 %collective-permute-start.1 = (f32[1,64,128]{2,1,0:T(8,128)}, f32[1,64,128]{2,1,0:T(8,128)S(1)}, u32[]{:S(2)}, u32[]{:S(2)}) collective-permute-start(f32[1,64,128]{2,1,0:T(8,128)} %param.5), channel_id=1, source_target_pairs={{0,16},{8,24},{16,0},{24,8},{1,17},{9,25},{17,1},{25,9},{2,18},{10... | collective-permute-start | bytes 98312 | tf_op jit(solution)/shard_map/ppermute | solution.py:324
  6.3 10.2 %collective-permute-start.5 = (f32[1,64,128]{2,1,0:T(8,128)}, f32[1,64,128]{2,1,0:T(8,128)S(1)}, u32[]{:S(2)}, u32[]{:S(2)}) collective-permute-start(f32[1,64,128]{2,1,0:T(8,128)} %param.5), channel_id=1, source_target_pairs={{0,2},{1,3},{2,0},{3,1},{4,6},{5,7},{6,4},{7,5},{8,10},{9,11},{10,... | collective-permute-start | bytes 98312 | tf_op jit(solution)/shard_map/ppermute | solution.py:359
  8.7 8.6 %collective-permute-start.6 = (f32[3,64,128]{2,1,0:T(8,128)S(1)}, f32[3,64,128]{2,1,0:T(8,128)S(1)}, u32[]{:S(2)}, u32[]{:S(2)}) collective-permute-start(f32[3,64,128]{2,1,0:T(8,128)S(1)} %constant_dynamic-update-slice_fusion.3), channel_id=1, source_target_pairs={{1,2},{2,1},{5,6},{6,5},{9,10},{10,9},{13,14},{14,13},{17,18},{18,... | collective-permute-start | bytes 294920 | tf_op jit(solution)/shard_map/ppermute | solution.py:356
  9.3 7.9 %collective-permute-start.4 = (f32[3,64,128]{2,1,0:T(8,128)S(1)}, f32[3,64,128]{2,1,0:T(8,128)S(1)}, u32[]{:S(2)}, u32[]{:S(2)}) collective-permute-start(f32[3,64,128]{2,1,0:T(8,128)S(1)} %constant_dynamic-update-slice_fusion.3), channel_id=1, source_target_pairs={{0,1},{1,0},{2,3},{3,2},{4,5},{5,4},{6,7},{7,6},{8,9},{9,8},{10,11... | collective-permute-start | bytes 294920 | tf_op jit(solution)/shard_map/ppermute | solution.py:356
  12.6 8.5 %collective-permute-start.8 = (f32[3,64,128]{2,1,0:T(8,128)S(1)}, f32[3,64,128]{2,1,0:T(8,128)S(1)}, u32[]{:S(2)}, u32[]{:S(2)}) collective-permute-start(f32[3,64,128]{2,1,0:T(8,128)S(1)} %constant_dynamic-update-slice_fusion), channel_id=1, source_target_pairs={{1,2},{2,1},{5,6},{6,5},{9,10},{10,9},{13,14},{14,13},{17,18},{18,... | collective-permute-start | bytes 294920 | tf_op jit(solution)/shard_map/ppermute | solution.py:324
  13.3 7.8 %collective-permute-start.7 = (f32[3,64,128]{2,1,0:T(8,128)S(1)}, f32[3,64,128]{2,1,0:T(8,128)S(1)}, u32[]{:S(2)}, u32[]{:S(2)}) collective-permute-start(f32[3,64,128]{2,1,0:T(8,128)S(1)} %constant_dynamic-update-slice_fusion), channel_id=1, source_target_pairs={{0,2},{1,3},{2,0},{3,1},{4,6},{5,7},{6,4},{7,5},{8,10},{9,11},{10,... | collective-permute-start | bytes 294920 | tf_op jit(solution)/shard_map/ppermute | solution.py:324
  16.5 4.6 %collective-permute-start.3 = (f32[3,64,128]{2,1,0:T(8,128)S(1)}, f32[3,64,128]{2,1,0:T(8,128)S(1)}, u32[]{:S(2)}, u32[]{:S(2)}) collective-permute-start(f32[3,64,128]{2,1,0:T(8,128)S(1)} %constant_dynamic-update-slice_fusion), channel_id=1, source_target_pairs={{0,1},{1,0},{2,3},{3,2},{4,5},{5,4},{6,7},{7,6},{8,9},{9,8},{10,11... | collective-permute-start | bytes 294920 | tf_op jit(solution)/shard_map/ppermute | solution.py:324
  21.2 2.2 %collective-permute-start.10 = (f32[4,3,64,128]{3,2,1,0:T(8,128)S(1)}, f32[4,3,64,128]{3,2,1,0:T(8,128)S(1)}, u32[]{:S(2)}, u32[]{:S(2)}) collective-permute-start(f32[4,3,64,128]{3,2,1,0:T(8,128)S(1)} %pad_maximum_fusion.1.near_rest), channel_id=1, source_target_pairs={{0,4},{4,0},{1,5},{5,1},{2,6},{6,2},{3,7},{7,3},{8,12},{12,8},{9,1... | collective-permute-start | bytes 1179656 | tf_op jit(solution)/shard_map/ppermute | solution.py:329
  21.3 0.7 %copy-start.2 = (s32[2,2]{1,0:T(2,128)S(1)}, s32[2,2]{1,0:T(2,128)}, u32[]{:S(2)}) copy-start(s32[2,2]{1,0:T(2,128)} %tilt_ref.1) | copy-start | bytes 52
  21.3 2.0 %copy-start = (bf16[512,512]{1,0:T(8,128)(2,1)S(1)}, bf16[512,512]{1,0:T(8,128)(2,1)}, u32[]{:S(2)}) copy-start(bf16[512,512]{1,0:T(8,128)(2,1)} %constant.20.clone.col_ref) | copy-start | bytes 1572868
  21.4 2.0 %copy-start.1 = (bf16[2,256,512]{2,1,0:T(8,128)(2,1)S(1)}, bf16[2,256,512]{2,1,0:T(8,128)(2,1)}, u32[]{:S(2)}) copy-start(bf16[2,256,512]{2,1,0:T(8,128)(2,1)} %constant.19.clone.row_ref) | copy-start | bytes 1572868
  21.4 2.0 %collective-permute-start.9 = (f32[4,2,64,128]{3,2,1,0:T(8,128)S(1)}, f32[4,2,64,128]{3,2,1,0:T(8,128)S(1)}, u32[]{:S(2)}, u32[]{:S(2)}) collective-permute-start(f32[4,2,64,128]{3,2,1,0:T(8,128)S(1)} %pad_maximum_fusion.2), channel_id=1, source_target_pairs={{0,4},{4,0},{1,5},{5,1},{2,6},{6,2},{3,7},{7,3},{8,12},{12,8},{9,1... | collective-permute-start | bytes 786440 | tf_op jit(solution)/shard_map/ppermute | solution.py:329
  30.7 1.4 %collective-permute-start.11 = (f32[1,3,64,128]{3,2,1,0:T(8,128)S(1)}, f32[1,3,64,128]{3,2,1,0:T(8,128)S(1)}, u32[]{:S(2)}, u32[]{:S(2)}) collective-permute-start(f32[1,3,64,128]{3,2,1,0:T(8,128)S(1)} %get-tuple-element.21), channel_id=1, source_target_pairs={{0,4},{4,0},{1,5},{5,1},{2,6},{6,2},{3,7},{7,3},{8,12},{12,8},{9,1... | collective-permute-start | bytes 294920 | tf_op jit(solution)/shard_map/ppermute | solution.py:329

commit v14 on v13

--- a/solution.py
+++ b/solution.py
@@ -214,18 +214,17 @@
 
 def wave_kernel(
     wave_ref, near_cos, near_sin, near_own, far_own, far_rest, row_ref, col_ref,
-    mine_ref, theirs_ref, far_cos, far_sin, kept_ref, moved_ref, left_ref, grad_ref, even_edge, odd_edge,
+    mine_ref, theirs_ref, far_cos, far_sin, kept_ref, moved_ref, left_ref, grad_ref, edge_ref,
 ):
     blocks, _, height, _ = wave_ref.shape
     count = near_cos.shape[0] - 1
     core, own_section, own_place = lax.axis_index("row"), lax.axis_index("depth"), lax.axis_index("col")
     near, far = pl.ds(0, height // 2), pl.ds(height // 2, height // 2)
     screens = (near_cos, near_sin, far_cos, far_sin)
-    row_matrix = row_ref[core]
+    row_matrix = row_ref.at[core]
     window = min(3, blocks)
     window_start = jnp.clip(own_place - 1, 0, blocks - window)
     own_in_window = own_place - window_start
-    edges = (even_edge, odd_edge)
 
     def far_screens(slice_index):
         bits = slice_index ^ own_section
@@ -234,25 +233,28 @@
             angle = jnp.where(bits == 0, far_own[held, 0], far_rest[held, jnp.maximum(bits - 1, 0)])
             far_cos[slice_index, col], far_sin[slice_index, col] = cos_sin(angle)
 
-    for edge_ref in edges:
-        clear_edge(edge_ref, 0, False)
-        clear_edge(edge_ref, blocks - 1, True)
+    clear_edge(edge_ref, 0, False)
+    clear_edge(edge_ref, blocks - 1, True)
     far_cos[count] = jnp.ones(far_cos.shape[1:], jnp.float32)
     far_sin[count] = jnp.zeros(far_cos.shape[1:], jnp.float32)
     far_screens(0)
 
-    waves = [(wave_ref[place, 0], wave_ref[place, 1]) for place in range(blocks)]
-    for tick in range(count):
-        entering = (wave_ref if tick == 0 else kept_ref)[own_place]
+    def held_waves(size):
+        return [(kept_ref[place, 0], kept_ref[place, 1]) for place in range(size)]
+
+    def forward(tick, carry):
+        entering = kept_ref[own_place]
         moved_ref[tick, 0], moved_ref[tick, 1] = turned(tick, own_place, screens, (entering[0], entering[1]))
-        waves = advance(tick, 0, waves, screens, row_matrix, col_ref, edges[tick % 2])
-        if tick + 1 < count:
-            far_screens(tick + 1)
+        waves = advance(tick, 0, held_waves(blocks), screens, row_matrix[...], col_ref, edge_ref)
+        far_screens(jnp.minimum(tick + 1, count - 1))
         keep(kept_ref, waves)
         left_ref[tick] = kept_ref[own_place]
-
-    for edge_ref in edges:
-        clear_edge(edge_ref, window - 1, True)
+        return carry
+
+    kept_ref[...] = wave_ref[...]
+    lax.fori_loop(0, count, forward, 0)
+
+    clear_edge(edge_ref, window - 1, True)
     waves = []
     for place in range(window):
         block = window_start + place
@@ -262,12 +264,19 @@
         misfit = 2.0 * (real * real + imag * imag - measured)
         waves.append((misfit * real, -misfit * imag))
 
-    for tick in range(count - 1):
-        waves = advance(count - tick, window_start, waves, screens, row_matrix, col_ref, edges[tick % 2])
+    keep(kept_ref, waves)
+
+    def backward(tick, carry):
+        waves = advance(
+            count - tick, window_start, held_waves(window), screens, row_matrix[...], col_ref, edge_ref
+        )
         keep(kept_ref, waves)
         arrived = count - 1 - tick
         pulled = kept_ref[own_in_window]
         grad_ref[arrived] = -(pulled[1] * moved_ref[arrived, 0] + pulled[0] * moved_ref[arrived, 1])
+        return carry
+
+    lax.fori_loop(0, count - 1, backward, 0)
 
     left, right = jnp.maximum(own_place - 1, 0), jnp.minimum(own_place + 1, blocks - 1)
     lane = lax.broadcasted_iota(jnp.int32, (2 * height, LANES), 1)
@@ -280,7 +289,7 @@
     edge_cells = jnp.where(
         lane < LANES // 2, jnp.where(has_right, cells(right), 0.0), jnp.where(has_left, cells(left), 0.0)
     )
-    done = row_product(row_matrix, jnp.concatenate([cells(own_place), edge_cells], axis=1))
+    done = row_product(row_matrix[...], jnp.concatenate([cells(own_place), edge_cells], axis=1))
     lane = lax.broadcasted_iota(jnp.int32, (height, LANES), 1)
     between = (lane >= HALO) & (lane < LANES - HALO)
     highs, lows, edges = [], [], []
@@ -385,7 +394,7 @@
         + [pltpu.VMEM(field, jnp.float32)]
         + [pltpu.VMEM((count, 2, height, tile_c), jnp.float32)] * 2
         + [pltpu.VMEM((count, height, tile_c), jnp.float32)]
-        + [pltpu.VMEM((blocks, height, 2 * LANES), jnp.bfloat16)] * 2,
+        + [pltpu.VMEM((blocks, height, 2 * LANES), jnp.bfloat16)],
         compiler_params=params(24),
     )(
         wave, near_cos, near_sin, near_own, far_own, far_rest,

time: 32.9 us -> 33.4 us (1.015)
  Pallas kernels: 9.12 us -> 9.56 us
    pallas_call x1, Pallas kernels: 7.3 us -> 7.75 us  [whole_field_body(): pl.pallas_call(wave_kernel, out_shape=(array(1, 3, tile_r, tile_c),) * 2,...]
where the time goes in v14:
time: 33.4 us; the launch traced here: 33.2 us
  starting transfers between devices  16.7 us (50%)
  Pallas kernels  9.56 us (29%)
  waiting for transfers between devices  5.18 us (16%)
  local copies, waits for them, and re-layouts  0.93 us (3%)
  between operations  0.77 us (2%)
    ppermute x6, starting transfers between devices, spread(): lax.ppermute(shard, axis, pairs)  10.2 us
    pallas_call x1, Pallas kernels, whole_field_body(): pl.pallas_call(wave_kernel, out_shape=(array(1, 3, tile_r, tile_c),) * 2,...  7.75 us
    ppermute x2, starting transfers between devices, whole_field_body(): near_own.append(lax.ppermute(packet, 'col', close))  3.94 us
    ppermute x6, waiting for transfers between devices, spread(): lax.ppermute(shard, axis, pairs)  3.91 us
    ppermute x1, starting transfers between devices, whole_field_body(): lax.ppermute(slab, 'col', further)  1.52 us
    ppermute x3, waiting for transfers between devices, swap_cores(): return lax.ppermute(value, 'row', [(0, 1), (1, 0)])  1.26 us
    pallas_call x1, Pallas kernels, whole_field_body(): pl.pallas_call(prepare_kernel, out_shape=(array(*field), array(*half_scre...  1.13 us
    ppermute x3, starting transfers between devices, swap_cores(): return lax.ppermute(value, 'row', [(0, 1), (1, 0)])  0.97 us
  transfers between devices with their start and end apart: 12, of which 3 were waited for; matrix products, arithmetic and copies ran while one was open for 3% of the time, Pallas kernels for 3%

profile of v14, /device:TPU:0, one launch (start us, length us, event | category | flops | bytes accessed | tf_op | source)
XLA Modules:
  0.0 33.2 jit_solution(1353513943086465231)
XLA Ops:
  0.6 0.0 copy-start.3
  0.6 3.1 %collective-permute-start = (f32[1,64,128]{2,1,0:T(8,128)}, f32[1,64,128]{2,1,0:T(8,128)S(1)}, u32[]{:S(2)}, u32[]{:S(2)}) collective-permute-start(f32[1,64,128]{2,1,0:T(8,128)} %param.5), channel_id=1, source_target_pairs={{0,8},{8,0},{16,24},{24,16},{1,9},{9,1},{17,25},{25,17},{2,10},{10... | collective-permute-start | bytes 98312 | tf_op jit(solution)/shard_map/ppermute | solution.py:333
  3.7 2.5 %collective-permute-start.2 = (f32[1,64,128]{2,1,0:T(8,128)}, f32[1,64,128]{2,1,0:T(8,128)S(1)}, u32[]{:S(2)}, u32[]{:S(2)}) collective-permute-start(f32[1,64,128]{2,1,0:T(8,128)} %param.5), channel_id=1, source_target_pairs={{0,24},{8,16},{16,8},{24,0},{1,25},{9,17},{17,9},{25,1},{2,26},{10... | collective-permute-start | bytes 98312 | tf_op jit(solution)/shard_map/ppermute | solution.py:333
  6.2 0.1 collective-permute-start.1
  6.3 0.0 collective-permute-done
  6.3 1.5 %collective-permute-start.5 = (f32[1,64,128]{2,1,0:T(8,128)}, f32[1,64,128]{2,1,0:T(8,128)S(1)}, u32[]{:S(2)}, u32[]{:S(2)}) collective-permute-start(f32[1,64,128]{2,1,0:T(8,128)} %param.5), channel_id=1, source_target_pairs={{0,2},{1,3},{2,0},{3,1},{4,6},{5,7},{6,4},{7,5},{8,10},{9,11},{10,... | collective-permute-start | bytes 98312 | tf_op jit(solution)/shard_map/ppermute | solution.py:368
  7.8 0.8 %constant_dynamic-update-slice_fusion.4 = f32[3,64,128]{2,1,0:T(8,128)S(1)} fusion(f32[1,64,128]{2,1,0:T(8,128)} %param.5), kind=kLoop, calls=%fused_computation.8 | loop fusion | bytes 65536
  8.6 0.0 copy-done.3
  8.7 0.7 %collective-permute-start.6 = (f32[3,64,128]{2,1,0:T(8,128)S(1)}, f32[3,64,128]{2,1,0:T(8,128)S(1)}, u32[]{:S(2)}, u32[]{:S(2)}) collective-permute-start(f32[3,64,128]{2,1,0:T(8,128)S(1)} %constant_dynamic-update-slice_fusion.3), channel_id=1, source_target_pairs={{1,2},{2,1},{5,6},{6,5},{9,10},{10,9},{13,14},{14,13},{17,18},{18,... | collective-permute-start | bytes 294920 | tf_op jit(solution)/shard_map/ppermute | solution.py:365
  9.3 3.3 %collective-permute-start.4 = (f32[3,64,128]{2,1,0:T(8,128)S(1)}, f32[3,64,128]{2,1,0:T(8,128)S(1)}, u32[]{:S(2)}, u32[]{:S(2)}) collective-permute-start(f32[3,64,128]{2,1,0:T(8,128)S(1)} %constant_dynamic-update-slice_fusion.3), channel_id=1, source_target_pairs={{0,1},{1,0},{2,3},{3,2},{4,5},{5,4},{6,7},{7,6},{8,9},{9,8},{10,11... | collective-permute-start | bytes 294920 | tf_op jit(solution)/shard_map/ppermute | solution.py:365
  12.6 0.0 collective-permute-done.1
  12.6 0.0 collective-permute-done.2
  12.6 0.7 %collective-permute-start.8 = (f32[3,64,128]{2,1,0:T(8,128)S(1)}, f32[3,64,128]{2,1,0:T(8,128)S(1)}, u32[]{:S(2)}, u32[]{:S(2)}) collective-permute-start(f32[3,64,128]{2,1,0:T(8,128)S(1)} %constant_dynamic-update-slice_fusion), channel_id=1, source_target_pairs={{1,2},{2,1},{5,6},{6,5},{9,10},{10,9},{13,14},{14,13},{17,18},{18,... | collective-permute-start | bytes 294920 | tf_op jit(solution)/shard_map/ppermute | solution.py:333
  13.3 3.2 %collective-permute-start.7 = (f32[3,64,128]{2,1,0:T(8,128)S(1)}, f32[3,64,128]{2,1,0:T(8,128)S(1)}, u32[]{:S(2)}, u32[]{:S(2)}) collective-permute-start(f32[3,64,128]{2,1,0:T(8,128)S(1)} %constant_dynamic-update-slice_fusion), channel_id=1, source_target_pairs={{0,2},{1,3},{2,0},{3,1},{4,6},{5,7},{6,4},{7,5},{8,10},{9,11},{10,... | collective-permute-start | bytes 294920 | tf_op jit(solution)/shard_map/ppermute | solution.py:333
  16.5 0.0 collective-permute-done.5
  16.5 0.7 %collective-permute-start.3 = (f32[3,64,128]{2,1,0:T(8,128)S(1)}, f32[3,64,128]{2,1,0:T(8,128)S(1)}, u32[]{:S(2)}, u32[]{:S(2)}) collective-permute-start(f32[3,64,128]{2,1,0:T(8,128)S(1)} %constant_dynamic-update-slice_fusion), channel_id=1, source_target_pairs={{0,1},{1,0},{2,3},{3,2},{4,5},{5,4},{6,7},{7,6},{8,9},{9,8},{10,11... | collective-permute-start | bytes 294920 | tf_op jit(solution)/shard_map/ppermute | solution.py:333
  17.2 0.0 collective-permute-done.6
  17.2 0.0 collective-permute-done.4
  17.3 3.9 %collective-permute-done.3 = f32[3,64,128]{2,1,0:T(8,128)S(1)} collective-permute-done((f32[3,64,128]{2,1,0:T(8,128)S(1)}, f32[3,64,128]{2,1,0:T(8,128)S(1)}, u32[]{:S(2)}, u32[]{:S(2)}) %collective-permute-start.3) | collective-permute-done | bytes 98336 | tf_op jit(solution)/shard_map/ppermute | solution.py:333
  21.2 0.0 collective-permute-done.8
  21.2 0.0 collective-permute-done.7
  21.2 0.1 collective-permute-start.10
  21.3 0.0 copy-start.2
  21.3 0.0 copy-start
  21.4 0.0 copy-start.1
  21.4 0.6 %collective-permute-start.9 = (f32[4,2,64,128]{3,2,1,0:T(8,128)S(1)}, f32[4,2,64,128]{3,2,1,0:T(8,128)S(1)}, u32[]{:S(2)}, u32[]{:S(2)}) collective-permute-start(f32[4,2,64,128]{3,2,1,0:T(8,128)S(1)} %pad_maximum_fusion.2), channel_id=1, source_target_pairs={{0,4},{4,0},{1,5},{5,1},{2,6},{6,2},{3,7},{7,3},{8,12},{12,8},{9,1... | collective-permute-start | bytes 786440 | tf_op jit(solution)/shard_map/ppermute | solution.py:338
  21.9 0.1 copy-done.2
  22.0 1.1 %shard_map.68 = (f32[4,2,128,128]{3,2,1,0:T(8,128)S(1)}, f32[5,4,64,128]{3,2,1,0:T(8,128)S(1)}, f32[5,4,64,128]{3,2,1,0:T(8,128)S(1)}) custom-call(s32[2,2]{1,0:T(2,128)S(1)} %copy-done.2, f32[4,3,64,128]{3,2,1,0:T(8,128)S(1)} %pad_maximum_fusion.near_own, f32[4,3,64,128]{3,2,1,0:T(8,128)S(1)} %pad_maximum_fusion.1.near_rest), custom_call_target="tpu_custom_call" | custom-call | flops 500000000 | bytes 1048576 | tf_op jit(solution)/shard_map/pallas_call | solution.py:380
  23.1 0.2 collective-permute-done.9.far_own
  23.4 0.0 collective-permute-done.10.far_rest
  23.4 0.0 copy-done
  23.4 0.0 copy-done.1
  23.4 7.8 %shard_map.69 = (f32[1,3,64,128]{3,2,1,0:T(8,128)S(1)}, f32[1,3,64,128]{3,2,1,0:T(8,128)S(1)}) custom-call(f32[4,2,128,128]{3,2,1,0:T(8,128)S(1)} %get-tuple-element.17.wave_ref, f32[5,4,64,128]{3,2,1,0:T(8,128)S(1)} %get-tuple-element.18.near_cos, f32[5,4,64,128]{3,2,1,0:T(8,128)S(1)} %get-tuple-element.19.near_sin, ...), custom_call_target="tpu_custom_call" | custom-call | tf_op jit(solution)/shard_map/pallas_call | solution.py:388
  31.1 0.3 %collective-permute-start.11 = (f32[1,3,64,128]{3,2,1,0:T(8,128)S(1)}, f32[1,3,64,128]{3,2,1,0:T(8,128)S(1)}, u32[]{:S(2)}, u32[]{:S(2)}) collective-permute-start(f32[1,3,64,128]{3,2,1,0:T(8,128)S(1)} %get-tuple-element.21), channel_id=1, source_target_pairs={{0,4},{4,0},{1,5},{5,1},{2,6},{6,2},{3,7},{7,3},{8,12},{12,8},{9,1... | collective-permute-start | bytes 294920 | tf_op jit(solution)/shard_map/ppermute | solution.py:338
  31.5 1.0 %collective-permute-done.11.received_ref = f32[1,3,64,128]{3,2,1,0:T(8,128)S(1)} collective-permute-done((f32[1,3,64,128]{3,2,1,0:T(8,128)S(1)}, f32[1,3,64,128]{3,2,1,0:T(8,128)S(1)}, u32[]{:S(2)}, u32[]{:S(2)}) %collective-permute-start.11) | collective-permute-done | bytes 98336 | tf_op jit(solution)/shard_map/ppermute | solution.py:338
  32.5 0.7 %shard_map.70 = (f32[1,64,128]{2,1,0:T(8,128)}, f32[2,1,2,64,128]{4,3,2,1,0:T(8,128)}) custom-call(f32[1,3,64,128]{3,2,1,0:T(8,128)S(1)} %get-tuple-element.20.mine_ref, f32[1,3,64,128]{3,2,1,0:T(8,128)S(1)} %collective-permute-done.11.received_ref), custom_call_target="tpu_custom_call" | custom-call | tf_op jit(solution)/shard_map/pallas_call | solution.py:403
  (9 shorter events, 0.1 us)
Async XLA Ops:
  0.6 8.0 %copy-start.3 = (f32[2,64,128]{2,1,0:T(8,128)S(1)}, f32[2,64,128]{2,1,0:T(8,128)}, u32[]{:S(2)}) copy-start(f32[2,64,128]{2,1,0:T(8,128)} %param.7) | copy-start | bytes 196612
  0.6 5.7 %collective-permute-start = (f32[1,64,128]{2,1,0:T(8,128)}, f32[1,64,128]{2,1,0:T(8,128)S(1)}, u32[]{:S(2)}, u32[]{:S(2)}) collective-permute-start(f32[1,64,128]{2,1,0:T(8,128)} %param.5), channel_id=1, source_target_pairs={{0,8},{8,0},{16,24},{24,16},{1,9},{9,1},{17,25},{25,17},{2,10},{10... | collective-permute-start | bytes 98312 | tf_op jit(solution)/shard_map/ppermute | solution.py:333
  3.7 8.9 %collective-permute-start.2 = (f32[1,64,128]{2,1,0:T(8,128)}, f32[1,64,128]{2,1,0:T(8,128)S(1)}, u32[]{:S(2)}, u32[]{:S(2)}) collective-permute-start(f32[1,64,128]{2,1,0:T(8,128)} %param.5), channel_id=1, source_target_pairs={{0,24},{8,16},{16,8},{24,0},{1,25},{9,17},{17,9},{25,1},{2,26},{10... | collective-permute-start | bytes 98312 | tf_op jit(solution)/shard_map/ppermute | solution.py:333
  6.2 6.4 %collective-permute-start.1 = (f32[1,64,128]{2,1,0:T(8,128)}, f32[1,64,128]{2,1,0:T(8,128)S(1)}, u32[]{:S(2)}, u32[]{:S(2)}) collective-permute-start(f32[1,64,128]{2,1,0:T(8,128)} %param.5), channel_id=1, source_target_pairs={{0,16},{8,24},{16,0},{24,8},{1,17},{9,25},{17,1},{25,9},{2,18},{10... | collective-permute-start | bytes 98312 | tf_op jit(solution)/shard_map/ppermute | solution.py:333
  6.3 10.2 %collective-permute-start.5 = (f32[1,64,128]{2,1,0:T(8,128)}, f32[1,64,128]{2,1,0:T(8,128)S(1)}, u32[]{:S(2)}, u32[]{:S(2)}) collective-permute-start(f32[1,64,128]{2,1,0:T(8,128)} %param.5), channel_id=1, source_target_pairs={{0,2},{1,3},{2,0},{3,1},{4,6},{5,7},{6,4},{7,5},{8,10},{9,11},{10,... | collective-permute-start | bytes 98312 | tf_op jit(solution)/shard_map/ppermute | solution.py:368
  8.7 8.6 %collective-permute-start.6 = (f32[3,64,128]{2,1,0:T(8,128)S(1)}, f32[3,64,128]{2,1,0:T(8,128)S(1)}, u32[]{:S(2)}, u32[]{:S(2)}) collective-permute-start(f32[3,64,128]{2,1,0:T(8,128)S(1)} %constant_dynamic-update-slice_fusion.3), channel_id=1, source_target_pairs={{1,2},{2,1},{5,6},{6,5},{9,10},{10,9},{13,14},{14,13},{17,18},{18,... | collective-permute-start | bytes 294920 | tf_op jit(solution)/shard_map/ppermute | solution.py:365
  9.3 7.9 %collective-permute-start.4 = (f32[3,64,128]{2,1,0:T(8,128)S(1)}, f32[3,64,128]{2,1,0:T(8,128)S(1)}, u32[]{:S(2)}, u32[]{:S(2)}) collective-permute-start(f32[3,64,128]{2,1,0:T(8,128)S(1)} %constant_dynamic-update-slice_fusion.3), channel_id=1, source_target_pairs={{0,1},{1,0},{2,3},{3,2},{4,5},{5,4},{6,7},{7,6},{8,9},{9,8},{10,11... | collective-permute-start | bytes 294920 | tf_op jit(solution)/shard_map/ppermute | solution.py:365
  12.6 8.5 %collective-permute-start.8 = (f32[3,64,128]{2,1,0:T(8,128)S(1)}, f32[3,64,128]{2,1,0:T(8,128)S(1)}, u32[]{:S(2)}, u32[]{:S(2)}) collective-permute-start(f32[3,64,128]{2,1,0:T(8,128)S(1)} %constant_dynamic-update-slice_fusion), channel_id=1, source_target_pairs={{1,2},{2,1},{5,6},{6,5},{9,10},{10,9},{13,14},{14,13},{17,18},{18,... | collective-permute-start | bytes 294920 | tf_op jit(solution)/shard_map/ppermute | solution.py:333
  13.3 7.8 %collective-permute-start.7 = (f32[3,64,128]{2,1,0:T(8,128)S(1)}, f32[3,64,128]{2,1,0:T(8,128)S(1)}, u32[]{:S(2)}, u32[]{:S(2)}) collective-permute-start(f32[3,64,128]{2,1,0:T(8,128)S(1)} %constant_dynamic-update-slice_fusion), channel_id=1, source_target_pairs={{0,2},{1,3},{2,0},{3,1},{4,6},{5,7},{6,4},{7,5},{8,10},{9,11},{10,... | collective-permute-start | bytes 294920 | tf_op jit(solution)/shard_map/ppermute | solution.py:333
  16.5 4.6 %collective-permute-start.3 = (f32[3,64,128]{2,1,0:T(8,128)S(1)}, f32[3,64,128]{2,1,0:T(8,128)S(1)}, u32[]{:S(2)}, u32[]{:S(2)}) collective-permute-start(f32[3,64,128]{2,1,0:T(8,128)S(1)} %constant_dynamic-update-slice_fusion), channel_id=1, source_target_pairs={{0,1},{1,0},{2,3},{3,2},{4,5},{5,4},{6,7},{7,6},{8,9},{9,8},{10,11... | collective-permute-start | bytes 294920 | tf_op jit(solution)/shard_map/ppermute | solution.py:333
  21.2 2.2 %collective-permute-start.10 = (f32[4,3,64,128]{3,2,1,0:T(8,128)S(1)}, f32[4,3,64,128]{3,2,1,0:T(8,128)S(1)}, u32[]{:S(2)}, u32[]{:S(2)}) collective-permute-start(f32[4,3,64,128]{3,2,1,0:T(8,128)S(1)} %pad_maximum_fusion.1.near_rest), channel_id=1, source_target_pairs={{0,4},{4,0},{1,5},{5,1},{2,6},{6,2},{3,7},{7,3},{8,12},{12,8},{9,1... | collective-permute-start | bytes 1179656 | tf_op jit(solution)/shard_map/ppermute | solution.py:338
  21.3 0.7 %copy-start.2 = (s32[2,2]{1,0:T(2,128)S(1)}, s32[2,2]{1,0:T(2,128)}, u32[]{:S(2)}) copy-start(s32[2,2]{1,0:T(2,128)} %tilt_ref.1) | copy-start | bytes 52
  21.3 2.0 %copy-start = (bf16[512,512]{1,0:T(8,128)(2,1)S(1)}, bf16[512,512]{1,0:T(8,128)(2,1)}, u32[]{:S(2)}) copy-start(bf16[512,512]{1,0:T(8,128)(2,1)} %constant.20.clone.col_ref) | copy-start | bytes 1572868
  21.4 2.0 %copy-start.1 = (bf16[2,256,512]{2,1,0:T(8,128)(2,1)S(1)}, bf16[2,256,512]{2,1,0:T(8,128)(2,1)}, u32[]{:S(2)}) copy-start(bf16[2,256,512]{2,1,0:T(8,128)(2,1)} %constant.19.clone.row_ref) | copy-start | bytes 1572868
  21.4 2.0 %collective-permute-start.9 = (f32[4,2,64,128]{3,2,1,0:T(8,128)S(1)}, f32[4,2,64,128]{3,2,1,0:T(8,128)S(1)}, u32[]{:S(2)}, u32[]{:S(2)}) collective-permute-start(f32[4,2,64,128]{3,2,1,0:T(8,128)S(1)} %pad_maximum_fusion.2), channel_id=1, source_target_pairs={{0,4},{4,0},{1,5},{5,1},{2,6},{6,2},{3,7},{7,3},{8,12},{12,8},{9,1... | collective-permute-start | bytes 786440 | tf_op jit(solution)/shard_map/ppermute | solution.py:338
  31.1 1.4 %collective-permute-start.11 = (f32[1,3,64,128]{3,2,1,0:T(8,128)S(1)}, f32[1,3,64,128]{3,2,1,0:T(8,128)S(1)}, u32[]{:S(2)}, u32[]{:S(2)}) collective-permute-start(f32[1,3,64,128]{3,2,1,0:T(8,128)S(1)} %get-tuple-element.21), channel_id=1, source_target_pairs={{0,4},{4,0},{1,5},{5,1},{2,6},{6,2},{3,7},{7,3},{8,12},{12,8},{9,1... | collective-permute-start | bytes 294920 | tf_op jit(solution)/shard_map/ppermute | solution.py:338

commit v15 on v13

--- a/solution.py
+++ b/solution.py
@@ -315,14 +315,13 @@
         copy.wait()
 
 
-def spread(shard, axis, reach=None):
+def spread(shard, axis):
     size = lax.axis_size(axis)
-    reach = size if reach is None else reach
-    pieces = []
-    for bits in range(1, size):
-        pairs = [(i, i ^ bits) for i in range(size) if abs(i - (i ^ bits)) <= reach]
-        pieces.append(lax.ppermute(shard, axis, pairs) if pairs else jnp.zeros_like(shard))
-    return pieces
+    return [lax.ppermute(shard, axis, [(i, i ^ bits) for i in range(size)]) for bits in range(1, size)]
+
+
+def exchange(value, pairs):
+    return lax.ppermute(value, "col", pairs)
 
 
 def swap_cores(value):
@@ -348,18 +347,12 @@
     other_depths[0], measured, slab = lax.optimization_barrier((other_depths[0], intensity, phase))
     other_depths = jnp.concatenate(other_depths, axis=0)
     packet = jnp.concatenate([slab, measured], axis=0)
-    near_own = [packet]
-    for bits in range(1, blocks):
-        pairs = [(i, i ^ bits) for i in range(blocks)]
-        close = [(i, j) for i, j in pairs if abs(i - j) <= 1]
-        if close:
-            near_own.append(lax.ppermute(packet, "col", close))
-        else:
-            further = [(i, j) for i, j in pairs if abs(i - j) <= 2]
-            arrived = lax.ppermute(slab, "col", further) if further else jnp.zeros_like(slab)
-            near_own.append(jnp.concatenate([arrived, jnp.zeros_like(measured)], axis=0))
-    near_own = jnp.stack(near_own)
-    arriving = spread(other_depths, "col", 2)
+    by_one, by_two, corner = [(i, i ^ 1) for i in range(4)], [(i, i ^ 2) for i in range(4)], [(1, 2), (2, 1)]
+    packet_near, packet_corner = exchange(packet, by_one), exchange(packet, corner)
+    whole_column = exchange(jnp.concatenate([slab, other_depths], axis=0), by_two)
+    packet_next = jnp.concatenate([whole_column[:1], jnp.zeros_like(measured)], axis=0)
+    near_own = jnp.stack([packet, packet_near, packet_next, packet_corner])
+    arriving = [exchange(other_depths, by_one), whole_column[1:], exchange(other_depths, corner)]
     arriving[0], near_own = lax.optimization_barrier((arriving[0], near_own))
     near_rest = jnp.stack([other_depths] + arriving)
     wanted = lax.dynamic_slice_in_dim(near_own, 2 - core, 1, 1)
@@ -577,10 +570,9 @@
         and batch == rows == 2
         and slices == sections
         and sections & (sections - 1) == 0
-        and cols & (cols - 1) == 0
+        and cols == 4
         and height == LANES
         and width == cols * LANES
-        and cols > 1
         and sections > 1
         and sections * HALO <= LANES
     )

time: 32.9 us -> 33.1 us (level)
  waiting for transfers between devices: 5.17 us -> 4.71 us
  starting transfers between devices: 16.7 us -> 17.1 us
    ppermute x9 -> x8, waiting for transfers between devices: 3.92 us -> 3.44 us  [the longest x5 3.43 us: exchange(): return lax.ppermute(value, 'col', pairs)]
    ppermute x9 -> x8, starting transfers between devices: 15.7 us -> 16.2 us  [the longest x5 10.5 us: exchange(): return lax.ppermute(value, 'col', pairs)]
    unnamed x11 -> x15, local copies, waits for them, and re-layouts: 0.89 us -> 0.89 us
  transfers between devices with their start and end apart: 12 -> 11, of which waited for: 3 -> 3; matrix products, arithmetic and copies ran while one was open for 3% -> 3% of each run, Pallas kernels for 3% -> 3%
where the time goes in v15:
time: 33.1 us; the launch traced here: 32.8 us
  starting transfers between devices  17.1 us (52%)
  Pallas kernels  9.13 us (28%)
  waiting for transfers between devices  4.71 us (14%)
  local copies, waits for them, and re-layouts  0.92 us (3%)
  between operations  0.78 us (2%)
    ppermute x5, starting transfers between devices, exchange(): return lax.ppermute(value, 'col', pairs)  10.5 us
    pallas_call x1, Pallas kernels, whole_field_body(): pl.pallas_call(wave_kernel, out_shape=(array(1, 3, tile_r, tile_c),) * 2,...  7.32 us
    ppermute x3, starting transfers between devices, spread(): lax.ppermute(shard, axis, [(i, i ^ bits) for i in range(size)])  5.68 us
    ppermute x5, waiting for transfers between devices, exchange(): return lax.ppermute(value, 'col', pairs)  3.43 us
    ppermute x3, waiting for transfers between devices, swap_cores(): return lax.ppermute(value, 'row', [(0, 1), (1, 0)])  1.28 us
    pallas_call x1, Pallas kernels, whole_field_body(): pl.pallas_call(prepare_kernel, out_shape=(array(*field), array(*half_scre...  1.13 us
    ppermute x3, starting transfers between devices, swap_cores(): return lax.ppermute(value, 'row', [(0, 1), (1, 0)])  0.95 us
    unnamed x15, local copies, waits for them, and re-layouts  0.89 us
  transfers between devices with their start and end apart: 11, of which 3 were waited for; matrix products, arithmetic and copies ran while one was open for 3% of the time, Pallas kernels for 3%

profile of v15, /device:TPU:0, one launch (start us, length us, event | category | flops | bytes accessed | tf_op | source)
XLA Modules:
  0.0 32.8 jit_solution(3405875209664028629)
XLA Ops:
  0.6 0.0 copy-start.4
  0.6 3.1 %collective-permute-start = (f32[1,64,128]{2,1,0:T(8,128)}, f32[1,64,128]{2,1,0:T(8,128)S(1)}, u32[]{:S(2)}, u32[]{:S(2)}) collective-permute-start(f32[1,64,128]{2,1,0:T(8,128)} %param.5), channel_id=1, source_target_pairs={{0,8},{8,0},{16,24},{24,16},{1,9},{9,1},{17,25},{25,17},{2,10},{10... | collective-permute-start | bytes 98312 | tf_op jit(solution)/shard_map/ppermute | solution.py:320
  3.7 2.5 %collective-permute-start.2 = (f32[1,64,128]{2,1,0:T(8,128)}, f32[1,64,128]{2,1,0:T(8,128)S(1)}, u32[]{:S(2)}, u32[]{:S(2)}) collective-permute-start(f32[1,64,128]{2,1,0:T(8,128)} %param.5), channel_id=1, source_target_pairs={{0,24},{8,16},{16,8},{24,0},{1,25},{9,17},{17,9},{25,1},{2,26},{10... | collective-permute-start | bytes 98312 | tf_op jit(solution)/shard_map/ppermute | solution.py:320
  6.2 0.1 collective-permute-start.1
  6.3 0.0 collective-permute-done
  6.3 0.8 %constant_dynamic-update-slice_fusion.4 = f32[3,64,128]{2,1,0:T(8,128)S(1)} fusion(f32[1,64,128]{2,1,0:T(8,128)} %param.5), kind=kLoop, calls=%fused_computation.11 | loop fusion | bytes 65536
  7.1 0.0 copy-done.4
  7.1 0.0 copy-start.3
  7.1 0.7 %collective-permute-start.6 = (f32[3,64,128]{2,1,0:T(8,128)S(1)}, f32[3,64,128]{2,1,0:T(8,128)S(1)}, u32[]{:S(2)}, u32[]{:S(2)}) collective-permute-start(f32[3,64,128]{2,1,0:T(8,128)S(1)} %constant_dynamic-update-slice_fusion.3), channel_id=1, source_target_pairs={{1,2},{2,1},{5,6},{6,5},{9,10},{10,9},{13,14},{14,13},{17,18},{18,... | collective-permute-start | bytes 294920 | tf_op jit(solution)/shard_map/ppermute | solution.py:324
  7.8 4.3 %collective-permute-start.4 = (f32[3,64,128]{2,1,0:T(8,128)S(1)}, f32[3,64,128]{2,1,0:T(8,128)S(1)}, u32[]{:S(2)}, u32[]{:S(2)}) collective-permute-start(f32[3,64,128]{2,1,0:T(8,128)S(1)} %constant_dynamic-update-slice_fusion.3), channel_id=1, source_target_pairs={{0,1},{1,0},{2,3},{3,2},{4,5},{5,4},{6,7},{7,6},{8,9},{9,8},{10,11... | collective-permute-start | bytes 294920 | tf_op jit(solution)/shard_map/ppermute | solution.py:324
  12.1 0.0 collective-permute-done.2
  12.1 0.0 collective-permute-done.1
  12.1 0.0 copy-done.3
  12.1 1.0 %collective-permute-start.5 = (f32[4,64,128]{2,1,0:T(8,128)S(1)}, f32[4,64,128]{2,1,0:T(8,128)S(1)}, u32[]{:S(2)}, u32[]{:S(2)}) collective-permute-start(f32[4,64,128]{2,1,0:T(8,128)S(1)} %pad_maximum_fusion.3), channel_id=1, source_target_pairs={{0,2},{1,3},{2,0},{3,1},{4,6},{5,7},{6,4},{7,5},{8,10},{9,11},{10,... | collective-permute-start | bytes 393224 | tf_op jit(solution)/shard_map/ppermute | solution.py:324
  13.2 0.0 copy-start.5
  13.2 0.7 %collective-permute-start.7 = (f32[3,64,128]{2,1,0:T(8,128)S(1)}, f32[3,64,128]{2,1,0:T(8,128)S(1)}, u32[]{:S(2)}, u32[]{:S(2)}) collective-permute-start(f32[3,64,128]{2,1,0:T(8,128)S(1)} %constant_dynamic-update-slice_fusion), channel_id=1, source_target_pairs={{1,2},{2,1},{5,6},{6,5},{9,10},{10,9},{13,14},{14,13},{17,18},{18,... | collective-permute-start | bytes 294920 | tf_op jit(solution)/shard_map/ppermute | solution.py:324
  13.9 3.8 %collective-permute-start.3 = (f32[3,64,128]{2,1,0:T(8,128)S(1)}, f32[3,64,128]{2,1,0:T(8,128)S(1)}, u32[]{:S(2)}, u32[]{:S(2)}) collective-permute-start(f32[3,64,128]{2,1,0:T(8,128)S(1)} %constant_dynamic-update-slice_fusion), channel_id=1, source_target_pairs={{0,1},{1,0},{2,3},{3,2},{4,5},{5,4},{6,7},{7,6},{8,9},{9,8},{10,11... | collective-permute-start | bytes 294920 | tf_op jit(solution)/shard_map/ppermute | solution.py:324
  17.7 0.0 collective-permute-done.5
  17.7 0.0 copy-done.5
  17.7 0.1 slice_bitcast_fusion
  17.8 0.0 collective-permute-done.6
  17.8 0.0 collective-permute-done.4
  17.8 3.4 %collective-permute-done.3 = f32[3,64,128]{2,1,0:T(8,128)S(1)} collective-permute-done((f32[3,64,128]{2,1,0:T(8,128)S(1)}, f32[3,64,128]{2,1,0:T(8,128)S(1)}, u32[]{:S(2)}, u32[]{:S(2)}) %collective-permute-start.3) | collective-permute-done | bytes 98336 | tf_op jit(solution)/shard_map/ppermute | solution.py:324
  21.3 0.0 collective-permute-done.7
  21.3 0.1 collective-permute-start.9
  21.4 0.0 copy-start.2
  21.4 0.0 copy-start
  21.4 0.0 copy-start.1
  21.5 0.6 %collective-permute-start.8 = (f32[4,2,64,128]{3,2,1,0:T(8,128)S(1)}, f32[4,2,64,128]{3,2,1,0:T(8,128)S(1)}, u32[]{:S(2)}, u32[]{:S(2)}) collective-permute-start(f32[4,2,64,128]{3,2,1,0:T(8,128)S(1)} %pad_maximum_fusion.2), channel_id=1, source_target_pairs={{0,4},{4,0},{1,5},{5,1},{2,6},{6,2},{3,7},{7,3},{8,12},{12,8},{9,1... | collective-permute-start | bytes 786440 | tf_op jit(solution)/shard_map/ppermute | solution.py:328
  22.0 0.1 copy-done.2
  22.1 1.1 %shard_map.68 = (f32[4,2,128,128]{3,2,1,0:T(8,128)S(1)}, f32[5,4,64,128]{3,2,1,0:T(8,128)S(1)}, f32[5,4,64,128]{3,2,1,0:T(8,128)S(1)}) custom-call(s32[2,2]{1,0:T(2,128)S(1)} %copy-done.2, f32[4,3,64,128]{3,2,1,0:T(8,128)S(1)} %pad_maximum_fusion.near_own, f32[4,3,64,128]{3,2,1,0:T(8,128)S(1)} %pad_maximum_fusion.1.near_rest), custom_call_target="tpu_custom_call" | custom-call | flops 500000000 | bytes 1048576 | tf_op jit(solution)/shard_map/pallas_call | solution.py:364
  23.2 0.2 collective-permute-done.8.far_own
  23.4 0.0 collective-permute-done.9.far_rest
  23.5 0.0 copy-done
  23.5 0.0 copy-done.1
  23.5 7.3 %shard_map.69 = (f32[1,3,64,128]{3,2,1,0:T(8,128)S(1)}, f32[1,3,64,128]{3,2,1,0:T(8,128)S(1)}) custom-call(f32[4,2,128,128]{3,2,1,0:T(8,128)S(1)} %get-tuple-element.17.wave_ref, f32[5,4,64,128]{3,2,1,0:T(8,128)S(1)} %get-tuple-element.18.near_cos, f32[5,4,64,128]{3,2,1,0:T(8,128)S(1)} %get-tuple-element.19.near_sin, ...), custom_call_target="tpu_custom_call" | custom-call | tf_op jit(solution)/shard_map/pallas_call | solution.py:372
  30.8 0.3 collective-permute-start.10
  31.1 1.0 %collective-permute-done.10.received_ref = f32[1,3,64,128]{3,2,1,0:T(8,128)S(1)} collective-permute-done((f32[1,3,64,128]{3,2,1,0:T(8,128)S(1)}, f32[1,3,64,128]{3,2,1,0:T(8,128)S(1)}, u32[]{:S(2)}, u32[]{:S(2)}) %collective-permute-start.10) | collective-permute-done | bytes 98336 | tf_op jit(solution)/shard_map/ppermute | solution.py:328
  32.1 0.7 %shard_map.70 = (f32[1,64,128]{2,1,0:T(8,128)}, f32[2,1,2,64,128]{4,3,2,1,0:T(8,128)}) custom-call(f32[1,3,64,128]{3,2,1,0:T(8,128)S(1)} %get-tuple-element.20.mine_ref, f32[1,3,64,128]{3,2,1,0:T(8,128)S(1)} %collective-permute-done.10.received_ref), custom_call_target="tpu_custom_call" | custom-call | tf_op jit(solution)/shard_map/pallas_call | solution.py:387
  (9 shorter events, 0.1 us)
Async XLA Ops:
  0.6 6.5 %copy-start.4 = (f32[2,64,128]{2,1,0:T(8,128)S(1)}, f32[2,64,128]{2,1,0:T(8,128)}, u32[]{:S(2)}) copy-start(f32[2,64,128]{2,1,0:T(8,128)} %param.7) | copy-start | bytes 196612
  0.6 5.7 %collective-permute-start = (f32[1,64,128]{2,1,0:T(8,128)}, f32[1,64,128]{2,1,0:T(8,128)S(1)}, u32[]{:S(2)}, u32[]{:S(2)}) collective-permute-start(f32[1,64,128]{2,1,0:T(8,128)} %param.5), channel_id=1, source_target_pairs={{0,8},{8,0},{16,24},{24,16},{1,9},{9,1},{17,25},{25,17},{2,10},{10... | collective-permute-start | bytes 98312 | tf_op jit(solution)/shard_map/ppermute | solution.py:320
  3.7 8.4 %collective-permute-start.2 = (f32[1,64,128]{2,1,0:T(8,128)}, f32[1,64,128]{2,1,0:T(8,128)S(1)}, u32[]{:S(2)}, u32[]{:S(2)}) collective-permute-start(f32[1,64,128]{2,1,0:T(8,128)} %param.5), channel_id=1, source_target_pairs={{0,24},{8,16},{16,8},{24,0},{1,25},{9,17},{17,9},{25,1},{2,26},{10... | collective-permute-start | bytes 98312 | tf_op jit(solution)/shard_map/ppermute | solution.py:320
  6.2 5.9 %collective-permute-start.1 = (f32[1,64,128]{2,1,0:T(8,128)}, f32[1,64,128]{2,1,0:T(8,128)S(1)}, u32[]{:S(2)}, u32[]{:S(2)}) collective-permute-start(f32[1,64,128]{2,1,0:T(8,128)} %param.5), channel_id=1, source_target_pairs={{0,16},{8,24},{16,0},{24,8},{1,17},{9,25},{17,1},{25,9},{2,18},{10... | collective-permute-start | bytes 98312 | tf_op jit(solution)/shard_map/ppermute | solution.py:320
  7.1 5.0 %copy-start.3 = (f32[1,64,128]{2,1,0:T(8,128)S(1)}, f32[1,64,128]{2,1,0:T(8,128)}, u32[]{:S(2)}) copy-start(f32[1,64,128]{2,1,0:T(8,128)} %param.5) | copy-start | bytes 98308
  7.1 10.6 %collective-permute-start.6 = (f32[3,64,128]{2,1,0:T(8,128)S(1)}, f32[3,64,128]{2,1,0:T(8,128)S(1)}, u32[]{:S(2)}, u32[]{:S(2)}) collective-permute-start(f32[3,64,128]{2,1,0:T(8,128)S(1)} %constant_dynamic-update-slice_fusion.3), channel_id=1, source_target_pairs={{1,2},{2,1},{5,6},{6,5},{9,10},{10,9},{13,14},{14,13},{17,18},{18,... | collective-permute-start | bytes 294920 | tf_op jit(solution)/shard_map/ppermute | solution.py:324
  7.8 10.0 %collective-permute-start.4 = (f32[3,64,128]{2,1,0:T(8,128)S(1)}, f32[3,64,128]{2,1,0:T(8,128)S(1)}, u32[]{:S(2)}, u32[]{:S(2)}) collective-permute-start(f32[3,64,128]{2,1,0:T(8,128)S(1)} %constant_dynamic-update-slice_fusion.3), channel_id=1, source_target_pairs={{0,1},{1,0},{2,3},{3,2},{4,5},{5,4},{6,7},{7,6},{8,9},{9,8},{10,11... | collective-permute-start | bytes 294920 | tf_op jit(solution)/shard_map/ppermute | solution.py:324
  12.1 5.6 %collective-permute-start.5 = (f32[4,64,128]{2,1,0:T(8,128)S(1)}, f32[4,64,128]{2,1,0:T(8,128)S(1)}, u32[]{:S(2)}, u32[]{:S(2)}) collective-permute-start(f32[4,64,128]{2,1,0:T(8,128)S(1)} %pad_maximum_fusion.3), channel_id=1, source_target_pairs={{0,2},{1,3},{2,0},{3,1},{4,6},{5,7},{6,4},{7,5},{8,10},{9,11},{10,... | collective-permute-start | bytes 393224 | tf_op jit(solution)/shard_map/ppermute | solution.py:324
  13.2 4.5 %copy-start.5 = (pred[3]{0:T(512)(128)(4,1)S(1)}, pred[3]{0:T(512)(128)(4,1)}, u32[]{:S(2)}) copy-start(pred[3]{0:T(512)(128)(4,1)} %constant.6.clone.1) | copy-start | bytes 13
  13.2 8.1 %collective-permute-start.7 = (f32[3,64,128]{2,1,0:T(8,128)S(1)}, f32[3,64,128]{2,1,0:T(8,128)S(1)}, u32[]{:S(2)}, u32[]{:S(2)}) collective-permute-start(f32[3,64,128]{2,1,0:T(8,128)S(1)} %constant_dynamic-update-slice_fusion), channel_id=1, source_target_pairs={{1,2},{2,1},{5,6},{6,5},{9,10},{10,9},{13,14},{14,13},{17,18},{18,... | collective-permute-start | bytes 294920 | tf_op jit(solution)/shard_map/ppermute | solution.py:324
  13.9 7.4 %collective-permute-start.3 = (f32[3,64,128]{2,1,0:T(8,128)S(1)}, f32[3,64,128]{2,1,0:T(8,128)S(1)}, u32[]{:S(2)}, u32[]{:S(2)}) collective-permute-start(f32[3,64,128]{2,1,0:T(8,128)S(1)} %constant_dynamic-update-slice_fusion), channel_id=1, source_target_pairs={{0,1},{1,0},{2,3},{3,2},{4,5},{5,4},{6,7},{7,6},{8,9},{9,8},{10,11... | collective-permute-start | bytes 294920 | tf_op jit(solution)/shard_map/ppermute | solution.py:324
  21.3 2.2 %collective-permute-start.9 = (f32[4,3,64,128]{3,2,1,0:T(8,128)S(1)}, f32[4,3,64,128]{3,2,1,0:T(8,128)S(1)}, u32[]{:S(2)}, u32[]{:S(2)}) collective-permute-start(f32[4,3,64,128]{3,2,1,0:T(8,128)S(1)} %pad_maximum_fusion.1.near_rest), channel_id=1, source_target_pairs={{0,4},{4,0},{1,5},{5,1},{2,6},{6,2},{3,7},{7,3},{8,12},{12,8},{9,1... | collective-permute-start | bytes 1179656 | tf_op jit(solution)/shard_map/ppermute | solution.py:328
  21.4 0.7 %copy-start.2 = (s32[2,2]{1,0:T(2,128)S(1)}, s32[2,2]{1,0:T(2,128)}, u32[]{:S(2)}) copy-start(s32[2,2]{1,0:T(2,128)} %tilt_ref.1) | copy-start | bytes 52
  21.4 2.0 %copy-start = (bf16[512,512]{1,0:T(8,128)(2,1)S(1)}, bf16[512,512]{1,0:T(8,128)(2,1)}, u32[]{:S(2)}) copy-start(bf16[512,512]{1,0:T(8,128)(2,1)} %constant.22.clone.col_ref) | copy-start | bytes 1572868
  21.4 2.0 %copy-start.1 = (bf16[2,256,512]{2,1,0:T(8,128)(2,1)S(1)}, bf16[2,256,512]{2,1,0:T(8,128)(2,1)}, u32[]{:S(2)}) copy-start(bf16[2,256,512]{2,1,0:T(8,128)(2,1)} %constant.21.clone.row_ref) | copy-start | bytes 1572868
  21.5 2.0 %collective-permute-start.8 = (f32[4,2,64,128]{3,2,1,0:T(8,128)S(1)}, f32[4,2,64,128]{3,2,1,0:T(8,128)S(1)}, u32[]{:S(2)}, u32[]{:S(2)}) collective-permute-start(f32[4,2,64,128]{3,2,1,0:T(8,128)S(1)} %pad_maximum_fusion.2), channel_id=1, source_target_pairs={{0,4},{4,0},{1,5},{5,1},{2,6},{6,2},{3,7},{7,3},{8,12},{12,8},{9,1... | collective-permute-start | bytes 786440 | tf_op jit(solution)/shard_map/ppermute | solution.py:328
  30.8 1.4 %collective-permute-start.10 = (f32[1,3,64,128]{3,2,1,0:T(8,128)S(1)}, f32[1,3,64,128]{3,2,1,0:T(8,128)S(1)}, u32[]{:S(2)}, u32[]{:S(2)}) collective-permute-start(f32[1,3,64,128]{3,2,1,0:T(8,128)S(1)} %get-tuple-element.21), channel_id=1, source_target_pairs={{0,4},{4,0},{1,5},{5,1},{2,6},{6,2},{3,7},{7,3},{8,12},{12,8},{9,1... | collective-permute-start | bytes 294920 | tf_op jit(solution)/shard_map/ppermute | solution.py:328

commit v16 on v15

--- a/solution.py
+++ b/solution.py
@@ -348,12 +348,11 @@
     other_depths = jnp.concatenate(other_depths, axis=0)
     packet = jnp.concatenate([slab, measured], axis=0)
     by_one, by_two, corner = [(i, i ^ 1) for i in range(4)], [(i, i ^ 2) for i in range(4)], [(1, 2), (2, 1)]
-    packet_near, packet_corner = exchange(packet, by_one), exchange(packet, corner)
-    whole_column = exchange(jnp.concatenate([slab, other_depths], axis=0), by_two)
-    packet_next = jnp.concatenate([whole_column[:1], jnp.zeros_like(measured)], axis=0)
+    packet_near, packet_next = exchange(packet, by_one), exchange(packet, by_two)
+    arriving = [exchange(other_depths, pairs) for pairs in (by_one, by_two, corner)]
+    packet_near, packet_next = lax.optimization_barrier((packet_near, packet_next))
+    packet_corner = exchange(packet_next, [(0, 1), (3, 2)])
     near_own = jnp.stack([packet, packet_near, packet_next, packet_corner])
-    arriving = [exchange(other_depths, by_one), whole_column[1:], exchange(other_depths, corner)]
-    arriving[0], near_own = lax.optimization_barrier((arriving[0], near_own))
     near_rest = jnp.stack([other_depths] + arriving)
     wanted = lax.dynamic_slice_in_dim(near_own, 2 - core, 1, 1)
     far_own = swap_cores(jnp.concatenate([near_own[:, :1], wanted], axis=1))

time: 33.1 us -> 34.2 us (1.033)
  starting transfers between devices: 17.1 us -> 17.8 us
  local copies, waits for them, and re-layouts: 0.92 us -> 1.39 us
    ppermute x5 -> x6, starting transfers between devices: 10.5 us -> 11.9 us  [exchange(): return lax.ppermute(value, 'col', pairs)]
    ppermute x3, waiting for transfers between devices: 0.01 us -> 1.38 us  [spread(): lax.ppermute(shard, axis, [(i, i ^ bits) for i in range(size)])]
    ppermute x5 -> x6, waiting for transfers between devices: 3.43 us -> 2.07 us  [exchange(): return lax.ppermute(value, 'col', pairs)]
    ppermute x3, starting transfers between devices: 0.95 us -> 0.21 us  [swap_cores(): return lax.ppermute(value, 'row', [(0, 1), (1, 0)])]
    unnamed x15 -> x11, local copies, waits for them, and re-layouts: 0.89 us -> 1.36 us
  transfers between devices with their start and end apart: 11 -> 12, of which waited for: 3 -> 4; matrix products, arithmetic and copies ran while one was open for 3% -> 3% of each run, Pallas kernels for 3% -> 3%
where the time goes in v16:
time: 34.2 us; the launch traced here: 33.9 us
  starting transfers between devices  17.8 us (52%)
  Pallas kernels  9.12 us (27%)
  waiting for transfers between devices  4.74 us (14%)
  local copies, waits for them, and re-layouts  1.39 us (4%)
  between operations  0.8 us (2%)
    ppermute x6, starting transfers between devices, exchange(): return lax.ppermute(value, 'col', pairs)  11.9 us
    pallas_call x1, Pallas kernels, whole_field_body(): pl.pallas_call(wave_kernel, out_shape=(array(1, 3, tile_r, tile_c),) * 2,...  7.31 us
    ppermute x3, starting transfers between devices, spread(): lax.ppermute(shard, axis, [(i, i ^ bits) for i in range(size)])  5.68 us
    ppermute x6, waiting for transfers between devices, exchange(): return lax.ppermute(value, 'col', pairs)  2.07 us
    ppermute x3, waiting for transfers between devices, spread(): lax.ppermute(shard, axis, [(i, i ^ bits) for i in range(size)])  1.38 us
    unnamed x11, local copies, waits for them, and re-layouts  1.36 us
    ppermute x3, waiting for transfers between devices, swap_cores(): return lax.ppermute(value, 'row', [(0, 1), (1, 0)])  1.29 us
    pallas_call x1, Pallas kernels, whole_field_body(): pl.pallas_call(prepare_kernel, out_shape=(array(*field), array(*half_scre...  1.13 us
  transfers between devices with their start and end apart: 12, of which 4 were waited for; matrix products, arithmetic and copies ran while one was open for 3% of the time, Pallas kernels for 3%

profile of v16, /device:TPU:0, one launch (start us, length us, event | category | flops | bytes accessed | tf_op | source)
XLA Modules:
  0.0 33.9 jit_solution(13497439885691718463)
XLA Ops:
  0.6 0.0 copy-start.3
  0.6 3.1 %collective-permute-start = (f32[1,64,128]{2,1,0:T(8,128)}, f32[1,64,128]{2,1,0:T(8,128)S(1)}, u32[]{:S(2)}, u32[]{:S(2)}) collective-permute-start(f32[1,64,128]{2,1,0:T(8,128)} %param.5), channel_id=1, source_target_pairs={{0,8},{8,0},{16,24},{24,16},{1,9},{9,1},{17,25},{25,17},{2,10},{10... | collective-permute-start | bytes 98312 | tf_op jit(solution)/shard_map/ppermute | solution.py:320
  3.7 2.5 %collective-permute-start.5 = (f32[1,64,128]{2,1,0:T(8,128)}, f32[1,64,128]{2,1,0:T(8,128)S(1)}, u32[]{:S(2)}, u32[]{:S(2)}) collective-permute-start(f32[1,64,128]{2,1,0:T(8,128)} %param.5), channel_id=1, source_target_pairs={{0,24},{8,16},{16,8},{24,0},{1,25},{9,17},{17,9},{25,1},{2,26},{10... | collective-permute-start | bytes 98312 | tf_op jit(solution)/shard_map/ppermute | solution.py:320
  6.2 0.1 collective-permute-start.4
  6.3 0.0 collective-permute-done
  6.3 0.8 %constant_dynamic-update-slice_fusion.1 = f32[3,64,128]{2,1,0:T(8,128)S(1)} fusion(f32[1,64,128]{2,1,0:T(8,128)} %param.5), kind=kLoop, calls=%fused_computation.4 | loop fusion | bytes 65536
  7.1 0.0 copy-done.3
  7.1 1.6 %collective-permute-start.2 = (f32[3,64,128]{2,1,0:T(8,128)S(1)}, f32[3,64,128]{2,1,0:T(8,128)S(1)}, u32[]{:S(2)}, u32[]{:S(2)}) collective-permute-start(f32[3,64,128]{2,1,0:T(8,128)S(1)} %constant_dynamic-update-slice_fusion), channel_id=1, source_target_pairs={{0,2},{1,3},{2,0},{3,1},{4,6},{5,7},{6,4},{7,5},{8,10},{9,11},{10,... | collective-permute-start | bytes 294920 | tf_op jit(solution)/shard_map/ppermute | solution.py:324
  8.7 1.5 %collective-permute-start.1 = (f32[3,64,128]{2,1,0:T(8,128)S(1)}, f32[3,64,128]{2,1,0:T(8,128)S(1)}, u32[]{:S(2)}, u32[]{:S(2)}) collective-permute-start(f32[3,64,128]{2,1,0:T(8,128)S(1)} %constant_dynamic-update-slice_fusion), channel_id=1, source_target_pairs={{0,1},{1,0},{2,3},{3,2},{4,5},{5,4},{6,7},{7,6},{8,9},{9,8},{10,11... | collective-permute-start | bytes 294920 | tf_op jit(solution)/shard_map/ppermute | solution.py:324
  10.2 1.4 %collective-permute-done.4 = f32[1,64,128]{2,1,0:T(8,128)S(1)} collective-permute-done((f32[1,64,128]{2,1,0:T(8,128)}, f32[1,64,128]{2,1,0:T(8,128)S(1)}, u32[]{:S(2)}, u32[]{:S(2)}) %collective-permute-start.4) | collective-permute-done | bytes 32800 | tf_op jit(solution)/shard_map/ppermute | solution.py:320
  11.6 0.0 collective-permute-done.5
  11.6 0.7 %collective-permute-start.8 = (f32[3,64,128]{2,1,0:T(8,128)S(1)}, f32[3,64,128]{2,1,0:T(8,128)S(1)}, u32[]{:S(2)}, u32[]{:S(2)}) collective-permute-start(f32[3,64,128]{2,1,0:T(8,128)S(1)} %constant_dynamic-update-slice_fusion.2), channel_id=1, source_target_pairs={{1,2},{2,1},{5,6},{6,5},{9,10},{10,9},{13,14},{14,13},{17,18},{18,... | collective-permute-start | bytes 294920 | tf_op jit(solution)/shard_map/ppermute | solution.py:324
  12.3 4.3 %collective-permute-start.7 = (f32[3,64,128]{2,1,0:T(8,128)S(1)}, f32[3,64,128]{2,1,0:T(8,128)S(1)}, u32[]{:S(2)}, u32[]{:S(2)}) collective-permute-start(f32[3,64,128]{2,1,0:T(8,128)S(1)} %constant_dynamic-update-slice_fusion.2), channel_id=1, source_target_pairs={{0,2},{1,3},{2,0},{3,1},{4,6},{5,7},{6,4},{7,5},{8,10},{9,11},{10,... | collective-permute-start | bytes 294920 | tf_op jit(solution)/shard_map/ppermute | solution.py:324
  16.5 0.1 collective-permute-start.6
  16.6 0.0 collective-permute-done.2
  16.6 0.0 collective-permute-done.1
  16.6 3.8 %collective-permute-start.3 = (f32[3,64,128]{2,1,0:T(8,128)S(1)}, f32[3,64,128]{2,1,0:T(8,128)S(1)}, u32[]{:S(2)}, u32[]{:S(2)}) collective-permute-start(f32[3,64,128]{2,1,0:T(8,128)S(1)} %collective-permute-done.2), channel_id=1, source_target_pairs={{0,1},{3,2},{4,5},{7,6},{8,9},{11,10},{12,13},{15,14},{16,17},{19,... | collective-permute-start | bytes 294920 | tf_op jit(solution)/shard_map/ppermute | solution.py:324
  20.5 0.0 collective-permute-done.8
  20.5 0.0 collective-permute-done.7
  20.5 0.7 %collective-permute-done.6 = f32[3,64,128]{2,1,0:T(8,128)S(1)} collective-permute-done((f32[3,64,128]{2,1,0:T(8,128)S(1)}, f32[3,64,128]{2,1,0:T(8,128)S(1)}, u32[]{:S(2)}, u32[]{:S(2)}) %collective-permute-start.6) | collective-permute-done | bytes 98336 | tf_op jit(solution)/shard_map/ppermute | solution.py:324
  21.2 0.1 collective-permute-start.10
  21.3 1.4 %collective-permute-done.3 = f32[3,64,128]{2,1,0:T(8,128)S(1)} collective-permute-done((f32[3,64,128]{2,1,0:T(8,128)S(1)}, f32[3,64,128]{2,1,0:T(8,128)S(1)}, u32[]{:S(2)}, u32[]{:S(2)}) %collective-permute-start.3) | collective-permute-done | bytes 98336 | tf_op jit(solution)/shard_map/ppermute | solution.py:324
  22.7 0.0 copy-start.2
  22.8 0.0 copy-start
  22.8 0.0 copy-start.1
  22.8 0.1 collective-permute-start.9
  22.9 0.5 %copy-done.2 = s32[2,2]{1,0:T(2,128)S(1)} copy-done((s32[2,2]{1,0:T(2,128)S(1)}, s32[2,2]{1,0:T(2,128)}, u32[]{:S(2)}) %copy-start.2) | copy-done | bytes 40
  23.4 1.1 %shard_map.68 = (f32[4,2,128,128]{3,2,1,0:T(8,128)S(1)}, f32[5,4,64,128]{3,2,1,0:T(8,128)S(1)}, f32[5,4,64,128]{3,2,1,0:T(8,128)S(1)}) custom-call(s32[2,2]{1,0:T(2,128)S(1)} %copy-done.2, f32[4,3,64,128]{3,2,1,0:T(8,128)S(1)} %pad_maximum_fusion.near_own, f32[4,3,64,128]{3,2,1,0:T(8,128)S(1)} %pad_maximum_fusion.1.near_rest), custom_call_target="tpu_custom_call" | custom-call | flops 500000000 | bytes 1048576 | tf_op jit(solution)/shard_map/pallas_call | solution.py:363
  24.5 0.0 collective-permute-done.9.far_own
  24.5 0.0 collective-permute-done.10.far_rest
  24.6 0.0 copy-done
  24.6 0.0 copy-done.1
  24.6 7.3 %shard_map.69 = (f32[1,3,64,128]{3,2,1,0:T(8,128)S(1)}, f32[1,3,64,128]{3,2,1,0:T(8,128)S(1)}) custom-call(f32[4,2,128,128]{3,2,1,0:T(8,128)S(1)} %get-tuple-element.17.wave_ref, f32[5,4,64,128]{3,2,1,0:T(8,128)S(1)} %get-tuple-element.18.near_cos, f32[5,4,64,128]{3,2,1,0:T(8,128)S(1)} %get-tuple-element.19.near_sin, ...), custom_call_target="tpu_custom_call" | custom-call | tf_op jit(solution)/shard_map/pallas_call | solution.py:371
  31.9 0.1 collective-permute-start.11
  32.0 1.3 %collective-permute-done.11.received_ref = f32[1,3,64,128]{3,2,1,0:T(8,128)S(1)} collective-permute-done((f32[1,3,64,128]{3,2,1,0:T(8,128)S(1)}, f32[1,3,64,128]{3,2,1,0:T(8,128)S(1)}, u32[]{:S(2)}, u32[]{:S(2)}) %collective-permute-start.11) | collective-permute-done | bytes 98336 | tf_op jit(solution)/shard_map/ppermute | solution.py:328
  33.3 0.7 %shard_map.70 = (f32[1,64,128]{2,1,0:T(8,128)}, f32[2,1,2,64,128]{4,3,2,1,0:T(8,128)}) custom-call(f32[1,3,64,128]{3,2,1,0:T(8,128)S(1)} %get-tuple-element.20.mine_ref, f32[1,3,64,128]{3,2,1,0:T(8,128)S(1)} %collective-permute-done.11.received_ref), custom_call_target="tpu_custom_call" | custom-call | tf_op jit(solution)/shard_map/pallas_call | solution.py:386
  (8 shorter events, 0.1 us)
Async XLA Ops:
  0.6 6.5 %copy-start.3 = (f32[2,64,128]{2,1,0:T(8,128)S(1)}, f32[2,64,128]{2,1,0:T(8,128)}, u32[]{:S(2)}) copy-start(f32[2,64,128]{2,1,0:T(8,128)} %param.7) | copy-start | bytes 196612
  0.6 5.7 %collective-permute-start = (f32[1,64,128]{2,1,0:T(8,128)}, f32[1,64,128]{2,1,0:T(8,128)S(1)}, u32[]{:S(2)}, u32[]{:S(2)}) collective-permute-start(f32[1,64,128]{2,1,0:T(8,128)} %param.5), channel_id=1, source_target_pairs={{0,8},{8,0},{16,24},{24,16},{1,9},{9,1},{17,25},{25,17},{2,10},{10... | collective-permute-start | bytes 98312 | tf_op jit(solution)/shard_map/ppermute | solution.py:320
  3.7 7.9 %collective-permute-start.5 = (f32[1,64,128]{2,1,0:T(8,128)}, f32[1,64,128]{2,1,0:T(8,128)S(1)}, u32[]{:S(2)}, u32[]{:S(2)}) collective-permute-start(f32[1,64,128]{2,1,0:T(8,128)} %param.5), channel_id=1, source_target_pairs={{0,24},{8,16},{16,8},{24,0},{1,25},{9,17},{17,9},{25,1},{2,26},{10... | collective-permute-start | bytes 98312 | tf_op jit(solution)/shard_map/ppermute | solution.py:320
  6.2 5.4 %collective-permute-start.4 = (f32[1,64,128]{2,1,0:T(8,128)}, f32[1,64,128]{2,1,0:T(8,128)S(1)}, u32[]{:S(2)}, u32[]{:S(2)}) collective-permute-start(f32[1,64,128]{2,1,0:T(8,128)} %param.5), channel_id=1, source_target_pairs={{0,16},{8,24},{16,0},{24,8},{1,17},{9,25},{17,1},{25,9},{2,18},{10... | collective-permute-start | bytes 98312 | tf_op jit(solution)/shard_map/ppermute | solution.py:320
  7.1 9.5 %collective-permute-start.2 = (f32[3,64,128]{2,1,0:T(8,128)S(1)}, f32[3,64,128]{2,1,0:T(8,128)S(1)}, u32[]{:S(2)}, u32[]{:S(2)}) collective-permute-start(f32[3,64,128]{2,1,0:T(8,128)S(1)} %constant_dynamic-update-slice_fusion), channel_id=1, source_target_pairs={{0,2},{1,3},{2,0},{3,1},{4,6},{5,7},{6,4},{7,5},{8,10},{9,11},{10,... | collective-permute-start | bytes 294920 | tf_op jit(solution)/shard_map/ppermute | solution.py:324
  8.7 7.9 %collective-permute-start.1 = (f32[3,64,128]{2,1,0:T(8,128)S(1)}, f32[3,64,128]{2,1,0:T(8,128)S(1)}, u32[]{:S(2)}, u32[]{:S(2)}) collective-permute-start(f32[3,64,128]{2,1,0:T(8,128)S(1)} %constant_dynamic-update-slice_fusion), channel_id=1, source_target_pairs={{0,1},{1,0},{2,3},{3,2},{4,5},{5,4},{6,7},{7,6},{8,9},{9,8},{10,11... | collective-permute-start | bytes 294920 | tf_op jit(solution)/shard_map/ppermute | solution.py:324
  11.6 8.9 %collective-permute-start.8 = (f32[3,64,128]{2,1,0:T(8,128)S(1)}, f32[3,64,128]{2,1,0:T(8,128)S(1)}, u32[]{:S(2)}, u32[]{:S(2)}) collective-permute-start(f32[3,64,128]{2,1,0:T(8,128)S(1)} %constant_dynamic-update-slice_fusion.2), channel_id=1, source_target_pairs={{1,2},{2,1},{5,6},{6,5},{9,10},{10,9},{13,14},{14,13},{17,18},{18,... | collective-permute-start | bytes 294920 | tf_op jit(solution)/shard_map/ppermute | solution.py:324
  12.3 8.2 %collective-permute-start.7 = (f32[3,64,128]{2,1,0:T(8,128)S(1)}, f32[3,64,128]{2,1,0:T(8,128)S(1)}, u32[]{:S(2)}, u32[]{:S(2)}) collective-permute-start(f32[3,64,128]{2,1,0:T(8,128)S(1)} %constant_dynamic-update-slice_fusion.2), channel_id=1, source_target_pairs={{0,2},{1,3},{2,0},{3,1},{4,6},{5,7},{6,4},{7,5},{8,10},{9,11},{10,... | collective-permute-start | bytes 294920 | tf_op jit(solution)/shard_map/ppermute | solution.py:324
  16.5 4.6 %collective-permute-start.6 = (f32[3,64,128]{2,1,0:T(8,128)S(1)}, f32[3,64,128]{2,1,0:T(8,128)S(1)}, u32[]{:S(2)}, u32[]{:S(2)}) collective-permute-start(f32[3,64,128]{2,1,0:T(8,128)S(1)} %constant_dynamic-update-slice_fusion.2), channel_id=1, source_target_pairs={{0,1},{1,0},{2,3},{3,2},{4,5},{5,4},{6,7},{7,6},{8,9},{9,8},{10,11... | collective-permute-start | bytes 294920 | tf_op jit(solution)/shard_map/ppermute | solution.py:324
  16.6 6.0 %collective-permute-start.3 = (f32[3,64,128]{2,1,0:T(8,128)S(1)}, f32[3,64,128]{2,1,0:T(8,128)S(1)}, u32[]{:S(2)}, u32[]{:S(2)}) collective-permute-start(f32[3,64,128]{2,1,0:T(8,128)S(1)} %collective-permute-done.2), channel_id=1, source_target_pairs={{0,1},{3,2},{4,5},{7,6},{8,9},{11,10},{12,13},{15,14},{16,17},{19,... | collective-permute-start | bytes 294920 | tf_op jit(solution)/shard_map/ppermute | solution.py:324
  21.2 3.4 %collective-permute-start.10 = (f32[4,3,64,128]{3,2,1,0:T(8,128)S(1)}, f32[4,3,64,128]{3,2,1,0:T(8,128)S(1)}, u32[]{:S(2)}, u32[]{:S(2)}) collective-permute-start(f32[4,3,64,128]{3,2,1,0:T(8,128)S(1)} %pad_maximum_fusion.1.near_rest), channel_id=1, source_target_pairs={{0,4},{4,0},{1,5},{5,1},{2,6},{6,2},{3,7},{7,3},{8,12},{12,8},{9,1... | collective-permute-start | bytes 1179656 | tf_op jit(solution)/shard_map/ppermute | solution.py:328
  22.7 0.7 %copy-start.2 = (s32[2,2]{1,0:T(2,128)S(1)}, s32[2,2]{1,0:T(2,128)}, u32[]{:S(2)}) copy-start(s32[2,2]{1,0:T(2,128)} %tilt_ref.1) | copy-start | bytes 52
  22.8 1.8 %copy-start = (bf16[512,512]{1,0:T(8,128)(2,1)S(1)}, bf16[512,512]{1,0:T(8,128)(2,1)}, u32[]{:S(2)}) copy-start(bf16[512,512]{1,0:T(8,128)(2,1)} %constant.18.clone.col_ref) | copy-start | bytes 1572868
  22.8 1.8 %copy-start.1 = (bf16[2,256,512]{2,1,0:T(8,128)(2,1)S(1)}, bf16[2,256,512]{2,1,0:T(8,128)(2,1)}, u32[]{:S(2)}) copy-start(bf16[2,256,512]{2,1,0:T(8,128)(2,1)} %constant.17.clone.row_ref) | copy-start | bytes 1572868
  22.8 1.8 %collective-permute-start.9 = (f32[4,2,64,128]{3,2,1,0:T(8,128)S(1)}, f32[4,2,64,128]{3,2,1,0:T(8,128)S(1)}, u32[]{:S(2)}, u32[]{:S(2)}) collective-permute-start(f32[4,2,64,128]{3,2,1,0:T(8,128)S(1)} %pad_maximum_fusion.2), channel_id=1, source_target_pairs={{0,4},{4,0},{1,5},{5,1},{2,6},{6,2},{3,7},{7,3},{8,12},{12,8},{9,1... | collective-permute-start | bytes 786440 | tf_op jit(solution)/shard_map/ppermute | solution.py:328
  31.9 1.4 %collective-permute-start.11 = (f32[1,3,64,128]{3,2,1,0:T(8,128)S(1)}, f32[1,3,64,128]{3,2,1,0:T(8,128)S(1)}, u32[]{:S(2)}, u32[]{:S(2)}) collective-permute-start(f32[1,3,64,128]{3,2,1,0:T(8,128)S(1)} %get-tuple-element.21), channel_id=1, source_target_pairs={{0,4},{4,0},{1,5},{5,1},{2,6},{6,2},{3,7},{7,3},{8,12},{12,8},{9,1... | collective-permute-start | bytes 294920 | tf_op jit(solution)/shard_map/ppermute | solution.py:328

commit v17 on v13

--- a/solution.py
+++ b/solution.py
@@ -178,21 +178,13 @@
         wave_ref[place, 0], wave_ref[place, 1] = wave
 
 
-def prepare_kernel(tilt_ref, near_own, near_rest, wave_ref, cos_ref, sin_ref):
+def first_kernel(tilt_ref, near_own, far_own, wave_ref, measured_ref, cos_ref, sin_ref):
     blocks, _, height, _ = wave_ref.shape
-    count = cos_ref.shape[0] - 1
-    core, own_section, own_place = lax.axis_index("row"), lax.axis_index("depth"), lax.axis_index("col")
-
-    def screens(col, carry):
+    core, own_place = lax.axis_index("row"), lax.axis_index("col")
+    for col in range(blocks):
         held = col ^ own_place
-        for bits in range(count):
-            angle = near_own[held, 0] if bits == 0 else near_rest[held, bits - 1]
-            cos_ref[bits ^ own_section, col], sin_ref[bits ^ own_section, col] = cos_sin(angle)
-        return carry
-
-    lax.fori_loop(0, blocks, screens, 0)
-    cos_ref[count] = jnp.ones(cos_ref.shape[1:], jnp.float32)
-    sin_ref[count] = jnp.zeros(cos_ref.shape[1:], jnp.float32)
+        measured_ref[col] = jnp.concatenate([near_own[held, 1 + core], far_own[held, 1]], axis=0)
+        cos_ref[col], sin_ref[col] = cos_sin(near_own[held, 0])
 
     def cycles(number, position, extent):
         fraction = (number * position).astype(jnp.float32) / extent
@@ -212,8 +204,25 @@
         wave_ref[block, 1] = row_sin * col_cos + row_cos * col_sin
 
 
+def second_kernel(near_rest, own_cos, own_sin, cos_ref, sin_ref):
+    blocks = own_cos.shape[0]
+    count = cos_ref.shape[0] - 1
+    own_section, own_place = lax.axis_index("depth"), lax.axis_index("col")
+
+    def screens(col, carry):
+        held = col ^ own_place
+        cos_ref[own_section, col], sin_ref[own_section, col] = own_cos[col], own_sin[col]
+        for bits in range(1, count):
+            cos_ref[bits ^ own_section, col], sin_ref[bits ^ own_section, col] = cos_sin(near_rest[held, bits - 1])
+        return carry
+
+    lax.fori_loop(0, blocks, screens, 0)
+    cos_ref[count] = jnp.ones(cos_ref.shape[1:], jnp.float32)
+    sin_ref[count] = jnp.zeros(cos_ref.shape[1:], jnp.float32)
+
+
 def wave_kernel(
-    wave_ref, near_cos, near_sin, near_own, far_own, far_rest, row_ref, col_ref,
+    wave_ref, near_cos, near_sin, measured_ref, far_own, far_rest, row_ref, col_ref,
     mine_ref, theirs_ref, far_cos, far_sin, kept_ref, moved_ref, left_ref, grad_ref, even_edge, odd_edge,
 ):
     blocks, _, height, _ = wave_ref.shape
@@ -256,10 +265,8 @@
     waves = []
     for place in range(window):
         block = window_start + place
-        held = block ^ own_place
-        measured = jnp.concatenate([near_own[held, 1 + core], far_own[held, 1]], axis=0)
         real, imag = kept_ref[block, 0], kept_ref[block, 1]
-        misfit = 2.0 * (real * real + imag * imag - measured)
+        misfit = 2.0 * (real * real + imag * imag - measured_ref[block])
         waves.append((misfit * real, -misfit * imag))
 
     for tick in range(count - 1):
@@ -360,7 +367,7 @@
             near_own.append(jnp.concatenate([arrived, jnp.zeros_like(measured)], axis=0))
     near_own = jnp.stack(near_own)
     arriving = spread(other_depths, "col", 2)
-    arriving[0], near_own = lax.optimization_barrier((arriving[0], near_own))
+    arriving[2], near_own = lax.optimization_barrier((arriving[2], near_own))
     near_rest = jnp.stack([other_depths] + arriving)
     wanted = lax.dynamic_slice_in_dim(near_own, 2 - core, 1, 1)
     far_own = swap_cores(jnp.concatenate([near_own[:, :1], wanted], axis=1))
@@ -368,14 +375,22 @@
 
     half_screens = (count + 1, blocks, tile_r, tile_c)
     field = (blocks, 2, height, tile_c)
-    wave, near_cos, near_sin = pl.pallas_call(
-        prepare_kernel,
-        out_shape=(array(*field), array(*half_screens), array(*half_screens)),
+    wave, measured, own_cos, own_sin = pl.pallas_call(
+        first_kernel,
+        out_shape=(array(*field), array(blocks, height, tile_c)) + (array(blocks, tile_r, tile_c),) * 2,
         in_specs=[smem, vmem, vmem],
-        out_specs=(vmem,) * 3,
+        out_specs=(vmem,) * 4,
+        compiler_params=params(8),
+        cost_estimate=pl.CostEstimate(flops=2 * 10**9, bytes_accessed=2**20, transcendentals=0),
+    )(tilt, near_own, far_own)
+    near_cos, near_sin = pl.pallas_call(
+        second_kernel,
+        out_shape=(array(*half_screens),) * 2,
+        in_specs=[vmem] * 3,
+        out_specs=(vmem,) * 2,
         compiler_params=params(8),
         cost_estimate=pl.CostEstimate(flops=5 * 10**8, bytes_accessed=2**20, transcendentals=0),
-    )(tilt, near_own, near_rest)
+    )(near_rest, own_cos, own_sin)
     mine, theirs = pl.pallas_call(
         wave_kernel,
         out_shape=(array(1, 3, tile_r, tile_c),) * 2,
@@ -388,7 +403,7 @@
         + [pltpu.VMEM((blocks, height, 2 * LANES), jnp.bfloat16)] * 2,
         compiler_params=params(24),
     )(
-        wave, near_cos, near_sin, near_own, far_own, far_rest,
+        wave, near_cos, near_sin, measured, far_own, far_rest,
         jnp.asarray(row_constant(height)), jnp.asarray(col_constant()),
     )
     return pl.pallas_call(

time: 32.9 us -> 34.1 us (1.036)
  local copies, waits for them, and re-layouts: 0.93 us -> 2.26 us
  starting transfers between devices: 16.7 us -> 16.1 us
    ppermute x1, starting transfers between devices: 1.52 us -> 3.12 us  [whole_field_body(): lax.ppermute(slab, 'col', further)]
    ppermute x2, starting transfers between devices: 3.94 us -> 2.4 us  [whole_field_body(): near_own.append(lax.ppermute(packet, 'col', close))]
    unnamed x11 -> x13, local copies, waits for them, and re-layouts: 0.89 us -> 2.22 us
    ppermute x3, starting transfers between devices: 0.98 us -> 0.21 us  [swap_cores(): return lax.ppermute(value, 'row', [(0, 1), (1, 0)])]
    pallas_call x1 -> x2, Pallas kernels: 1.13 us -> 1.16 us  [the longest x1 0.81 us: whole_field_body(): pl.pallas_call(first_kernel, out_shape=(array(*field), array(blocks, heig...]
where the time goes in v17:
time: 34.1 us; the launch traced here: 33.9 us
  starting transfers between devices  16.1 us (47%)
  Pallas kernels  9.15 us (27%)
  waiting for transfers between devices  5.45 us (16%)
  local copies, waits for them, and re-layouts  2.26 us (7%)
  between operations  0.81 us (2%)
    ppermute x6, starting transfers between devices, spread(): lax.ppermute(shard, axis, pairs)  10.4 us
    pallas_call x1, Pallas kernels, whole_field_body(): pl.pallas_call(wave_kernel, out_shape=(array(1, 3, tile_r, tile_c),) * 2,...  7.3 us
    ppermute x6, waiting for transfers between devices, spread(): lax.ppermute(shard, axis, pairs)  4.15 us
    ppermute x1, starting transfers between devices, whole_field_body(): lax.ppermute(slab, 'col', further)  3.12 us
    ppermute x2, starting transfers between devices, whole_field_body(): near_own.append(lax.ppermute(packet, 'col', close))  2.4 us
    unnamed x13, local copies, waits for them, and re-layouts  2.22 us
    ppermute x3, waiting for transfers between devices, swap_cores(): return lax.ppermute(value, 'row', [(0, 1), (1, 0)])  1.29 us
    pallas_call x1, Pallas kernels, whole_field_body(): pl.pallas_call(first_kernel, out_shape=(array(*field), array(blocks, heig...  0.81 us
  transfers between devices with their start and end apart: 12, of which 3 were waited for; matrix products, arithmetic and copies ran while one was open for 3% of the time, Pallas kernels for 3%

profile of v17, /device:TPU:0, one launch (start us, length us, event | category | flops | bytes accessed | tf_op | source)
XLA Modules:
  0.0 33.9 jit_solution(16834447651260337940)
XLA Ops:
  0.6 0.0 copy-start.3
  0.6 3.1 %collective-permute-start = (f32[1,64,128]{2,1,0:T(8,128)}, f32[1,64,128]{2,1,0:T(8,128)S(1)}, u32[]{:S(2)}, u32[]{:S(2)}) collective-permute-start(f32[1,64,128]{2,1,0:T(8,128)} %param.5), channel_id=1, source_target_pairs={{0,8},{8,0},{16,24},{24,16},{1,9},{9,1},{17,25},{25,17},{2,10},{10... | collective-permute-start | bytes 98312 | tf_op jit(solution)/shard_map/ppermute | solution.py:331
  3.7 2.6 %collective-permute-start.1 = (f32[1,64,128]{2,1,0:T(8,128)}, f32[1,64,128]{2,1,0:T(8,128)S(1)}, u32[]{:S(2)}, u32[]{:S(2)}) collective-permute-start(f32[1,64,128]{2,1,0:T(8,128)} %param.5), channel_id=1, source_target_pairs={{0,16},{8,24},{16,0},{24,8},{1,17},{9,25},{17,1},{25,9},{2,18},{10... | collective-permute-start | bytes 98312 | tf_op jit(solution)/shard_map/ppermute | solution.py:331
  6.3 0.0 collective-permute-start.2
  6.3 0.0 collective-permute-done
  6.3 0.8 %constant_dynamic-update-slice_fusion.4 = f32[3,64,128]{2,1,0:T(8,128)S(1)} fusion(f32[1,64,128]{2,1,0:T(8,128)} %param.5), kind=kLoop, calls=%fused_computation.8 | loop fusion | bytes 65536
  7.1 0.0 copy-done.3
  7.2 0.0 copy-start.4
  7.2 1.7 %collective-permute-start.4 = (f32[3,64,128]{2,1,0:T(8,128)S(1)}, f32[3,64,128]{2,1,0:T(8,128)S(1)}, u32[]{:S(2)}, u32[]{:S(2)}) collective-permute-start(f32[3,64,128]{2,1,0:T(8,128)S(1)} %constant_dynamic-update-slice_fusion.3), channel_id=1, source_target_pairs={{0,1},{1,0},{2,3},{3,2},{4,5},{5,4},{6,7},{7,6},{8,9},{9,8},{10,11... | collective-permute-start | bytes 294920 | tf_op jit(solution)/shard_map/ppermute | solution.py:363
  8.9 0.7 %collective-permute-start.6 = (f32[3,64,128]{2,1,0:T(8,128)S(1)}, f32[3,64,128]{2,1,0:T(8,128)S(1)}, u32[]{:S(2)}, u32[]{:S(2)}) collective-permute-start(f32[3,64,128]{2,1,0:T(8,128)S(1)} %constant_dynamic-update-slice_fusion.3), channel_id=1, source_target_pairs={{1,2},{2,1},{5,6},{6,5},{9,10},{10,9},{13,14},{14,13},{17,18},{18,... | collective-permute-start | bytes 294920 | tf_op jit(solution)/shard_map/ppermute | solution.py:363
  9.6 0.0 copy-done.4
  9.6 3.1 %collective-permute-start.5 = (f32[1,64,128]{2,1,0:T(8,128)S(1)}, f32[1,64,128]{2,1,0:T(8,128)S(1)}, u32[]{:S(2)}, u32[]{:S(2)}) collective-permute-start(f32[1,64,128]{2,1,0:T(8,128)S(1)} %copy-done.4), channel_id=1, source_target_pairs={{0,2},{1,3},{2,0},{3,1},{4,6},{5,7},{6,4},{7,5},{8,10},{9,11},{10,... | collective-permute-start | bytes 98312 | tf_op jit(solution)/shard_map/ppermute | solution.py:366
  12.7 0.0 collective-permute-done.1
  12.7 0.0 collective-permute-done.2
  12.7 0.7 %collective-permute-start.3 = (f32[3,64,128]{2,1,0:T(8,128)S(1)}, f32[3,64,128]{2,1,0:T(8,128)S(1)}, u32[]{:S(2)}, u32[]{:S(2)}) collective-permute-start(f32[3,64,128]{2,1,0:T(8,128)S(1)} %constant_dynamic-update-slice_fusion), channel_id=1, source_target_pairs={{1,2},{2,1},{5,6},{6,5},{9,10},{10,9},{13,14},{14,13},{17,18},{18,... | collective-permute-start | bytes 294920 | tf_op jit(solution)/shard_map/ppermute | solution.py:331
  13.4 3.8 %collective-permute-start.8 = (f32[3,64,128]{2,1,0:T(8,128)S(1)}, f32[3,64,128]{2,1,0:T(8,128)S(1)}, u32[]{:S(2)}, u32[]{:S(2)}) collective-permute-start(f32[3,64,128]{2,1,0:T(8,128)S(1)} %constant_dynamic-update-slice_fusion), channel_id=1, source_target_pairs={{0,1},{1,0},{2,3},{3,2},{4,5},{5,4},{6,7},{7,6},{8,9},{9,8},{10,11... | collective-permute-start | bytes 294920 | tf_op jit(solution)/shard_map/ppermute | solution.py:331
  17.2 0.0 collective-permute-done.5
  17.2 0.3 collective-permute-start.9
  17.5 0.0 collective-permute-done.4
  17.5 0.0 collective-permute-done.6
  17.5 0.0 collective-permute-done.3
  17.6 0.1 collective-permute-start.7
  17.7 3.1 %collective-permute-done.8 = f32[3,64,128]{2,1,0:T(8,128)S(1)} collective-permute-done((f32[3,64,128]{2,1,0:T(8,128)S(1)}, f32[3,64,128]{2,1,0:T(8,128)S(1)}, u32[]{:S(2)}, u32[]{:S(2)}) %collective-permute-start.8) | collective-permute-done | bytes 98336 | tf_op jit(solution)/shard_map/ppermute | solution.py:331
  20.8 1.1 %collective-permute-done.9 = f32[3,64,128]{2,1,0:T(8,128)S(1)} collective-permute-done((f32[3,64,128]{2,1,0:T(8,128)S(1)}, f32[3,64,128]{2,1,0:T(8,128)S(1)}, u32[]{:S(2)}, u32[]{:S(2)}) %collective-permute-start.9) | collective-permute-done | bytes 98336 | tf_op jit(solution)/shard_map/ppermute | solution.py:331
  21.8 0.0 copy-start.2
  21.9 0.1 collective-permute-start.10
  21.9 0.0 collective-permute-done.7.far_own
  21.9 0.6 %copy-done.2 = s32[2,2]{1,0:T(2,128)S(1)} copy-done((s32[2,2]{1,0:T(2,128)S(1)}, s32[2,2]{1,0:T(2,128)}, u32[]{:S(2)}) %copy-start.2) | copy-done | bytes 40
  22.5 0.8 %shard_map.68 = (f32[4,2,128,128]{3,2,1,0:T(8,128)S(1)}, f32[4,128,128]{2,1,0:T(8,128)S(1)}, f32[4,64,128]{2,1,0:T(8,128)S(1)}, f32[4,64,128]{2,1,0:T(8,128)S(1)}) custom-call(s32[2,2]{1,0:T(2,128)S(1)} %copy-done.2, f32[4,3,64,128]{3,2,1,0:T(8,128)S(1)} %pad_maximum_fusion.near_own, f32[4,2,64,128]{3,2,1,0:T(8,128)S(1)} %collective-permute-done.7.far_own), custom_call_target="tpu_custom_call" | custom-call | flops 2000000000 | bytes 1048576 | tf_op jit(solution)/shard_map/pallas_call | solution.py:378
  23.3 0.0 copy-start
  23.3 0.0 copy-start.1
  23.3 0.4 %shard_map.69 = (f32[5,4,64,128]{3,2,1,0:T(8,128)S(1)}, f32[5,4,64,128]{3,2,1,0:T(8,128)S(1)}) custom-call(f32[4,3,64,128]{3,2,1,0:T(8,128)S(1)} %pad_maximum_fusion.1.near_rest, f32[4,64,128]{2,1,0:T(8,128)S(1)} %get-tuple-element.21.own_cos, f32[4,64,128]{2,1,0:T(8,128)S(1)} %get-tuple-element.22.own_sin), custom_call_target="tpu_custom_call" | custom-call | flops 500000000 | bytes 1048576 | tf_op jit(solution)/shard_map/pallas_call | solution.py:386
  23.7 0.0 collective-permute-done.10.far_rest
  23.7 0.7 %copy-done = bf16[2,256,512]{2,1,0:T(8,128)(2,1)S(1)} copy-done((bf16[2,256,512]{2,1,0:T(8,128)(2,1)S(1)}, bf16[2,256,512]{2,1,0:T(8,128)(2,1)}, u32[]{:S(2)}) %copy-start) | copy-done | bytes 524312
  24.4 0.2 copy-done.1
  24.5 7.3 %shard_map.70 = (f32[1,3,64,128]{3,2,1,0:T(8,128)S(1)}, f32[1,3,64,128]{3,2,1,0:T(8,128)S(1)}) custom-call(f32[4,2,128,128]{3,2,1,0:T(8,128)S(1)} %get-tuple-element.19.wave_ref, f32[5,4,64,128]{3,2,1,0:T(8,128)S(1)} %get-tuple-element.23.near_cos, f32[5,4,64,128]{3,2,1,0:T(8,128)S(1)} %get-tuple-element.24.near_sin, ...), custom_call_target="tpu_custom_call" | custom-call | tf_op jit(solution)/shard_map/pallas_call | solution.py:394
  31.8 0.1 collective-permute-start.11
  31.9 1.3 %collective-permute-done.11.received_ref = f32[1,3,64,128]{3,2,1,0:T(8,128)S(1)} collective-permute-done((f32[1,3,64,128]{3,2,1,0:T(8,128)S(1)}, f32[1,3,64,128]{3,2,1,0:T(8,128)S(1)}, u32[]{:S(2)}, u32[]{:S(2)}) %collective-permute-start.11) | collective-permute-done | bytes 98336 | tf_op jit(solution)/shard_map/ppermute | solution.py:336
  33.2 0.7 %shard_map.71 = (f32[1,64,128]{2,1,0:T(8,128)}, f32[2,1,2,64,128]{4,3,2,1,0:T(8,128)}) custom-call(f32[1,3,64,128]{3,2,1,0:T(8,128)S(1)} %get-tuple-element.26.mine_ref, f32[1,3,64,128]{3,2,1,0:T(8,128)S(1)} %collective-permute-done.11.received_ref), custom_call_target="tpu_custom_call" | custom-call | tf_op jit(solution)/shard_map/pallas_call | solution.py:409
  (9 shorter events, 0.1 us)
Async XLA Ops:
  0.6 6.5 %copy-start.3 = (f32[2,64,128]{2,1,0:T(8,128)S(1)}, f32[2,64,128]{2,1,0:T(8,128)}, u32[]{:S(2)}) copy-start(f32[2,64,128]{2,1,0:T(8,128)} %param.7) | copy-start | bytes 196612
  0.6 5.7 %collective-permute-start = (f32[1,64,128]{2,1,0:T(8,128)}, f32[1,64,128]{2,1,0:T(8,128)S(1)}, u32[]{:S(2)}, u32[]{:S(2)}) collective-permute-start(f32[1,64,128]{2,1,0:T(8,128)} %param.5), channel_id=1, source_target_pairs={{0,8},{8,0},{16,24},{24,16},{1,9},{9,1},{17,25},{25,17},{2,10},{10... | collective-permute-start | bytes 98312 | tf_op jit(solution)/shard_map/ppermute | solution.py:331
  3.7 9.0 %collective-permute-start.1 = (f32[1,64,128]{2,1,0:T(8,128)}, f32[1,64,128]{2,1,0:T(8,128)S(1)}, u32[]{:S(2)}, u32[]{:S(2)}) collective-permute-start(f32[1,64,128]{2,1,0:T(8,128)} %param.5), channel_id=1, source_target_pairs={{0,16},{8,24},{16,0},{24,8},{1,17},{9,25},{17,1},{25,9},{2,18},{10... | collective-permute-start | bytes 98312 | tf_op jit(solution)/shard_map/ppermute | solution.py:331
  6.3 6.4 %collective-permute-start.2 = (f32[1,64,128]{2,1,0:T(8,128)}, f32[1,64,128]{2,1,0:T(8,128)S(1)}, u32[]{:S(2)}, u32[]{:S(2)}) collective-permute-start(f32[1,64,128]{2,1,0:T(8,128)} %param.5), channel_id=1, source_target_pairs={{0,24},{8,16},{16,8},{24,0},{1,25},{9,17},{17,9},{25,1},{2,26},{10... | collective-permute-start | bytes 98312 | tf_op jit(solution)/shard_map/ppermute | solution.py:331
  7.2 2.4 %copy-start.4 = (f32[1,64,128]{2,1,0:T(8,128)S(1)}, f32[1,64,128]{2,1,0:T(8,128)}, u32[]{:S(2)}) copy-start(f32[1,64,128]{2,1,0:T(8,128)} %param.5) | copy-start | bytes 98308
  7.2 10.3 %collective-permute-start.4 = (f32[3,64,128]{2,1,0:T(8,128)S(1)}, f32[3,64,128]{2,1,0:T(8,128)S(1)}, u32[]{:S(2)}, u32[]{:S(2)}) collective-permute-start(f32[3,64,128]{2,1,0:T(8,128)S(1)} %constant_dynamic-update-slice_fusion.3), channel_id=1, source_target_pairs={{0,1},{1,0},{2,3},{3,2},{4,5},{5,4},{6,7},{7,6},{8,9},{9,8},{10,11... | collective-permute-start | bytes 294920 | tf_op jit(solution)/shard_map/ppermute | solution.py:363
  8.9 8.6 %collective-permute-start.6 = (f32[3,64,128]{2,1,0:T(8,128)S(1)}, f32[3,64,128]{2,1,0:T(8,128)S(1)}, u32[]{:S(2)}, u32[]{:S(2)}) collective-permute-start(f32[3,64,128]{2,1,0:T(8,128)S(1)} %constant_dynamic-update-slice_fusion.3), channel_id=1, source_target_pairs={{1,2},{2,1},{5,6},{6,5},{9,10},{10,9},{13,14},{14,13},{17,18},{18,... | collective-permute-start | bytes 294920 | tf_op jit(solution)/shard_map/ppermute | solution.py:363
  9.6 7.6 %collective-permute-start.5 = (f32[1,64,128]{2,1,0:T(8,128)S(1)}, f32[1,64,128]{2,1,0:T(8,128)S(1)}, u32[]{:S(2)}, u32[]{:S(2)}) collective-permute-start(f32[1,64,128]{2,1,0:T(8,128)S(1)} %copy-done.4), channel_id=1, source_target_pairs={{0,2},{1,3},{2,0},{3,1},{4,6},{5,7},{6,4},{7,5},{8,10},{9,11},{10,... | collective-permute-start | bytes 98312 | tf_op jit(solution)/shard_map/ppermute | solution.py:366
  12.7 4.8 %collective-permute-start.3 = (f32[3,64,128]{2,1,0:T(8,128)S(1)}, f32[3,64,128]{2,1,0:T(8,128)S(1)}, u32[]{:S(2)}, u32[]{:S(2)}) collective-permute-start(f32[3,64,128]{2,1,0:T(8,128)S(1)} %constant_dynamic-update-slice_fusion), channel_id=1, source_target_pairs={{1,2},{2,1},{5,6},{6,5},{9,10},{10,9},{13,14},{14,13},{17,18},{18,... | collective-permute-start | bytes 294920 | tf_op jit(solution)/shard_map/ppermute | solution.py:331
  13.4 7.3 %collective-permute-start.8 = (f32[3,64,128]{2,1,0:T(8,128)S(1)}, f32[3,64,128]{2,1,0:T(8,128)S(1)}, u32[]{:S(2)}, u32[]{:S(2)}) collective-permute-start(f32[3,64,128]{2,1,0:T(8,128)S(1)} %constant_dynamic-update-slice_fusion), channel_id=1, source_target_pairs={{0,1},{1,0},{2,3},{3,2},{4,5},{5,4},{6,7},{7,6},{8,9},{9,8},{10,11... | collective-permute-start | bytes 294920 | tf_op jit(solution)/shard_map/ppermute | solution.py:331
  17.2 4.6 %collective-permute-start.9 = (f32[3,64,128]{2,1,0:T(8,128)S(1)}, f32[3,64,128]{2,1,0:T(8,128)S(1)}, u32[]{:S(2)}, u32[]{:S(2)}) collective-permute-start(f32[3,64,128]{2,1,0:T(8,128)S(1)} %constant_dynamic-update-slice_fusion), channel_id=1, source_target_pairs={{0,2},{1,3},{2,0},{3,1},{4,6},{5,7},{6,4},{7,5},{8,10},{9,11},{10,... | collective-permute-start | bytes 294920 | tf_op jit(solution)/shard_map/ppermute | solution.py:331
  17.6 4.3 %collective-permute-start.7 = (f32[4,2,64,128]{3,2,1,0:T(8,128)S(1)}, f32[4,2,64,128]{3,2,1,0:T(8,128)S(1)}, u32[]{:S(2)}, u32[]{:S(2)}) collective-permute-start(f32[4,2,64,128]{3,2,1,0:T(8,128)S(1)} %pad_maximum_fusion.2), channel_id=1, source_target_pairs={{0,4},{4,0},{1,5},{5,1},{2,6},{6,2},{3,7},{7,3},{8,12},{12,8},{9,1... | collective-permute-start | bytes 786440 | tf_op jit(solution)/shard_map/ppermute | solution.py:336
  21.8 0.7 %copy-start.2 = (s32[2,2]{1,0:T(2,128)S(1)}, s32[2,2]{1,0:T(2,128)}, u32[]{:S(2)}) copy-start(s32[2,2]{1,0:T(2,128)} %tilt_ref.1) | copy-start | bytes 52
  21.9 1.9 %collective-permute-start.10 = (f32[4,3,64,128]{3,2,1,0:T(8,128)S(1)}, f32[4,3,64,128]{3,2,1,0:T(8,128)S(1)}, u32[]{:S(2)}, u32[]{:S(2)}) collective-permute-start(f32[4,3,64,128]{3,2,1,0:T(8,128)S(1)} %pad_maximum_fusion.1.near_rest), channel_id=1, source_target_pairs={{0,4},{4,0},{1,5},{5,1},{2,6},{6,2},{3,7},{7,3},{8,12},{12,8},{9,1... | collective-permute-start | bytes 1179656 | tf_op jit(solution)/shard_map/ppermute | solution.py:336
  23.3 1.0 %copy-start = (bf16[2,256,512]{2,1,0:T(8,128)(2,1)S(1)}, bf16[2,256,512]{2,1,0:T(8,128)(2,1)}, u32[]{:S(2)}) copy-start(bf16[2,256,512]{2,1,0:T(8,128)(2,1)} %constant.19.clone.row_ref) | copy-start | bytes 1572868
  23.3 1.2 %copy-start.1 = (bf16[512,512]{1,0:T(8,128)(2,1)S(1)}, bf16[512,512]{1,0:T(8,128)(2,1)}, u32[]{:S(2)}) copy-start(bf16[512,512]{1,0:T(8,128)(2,1)} %constant.20.clone.col_ref) | copy-start | bytes 1572868
  31.8 1.4 %collective-permute-start.11 = (f32[1,3,64,128]{3,2,1,0:T(8,128)S(1)}, f32[1,3,64,128]{3,2,1,0:T(8,128)S(1)}, u32[]{:S(2)}, u32[]{:S(2)}) collective-permute-start(f32[1,3,64,128]{3,2,1,0:T(8,128)S(1)} %get-tuple-element.27), channel_id=1, source_target_pairs={{0,4},{4,0},{1,5},{5,1},{2,6},{6,2},{3,7},{7,3},{8,12},{12,8},{9,1... | collective-permute-start | bytes 294920 | tf_op jit(solution)/shard_map/ppermute | solution.py:336

commit v18 on v17

--- a/solution.py
+++ b/solution.py
@@ -178,6 +178,17 @@
         wave_ref[place, 0], wave_ref[place, 1] = wave
 
 
+def load_kernel(row_from, col_from, row_to, col_to, sems):
+    copies = [
+        pltpu.make_async_copy(row_from.at[lax.axis_index("row")], row_to, sems.at[0]),
+        pltpu.make_async_copy(col_from, col_to, sems.at[1]),
+    ]
+    for copy in copies:
+        copy.start()
+    for copy in copies:
+        copy.wait()
+
+
 def first_kernel(tilt_ref, near_own, far_own, wave_ref, measured_ref, cos_ref, sin_ref):
     blocks, _, height, _ = wave_ref.shape
     core, own_place = lax.axis_index("row"), lax.axis_index("col")
@@ -230,7 +241,7 @@
     core, own_section, own_place = lax.axis_index("row"), lax.axis_index("depth"), lax.axis_index("col")
     near, far = pl.ds(0, height // 2), pl.ds(height // 2, height // 2)
     screens = (near_cos, near_sin, far_cos, far_sin)
-    row_matrix = row_ref[core]
+    row_matrix = row_ref[...]
     window = min(3, blocks)
     window_start = jnp.clip(own_place - 1, 0, blocks - window)
     own_in_window = own_place - window_start
@@ -367,7 +378,21 @@
             near_own.append(jnp.concatenate([arrived, jnp.zeros_like(measured)], axis=0))
     near_own = jnp.stack(near_own)
     arriving = spread(other_depths, "col", 2)
-    arriving[2], near_own = lax.optimization_barrier((arriving[2], near_own))
+    row_all, col_all = jnp.asarray(row_constant(height)), jnp.asarray(col_constant())
+    arriving[2], near_own, row_all, col_all = lax.optimization_barrier((arriving[2], near_own, row_all, col_all))
+    row_matrix, col_matrix = pl.pallas_call(
+        load_kernel,
+        out_shape=(
+            jax.ShapeDtypeStruct(row_all.shape[1:], row_all.dtype),
+            jax.ShapeDtypeStruct(col_all.shape, col_all.dtype),
+        ),
+        in_specs=[hbm, hbm],
+        out_specs=(vmem, vmem),
+        scratch_shapes=[pltpu.SemaphoreType.DMA((2,))],
+        compiler_params=params(2),
+        cost_estimate=pl.CostEstimate(flops=10**8, bytes_accessed=2**20, transcendentals=0),
+    )(row_all, col_all)
+    arriving[1], row_matrix, col_matrix = lax.optimization_barrier((arriving[1], row_matrix, col_matrix))
     near_rest = jnp.stack([other_depths] + arriving)
     wanted = lax.dynamic_slice_in_dim(near_own, 2 - core, 1, 1)
     far_own = swap_cores(jnp.concatenate([near_own[:, :1], wanted], axis=1))
@@ -404,7 +429,7 @@
         compiler_params=params(24),
     )(
         wave, near_cos, near_sin, measured, far_own, far_rest,
-        jnp.asarray(row_constant(height)), jnp.asarray(col_constant()),
+        row_matrix, col_matrix,
     )
     return pl.pallas_call(
         finish_kernel,

time: 34.1 us -> 33.3 us (0.977)
  waiting for transfers between devices: 5.45 us -> 4.27 us
    ppermute x1, starting transfers between devices: 3.12 us -> 1.71 us  [whole_field_body(): lax.ppermute(slab, 'col', further)]
    ppermute x2, starting transfers between devices: 2.4 us -> 3.76 us  [whole_field_body(): near_own.append(lax.ppermute(packet, 'col', close))]
    ppermute x6, waiting for transfers between devices: 4.15 us -> 3.04 us  [spread(): lax.ppermute(shard, axis, pairs)]
    unnamed x13 -> x11, local copies, waits for them, and re-layouts: 2.22 us -> 2.44 us
  transfers between devices with their start and end apart: 12 -> 12, of which waited for: 3 -> 3; matrix products, arithmetic and copies ran while one was open for 3% -> 3% of each run, Pallas kernels for 3% -> 4%
where the time goes in v18:
time: 33.3 us; the launch traced here: 33 us
  starting transfers between devices  16.2 us (49%)
  Pallas kernels  9.23 us (28%)
  waiting for transfers between devices  4.27 us (13%)
  local copies, waits for them, and re-layouts  2.48 us (7%)
  between operations  0.8 us (2%)
    ppermute x6, starting transfers between devices, spread(): lax.ppermute(shard, axis, pairs)  10.4 us
    pallas_call x1, Pallas kernels, whole_field_body(): pl.pallas_call(wave_kernel, out_shape=(array(1, 3, tile_r, tile_c),) * 2,...  7.3 us
    ppermute x2, starting transfers between devices, whole_field_body(): near_own.append(lax.ppermute(packet, 'col', close))  3.76 us
    ppermute x6, waiting for transfers between devices, spread(): lax.ppermute(shard, axis, pairs)  3.04 us
    unnamed x11, local copies, waits for them, and re-layouts  2.44 us
    ppermute x1, starting transfers between devices, whole_field_body(): lax.ppermute(slab, 'col', further)  1.71 us
    ppermute x3, waiting for transfers between devices, swap_cores(): return lax.ppermute(value, 'row', [(0, 1), (1, 0)])  1.22 us
    pallas_call x1, Pallas kernels, whole_field_body(): pl.pallas_call(first_kernel, out_shape=(array(*field), array(blocks, heig...  0.81 us
  transfers between devices with their start and end apart: 12, of which 3 were waited for; matrix products, arithmetic and copies ran while one was open for 3% of the time, Pallas kernels for 4%

profile of v18, /device:TPU:0, one launch (start us, length us, event | category | flops | bytes accessed | tf_op | source)
XLA Modules:
  0.0 33.0 jit_solution(2273292332374027688)
XLA Ops:
  0.6 0.0 copy-start.3
  0.6 3.1 %collective-permute-start = (f32[1,64,128]{2,1,0:T(8,128)}, f32[1,64,128]{2,1,0:T(8,128)S(1)}, u32[]{:S(2)}, u32[]{:S(2)}) collective-permute-start(f32[1,64,128]{2,1,0:T(8,128)} %param.5), channel_id=1, source_target_pairs={{0,8},{8,0},{16,24},{24,16},{1,9},{9,1},{17,25},{25,17},{2,10},{10... | collective-permute-start | bytes 98312 | tf_op jit(solution)/shard_map/ppermute | solution.py:342
  3.7 2.6 %collective-permute-start.1 = (f32[1,64,128]{2,1,0:T(8,128)}, f32[1,64,128]{2,1,0:T(8,128)S(1)}, u32[]{:S(2)}, u32[]{:S(2)}) collective-permute-start(f32[1,64,128]{2,1,0:T(8,128)} %param.5), channel_id=1, source_target_pairs={{0,16},{8,24},{16,0},{24,8},{1,17},{9,25},{17,1},{25,9},{2,18},{10... | collective-permute-start | bytes 98312 | tf_op jit(solution)/shard_map/ppermute | solution.py:342
  6.3 0.0 collective-permute-start.2
  6.3 0.0 collective-permute-done
  6.3 0.8 %constant_dynamic-update-slice_fusion.4 = f32[3,64,128]{2,1,0:T(8,128)S(1)} fusion(f32[1,64,128]{2,1,0:T(8,128)} %param.5), kind=kLoop, calls=%fused_computation.8 | loop fusion | bytes 65536
  7.1 1.7 %collective-permute-start.5 = (f32[1,64,128]{2,1,0:T(8,128)}, f32[1,64,128]{2,1,0:T(8,128)S(1)}, u32[]{:S(2)}, u32[]{:S(2)}) collective-permute-start(f32[1,64,128]{2,1,0:T(8,128)} %param.5), channel_id=1, source_target_pairs={{0,2},{1,3},{2,0},{3,1},{4,6},{5,7},{6,4},{7,5},{8,10},{9,11},{10,... | collective-permute-start | bytes 98312 | tf_op jit(solution)/shard_map/ppermute | solution.py:377
  8.9 0.0 copy-done.3
  8.9 0.7 %collective-permute-start.6 = (f32[3,64,128]{2,1,0:T(8,128)S(1)}, f32[3,64,128]{2,1,0:T(8,128)S(1)}, u32[]{:S(2)}, u32[]{:S(2)}) collective-permute-start(f32[3,64,128]{2,1,0:T(8,128)S(1)} %constant_dynamic-update-slice_fusion.3), channel_id=1, source_target_pairs={{1,2},{2,1},{5,6},{6,5},{9,10},{10,9},{13,14},{14,13},{17,18},{18,... | collective-permute-start | bytes 294920 | tf_op jit(solution)/shard_map/ppermute | solution.py:374
  9.5 3.1 %collective-permute-start.4 = (f32[3,64,128]{2,1,0:T(8,128)S(1)}, f32[3,64,128]{2,1,0:T(8,128)S(1)}, u32[]{:S(2)}, u32[]{:S(2)}) collective-permute-start(f32[3,64,128]{2,1,0:T(8,128)S(1)} %constant_dynamic-update-slice_fusion.3), channel_id=1, source_target_pairs={{0,1},{1,0},{2,3},{3,2},{4,5},{5,4},{6,7},{7,6},{8,9},{9,8},{10,11... | collective-permute-start | bytes 294920 | tf_op jit(solution)/shard_map/ppermute | solution.py:374
  12.6 0.0 collective-permute-done.1
  12.6 0.0 collective-permute-done.2
  12.7 0.7 %collective-permute-start.3 = (f32[3,64,128]{2,1,0:T(8,128)S(1)}, f32[3,64,128]{2,1,0:T(8,128)S(1)}, u32[]{:S(2)}, u32[]{:S(2)}) collective-permute-start(f32[3,64,128]{2,1,0:T(8,128)S(1)} %constant_dynamic-update-slice_fusion), channel_id=1, source_target_pairs={{1,2},{2,1},{5,6},{6,5},{9,10},{10,9},{13,14},{14,13},{17,18},{18,... | collective-permute-start | bytes 294920 | tf_op jit(solution)/shard_map/ppermute | solution.py:342
  13.3 3.8 %collective-permute-start.9 = (f32[3,64,128]{2,1,0:T(8,128)S(1)}, f32[3,64,128]{2,1,0:T(8,128)S(1)}, u32[]{:S(2)}, u32[]{:S(2)}) collective-permute-start(f32[3,64,128]{2,1,0:T(8,128)S(1)} %constant_dynamic-update-slice_fusion), channel_id=1, source_target_pairs={{0,2},{1,3},{2,0},{3,1},{4,6},{5,7},{6,4},{7,5},{8,10},{9,11},{10,... | collective-permute-start | bytes 294920 | tf_op jit(solution)/shard_map/ppermute | solution.py:342
  17.2 0.0 collective-permute-done.5
  17.2 0.2 collective-permute-start.8
  17.4 0.0 collective-permute-done.6
  17.4 0.0 collective-permute-done.4
  17.5 0.0 copy-start
  17.5 0.0 copy-start.1
  17.5 0.0 collective-permute-done.3
  17.6 0.1 collective-permute-start.7
  17.6 0.9 %copy-done = bf16[2,256,512]{2,1,0:T(8,128)(2,1)S(1)} copy-done((bf16[2,256,512]{2,1,0:T(8,128)(2,1)S(1)}, bf16[2,256,512]{2,1,0:T(8,128)(2,1)}, u32[]{:S(2)}) %copy-start) | copy-done | bytes 524312
  18.5 0.2 copy-done.1
  18.7 0.1 shard_map.69
  18.8 1.1 %collective-permute-done.9 = f32[3,64,128]{2,1,0:T(8,128)S(1)} collective-permute-done((f32[3,64,128]{2,1,0:T(8,128)S(1)}, f32[3,64,128]{2,1,0:T(8,128)S(1)}, u32[]{:S(2)}, u32[]{:S(2)}) %collective-permute-start.9) | collective-permute-done | bytes 98336 | tf_op jit(solution)/shard_map/ppermute | solution.py:342
  19.9 1.9 %collective-permute-done.8 = f32[3,64,128]{2,1,0:T(8,128)S(1)} collective-permute-done((f32[3,64,128]{2,1,0:T(8,128)S(1)}, f32[3,64,128]{2,1,0:T(8,128)S(1)}, u32[]{:S(2)}, u32[]{:S(2)}) %collective-permute-start.8) | collective-permute-done | bytes 98336 | tf_op jit(solution)/shard_map/ppermute | solution.py:342
  21.8 0.0 copy-start.2
  21.8 0.1 collective-permute-start.10
  21.9 0.0 collective-permute-done.7.far_own
  21.9 0.6 %copy-done.2 = s32[2,2]{1,0:T(2,128)S(1)} copy-done((s32[2,2]{1,0:T(2,128)S(1)}, s32[2,2]{1,0:T(2,128)}, u32[]{:S(2)}) %copy-start.2) | copy-done | bytes 40
  22.5 0.8 %shard_map.68 = (f32[4,2,128,128]{3,2,1,0:T(8,128)S(1)}, f32[4,128,128]{2,1,0:T(8,128)S(1)}, f32[4,64,128]{2,1,0:T(8,128)S(1)}, f32[4,64,128]{2,1,0:T(8,128)S(1)}) custom-call(s32[2,2]{1,0:T(2,128)S(1)} %copy-done.2, f32[4,3,64,128]{3,2,1,0:T(8,128)S(1)} %pad_maximum_fusion.near_own, f32[4,2,64,128]{3,2,1,0:T(8,128)S(1)} %collective-permute-done.7.far_own), custom_call_target="tpu_custom_call" | custom-call | flops 2000000000 | bytes 1048576 | tf_op jit(solution)/shard_map/pallas_call | solution.py:403
  23.3 0.4 %shard_map.70 = (f32[5,4,64,128]{3,2,1,0:T(8,128)S(1)}, f32[5,4,64,128]{3,2,1,0:T(8,128)S(1)}) custom-call(f32[4,3,64,128]{3,2,1,0:T(8,128)S(1)} %pad_maximum_fusion.1.near_rest, f32[4,64,128]{2,1,0:T(8,128)S(1)} %get-tuple-element.33.own_cos, f32[4,64,128]{2,1,0:T(8,128)S(1)} %get-tuple-element.34.own_sin), custom_call_target="tpu_custom_call" | custom-call | flops 500000000 | bytes 1048576 | tf_op jit(solution)/shard_map/pallas_call | solution.py:411
  23.6 0.0 collective-permute-done.10.far_rest
  23.7 7.3 %shard_map.71 = (f32[1,3,64,128]{3,2,1,0:T(8,128)S(1)}, f32[1,3,64,128]{3,2,1,0:T(8,128)S(1)}) custom-call(f32[4,2,128,128]{3,2,1,0:T(8,128)S(1)} %get-tuple-element.26.wave_ref, f32[5,4,64,128]{3,2,1,0:T(8,128)S(1)} %get-tuple-element.35.near_cos, f32[5,4,64,128]{3,2,1,0:T(8,128)S(1)} %get-tuple-element.36.near_sin, ...), custom_call_target="tpu_custom_call" | custom-call | tf_op jit(solution)/shard_map/pallas_call | solution.py:419
  31.0 0.1 collective-permute-start.11
  31.1 1.2 %collective-permute-done.11.received_ref = f32[1,3,64,128]{3,2,1,0:T(8,128)S(1)} collective-permute-done((f32[1,3,64,128]{3,2,1,0:T(8,128)S(1)}, f32[1,3,64,128]{3,2,1,0:T(8,128)S(1)}, u32[]{:S(2)}, u32[]{:S(2)}) %collective-permute-start.11) | collective-permute-done | bytes 98336 | tf_op jit(solution)/shard_map/ppermute | solution.py:347
  32.3 0.7 %shard_map.72 = (f32[1,64,128]{2,1,0:T(8,128)}, f32[2,1,2,64,128]{4,3,2,1,0:T(8,128)}) custom-call(f32[1,3,64,128]{3,2,1,0:T(8,128)S(1)} %get-tuple-element.40.mine_ref, f32[1,3,64,128]{3,2,1,0:T(8,128)S(1)} %collective-permute-done.11.received_ref), custom_call_target="tpu_custom_call" | custom-call | tf_op jit(solution)/shard_map/pallas_call | solution.py:434
  (9 shorter events, 0.1 us)
Async XLA Ops:
  0.6 8.2 %copy-start.3 = (f32[2,64,128]{2,1,0:T(8,128)S(1)}, f32[2,64,128]{2,1,0:T(8,128)}, u32[]{:S(2)}) copy-start(f32[2,64,128]{2,1,0:T(8,128)} %param.7) | copy-start | bytes 196612
  0.6 5.7 %collective-permute-start = (f32[1,64,128]{2,1,0:T(8,128)}, f32[1,64,128]{2,1,0:T(8,128)S(1)}, u32[]{:S(2)}, u32[]{:S(2)}) collective-permute-start(f32[1,64,128]{2,1,0:T(8,128)} %param.5), channel_id=1, source_target_pairs={{0,8},{8,0},{16,24},{24,16},{1,9},{9,1},{17,25},{25,17},{2,10},{10... | collective-permute-start | bytes 98312 | tf_op jit(solution)/shard_map/ppermute | solution.py:342
  3.7 8.9 %collective-permute-start.1 = (f32[1,64,128]{2,1,0:T(8,128)}, f32[1,64,128]{2,1,0:T(8,128)S(1)}, u32[]{:S(2)}, u32[]{:S(2)}) collective-permute-start(f32[1,64,128]{2,1,0:T(8,128)} %param.5), channel_id=1, source_target_pairs={{0,16},{8,24},{16,0},{24,8},{1,17},{9,25},{17,1},{25,9},{2,18},{10... | collective-permute-start | bytes 98312 | tf_op jit(solution)/shard_map/ppermute | solution.py:342
  6.3 6.3 %collective-permute-start.2 = (f32[1,64,128]{2,1,0:T(8,128)}, f32[1,64,128]{2,1,0:T(8,128)S(1)}, u32[]{:S(2)}, u32[]{:S(2)}) collective-permute-start(f32[1,64,128]{2,1,0:T(8,128)} %param.5), channel_id=1, source_target_pairs={{0,24},{8,16},{16,8},{24,0},{1,25},{9,17},{17,9},{25,1},{2,26},{10... | collective-permute-start | bytes 98312 | tf_op jit(solution)/shard_map/ppermute | solution.py:342
  7.1 10.0 %collective-permute-start.5 = (f32[1,64,128]{2,1,0:T(8,128)}, f32[1,64,128]{2,1,0:T(8,128)S(1)}, u32[]{:S(2)}, u32[]{:S(2)}) collective-permute-start(f32[1,64,128]{2,1,0:T(8,128)} %param.5), channel_id=1, source_target_pairs={{0,2},{1,3},{2,0},{3,1},{4,6},{5,7},{6,4},{7,5},{8,10},{9,11},{10,... | collective-permute-start | bytes 98312 | tf_op jit(solution)/shard_map/ppermute | solution.py:377
  8.9 8.6 %collective-permute-start.6 = (f32[3,64,128]{2,1,0:T(8,128)S(1)}, f32[3,64,128]{2,1,0:T(8,128)S(1)}, u32[]{:S(2)}, u32[]{:S(2)}) collective-permute-start(f32[3,64,128]{2,1,0:T(8,128)S(1)} %constant_dynamic-update-slice_fusion.3), channel_id=1, source_target_pairs={{1,2},{2,1},{5,6},{6,5},{9,10},{10,9},{13,14},{14,13},{17,18},{18,... | collective-permute-start | bytes 294920 | tf_op jit(solution)/shard_map/ppermute | solution.py:374
  9.5 7.9 %collective-permute-start.4 = (f32[3,64,128]{2,1,0:T(8,128)S(1)}, f32[3,64,128]{2,1,0:T(8,128)S(1)}, u32[]{:S(2)}, u32[]{:S(2)}) collective-permute-start(f32[3,64,128]{2,1,0:T(8,128)S(1)} %constant_dynamic-update-slice_fusion.3), channel_id=1, source_target_pairs={{0,1},{1,0},{2,3},{3,2},{4,5},{5,4},{6,7},{7,6},{8,9},{9,8},{10,11... | collective-permute-start | bytes 294920 | tf_op jit(solution)/shard_map/ppermute | solution.py:374
  12.7 4.8 %collective-permute-start.3 = (f32[3,64,128]{2,1,0:T(8,128)S(1)}, f32[3,64,128]{2,1,0:T(8,128)S(1)}, u32[]{:S(2)}, u32[]{:S(2)}) collective-permute-start(f32[3,64,128]{2,1,0:T(8,128)S(1)} %constant_dynamic-update-slice_fusion), channel_id=1, source_target_pairs={{1,2},{2,1},{5,6},{6,5},{9,10},{10,9},{13,14},{14,13},{17,18},{18,... | collective-permute-start | bytes 294920 | tf_op jit(solution)/shard_map/ppermute | solution.py:342
  13.3 6.5 %collective-permute-start.9 = (f32[3,64,128]{2,1,0:T(8,128)S(1)}, f32[3,64,128]{2,1,0:T(8,128)S(1)}, u32[]{:S(2)}, u32[]{:S(2)}) collective-permute-start(f32[3,64,128]{2,1,0:T(8,128)S(1)} %constant_dynamic-update-slice_fusion), channel_id=1, source_target_pairs={{0,2},{1,3},{2,0},{3,1},{4,6},{5,7},{6,4},{7,5},{8,10},{9,11},{10,... | collective-permute-start | bytes 294920 | tf_op jit(solution)/shard_map/ppermute | solution.py:342
  17.2 4.6 %collective-permute-start.8 = (f32[3,64,128]{2,1,0:T(8,128)S(1)}, f32[3,64,128]{2,1,0:T(8,128)S(1)}, u32[]{:S(2)}, u32[]{:S(2)}) collective-permute-start(f32[3,64,128]{2,1,0:T(8,128)S(1)} %constant_dynamic-update-slice_fusion), channel_id=1, source_target_pairs={{0,1},{1,0},{2,3},{3,2},{4,5},{5,4},{6,7},{7,6},{8,9},{9,8},{10,11... | collective-permute-start | bytes 294920 | tf_op jit(solution)/shard_map/ppermute | solution.py:342
  17.5 1.0 %copy-start = (bf16[2,256,512]{2,1,0:T(8,128)(2,1)S(1)}, bf16[2,256,512]{2,1,0:T(8,128)(2,1)}, u32[]{:S(2)}) copy-start(bf16[2,256,512]{2,1,0:T(8,128)(2,1)} %constant.19.clone.row_from) | copy-start | bytes 1572868
  17.5 1.2 %copy-start.1 = (bf16[512,512]{1,0:T(8,128)(2,1)S(1)}, bf16[512,512]{1,0:T(8,128)(2,1)}, u32[]{:S(2)}) copy-start(bf16[512,512]{1,0:T(8,128)(2,1)} %constant.20.clone.col_from) | copy-start | bytes 1572868
  17.6 4.3 %collective-permute-start.7 = (f32[4,2,64,128]{3,2,1,0:T(8,128)S(1)}, f32[4,2,64,128]{3,2,1,0:T(8,128)S(1)}, u32[]{:S(2)}, u32[]{:S(2)}) collective-permute-start(f32[4,2,64,128]{3,2,1,0:T(8,128)S(1)} %pad_maximum_fusion.2), channel_id=1, source_target_pairs={{0,4},{4,0},{1,5},{5,1},{2,6},{6,2},{3,7},{7,3},{8,12},{12,8},{9,1... | collective-permute-start | bytes 786440 | tf_op jit(solution)/shard_map/ppermute | solution.py:347
  21.8 0.7 %copy-start.2 = (s32[2,2]{1,0:T(2,128)S(1)}, s32[2,2]{1,0:T(2,128)}, u32[]{:S(2)}) copy-start(s32[2,2]{1,0:T(2,128)} %tilt_ref.1) | copy-start | bytes 52
  21.8 1.8 %collective-permute-start.10 = (f32[4,3,64,128]{3,2,1,0:T(8,128)S(1)}, f32[4,3,64,128]{3,2,1,0:T(8,128)S(1)}, u32[]{:S(2)}, u32[]{:S(2)}) collective-permute-start(f32[4,3,64,128]{3,2,1,0:T(8,128)S(1)} %pad_maximum_fusion.1.near_rest), channel_id=1, source_target_pairs={{0,4},{4,0},{1,5},{5,1},{2,6},{6,2},{3,7},{7,3},{8,12},{12,8},{9,1... | collective-permute-start | bytes 1179656 | tf_op jit(solution)/shard_map/ppermute | solution.py:347
  31.0 1.4 %collective-permute-start.11 = (f32[1,3,64,128]{3,2,1,0:T(8,128)S(1)}, f32[1,3,64,128]{3,2,1,0:T(8,128)S(1)}, u32[]{:S(2)}, u32[]{:S(2)}) collective-permute-start(f32[1,3,64,128]{3,2,1,0:T(8,128)S(1)} %get-tuple-element.41), channel_id=1, source_target_pairs={{0,4},{4,0},{1,5},{5,1},{2,6},{6,2},{3,7},{7,3},{8,12},{12,8},{9,1... | collective-permute-start | bytes 294920 | tf_op jit(solution)/shard_map/ppermute | solution.py:347

commit v19 on v18

--- a/solution.py
+++ b/solution.py
@@ -178,24 +178,15 @@
         wave_ref[place, 0], wave_ref[place, 1] = wave
 
 
-def load_kernel(row_from, col_from, row_to, col_to, sems):
+def load_kernel(tilt_ref, row_from, col_from, row_to, col_to, wave_ref, sems):
+    blocks, _, height, _ = wave_ref.shape
+    core = lax.axis_index("row")
     copies = [
-        pltpu.make_async_copy(row_from.at[lax.axis_index("row")], row_to, sems.at[0]),
+        pltpu.make_async_copy(row_from.at[core], row_to, sems.at[0]),
         pltpu.make_async_copy(col_from, col_to, sems.at[1]),
     ]
     for copy in copies:
         copy.start()
-    for copy in copies:
-        copy.wait()
-
-
-def first_kernel(tilt_ref, near_own, far_own, wave_ref, measured_ref, cos_ref, sin_ref):
-    blocks, _, height, _ = wave_ref.shape
-    core, own_place = lax.axis_index("row"), lax.axis_index("col")
-    for col in range(blocks):
-        held = col ^ own_place
-        measured_ref[col] = jnp.concatenate([near_own[held, 1 + core], far_own[held, 1]], axis=0)
-        cos_ref[col], sin_ref[col] = cos_sin(near_own[held, 0])
 
     def cycles(number, position, extent):
         fraction = (number * position).astype(jnp.float32) / extent
@@ -213,6 +204,16 @@
         col_cos, col_sin = col_cos[:1], col_sin[:1]
         wave_ref[block, 0] = row_cos * col_cos - row_sin * col_sin
         wave_ref[block, 1] = row_sin * col_cos + row_cos * col_sin
+    for copy in copies:
+        copy.wait()
+
+
+def first_kernel(near_own, far_own, measured_ref, cos_ref, sin_ref):
+    core, own_place = lax.axis_index("row"), lax.axis_index("col")
+    for col in range(measured_ref.shape[0]):
+        held = col ^ own_place
+        measured_ref[col] = jnp.concatenate([near_own[held, 1 + core], far_own[held, 1]], axis=0)
+        cos_ref[col], sin_ref[col] = cos_sin(near_own[held, 0])
 
 
 def second_kernel(near_rest, own_cos, own_sin, cos_ref, sin_ref):
@@ -380,34 +381,35 @@
     arriving = spread(other_depths, "col", 2)
     row_all, col_all = jnp.asarray(row_constant(height)), jnp.asarray(col_constant())
     arriving[2], near_own, row_all, col_all = lax.optimization_barrier((arriving[2], near_own, row_all, col_all))
-    row_matrix, col_matrix = pl.pallas_call(
+    half_screens = (count + 1, blocks, tile_r, tile_c)
+    field = (blocks, 2, height, tile_c)
+    row_matrix, col_matrix, wave = pl.pallas_call(
         load_kernel,
         out_shape=(
             jax.ShapeDtypeStruct(row_all.shape[1:], row_all.dtype),
             jax.ShapeDtypeStruct(col_all.shape, col_all.dtype),
+            array(*field),
         ),
-        in_specs=[hbm, hbm],
-        out_specs=(vmem, vmem),
+        in_specs=[smem, hbm, hbm],
+        out_specs=(vmem, vmem, vmem),
         scratch_shapes=[pltpu.SemaphoreType.DMA((2,))],
-        compiler_params=params(2),
+        compiler_params=params(4),
         cost_estimate=pl.CostEstimate(flops=10**8, bytes_accessed=2**20, transcendentals=0),
-    )(row_all, col_all)
+    )(tilt, row_all, col_all)
     arriving[1], row_matrix, col_matrix = lax.optimization_barrier((arriving[1], row_matrix, col_matrix))
     near_rest = jnp.stack([other_depths] + arriving)
     wanted = lax.dynamic_slice_in_dim(near_own, 2 - core, 1, 1)
     far_own = swap_cores(jnp.concatenate([near_own[:, :1], wanted], axis=1))
     far_rest = swap_cores(near_rest)
 
-    half_screens = (count + 1, blocks, tile_r, tile_c)
-    field = (blocks, 2, height, tile_c)
-    wave, measured, own_cos, own_sin = pl.pallas_call(
+    measured, own_cos, own_sin = pl.pallas_call(
         first_kernel,
-        out_shape=(array(*field), array(blocks, height, tile_c)) + (array(blocks, tile_r, tile_c),) * 2,
-        in_specs=[smem, vmem, vmem],
-        out_specs=(vmem,) * 4,
+        out_shape=(array(blocks, height, tile_c),) + (array(blocks, tile_r, tile_c),) * 2,
+        in_specs=[vmem, vmem],
+        out_specs=(vmem,) * 3,
         compiler_params=params(8),
-        cost_estimate=pl.CostEstimate(flops=2 * 10**9, bytes_accessed=2**20, transcendentals=0),
-    )(tilt, near_own, far_own)
+        cost_estimate=pl.CostEstimate(flops=3 * 10**9, bytes_accessed=2**20, transcendentals=0),
+    )(near_own, far_own)
     near_cos, near_sin = pl.pallas_call(
         second_kernel,
         out_shape=(array(*half_screens),) * 2,

time: 33.3 us -> 33.2 us (level)
  local copies, waits for them, and re-layouts: 2.48 us -> 1.91 us
  waiting for transfers between devices: 4.27 us -> 4.71 us
    ppermute x3, waiting for transfers between devices: 1.22 us -> 2.38 us  [swap_cores(): return lax.ppermute(value, 'row', [(0, 1), (1, 0)])]
    ppermute x6, waiting for transfers between devices: 3.04 us -> 2.32 us  [spread(): lax.ppermute(shard, axis, pairs)]
    pallas_call x1, Pallas kernels: 0.07 us -> 0.79 us  [whole_field_body(): pl.pallas_call(load_kernel, out_shape=(jax.ShapeDtypeStruct(row_all.shape...]
    pallas_call x1, Pallas kernels: 0.81 us -> 0.12 us  [whole_field_body(): pl.pallas_call(first_kernel, out_shape=(array(blocks, height, tile_c),) +...]
    unnamed x11, local copies, waits for them, and re-layouts: 2.44 us -> 1.87 us
  transfers between devices with their start and end apart: 12 -> 12, of which waited for: 3 -> 4; matrix products, arithmetic and copies ran while one was open for 3% -> 3% of each run, Pallas kernels for 4% -> 4%
where the time goes in v19:
time: 33.2 us; the launch traced here: 33 us
  starting transfers between devices  16.2 us (49%)
  Pallas kernels  9.25 us (28%)
  waiting for transfers between devices  4.71 us (14%)
  local copies, waits for them, and re-layouts  1.91 us (6%)
  between operations  0.8 us (2%)
    ppermute x6, starting transfers between devices, spread(): lax.ppermute(shard, axis, pairs)  10.4 us
    pallas_call x1, Pallas kernels, whole_field_body(): pl.pallas_call(wave_kernel, out_shape=(array(1, 3, tile_r, tile_c),) * 2,...  7.3 us
    ppermute x2, starting transfers between devices, whole_field_body(): near_own.append(lax.ppermute(packet, 'col', close))  3.76 us
    ppermute x3, waiting for transfers between devices, swap_cores(): return lax.ppermute(value, 'row', [(0, 1), (1, 0)])  2.38 us
    ppermute x6, waiting for transfers between devices, spread(): lax.ppermute(shard, axis, pairs)  2.32 us
    unnamed x11, local copies, waits for them, and re-layouts  1.87 us
    ppermute x1, starting transfers between devices, whole_field_body(): lax.ppermute(slab, 'col', further)  1.71 us
    pallas_call x1, Pallas kernels, whole_field_body(): pl.pallas_call(load_kernel, out_shape=(jax.ShapeDtypeStruct(row_all.shape...  0.79 us
  transfers between devices with their start and end apart: 12, of which 4 were waited for; matrix products, arithmetic and copies ran while one was open for 3% of the time, Pallas kernels for 4%

profile of v19, /device:TPU:0, one launch (start us, length us, event | category | flops | bytes accessed | tf_op | source)
XLA Modules:
  0.0 33.0 jit_solution(7990062221442199074)
XLA Ops:
  0.6 0.0 copy-start.3
  0.6 3.1 %collective-permute-start = (f32[1,64,128]{2,1,0:T(8,128)}, f32[1,64,128]{2,1,0:T(8,128)S(1)}, u32[]{:S(2)}, u32[]{:S(2)}) collective-permute-start(f32[1,64,128]{2,1,0:T(8,128)} %param.5), channel_id=1, source_target_pairs={{0,8},{8,0},{16,24},{24,16},{1,9},{9,1},{17,25},{25,17},{2,10},{10... | collective-permute-start | bytes 98312 | tf_op jit(solution)/shard_map/ppermute | solution.py:343
  3.7 2.6 %collective-permute-start.1 = (f32[1,64,128]{2,1,0:T(8,128)}, f32[1,64,128]{2,1,0:T(8,128)S(1)}, u32[]{:S(2)}, u32[]{:S(2)}) collective-permute-start(f32[1,64,128]{2,1,0:T(8,128)} %param.5), channel_id=1, source_target_pairs={{0,16},{8,24},{16,0},{24,8},{1,17},{9,25},{17,1},{25,9},{2,18},{10... | collective-permute-start | bytes 98312 | tf_op jit(solution)/shard_map/ppermute | solution.py:343
  6.3 0.0 collective-permute-start.2
  6.3 0.0 collective-permute-done
  6.3 0.8 %constant_dynamic-update-slice_fusion.4 = f32[3,64,128]{2,1,0:T(8,128)S(1)} fusion(f32[1,64,128]{2,1,0:T(8,128)} %param.5), kind=kLoop, calls=%fused_computation.8 | loop fusion | bytes 65536
  7.1 1.7 %collective-permute-start.5 = (f32[1,64,128]{2,1,0:T(8,128)}, f32[1,64,128]{2,1,0:T(8,128)S(1)}, u32[]{:S(2)}, u32[]{:S(2)}) collective-permute-start(f32[1,64,128]{2,1,0:T(8,128)} %param.5), channel_id=1, source_target_pairs={{0,2},{1,3},{2,0},{3,1},{4,6},{5,7},{6,4},{7,5},{8,10},{9,11},{10,... | collective-permute-start | bytes 98312 | tf_op jit(solution)/shard_map/ppermute | solution.py:378
  8.9 0.0 copy-done.3
  8.9 0.7 %collective-permute-start.6 = (f32[3,64,128]{2,1,0:T(8,128)S(1)}, f32[3,64,128]{2,1,0:T(8,128)S(1)}, u32[]{:S(2)}, u32[]{:S(2)}) collective-permute-start(f32[3,64,128]{2,1,0:T(8,128)S(1)} %constant_dynamic-update-slice_fusion.3), channel_id=1, source_target_pairs={{1,2},{2,1},{5,6},{6,5},{9,10},{10,9},{13,14},{14,13},{17,18},{18,... | collective-permute-start | bytes 294920 | tf_op jit(solution)/shard_map/ppermute | solution.py:375
  9.5 3.1 %collective-permute-start.4 = (f32[3,64,128]{2,1,0:T(8,128)S(1)}, f32[3,64,128]{2,1,0:T(8,128)S(1)}, u32[]{:S(2)}, u32[]{:S(2)}) collective-permute-start(f32[3,64,128]{2,1,0:T(8,128)S(1)} %constant_dynamic-update-slice_fusion.3), channel_id=1, source_target_pairs={{0,1},{1,0},{2,3},{3,2},{4,5},{5,4},{6,7},{7,6},{8,9},{9,8},{10,11... | collective-permute-start | bytes 294920 | tf_op jit(solution)/shard_map/ppermute | solution.py:375
  12.6 0.0 collective-permute-done.1
  12.6 0.0 collective-permute-done.2
  12.7 0.7 %collective-permute-start.3 = (f32[3,64,128]{2,1,0:T(8,128)S(1)}, f32[3,64,128]{2,1,0:T(8,128)S(1)}, u32[]{:S(2)}, u32[]{:S(2)}) collective-permute-start(f32[3,64,128]{2,1,0:T(8,128)S(1)} %constant_dynamic-update-slice_fusion), channel_id=1, source_target_pairs={{1,2},{2,1},{5,6},{6,5},{9,10},{10,9},{13,14},{14,13},{17,18},{18,... | collective-permute-start | bytes 294920 | tf_op jit(solution)/shard_map/ppermute | solution.py:343
  13.3 3.8 %collective-permute-start.8 = (f32[3,64,128]{2,1,0:T(8,128)S(1)}, f32[3,64,128]{2,1,0:T(8,128)S(1)}, u32[]{:S(2)}, u32[]{:S(2)}) collective-permute-start(f32[3,64,128]{2,1,0:T(8,128)S(1)} %constant_dynamic-update-slice_fusion), channel_id=1, source_target_pairs={{0,2},{1,3},{2,0},{3,1},{4,6},{5,7},{6,4},{7,5},{8,10},{9,11},{10,... | collective-permute-start | bytes 294920 | tf_op jit(solution)/shard_map/ppermute | solution.py:343
  17.2 0.0 collective-permute-done.5
  17.2 0.2 collective-permute-start.7
  17.4 0.0 collective-permute-done.6
  17.4 0.0 collective-permute-done.4
  17.5 0.0 copy-start
  17.5 0.0 copy-start.1
  17.5 0.0 collective-permute-done.3
  17.5 0.0 copy-start.2
  17.6 0.1 collective-permute-start.9
  17.7 0.9 %copy-done = bf16[2,256,512]{2,1,0:T(8,128)(2,1)S(1)} copy-done((bf16[2,256,512]{2,1,0:T(8,128)(2,1)S(1)}, bf16[2,256,512]{2,1,0:T(8,128)(2,1)}, u32[]{:S(2)}) %copy-start) | copy-done | bytes 524312
  18.5 0.2 copy-done.1
  18.7 0.0 copy-done.2
  18.7 0.8 %shard_map.68 = (bf16[256,512]{1,0:T(8,128)(2,1)S(1)}, bf16[512,512]{1,0:T(8,128)(2,1)S(1)}, f32[4,2,128,128]{3,2,1,0:T(8,128)S(1)}) custom-call(s32[2,2]{1,0:T(2,128)S(1)} %copy-done.2, bf16[2,256,512]{2,1,0:T(8,128)(2,1)S(1)} %copy-done, bf16[512,512]{1,0:T(8,128)(2,1)S(1)} %copy-done.1), custom_call_target="tpu_custom_call" | custom-call | flops 100000000 | bytes 1048576 | tf_op jit(solution)/shard_map/pallas_call | solution.py:386
  19.5 0.4 %collective-permute-done.8 = f32[3,64,128]{2,1,0:T(8,128)S(1)} collective-permute-done((f32[3,64,128]{2,1,0:T(8,128)S(1)}, f32[3,64,128]{2,1,0:T(8,128)S(1)}, u32[]{:S(2)}, u32[]{:S(2)}) %collective-permute-start.8) | collective-permute-done | bytes 98336 | tf_op jit(solution)/shard_map/ppermute | solution.py:343
  19.9 1.9 %collective-permute-done.7 = f32[3,64,128]{2,1,0:T(8,128)S(1)} collective-permute-done((f32[3,64,128]{2,1,0:T(8,128)S(1)}, f32[3,64,128]{2,1,0:T(8,128)S(1)}, u32[]{:S(2)}, u32[]{:S(2)}) %collective-permute-start.7) | collective-permute-done | bytes 98336 | tf_op jit(solution)/shard_map/ppermute | solution.py:343
  21.8 0.1 collective-permute-start.10
  21.9 0.0 collective-permute-done.9.far_own
  21.9 0.1 shard_map.69
  22.0 0.4 %shard_map.70 = (f32[5,4,64,128]{3,2,1,0:T(8,128)S(1)}, f32[5,4,64,128]{3,2,1,0:T(8,128)S(1)}) custom-call(f32[4,3,64,128]{3,2,1,0:T(8,128)S(1)} %pad_maximum_fusion.1.near_rest, f32[4,64,128]{2,1,0:T(8,128)S(1)} %get-tuple-element.33.own_cos, f32[4,64,128]{2,1,0:T(8,128)S(1)} %get-tuple-element.34.own_sin), custom_call_target="tpu_custom_call" | custom-call | flops 500000000 | bytes 1048576 | tf_op jit(solution)/shard_map/pallas_call | solution.py:413
  22.4 1.2 %collective-permute-done.10.far_rest = f32[4,3,64,128]{3,2,1,0:T(8,128)S(1)} collective-permute-done((f32[4,3,64,128]{3,2,1,0:T(8,128)S(1)}, f32[4,3,64,128]{3,2,1,0:T(8,128)S(1)}, u32[]{:S(2)}, u32[]{:S(2)}) %collective-permute-start.10) | collective-permute-done | bytes 393248 | tf_op jit(solution)/shard_map/ppermute | solution.py:348
  23.6 7.3 %shard_map.71 = (f32[1,3,64,128]{3,2,1,0:T(8,128)S(1)}, f32[1,3,64,128]{3,2,1,0:T(8,128)S(1)}) custom-call(f32[4,2,128,128]{3,2,1,0:T(8,128)S(1)} %get-tuple-element.27.wave_ref, f32[5,4,64,128]{3,2,1,0:T(8,128)S(1)} %get-tuple-element.35.near_cos, f32[5,4,64,128]{3,2,1,0:T(8,128)S(1)} %get-tuple-element.36.near_sin, ...), custom_call_target="tpu_custom_call" | custom-call | tf_op jit(solution)/shard_map/pallas_call | solution.py:421
  30.9 0.2 collective-permute-start.11
  31.1 1.2 %collective-permute-done.11.received_ref = f32[1,3,64,128]{3,2,1,0:T(8,128)S(1)} collective-permute-done((f32[1,3,64,128]{3,2,1,0:T(8,128)S(1)}, f32[1,3,64,128]{3,2,1,0:T(8,128)S(1)}, u32[]{:S(2)}, u32[]{:S(2)}) %collective-permute-start.11) | collective-permute-done | bytes 98336 | tf_op jit(solution)/shard_map/ppermute | solution.py:348
  32.3 0.7 %shard_map.72 = (f32[1,64,128]{2,1,0:T(8,128)}, f32[2,1,2,64,128]{4,3,2,1,0:T(8,128)}) custom-call(f32[1,3,64,128]{3,2,1,0:T(8,128)S(1)} %get-tuple-element.40.mine_ref, f32[1,3,64,128]{3,2,1,0:T(8,128)S(1)} %collective-permute-done.11.received_ref), custom_call_target="tpu_custom_call" | custom-call | tf_op jit(solution)/shard_map/pallas_call | solution.py:436
  (9 shorter events, 0.1 us)
Async XLA Ops:
  0.6 8.2 %copy-start.3 = (f32[2,64,128]{2,1,0:T(8,128)S(1)}, f32[2,64,128]{2,1,0:T(8,128)}, u32[]{:S(2)}) copy-start(f32[2,64,128]{2,1,0:T(8,128)} %param.7) | copy-start | bytes 196612
  0.6 5.7 %collective-permute-start = (f32[1,64,128]{2,1,0:T(8,128)}, f32[1,64,128]{2,1,0:T(8,128)S(1)}, u32[]{:S(2)}, u32[]{:S(2)}) collective-permute-start(f32[1,64,128]{2,1,0:T(8,128)} %param.5), channel_id=1, source_target_pairs={{0,8},{8,0},{16,24},{24,16},{1,9},{9,1},{17,25},{25,17},{2,10},{10... | collective-permute-start | bytes 98312 | tf_op jit(solution)/shard_map/ppermute | solution.py:343
  3.7 8.9 %collective-permute-start.1 = (f32[1,64,128]{2,1,0:T(8,128)}, f32[1,64,128]{2,1,0:T(8,128)S(1)}, u32[]{:S(2)}, u32[]{:S(2)}) collective-permute-start(f32[1,64,128]{2,1,0:T(8,128)} %param.5), channel_id=1, source_target_pairs={{0,16},{8,24},{16,0},{24,8},{1,17},{9,25},{17,1},{25,9},{2,18},{10... | collective-permute-start | bytes 98312 | tf_op jit(solution)/shard_map/ppermute | solution.py:343
  6.3 6.3 %collective-permute-start.2 = (f32[1,64,128]{2,1,0:T(8,128)}, f32[1,64,128]{2,1,0:T(8,128)S(1)}, u32[]{:S(2)}, u32[]{:S(2)}) collective-permute-start(f32[1,64,128]{2,1,0:T(8,128)} %param.5), channel_id=1, source_target_pairs={{0,24},{8,16},{16,8},{24,0},{1,25},{9,17},{17,9},{25,1},{2,26},{10... | collective-permute-start | bytes 98312 | tf_op jit(solution)/shard_map/ppermute | solution.py:343
  7.1 10.0 %collective-permute-start.5 = (f32[1,64,128]{2,1,0:T(8,128)}, f32[1,64,128]{2,1,0:T(8,128)S(1)}, u32[]{:S(2)}, u32[]{:S(2)}) collective-permute-start(f32[1,64,128]{2,1,0:T(8,128)} %param.5), channel_id=1, source_target_pairs={{0,2},{1,3},{2,0},{3,1},{4,6},{5,7},{6,4},{7,5},{8,10},{9,11},{10,... | collective-permute-start | bytes 98312 | tf_op jit(solution)/shard_map/ppermute | solution.py:378
  8.9 8.6 %collective-permute-start.6 = (f32[3,64,128]{2,1,0:T(8,128)S(1)}, f32[3,64,128]{2,1,0:T(8,128)S(1)}, u32[]{:S(2)}, u32[]{:S(2)}) collective-permute-start(f32[3,64,128]{2,1,0:T(8,128)S(1)} %constant_dynamic-update-slice_fusion.3), channel_id=1, source_target_pairs={{1,2},{2,1},{5,6},{6,5},{9,10},{10,9},{13,14},{14,13},{17,18},{18,... | collective-permute-start | bytes 294920 | tf_op jit(solution)/shard_map/ppermute | solution.py:375
  9.5 7.9 %collective-permute-start.4 = (f32[3,64,128]{2,1,0:T(8,128)S(1)}, f32[3,64,128]{2,1,0:T(8,128)S(1)}, u32[]{:S(2)}, u32[]{:S(2)}) collective-permute-start(f32[3,64,128]{2,1,0:T(8,128)S(1)} %constant_dynamic-update-slice_fusion.3), channel_id=1, source_target_pairs={{0,1},{1,0},{2,3},{3,2},{4,5},{5,4},{6,7},{7,6},{8,9},{9,8},{10,11... | collective-permute-start | bytes 294920 | tf_op jit(solution)/shard_map/ppermute | solution.py:375
  12.7 4.8 %collective-permute-start.3 = (f32[3,64,128]{2,1,0:T(8,128)S(1)}, f32[3,64,128]{2,1,0:T(8,128)S(1)}, u32[]{:S(2)}, u32[]{:S(2)}) collective-permute-start(f32[3,64,128]{2,1,0:T(8,128)S(1)} %constant_dynamic-update-slice_fusion), channel_id=1, source_target_pairs={{1,2},{2,1},{5,6},{6,5},{9,10},{10,9},{13,14},{14,13},{17,18},{18,... | collective-permute-start | bytes 294920 | tf_op jit(solution)/shard_map/ppermute | solution.py:343
  13.3 6.5 %collective-permute-start.8 = (f32[3,64,128]{2,1,0:T(8,128)S(1)}, f32[3,64,128]{2,1,0:T(8,128)S(1)}, u32[]{:S(2)}, u32[]{:S(2)}) collective-permute-start(f32[3,64,128]{2,1,0:T(8,128)S(1)} %constant_dynamic-update-slice_fusion), channel_id=1, source_target_pairs={{0,2},{1,3},{2,0},{3,1},{4,6},{5,7},{6,4},{7,5},{8,10},{9,11},{10,... | collective-permute-start | bytes 294920 | tf_op jit(solution)/shard_map/ppermute | solution.py:343
  17.2 4.6 %collective-permute-start.7 = (f32[3,64,128]{2,1,0:T(8,128)S(1)}, f32[3,64,128]{2,1,0:T(8,128)S(1)}, u32[]{:S(2)}, u32[]{:S(2)}) collective-permute-start(f32[3,64,128]{2,1,0:T(8,128)S(1)} %constant_dynamic-update-slice_fusion), channel_id=1, source_target_pairs={{0,1},{1,0},{2,3},{3,2},{4,5},{5,4},{6,7},{7,6},{8,9},{9,8},{10,11... | collective-permute-start | bytes 294920 | tf_op jit(solution)/shard_map/ppermute | solution.py:343
  17.5 1.0 %copy-start = (bf16[2,256,512]{2,1,0:T(8,128)(2,1)S(1)}, bf16[2,256,512]{2,1,0:T(8,128)(2,1)}, u32[]{:S(2)}) copy-start(bf16[2,256,512]{2,1,0:T(8,128)(2,1)} %constant.19.clone.row_from) | copy-start | bytes 1572868
  17.5 1.2 %copy-start.1 = (bf16[512,512]{1,0:T(8,128)(2,1)S(1)}, bf16[512,512]{1,0:T(8,128)(2,1)}, u32[]{:S(2)}) copy-start(bf16[512,512]{1,0:T(8,128)(2,1)} %constant.20.clone.col_from) | copy-start | bytes 1572868
  17.5 1.1 %copy-start.2 = (s32[2,2]{1,0:T(2,128)S(1)}, s32[2,2]{1,0:T(2,128)}, u32[]{:S(2)}) copy-start(s32[2,2]{1,0:T(2,128)} %tilt_ref.1) | copy-start | bytes 52
  17.6 4.3 %collective-permute-start.9 = (f32[4,2,64,128]{3,2,1,0:T(8,128)S(1)}, f32[4,2,64,128]{3,2,1,0:T(8,128)S(1)}, u32[]{:S(2)}, u32[]{:S(2)}) collective-permute-start(f32[4,2,64,128]{3,2,1,0:T(8,128)S(1)} %pad_maximum_fusion.2), channel_id=1, source_target_pairs={{0,4},{4,0},{1,5},{5,1},{2,6},{6,2},{3,7},{7,3},{8,12},{12,8},{9,1... | collective-permute-start | bytes 786440 | tf_op jit(solution)/shard_map/ppermute | solution.py:348
  21.8 1.8 %collective-permute-start.10 = (f32[4,3,64,128]{3,2,1,0:T(8,128)S(1)}, f32[4,3,64,128]{3,2,1,0:T(8,128)S(1)}, u32[]{:S(2)}, u32[]{:S(2)}) collective-permute-start(f32[4,3,64,128]{3,2,1,0:T(8,128)S(1)} %pad_maximum_fusion.1.near_rest), channel_id=1, source_target_pairs={{0,4},{4,0},{1,5},{5,1},{2,6},{6,2},{3,7},{7,3},{8,12},{12,8},{9,1... | collective-permute-start | bytes 1179656 | tf_op jit(solution)/shard_map/ppermute | solution.py:348
  30.9 1.4 %collective-permute-start.11 = (f32[1,3,64,128]{3,2,1,0:T(8,128)S(1)}, f32[1,3,64,128]{3,2,1,0:T(8,128)S(1)}, u32[]{:S(2)}, u32[]{:S(2)}) collective-permute-start(f32[1,3,64,128]{3,2,1,0:T(8,128)S(1)} %get-tuple-element.41), channel_id=1, source_target_pairs={{0,4},{4,0},{1,5},{5,1},{2,6},{6,2},{3,7},{7,3},{8,12},{12,8},{9,1... | collective-permute-start | bytes 294920 | tf_op jit(solution)/shard_map/ppermute | solution.py:348

commit v20 on v19

--- a/solution.py
+++ b/solution.py
@@ -380,7 +380,7 @@
     near_own = jnp.stack(near_own)
     arriving = spread(other_depths, "col", 2)
     row_all, col_all = jnp.asarray(row_constant(height)), jnp.asarray(col_constant())
-    arriving[2], near_own, row_all, col_all = lax.optimization_barrier((arriving[2], near_own, row_all, col_all))
+    near_own, row_all, col_all = lax.optimization_barrier((near_own, row_all, col_all))
     half_screens = (count + 1, blocks, tile_r, tile_c)
     field = (blocks, 2, height, tile_c)
     row_matrix, col_matrix, wave = pl.pallas_call(
@@ -396,7 +396,9 @@
         compiler_params=params(4),
         cost_estimate=pl.CostEstimate(flops=10**8, bytes_accessed=2**20, transcendentals=0),
     )(tilt, row_all, col_all)
-    arriving[1], row_matrix, col_matrix = lax.optimization_barrier((arriving[1], row_matrix, col_matrix))
+    arriving[2], near_own, row_matrix, col_matrix, wave = lax.optimization_barrier(
+        (arriving[2], near_own, row_matrix, col_matrix, wave)
+    )
     near_rest = jnp.stack([other_depths] + arriving)
     wanted = lax.dynamic_slice_in_dim(near_own, 2 - core, 1, 1)
     far_own = swap_cores(jnp.concatenate([near_own[:, :1], wanted], axis=1))
@@ -408,7 +410,7 @@
         in_specs=[vmem, vmem],
         out_specs=(vmem,) * 3,
         compiler_params=params(8),
-        cost_estimate=pl.CostEstimate(flops=3 * 10**9, bytes_accessed=2**20, transcendentals=0),
+        cost_estimate=pl.CostEstimate(flops=2 * 10**9, bytes_accessed=2**20, transcendentals=0),
     )(near_own, far_own)
     near_cos, near_sin = pl.pallas_call(
         second_kernel,

time: 33.2 us -> 33.2 us (level)
  local copies, waits for them, and re-layouts: 1.91 us -> 1.5 us
    ppermute x1, starting transfers between devices: 1.71 us -> 3.12 us  [whole_field_body(): lax.ppermute(slab, 'col', further)]
    ppermute x2, starting transfers between devices: 3.76 us -> 2.4 us  [whole_field_body(): near_own.append(lax.ppermute(packet, 'col', close))]
    unnamed x11 -> x13, local copies, waits for them, and re-layouts: 1.87 us -> 1.46 us
where the time goes in v20:
time: 33.2 us; the launch traced here: 33 us
  starting transfers between devices  16.4 us (49%)
  Pallas kernels  9.24 us (28%)
  waiting for transfers between devices  4.94 us (15%)
  local copies, waits for them, and re-layouts  1.5 us (5%)
  between operations  0.82 us (2%)
    ppermute x6, starting transfers between devices, spread(): lax.ppermute(shard, axis, pairs)  10.6 us
    pallas_call x1, Pallas kernels, whole_field_body(): pl.pallas_call(wave_kernel, out_shape=(array(1, 3, tile_r, tile_c),) * 2,...  7.3 us
    ppermute x1, starting transfers between devices, whole_field_body(): lax.ppermute(slab, 'col', further)  3.12 us
    ppermute x6, waiting for transfers between devices, spread(): lax.ppermute(shard, axis, pairs)  2.55 us
    ppermute x2, starting transfers between devices, whole_field_body(): near_own.append(lax.ppermute(packet, 'col', close))  2.4 us
    ppermute x3, waiting for transfers between devices, swap_cores(): return lax.ppermute(value, 'row', [(0, 1), (1, 0)])  2.38 us
    unnamed x13, local copies, waits for them, and re-layouts  1.46 us
    pallas_call x1, Pallas kernels, whole_field_body(): pl.pallas_call(load_kernel, out_shape=(jax.ShapeDtypeStruct(row_all.shape...  0.79 us
  transfers between devices with their start and end apart: 12, of which 4 were waited for; matrix products, arithmetic and copies ran while one was open for 3% of the time, Pallas kernels for 4%

profile of v20, /device:TPU:0, one launch (start us, length us, event | category | flops | bytes accessed | tf_op | source)
XLA Modules:
  0.0 33.0 jit_solution(4346647946533945819)
XLA Ops:
  0.6 0.0 copy-start.3
  0.6 3.1 %collective-permute-start = (f32[1,64,128]{2,1,0:T(8,128)}, f32[1,64,128]{2,1,0:T(8,128)S(1)}, u32[]{:S(2)}, u32[]{:S(2)}) collective-permute-start(f32[1,64,128]{2,1,0:T(8,128)} %param.5), channel_id=1, source_target_pairs={{0,8},{8,0},{16,24},{24,16},{1,9},{9,1},{17,25},{25,17},{2,10},{10... | collective-permute-start | bytes 98312 | tf_op jit(solution)/shard_map/ppermute | solution.py:343
  3.7 2.6 %collective-permute-start.1 = (f32[1,64,128]{2,1,0:T(8,128)}, f32[1,64,128]{2,1,0:T(8,128)S(1)}, u32[]{:S(2)}, u32[]{:S(2)}) collective-permute-start(f32[1,64,128]{2,1,0:T(8,128)} %param.5), channel_id=1, source_target_pairs={{0,16},{8,24},{16,0},{24,8},{1,17},{9,25},{17,1},{25,9},{2,18},{10... | collective-permute-start | bytes 98312 | tf_op jit(solution)/shard_map/ppermute | solution.py:343
  6.3 0.0 collective-permute-start.2
  6.3 0.0 collective-permute-done
  6.3 0.8 %constant_dynamic-update-slice_fusion.4 = f32[3,64,128]{2,1,0:T(8,128)S(1)} fusion(f32[1,64,128]{2,1,0:T(8,128)} %param.5), kind=kLoop, calls=%fused_computation.8 | loop fusion | bytes 65536
  7.1 0.0 copy-done.3
  7.2 0.0 copy-start.4
  7.2 1.7 %collective-permute-start.4 = (f32[3,64,128]{2,1,0:T(8,128)S(1)}, f32[3,64,128]{2,1,0:T(8,128)S(1)}, u32[]{:S(2)}, u32[]{:S(2)}) collective-permute-start(f32[3,64,128]{2,1,0:T(8,128)S(1)} %constant_dynamic-update-slice_fusion.3), channel_id=1, source_target_pairs={{0,1},{1,0},{2,3},{3,2},{4,5},{5,4},{6,7},{7,6},{8,9},{9,8},{10,11... | collective-permute-start | bytes 294920 | tf_op jit(solution)/shard_map/ppermute | solution.py:375
  8.9 0.7 %collective-permute-start.6 = (f32[3,64,128]{2,1,0:T(8,128)S(1)}, f32[3,64,128]{2,1,0:T(8,128)S(1)}, u32[]{:S(2)}, u32[]{:S(2)}) collective-permute-start(f32[3,64,128]{2,1,0:T(8,128)S(1)} %constant_dynamic-update-slice_fusion.3), channel_id=1, source_target_pairs={{1,2},{2,1},{5,6},{6,5},{9,10},{10,9},{13,14},{14,13},{17,18},{18,... | collective-permute-start | bytes 294920 | tf_op jit(solution)/shard_map/ppermute | solution.py:375
  9.6 0.0 copy-done.4
  9.6 3.1 %collective-permute-start.5 = (f32[1,64,128]{2,1,0:T(8,128)S(1)}, f32[1,64,128]{2,1,0:T(8,128)S(1)}, u32[]{:S(2)}, u32[]{:S(2)}) collective-permute-start(f32[1,64,128]{2,1,0:T(8,128)S(1)} %copy-done.4), channel_id=1, source_target_pairs={{0,2},{1,3},{2,0},{3,1},{4,6},{5,7},{6,4},{7,5},{8,10},{9,11},{10,... | collective-permute-start | bytes 98312 | tf_op jit(solution)/shard_map/ppermute | solution.py:378
  12.7 0.0 copy-start
  12.7 0.0 copy-start.1
  12.7 0.0 collective-permute-done.1
  12.7 0.0 collective-permute-done.2
  12.7 0.8 %collective-permute-start.3 = (f32[3,64,128]{2,1,0:T(8,128)S(1)}, f32[3,64,128]{2,1,0:T(8,128)S(1)}, u32[]{:S(2)}, u32[]{:S(2)}) collective-permute-start(f32[3,64,128]{2,1,0:T(8,128)S(1)} %constant_dynamic-update-slice_fusion), channel_id=1, source_target_pairs={{1,2},{2,1},{5,6},{6,5},{9,10},{10,9},{13,14},{14,13},{17,18},{18,... | collective-permute-start | bytes 294920 | tf_op jit(solution)/shard_map/ppermute | solution.py:343
  13.6 3.6 %collective-permute-start.7 = (f32[3,64,128]{2,1,0:T(8,128)S(1)}, f32[3,64,128]{2,1,0:T(8,128)S(1)}, u32[]{:S(2)}, u32[]{:S(2)}) collective-permute-start(f32[3,64,128]{2,1,0:T(8,128)S(1)} %constant_dynamic-update-slice_fusion), channel_id=1, source_target_pairs={{0,1},{1,0},{2,3},{3,2},{4,5},{5,4},{6,7},{7,6},{8,9},{9,8},{10,11... | collective-permute-start | bytes 294920 | tf_op jit(solution)/shard_map/ppermute | solution.py:343
  17.2 0.0 collective-permute-done.5
  17.2 0.4 %collective-permute-start.8 = (f32[3,64,128]{2,1,0:T(8,128)S(1)}, f32[3,64,128]{2,1,0:T(8,128)S(1)}, u32[]{:S(2)}, u32[]{:S(2)}) collective-permute-start(f32[3,64,128]{2,1,0:T(8,128)S(1)} %constant_dynamic-update-slice_fusion), channel_id=1, source_target_pairs={{0,2},{1,3},{2,0},{3,1},{4,6},{5,7},{6,4},{7,5},{8,10},{9,11},{10,... | collective-permute-start | bytes 294920 | tf_op jit(solution)/shard_map/ppermute | solution.py:343
  17.6 0.0 collective-permute-done.4
  17.6 0.0 collective-permute-done.6
  17.7 0.0 copy-start.2
  17.7 0.0 copy-done
  17.7 0.0 copy-done.1
  17.7 0.6 %copy-done.2 = s32[2,2]{1,0:T(2,128)S(1)} copy-done((s32[2,2]{1,0:T(2,128)S(1)}, s32[2,2]{1,0:T(2,128)}, u32[]{:S(2)}) %copy-start.2) | copy-done | bytes 40
  18.3 0.8 %shard_map.68 = (bf16[256,512]{1,0:T(8,128)(2,1)S(1)}, bf16[512,512]{1,0:T(8,128)(2,1)S(1)}, f32[4,2,128,128]{3,2,1,0:T(8,128)S(1)}) custom-call(s32[2,2]{1,0:T(2,128)S(1)} %copy-done.2, bf16[2,256,512]{2,1,0:T(8,128)(2,1)S(1)} %copy-done, bf16[512,512]{1,0:T(8,128)(2,1)S(1)} %copy-done.1), custom_call_target="tpu_custom_call" | custom-call | flops 100000000 | bytes 1048576 | tf_op jit(solution)/shard_map/pallas_call | solution.py:386
  19.1 0.0 collective-permute-done.3
  19.2 0.1 collective-permute-start.9
  19.3 1.5 %collective-permute-done.7 = f32[3,64,128]{2,1,0:T(8,128)S(1)} collective-permute-done((f32[3,64,128]{2,1,0:T(8,128)S(1)}, f32[3,64,128]{2,1,0:T(8,128)S(1)}, u32[]{:S(2)}, u32[]{:S(2)}) %collective-permute-start.7) | collective-permute-done | bytes 98336 | tf_op jit(solution)/shard_map/ppermute | solution.py:343
  20.8 1.1 %collective-permute-done.8 = f32[3,64,128]{2,1,0:T(8,128)S(1)} collective-permute-done((f32[3,64,128]{2,1,0:T(8,128)S(1)}, f32[3,64,128]{2,1,0:T(8,128)S(1)}, u32[]{:S(2)}, u32[]{:S(2)}) %collective-permute-start.8) | collective-permute-done | bytes 98336 | tf_op jit(solution)/shard_map/ppermute | solution.py:343
  21.9 0.1 collective-permute-start.10
  21.9 0.0 collective-permute-done.9.far_own
  21.9 0.1 shard_map.69
  22.1 0.4 %shard_map.70 = (f32[5,4,64,128]{3,2,1,0:T(8,128)S(1)}, f32[5,4,64,128]{3,2,1,0:T(8,128)S(1)}) custom-call(f32[4,3,64,128]{3,2,1,0:T(8,128)S(1)} %pad_maximum_fusion.1.near_rest, f32[4,64,128]{2,1,0:T(8,128)S(1)} %get-tuple-element.35.own_cos, f32[4,64,128]{2,1,0:T(8,128)S(1)} %get-tuple-element.36.own_sin), custom_call_target="tpu_custom_call" | custom-call | flops 500000000 | bytes 1048576 | tf_op jit(solution)/shard_map/pallas_call | solution.py:415
  22.4 1.2 %collective-permute-done.10.far_rest = f32[4,3,64,128]{3,2,1,0:T(8,128)S(1)} collective-permute-done((f32[4,3,64,128]{3,2,1,0:T(8,128)S(1)}, f32[4,3,64,128]{3,2,1,0:T(8,128)S(1)}, u32[]{:S(2)}, u32[]{:S(2)}) %collective-permute-start.10) | collective-permute-done | bytes 393248 | tf_op jit(solution)/shard_map/ppermute | solution.py:348
  23.6 7.3 %shard_map.71 = (f32[1,3,64,128]{3,2,1,0:T(8,128)S(1)}, f32[1,3,64,128]{3,2,1,0:T(8,128)S(1)}) custom-call(f32[4,2,128,128]{3,2,1,0:T(8,128)S(1)} %get-tuple-element.32.wave_ref, f32[5,4,64,128]{3,2,1,0:T(8,128)S(1)} %get-tuple-element.37.near_cos, f32[5,4,64,128]{3,2,1,0:T(8,128)S(1)} %get-tuple-element.38.near_sin, ...), custom_call_target="tpu_custom_call" | custom-call | tf_op jit(solution)/shard_map/pallas_call | solution.py:423
  30.9 0.2 collective-permute-start.11
  31.1 1.2 %collective-permute-done.11.received_ref = f32[1,3,64,128]{3,2,1,0:T(8,128)S(1)} collective-permute-done((f32[1,3,64,128]{3,2,1,0:T(8,128)S(1)}, f32[1,3,64,128]{3,2,1,0:T(8,128)S(1)}, u32[]{:S(2)}, u32[]{:S(2)}) %collective-permute-start.11) | collective-permute-done | bytes 98336 | tf_op jit(solution)/shard_map/ppermute | solution.py:348
  32.3 0.7 %shard_map.72 = (f32[1,64,128]{2,1,0:T(8,128)}, f32[2,1,2,64,128]{4,3,2,1,0:T(8,128)}) custom-call(f32[1,3,64,128]{3,2,1,0:T(8,128)S(1)} %get-tuple-element.42.mine_ref, f32[1,3,64,128]{3,2,1,0:T(8,128)S(1)} %collective-permute-done.11.received_ref), custom_call_target="tpu_custom_call" | custom-call | tf_op jit(solution)/shard_map/pallas_call | solution.py:438
  (9 shorter events, 0.1 us)
Async XLA Ops:
  0.6 6.5 %copy-start.3 = (f32[2,64,128]{2,1,0:T(8,128)S(1)}, f32[2,64,128]{2,1,0:T(8,128)}, u32[]{:S(2)}) copy-start(f32[2,64,128]{2,1,0:T(8,128)} %param.7) | copy-start | bytes 196612
  0.6 5.7 %collective-permute-start = (f32[1,64,128]{2,1,0:T(8,128)}, f32[1,64,128]{2,1,0:T(8,128)S(1)}, u32[]{:S(2)}, u32[]{:S(2)}) collective-permute-start(f32[1,64,128]{2,1,0:T(8,128)} %param.5), channel_id=1, source_target_pairs={{0,8},{8,0},{16,24},{24,16},{1,9},{9,1},{17,25},{25,17},{2,10},{10... | collective-permute-start | bytes 98312 | tf_op jit(solution)/shard_map/ppermute | solution.py:343
  3.7 9.0 %collective-permute-start.1 = (f32[1,64,128]{2,1,0:T(8,128)}, f32[1,64,128]{2,1,0:T(8,128)S(1)}, u32[]{:S(2)}, u32[]{:S(2)}) collective-permute-start(f32[1,64,128]{2,1,0:T(8,128)} %param.5), channel_id=1, source_target_pairs={{0,16},{8,24},{16,0},{24,8},{1,17},{9,25},{17,1},{25,9},{2,18},{10... | collective-permute-start | bytes 98312 | tf_op jit(solution)/shard_map/ppermute | solution.py:343
  6.3 6.4 %collective-permute-start.2 = (f32[1,64,128]{2,1,0:T(8,128)}, f32[1,64,128]{2,1,0:T(8,128)S(1)}, u32[]{:S(2)}, u32[]{:S(2)}) collective-permute-start(f32[1,64,128]{2,1,0:T(8,128)} %param.5), channel_id=1, source_target_pairs={{0,24},{8,16},{16,8},{24,0},{1,25},{9,17},{17,9},{25,1},{2,26},{10... | collective-permute-start | bytes 98312 | tf_op jit(solution)/shard_map/ppermute | solution.py:343
  7.2 2.4 %copy-start.4 = (f32[1,64,128]{2,1,0:T(8,128)S(1)}, f32[1,64,128]{2,1,0:T(8,128)}, u32[]{:S(2)}) copy-start(f32[1,64,128]{2,1,0:T(8,128)} %param.5) | copy-start | bytes 98308
  7.2 10.5 %collective-permute-start.4 = (f32[3,64,128]{2,1,0:T(8,128)S(1)}, f32[3,64,128]{2,1,0:T(8,128)S(1)}, u32[]{:S(2)}, u32[]{:S(2)}) collective-permute-start(f32[3,64,128]{2,1,0:T(8,128)S(1)} %constant_dynamic-update-slice_fusion.3), channel_id=1, source_target_pairs={{0,1},{1,0},{2,3},{3,2},{4,5},{5,4},{6,7},{7,6},{8,9},{9,8},{10,11... | collective-permute-start | bytes 294920 | tf_op jit(solution)/shard_map/ppermute | solution.py:375
  8.9 8.7 %collective-permute-start.6 = (f32[3,64,128]{2,1,0:T(8,128)S(1)}, f32[3,64,128]{2,1,0:T(8,128)S(1)}, u32[]{:S(2)}, u32[]{:S(2)}) collective-permute-start(f32[3,64,128]{2,1,0:T(8,128)S(1)} %constant_dynamic-update-slice_fusion.3), channel_id=1, source_target_pairs={{1,2},{2,1},{5,6},{6,5},{9,10},{10,9},{13,14},{14,13},{17,18},{18,... | collective-permute-start | bytes 294920 | tf_op jit(solution)/shard_map/ppermute | solution.py:375
  9.6 7.6 %collective-permute-start.5 = (f32[1,64,128]{2,1,0:T(8,128)S(1)}, f32[1,64,128]{2,1,0:T(8,128)S(1)}, u32[]{:S(2)}, u32[]{:S(2)}) collective-permute-start(f32[1,64,128]{2,1,0:T(8,128)S(1)} %copy-done.4), channel_id=1, source_target_pairs={{0,2},{1,3},{2,0},{3,1},{4,6},{5,7},{6,4},{7,5},{8,10},{9,11},{10,... | collective-permute-start | bytes 98312 | tf_op jit(solution)/shard_map/ppermute | solution.py:378
  12.7 5.0 %copy-start = (bf16[2,256,512]{2,1,0:T(8,128)(2,1)S(1)}, bf16[2,256,512]{2,1,0:T(8,128)(2,1)}, u32[]{:S(2)}) copy-start(bf16[2,256,512]{2,1,0:T(8,128)(2,1)} %constant.19.clone.row_from) | copy-start | bytes 1572868
  12.7 5.0 %copy-start.1 = (bf16[512,512]{1,0:T(8,128)(2,1)S(1)}, bf16[512,512]{1,0:T(8,128)(2,1)}, u32[]{:S(2)}) copy-start(bf16[512,512]{1,0:T(8,128)(2,1)} %constant.20.clone.col_from) | copy-start | bytes 1572868
  12.7 6.4 %collective-permute-start.3 = (f32[3,64,128]{2,1,0:T(8,128)S(1)}, f32[3,64,128]{2,1,0:T(8,128)S(1)}, u32[]{:S(2)}, u32[]{:S(2)}) collective-permute-start(f32[3,64,128]{2,1,0:T(8,128)S(1)} %constant_dynamic-update-slice_fusion), channel_id=1, source_target_pairs={{1,2},{2,1},{5,6},{6,5},{9,10},{10,9},{13,14},{14,13},{17,18},{18,... | collective-permute-start | bytes 294920 | tf_op jit(solution)/shard_map/ppermute | solution.py:343
  13.6 7.2 %collective-permute-start.7 = (f32[3,64,128]{2,1,0:T(8,128)S(1)}, f32[3,64,128]{2,1,0:T(8,128)S(1)}, u32[]{:S(2)}, u32[]{:S(2)}) collective-permute-start(f32[3,64,128]{2,1,0:T(8,128)S(1)} %constant_dynamic-update-slice_fusion), channel_id=1, source_target_pairs={{0,1},{1,0},{2,3},{3,2},{4,5},{5,4},{6,7},{7,6},{8,9},{9,8},{10,11... | collective-permute-start | bytes 294920 | tf_op jit(solution)/shard_map/ppermute | solution.py:343
  17.2 4.6 %collective-permute-start.8 = (f32[3,64,128]{2,1,0:T(8,128)S(1)}, f32[3,64,128]{2,1,0:T(8,128)S(1)}, u32[]{:S(2)}, u32[]{:S(2)}) collective-permute-start(f32[3,64,128]{2,1,0:T(8,128)S(1)} %constant_dynamic-update-slice_fusion), channel_id=1, source_target_pairs={{0,2},{1,3},{2,0},{3,1},{4,6},{5,7},{6,4},{7,5},{8,10},{9,11},{10,... | collective-permute-start | bytes 294920 | tf_op jit(solution)/shard_map/ppermute | solution.py:343
  17.7 0.7 %copy-start.2 = (s32[2,2]{1,0:T(2,128)S(1)}, s32[2,2]{1,0:T(2,128)}, u32[]{:S(2)}) copy-start(s32[2,2]{1,0:T(2,128)} %tilt_ref.1) | copy-start | bytes 52
  19.2 2.7 %collective-permute-start.9 = (f32[4,2,64,128]{3,2,1,0:T(8,128)S(1)}, f32[4,2,64,128]{3,2,1,0:T(8,128)S(1)}, u32[]{:S(2)}, u32[]{:S(2)}) collective-permute-start(f32[4,2,64,128]{3,2,1,0:T(8,128)S(1)} %pad_maximum_fusion.2), channel_id=1, source_target_pairs={{0,4},{4,0},{1,5},{5,1},{2,6},{6,2},{3,7},{7,3},{8,12},{12,8},{9,1... | collective-permute-start | bytes 786440 | tf_op jit(solution)/shard_map/ppermute | solution.py:348
  21.9 1.8 %collective-permute-start.10 = (f32[4,3,64,128]{3,2,1,0:T(8,128)S(1)}, f32[4,3,64,128]{3,2,1,0:T(8,128)S(1)}, u32[]{:S(2)}, u32[]{:S(2)}) collective-permute-start(f32[4,3,64,128]{3,2,1,0:T(8,128)S(1)} %pad_maximum_fusion.1.near_rest), channel_id=1, source_target_pairs={{0,4},{4,0},{1,5},{5,1},{2,6},{6,2},{3,7},{7,3},{8,12},{12,8},{9,1... | collective-permute-start | bytes 1179656 | tf_op jit(solution)/shard_map/ppermute | solution.py:348
  30.9 1.4 %collective-permute-start.11 = (f32[1,3,64,128]{3,2,1,0:T(8,128)S(1)}, f32[1,3,64,128]{3,2,1,0:T(8,128)S(1)}, u32[]{:S(2)}, u32[]{:S(2)}) collective-permute-start(f32[1,3,64,128]{3,2,1,0:T(8,128)S(1)} %get-tuple-element.43), channel_id=1, source_target_pairs={{0,4},{4,0},{1,5},{5,1},{2,6},{6,2},{3,7},{7,3},{8,12},{12,8},{9,1... | collective-permute-start | bytes 294920 | tf_op jit(solution)/shard_map/ppermute | solution.py:348

commit v21 on v20

--- a/solution.py
+++ b/solution.py
@@ -178,7 +178,7 @@
         wave_ref[place, 0], wave_ref[place, 1] = wave
 
 
-def load_kernel(tilt_ref, row_from, col_from, row_to, col_to, wave_ref, sems):
+def load_kernel(tilt_ref, near_own, row_from, col_from, row_to, col_to, wave_ref, cos_ref, sin_ref, sems):
     blocks, _, height, _ = wave_ref.shape
     core = lax.axis_index("row")
     copies = [
@@ -187,6 +187,8 @@
     ]
     for copy in copies:
         copy.start()
+    for col in range(blocks):
+        cos_ref[col], sin_ref[col] = cos_sin(near_own[col ^ lax.axis_index("col"), 0])
 
     def cycles(number, position, extent):
         fraction = (number * position).astype(jnp.float32) / extent
@@ -208,14 +210,6 @@
         copy.wait()
 
 
-def first_kernel(near_own, far_own, measured_ref, cos_ref, sin_ref):
-    core, own_place = lax.axis_index("row"), lax.axis_index("col")
-    for col in range(measured_ref.shape[0]):
-        held = col ^ own_place
-        measured_ref[col] = jnp.concatenate([near_own[held, 1 + core], far_own[held, 1]], axis=0)
-        cos_ref[col], sin_ref[col] = cos_sin(near_own[held, 0])
-
-
 def second_kernel(near_rest, own_cos, own_sin, cos_ref, sin_ref):
     blocks = own_cos.shape[0]
     count = cos_ref.shape[0] - 1
@@ -234,7 +228,7 @@
 
 
 def wave_kernel(
-    wave_ref, near_cos, near_sin, measured_ref, far_own, far_rest, row_ref, col_ref,
+    wave_ref, near_cos, near_sin, near_own, far_first, far_second, row_ref, col_ref,
     mine_ref, theirs_ref, far_cos, far_sin, kept_ref, moved_ref, left_ref, grad_ref, even_edge, odd_edge,
 ):
     blocks, _, height, _ = wave_ref.shape
@@ -252,7 +246,10 @@
         bits = slice_index ^ own_section
         for col in range(blocks):
             held = col ^ own_place
-            angle = jnp.where(bits == 0, far_own[held, 0], far_rest[held, jnp.maximum(bits - 1, 0)])
+            others = jnp.maximum(bits - 1, 0)
+            in_first = (bits == 0) | (held == 3)
+            place = jnp.where(bits == 0, 2 * held, 2 * blocks + others)
+            angle = jnp.where(in_first, far_first[place], far_second[jnp.minimum(held, 2) * (count - 1) + others])
             far_cos[slice_index, col], far_sin[slice_index, col] = cos_sin(angle)
 
     for edge_ref in edges:
@@ -278,7 +275,9 @@
     for place in range(window):
         block = window_start + place
         real, imag = kept_ref[block, 0], kept_ref[block, 1]
-        misfit = 2.0 * (real * real + imag * imag - measured_ref[block])
+        held = block ^ own_place
+        measured = jnp.concatenate([near_own[held, 1 + core], far_first[2 * held + 1]], axis=0)
+        misfit = 2.0 * (real * real + imag * imag - measured)
         waves.append((misfit * real, -misfit * imag))
 
     for tick in range(count - 1):
@@ -383,35 +382,30 @@
     near_own, row_all, col_all = lax.optimization_barrier((near_own, row_all, col_all))
     half_screens = (count + 1, blocks, tile_r, tile_c)
     field = (blocks, 2, height, tile_c)
-    row_matrix, col_matrix, wave = pl.pallas_call(
+    row_matrix, col_matrix, wave, own_cos, own_sin = pl.pallas_call(
         load_kernel,
         out_shape=(
             jax.ShapeDtypeStruct(row_all.shape[1:], row_all.dtype),
             jax.ShapeDtypeStruct(col_all.shape, col_all.dtype),
             array(*field),
+            array(blocks, tile_r, tile_c),
+            array(blocks, tile_r, tile_c),
         ),
-        in_specs=[smem, hbm, hbm],
-        out_specs=(vmem, vmem, vmem),
+        in_specs=[smem, vmem, hbm, hbm],
+        out_specs=(vmem,) * 5,
         scratch_shapes=[pltpu.SemaphoreType.DMA((2,))],
         compiler_params=params(4),
         cost_estimate=pl.CostEstimate(flops=10**8, bytes_accessed=2**20, transcendentals=0),
-    )(tilt, row_all, col_all)
-    arriving[2], near_own, row_matrix, col_matrix, wave = lax.optimization_barrier(
-        (arriving[2], near_own, row_matrix, col_matrix, wave)
+    )(tilt, near_own, row_all, col_all)
+    arriving[2], near_own, row_matrix, col_matrix, wave, own_cos, own_sin = lax.optimization_barrier(
+        (arriving[2], near_own, row_matrix, col_matrix, wave, own_cos, own_sin)
     )
+    wanted = lax.dynamic_slice_in_dim(near_own, 2 - core, 1, 1)
+    packets = jnp.concatenate([near_own[:, :1], wanted], axis=1).reshape(2 * blocks, tile_r, tile_c)
+    far_first = swap_cores(jnp.concatenate([packets, arriving[2]], axis=0))
+    far_second = swap_cores(jnp.concatenate([other_depths] + arriving[:2], axis=0))
     near_rest = jnp.stack([other_depths] + arriving)
-    wanted = lax.dynamic_slice_in_dim(near_own, 2 - core, 1, 1)
-    far_own = swap_cores(jnp.concatenate([near_own[:, :1], wanted], axis=1))
-    far_rest = swap_cores(near_rest)
-
-    measured, own_cos, own_sin = pl.pallas_call(
-        first_kernel,
-        out_shape=(array(blocks, height, tile_c),) + (array(blocks, tile_r, tile_c),) * 2,
-        in_specs=[vmem, vmem],
-        out_specs=(vmem,) * 3,
-        compiler_params=params(8),
-        cost_estimate=pl.CostEstimate(flops=2 * 10**9, bytes_accessed=2**20, transcendentals=0),
-    )(near_own, far_own)
+
     near_cos, near_sin = pl.pallas_call(
         second_kernel,
         out_shape=(array(*half_screens),) * 2,
@@ -432,7 +426,7 @@
         + [pltpu.VMEM((blocks, height, 2 * LANES), jnp.bfloat16)] * 2,
         compiler_params=params(24),
     )(
-        wave, near_cos, near_sin, measured, far_own, far_rest,
+        wave, near_cos, near_sin, near_own, far_first, far_second,
         row_matrix, col_matrix,
     )
     return pl.pallas_call(

time: 33.2 us -> 33.1 us (level)
    ppermute x1, starting transfers between devices: 3.12 us -> 1.71 us  [whole_field_body(): lax.ppermute(slab, 'col', further)]
    ppermute x2, starting transfers between devices: 2.4 us -> 3.76 us  [whole_field_body(): near_own.append(lax.ppermute(packet, 'col', close))]
  transfers between devices with their start and end apart: 12 -> 12, of which waited for: 4 -> 3; matrix products, arithmetic and copies ran while one was open for 3% -> 3% of each run, Pallas kernels for 4% -> 4%
where the time goes in v21:
time: 33.1 us; the launch traced here: 32.8 us
  starting transfers between devices  16.3 us (49%)
  Pallas kernels  9.23 us (28%)
  waiting for transfers between devices  4.8 us (15%)
  local copies, waits for them, and re-layouts  1.53 us (5%)
  between operations  0.83 us (3%)
    ppermute x6, starting transfers between devices, spread(): lax.ppermute(shard, axis, pairs)  10.5 us
    pallas_call x1, Pallas kernels, whole_field_body(): pl.pallas_call(wave_kernel, out_shape=(array(1, 3, tile_r, tile_c),) * 2,...  7.3 us
    ppermute x2, starting transfers between devices, whole_field_body(): near_own.append(lax.ppermute(packet, 'col', close))  3.76 us
    ppermute x6, waiting for transfers between devices, spread(): lax.ppermute(shard, axis, pairs)  2.45 us
    ppermute x3, waiting for transfers between devices, swap_cores(): return lax.ppermute(value, 'row', [(0, 1), (1, 0)])  2.35 us
    ppermute x1, starting transfers between devices, whole_field_body(): lax.ppermute(slab, 'col', further)  1.71 us
    unnamed x13, local copies, waits for them, and re-layouts  1.49 us
    pallas_call x1, Pallas kernels, whole_field_body(): pl.pallas_call(load_kernel, out_shape=(jax.ShapeDtypeStruct(row_all.shape...  0.89 us
  transfers between devices with their start and end apart: 12, of which 3 were waited for; matrix products, arithmetic and copies ran while one was open for 3% of the time, Pallas kernels for 4%

profile of v21, /device:TPU:0, one launch (start us, length us, event | category | flops | bytes accessed | tf_op | source)
XLA Modules:
  0.0 32.8 jit_solution(17585889511560659755)
XLA Ops:
  0.6 0.0 copy-start.3
  0.6 3.1 %collective-permute-start = (f32[1,64,128]{2,1,0:T(8,128)}, f32[1,64,128]{2,1,0:T(8,128)S(1)}, u32[]{:S(2)}, u32[]{:S(2)}) collective-permute-start(f32[1,64,128]{2,1,0:T(8,128)} %param.5), channel_id=1, source_target_pairs={{0,8},{8,0},{16,24},{24,16},{1,9},{9,1},{17,25},{25,17},{2,10},{10... | collective-permute-start | bytes 98312 | tf_op jit(solution)/shard_map/ppermute | solution.py:342
  3.7 2.6 %collective-permute-start.1 = (f32[1,64,128]{2,1,0:T(8,128)}, f32[1,64,128]{2,1,0:T(8,128)S(1)}, u32[]{:S(2)}, u32[]{:S(2)}) collective-permute-start(f32[1,64,128]{2,1,0:T(8,128)} %param.5), channel_id=1, source_target_pairs={{0,16},{8,24},{16,0},{24,8},{1,17},{9,25},{17,1},{25,9},{2,18},{10... | collective-permute-start | bytes 98312 | tf_op jit(solution)/shard_map/ppermute | solution.py:342
  6.3 0.0 collective-permute-start.2
  6.3 0.0 collective-permute-done
  6.3 0.8 %constant_dynamic-update-slice_fusion.4 = f32[3,64,128]{2,1,0:T(8,128)S(1)} fusion(f32[1,64,128]{2,1,0:T(8,128)} %param.5), kind=kLoop, calls=%fused_computation.9 | loop fusion | bytes 65536
  7.1 1.7 %collective-permute-start.5 = (f32[1,64,128]{2,1,0:T(8,128)}, f32[1,64,128]{2,1,0:T(8,128)S(1)}, u32[]{:S(2)}, u32[]{:S(2)}) collective-permute-start(f32[1,64,128]{2,1,0:T(8,128)} %param.5), channel_id=1, source_target_pairs={{0,2},{1,3},{2,0},{3,1},{4,6},{5,7},{6,4},{7,5},{8,10},{9,11},{10,... | collective-permute-start | bytes 98312 | tf_op jit(solution)/shard_map/ppermute | solution.py:377
  8.9 0.0 copy-done.3
  8.9 0.7 %collective-permute-start.6 = (f32[3,64,128]{2,1,0:T(8,128)S(1)}, f32[3,64,128]{2,1,0:T(8,128)S(1)}, u32[]{:S(2)}, u32[]{:S(2)}) collective-permute-start(f32[3,64,128]{2,1,0:T(8,128)S(1)} %constant_dynamic-update-slice_fusion.3), channel_id=1, source_target_pairs={{1,2},{2,1},{5,6},{6,5},{9,10},{10,9},{13,14},{14,13},{17,18},{18,... | collective-permute-start | bytes 294920 | tf_op jit(solution)/shard_map/ppermute | solution.py:374
  9.5 3.1 %collective-permute-start.4 = (f32[3,64,128]{2,1,0:T(8,128)S(1)}, f32[3,64,128]{2,1,0:T(8,128)S(1)}, u32[]{:S(2)}, u32[]{:S(2)}) collective-permute-start(f32[3,64,128]{2,1,0:T(8,128)S(1)} %constant_dynamic-update-slice_fusion.3), channel_id=1, source_target_pairs={{0,1},{1,0},{2,3},{3,2},{4,5},{5,4},{6,7},{7,6},{8,9},{9,8},{10,11... | collective-permute-start | bytes 294920 | tf_op jit(solution)/shard_map/ppermute | solution.py:374
  12.6 0.0 collective-permute-done.1
  12.6 0.0 copy-start.1
  12.7 0.0 copy-start
  12.7 0.0 collective-permute-done.2
  12.7 0.8 %collective-permute-start.3 = (f32[3,64,128]{2,1,0:T(8,128)S(1)}, f32[3,64,128]{2,1,0:T(8,128)S(1)}, u32[]{:S(2)}, u32[]{:S(2)}) collective-permute-start(f32[3,64,128]{2,1,0:T(8,128)S(1)} %get-tuple-element.49), channel_id=1, source_target_pairs={{1,2},{2,1},{5,6},{6,5},{9,10},{10,9},{13,14},{14,13},{17,18},{18,... | collective-permute-start | bytes 294920 | tf_op jit(solution)/shard_map/ppermute | solution.py:342
  13.5 3.7 %collective-permute-start.8 = (f32[3,64,128]{2,1,0:T(8,128)S(1)}, f32[3,64,128]{2,1,0:T(8,128)S(1)}, u32[]{:S(2)}, u32[]{:S(2)}) collective-permute-start(f32[3,64,128]{2,1,0:T(8,128)S(1)} %get-tuple-element.49), channel_id=1, source_target_pairs={{0,2},{1,3},{2,0},{3,1},{4,6},{5,7},{6,4},{7,5},{8,10},{9,11},{10,... | collective-permute-start | bytes 294920 | tf_op jit(solution)/shard_map/ppermute | solution.py:342
  17.2 0.0 collective-permute-done.5
  17.2 0.4 %collective-permute-start.7 = (f32[3,64,128]{2,1,0:T(8,128)S(1)}, f32[3,64,128]{2,1,0:T(8,128)S(1)}, u32[]{:S(2)}, u32[]{:S(2)}) collective-permute-start(f32[3,64,128]{2,1,0:T(8,128)S(1)} %get-tuple-element.49), channel_id=1, source_target_pairs={{0,1},{1,0},{2,3},{3,2},{4,5},{5,4},{6,7},{7,6},{8,9},{9,8},{10,11... | collective-permute-start | bytes 294920 | tf_op jit(solution)/shard_map/ppermute | solution.py:342
  17.6 0.0 collective-permute-done.6
  17.6 0.0 collective-permute-done.4
  17.6 0.0 copy-start.2
  17.6 0.0 copy-done.1
  17.7 0.0 copy-done
  17.7 0.6 %copy-done.2 = s32[2,2]{1,0:T(2,128)S(1)} copy-done((s32[2,2]{1,0:T(2,128)S(1)}, s32[2,2]{1,0:T(2,128)}, u32[]{:S(2)}) %copy-start.2) | copy-done | bytes 40
  18.3 0.9 %shard_map.68 = (bf16[256,512]{1,0:T(8,128)(2,1)S(1)}, bf16[512,512]{1,0:T(8,128)(2,1)S(1)}, f32[4,2,128,128]{3,2,1,0:T(8,128)S(1)}, f32[4,64,128]{2,1,0:T(8,128)S(1)}, f32[4,64,128]{2,1,0:T(8,128)S(1)}) custom-call(s32[2,2]{1,0:T(2,128)S(1)} %copy-done.2, f32[4,3,64,128]{3,2,1,0:T(8,128)S(1)} %pad_maximum_fusion.near_own, bf16[2,256,512]{2,1,0:T(8,128)(2,1)S(1)} %copy-done, ...), custom_call_target="tpu_custom_call" | custom-call | flops 100000000 | bytes 1048576 | tf_op jit(solution)/shard_map/pallas_call | solution.py:385
  19.2 0.0 collective-permute-done.3
  19.3 0.1 collective-permute-start.9
  19.4 2.4 %collective-permute-done.7 = f32[3,64,128]{2,1,0:T(8,128)S(1)} collective-permute-done((f32[3,64,128]{2,1,0:T(8,128)S(1)}, f32[3,64,128]{2,1,0:T(8,128)S(1)}, u32[]{:S(2)}, u32[]{:S(2)}) %collective-permute-start.7) | collective-permute-done | bytes 98336 | tf_op jit(solution)/shard_map/ppermute | solution.py:342
  21.8 0.0 collective-permute-done.8
  21.8 0.1 collective-permute-start.10
  21.9 0.4 %shard_map.69 = (f32[5,4,64,128]{3,2,1,0:T(8,128)S(1)}, f32[5,4,64,128]{3,2,1,0:T(8,128)S(1)}) custom-call(f32[4,3,64,128]{3,2,1,0:T(8,128)S(1)} %pad_maximum_fusion.1.near_rest, f32[4,64,128]{2,1,0:T(8,128)S(1)} %get-tuple-element.37.own_cos, f32[4,64,128]{2,1,0:T(8,128)S(1)} %get-tuple-element.38.own_sin), custom_call_target="tpu_custom_call" | custom-call | flops 500000000 | bytes 1048576 | tf_op jit(solution)/shard_map/pallas_call | solution.py:409
  22.3 1.2 %collective-permute-done.10.far_second = f32[9,64,128]{2,1,0:T(8,128)S(1)} collective-permute-done((f32[9,64,128]{2,1,0:T(8,128)S(1)}, f32[9,64,128]{2,1,0:T(8,128)S(1)}, u32[]{:S(2)}, u32[]{:S(2)}) %collective-permute-start.10) | collective-permute-done | bytes 294944 | tf_op jit(solution)/shard_map/ppermute | solution.py:347
  23.5 0.0 collective-permute-done.9.far_first
  23.5 7.3 %shard_map.70 = (f32[1,3,64,128]{3,2,1,0:T(8,128)S(1)}, f32[1,3,64,128]{3,2,1,0:T(8,128)S(1)}) custom-call(f32[4,2,128,128]{3,2,1,0:T(8,128)S(1)} %get-tuple-element.35.wave_ref, f32[5,4,64,128]{3,2,1,0:T(8,128)S(1)} %get-tuple-element.39.near_cos, f32[5,4,64,128]{3,2,1,0:T(8,128)S(1)} %get-tuple-element.40.near_sin, ...), custom_call_target="tpu_custom_call" | custom-call | tf_op jit(solution)/shard_map/pallas_call | solution.py:417
  30.8 0.2 collective-permute-start.11
  31.0 1.2 %collective-permute-done.11.received_ref = f32[1,3,64,128]{3,2,1,0:T(8,128)S(1)} collective-permute-done((f32[1,3,64,128]{3,2,1,0:T(8,128)S(1)}, f32[1,3,64,128]{3,2,1,0:T(8,128)S(1)}, u32[]{:S(2)}, u32[]{:S(2)}) %collective-permute-start.11) | collective-permute-done | bytes 98336 | tf_op jit(solution)/shard_map/ppermute | solution.py:347
  32.1 0.7 %shard_map.71 = (f32[1,64,128]{2,1,0:T(8,128)}, f32[2,1,2,64,128]{4,3,2,1,0:T(8,128)}) custom-call(f32[1,3,64,128]{3,2,1,0:T(8,128)S(1)} %get-tuple-element.44.mine_ref, f32[1,3,64,128]{3,2,1,0:T(8,128)S(1)} %collective-permute-done.11.received_ref), custom_call_target="tpu_custom_call" | custom-call | tf_op jit(solution)/shard_map/pallas_call | solution.py:432
  (12 shorter events, 0.2 us)
Async XLA Ops:
  0.6 8.2 %copy-start.3 = (f32[2,64,128]{2,1,0:T(8,128)S(1)}, f32[2,64,128]{2,1,0:T(8,128)}, u32[]{:S(2)}) copy-start(f32[2,64,128]{2,1,0:T(8,128)} %param.7) | copy-start | bytes 196612
  0.6 5.7 %collective-permute-start = (f32[1,64,128]{2,1,0:T(8,128)}, f32[1,64,128]{2,1,0:T(8,128)S(1)}, u32[]{:S(2)}, u32[]{:S(2)}) collective-permute-start(f32[1,64,128]{2,1,0:T(8,128)} %param.5), channel_id=1, source_target_pairs={{0,8},{8,0},{16,24},{24,16},{1,9},{9,1},{17,25},{25,17},{2,10},{10... | collective-permute-start | bytes 98312 | tf_op jit(solution)/shard_map/ppermute | solution.py:342
  3.7 8.9 %collective-permute-start.1 = (f32[1,64,128]{2,1,0:T(8,128)}, f32[1,64,128]{2,1,0:T(8,128)S(1)}, u32[]{:S(2)}, u32[]{:S(2)}) collective-permute-start(f32[1,64,128]{2,1,0:T(8,128)} %param.5), channel_id=1, source_target_pairs={{0,16},{8,24},{16,0},{24,8},{1,17},{9,25},{17,1},{25,9},{2,18},{10... | collective-permute-start | bytes 98312 | tf_op jit(solution)/shard_map/ppermute | solution.py:342
  6.3 6.4 %collective-permute-start.2 = (f32[1,64,128]{2,1,0:T(8,128)}, f32[1,64,128]{2,1,0:T(8,128)S(1)}, u32[]{:S(2)}, u32[]{:S(2)}) collective-permute-start(f32[1,64,128]{2,1,0:T(8,128)} %param.5), channel_id=1, source_target_pairs={{0,24},{8,16},{16,8},{24,0},{1,25},{9,17},{17,9},{25,1},{2,26},{10... | collective-permute-start | bytes 98312 | tf_op jit(solution)/shard_map/ppermute | solution.py:342
  7.1 10.0 %collective-permute-start.5 = (f32[1,64,128]{2,1,0:T(8,128)}, f32[1,64,128]{2,1,0:T(8,128)S(1)}, u32[]{:S(2)}, u32[]{:S(2)}) collective-permute-start(f32[1,64,128]{2,1,0:T(8,128)} %param.5), channel_id=1, source_target_pairs={{0,2},{1,3},{2,0},{3,1},{4,6},{5,7},{6,4},{7,5},{8,10},{9,11},{10,... | collective-permute-start | bytes 98312 | tf_op jit(solution)/shard_map/ppermute | solution.py:377
  8.9 8.7 %collective-permute-start.6 = (f32[3,64,128]{2,1,0:T(8,128)S(1)}, f32[3,64,128]{2,1,0:T(8,128)S(1)}, u32[]{:S(2)}, u32[]{:S(2)}) collective-permute-start(f32[3,64,128]{2,1,0:T(8,128)S(1)} %constant_dynamic-update-slice_fusion.3), channel_id=1, source_target_pairs={{1,2},{2,1},{5,6},{6,5},{9,10},{10,9},{13,14},{14,13},{17,18},{18,... | collective-permute-start | bytes 294920 | tf_op jit(solution)/shard_map/ppermute | solution.py:374
  9.5 8.0 %collective-permute-start.4 = (f32[3,64,128]{2,1,0:T(8,128)S(1)}, f32[3,64,128]{2,1,0:T(8,128)S(1)}, u32[]{:S(2)}, u32[]{:S(2)}) collective-permute-start(f32[3,64,128]{2,1,0:T(8,128)S(1)} %constant_dynamic-update-slice_fusion.3), channel_id=1, source_target_pairs={{0,1},{1,0},{2,3},{3,2},{4,5},{5,4},{6,7},{7,6},{8,9},{9,8},{10,11... | collective-permute-start | bytes 294920 | tf_op jit(solution)/shard_map/ppermute | solution.py:374
  12.6 5.0 %copy-start.1 = (bf16[512,512]{1,0:T(8,128)(2,1)S(1)}, bf16[512,512]{1,0:T(8,128)(2,1)}, u32[]{:S(2)}) copy-start(bf16[512,512]{1,0:T(8,128)(2,1)} %constant.20.clone.col_from) | copy-start | bytes 1572868
  12.7 5.0 %copy-start = (bf16[2,256,512]{2,1,0:T(8,128)(2,1)S(1)}, bf16[2,256,512]{2,1,0:T(8,128)(2,1)}, u32[]{:S(2)}) copy-start(bf16[2,256,512]{2,1,0:T(8,128)(2,1)} %constant.19.clone.row_from) | copy-start | bytes 1572868
  12.7 6.5 %collective-permute-start.3 = (f32[3,64,128]{2,1,0:T(8,128)S(1)}, f32[3,64,128]{2,1,0:T(8,128)S(1)}, u32[]{:S(2)}, u32[]{:S(2)}) collective-permute-start(f32[3,64,128]{2,1,0:T(8,128)S(1)} %get-tuple-element.49), channel_id=1, source_target_pairs={{1,2},{2,1},{5,6},{6,5},{9,10},{10,9},{13,14},{14,13},{17,18},{18,... | collective-permute-start | bytes 294920 | tf_op jit(solution)/shard_map/ppermute | solution.py:342
  13.5 8.3 %collective-permute-start.8 = (f32[3,64,128]{2,1,0:T(8,128)S(1)}, f32[3,64,128]{2,1,0:T(8,128)S(1)}, u32[]{:S(2)}, u32[]{:S(2)}) collective-permute-start(f32[3,64,128]{2,1,0:T(8,128)S(1)} %get-tuple-element.49), channel_id=1, source_target_pairs={{0,2},{1,3},{2,0},{3,1},{4,6},{5,7},{6,4},{7,5},{8,10},{9,11},{10,... | collective-permute-start | bytes 294920 | tf_op jit(solution)/shard_map/ppermute | solution.py:342
  17.2 4.6 %collective-permute-start.7 = (f32[3,64,128]{2,1,0:T(8,128)S(1)}, f32[3,64,128]{2,1,0:T(8,128)S(1)}, u32[]{:S(2)}, u32[]{:S(2)}) collective-permute-start(f32[3,64,128]{2,1,0:T(8,128)S(1)} %get-tuple-element.49), channel_id=1, source_target_pairs={{0,1},{1,0},{2,3},{3,2},{4,5},{5,4},{6,7},{7,6},{8,9},{9,8},{10,11... | collective-permute-start | bytes 294920 | tf_op jit(solution)/shard_map/ppermute | solution.py:342
  17.6 0.7 %copy-start.2 = (s32[2,2]{1,0:T(2,128)S(1)}, s32[2,2]{1,0:T(2,128)}, u32[]{:S(2)}) copy-start(s32[2,2]{1,0:T(2,128)} %tilt_ref.1) | copy-start | bytes 52
  19.3 4.2 %collective-permute-start.9 = (f32[11,64,128]{2,1,0:T(8,128)S(1)}, f32[11,64,128]{2,1,0:T(8,128)S(1)}, u32[]{:S(2)}, u32[]{:S(2)}) collective-permute-start(f32[11,64,128]{2,1,0:T(8,128)S(1)} %pad_maximum_fusion.2), channel_id=1, source_target_pairs={{0,4},{4,0},{1,5},{5,1},{2,6},{6,2},{3,7},{7,3},{8,12},{12,8},{9,1... | collective-permute-start | bytes 1081352 | tf_op jit(solution)/shard_map/ppermute | solution.py:347
  21.8 1.6 %collective-permute-start.10 = (f32[9,64,128]{2,1,0:T(8,128)S(1)}, f32[9,64,128]{2,1,0:T(8,128)S(1)}, u32[]{:S(2)}, u32[]{:S(2)}) collective-permute-start(f32[9,64,128]{2,1,0:T(8,128)S(1)} %constant_dynamic-update-slice_fusion.5), channel_id=1, source_target_pairs={{0,4},{4,0},{1,5},{5,1},{2,6},{6,2},{3,7},{7,3},{8,12},{12,8},{9,1... | collective-permute-start | bytes 884744 | tf_op jit(solution)/shard_map/ppermute | solution.py:347
  30.8 1.4 %collective-permute-start.11 = (f32[1,3,64,128]{3,2,1,0:T(8,128)S(1)}, f32[1,3,64,128]{3,2,1,0:T(8,128)S(1)}, u32[]{:S(2)}, u32[]{:S(2)}) collective-permute-start(f32[1,3,64,128]{3,2,1,0:T(8,128)S(1)} %get-tuple-element.45), channel_id=1, source_target_pairs={{0,4},{4,0},{1,5},{5,1},{2,6},{6,2},{3,7},{7,3},{8,12},{12,8},{9,1... | collective-permute-start | bytes 294920 | tf_op jit(solution)/shard_map/ppermute | solution.py:347

commit v22 on v21

--- a/solution.py
+++ b/solution.py
@@ -333,13 +333,11 @@
         copy.wait()
 
 
-def spread(shard, axis, reach=None):
-    size = lax.axis_size(axis)
-    reach = size if reach is None else reach
+def spread(shard, axis, all_bits, reach=3):
     pieces = []
-    for bits in range(1, size):
-        pairs = [(i, i ^ bits) for i in range(size) if abs(i - (i ^ bits)) <= reach]
-        pieces.append(lax.ppermute(shard, axis, pairs) if pairs else jnp.zeros_like(shard))
+    for bits in all_bits:
+        pairs = [(i, i ^ bits) for i in range(4) if abs(i - (i ^ bits)) <= reach]
+        pieces.append(lax.ppermute(shard, axis, pairs))
     return pieces
 
 
@@ -362,8 +360,9 @@
     def params(mebibytes):
         return pltpu.CompilerParams(vmem_limit_bytes=mebibytes * 2**20)
 
-    other_depths = spread(phase, "depth")
+    other_depths = spread(phase, "depth", (1, 3))
     other_depths[0], measured, slab = lax.optimization_barrier((other_depths[0], intensity, phase))
+    other_depths[1:1] = spread(slab, "depth", (2,))
     other_depths = jnp.concatenate(other_depths, axis=0)
     packet = jnp.concatenate([slab, measured], axis=0)
     near_own = [packet]
@@ -377,7 +376,7 @@
             arrived = lax.ppermute(slab, "col", further) if further else jnp.zeros_like(slab)
             near_own.append(jnp.concatenate([arrived, jnp.zeros_like(measured)], axis=0))
     near_own = jnp.stack(near_own)
-    arriving = spread(other_depths, "col", 2)
+    arriving = spread(other_depths, "col", (1, 2, 3), 2)
     row_all, col_all = jnp.asarray(row_constant(height)), jnp.asarray(col_constant())
     near_own, row_all, col_all = lax.optimization_barrier((near_own, row_all, col_all))
     half_screens = (count + 1, blocks, tile_r, tile_c)
@@ -614,12 +613,10 @@
         4 * height * width * (slices + batch) <= GATHER_BUDGET
         and batch == rows == 2
         and slices == sections
-        and sections & (sections - 1) == 0
-        and cols & (cols - 1) == 0
+        and sections == 4
+        and cols == 4
         and height == LANES
         and width == cols * LANES
-        and cols > 1
-        and sections > 1
         and sections * HALO <= LANES
     )
 

time: 33.1 us -> 35 us (1.057)
  starting transfers between devices: 16.3 us -> 19 us
  waiting for transfers between devices: 4.8 us -> 4.12 us
    ppermute x6, starting transfers between devices: 10.5 us -> 13.2 us  [spread(): pieces.append(lax.ppermute(shard, axis, pairs))]
    ppermute x6, waiting for transfers between devices: 2.45 us -> 1.78 us  [spread(): pieces.append(lax.ppermute(shard, axis, pairs))]
where the time goes in v22:
time: 35 us; the launch traced here: 34.8 us
  starting transfers between devices  19 us (54%)
  Pallas kernels  9.22 us (26%)
  waiting for transfers between devices  4.12 us (12%)
  local copies, waits for them, and re-layouts  1.5 us (4%)
  between operations  0.83 us (2%)
    ppermute x6, starting transfers between devices, spread(): pieces.append(lax.ppermute(shard, axis, pairs))  13.2 us
    pallas_call x1, Pallas kernels, whole_field_body(): pl.pallas_call(wave_kernel, out_shape=(array(1, 3, tile_r, tile_c),) * 2,...  7.3 us
    ppermute x2, starting transfers between devices, whole_field_body(): near_own.append(lax.ppermute(packet, 'col', close))  3.94 us
    ppermute x3, waiting for transfers between devices, swap_cores(): return lax.ppermute(value, 'row', [(0, 1), (1, 0)])  2.34 us
    ppermute x6, waiting for transfers between devices, spread(): pieces.append(lax.ppermute(shard, axis, pairs))  1.78 us
    ppermute x1, starting transfers between devices, whole_field_body(): lax.ppermute(slab, 'col', further)  1.52 us
    unnamed x13, local copies, waits for them, and re-layouts  1.46 us
    pallas_call x1, Pallas kernels, whole_field_body(): pl.pallas_call(load_kernel, out_shape=(jax.ShapeDtypeStruct(row_all.shape...  0.89 us
  transfers between devices with their start and end apart: 12, of which 3 were waited for; matrix products, arithmetic and copies ran while one was open for 3% of the time, Pallas kernels for 4%

profile of v22, /device:TPU:0, one launch (start us, length us, event | category | flops | bytes accessed | tf_op | source)
XLA Modules:
  0.0 34.8 jit_solution(7381671295251288208)
XLA Ops:
  0.6 0.0 copy-start.3
  0.6 3.1 %collective-permute-start = (f32[1,64,128]{2,1,0:T(8,128)}, f32[1,64,128]{2,1,0:T(8,128)S(1)}, u32[]{:S(2)}, u32[]{:S(2)}) collective-permute-start(f32[1,64,128]{2,1,0:T(8,128)} %param.5), channel_id=1, source_target_pairs={{0,8},{8,0},{16,24},{24,16},{1,9},{9,1},{17,25},{25,17},{2,10},{10... | collective-permute-start | bytes 98312 | tf_op jit(solution)/shard_map/ppermute | solution.py:340
  3.7 2.5 %collective-permute-start.2 = (f32[1,64,128]{2,1,0:T(8,128)}, f32[1,64,128]{2,1,0:T(8,128)S(1)}, u32[]{:S(2)}, u32[]{:S(2)}) collective-permute-start(f32[1,64,128]{2,1,0:T(8,128)} %param.5), channel_id=1, source_target_pairs={{0,24},{8,16},{16,8},{24,0},{1,25},{9,17},{17,9},{25,1},{2,26},{10... | collective-permute-start | bytes 98312 | tf_op jit(solution)/shard_map/ppermute | solution.py:340
  6.2 0.0 collective-permute-done
  6.2 2.9 %collective-permute-start.1 = (f32[1,64,128]{2,1,0:T(8,128)}, f32[1,64,128]{2,1,0:T(8,128)S(1)}, u32[]{:S(2)}, u32[]{:S(2)}) collective-permute-start(f32[1,64,128]{2,1,0:T(8,128)} %param.5), channel_id=1, source_target_pairs={{0,16},{8,24},{16,0},{24,8},{1,17},{9,25},{17,1},{25,9},{2,18},{10... | collective-permute-start | bytes 98312 | tf_op jit(solution)/shard_map/ppermute | solution.py:340
  9.2 0.8 %constant_dynamic-update-slice_fusion.4 = f32[3,64,128]{2,1,0:T(8,128)S(1)} fusion(f32[1,64,128]{2,1,0:T(8,128)} %param.5), kind=kLoop, calls=%fused_computation.9 | loop fusion | bytes 65536
  9.9 1.5 %collective-permute-start.5 = (f32[1,64,128]{2,1,0:T(8,128)}, f32[1,64,128]{2,1,0:T(8,128)S(1)}, u32[]{:S(2)}, u32[]{:S(2)}) collective-permute-start(f32[1,64,128]{2,1,0:T(8,128)} %param.5), channel_id=1, source_target_pairs={{0,2},{1,3},{2,0},{3,1},{4,6},{5,7},{6,4},{7,5},{8,10},{9,11},{10,... | collective-permute-start | bytes 98312 | tf_op jit(solution)/shard_map/ppermute | solution.py:376
  11.5 0.0 copy-done.3
  11.5 0.7 %collective-permute-start.6 = (f32[3,64,128]{2,1,0:T(8,128)S(1)}, f32[3,64,128]{2,1,0:T(8,128)S(1)}, u32[]{:S(2)}, u32[]{:S(2)}) collective-permute-start(f32[3,64,128]{2,1,0:T(8,128)S(1)} %constant_dynamic-update-slice_fusion.3), channel_id=1, source_target_pairs={{1,2},{2,1},{5,6},{6,5},{9,10},{10,9},{13,14},{14,13},{17,18},{18,... | collective-permute-start | bytes 294920 | tf_op jit(solution)/shard_map/ppermute | solution.py:373
  12.2 3.3 %collective-permute-start.4 = (f32[3,64,128]{2,1,0:T(8,128)S(1)}, f32[3,64,128]{2,1,0:T(8,128)S(1)}, u32[]{:S(2)}, u32[]{:S(2)}) collective-permute-start(f32[3,64,128]{2,1,0:T(8,128)S(1)} %constant_dynamic-update-slice_fusion.3), channel_id=1, source_target_pairs={{0,1},{1,0},{2,3},{3,2},{4,5},{5,4},{6,7},{7,6},{8,9},{9,8},{10,11... | collective-permute-start | bytes 294920 | tf_op jit(solution)/shard_map/ppermute | solution.py:373
  15.4 0.0 collective-permute-done.1
  15.4 0.0 copy-start.1
  15.5 0.0 copy-start
  15.5 0.0 collective-permute-done.2
  15.5 0.8 %collective-permute-start.3 = (f32[3,64,128]{2,1,0:T(8,128)S(1)}, f32[3,64,128]{2,1,0:T(8,128)S(1)}, u32[]{:S(2)}, u32[]{:S(2)}) collective-permute-start(f32[3,64,128]{2,1,0:T(8,128)S(1)} %get-tuple-element.49), channel_id=1, source_target_pairs={{1,2},{2,1},{5,6},{6,5},{9,10},{10,9},{13,14},{14,13},{17,18},{18,... | collective-permute-start | bytes 294920 | tf_op jit(solution)/shard_map/ppermute | solution.py:340
  16.3 2.8 %collective-permute-start.8 = (f32[3,64,128]{2,1,0:T(8,128)S(1)}, f32[3,64,128]{2,1,0:T(8,128)S(1)}, u32[]{:S(2)}, u32[]{:S(2)}) collective-permute-start(f32[3,64,128]{2,1,0:T(8,128)S(1)} %get-tuple-element.49), channel_id=1, source_target_pairs={{0,2},{1,3},{2,0},{3,1},{4,6},{5,7},{6,4},{7,5},{8,10},{9,11},{10,... | collective-permute-start | bytes 294920 | tf_op jit(solution)/shard_map/ppermute | solution.py:340
  19.1 0.0 collective-permute-done.5
  19.1 1.1 %collective-permute-start.7 = (f32[3,64,128]{2,1,0:T(8,128)S(1)}, f32[3,64,128]{2,1,0:T(8,128)S(1)}, u32[]{:S(2)}, u32[]{:S(2)}) collective-permute-start(f32[3,64,128]{2,1,0:T(8,128)S(1)} %get-tuple-element.49), channel_id=1, source_target_pairs={{0,1},{1,0},{2,3},{3,2},{4,5},{5,4},{6,7},{7,6},{8,9},{9,8},{10,11... | collective-permute-start | bytes 294920 | tf_op jit(solution)/shard_map/ppermute | solution.py:340
  20.2 0.0 collective-permute-done.6
  20.2 0.0 collective-permute-done.4
  20.2 0.0 copy-start.2
  20.3 0.0 copy-done.1
  20.3 0.0 copy-done
  20.3 0.6 %copy-done.2 = s32[2,2]{1,0:T(2,128)S(1)} copy-done((s32[2,2]{1,0:T(2,128)S(1)}, s32[2,2]{1,0:T(2,128)}, u32[]{:S(2)}) %copy-start.2) | copy-done | bytes 40
  20.9 0.9 %shard_map.68 = (bf16[256,512]{1,0:T(8,128)(2,1)S(1)}, bf16[512,512]{1,0:T(8,128)(2,1)S(1)}, f32[4,2,128,128]{3,2,1,0:T(8,128)S(1)}, f32[4,64,128]{2,1,0:T(8,128)S(1)}, f32[4,64,128]{2,1,0:T(8,128)S(1)}) custom-call(s32[2,2]{1,0:T(2,128)S(1)} %copy-done.2, f32[4,3,64,128]{3,2,1,0:T(8,128)S(1)} %pad_maximum_fusion.near_own, bf16[2,256,512]{2,1,0:T(8,128)(2,1)S(1)} %copy-done, ...), custom_call_target="tpu_custom_call" | custom-call | flops 100000000 | bytes 1048576 | tf_op jit(solution)/shard_map/pallas_call | solution.py:384
  21.8 0.0 collective-permute-done.3
  21.9 0.1 collective-permute-start.9
  22.0 1.8 %collective-permute-done.7 = f32[3,64,128]{2,1,0:T(8,128)S(1)} collective-permute-done((f32[3,64,128]{2,1,0:T(8,128)S(1)}, f32[3,64,128]{2,1,0:T(8,128)S(1)}, u32[]{:S(2)}, u32[]{:S(2)}) %collective-permute-start.7) | collective-permute-done | bytes 98336 | tf_op jit(solution)/shard_map/ppermute | solution.py:340
  23.7 0.0 collective-permute-done.8
  23.8 0.1 collective-permute-start.10
  23.9 0.4 %shard_map.69 = (f32[5,4,64,128]{3,2,1,0:T(8,128)S(1)}, f32[5,4,64,128]{3,2,1,0:T(8,128)S(1)}) custom-call(f32[4,3,64,128]{3,2,1,0:T(8,128)S(1)} %pad_maximum_fusion.1.near_rest, f32[4,64,128]{2,1,0:T(8,128)S(1)} %get-tuple-element.37.own_cos, f32[4,64,128]{2,1,0:T(8,128)S(1)} %get-tuple-element.38.own_sin), custom_call_target="tpu_custom_call" | custom-call | flops 500000000 | bytes 1048576 | tf_op jit(solution)/shard_map/pallas_call | solution.py:408
  24.2 1.2 %collective-permute-done.10.far_second = f32[9,64,128]{2,1,0:T(8,128)S(1)} collective-permute-done((f32[9,64,128]{2,1,0:T(8,128)S(1)}, f32[9,64,128]{2,1,0:T(8,128)S(1)}, u32[]{:S(2)}, u32[]{:S(2)}) %collective-permute-start.10) | collective-permute-done | bytes 294944 | tf_op jit(solution)/shard_map/ppermute | solution.py:345
  25.4 0.0 collective-permute-done.9.far_first
  25.4 7.3 %shard_map.70 = (f32[1,3,64,128]{3,2,1,0:T(8,128)S(1)}, f32[1,3,64,128]{3,2,1,0:T(8,128)S(1)}) custom-call(f32[4,2,128,128]{3,2,1,0:T(8,128)S(1)} %get-tuple-element.35.wave_ref, f32[5,4,64,128]{3,2,1,0:T(8,128)S(1)} %get-tuple-element.39.near_cos, f32[5,4,64,128]{3,2,1,0:T(8,128)S(1)} %get-tuple-element.40.near_sin, ...), custom_call_target="tpu_custom_call" | custom-call | tf_op jit(solution)/shard_map/pallas_call | solution.py:416
  32.7 0.2 collective-permute-start.11
  32.9 1.2 %collective-permute-done.11.received_ref = f32[1,3,64,128]{3,2,1,0:T(8,128)S(1)} collective-permute-done((f32[1,3,64,128]{3,2,1,0:T(8,128)S(1)}, f32[1,3,64,128]{3,2,1,0:T(8,128)S(1)}, u32[]{:S(2)}, u32[]{:S(2)}) %collective-permute-start.11) | collective-permute-done | bytes 98336 | tf_op jit(solution)/shard_map/ppermute | solution.py:345
  34.1 0.7 %shard_map.71 = (f32[1,64,128]{2,1,0:T(8,128)}, f32[2,1,2,64,128]{4,3,2,1,0:T(8,128)}) custom-call(f32[1,3,64,128]{3,2,1,0:T(8,128)S(1)} %get-tuple-element.44.mine_ref, f32[1,3,64,128]{3,2,1,0:T(8,128)S(1)} %collective-permute-done.11.received_ref), custom_call_target="tpu_custom_call" | custom-call | tf_op jit(solution)/shard_map/pallas_call | solution.py:431
  (12 shorter events, 0.2 us)
Async XLA Ops:
  0.6 10.8 %copy-start.3 = (f32[2,64,128]{2,1,0:T(8,128)S(1)}, f32[2,64,128]{2,1,0:T(8,128)}, u32[]{:S(2)}) copy-start(f32[2,64,128]{2,1,0:T(8,128)} %param.7) | copy-start | bytes 196612
  0.6 5.6 %collective-permute-start = (f32[1,64,128]{2,1,0:T(8,128)}, f32[1,64,128]{2,1,0:T(8,128)S(1)}, u32[]{:S(2)}, u32[]{:S(2)}) collective-permute-start(f32[1,64,128]{2,1,0:T(8,128)} %param.5), channel_id=1, source_target_pairs={{0,8},{8,0},{16,24},{24,16},{1,9},{9,1},{17,25},{25,17},{2,10},{10... | collective-permute-start | bytes 98312 | tf_op jit(solution)/shard_map/ppermute | solution.py:340
  3.7 11.8 %collective-permute-start.2 = (f32[1,64,128]{2,1,0:T(8,128)}, f32[1,64,128]{2,1,0:T(8,128)S(1)}, u32[]{:S(2)}, u32[]{:S(2)}) collective-permute-start(f32[1,64,128]{2,1,0:T(8,128)} %param.5), channel_id=1, source_target_pairs={{0,24},{8,16},{16,8},{24,0},{1,25},{9,17},{17,9},{25,1},{2,26},{10... | collective-permute-start | bytes 98312 | tf_op jit(solution)/shard_map/ppermute | solution.py:340
  6.2 9.2 %collective-permute-start.1 = (f32[1,64,128]{2,1,0:T(8,128)}, f32[1,64,128]{2,1,0:T(8,128)S(1)}, u32[]{:S(2)}, u32[]{:S(2)}) collective-permute-start(f32[1,64,128]{2,1,0:T(8,128)} %param.5), channel_id=1, source_target_pairs={{0,16},{8,24},{16,0},{24,8},{1,17},{9,25},{17,1},{25,9},{2,18},{10... | collective-permute-start | bytes 98312 | tf_op jit(solution)/shard_map/ppermute | solution.py:340
  9.9 9.2 %collective-permute-start.5 = (f32[1,64,128]{2,1,0:T(8,128)}, f32[1,64,128]{2,1,0:T(8,128)S(1)}, u32[]{:S(2)}, u32[]{:S(2)}) collective-permute-start(f32[1,64,128]{2,1,0:T(8,128)} %param.5), channel_id=1, source_target_pairs={{0,2},{1,3},{2,0},{3,1},{4,6},{5,7},{6,4},{7,5},{8,10},{9,11},{10,... | collective-permute-start | bytes 98312 | tf_op jit(solution)/shard_map/ppermute | solution.py:376
  11.5 8.7 %collective-permute-start.6 = (f32[3,64,128]{2,1,0:T(8,128)S(1)}, f32[3,64,128]{2,1,0:T(8,128)S(1)}, u32[]{:S(2)}, u32[]{:S(2)}) collective-permute-start(f32[3,64,128]{2,1,0:T(8,128)S(1)} %constant_dynamic-update-slice_fusion.3), channel_id=1, source_target_pairs={{1,2},{2,1},{5,6},{6,5},{9,10},{10,9},{13,14},{14,13},{17,18},{18,... | collective-permute-start | bytes 294920 | tf_op jit(solution)/shard_map/ppermute | solution.py:373
  12.2 8.0 %collective-permute-start.4 = (f32[3,64,128]{2,1,0:T(8,128)S(1)}, f32[3,64,128]{2,1,0:T(8,128)S(1)}, u32[]{:S(2)}, u32[]{:S(2)}) collective-permute-start(f32[3,64,128]{2,1,0:T(8,128)S(1)} %constant_dynamic-update-slice_fusion.3), channel_id=1, source_target_pairs={{0,1},{1,0},{2,3},{3,2},{4,5},{5,4},{6,7},{7,6},{8,9},{9,8},{10,11... | collective-permute-start | bytes 294920 | tf_op jit(solution)/shard_map/ppermute | solution.py:373
  15.4 4.8 %copy-start.1 = (bf16[512,512]{1,0:T(8,128)(2,1)S(1)}, bf16[512,512]{1,0:T(8,128)(2,1)}, u32[]{:S(2)}) copy-start(bf16[512,512]{1,0:T(8,128)(2,1)} %constant.20.clone.col_from) | copy-start | bytes 1572868
  15.5 4.8 %copy-start = (bf16[2,256,512]{2,1,0:T(8,128)(2,1)S(1)}, bf16[2,256,512]{2,1,0:T(8,128)(2,1)}, u32[]{:S(2)}) copy-start(bf16[2,256,512]{2,1,0:T(8,128)(2,1)} %constant.19.clone.row_from) | copy-start | bytes 1572868
  15.5 6.3 %collective-permute-start.3 = (f32[3,64,128]{2,1,0:T(8,128)S(1)}, f32[3,64,128]{2,1,0:T(8,128)S(1)}, u32[]{:S(2)}, u32[]{:S(2)}) collective-permute-start(f32[3,64,128]{2,1,0:T(8,128)S(1)} %get-tuple-element.49), channel_id=1, source_target_pairs={{1,2},{2,1},{5,6},{6,5},{9,10},{10,9},{13,14},{14,13},{17,18},{18,... | collective-permute-start | bytes 294920 | tf_op jit(solution)/shard_map/ppermute | solution.py:340
  16.3 7.4 %collective-permute-start.8 = (f32[3,64,128]{2,1,0:T(8,128)S(1)}, f32[3,64,128]{2,1,0:T(8,128)S(1)}, u32[]{:S(2)}, u32[]{:S(2)}) collective-permute-start(f32[3,64,128]{2,1,0:T(8,128)S(1)} %get-tuple-element.49), channel_id=1, source_target_pairs={{0,2},{1,3},{2,0},{3,1},{4,6},{5,7},{6,4},{7,5},{8,10},{9,11},{10,... | collective-permute-start | bytes 294920 | tf_op jit(solution)/shard_map/ppermute | solution.py:340
  19.1 4.6 %collective-permute-start.7 = (f32[3,64,128]{2,1,0:T(8,128)S(1)}, f32[3,64,128]{2,1,0:T(8,128)S(1)}, u32[]{:S(2)}, u32[]{:S(2)}) collective-permute-start(f32[3,64,128]{2,1,0:T(8,128)S(1)} %get-tuple-element.49), channel_id=1, source_target_pairs={{0,1},{1,0},{2,3},{3,2},{4,5},{5,4},{6,7},{7,6},{8,9},{9,8},{10,11... | collective-permute-start | bytes 294920 | tf_op jit(solution)/shard_map/ppermute | solution.py:340
  20.2 0.7 %copy-start.2 = (s32[2,2]{1,0:T(2,128)S(1)}, s32[2,2]{1,0:T(2,128)}, u32[]{:S(2)}) copy-start(s32[2,2]{1,0:T(2,128)} %tilt_ref.1) | copy-start | bytes 52
  21.9 3.5 %collective-permute-start.9 = (f32[11,64,128]{2,1,0:T(8,128)S(1)}, f32[11,64,128]{2,1,0:T(8,128)S(1)}, u32[]{:S(2)}, u32[]{:S(2)}) collective-permute-start(f32[11,64,128]{2,1,0:T(8,128)S(1)} %pad_maximum_fusion.2), channel_id=1, source_target_pairs={{0,4},{4,0},{1,5},{5,1},{2,6},{6,2},{3,7},{7,3},{8,12},{12,8},{9,1... | collective-permute-start | bytes 1081352 | tf_op jit(solution)/shard_map/ppermute | solution.py:345
  23.8 1.6 %collective-permute-start.10 = (f32[9,64,128]{2,1,0:T(8,128)S(1)}, f32[9,64,128]{2,1,0:T(8,128)S(1)}, u32[]{:S(2)}, u32[]{:S(2)}) collective-permute-start(f32[9,64,128]{2,1,0:T(8,128)S(1)} %constant_dynamic-update-slice_fusion.5), channel_id=1, source_target_pairs={{0,4},{4,0},{1,5},{5,1},{2,6},{6,2},{3,7},{7,3},{8,12},{12,8},{9,1... | collective-permute-start | bytes 884744 | tf_op jit(solution)/shard_map/ppermute | solution.py:345
  32.7 1.4 %collective-permute-start.11 = (f32[1,3,64,128]{3,2,1,0:T(8,128)S(1)}, f32[1,3,64,128]{3,2,1,0:T(8,128)S(1)}, u32[]{:S(2)}, u32[]{:S(2)}) collective-permute-start(f32[1,3,64,128]{3,2,1,0:T(8,128)S(1)} %get-tuple-element.45), channel_id=1, source_target_pairs={{0,4},{4,0},{1,5},{5,1},{2,6},{6,2},{3,7},{7,3},{8,12},{12,8},{9,1... | collective-permute-start | bytes 294920 | tf_op jit(solution)/shard_map/ppermute | solution.py:345

commit v23 on v22

--- a/solution.py
+++ b/solution.py
@@ -219,7 +219,7 @@
         held = col ^ own_place
         cos_ref[own_section, col], sin_ref[own_section, col] = own_cos[col], own_sin[col]
         for bits in range(1, count):
-            cos_ref[bits ^ own_section, col], sin_ref[bits ^ own_section, col] = cos_sin(near_rest[held, bits - 1])
+            cos_ref[bits ^ own_section, col], sin_ref[bits ^ own_section, col] = cos_sin(near_rest[held, (4 - bits) % 3])
         return carry
 
     lax.fori_loop(0, blocks, screens, 0)
@@ -246,7 +246,7 @@
         bits = slice_index ^ own_section
         for col in range(blocks):
             held = col ^ own_place
-            others = jnp.maximum(bits - 1, 0)
+            others = lax.rem(4 - bits, 3)
             in_first = (bits == 0) | (held == 3)
             place = jnp.where(bits == 0, 2 * held, 2 * blocks + others)
             angle = jnp.where(in_first, far_first[place], far_second[jnp.minimum(held, 2) * (count - 1) + others])
@@ -360,9 +360,9 @@
     def params(mebibytes):
         return pltpu.CompilerParams(vmem_limit_bytes=mebibytes * 2**20)
 
-    other_depths = spread(phase, "depth", (1, 3))
-    other_depths[0], measured, slab = lax.optimization_barrier((other_depths[0], intensity, phase))
-    other_depths[1:1] = spread(slab, "depth", (2,))
+    first_depth, farthest, two_away = spread(phase, "depth", (1, 3, 2))
+    first_depth, measured, slab = lax.optimization_barrier((first_depth, intensity, phase))
+    other_depths = [first_depth, farthest, two_away]
     other_depths = jnp.concatenate(other_depths, axis=0)
     packet = jnp.concatenate([slab, measured], axis=0)
     near_own = [packet]

time: 35 us -> 32.3 us (0.923)
  starting transfers between devices: 19 us -> 16.1 us
    ppermute x6, starting transfers between devices: 13.2 us -> 10.3 us  [spread(): pieces.append(lax.ppermute(shard, axis, pairs))]
where the time goes in v23:
time: 32.3 us; the launch traced here: 32.1 us
  starting transfers between devices  16.1 us (50%)
  Pallas kernels  9.13 us (28%)
  waiting for transfers between devices  4.35 us (13%)
  local copies, waits for them, and re-layouts  1.5 us (5%)
  between operations  0.83 us (3%)
    ppermute x6, starting transfers between devices, spread(): pieces.append(lax.ppermute(shard, axis, pairs))  10.3 us
    pallas_call x1, Pallas kernels, whole_field_body(): pl.pallas_call(wave_kernel, out_shape=(array(1, 3, tile_r, tile_c),) * 2,...  7.2 us
    ppermute x2, starting transfers between devices, whole_field_body(): near_own.append(lax.ppermute(packet, 'col', close))  3.94 us
    ppermute x3, waiting for transfers between devices, swap_cores(): return lax.ppermute(value, 'row', [(0, 1), (1, 0)])  2.34 us
    ppermute x6, waiting for transfers between devices, spread(): pieces.append(lax.ppermute(shard, axis, pairs))  2.01 us
    ppermute x1, starting transfers between devices, whole_field_body(): lax.ppermute(slab, 'col', further)  1.52 us
    unnamed x13, local copies, waits for them, and re-layouts  1.46 us
    pallas_call x1, Pallas kernels, whole_field_body(): pl.pallas_call(load_kernel, out_shape=(jax.ShapeDtypeStruct(row_all.shape...  0.89 us
  transfers between devices with their start and end apart: 12, of which 3 were waited for; matrix products, arithmetic and copies ran while one was open for 3% of the time, Pallas kernels for 4%

profile of v23, /device:TPU:0, one launch (start us, length us, event | category | flops | bytes accessed | tf_op | source)
XLA Modules:
  0.0 32.1 jit_solution(17455831547132706866)
XLA Ops:
  0.6 0.0 copy-start.3
  0.6 3.1 %collective-permute-start = (f32[1,64,128]{2,1,0:T(8,128)}, f32[1,64,128]{2,1,0:T(8,128)S(1)}, u32[]{:S(2)}, u32[]{:S(2)}) collective-permute-start(f32[1,64,128]{2,1,0:T(8,128)} %param.5), channel_id=1, source_target_pairs={{0,8},{8,0},{16,24},{24,16},{1,9},{9,1},{17,25},{25,17},{2,10},{10... | collective-permute-start | bytes 98312 | tf_op jit(solution)/shard_map/ppermute | solution.py:340
  3.7 2.5 %collective-permute-start.1 = (f32[1,64,128]{2,1,0:T(8,128)}, f32[1,64,128]{2,1,0:T(8,128)S(1)}, u32[]{:S(2)}, u32[]{:S(2)}) collective-permute-start(f32[1,64,128]{2,1,0:T(8,128)} %param.5), channel_id=1, source_target_pairs={{0,24},{8,16},{16,8},{24,0},{1,25},{9,17},{17,9},{25,1},{2,26},{10... | collective-permute-start | bytes 98312 | tf_op jit(solution)/shard_map/ppermute | solution.py:340
  6.2 0.1 collective-permute-start.2
  6.3 0.0 collective-permute-done
  6.3 0.8 %constant_dynamic-update-slice_fusion.4 = f32[3,64,128]{2,1,0:T(8,128)S(1)} fusion(f32[1,64,128]{2,1,0:T(8,128)} %param.5), kind=kLoop, calls=%fused_computation.9 | loop fusion | bytes 65536
  7.1 1.5 %collective-permute-start.5 = (f32[1,64,128]{2,1,0:T(8,128)}, f32[1,64,128]{2,1,0:T(8,128)S(1)}, u32[]{:S(2)}, u32[]{:S(2)}) collective-permute-start(f32[1,64,128]{2,1,0:T(8,128)} %param.5), channel_id=1, source_target_pairs={{0,2},{1,3},{2,0},{3,1},{4,6},{5,7},{6,4},{7,5},{8,10},{9,11},{10,... | collective-permute-start | bytes 98312 | tf_op jit(solution)/shard_map/ppermute | solution.py:376
  8.6 0.0 copy-done.3
  8.6 0.7 %collective-permute-start.6 = (f32[3,64,128]{2,1,0:T(8,128)S(1)}, f32[3,64,128]{2,1,0:T(8,128)S(1)}, u32[]{:S(2)}, u32[]{:S(2)}) collective-permute-start(f32[3,64,128]{2,1,0:T(8,128)S(1)} %constant_dynamic-update-slice_fusion.3), channel_id=1, source_target_pairs={{1,2},{2,1},{5,6},{6,5},{9,10},{10,9},{13,14},{14,13},{17,18},{18,... | collective-permute-start | bytes 294920 | tf_op jit(solution)/shard_map/ppermute | solution.py:373
  9.3 3.3 %collective-permute-start.4 = (f32[3,64,128]{2,1,0:T(8,128)S(1)}, f32[3,64,128]{2,1,0:T(8,128)S(1)}, u32[]{:S(2)}, u32[]{:S(2)}) collective-permute-start(f32[3,64,128]{2,1,0:T(8,128)S(1)} %constant_dynamic-update-slice_fusion.3), channel_id=1, source_target_pairs={{0,1},{1,0},{2,3},{3,2},{4,5},{5,4},{6,7},{7,6},{8,9},{9,8},{10,11... | collective-permute-start | bytes 294920 | tf_op jit(solution)/shard_map/ppermute | solution.py:373
  12.6 0.0 collective-permute-done.1
  12.6 0.0 copy-start.1
  12.6 0.0 copy-start
  12.7 0.0 collective-permute-done.2
  12.7 0.8 %collective-permute-start.3 = (f32[3,64,128]{2,1,0:T(8,128)S(1)}, f32[3,64,128]{2,1,0:T(8,128)S(1)}, u32[]{:S(2)}, u32[]{:S(2)}) collective-permute-start(f32[3,64,128]{2,1,0:T(8,128)S(1)} %get-tuple-element.49), channel_id=1, source_target_pairs={{1,2},{2,1},{5,6},{6,5},{9,10},{10,9},{13,14},{14,13},{17,18},{18,... | collective-permute-start | bytes 294920 | tf_op jit(solution)/shard_map/ppermute | solution.py:340
  13.5 3.0 %collective-permute-start.8 = (f32[3,64,128]{2,1,0:T(8,128)S(1)}, f32[3,64,128]{2,1,0:T(8,128)S(1)}, u32[]{:S(2)}, u32[]{:S(2)}) collective-permute-start(f32[3,64,128]{2,1,0:T(8,128)S(1)} %get-tuple-element.49), channel_id=1, source_target_pairs={{0,2},{1,3},{2,0},{3,1},{4,6},{5,7},{6,4},{7,5},{8,10},{9,11},{10,... | collective-permute-start | bytes 294920 | tf_op jit(solution)/shard_map/ppermute | solution.py:340
  16.5 0.0 collective-permute-done.5
  16.5 0.8 %collective-permute-start.7 = (f32[3,64,128]{2,1,0:T(8,128)S(1)}, f32[3,64,128]{2,1,0:T(8,128)S(1)}, u32[]{:S(2)}, u32[]{:S(2)}) collective-permute-start(f32[3,64,128]{2,1,0:T(8,128)S(1)} %get-tuple-element.49), channel_id=1, source_target_pairs={{0,1},{1,0},{2,3},{3,2},{4,5},{5,4},{6,7},{7,6},{8,9},{9,8},{10,11... | collective-permute-start | bytes 294920 | tf_op jit(solution)/shard_map/ppermute | solution.py:340
  17.4 0.0 collective-permute-done.6
  17.4 0.0 collective-permute-done.4
  17.4 0.0 copy-start.2
  17.4 0.0 copy-done.1
  17.4 0.0 copy-done
  17.4 0.6 %copy-done.2 = s32[2,2]{1,0:T(2,128)S(1)} copy-done((s32[2,2]{1,0:T(2,128)S(1)}, s32[2,2]{1,0:T(2,128)}, u32[]{:S(2)}) %copy-start.2) | copy-done | bytes 40
  18.1 0.9 %shard_map.68 = (bf16[256,512]{1,0:T(8,128)(2,1)S(1)}, bf16[512,512]{1,0:T(8,128)(2,1)S(1)}, f32[4,2,128,128]{3,2,1,0:T(8,128)S(1)}, f32[4,64,128]{2,1,0:T(8,128)S(1)}, f32[4,64,128]{2,1,0:T(8,128)S(1)}) custom-call(s32[2,2]{1,0:T(2,128)S(1)} %copy-done.2, f32[4,3,64,128]{3,2,1,0:T(8,128)S(1)} %pad_maximum_fusion.near_own, bf16[2,256,512]{2,1,0:T(8,128)(2,1)S(1)} %copy-done, ...), custom_call_target="tpu_custom_call" | custom-call | flops 100000000 | bytes 1048576 | tf_op jit(solution)/shard_map/pallas_call | solution.py:384
  19.0 0.0 collective-permute-done.3
  19.1 0.1 collective-permute-start.9
  19.1 2.0 %collective-permute-done.7 = f32[3,64,128]{2,1,0:T(8,128)S(1)} collective-permute-done((f32[3,64,128]{2,1,0:T(8,128)S(1)}, f32[3,64,128]{2,1,0:T(8,128)S(1)}, u32[]{:S(2)}, u32[]{:S(2)}) %collective-permute-start.7) | collective-permute-done | bytes 98336 | tf_op jit(solution)/shard_map/ppermute | solution.py:340
  21.1 0.0 collective-permute-done.8
  21.2 0.1 collective-permute-start.10
  21.3 0.4 %shard_map.69 = (f32[5,4,64,128]{3,2,1,0:T(8,128)S(1)}, f32[5,4,64,128]{3,2,1,0:T(8,128)S(1)}) custom-call(f32[4,3,64,128]{3,2,1,0:T(8,128)S(1)} %pad_maximum_fusion.1.near_rest, f32[4,64,128]{2,1,0:T(8,128)S(1)} %get-tuple-element.37.own_cos, f32[4,64,128]{2,1,0:T(8,128)S(1)} %get-tuple-element.38.own_sin), custom_call_target="tpu_custom_call" | custom-call | flops 500000000 | bytes 1048576 | tf_op jit(solution)/shard_map/pallas_call | solution.py:408
  21.6 1.2 %collective-permute-done.10.far_second = f32[9,64,128]{2,1,0:T(8,128)S(1)} collective-permute-done((f32[9,64,128]{2,1,0:T(8,128)S(1)}, f32[9,64,128]{2,1,0:T(8,128)S(1)}, u32[]{:S(2)}, u32[]{:S(2)}) %collective-permute-start.10) | collective-permute-done | bytes 294944 | tf_op jit(solution)/shard_map/ppermute | solution.py:345
  22.8 0.0 collective-permute-done.9.far_first
  22.8 7.2 %shard_map.70 = (f32[1,3,64,128]{3,2,1,0:T(8,128)S(1)}, f32[1,3,64,128]{3,2,1,0:T(8,128)S(1)}) custom-call(f32[4,2,128,128]{3,2,1,0:T(8,128)S(1)} %get-tuple-element.35.wave_ref, f32[5,4,64,128]{3,2,1,0:T(8,128)S(1)} %get-tuple-element.39.near_cos, f32[5,4,64,128]{3,2,1,0:T(8,128)S(1)} %get-tuple-element.40.near_sin, ...), custom_call_target="tpu_custom_call" | custom-call | tf_op jit(solution)/shard_map/pallas_call | solution.py:416
  30.0 0.2 collective-permute-start.11
  30.2 1.2 %collective-permute-done.11.received_ref = f32[1,3,64,128]{3,2,1,0:T(8,128)S(1)} collective-permute-done((f32[1,3,64,128]{3,2,1,0:T(8,128)S(1)}, f32[1,3,64,128]{3,2,1,0:T(8,128)S(1)}, u32[]{:S(2)}, u32[]{:S(2)}) %collective-permute-start.11) | collective-permute-done | bytes 98336 | tf_op jit(solution)/shard_map/ppermute | solution.py:345
  31.4 0.7 %shard_map.71 = (f32[1,64,128]{2,1,0:T(8,128)}, f32[2,1,2,64,128]{4,3,2,1,0:T(8,128)}) custom-call(f32[1,3,64,128]{3,2,1,0:T(8,128)S(1)} %get-tuple-element.44.mine_ref, f32[1,3,64,128]{3,2,1,0:T(8,128)S(1)} %collective-permute-done.11.received_ref), custom_call_target="tpu_custom_call" | custom-call | tf_op jit(solution)/shard_map/pallas_call | solution.py:431
  (12 shorter events, 0.2 us)
Async XLA Ops:
  0.6 8.0 %copy-start.3 = (f32[2,64,128]{2,1,0:T(8,128)S(1)}, f32[2,64,128]{2,1,0:T(8,128)}, u32[]{:S(2)}) copy-start(f32[2,64,128]{2,1,0:T(8,128)} %param.7) | copy-start | bytes 196612
  0.6 5.7 %collective-permute-start = (f32[1,64,128]{2,1,0:T(8,128)}, f32[1,64,128]{2,1,0:T(8,128)S(1)}, u32[]{:S(2)}, u32[]{:S(2)}) collective-permute-start(f32[1,64,128]{2,1,0:T(8,128)} %param.5), channel_id=1, source_target_pairs={{0,8},{8,0},{16,24},{24,16},{1,9},{9,1},{17,25},{25,17},{2,10},{10... | collective-permute-start | bytes 98312 | tf_op jit(solution)/shard_map/ppermute | solution.py:340
  3.7 8.9 %collective-permute-start.1 = (f32[1,64,128]{2,1,0:T(8,128)}, f32[1,64,128]{2,1,0:T(8,128)S(1)}, u32[]{:S(2)}, u32[]{:S(2)}) collective-permute-start(f32[1,64,128]{2,1,0:T(8,128)} %param.5), channel_id=1, source_target_pairs={{0,24},{8,16},{16,8},{24,0},{1,25},{9,17},{17,9},{25,1},{2,26},{10... | collective-permute-start | bytes 98312 | tf_op jit(solution)/shard_map/ppermute | solution.py:340
  6.2 6.4 %collective-permute-start.2 = (f32[1,64,128]{2,1,0:T(8,128)}, f32[1,64,128]{2,1,0:T(8,128)S(1)}, u32[]{:S(2)}, u32[]{:S(2)}) collective-permute-start(f32[1,64,128]{2,1,0:T(8,128)} %param.5), channel_id=1, source_target_pairs={{0,16},{8,24},{16,0},{24,8},{1,17},{9,25},{17,1},{25,9},{2,18},{10... | collective-permute-start | bytes 98312 | tf_op jit(solution)/shard_map/ppermute | solution.py:340
  7.1 9.4 %collective-permute-start.5 = (f32[1,64,128]{2,1,0:T(8,128)}, f32[1,64,128]{2,1,0:T(8,128)S(1)}, u32[]{:S(2)}, u32[]{:S(2)}) collective-permute-start(f32[1,64,128]{2,1,0:T(8,128)} %param.5), channel_id=1, source_target_pairs={{0,2},{1,3},{2,0},{3,1},{4,6},{5,7},{6,4},{7,5},{8,10},{9,11},{10,... | collective-permute-start | bytes 98312 | tf_op jit(solution)/shard_map/ppermute | solution.py:376
  8.6 8.7 %collective-permute-start.6 = (f32[3,64,128]{2,1,0:T(8,128)S(1)}, f32[3,64,128]{2,1,0:T(8,128)S(1)}, u32[]{:S(2)}, u32[]{:S(2)}) collective-permute-start(f32[3,64,128]{2,1,0:T(8,128)S(1)} %constant_dynamic-update-slice_fusion.3), channel_id=1, source_target_pairs={{1,2},{2,1},{5,6},{6,5},{9,10},{10,9},{13,14},{14,13},{17,18},{18,... | collective-permute-start | bytes 294920 | tf_op jit(solution)/shard_map/ppermute | solution.py:373
  9.3 8.0 %collective-permute-start.4 = (f32[3,64,128]{2,1,0:T(8,128)S(1)}, f32[3,64,128]{2,1,0:T(8,128)S(1)}, u32[]{:S(2)}, u32[]{:S(2)}) collective-permute-start(f32[3,64,128]{2,1,0:T(8,128)S(1)} %constant_dynamic-update-slice_fusion.3), channel_id=1, source_target_pairs={{0,1},{1,0},{2,3},{3,2},{4,5},{5,4},{6,7},{7,6},{8,9},{9,8},{10,11... | collective-permute-start | bytes 294920 | tf_op jit(solution)/shard_map/ppermute | solution.py:373
  12.6 4.8 %copy-start.1 = (bf16[512,512]{1,0:T(8,128)(2,1)S(1)}, bf16[512,512]{1,0:T(8,128)(2,1)}, u32[]{:S(2)}) copy-start(bf16[512,512]{1,0:T(8,128)(2,1)} %constant.20.clone.col_from) | copy-start | bytes 1572868
  12.6 4.8 %copy-start = (bf16[2,256,512]{2,1,0:T(8,128)(2,1)S(1)}, bf16[2,256,512]{2,1,0:T(8,128)(2,1)}, u32[]{:S(2)}) copy-start(bf16[2,256,512]{2,1,0:T(8,128)(2,1)} %constant.19.clone.row_from) | copy-start | bytes 1572868
  12.7 6.3 %collective-permute-start.3 = (f32[3,64,128]{2,1,0:T(8,128)S(1)}, f32[3,64,128]{2,1,0:T(8,128)S(1)}, u32[]{:S(2)}, u32[]{:S(2)}) collective-permute-start(f32[3,64,128]{2,1,0:T(8,128)S(1)} %get-tuple-element.49), channel_id=1, source_target_pairs={{1,2},{2,1},{5,6},{6,5},{9,10},{10,9},{13,14},{14,13},{17,18},{18,... | collective-permute-start | bytes 294920 | tf_op jit(solution)/shard_map/ppermute | solution.py:340
  13.5 7.7 %collective-permute-start.8 = (f32[3,64,128]{2,1,0:T(8,128)S(1)}, f32[3,64,128]{2,1,0:T(8,128)S(1)}, u32[]{:S(2)}, u32[]{:S(2)}) collective-permute-start(f32[3,64,128]{2,1,0:T(8,128)S(1)} %get-tuple-element.49), channel_id=1, source_target_pairs={{0,2},{1,3},{2,0},{3,1},{4,6},{5,7},{6,4},{7,5},{8,10},{9,11},{10,... | collective-permute-start | bytes 294920 | tf_op jit(solution)/shard_map/ppermute | solution.py:340
  16.5 4.6 %collective-permute-start.7 = (f32[3,64,128]{2,1,0:T(8,128)S(1)}, f32[3,64,128]{2,1,0:T(8,128)S(1)}, u32[]{:S(2)}, u32[]{:S(2)}) collective-permute-start(f32[3,64,128]{2,1,0:T(8,128)S(1)} %get-tuple-element.49), channel_id=1, source_target_pairs={{0,1},{1,0},{2,3},{3,2},{4,5},{5,4},{6,7},{7,6},{8,9},{9,8},{10,11... | collective-permute-start | bytes 294920 | tf_op jit(solution)/shard_map/ppermute | solution.py:340
  17.4 0.7 %copy-start.2 = (s32[2,2]{1,0:T(2,128)S(1)}, s32[2,2]{1,0:T(2,128)}, u32[]{:S(2)}) copy-start(s32[2,2]{1,0:T(2,128)} %tilt_ref.1) | copy-start | bytes 52
  19.1 3.8 %collective-permute-start.9 = (f32[11,64,128]{2,1,0:T(8,128)S(1)}, f32[11,64,128]{2,1,0:T(8,128)S(1)}, u32[]{:S(2)}, u32[]{:S(2)}) collective-permute-start(f32[11,64,128]{2,1,0:T(8,128)S(1)} %pad_maximum_fusion.2), channel_id=1, source_target_pairs={{0,4},{4,0},{1,5},{5,1},{2,6},{6,2},{3,7},{7,3},{8,12},{12,8},{9,1... | collective-permute-start | bytes 1081352 | tf_op jit(solution)/shard_map/ppermute | solution.py:345
  21.2 1.6 %collective-permute-start.10 = (f32[9,64,128]{2,1,0:T(8,128)S(1)}, f32[9,64,128]{2,1,0:T(8,128)S(1)}, u32[]{:S(2)}, u32[]{:S(2)}) collective-permute-start(f32[9,64,128]{2,1,0:T(8,128)S(1)} %constant_dynamic-update-slice_fusion.5), channel_id=1, source_target_pairs={{0,4},{4,0},{1,5},{5,1},{2,6},{6,2},{3,7},{7,3},{8,12},{12,8},{9,1... | collective-permute-start | bytes 884744 | tf_op jit(solution)/shard_map/ppermute | solution.py:345
  30.0 1.4 %collective-permute-start.11 = (f32[1,3,64,128]{3,2,1,0:T(8,128)S(1)}, f32[1,3,64,128]{3,2,1,0:T(8,128)S(1)}, u32[]{:S(2)}, u32[]{:S(2)}) collective-permute-start(f32[1,3,64,128]{3,2,1,0:T(8,128)S(1)} %get-tuple-element.45), channel_id=1, source_target_pairs={{0,4},{4,0},{1,5},{5,1},{2,6},{6,2},{3,7},{7,3},{8,12},{12,8},{9,1... | collective-permute-start | bytes 294920 | tf_op jit(solution)/shard_map/ppermute | solution.py:345

commit v24 on v23

--- a/solution.py
+++ b/solution.py
@@ -365,16 +365,7 @@
     other_depths = [first_depth, farthest, two_away]
     other_depths = jnp.concatenate(other_depths, axis=0)
     packet = jnp.concatenate([slab, measured], axis=0)
-    near_own = [packet]
-    for bits in range(1, blocks):
-        pairs = [(i, i ^ bits) for i in range(blocks)]
-        close = [(i, j) for i, j in pairs if abs(i - j) <= 1]
-        if close:
-            near_own.append(lax.ppermute(packet, "col", close))
-        else:
-            further = [(i, j) for i, j in pairs if abs(i - j) <= 2]
-            arrived = lax.ppermute(slab, "col", further) if further else jnp.zeros_like(slab)
-            near_own.append(jnp.concatenate([arrived, jnp.zeros_like(measured)], axis=0))
+    near_own = [packet] + spread(packet, "col", (1, 2, 3), 2)
     near_own = jnp.stack(near_own)
     arriving = spread(other_depths, "col", (1, 2, 3), 2)
     row_all, col_all = jnp.asarray(row_constant(height)), jnp.asarray(col_constant())

time: 32.3 us -> 33.5 us (1.037)
  waiting for transfers between devices: 4.35 us -> 5.1 us
  starting transfers between devices: 16.1 us -> 16.7 us
    ppermute x6 -> x9, starting transfers between devices: 10.3 us -> 16.3 us  [spread(): pieces.append(lax.ppermute(shard, axis, pairs))]
    ppermute x3 -> x0, starting transfers between devices: 5.46 us -> none  [the longest x2 3.94 us: whole_field_body(): near_own.append(lax.ppermute(packet, 'col', close))]
    ppermute x6 -> x9, waiting for transfers between devices: 2.01 us -> 2.76 us  [spread(): pieces.append(lax.ppermute(shard, axis, pairs))]
where the time goes in v24:
time: 33.5 us; the launch traced here: 33.3 us
  starting transfers between devices  16.7 us (50%)
  Pallas kernels  9.14 us (27%)
  waiting for transfers between devices  5.1 us (15%)
  local copies, waits for them, and re-layouts  1.49 us (4%)
  between operations  0.81 us (2%)
    ppermute x9, starting transfers between devices, spread(): pieces.append(lax.ppermute(shard, axis, pairs))  16.3 us
    pallas_call x1, Pallas kernels, whole_field_body(): pl.pallas_call(wave_kernel, out_shape=(array(1, 3, tile_r, tile_c),) * 2,...  7.21 us
    ppermute x9, waiting for transfers between devices, spread(): pieces.append(lax.ppermute(shard, axis, pairs))  2.76 us
    ppermute x3, waiting for transfers between devices, swap_cores(): return lax.ppermute(value, 'row', [(0, 1), (1, 0)])  2.34 us
    unnamed x13, local copies, waits for them, and re-layouts  1.45 us
    pallas_call x1, Pallas kernels, whole_field_body(): pl.pallas_call(load_kernel, out_shape=(jax.ShapeDtypeStruct(row_all.shape...  0.89 us
    pallas_call x1, Pallas kernels, whole_field_body(): pl.pallas_call(finish_kernel, out_shape=(array(*phase.shape), array(2, 1,...  0.69 us
  transfers between devices with their start and end apart: 12, of which 3 were waited for; matrix products, arithmetic and copies ran while one was open for 3% of the time, Pallas kernels for 4%

profile of v24, /device:TPU:0, one launch (start us, length us, event | category | flops | bytes accessed | tf_op | source)
XLA Modules:
  0.0 33.3 jit_solution(5906107024636388552)
XLA Ops:
  0.6 0.0 copy-start.3
  0.6 3.1 %collective-permute-start = (f32[1,64,128]{2,1,0:T(8,128)}, f32[1,64,128]{2,1,0:T(8,128)S(1)}, u32[]{:S(2)}, u32[]{:S(2)}) collective-permute-start(f32[1,64,128]{2,1,0:T(8,128)} %param.5), channel_id=1, source_target_pairs={{0,8},{8,0},{16,24},{24,16},{1,9},{9,1},{17,25},{25,17},{2,10},{10... | collective-permute-start | bytes 98312 | tf_op jit(solution)/shard_map/ppermute | solution.py:340
  3.7 2.5 %collective-permute-start.1 = (f32[1,64,128]{2,1,0:T(8,128)}, f32[1,64,128]{2,1,0:T(8,128)S(1)}, u32[]{:S(2)}, u32[]{:S(2)}) collective-permute-start(f32[1,64,128]{2,1,0:T(8,128)} %param.5), channel_id=1, source_target_pairs={{0,24},{8,16},{16,8},{24,0},{1,25},{9,17},{17,9},{25,1},{2,26},{10... | collective-permute-start | bytes 98312 | tf_op jit(solution)/shard_map/ppermute | solution.py:340
  6.2 0.1 collective-permute-start.2
  6.3 0.0 collective-permute-done
  6.3 0.8 %constant_dynamic-update-slice_fusion.4 = f32[3,64,128]{2,1,0:T(8,128)S(1)} fusion(f32[1,64,128]{2,1,0:T(8,128)} %param.5), kind=kLoop, calls=%fused_computation.8 | loop fusion | bytes 65536
  7.1 0.0 copy-done.3
  7.1 0.7 %collective-permute-start.6 = (f32[3,64,128]{2,1,0:T(8,128)S(1)}, f32[3,64,128]{2,1,0:T(8,128)S(1)}, u32[]{:S(2)}, u32[]{:S(2)}) collective-permute-start(f32[3,64,128]{2,1,0:T(8,128)S(1)} %constant_dynamic-update-slice_fusion.3), channel_id=1, source_target_pairs={{1,2},{2,1},{5,6},{6,5},{9,10},{10,9},{13,14},{14,13},{17,18},{18,... | collective-permute-start | bytes 294920 | tf_op jit(solution)/shard_map/ppermute | solution.py:340
  7.8 4.3 %collective-permute-start.5 = (f32[3,64,128]{2,1,0:T(8,128)S(1)}, f32[3,64,128]{2,1,0:T(8,128)S(1)}, u32[]{:S(2)}, u32[]{:S(2)}) collective-permute-start(f32[3,64,128]{2,1,0:T(8,128)S(1)} %constant_dynamic-update-slice_fusion.3), channel_id=1, source_target_pairs={{0,2},{1,3},{2,0},{3,1},{4,6},{5,7},{6,4},{7,5},{8,10},{9,11},{10,... | collective-permute-start | bytes 294920 | tf_op jit(solution)/shard_map/ppermute | solution.py:340
  12.1 0.1 collective-permute-start.4
  12.2 0.0 copy-start.1
  12.2 0.0 copy-start
  12.2 0.0 collective-permute-done.1
  12.2 0.0 collective-permute-done.2
  12.2 0.8 %collective-permute-start.3 = (f32[3,64,128]{2,1,0:T(8,128)S(1)}, f32[3,64,128]{2,1,0:T(8,128)S(1)}, u32[]{:S(2)}, u32[]{:S(2)}) collective-permute-start(f32[3,64,128]{2,1,0:T(8,128)S(1)} %get-tuple-element.49), channel_id=1, source_target_pairs={{1,2},{2,1},{5,6},{6,5},{9,10},{10,9},{13,14},{14,13},{17,18},{18,... | collective-permute-start | bytes 294920 | tf_op jit(solution)/shard_map/ppermute | solution.py:340
  13.0 4.7 %collective-permute-start.8 = (f32[3,64,128]{2,1,0:T(8,128)S(1)}, f32[3,64,128]{2,1,0:T(8,128)S(1)}, u32[]{:S(2)}, u32[]{:S(2)}) collective-permute-start(f32[3,64,128]{2,1,0:T(8,128)S(1)} %get-tuple-element.49), channel_id=1, source_target_pairs={{0,2},{1,3},{2,0},{3,1},{4,6},{5,7},{6,4},{7,5},{8,10},{9,11},{10,... | collective-permute-start | bytes 294920 | tf_op jit(solution)/shard_map/ppermute | solution.py:340
  17.7 0.0 collective-permute-done.6
  17.7 0.1 collective-permute-start.7
  17.9 0.0 collective-permute-done.5
  17.9 0.0 collective-permute-done.4
  17.9 0.0 copy-start.2
  17.9 0.0 copy-done.1
  17.9 0.0 copy-done
  17.9 0.6 %copy-done.2 = s32[2,2]{1,0:T(2,128)S(1)} copy-done((s32[2,2]{1,0:T(2,128)S(1)}, s32[2,2]{1,0:T(2,128)}, u32[]{:S(2)}) %copy-start.2) | copy-done | bytes 40
  18.5 0.9 %shard_map.68 = (bf16[256,512]{1,0:T(8,128)(2,1)S(1)}, bf16[512,512]{1,0:T(8,128)(2,1)S(1)}, f32[4,2,128,128]{3,2,1,0:T(8,128)S(1)}, f32[4,64,128]{2,1,0:T(8,128)S(1)}, f32[4,64,128]{2,1,0:T(8,128)S(1)}) custom-call(s32[2,2]{1,0:T(2,128)S(1)} %copy-done.2, f32[4,3,64,128]{3,2,1,0:T(8,128)S(1)} %pad_maximum_fusion.near_own, bf16[2,256,512]{2,1,0:T(8,128)(2,1)S(1)} %copy-done, ...), custom_call_target="tpu_custom_call" | custom-call | flops 100000000 | bytes 1048576 | tf_op jit(solution)/shard_map/pallas_call | solution.py:375
  19.4 0.0 collective-permute-done.3
  19.5 0.1 collective-permute-start.9
  19.6 2.7 %collective-permute-done.7 = f32[3,64,128]{2,1,0:T(8,128)S(1)} collective-permute-done((f32[3,64,128]{2,1,0:T(8,128)S(1)}, f32[3,64,128]{2,1,0:T(8,128)S(1)}, u32[]{:S(2)}, u32[]{:S(2)}) %collective-permute-start.7) | collective-permute-done | bytes 98336 | tf_op jit(solution)/shard_map/ppermute | solution.py:340
  22.4 0.0 collective-permute-done.8
  22.4 0.1 collective-permute-start.10
  22.5 0.4 %shard_map.69 = (f32[5,4,64,128]{3,2,1,0:T(8,128)S(1)}, f32[5,4,64,128]{3,2,1,0:T(8,128)S(1)}) custom-call(f32[4,3,64,128]{3,2,1,0:T(8,128)S(1)} %pad_maximum_fusion.1.near_rest, f32[4,64,128]{2,1,0:T(8,128)S(1)} %get-tuple-element.37.own_cos, f32[4,64,128]{2,1,0:T(8,128)S(1)} %get-tuple-element.38.own_sin), custom_call_target="tpu_custom_call" | custom-call | flops 500000000 | bytes 1048576 | tf_op jit(solution)/shard_map/pallas_call | solution.py:399
  22.9 1.2 %collective-permute-done.10.far_second = f32[9,64,128]{2,1,0:T(8,128)S(1)} collective-permute-done((f32[9,64,128]{2,1,0:T(8,128)S(1)}, f32[9,64,128]{2,1,0:T(8,128)S(1)}, u32[]{:S(2)}, u32[]{:S(2)}) %collective-permute-start.10) | collective-permute-done | bytes 294944 | tf_op jit(solution)/shard_map/ppermute | solution.py:345
  24.0 0.0 collective-permute-done.9.far_first
  24.0 7.2 %shard_map.70 = (f32[1,3,64,128]{3,2,1,0:T(8,128)S(1)}, f32[1,3,64,128]{3,2,1,0:T(8,128)S(1)}) custom-call(f32[4,2,128,128]{3,2,1,0:T(8,128)S(1)} %get-tuple-element.35.wave_ref, f32[5,4,64,128]{3,2,1,0:T(8,128)S(1)} %get-tuple-element.39.near_cos, f32[5,4,64,128]{3,2,1,0:T(8,128)S(1)} %get-tuple-element.40.near_sin, ...), custom_call_target="tpu_custom_call" | custom-call | tf_op jit(solution)/shard_map/pallas_call | solution.py:407
  31.3 0.2 collective-permute-start.11
  31.5 1.2 %collective-permute-done.11.received_ref = f32[1,3,64,128]{3,2,1,0:T(8,128)S(1)} collective-permute-done((f32[1,3,64,128]{3,2,1,0:T(8,128)S(1)}, f32[1,3,64,128]{3,2,1,0:T(8,128)S(1)}, u32[]{:S(2)}, u32[]{:S(2)}) %collective-permute-start.11) | collective-permute-done | bytes 98336 | tf_op jit(solution)/shard_map/ppermute | solution.py:345
  32.6 0.7 %shard_map.71 = (f32[1,64,128]{2,1,0:T(8,128)}, f32[2,1,2,64,128]{4,3,2,1,0:T(8,128)}) custom-call(f32[1,3,64,128]{3,2,1,0:T(8,128)S(1)} %get-tuple-element.44.mine_ref, f32[1,3,64,128]{3,2,1,0:T(8,128)S(1)} %collective-permute-done.11.received_ref), custom_call_target="tpu_custom_call" | custom-call | tf_op jit(solution)/shard_map/pallas_call | solution.py:422
  (11 shorter events, 0.2 us)
Async XLA Ops:
  0.6 6.5 %copy-start.3 = (f32[2,64,128]{2,1,0:T(8,128)S(1)}, f32[2,64,128]{2,1,0:T(8,128)}, u32[]{:S(2)}) copy-start(f32[2,64,128]{2,1,0:T(8,128)} %param.7) | copy-start | bytes 196612
  0.6 5.7 %collective-permute-start = (f32[1,64,128]{2,1,0:T(8,128)}, f32[1,64,128]{2,1,0:T(8,128)S(1)}, u32[]{:S(2)}, u32[]{:S(2)}) collective-permute-start(f32[1,64,128]{2,1,0:T(8,128)} %param.5), channel_id=1, source_target_pairs={{0,8},{8,0},{16,24},{24,16},{1,9},{9,1},{17,25},{25,17},{2,10},{10... | collective-permute-start | bytes 98312 | tf_op jit(solution)/shard_map/ppermute | solution.py:340
  3.7 8.5 %collective-permute-start.1 = (f32[1,64,128]{2,1,0:T(8,128)}, f32[1,64,128]{2,1,0:T(8,128)S(1)}, u32[]{:S(2)}, u32[]{:S(2)}) collective-permute-start(f32[1,64,128]{2,1,0:T(8,128)} %param.5), channel_id=1, source_target_pairs={{0,24},{8,16},{16,8},{24,0},{1,25},{9,17},{17,9},{25,1},{2,26},{10... | collective-permute-start | bytes 98312 | tf_op jit(solution)/shard_map/ppermute | solution.py:340
  6.2 6.0 %collective-permute-start.2 = (f32[1,64,128]{2,1,0:T(8,128)}, f32[1,64,128]{2,1,0:T(8,128)S(1)}, u32[]{:S(2)}, u32[]{:S(2)}) collective-permute-start(f32[1,64,128]{2,1,0:T(8,128)} %param.5), channel_id=1, source_target_pairs={{0,16},{8,24},{16,0},{24,8},{1,17},{9,25},{17,1},{25,9},{2,18},{10... | collective-permute-start | bytes 98312 | tf_op jit(solution)/shard_map/ppermute | solution.py:340
  7.1 10.6 %collective-permute-start.6 = (f32[3,64,128]{2,1,0:T(8,128)S(1)}, f32[3,64,128]{2,1,0:T(8,128)S(1)}, u32[]{:S(2)}, u32[]{:S(2)}) collective-permute-start(f32[3,64,128]{2,1,0:T(8,128)S(1)} %constant_dynamic-update-slice_fusion.3), channel_id=1, source_target_pairs={{1,2},{2,1},{5,6},{6,5},{9,10},{10,9},{13,14},{14,13},{17,18},{18,... | collective-permute-start | bytes 294920 | tf_op jit(solution)/shard_map/ppermute | solution.py:340
  7.8 10.1 %collective-permute-start.5 = (f32[3,64,128]{2,1,0:T(8,128)S(1)}, f32[3,64,128]{2,1,0:T(8,128)S(1)}, u32[]{:S(2)}, u32[]{:S(2)}) collective-permute-start(f32[3,64,128]{2,1,0:T(8,128)S(1)} %constant_dynamic-update-slice_fusion.3), channel_id=1, source_target_pairs={{0,2},{1,3},{2,0},{3,1},{4,6},{5,7},{6,4},{7,5},{8,10},{9,11},{10,... | collective-permute-start | bytes 294920 | tf_op jit(solution)/shard_map/ppermute | solution.py:340
  12.1 5.8 %collective-permute-start.4 = (f32[3,64,128]{2,1,0:T(8,128)S(1)}, f32[3,64,128]{2,1,0:T(8,128)S(1)}, u32[]{:S(2)}, u32[]{:S(2)}) collective-permute-start(f32[3,64,128]{2,1,0:T(8,128)S(1)} %constant_dynamic-update-slice_fusion.3), channel_id=1, source_target_pairs={{0,1},{1,0},{2,3},{3,2},{4,5},{5,4},{6,7},{7,6},{8,9},{9,8},{10,11... | collective-permute-start | bytes 294920 | tf_op jit(solution)/shard_map/ppermute | solution.py:340
  12.2 5.7 %copy-start.1 = (bf16[512,512]{1,0:T(8,128)(2,1)S(1)}, bf16[512,512]{1,0:T(8,128)(2,1)}, u32[]{:S(2)}) copy-start(bf16[512,512]{1,0:T(8,128)(2,1)} %constant.18.clone.col_from) | copy-start | bytes 1572868
  12.2 5.7 %copy-start = (bf16[2,256,512]{2,1,0:T(8,128)(2,1)S(1)}, bf16[2,256,512]{2,1,0:T(8,128)(2,1)}, u32[]{:S(2)}) copy-start(bf16[2,256,512]{2,1,0:T(8,128)(2,1)} %constant.17.clone.row_from) | copy-start | bytes 1572868
  12.2 7.2 %collective-permute-start.3 = (f32[3,64,128]{2,1,0:T(8,128)S(1)}, f32[3,64,128]{2,1,0:T(8,128)S(1)}, u32[]{:S(2)}, u32[]{:S(2)}) collective-permute-start(f32[3,64,128]{2,1,0:T(8,128)S(1)} %get-tuple-element.49), channel_id=1, source_target_pairs={{1,2},{2,1},{5,6},{6,5},{9,10},{10,9},{13,14},{14,13},{17,18},{18,... | collective-permute-start | bytes 294920 | tf_op jit(solution)/shard_map/ppermute | solution.py:340
  13.0 9.3 %collective-permute-start.8 = (f32[3,64,128]{2,1,0:T(8,128)S(1)}, f32[3,64,128]{2,1,0:T(8,128)S(1)}, u32[]{:S(2)}, u32[]{:S(2)}) collective-permute-start(f32[3,64,128]{2,1,0:T(8,128)S(1)} %get-tuple-element.49), channel_id=1, source_target_pairs={{0,2},{1,3},{2,0},{3,1},{4,6},{5,7},{6,4},{7,5},{8,10},{9,11},{10,... | collective-permute-start | bytes 294920 | tf_op jit(solution)/shard_map/ppermute | solution.py:340
  17.7 4.6 %collective-permute-start.7 = (f32[3,64,128]{2,1,0:T(8,128)S(1)}, f32[3,64,128]{2,1,0:T(8,128)S(1)}, u32[]{:S(2)}, u32[]{:S(2)}) collective-permute-start(f32[3,64,128]{2,1,0:T(8,128)S(1)} %get-tuple-element.49), channel_id=1, source_target_pairs={{0,1},{1,0},{2,3},{3,2},{4,5},{5,4},{6,7},{7,6},{8,9},{9,8},{10,11... | collective-permute-start | bytes 294920 | tf_op jit(solution)/shard_map/ppermute | solution.py:340
  17.9 0.7 %copy-start.2 = (s32[2,2]{1,0:T(2,128)S(1)}, s32[2,2]{1,0:T(2,128)}, u32[]{:S(2)}) copy-start(s32[2,2]{1,0:T(2,128)} %tilt_ref.1) | copy-start | bytes 52
  19.5 4.5 %collective-permute-start.9 = (f32[11,64,128]{2,1,0:T(8,128)S(1)}, f32[11,64,128]{2,1,0:T(8,128)S(1)}, u32[]{:S(2)}, u32[]{:S(2)}) collective-permute-start(f32[11,64,128]{2,1,0:T(8,128)S(1)} %pad_maximum_fusion.2), channel_id=1, source_target_pairs={{0,4},{4,0},{1,5},{5,1},{2,6},{6,2},{3,7},{7,3},{8,12},{12,8},{9,1... | collective-permute-start | bytes 1081352 | tf_op jit(solution)/shard_map/ppermute | solution.py:345
  22.4 1.6 %collective-permute-start.10 = (f32[9,64,128]{2,1,0:T(8,128)S(1)}, f32[9,64,128]{2,1,0:T(8,128)S(1)}, u32[]{:S(2)}, u32[]{:S(2)}) collective-permute-start(f32[9,64,128]{2,1,0:T(8,128)S(1)} %constant_dynamic-update-slice_fusion.5), channel_id=1, source_target_pairs={{0,4},{4,0},{1,5},{5,1},{2,6},{6,2},{3,7},{7,3},{8,12},{12,8},{9,1... | collective-permute-start | bytes 884744 | tf_op jit(solution)/shard_map/ppermute | solution.py:345
  31.3 1.4 %collective-permute-start.11 = (f32[1,3,64,128]{3,2,1,0:T(8,128)S(1)}, f32[1,3,64,128]{3,2,1,0:T(8,128)S(1)}, u32[]{:S(2)}, u32[]{:S(2)}) collective-permute-start(f32[1,3,64,128]{3,2,1,0:T(8,128)S(1)} %get-tuple-element.45), channel_id=1, source_target_pairs={{0,4},{4,0},{1,5},{5,1},{2,6},{6,2},{3,7},{7,3},{8,12},{12,8},{9,1... | collective-permute-start | bytes 294920 | tf_op jit(solution)/shard_map/ppermute | solution.py:345

commit v25 on v23

--- a/solution.py
+++ b/solution.py
@@ -103,14 +103,22 @@
     return cos * real - sin * imag, cos * imag + sin * real
 
 
-def row_product(row_matrix, columns):
-    high, low = halves(columns)
-    whole, width = columns.shape
-    wide = jnp.dot(
-        row_matrix[:, :whole], jnp.concatenate([high, low], axis=1), preferred_element_type=jnp.float32
-    )
-    rest = jnp.dot(row_matrix[:, whole:], high, preferred_element_type=jnp.float32)
-    return wide[:, :width] + wide[:, width:] + rest
+def row_products(row_matrix, chunks):
+    whole = row_matrix.shape[0]
+    highs, wides = [], []
+    for columns in chunks:
+        high, low = halves(columns)
+        highs.append(high)
+        wide = jnp.dot(
+            row_matrix[:, :whole], jnp.concatenate([high, low], axis=1), preferred_element_type=jnp.float32
+        )
+        wides.append(wide[:, : columns.shape[1]] + wide[:, columns.shape[1] :])
+    rest = jnp.dot(row_matrix[:, whole:], jnp.concatenate(highs, axis=1), preferred_element_type=jnp.float32)
+    done, begin = [], 0
+    for wide in wides:
+        done.append(wide + rest[:, begin : begin + wide.shape[1]])
+        begin += wide.shape[1]
+    return done
 
 
 def col_product(high, low, col_ref):
@@ -129,11 +137,14 @@
     size, height = len(waves), waves[0][0].shape[0]
     chunks = [range(place, min(place + 2, size)) for place in range(0, size, 2)]
     highs, lows = [], []
-    for chunk in chunks:
-        columns = [
-            jnp.concatenate(turned(slice_index, start + place, screens, waves[place]), axis=0) for place in chunk
-        ]
-        done = row_product(row_matrix, jnp.concatenate(columns, axis=1))
+    columns = [
+        jnp.concatenate(
+            [jnp.concatenate(turned(slice_index, start + place, screens, waves[place]), axis=0) for place in chunk],
+            axis=1,
+        )
+        for chunk in chunks
+    ]
+    for chunk, done in zip(chunks, row_products(row_matrix, columns)):
         for sub, place in enumerate(chunk):
             own_high, own_low = [], []
             for part in range(2):
@@ -298,7 +309,7 @@
     edge_cells = jnp.where(
         lane < LANES // 2, jnp.where(has_right, cells(right), 0.0), jnp.where(has_left, cells(left), 0.0)
     )
-    done = row_product(row_matrix, jnp.concatenate([cells(own_place), edge_cells], axis=1))
+    done = row_products(row_matrix, [jnp.concatenate([cells(own_place), edge_cells], axis=1)])[0]
     lane = lax.broadcasted_iota(jnp.int32, (height, LANES), 1)
     between = (lane >= HALO) & (lane < LANES - HALO)
     highs, lows, edges = [], [], []

time: 32.3 us -> 32.3 us (level)
  no operation moved by 1% of the time
where the time goes in v25:
time: 32.3 us; the launch traced here: 32 us
  starting transfers between devices  16.2 us (50%)
  Pallas kernels  9.08 us (28%)
  waiting for transfers between devices  4.34 us (13%)
  local copies, waits for them, and re-layouts  1.5 us (5%)
  between operations  0.83 us (3%)
    ppermute x6, starting transfers between devices, spread(): pieces.append(lax.ppermute(shard, axis, pairs))  10.3 us
    pallas_call x1, Pallas kernels, whole_field_body(): pl.pallas_call(wave_kernel, out_shape=(array(1, 3, tile_r, tile_c),) * 2,...  7.15 us
    ppermute x2, starting transfers between devices, whole_field_body(): near_own.append(lax.ppermute(packet, 'col', close))  3.94 us
    ppermute x3, waiting for transfers between devices, swap_cores(): return lax.ppermute(value, 'row', [(0, 1), (1, 0)])  2.32 us
    ppermute x6, waiting for transfers between devices, spread(): pieces.append(lax.ppermute(shard, axis, pairs))  2.01 us
    ppermute x1, starting transfers between devices, whole_field_body(): lax.ppermute(slab, 'col', further)  1.52 us
    unnamed x13, local copies, waits for them, and re-layouts  1.46 us
    pallas_call x1, Pallas kernels, whole_field_body(): pl.pallas_call(load_kernel, out_shape=(jax.ShapeDtypeStruct(row_all.shape...  0.89 us
  transfers between devices with their start and end apart: 12, of which 3 were waited for; matrix products, arithmetic and copies ran while one was open for 3% of the time, Pallas kernels for 4%

profile of v25, /device:TPU:0, one launch (start us, length us, event | category | flops | bytes accessed | tf_op | source)
XLA Modules:
  0.0 32.0 jit_solution(2603601442665657154)
XLA Ops:
  0.6 0.0 copy-start.3
  0.6 3.1 %collective-permute-start = (f32[1,64,128]{2,1,0:T(8,128)}, f32[1,64,128]{2,1,0:T(8,128)S(1)}, u32[]{:S(2)}, u32[]{:S(2)}) collective-permute-start(f32[1,64,128]{2,1,0:T(8,128)} %param.5), channel_id=1, source_target_pairs={{0,8},{8,0},{16,24},{24,16},{1,9},{9,1},{17,25},{25,17},{2,10},{10... | collective-permute-start | bytes 98312 | tf_op jit(solution)/shard_map/ppermute | solution.py:351
  3.7 2.5 %collective-permute-start.1 = (f32[1,64,128]{2,1,0:T(8,128)}, f32[1,64,128]{2,1,0:T(8,128)S(1)}, u32[]{:S(2)}, u32[]{:S(2)}) collective-permute-start(f32[1,64,128]{2,1,0:T(8,128)} %param.5), channel_id=1, source_target_pairs={{0,24},{8,16},{16,8},{24,0},{1,25},{9,17},{17,9},{25,1},{2,26},{10... | collective-permute-start | bytes 98312 | tf_op jit(solution)/shard_map/ppermute | solution.py:351
  6.2 0.1 collective-permute-start.2
  6.3 0.0 collective-permute-done
  6.3 0.8 %constant_dynamic-update-slice_fusion.4 = f32[3,64,128]{2,1,0:T(8,128)S(1)} fusion(f32[1,64,128]{2,1,0:T(8,128)} %param.5), kind=kLoop, calls=%fused_computation.9 | loop fusion | bytes 65536
  7.1 1.5 %collective-permute-start.5 = (f32[1,64,128]{2,1,0:T(8,128)}, f32[1,64,128]{2,1,0:T(8,128)S(1)}, u32[]{:S(2)}, u32[]{:S(2)}) collective-permute-start(f32[1,64,128]{2,1,0:T(8,128)} %param.5), channel_id=1, source_target_pairs={{0,2},{1,3},{2,0},{3,1},{4,6},{5,7},{6,4},{7,5},{8,10},{9,11},{10,... | collective-permute-start | bytes 98312 | tf_op jit(solution)/shard_map/ppermute | solution.py:387
  8.6 0.0 copy-done.3
  8.6 0.7 %collective-permute-start.6 = (f32[3,64,128]{2,1,0:T(8,128)S(1)}, f32[3,64,128]{2,1,0:T(8,128)S(1)}, u32[]{:S(2)}, u32[]{:S(2)}) collective-permute-start(f32[3,64,128]{2,1,0:T(8,128)S(1)} %constant_dynamic-update-slice_fusion.3), channel_id=1, source_target_pairs={{1,2},{2,1},{5,6},{6,5},{9,10},{10,9},{13,14},{14,13},{17,18},{18,... | collective-permute-start | bytes 294920 | tf_op jit(solution)/shard_map/ppermute | solution.py:384
  9.3 3.3 %collective-permute-start.4 = (f32[3,64,128]{2,1,0:T(8,128)S(1)}, f32[3,64,128]{2,1,0:T(8,128)S(1)}, u32[]{:S(2)}, u32[]{:S(2)}) collective-permute-start(f32[3,64,128]{2,1,0:T(8,128)S(1)} %constant_dynamic-update-slice_fusion.3), channel_id=1, source_target_pairs={{0,1},{1,0},{2,3},{3,2},{4,5},{5,4},{6,7},{7,6},{8,9},{9,8},{10,11... | collective-permute-start | bytes 294920 | tf_op jit(solution)/shard_map/ppermute | solution.py:384
  12.6 0.0 collective-permute-done.1
  12.6 0.0 copy-start.1
  12.6 0.0 copy-start
  12.7 0.0 collective-permute-done.2
  12.7 0.8 %collective-permute-start.3 = (f32[3,64,128]{2,1,0:T(8,128)S(1)}, f32[3,64,128]{2,1,0:T(8,128)S(1)}, u32[]{:S(2)}, u32[]{:S(2)}) collective-permute-start(f32[3,64,128]{2,1,0:T(8,128)S(1)} %get-tuple-element.49), channel_id=1, source_target_pairs={{1,2},{2,1},{5,6},{6,5},{9,10},{10,9},{13,14},{14,13},{17,18},{18,... | collective-permute-start | bytes 294920 | tf_op jit(solution)/shard_map/ppermute | solution.py:351
  13.5 3.0 %collective-permute-start.8 = (f32[3,64,128]{2,1,0:T(8,128)S(1)}, f32[3,64,128]{2,1,0:T(8,128)S(1)}, u32[]{:S(2)}, u32[]{:S(2)}) collective-permute-start(f32[3,64,128]{2,1,0:T(8,128)S(1)} %get-tuple-element.49), channel_id=1, source_target_pairs={{0,2},{1,3},{2,0},{3,1},{4,6},{5,7},{6,4},{7,5},{8,10},{9,11},{10,... | collective-permute-start | bytes 294920 | tf_op jit(solution)/shard_map/ppermute | solution.py:351
  16.5 0.0 collective-permute-done.5
  16.5 0.8 %collective-permute-start.7 = (f32[3,64,128]{2,1,0:T(8,128)S(1)}, f32[3,64,128]{2,1,0:T(8,128)S(1)}, u32[]{:S(2)}, u32[]{:S(2)}) collective-permute-start(f32[3,64,128]{2,1,0:T(8,128)S(1)} %get-tuple-element.49), channel_id=1, source_target_pairs={{0,1},{1,0},{2,3},{3,2},{4,5},{5,4},{6,7},{7,6},{8,9},{9,8},{10,11... | collective-permute-start | bytes 294920 | tf_op jit(solution)/shard_map/ppermute | solution.py:351
  17.4 0.0 collective-permute-done.6
  17.4 0.0 collective-permute-done.4
  17.4 0.0 copy-start.2
  17.4 0.0 copy-done.1
  17.4 0.0 copy-done
  17.4 0.6 %copy-done.2 = s32[2,2]{1,0:T(2,128)S(1)} copy-done((s32[2,2]{1,0:T(2,128)S(1)}, s32[2,2]{1,0:T(2,128)}, u32[]{:S(2)}) %copy-start.2) | copy-done | bytes 40
  18.1 0.9 %shard_map.68 = (bf16[256,512]{1,0:T(8,128)(2,1)S(1)}, bf16[512,512]{1,0:T(8,128)(2,1)S(1)}, f32[4,2,128,128]{3,2,1,0:T(8,128)S(1)}, f32[4,64,128]{2,1,0:T(8,128)S(1)}, f32[4,64,128]{2,1,0:T(8,128)S(1)}) custom-call(s32[2,2]{1,0:T(2,128)S(1)} %copy-done.2, f32[4,3,64,128]{3,2,1,0:T(8,128)S(1)} %pad_maximum_fusion.near_own, bf16[2,256,512]{2,1,0:T(8,128)(2,1)S(1)} %copy-done, ...), custom_call_target="tpu_custom_call" | custom-call | flops 100000000 | bytes 1048576 | tf_op jit(solution)/shard_map/pallas_call | solution.py:395
  19.0 0.0 collective-permute-done.3
  19.1 0.1 collective-permute-start.9
  19.1 2.0 %collective-permute-done.7 = f32[3,64,128]{2,1,0:T(8,128)S(1)} collective-permute-done((f32[3,64,128]{2,1,0:T(8,128)S(1)}, f32[3,64,128]{2,1,0:T(8,128)S(1)}, u32[]{:S(2)}, u32[]{:S(2)}) %collective-permute-start.7) | collective-permute-done | bytes 98336 | tf_op jit(solution)/shard_map/ppermute | solution.py:351
  21.1 0.0 collective-permute-done.8
  21.2 0.1 collective-permute-start.10
  21.3 0.4 %shard_map.69 = (f32[5,4,64,128]{3,2,1,0:T(8,128)S(1)}, f32[5,4,64,128]{3,2,1,0:T(8,128)S(1)}) custom-call(f32[4,3,64,128]{3,2,1,0:T(8,128)S(1)} %pad_maximum_fusion.1.near_rest, f32[4,64,128]{2,1,0:T(8,128)S(1)} %get-tuple-element.37.own_cos, f32[4,64,128]{2,1,0:T(8,128)S(1)} %get-tuple-element.38.own_sin), custom_call_target="tpu_custom_call" | custom-call | flops 500000000 | bytes 1048576 | tf_op jit(solution)/shard_map/pallas_call | solution.py:419
  21.6 1.2 %collective-permute-done.10.far_second = f32[9,64,128]{2,1,0:T(8,128)S(1)} collective-permute-done((f32[9,64,128]{2,1,0:T(8,128)S(1)}, f32[9,64,128]{2,1,0:T(8,128)S(1)}, u32[]{:S(2)}, u32[]{:S(2)}) %collective-permute-start.10) | collective-permute-done | bytes 294944 | tf_op jit(solution)/shard_map/ppermute | solution.py:356
  22.8 0.0 collective-permute-done.9.far_first
  22.8 7.2 %shard_map.70 = (f32[1,3,64,128]{3,2,1,0:T(8,128)S(1)}, f32[1,3,64,128]{3,2,1,0:T(8,128)S(1)}) custom-call(f32[4,2,128,128]{3,2,1,0:T(8,128)S(1)} %get-tuple-element.35.wave_ref, f32[5,4,64,128]{3,2,1,0:T(8,128)S(1)} %get-tuple-element.39.near_cos, f32[5,4,64,128]{3,2,1,0:T(8,128)S(1)} %get-tuple-element.40.near_sin, ...), custom_call_target="tpu_custom_call" | custom-call | tf_op jit(solution)/shard_map/pallas_call | solution.py:427
  30.0 0.2 collective-permute-start.11
  30.2 1.1 %collective-permute-done.11.received_ref = f32[1,3,64,128]{3,2,1,0:T(8,128)S(1)} collective-permute-done((f32[1,3,64,128]{3,2,1,0:T(8,128)S(1)}, f32[1,3,64,128]{3,2,1,0:T(8,128)S(1)}, u32[]{:S(2)}, u32[]{:S(2)}) %collective-permute-start.11) | collective-permute-done | bytes 98336 | tf_op jit(solution)/shard_map/ppermute | solution.py:356
  31.3 0.7 %shard_map.71 = (f32[1,64,128]{2,1,0:T(8,128)}, f32[2,1,2,64,128]{4,3,2,1,0:T(8,128)}) custom-call(f32[1,3,64,128]{3,2,1,0:T(8,128)S(1)} %get-tuple-element.44.mine_ref, f32[1,3,64,128]{3,2,1,0:T(8,128)S(1)} %collective-permute-done.11.received_ref), custom_call_target="tpu_custom_call" | custom-call | tf_op jit(solution)/shard_map/pallas_call | solution.py:442
  (12 shorter events, 0.2 us)
Async XLA Ops:
  0.6 8.0 %copy-start.3 = (f32[2,64,128]{2,1,0:T(8,128)S(1)}, f32[2,64,128]{2,1,0:T(8,128)}, u32[]{:S(2)}) copy-start(f32[2,64,128]{2,1,0:T(8,128)} %param.7) | copy-start | bytes 196612
  0.6 5.7 %collective-permute-start = (f32[1,64,128]{2,1,0:T(8,128)}, f32[1,64,128]{2,1,0:T(8,128)S(1)}, u32[]{:S(2)}, u32[]{:S(2)}) collective-permute-start(f32[1,64,128]{2,1,0:T(8,128)} %param.5), channel_id=1, source_target_pairs={{0,8},{8,0},{16,24},{24,16},{1,9},{9,1},{17,25},{25,17},{2,10},{10... | collective-permute-start | bytes 98312 | tf_op jit(solution)/shard_map/ppermute | solution.py:351
  3.7 8.9 %collective-permute-start.1 = (f32[1,64,128]{2,1,0:T(8,128)}, f32[1,64,128]{2,1,0:T(8,128)S(1)}, u32[]{:S(2)}, u32[]{:S(2)}) collective-permute-start(f32[1,64,128]{2,1,0:T(8,128)} %param.5), channel_id=1, source_target_pairs={{0,24},{8,16},{16,8},{24,0},{1,25},{9,17},{17,9},{25,1},{2,26},{10... | collective-permute-start | bytes 98312 | tf_op jit(solution)/shard_map/ppermute | solution.py:351
  6.2 6.4 %collective-permute-start.2 = (f32[1,64,128]{2,1,0:T(8,128)}, f32[1,64,128]{2,1,0:T(8,128)S(1)}, u32[]{:S(2)}, u32[]{:S(2)}) collective-permute-start(f32[1,64,128]{2,1,0:T(8,128)} %param.5), channel_id=1, source_target_pairs={{0,16},{8,24},{16,0},{24,8},{1,17},{9,25},{17,1},{25,9},{2,18},{10... | collective-permute-start | bytes 98312 | tf_op jit(solution)/shard_map/ppermute | solution.py:351
  7.1 9.4 %collective-permute-start.5 = (f32[1,64,128]{2,1,0:T(8,128)}, f32[1,64,128]{2,1,0:T(8,128)S(1)}, u32[]{:S(2)}, u32[]{:S(2)}) collective-permute-start(f32[1,64,128]{2,1,0:T(8,128)} %param.5), channel_id=1, source_target_pairs={{0,2},{1,3},{2,0},{3,1},{4,6},{5,7},{6,4},{7,5},{8,10},{9,11},{10,... | collective-permute-start | bytes 98312 | tf_op jit(solution)/shard_map/ppermute | solution.py:387
  8.6 8.7 %collective-permute-start.6 = (f32[3,64,128]{2,1,0:T(8,128)S(1)}, f32[3,64,128]{2,1,0:T(8,128)S(1)}, u32[]{:S(2)}, u32[]{:S(2)}) collective-permute-start(f32[3,64,128]{2,1,0:T(8,128)S(1)} %constant_dynamic-update-slice_fusion.3), channel_id=1, source_target_pairs={{1,2},{2,1},{5,6},{6,5},{9,10},{10,9},{13,14},{14,13},{17,18},{18,... | collective-permute-start | bytes 294920 | tf_op jit(solution)/shard_map/ppermute | solution.py:384
  9.3 8.0 %collective-permute-start.4 = (f32[3,64,128]{2,1,0:T(8,128)S(1)}, f32[3,64,128]{2,1,0:T(8,128)S(1)}, u32[]{:S(2)}, u32[]{:S(2)}) collective-permute-start(f32[3,64,128]{2,1,0:T(8,128)S(1)} %constant_dynamic-update-slice_fusion.3), channel_id=1, source_target_pairs={{0,1},{1,0},{2,3},{3,2},{4,5},{5,4},{6,7},{7,6},{8,9},{9,8},{10,11... | collective-permute-start | bytes 294920 | tf_op jit(solution)/shard_map/ppermute | solution.py:384
  12.6 4.8 %copy-start.1 = (bf16[512,512]{1,0:T(8,128)(2,1)S(1)}, bf16[512,512]{1,0:T(8,128)(2,1)}, u32[]{:S(2)}) copy-start(bf16[512,512]{1,0:T(8,128)(2,1)} %constant.20.clone.col_from) | copy-start | bytes 1572868
  12.6 4.8 %copy-start = (bf16[2,256,512]{2,1,0:T(8,128)(2,1)S(1)}, bf16[2,256,512]{2,1,0:T(8,128)(2,1)}, u32[]{:S(2)}) copy-start(bf16[2,256,512]{2,1,0:T(8,128)(2,1)} %constant.19.clone.row_from) | copy-start | bytes 1572868
  12.7 6.3 %collective-permute-start.3 = (f32[3,64,128]{2,1,0:T(8,128)S(1)}, f32[3,64,128]{2,1,0:T(8,128)S(1)}, u32[]{:S(2)}, u32[]{:S(2)}) collective-permute-start(f32[3,64,128]{2,1,0:T(8,128)S(1)} %get-tuple-element.49), channel_id=1, source_target_pairs={{1,2},{2,1},{5,6},{6,5},{9,10},{10,9},{13,14},{14,13},{17,18},{18,... | collective-permute-start | bytes 294920 | tf_op jit(solution)/shard_map/ppermute | solution.py:351
  13.5 7.7 %collective-permute-start.8 = (f32[3,64,128]{2,1,0:T(8,128)S(1)}, f32[3,64,128]{2,1,0:T(8,128)S(1)}, u32[]{:S(2)}, u32[]{:S(2)}) collective-permute-start(f32[3,64,128]{2,1,0:T(8,128)S(1)} %get-tuple-element.49), channel_id=1, source_target_pairs={{0,2},{1,3},{2,0},{3,1},{4,6},{5,7},{6,4},{7,5},{8,10},{9,11},{10,... | collective-permute-start | bytes 294920 | tf_op jit(solution)/shard_map/ppermute | solution.py:351
  16.5 4.6 %collective-permute-start.7 = (f32[3,64,128]{2,1,0:T(8,128)S(1)}, f32[3,64,128]{2,1,0:T(8,128)S(1)}, u32[]{:S(2)}, u32[]{:S(2)}) collective-permute-start(f32[3,64,128]{2,1,0:T(8,128)S(1)} %get-tuple-element.49), channel_id=1, source_target_pairs={{0,1},{1,0},{2,3},{3,2},{4,5},{5,4},{6,7},{7,6},{8,9},{9,8},{10,11... | collective-permute-start | bytes 294920 | tf_op jit(solution)/shard_map/ppermute | solution.py:351
  17.4 0.7 %copy-start.2 = (s32[2,2]{1,0:T(2,128)S(1)}, s32[2,2]{1,0:T(2,128)}, u32[]{:S(2)}) copy-start(s32[2,2]{1,0:T(2,128)} %tilt_ref.1) | copy-start | bytes 52
  19.1 3.8 %collective-permute-start.9 = (f32[11,64,128]{2,1,0:T(8,128)S(1)}, f32[11,64,128]{2,1,0:T(8,128)S(1)}, u32[]{:S(2)}, u32[]{:S(2)}) collective-permute-start(f32[11,64,128]{2,1,0:T(8,128)S(1)} %pad_maximum_fusion.2), channel_id=1, source_target_pairs={{0,4},{4,0},{1,5},{5,1},{2,6},{6,2},{3,7},{7,3},{8,12},{12,8},{9,1... | collective-permute-start | bytes 1081352 | tf_op jit(solution)/shard_map/ppermute | solution.py:356
  21.2 1.6 %collective-permute-start.10 = (f32[9,64,128]{2,1,0:T(8,128)S(1)}, f32[9,64,128]{2,1,0:T(8,128)S(1)}, u32[]{:S(2)}, u32[]{:S(2)}) collective-permute-start(f32[9,64,128]{2,1,0:T(8,128)S(1)} %constant_dynamic-update-slice_fusion.5), channel_id=1, source_target_pairs={{0,4},{4,0},{1,5},{5,1},{2,6},{6,2},{3,7},{7,3},{8,12},{12,8},{9,1... | collective-permute-start | bytes 884744 | tf_op jit(solution)/shard_map/ppermute | solution.py:356
  30.0 1.4 %collective-permute-start.11 = (f32[1,3,64,128]{3,2,1,0:T(8,128)S(1)}, f32[1,3,64,128]{3,2,1,0:T(8,128)S(1)}, u32[]{:S(2)}, u32[]{:S(2)}) collective-permute-start(f32[1,3,64,128]{3,2,1,0:T(8,128)S(1)} %get-tuple-element.45), channel_id=1, source_target_pairs={{0,4},{4,0},{1,5},{5,1},{2,6},{6,2},{3,7},{7,3},{8,12},{12,8},{9,1... | collective-permute-start | bytes 294920 | tf_op jit(solution)/shard_map/ppermute | solution.py:356

commit v26 on v25

--- a/solution.py
+++ b/solution.py
@@ -133,13 +133,19 @@
     return high, rest.astype(jnp.bfloat16), pltpu.roll(rest, LANES // 2, 1).astype(jnp.bfloat16)
 
 
-def advance(slice_index, start, waves, screens, row_matrix, col_ref, edge_ref):
+def advance(slice_index, start, waves, screens, row_matrix, col_ref, edge_ref, outer=None):
     size, height = len(waves), waves[0][0].shape[0]
     chunks = [range(place, min(place + 2, size)) for place in range(0, size, 2)]
     highs, lows = [], []
     columns = [
         jnp.concatenate(
-            [jnp.concatenate(turned(slice_index, start + place, screens, waves[place]), axis=0) for place in chunk],
+            [
+                jnp.concatenate(
+                    waves[place] if slice_index is None else turned(slice_index, start + place, screens, waves[place]),
+                    axis=0,
+                )
+                for place in chunk
+            ],
             axis=1,
         )
         for chunk in chunks
@@ -161,10 +167,18 @@
                     edge_ref[place + 1, :, pl.ds(edge + HALO, HALO)] = swung[:, HALO : 2 * HALO]
             highs.append(jnp.concatenate(own_high, axis=1))
             lows.append(jnp.concatenate(own_low, axis=1))
+    edge_parts = [edge_ref[place] for place in range(size)]
+    if outer is not None:
+        index, high_ref, low_ref = outer
+        for end, place in enumerate((0, size - 1)):
+            high_ref[end], low_ref[end] = highs[place], lows[place]
+        highs = highs[1:-1] + [high_ref[index]]
+        lows = lows[1:-1] + [low_ref[index]]
+        edge_parts = edge_parts[1:-1] + [edge_ref[index * (size - 1)]]
+        chunks = [range(place, min(place + 2, size - 1)) for place in range(0, size - 1, 2)]
     results = []
     for chunk in chunks:
-        rows = len(chunk) * height
-        edges = edge_ref[pl.ds(chunk[0], len(chunk))].reshape(rows, 2 * LANES)
+        edges = jnp.concatenate([edge_parts[place] for place in chunk], axis=0)
         own = jnp.concatenate([highs[place] for place in chunk], axis=0)
         total = col_product(
             jnp.concatenate([own, edges], axis=1),
@@ -223,7 +237,7 @@
 
 def second_kernel(near_rest, own_cos, own_sin, cos_ref, sin_ref):
     blocks = own_cos.shape[0]
-    count = cos_ref.shape[0] - 1
+    count = cos_ref.shape[0]
     own_section, own_place = lax.axis_index("depth"), lax.axis_index("col")
 
     def screens(col, carry):
@@ -234,16 +248,15 @@
         return carry
 
     lax.fori_loop(0, blocks, screens, 0)
-    cos_ref[count] = jnp.ones(cos_ref.shape[1:], jnp.float32)
-    sin_ref[count] = jnp.zeros(cos_ref.shape[1:], jnp.float32)
 
 
 def wave_kernel(
     wave_ref, near_cos, near_sin, near_own, far_first, far_second, row_ref, col_ref,
     mine_ref, theirs_ref, far_cos, far_sin, kept_ref, moved_ref, left_ref, grad_ref, even_edge, odd_edge,
+    outer_high, outer_low,
 ):
     blocks, _, height, _ = wave_ref.shape
-    count = near_cos.shape[0] - 1
+    count = near_cos.shape[0]
     core, own_section, own_place = lax.axis_index("row"), lax.axis_index("depth"), lax.axis_index("col")
     near, far = pl.ds(0, height // 2), pl.ds(height // 2, height // 2)
     screens = (near_cos, near_sin, far_cos, far_sin)
@@ -266,18 +279,20 @@
     for edge_ref in edges:
         clear_edge(edge_ref, 0, False)
         clear_edge(edge_ref, blocks - 1, True)
-    far_cos[count] = jnp.ones(far_cos.shape[1:], jnp.float32)
-    far_sin[count] = jnp.zeros(far_cos.shape[1:], jnp.float32)
     far_screens(0)
 
     waves = [(wave_ref[place, 0], wave_ref[place, 1]) for place in range(blocks)]
     for tick in range(count):
         entering = (wave_ref if tick == 0 else kept_ref)[own_place]
         moved_ref[tick, 0], moved_ref[tick, 1] = turned(tick, own_place, screens, (entering[0], entering[1]))
-        waves = advance(tick, 0, waves, screens, row_matrix, col_ref, edges[tick % 2])
+        outer = (window_start, outer_high, outer_low) if tick + 1 == count else None
+        waves = advance(tick, 0, waves, screens, row_matrix, col_ref, edges[tick % 2], outer)
         if tick + 1 < count:
             far_screens(tick + 1)
-        keep(kept_ref, waves)
+            keep(kept_ref, waves)
+        else:
+            for place, wave in zip((1, 2, window_start * (blocks - 1)), waves):
+                kept_ref[place, 0], kept_ref[place, 1] = wave
         left_ref[tick] = kept_ref[own_place]
 
     for edge_ref in edges:
@@ -292,7 +307,8 @@
         waves.append((misfit * real, -misfit * imag))
 
     for tick in range(count - 1):
-        waves = advance(count - tick, window_start, waves, screens, row_matrix, col_ref, edges[tick % 2])
+        passed = count - tick if tick else None
+        waves = advance(passed, window_start, waves, screens, row_matrix, col_ref, edges[tick % 2])
         keep(kept_ref, waves)
         arrived = count - 1 - tick
         pulled = kept_ref[own_in_window]
@@ -390,7 +406,7 @@
     arriving = spread(other_depths, "col", (1, 2, 3), 2)
     row_all, col_all = jnp.asarray(row_constant(height)), jnp.asarray(col_constant())
     near_own, row_all, col_all = lax.optimization_barrier((near_own, row_all, col_all))
-    half_screens = (count + 1, blocks, tile_r, tile_c)
+    half_screens = (count, blocks, tile_r, tile_c)
     field = (blocks, 2, height, tile_c)
     row_matrix, col_matrix, wave, own_cos, own_sin = pl.pallas_call(
         load_kernel,
@@ -433,7 +449,8 @@
         + [pltpu.VMEM(field, jnp.float32)]
         + [pltpu.VMEM((count, 2, height, tile_c), jnp.float32)] * 2
         + [pltpu.VMEM((count, height, tile_c), jnp.float32)]
-        + [pltpu.VMEM((blocks, height, 2 * LANES), jnp.bfloat16)] * 2,
+        + [pltpu.VMEM((blocks, height, 2 * LANES), jnp.bfloat16)] * 2
+        + [pltpu.VMEM((2, height, 2 * LANES), jnp.bfloat16)] * 2,
         compiler_params=params(24),
     )(
         wave, near_cos, near_sin, near_own, far_first, far_second,

time: 32.3 us -> 32.2 us (level)
  no operation moved by 1% of the time
where the time goes in v26:
time: 32.2 us; the launch traced here: 31.9 us
  starting transfers between devices  16.1 us (50%)
  Pallas kernels  8.97 us (28%)
  waiting for transfers between devices  4.38 us (14%)
  local copies, waits for them, and re-layouts  1.5 us (5%)
  between operations  0.84 us (3%)
    ppermute x6, starting transfers between devices, spread(): pieces.append(lax.ppermute(shard, axis, pairs))  10.3 us
    pallas_call x1, Pallas kernels, whole_field_body(): pl.pallas_call(wave_kernel, out_shape=(array(1, 3, tile_r, tile_c),) * 2,...  7.06 us
    ppermute x2, starting transfers between devices, whole_field_body(): near_own.append(lax.ppermute(packet, 'col', close))  3.94 us
    ppermute x3, waiting for transfers between devices, swap_cores(): return lax.ppermute(value, 'row', [(0, 1), (1, 0)])  2.36 us
    ppermute x6, waiting for transfers between devices, spread(): pieces.append(lax.ppermute(shard, axis, pairs))  2.01 us
    ppermute x1, starting transfers between devices, whole_field_body(): lax.ppermute(slab, 'col', further)  1.52 us
    unnamed x13, local copies, waits for them, and re-layouts  1.46 us
    pallas_call x1, Pallas kernels, whole_field_body(): pl.pallas_call(load_kernel, out_shape=(jax.ShapeDtypeStruct(row_all.shape...  0.89 us
  transfers between devices with their start and end apart: 12, of which 3 were waited for; matrix products, arithmetic and copies ran while one was open for 3% of the time, Pallas kernels for 4%

profile of v26, /device:TPU:0, one launch (start us, length us, event | category | flops | bytes accessed | tf_op | source)
XLA Modules:
  0.0 31.9 jit_solution(5130901362741518428)
XLA Ops:
  0.6 0.0 copy-start.3
  0.6 3.1 %collective-permute-start = (f32[1,64,128]{2,1,0:T(8,128)}, f32[1,64,128]{2,1,0:T(8,128)S(1)}, u32[]{:S(2)}, u32[]{:S(2)}) collective-permute-start(f32[1,64,128]{2,1,0:T(8,128)} %param.5), channel_id=1, source_target_pairs={{0,8},{8,0},{16,24},{24,16},{1,9},{9,1},{17,25},{25,17},{2,10},{10... | collective-permute-start | bytes 98312 | tf_op jit(solution)/shard_map/ppermute | solution.py:367
  3.7 2.5 %collective-permute-start.1 = (f32[1,64,128]{2,1,0:T(8,128)}, f32[1,64,128]{2,1,0:T(8,128)S(1)}, u32[]{:S(2)}, u32[]{:S(2)}) collective-permute-start(f32[1,64,128]{2,1,0:T(8,128)} %param.5), channel_id=1, source_target_pairs={{0,24},{8,16},{16,8},{24,0},{1,25},{9,17},{17,9},{25,1},{2,26},{10... | collective-permute-start | bytes 98312 | tf_op jit(solution)/shard_map/ppermute | solution.py:367
  6.2 0.1 collective-permute-start.2
  6.3 0.0 collective-permute-done
  6.3 0.8 %constant_dynamic-update-slice_fusion.4 = f32[3,64,128]{2,1,0:T(8,128)S(1)} fusion(f32[1,64,128]{2,1,0:T(8,128)} %param.5), kind=kLoop, calls=%fused_computation.9 | loop fusion | bytes 65536
  7.1 1.5 %collective-permute-start.5 = (f32[1,64,128]{2,1,0:T(8,128)}, f32[1,64,128]{2,1,0:T(8,128)S(1)}, u32[]{:S(2)}, u32[]{:S(2)}) collective-permute-start(f32[1,64,128]{2,1,0:T(8,128)} %param.5), channel_id=1, source_target_pairs={{0,2},{1,3},{2,0},{3,1},{4,6},{5,7},{6,4},{7,5},{8,10},{9,11},{10,... | collective-permute-start | bytes 98312 | tf_op jit(solution)/shard_map/ppermute | solution.py:403
  8.6 0.0 copy-done.3
  8.6 0.7 %collective-permute-start.6 = (f32[3,64,128]{2,1,0:T(8,128)S(1)}, f32[3,64,128]{2,1,0:T(8,128)S(1)}, u32[]{:S(2)}, u32[]{:S(2)}) collective-permute-start(f32[3,64,128]{2,1,0:T(8,128)S(1)} %constant_dynamic-update-slice_fusion.3), channel_id=1, source_target_pairs={{1,2},{2,1},{5,6},{6,5},{9,10},{10,9},{13,14},{14,13},{17,18},{18,... | collective-permute-start | bytes 294920 | tf_op jit(solution)/shard_map/ppermute | solution.py:400
  9.3 3.3 %collective-permute-start.4 = (f32[3,64,128]{2,1,0:T(8,128)S(1)}, f32[3,64,128]{2,1,0:T(8,128)S(1)}, u32[]{:S(2)}, u32[]{:S(2)}) collective-permute-start(f32[3,64,128]{2,1,0:T(8,128)S(1)} %constant_dynamic-update-slice_fusion.3), channel_id=1, source_target_pairs={{0,1},{1,0},{2,3},{3,2},{4,5},{5,4},{6,7},{7,6},{8,9},{9,8},{10,11... | collective-permute-start | bytes 294920 | tf_op jit(solution)/shard_map/ppermute | solution.py:400
  12.6 0.0 collective-permute-done.1
  12.6 0.0 copy-start.1
  12.6 0.0 copy-start
  12.7 0.0 collective-permute-done.2
  12.7 0.8 %collective-permute-start.3 = (f32[3,64,128]{2,1,0:T(8,128)S(1)}, f32[3,64,128]{2,1,0:T(8,128)S(1)}, u32[]{:S(2)}, u32[]{:S(2)}) collective-permute-start(f32[3,64,128]{2,1,0:T(8,128)S(1)} %get-tuple-element.49), channel_id=1, source_target_pairs={{1,2},{2,1},{5,6},{6,5},{9,10},{10,9},{13,14},{14,13},{17,18},{18,... | collective-permute-start | bytes 294920 | tf_op jit(solution)/shard_map/ppermute | solution.py:367
  13.5 3.0 %collective-permute-start.8 = (f32[3,64,128]{2,1,0:T(8,128)S(1)}, f32[3,64,128]{2,1,0:T(8,128)S(1)}, u32[]{:S(2)}, u32[]{:S(2)}) collective-permute-start(f32[3,64,128]{2,1,0:T(8,128)S(1)} %get-tuple-element.49), channel_id=1, source_target_pairs={{0,2},{1,3},{2,0},{3,1},{4,6},{5,7},{6,4},{7,5},{8,10},{9,11},{10,... | collective-permute-start | bytes 294920 | tf_op jit(solution)/shard_map/ppermute | solution.py:367
  16.5 0.0 collective-permute-done.5
  16.5 0.8 %collective-permute-start.7 = (f32[3,64,128]{2,1,0:T(8,128)S(1)}, f32[3,64,128]{2,1,0:T(8,128)S(1)}, u32[]{:S(2)}, u32[]{:S(2)}) collective-permute-start(f32[3,64,128]{2,1,0:T(8,128)S(1)} %get-tuple-element.49), channel_id=1, source_target_pairs={{0,1},{1,0},{2,3},{3,2},{4,5},{5,4},{6,7},{7,6},{8,9},{9,8},{10,11... | collective-permute-start | bytes 294920 | tf_op jit(solution)/shard_map/ppermute | solution.py:367
  17.4 0.0 collective-permute-done.6
  17.4 0.0 collective-permute-done.4
  17.4 0.0 copy-start.2
  17.4 0.0 copy-done.1
  17.4 0.0 copy-done
  17.4 0.6 %copy-done.2 = s32[2,2]{1,0:T(2,128)S(1)} copy-done((s32[2,2]{1,0:T(2,128)S(1)}, s32[2,2]{1,0:T(2,128)}, u32[]{:S(2)}) %copy-start.2) | copy-done | bytes 40
  18.1 0.9 %shard_map.68 = (bf16[256,512]{1,0:T(8,128)(2,1)S(1)}, bf16[512,512]{1,0:T(8,128)(2,1)S(1)}, f32[4,2,128,128]{3,2,1,0:T(8,128)S(1)}, f32[4,64,128]{2,1,0:T(8,128)S(1)}, f32[4,64,128]{2,1,0:T(8,128)S(1)}) custom-call(s32[2,2]{1,0:T(2,128)S(1)} %copy-done.2, f32[4,3,64,128]{3,2,1,0:T(8,128)S(1)} %pad_maximum_fusion.near_own, bf16[2,256,512]{2,1,0:T(8,128)(2,1)S(1)} %copy-done, ...), custom_call_target="tpu_custom_call" | custom-call | flops 100000000 | bytes 1048576 | tf_op jit(solution)/shard_map/pallas_call | solution.py:411
  19.0 0.0 collective-permute-done.3
  19.1 0.1 collective-permute-start.9
  19.1 2.0 %collective-permute-done.7 = f32[3,64,128]{2,1,0:T(8,128)S(1)} collective-permute-done((f32[3,64,128]{2,1,0:T(8,128)S(1)}, f32[3,64,128]{2,1,0:T(8,128)S(1)}, u32[]{:S(2)}, u32[]{:S(2)}) %collective-permute-start.7) | collective-permute-done | bytes 98336 | tf_op jit(solution)/shard_map/ppermute | solution.py:367
  21.1 0.0 collective-permute-done.8
  21.2 0.1 collective-permute-start.10
  21.3 0.3 %shard_map.69 = (f32[4,4,64,128]{3,2,1,0:T(8,128)S(1)}, f32[4,4,64,128]{3,2,1,0:T(8,128)S(1)}) custom-call(f32[4,3,64,128]{3,2,1,0:T(8,128)S(1)} %pad_maximum_fusion.1.near_rest, f32[4,64,128]{2,1,0:T(8,128)S(1)} %get-tuple-element.37.own_cos, f32[4,64,128]{2,1,0:T(8,128)S(1)} %get-tuple-element.38.own_sin), custom_call_target="tpu_custom_call" | custom-call | flops 500000000 | bytes 1048576 | tf_op jit(solution)/shard_map/pallas_call | solution.py:435
  21.6 1.2 %collective-permute-done.10.far_second = f32[9,64,128]{2,1,0:T(8,128)S(1)} collective-permute-done((f32[9,64,128]{2,1,0:T(8,128)S(1)}, f32[9,64,128]{2,1,0:T(8,128)S(1)}, u32[]{:S(2)}, u32[]{:S(2)}) %collective-permute-start.10) | collective-permute-done | bytes 294944 | tf_op jit(solution)/shard_map/ppermute | solution.py:372
  22.8 0.0 collective-permute-done.9.far_first
  22.8 7.1 %shard_map.70 = (f32[1,3,64,128]{3,2,1,0:T(8,128)S(1)}, f32[1,3,64,128]{3,2,1,0:T(8,128)S(1)}) custom-call(f32[4,2,128,128]{3,2,1,0:T(8,128)S(1)} %get-tuple-element.35.wave_ref, f32[4,4,64,128]{3,2,1,0:T(8,128)S(1)} %get-tuple-element.39.near_cos, f32[4,4,64,128]{3,2,1,0:T(8,128)S(1)} %get-tuple-element.40.near_sin, ...), custom_call_target="tpu_custom_call" | custom-call | tf_op jit(solution)/shard_map/pallas_call | solution.py:443
  29.9 0.2 collective-permute-start.11
  30.1 1.2 %collective-permute-done.11.received_ref = f32[1,3,64,128]{3,2,1,0:T(8,128)S(1)} collective-permute-done((f32[1,3,64,128]{3,2,1,0:T(8,128)S(1)}, f32[1,3,64,128]{3,2,1,0:T(8,128)S(1)}, u32[]{:S(2)}, u32[]{:S(2)}) %collective-permute-start.11) | collective-permute-done | bytes 98336 | tf_op jit(solution)/shard_map/ppermute | solution.py:372
  31.2 0.7 %shard_map.71 = (f32[1,64,128]{2,1,0:T(8,128)}, f32[2,1,2,64,128]{4,3,2,1,0:T(8,128)}) custom-call(f32[1,3,64,128]{3,2,1,0:T(8,128)S(1)} %get-tuple-element.44.mine_ref, f32[1,3,64,128]{3,2,1,0:T(8,128)S(1)} %collective-permute-done.11.received_ref), custom_call_target="tpu_custom_call" | custom-call | tf_op jit(solution)/shard_map/pallas_call | solution.py:459
  (12 shorter events, 0.2 us)
Async XLA Ops:
  0.6 8.0 %copy-start.3 = (f32[2,64,128]{2,1,0:T(8,128)S(1)}, f32[2,64,128]{2,1,0:T(8,128)}, u32[]{:S(2)}) copy-start(f32[2,64,128]{2,1,0:T(8,128)} %param.7) | copy-start | bytes 196612
  0.6 5.7 %collective-permute-start = (f32[1,64,128]{2,1,0:T(8,128)}, f32[1,64,128]{2,1,0:T(8,128)S(1)}, u32[]{:S(2)}, u32[]{:S(2)}) collective-permute-start(f32[1,64,128]{2,1,0:T(8,128)} %param.5), channel_id=1, source_target_pairs={{0,8},{8,0},{16,24},{24,16},{1,9},{9,1},{17,25},{25,17},{2,10},{10... | collective-permute-start | bytes 98312 | tf_op jit(solution)/shard_map/ppermute | solution.py:367
  3.7 8.9 %collective-permute-start.1 = (f32[1,64,128]{2,1,0:T(8,128)}, f32[1,64,128]{2,1,0:T(8,128)S(1)}, u32[]{:S(2)}, u32[]{:S(2)}) collective-permute-start(f32[1,64,128]{2,1,0:T(8,128)} %param.5), channel_id=1, source_target_pairs={{0,24},{8,16},{16,8},{24,0},{1,25},{9,17},{17,9},{25,1},{2,26},{10... | collective-permute-start | bytes 98312 | tf_op jit(solution)/shard_map/ppermute | solution.py:367
  6.2 6.4 %collective-permute-start.2 = (f32[1,64,128]{2,1,0:T(8,128)}, f32[1,64,128]{2,1,0:T(8,128)S(1)}, u32[]{:S(2)}, u32[]{:S(2)}) collective-permute-start(f32[1,64,128]{2,1,0:T(8,128)} %param.5), channel_id=1, source_target_pairs={{0,16},{8,24},{16,0},{24,8},{1,17},{9,25},{17,1},{25,9},{2,18},{10... | collective-permute-start | bytes 98312 | tf_op jit(solution)/shard_map/ppermute | solution.py:367
  7.1 9.4 %collective-permute-start.5 = (f32[1,64,128]{2,1,0:T(8,128)}, f32[1,64,128]{2,1,0:T(8,128)S(1)}, u32[]{:S(2)}, u32[]{:S(2)}) collective-permute-start(f32[1,64,128]{2,1,0:T(8,128)} %param.5), channel_id=1, source_target_pairs={{0,2},{1,3},{2,0},{3,1},{4,6},{5,7},{6,4},{7,5},{8,10},{9,11},{10,... | collective-permute-start | bytes 98312 | tf_op jit(solution)/shard_map/ppermute | solution.py:403
  8.6 8.7 %collective-permute-start.6 = (f32[3,64,128]{2,1,0:T(8,128)S(1)}, f32[3,64,128]{2,1,0:T(8,128)S(1)}, u32[]{:S(2)}, u32[]{:S(2)}) collective-permute-start(f32[3,64,128]{2,1,0:T(8,128)S(1)} %constant_dynamic-update-slice_fusion.3), channel_id=1, source_target_pairs={{1,2},{2,1},{5,6},{6,5},{9,10},{10,9},{13,14},{14,13},{17,18},{18,... | collective-permute-start | bytes 294920 | tf_op jit(solution)/shard_map/ppermute | solution.py:400
  9.3 8.0 %collective-permute-start.4 = (f32[3,64,128]{2,1,0:T(8,128)S(1)}, f32[3,64,128]{2,1,0:T(8,128)S(1)}, u32[]{:S(2)}, u32[]{:S(2)}) collective-permute-start(f32[3,64,128]{2,1,0:T(8,128)S(1)} %constant_dynamic-update-slice_fusion.3), channel_id=1, source_target_pairs={{0,1},{1,0},{2,3},{3,2},{4,5},{5,4},{6,7},{7,6},{8,9},{9,8},{10,11... | collective-permute-start | bytes 294920 | tf_op jit(solution)/shard_map/ppermute | solution.py:400
  12.6 4.8 %copy-start.1 = (bf16[512,512]{1,0:T(8,128)(2,1)S(1)}, bf16[512,512]{1,0:T(8,128)(2,1)}, u32[]{:S(2)}) copy-start(bf16[512,512]{1,0:T(8,128)(2,1)} %constant.20.clone.col_from) | copy-start | bytes 1572868
  12.6 4.8 %copy-start = (bf16[2,256,512]{2,1,0:T(8,128)(2,1)S(1)}, bf16[2,256,512]{2,1,0:T(8,128)(2,1)}, u32[]{:S(2)}) copy-start(bf16[2,256,512]{2,1,0:T(8,128)(2,1)} %constant.19.clone.row_from) | copy-start | bytes 1572868
  12.7 6.3 %collective-permute-start.3 = (f32[3,64,128]{2,1,0:T(8,128)S(1)}, f32[3,64,128]{2,1,0:T(8,128)S(1)}, u32[]{:S(2)}, u32[]{:S(2)}) collective-permute-start(f32[3,64,128]{2,1,0:T(8,128)S(1)} %get-tuple-element.49), channel_id=1, source_target_pairs={{1,2},{2,1},{5,6},{6,5},{9,10},{10,9},{13,14},{14,13},{17,18},{18,... | collective-permute-start | bytes 294920 | tf_op jit(solution)/shard_map/ppermute | solution.py:367
  13.5 7.7 %collective-permute-start.8 = (f32[3,64,128]{2,1,0:T(8,128)S(1)}, f32[3,64,128]{2,1,0:T(8,128)S(1)}, u32[]{:S(2)}, u32[]{:S(2)}) collective-permute-start(f32[3,64,128]{2,1,0:T(8,128)S(1)} %get-tuple-element.49), channel_id=1, source_target_pairs={{0,2},{1,3},{2,0},{3,1},{4,6},{5,7},{6,4},{7,5},{8,10},{9,11},{10,... | collective-permute-start | bytes 294920 | tf_op jit(solution)/shard_map/ppermute | solution.py:367
  16.5 4.6 %collective-permute-start.7 = (f32[3,64,128]{2,1,0:T(8,128)S(1)}, f32[3,64,128]{2,1,0:T(8,128)S(1)}, u32[]{:S(2)}, u32[]{:S(2)}) collective-permute-start(f32[3,64,128]{2,1,0:T(8,128)S(1)} %get-tuple-element.49), channel_id=1, source_target_pairs={{0,1},{1,0},{2,3},{3,2},{4,5},{5,4},{6,7},{7,6},{8,9},{9,8},{10,11... | collective-permute-start | bytes 294920 | tf_op jit(solution)/shard_map/ppermute | solution.py:367
  17.4 0.7 %copy-start.2 = (s32[2,2]{1,0:T(2,128)S(1)}, s32[2,2]{1,0:T(2,128)}, u32[]{:S(2)}) copy-start(s32[2,2]{1,0:T(2,128)} %tilt_ref.1) | copy-start | bytes 52
  19.1 3.8 %collective-permute-start.9 = (f32[11,64,128]{2,1,0:T(8,128)S(1)}, f32[11,64,128]{2,1,0:T(8,128)S(1)}, u32[]{:S(2)}, u32[]{:S(2)}) collective-permute-start(f32[11,64,128]{2,1,0:T(8,128)S(1)} %pad_maximum_fusion.2), channel_id=1, source_target_pairs={{0,4},{4,0},{1,5},{5,1},{2,6},{6,2},{3,7},{7,3},{8,12},{12,8},{9,1... | collective-permute-start | bytes 1081352 | tf_op jit(solution)/shard_map/ppermute | solution.py:372
  21.2 1.6 %collective-permute-start.10 = (f32[9,64,128]{2,1,0:T(8,128)S(1)}, f32[9,64,128]{2,1,0:T(8,128)S(1)}, u32[]{:S(2)}, u32[]{:S(2)}) collective-permute-start(f32[9,64,128]{2,1,0:T(8,128)S(1)} %constant_dynamic-update-slice_fusion.5), channel_id=1, source_target_pairs={{0,4},{4,0},{1,5},{5,1},{2,6},{6,2},{3,7},{7,3},{8,12},{12,8},{9,1... | collective-permute-start | bytes 884744 | tf_op jit(solution)/shard_map/ppermute | solution.py:372
  29.9 1.4 %collective-permute-start.11 = (f32[1,3,64,128]{3,2,1,0:T(8,128)S(1)}, f32[1,3,64,128]{3,2,1,0:T(8,128)S(1)}, u32[]{:S(2)}, u32[]{:S(2)}) collective-permute-start(f32[1,3,64,128]{3,2,1,0:T(8,128)S(1)} %get-tuple-element.45), channel_id=1, source_target_pairs={{0,4},{4,0},{1,5},{5,1},{2,6},{6,2},{3,7},{7,3},{8,12},{12,8},{9,1... | collective-permute-start | bytes 294920 | tf_op jit(solution)/shard_map/ppermute | solution.py:372

commit v27 on v26

--- a/solution.py
+++ b/solution.py
@@ -177,13 +177,19 @@
         edge_parts = edge_parts[1:-1] + [edge_ref[index * (size - 1)]]
         chunks = [range(place, min(place + 2, size - 1)) for place in range(0, size - 1, 2)]
     results = []
+    rest = jnp.dot(
+        jnp.concatenate([lows[place] for chunk in chunks for place in chunk], axis=0),
+        col_ref[: 2 * LANES, : 2 * LANES],
+        preferred_element_type=jnp.float32,
+    )
     for chunk in chunks:
         edges = jnp.concatenate([edge_parts[place] for place in chunk], axis=0)
         own = jnp.concatenate([highs[place] for place in chunk], axis=0)
-        total = col_product(
-            jnp.concatenate([own, edges], axis=1),
-            jnp.concatenate([lows[place] for place in chunk], axis=0),
-            col_ref,
+        wide = jnp.dot(jnp.concatenate([own, edges], axis=1), col_ref[...], preferred_element_type=jnp.float32)
+        total = (
+            wide[:, : 2 * LANES]
+            + wide[:, 2 * LANES :]
+            + rest[chunk[0] * height : (chunk[0] + len(chunk)) * height]
         )
         for sub in range(len(chunk)):
             block = total[sub * height : (sub + 1) * height]

time: 32.2 us -> 33.2 us (1.031)
  Pallas kernels: 8.97 us -> 10 us
    pallas_call x1, Pallas kernels: 7.06 us -> 8.11 us  [whole_field_body(): pl.pallas_call(wave_kernel, out_shape=(array(1, 3, tile_r, tile_c),) * 2,...]
where the time goes in v27:
time: 33.2 us; the launch traced here: 33 us
  starting transfers between devices  16.1 us (48%)
  Pallas kernels  10 us (30%)
  waiting for transfers between devices  4.38 us (13%)
  local copies, waits for them, and re-layouts  1.5 us (5%)
  between operations  0.84 us (3%)
    ppermute x6, starting transfers between devices, spread(): pieces.append(lax.ppermute(shard, axis, pairs))  10.3 us
    pallas_call x1, Pallas kernels, whole_field_body(): pl.pallas_call(wave_kernel, out_shape=(array(1, 3, tile_r, tile_c),) * 2,...  8.11 us
    ppermute x2, starting transfers between devices, whole_field_body(): near_own.append(lax.ppermute(packet, 'col', close))  3.94 us
    ppermute x3, waiting for transfers between devices, swap_cores(): return lax.ppermute(value, 'row', [(0, 1), (1, 0)])  2.36 us
    ppermute x6, waiting for transfers between devices, spread(): pieces.append(lax.ppermute(shard, axis, pairs))  2.01 us
    ppermute x1, starting transfers between devices, whole_field_body(): lax.ppermute(slab, 'col', further)  1.52 us
    unnamed x13, local copies, waits for them, and re-layouts  1.46 us
    pallas_call x1, Pallas kernels, whole_field_body(): pl.pallas_call(load_kernel, out_shape=(jax.ShapeDtypeStruct(row_all.shape...  0.89 us
  transfers between devices with their start and end apart: 12, of which 3 were waited for; matrix products, arithmetic and copies ran while one was open for 3% of the time, Pallas kernels for 4%

profile of v27, /device:TPU:0, one launch (start us, length us, event | category | flops | bytes accessed | tf_op | source)
XLA Modules:
  0.0 33.0 jit_solution(13881393132256023616)
XLA Ops:
  0.6 0.0 copy-start.3
  0.6 3.1 %collective-permute-start = (f32[1,64,128]{2,1,0:T(8,128)}, f32[1,64,128]{2,1,0:T(8,128)S(1)}, u32[]{:S(2)}, u32[]{:S(2)}) collective-permute-start(f32[1,64,128]{2,1,0:T(8,128)} %param.5), channel_id=1, source_target_pairs={{0,8},{8,0},{16,24},{24,16},{1,9},{9,1},{17,25},{25,17},{2,10},{10... | collective-permute-start | bytes 98312 | tf_op jit(solution)/shard_map/ppermute | solution.py:373
  3.7 2.5 %collective-permute-start.1 = (f32[1,64,128]{2,1,0:T(8,128)}, f32[1,64,128]{2,1,0:T(8,128)S(1)}, u32[]{:S(2)}, u32[]{:S(2)}) collective-permute-start(f32[1,64,128]{2,1,0:T(8,128)} %param.5), channel_id=1, source_target_pairs={{0,24},{8,16},{16,8},{24,0},{1,25},{9,17},{17,9},{25,1},{2,26},{10... | collective-permute-start | bytes 98312 | tf_op jit(solution)/shard_map/ppermute | solution.py:373
  6.2 0.1 collective-permute-start.2
  6.3 0.0 collective-permute-done
  6.3 0.8 %constant_dynamic-update-slice_fusion.4 = f32[3,64,128]{2,1,0:T(8,128)S(1)} fusion(f32[1,64,128]{2,1,0:T(8,128)} %param.5), kind=kLoop, calls=%fused_computation.9 | loop fusion | bytes 65536
  7.1 1.5 %collective-permute-start.5 = (f32[1,64,128]{2,1,0:T(8,128)}, f32[1,64,128]{2,1,0:T(8,128)S(1)}, u32[]{:S(2)}, u32[]{:S(2)}) collective-permute-start(f32[1,64,128]{2,1,0:T(8,128)} %param.5), channel_id=1, source_target_pairs={{0,2},{1,3},{2,0},{3,1},{4,6},{5,7},{6,4},{7,5},{8,10},{9,11},{10,... | collective-permute-start | bytes 98312 | tf_op jit(solution)/shard_map/ppermute | solution.py:409
  8.6 0.0 copy-done.3
  8.6 0.7 %collective-permute-start.6 = (f32[3,64,128]{2,1,0:T(8,128)S(1)}, f32[3,64,128]{2,1,0:T(8,128)S(1)}, u32[]{:S(2)}, u32[]{:S(2)}) collective-permute-start(f32[3,64,128]{2,1,0:T(8,128)S(1)} %constant_dynamic-update-slice_fusion.3), channel_id=1, source_target_pairs={{1,2},{2,1},{5,6},{6,5},{9,10},{10,9},{13,14},{14,13},{17,18},{18,... | collective-permute-start | bytes 294920 | tf_op jit(solution)/shard_map/ppermute | solution.py:406
  9.3 3.3 %collective-permute-start.4 = (f32[3,64,128]{2,1,0:T(8,128)S(1)}, f32[3,64,128]{2,1,0:T(8,128)S(1)}, u32[]{:S(2)}, u32[]{:S(2)}) collective-permute-start(f32[3,64,128]{2,1,0:T(8,128)S(1)} %constant_dynamic-update-slice_fusion.3), channel_id=1, source_target_pairs={{0,1},{1,0},{2,3},{3,2},{4,5},{5,4},{6,7},{7,6},{8,9},{9,8},{10,11... | collective-permute-start | bytes 294920 | tf_op jit(solution)/shard_map/ppermute | solution.py:406
  12.6 0.0 collective-permute-done.1
  12.6 0.0 copy-start.1
  12.6 0.0 copy-start
  12.7 0.0 collective-permute-done.2
  12.7 0.8 %collective-permute-start.3 = (f32[3,64,128]{2,1,0:T(8,128)S(1)}, f32[3,64,128]{2,1,0:T(8,128)S(1)}, u32[]{:S(2)}, u32[]{:S(2)}) collective-permute-start(f32[3,64,128]{2,1,0:T(8,128)S(1)} %get-tuple-element.49), channel_id=1, source_target_pairs={{1,2},{2,1},{5,6},{6,5},{9,10},{10,9},{13,14},{14,13},{17,18},{18,... | collective-permute-start | bytes 294920 | tf_op jit(solution)/shard_map/ppermute | solution.py:373
  13.5 3.0 %collective-permute-start.8 = (f32[3,64,128]{2,1,0:T(8,128)S(1)}, f32[3,64,128]{2,1,0:T(8,128)S(1)}, u32[]{:S(2)}, u32[]{:S(2)}) collective-permute-start(f32[3,64,128]{2,1,0:T(8,128)S(1)} %get-tuple-element.49), channel_id=1, source_target_pairs={{0,2},{1,3},{2,0},{3,1},{4,6},{5,7},{6,4},{7,5},{8,10},{9,11},{10,... | collective-permute-start | bytes 294920 | tf_op jit(solution)/shard_map/ppermute | solution.py:373
  16.5 0.0 collective-permute-done.5
  16.5 0.8 %collective-permute-start.7 = (f32[3,64,128]{2,1,0:T(8,128)S(1)}, f32[3,64,128]{2,1,0:T(8,128)S(1)}, u32[]{:S(2)}, u32[]{:S(2)}) collective-permute-start(f32[3,64,128]{2,1,0:T(8,128)S(1)} %get-tuple-element.49), channel_id=1, source_target_pairs={{0,1},{1,0},{2,3},{3,2},{4,5},{5,4},{6,7},{7,6},{8,9},{9,8},{10,11... | collective-permute-start | bytes 294920 | tf_op jit(solution)/shard_map/ppermute | solution.py:373
  17.4 0.0 collective-permute-done.6
  17.4 0.0 collective-permute-done.4
  17.4 0.0 copy-start.2
  17.4 0.0 copy-done.1
  17.4 0.0 copy-done
  17.4 0.6 %copy-done.2 = s32[2,2]{1,0:T(2,128)S(1)} copy-done((s32[2,2]{1,0:T(2,128)S(1)}, s32[2,2]{1,0:T(2,128)}, u32[]{:S(2)}) %copy-start.2) | copy-done | bytes 40
  18.1 0.9 %shard_map.68 = (bf16[256,512]{1,0:T(8,128)(2,1)S(1)}, bf16[512,512]{1,0:T(8,128)(2,1)S(1)}, f32[4,2,128,128]{3,2,1,0:T(8,128)S(1)}, f32[4,64,128]{2,1,0:T(8,128)S(1)}, f32[4,64,128]{2,1,0:T(8,128)S(1)}) custom-call(s32[2,2]{1,0:T(2,128)S(1)} %copy-done.2, f32[4,3,64,128]{3,2,1,0:T(8,128)S(1)} %pad_maximum_fusion.near_own, bf16[2,256,512]{2,1,0:T(8,128)(2,1)S(1)} %copy-done, ...), custom_call_target="tpu_custom_call" | custom-call | flops 100000000 | bytes 1048576 | tf_op jit(solution)/shard_map/pallas_call | solution.py:417
  19.0 0.0 collective-permute-done.3
  19.1 0.1 collective-permute-start.9
  19.1 2.0 %collective-permute-done.7 = f32[3,64,128]{2,1,0:T(8,128)S(1)} collective-permute-done((f32[3,64,128]{2,1,0:T(8,128)S(1)}, f32[3,64,128]{2,1,0:T(8,128)S(1)}, u32[]{:S(2)}, u32[]{:S(2)}) %collective-permute-start.7) | collective-permute-done | bytes 98336 | tf_op jit(solution)/shard_map/ppermute | solution.py:373
  21.1 0.0 collective-permute-done.8
  21.2 0.1 collective-permute-start.10
  21.3 0.3 %shard_map.69 = (f32[4,4,64,128]{3,2,1,0:T(8,128)S(1)}, f32[4,4,64,128]{3,2,1,0:T(8,128)S(1)}) custom-call(f32[4,3,64,128]{3,2,1,0:T(8,128)S(1)} %pad_maximum_fusion.1.near_rest, f32[4,64,128]{2,1,0:T(8,128)S(1)} %get-tuple-element.37.own_cos, f32[4,64,128]{2,1,0:T(8,128)S(1)} %get-tuple-element.38.own_sin), custom_call_target="tpu_custom_call" | custom-call | flops 500000000 | bytes 1048576 | tf_op jit(solution)/shard_map/pallas_call | solution.py:441
  21.6 1.2 %collective-permute-done.10.far_second = f32[9,64,128]{2,1,0:T(8,128)S(1)} collective-permute-done((f32[9,64,128]{2,1,0:T(8,128)S(1)}, f32[9,64,128]{2,1,0:T(8,128)S(1)}, u32[]{:S(2)}, u32[]{:S(2)}) %collective-permute-start.10) | collective-permute-done | bytes 294944 | tf_op jit(solution)/shard_map/ppermute | solution.py:378
  22.8 0.0 collective-permute-done.9.far_first
  22.8 8.1 %shard_map.70 = (f32[1,3,64,128]{3,2,1,0:T(8,128)S(1)}, f32[1,3,64,128]{3,2,1,0:T(8,128)S(1)}) custom-call(f32[4,2,128,128]{3,2,1,0:T(8,128)S(1)} %get-tuple-element.35.wave_ref, f32[4,4,64,128]{3,2,1,0:T(8,128)S(1)} %get-tuple-element.39.near_cos, f32[4,4,64,128]{3,2,1,0:T(8,128)S(1)} %get-tuple-element.40.near_sin, ...), custom_call_target="tpu_custom_call" | custom-call | tf_op jit(solution)/shard_map/pallas_call | solution.py:449
  30.9 0.2 collective-permute-start.11
  31.1 1.2 %collective-permute-done.11.received_ref = f32[1,3,64,128]{3,2,1,0:T(8,128)S(1)} collective-permute-done((f32[1,3,64,128]{3,2,1,0:T(8,128)S(1)}, f32[1,3,64,128]{3,2,1,0:T(8,128)S(1)}, u32[]{:S(2)}, u32[]{:S(2)}) %collective-permute-start.11) | collective-permute-done | bytes 98336 | tf_op jit(solution)/shard_map/ppermute | solution.py:378
  32.3 0.7 %shard_map.71 = (f32[1,64,128]{2,1,0:T(8,128)}, f32[2,1,2,64,128]{4,3,2,1,0:T(8,128)}) custom-call(f32[1,3,64,128]{3,2,1,0:T(8,128)S(1)} %get-tuple-element.44.mine_ref, f32[1,3,64,128]{3,2,1,0:T(8,128)S(1)} %collective-permute-done.11.received_ref), custom_call_target="tpu_custom_call" | custom-call | tf_op jit(solution)/shard_map/pallas_call | solution.py:465
  (12 shorter events, 0.2 us)
Async XLA Ops:
  0.6 8.0 %copy-start.3 = (f32[2,64,128]{2,1,0:T(8,128)S(1)}, f32[2,64,128]{2,1,0:T(8,128)}, u32[]{:S(2)}) copy-start(f32[2,64,128]{2,1,0:T(8,128)} %param.7) | copy-start | bytes 196612
  0.6 5.7 %collective-permute-start = (f32[1,64,128]{2,1,0:T(8,128)}, f32[1,64,128]{2,1,0:T(8,128)S(1)}, u32[]{:S(2)}, u32[]{:S(2)}) collective-permute-start(f32[1,64,128]{2,1,0:T(8,128)} %param.5), channel_id=1, source_target_pairs={{0,8},{8,0},{16,24},{24,16},{1,9},{9,1},{17,25},{25,17},{2,10},{10... | collective-permute-start | bytes 98312 | tf_op jit(solution)/shard_map/ppermute | solution.py:373
  3.7 8.9 %collective-permute-start.1 = (f32[1,64,128]{2,1,0:T(8,128)}, f32[1,64,128]{2,1,0:T(8,128)S(1)}, u32[]{:S(2)}, u32[]{:S(2)}) collective-permute-start(f32[1,64,128]{2,1,0:T(8,128)} %param.5), channel_id=1, source_target_pairs={{0,24},{8,16},{16,8},{24,0},{1,25},{9,17},{17,9},{25,1},{2,26},{10... | collective-permute-start | bytes 98312 | tf_op jit(solution)/shard_map/ppermute | solution.py:373
  6.2 6.4 %collective-permute-start.2 = (f32[1,64,128]{2,1,0:T(8,128)}, f32[1,64,128]{2,1,0:T(8,128)S(1)}, u32[]{:S(2)}, u32[]{:S(2)}) collective-permute-start(f32[1,64,128]{2,1,0:T(8,128)} %param.5), channel_id=1, source_target_pairs={{0,16},{8,24},{16,0},{24,8},{1,17},{9,25},{17,1},{25,9},{2,18},{10... | collective-permute-start | bytes 98312 | tf_op jit(solution)/shard_map/ppermute | solution.py:373
  7.1 9.4 %collective-permute-start.5 = (f32[1,64,128]{2,1,0:T(8,128)}, f32[1,64,128]{2,1,0:T(8,128)S(1)}, u32[]{:S(2)}, u32[]{:S(2)}) collective-permute-start(f32[1,64,128]{2,1,0:T(8,128)} %param.5), channel_id=1, source_target_pairs={{0,2},{1,3},{2,0},{3,1},{4,6},{5,7},{6,4},{7,5},{8,10},{9,11},{10,... | collective-permute-start | bytes 98312 | tf_op jit(solution)/shard_map/ppermute | solution.py:409
  8.6 8.7 %collective-permute-start.6 = (f32[3,64,128]{2,1,0:T(8,128)S(1)}, f32[3,64,128]{2,1,0:T(8,128)S(1)}, u32[]{:S(2)}, u32[]{:S(2)}) collective-permute-start(f32[3,64,128]{2,1,0:T(8,128)S(1)} %constant_dynamic-update-slice_fusion.3), channel_id=1, source_target_pairs={{1,2},{2,1},{5,6},{6,5},{9,10},{10,9},{13,14},{14,13},{17,18},{18,... | collective-permute-start | bytes 294920 | tf_op jit(solution)/shard_map/ppermute | solution.py:406
  9.3 8.0 %collective-permute-start.4 = (f32[3,64,128]{2,1,0:T(8,128)S(1)}, f32[3,64,128]{2,1,0:T(8,128)S(1)}, u32[]{:S(2)}, u32[]{:S(2)}) collective-permute-start(f32[3,64,128]{2,1,0:T(8,128)S(1)} %constant_dynamic-update-slice_fusion.3), channel_id=1, source_target_pairs={{0,1},{1,0},{2,3},{3,2},{4,5},{5,4},{6,7},{7,6},{8,9},{9,8},{10,11... | collective-permute-start | bytes 294920 | tf_op jit(solution)/shard_map/ppermute | solution.py:406
  12.6 4.8 %copy-start.1 = (bf16[512,512]{1,0:T(8,128)(2,1)S(1)}, bf16[512,512]{1,0:T(8,128)(2,1)}, u32[]{:S(2)}) copy-start(bf16[512,512]{1,0:T(8,128)(2,1)} %constant.20.clone.col_from) | copy-start | bytes 1572868
  12.6 4.8 %copy-start = (bf16[2,256,512]{2,1,0:T(8,128)(2,1)S(1)}, bf16[2,256,512]{2,1,0:T(8,128)(2,1)}, u32[]{:S(2)}) copy-start(bf16[2,256,512]{2,1,0:T(8,128)(2,1)} %constant.19.clone.row_from) | copy-start | bytes 1572868
  12.7 6.3 %collective-permute-start.3 = (f32[3,64,128]{2,1,0:T(8,128)S(1)}, f32[3,64,128]{2,1,0:T(8,128)S(1)}, u32[]{:S(2)}, u32[]{:S(2)}) collective-permute-start(f32[3,64,128]{2,1,0:T(8,128)S(1)} %get-tuple-element.49), channel_id=1, source_target_pairs={{1,2},{2,1},{5,6},{6,5},{9,10},{10,9},{13,14},{14,13},{17,18},{18,... | collective-permute-start | bytes 294920 | tf_op jit(solution)/shard_map/ppermute | solution.py:373
  13.5 7.7 %collective-permute-start.8 = (f32[3,64,128]{2,1,0:T(8,128)S(1)}, f32[3,64,128]{2,1,0:T(8,128)S(1)}, u32[]{:S(2)}, u32[]{:S(2)}) collective-permute-start(f32[3,64,128]{2,1,0:T(8,128)S(1)} %get-tuple-element.49), channel_id=1, source_target_pairs={{0,2},{1,3},{2,0},{3,1},{4,6},{5,7},{6,4},{7,5},{8,10},{9,11},{10,... | collective-permute-start | bytes 294920 | tf_op jit(solution)/shard_map/ppermute | solution.py:373
  16.5 4.6 %collective-permute-start.7 = (f32[3,64,128]{2,1,0:T(8,128)S(1)}, f32[3,64,128]{2,1,0:T(8,128)S(1)}, u32[]{:S(2)}, u32[]{:S(2)}) collective-permute-start(f32[3,64,128]{2,1,0:T(8,128)S(1)} %get-tuple-element.49), channel_id=1, source_target_pairs={{0,1},{1,0},{2,3},{3,2},{4,5},{5,4},{6,7},{7,6},{8,9},{9,8},{10,11... | collective-permute-start | bytes 294920 | tf_op jit(solution)/shard_map/ppermute | solution.py:373
  17.4 0.7 %copy-start.2 = (s32[2,2]{1,0:T(2,128)S(1)}, s32[2,2]{1,0:T(2,128)}, u32[]{:S(2)}) copy-start(s32[2,2]{1,0:T(2,128)} %tilt_ref.1) | copy-start | bytes 52
  19.1 3.8 %collective-permute-start.9 = (f32[11,64,128]{2,1,0:T(8,128)S(1)}, f32[11,64,128]{2,1,0:T(8,128)S(1)}, u32[]{:S(2)}, u32[]{:S(2)}) collective-permute-start(f32[11,64,128]{2,1,0:T(8,128)S(1)} %pad_maximum_fusion.2), channel_id=1, source_target_pairs={{0,4},{4,0},{1,5},{5,1},{2,6},{6,2},{3,7},{7,3},{8,12},{12,8},{9,1... | collective-permute-start | bytes 1081352 | tf_op jit(solution)/shard_map/ppermute | solution.py:378
  21.2 1.6 %collective-permute-start.10 = (f32[9,64,128]{2,1,0:T(8,128)S(1)}, f32[9,64,128]{2,1,0:T(8,128)S(1)}, u32[]{:S(2)}, u32[]{:S(2)}) collective-permute-start(f32[9,64,128]{2,1,0:T(8,128)S(1)} %constant_dynamic-update-slice_fusion.5), channel_id=1, source_target_pairs={{0,4},{4,0},{1,5},{5,1},{2,6},{6,2},{3,7},{7,3},{8,12},{12,8},{9,1... | collective-permute-start | bytes 884744 | tf_op jit(solution)/shard_map/ppermute | solution.py:378
  30.9 1.4 %collective-permute-start.11 = (f32[1,3,64,128]{3,2,1,0:T(8,128)S(1)}, f32[1,3,64,128]{3,2,1,0:T(8,128)S(1)}, u32[]{:S(2)}, u32[]{:S(2)}) collective-permute-start(f32[1,3,64,128]{3,2,1,0:T(8,128)S(1)} %get-tuple-element.45), channel_id=1, source_target_pairs={{0,4},{4,0},{1,5},{5,1},{2,6},{6,2},{3,7},{7,3},{8,12},{12,8},{9,1... | collective-permute-start | bytes 294920 | tf_op jit(solution)/shard_map/ppermute | solution.py:378

commit v28 on v26

--- a/solution.py
+++ b/solution.py
@@ -285,10 +285,11 @@
     for tick in range(count):
         entering = (wave_ref if tick == 0 else kept_ref)[own_place]
         moved_ref[tick, 0], moved_ref[tick, 1] = turned(tick, own_place, screens, (entering[0], entering[1]))
+        if tick + 1 < count:
+            far_screens(tick + 1)
         outer = (window_start, outer_high, outer_low) if tick + 1 == count else None
         waves = advance(tick, 0, waves, screens, row_matrix, col_ref, edges[tick % 2], outer)
         if tick + 1 < count:
-            far_screens(tick + 1)
             keep(kept_ref, waves)
         else:
             for place, wave in zip((1, 2, window_start * (blocks - 1)), waves):

time: 32.2 us -> 32.2 us (level)
  no operation moved by 1% of the time
where the time goes in v28:
time: 32.2 us; the launch traced here: 31.9 us
  starting transfers between devices  16.1 us (50%)
  Pallas kernels  8.97 us (28%)
  waiting for transfers between devices  4.38 us (14%)
  local copies, waits for them, and re-layouts  1.5 us (5%)
  between operations  0.84 us (3%)
    ppermute x6, starting transfers between devices, spread(): pieces.append(lax.ppermute(shard, axis, pairs))  10.3 us
    pallas_call x1, Pallas kernels, whole_field_body(): pl.pallas_call(wave_kernel, out_shape=(array(1, 3, tile_r, tile_c),) * 2,...  7.06 us
    ppermute x2, starting transfers between devices, whole_field_body(): near_own.append(lax.ppermute(packet, 'col', close))  3.94 us
    ppermute x3, waiting for transfers between devices, swap_cores(): return lax.ppermute(value, 'row', [(0, 1), (1, 0)])  2.36 us
    ppermute x6, waiting for transfers between devices, spread(): pieces.append(lax.ppermute(shard, axis, pairs))  2.01 us
    ppermute x1, starting transfers between devices, whole_field_body(): lax.ppermute(slab, 'col', further)  1.52 us
    unnamed x13, local copies, waits for them, and re-layouts  1.46 us
    pallas_call x1, Pallas kernels, whole_field_body(): pl.pallas_call(load_kernel, out_shape=(jax.ShapeDtypeStruct(row_all.shape...  0.89 us
  transfers between devices with their start and end apart: 12, of which 3 were waited for; matrix products, arithmetic and copies ran while one was open for 3% of the time, Pallas kernels for 4%

profile of v28, /device:TPU:0, one launch (start us, length us, event | category | flops | bytes accessed | tf_op | source)
XLA Modules:
  0.0 31.9 jit_solution(5130901362741518428)
XLA Ops:
  0.6 0.0 copy-start.3
  0.6 3.1 %collective-permute-start = (f32[1,64,128]{2,1,0:T(8,128)}, f32[1,64,128]{2,1,0:T(8,128)S(1)}, u32[]{:S(2)}, u32[]{:S(2)}) collective-permute-start(f32[1,64,128]{2,1,0:T(8,128)} %param.5), channel_id=1, source_target_pairs={{0,8},{8,0},{16,24},{24,16},{1,9},{9,1},{17,25},{25,17},{2,10},{10... | collective-permute-start | bytes 98312 | tf_op jit(solution)/shard_map/ppermute | solution.py:368
  3.7 2.5 %collective-permute-start.1 = (f32[1,64,128]{2,1,0:T(8,128)}, f32[1,64,128]{2,1,0:T(8,128)S(1)}, u32[]{:S(2)}, u32[]{:S(2)}) collective-permute-start(f32[1,64,128]{2,1,0:T(8,128)} %param.5), channel_id=1, source_target_pairs={{0,24},{8,16},{16,8},{24,0},{1,25},{9,17},{17,9},{25,1},{2,26},{10... | collective-permute-start | bytes 98312 | tf_op jit(solution)/shard_map/ppermute | solution.py:368
  6.2 0.1 collective-permute-start.2
  6.3 0.0 collective-permute-done
  6.3 0.8 %constant_dynamic-update-slice_fusion.4 = f32[3,64,128]{2,1,0:T(8,128)S(1)} fusion(f32[1,64,128]{2,1,0:T(8,128)} %param.5), kind=kLoop, calls=%fused_computation.9 | loop fusion | bytes 65536
  7.1 1.5 %collective-permute-start.5 = (f32[1,64,128]{2,1,0:T(8,128)}, f32[1,64,128]{2,1,0:T(8,128)S(1)}, u32[]{:S(2)}, u32[]{:S(2)}) collective-permute-start(f32[1,64,128]{2,1,0:T(8,128)} %param.5), channel_id=1, source_target_pairs={{0,2},{1,3},{2,0},{3,1},{4,6},{5,7},{6,4},{7,5},{8,10},{9,11},{10,... | collective-permute-start | bytes 98312 | tf_op jit(solution)/shard_map/ppermute | solution.py:404
  8.6 0.0 copy-done.3
  8.6 0.7 %collective-permute-start.6 = (f32[3,64,128]{2,1,0:T(8,128)S(1)}, f32[3,64,128]{2,1,0:T(8,128)S(1)}, u32[]{:S(2)}, u32[]{:S(2)}) collective-permute-start(f32[3,64,128]{2,1,0:T(8,128)S(1)} %constant_dynamic-update-slice_fusion.3), channel_id=1, source_target_pairs={{1,2},{2,1},{5,6},{6,5},{9,10},{10,9},{13,14},{14,13},{17,18},{18,... | collective-permute-start | bytes 294920 | tf_op jit(solution)/shard_map/ppermute | solution.py:401
  9.3 3.3 %collective-permute-start.4 = (f32[3,64,128]{2,1,0:T(8,128)S(1)}, f32[3,64,128]{2,1,0:T(8,128)S(1)}, u32[]{:S(2)}, u32[]{:S(2)}) collective-permute-start(f32[3,64,128]{2,1,0:T(8,128)S(1)} %constant_dynamic-update-slice_fusion.3), channel_id=1, source_target_pairs={{0,1},{1,0},{2,3},{3,2},{4,5},{5,4},{6,7},{7,6},{8,9},{9,8},{10,11... | collective-permute-start | bytes 294920 | tf_op jit(solution)/shard_map/ppermute | solution.py:401
  12.6 0.0 collective-permute-done.1
  12.6 0.0 copy-start.1
  12.6 0.0 copy-start
  12.7 0.0 collective-permute-done.2
  12.7 0.8 %collective-permute-start.3 = (f32[3,64,128]{2,1,0:T(8,128)S(1)}, f32[3,64,128]{2,1,0:T(8,128)S(1)}, u32[]{:S(2)}, u32[]{:S(2)}) collective-permute-start(f32[3,64,128]{2,1,0:T(8,128)S(1)} %get-tuple-element.49), channel_id=1, source_target_pairs={{1,2},{2,1},{5,6},{6,5},{9,10},{10,9},{13,14},{14,13},{17,18},{18,... | collective-permute-start | bytes 294920 | tf_op jit(solution)/shard_map/ppermute | solution.py:368
  13.5 3.0 %collective-permute-start.8 = (f32[3,64,128]{2,1,0:T(8,128)S(1)}, f32[3,64,128]{2,1,0:T(8,128)S(1)}, u32[]{:S(2)}, u32[]{:S(2)}) collective-permute-start(f32[3,64,128]{2,1,0:T(8,128)S(1)} %get-tuple-element.49), channel_id=1, source_target_pairs={{0,2},{1,3},{2,0},{3,1},{4,6},{5,7},{6,4},{7,5},{8,10},{9,11},{10,... | collective-permute-start | bytes 294920 | tf_op jit(solution)/shard_map/ppermute | solution.py:368
  16.5 0.0 collective-permute-done.5
  16.5 0.8 %collective-permute-start.7 = (f32[3,64,128]{2,1,0:T(8,128)S(1)}, f32[3,64,128]{2,1,0:T(8,128)S(1)}, u32[]{:S(2)}, u32[]{:S(2)}) collective-permute-start(f32[3,64,128]{2,1,0:T(8,128)S(1)} %get-tuple-element.49), channel_id=1, source_target_pairs={{0,1},{1,0},{2,3},{3,2},{4,5},{5,4},{6,7},{7,6},{8,9},{9,8},{10,11... | collective-permute-start | bytes 294920 | tf_op jit(solution)/shard_map/ppermute | solution.py:368
  17.4 0.0 collective-permute-done.6
  17.4 0.0 collective-permute-done.4
  17.4 0.0 copy-start.2
  17.4 0.0 copy-done.1
  17.4 0.0 copy-done
  17.4 0.6 %copy-done.2 = s32[2,2]{1,0:T(2,128)S(1)} copy-done((s32[2,2]{1,0:T(2,128)S(1)}, s32[2,2]{1,0:T(2,128)}, u32[]{:S(2)}) %copy-start.2) | copy-done | bytes 40
  18.1 0.9 %shard_map.68 = (bf16[256,512]{1,0:T(8,128)(2,1)S(1)}, bf16[512,512]{1,0:T(8,128)(2,1)S(1)}, f32[4,2,128,128]{3,2,1,0:T(8,128)S(1)}, f32[4,64,128]{2,1,0:T(8,128)S(1)}, f32[4,64,128]{2,1,0:T(8,128)S(1)}) custom-call(s32[2,2]{1,0:T(2,128)S(1)} %copy-done.2, f32[4,3,64,128]{3,2,1,0:T(8,128)S(1)} %pad_maximum_fusion.near_own, bf16[2,256,512]{2,1,0:T(8,128)(2,1)S(1)} %copy-done, ...), custom_call_target="tpu_custom_call" | custom-call | flops 100000000 | bytes 1048576 | tf_op jit(solution)/shard_map/pallas_call | solution.py:412
  19.0 0.0 collective-permute-done.3
  19.1 0.1 collective-permute-start.9
  19.1 2.0 %collective-permute-done.7 = f32[3,64,128]{2,1,0:T(8,128)S(1)} collective-permute-done((f32[3,64,128]{2,1,0:T(8,128)S(1)}, f32[3,64,128]{2,1,0:T(8,128)S(1)}, u32[]{:S(2)}, u32[]{:S(2)}) %collective-permute-start.7) | collective-permute-done | bytes 98336 | tf_op jit(solution)/shard_map/ppermute | solution.py:368
  21.1 0.0 collective-permute-done.8
  21.2 0.1 collective-permute-start.10
  21.3 0.3 %shard_map.69 = (f32[4,4,64,128]{3,2,1,0:T(8,128)S(1)}, f32[4,4,64,128]{3,2,1,0:T(8,128)S(1)}) custom-call(f32[4,3,64,128]{3,2,1,0:T(8,128)S(1)} %pad_maximum_fusion.1.near_rest, f32[4,64,128]{2,1,0:T(8,128)S(1)} %get-tuple-element.37.own_cos, f32[4,64,128]{2,1,0:T(8,128)S(1)} %get-tuple-element.38.own_sin), custom_call_target="tpu_custom_call" | custom-call | flops 500000000 | bytes 1048576 | tf_op jit(solution)/shard_map/pallas_call | solution.py:436
  21.6 1.2 %collective-permute-done.10.far_second = f32[9,64,128]{2,1,0:T(8,128)S(1)} collective-permute-done((f32[9,64,128]{2,1,0:T(8,128)S(1)}, f32[9,64,128]{2,1,0:T(8,128)S(1)}, u32[]{:S(2)}, u32[]{:S(2)}) %collective-permute-start.10) | collective-permute-done | bytes 294944 | tf_op jit(solution)/shard_map/ppermute | solution.py:373
  22.8 0.0 collective-permute-done.9.far_first
  22.8 7.1 %shard_map.70 = (f32[1,3,64,128]{3,2,1,0:T(8,128)S(1)}, f32[1,3,64,128]{3,2,1,0:T(8,128)S(1)}) custom-call(f32[4,2,128,128]{3,2,1,0:T(8,128)S(1)} %get-tuple-element.35.wave_ref, f32[4,4,64,128]{3,2,1,0:T(8,128)S(1)} %get-tuple-element.39.near_cos, f32[4,4,64,128]{3,2,1,0:T(8,128)S(1)} %get-tuple-element.40.near_sin, ...), custom_call_target="tpu_custom_call" | custom-call | tf_op jit(solution)/shard_map/pallas_call | solution.py:444
  29.9 0.2 collective-permute-start.11
  30.1 1.2 %collective-permute-done.11.received_ref = f32[1,3,64,128]{3,2,1,0:T(8,128)S(1)} collective-permute-done((f32[1,3,64,128]{3,2,1,0:T(8,128)S(1)}, f32[1,3,64,128]{3,2,1,0:T(8,128)S(1)}, u32[]{:S(2)}, u32[]{:S(2)}) %collective-permute-start.11) | collective-permute-done | bytes 98336 | tf_op jit(solution)/shard_map/ppermute | solution.py:373
  31.2 0.7 %shard_map.71 = (f32[1,64,128]{2,1,0:T(8,128)}, f32[2,1,2,64,128]{4,3,2,1,0:T(8,128)}) custom-call(f32[1,3,64,128]{3,2,1,0:T(8,128)S(1)} %get-tuple-element.44.mine_ref, f32[1,3,64,128]{3,2,1,0:T(8,128)S(1)} %collective-permute-done.11.received_ref), custom_call_target="tpu_custom_call" | custom-call | tf_op jit(solution)/shard_map/pallas_call | solution.py:460
  (12 shorter events, 0.2 us)
Async XLA Ops:
  0.6 8.0 %copy-start.3 = (f32[2,64,128]{2,1,0:T(8,128)S(1)}, f32[2,64,128]{2,1,0:T(8,128)}, u32[]{:S(2)}) copy-start(f32[2,64,128]{2,1,0:T(8,128)} %param.7) | copy-start | bytes 196612
  0.6 5.7 %collective-permute-start = (f32[1,64,128]{2,1,0:T(8,128)}, f32[1,64,128]{2,1,0:T(8,128)S(1)}, u32[]{:S(2)}, u32[]{:S(2)}) collective-permute-start(f32[1,64,128]{2,1,0:T(8,128)} %param.5), channel_id=1, source_target_pairs={{0,8},{8,0},{16,24},{24,16},{1,9},{9,1},{17,25},{25,17},{2,10},{10... | collective-permute-start | bytes 98312 | tf_op jit(solution)/shard_map/ppermute | solution.py:368
  3.7 8.9 %collective-permute-start.1 = (f32[1,64,128]{2,1,0:T(8,128)}, f32[1,64,128]{2,1,0:T(8,128)S(1)}, u32[]{:S(2)}, u32[]{:S(2)}) collective-permute-start(f32[1,64,128]{2,1,0:T(8,128)} %param.5), channel_id=1, source_target_pairs={{0,24},{8,16},{16,8},{24,0},{1,25},{9,17},{17,9},{25,1},{2,26},{10... | collective-permute-start | bytes 98312 | tf_op jit(solution)/shard_map/ppermute | solution.py:368
  6.2 6.4 %collective-permute-start.2 = (f32[1,64,128]{2,1,0:T(8,128)}, f32[1,64,128]{2,1,0:T(8,128)S(1)}, u32[]{:S(2)}, u32[]{:S(2)}) collective-permute-start(f32[1,64,128]{2,1,0:T(8,128)} %param.5), channel_id=1, source_target_pairs={{0,16},{8,24},{16,0},{24,8},{1,17},{9,25},{17,1},{25,9},{2,18},{10... | collective-permute-start | bytes 98312 | tf_op jit(solution)/shard_map/ppermute | solution.py:368
  7.1 9.4 %collective-permute-start.5 = (f32[1,64,128]{2,1,0:T(8,128)}, f32[1,64,128]{2,1,0:T(8,128)S(1)}, u32[]{:S(2)}, u32[]{:S(2)}) collective-permute-start(f32[1,64,128]{2,1,0:T(8,128)} %param.5), channel_id=1, source_target_pairs={{0,2},{1,3},{2,0},{3,1},{4,6},{5,7},{6,4},{7,5},{8,10},{9,11},{10,... | collective-permute-start | bytes 98312 | tf_op jit(solution)/shard_map/ppermute | solution.py:404
  8.6 8.7 %collective-permute-start.6 = (f32[3,64,128]{2,1,0:T(8,128)S(1)}, f32[3,64,128]{2,1,0:T(8,128)S(1)}, u32[]{:S(2)}, u32[]{:S(2)}) collective-permute-start(f32[3,64,128]{2,1,0:T(8,128)S(1)} %constant_dynamic-update-slice_fusion.3), channel_id=1, source_target_pairs={{1,2},{2,1},{5,6},{6,5},{9,10},{10,9},{13,14},{14,13},{17,18},{18,... | collective-permute-start | bytes 294920 | tf_op jit(solution)/shard_map/ppermute | solution.py:401
  9.3 8.0 %collective-permute-start.4 = (f32[3,64,128]{2,1,0:T(8,128)S(1)}, f32[3,64,128]{2,1,0:T(8,128)S(1)}, u32[]{:S(2)}, u32[]{:S(2)}) collective-permute-start(f32[3,64,128]{2,1,0:T(8,128)S(1)} %constant_dynamic-update-slice_fusion.3), channel_id=1, source_target_pairs={{0,1},{1,0},{2,3},{3,2},{4,5},{5,4},{6,7},{7,6},{8,9},{9,8},{10,11... | collective-permute-start | bytes 294920 | tf_op jit(solution)/shard_map/ppermute | solution.py:401
  12.6 4.8 %copy-start.1 = (bf16[512,512]{1,0:T(8,128)(2,1)S(1)}, bf16[512,512]{1,0:T(8,128)(2,1)}, u32[]{:S(2)}) copy-start(bf16[512,512]{1,0:T(8,128)(2,1)} %constant.20.clone.col_from) | copy-start | bytes 1572868
  12.6 4.8 %copy-start = (bf16[2,256,512]{2,1,0:T(8,128)(2,1)S(1)}, bf16[2,256,512]{2,1,0:T(8,128)(2,1)}, u32[]{:S(2)}) copy-start(bf16[2,256,512]{2,1,0:T(8,128)(2,1)} %constant.19.clone.row_from) | copy-start | bytes 1572868
  12.7 6.3 %collective-permute-start.3 = (f32[3,64,128]{2,1,0:T(8,128)S(1)}, f32[3,64,128]{2,1,0:T(8,128)S(1)}, u32[]{:S(2)}, u32[]{:S(2)}) collective-permute-start(f32[3,64,128]{2,1,0:T(8,128)S(1)} %get-tuple-element.49), channel_id=1, source_target_pairs={{1,2},{2,1},{5,6},{6,5},{9,10},{10,9},{13,14},{14,13},{17,18},{18,... | collective-permute-start | bytes 294920 | tf_op jit(solution)/shard_map/ppermute | solution.py:368
  13.5 7.7 %collective-permute-start.8 = (f32[3,64,128]{2,1,0:T(8,128)S(1)}, f32[3,64,128]{2,1,0:T(8,128)S(1)}, u32[]{:S(2)}, u32[]{:S(2)}) collective-permute-start(f32[3,64,128]{2,1,0:T(8,128)S(1)} %get-tuple-element.49), channel_id=1, source_target_pairs={{0,2},{1,3},{2,0},{3,1},{4,6},{5,7},{6,4},{7,5},{8,10},{9,11},{10,... | collective-permute-start | bytes 294920 | tf_op jit(solution)/shard_map/ppermute | solution.py:368
  16.5 4.6 %collective-permute-start.7 = (f32[3,64,128]{2,1,0:T(8,128)S(1)}, f32[3,64,128]{2,1,0:T(8,128)S(1)}, u32[]{:S(2)}, u32[]{:S(2)}) collective-permute-start(f32[3,64,128]{2,1,0:T(8,128)S(1)} %get-tuple-element.49), channel_id=1, source_target_pairs={{0,1},{1,0},{2,3},{3,2},{4,5},{5,4},{6,7},{7,6},{8,9},{9,8},{10,11... | collective-permute-start | bytes 294920 | tf_op jit(solution)/shard_map/ppermute | solution.py:368
  17.4 0.7 %copy-start.2 = (s32[2,2]{1,0:T(2,128)S(1)}, s32[2,2]{1,0:T(2,128)}, u32[]{:S(2)}) copy-start(s32[2,2]{1,0:T(2,128)} %tilt_ref.1) | copy-start | bytes 52
  19.1 3.8 %collective-permute-start.9 = (f32[11,64,128]{2,1,0:T(8,128)S(1)}, f32[11,64,128]{2,1,0:T(8,128)S(1)}, u32[]{:S(2)}, u32[]{:S(2)}) collective-permute-start(f32[11,64,128]{2,1,0:T(8,128)S(1)} %pad_maximum_fusion.2), channel_id=1, source_target_pairs={{0,4},{4,0},{1,5},{5,1},{2,6},{6,2},{3,7},{7,3},{8,12},{12,8},{9,1... | collective-permute-start | bytes 1081352 | tf_op jit(solution)/shard_map/ppermute | solution.py:373
  21.2 1.6 %collective-permute-start.10 = (f32[9,64,128]{2,1,0:T(8,128)S(1)}, f32[9,64,128]{2,1,0:T(8,128)S(1)}, u32[]{:S(2)}, u32[]{:S(2)}) collective-permute-start(f32[9,64,128]{2,1,0:T(8,128)S(1)} %constant_dynamic-update-slice_fusion.5), channel_id=1, source_target_pairs={{0,4},{4,0},{1,5},{5,1},{2,6},{6,2},{3,7},{7,3},{8,12},{12,8},{9,1... | collective-permute-start | bytes 884744 | tf_op jit(solution)/shard_map/ppermute | solution.py:373
  29.9 1.4 %collective-permute-start.11 = (f32[1,3,64,128]{3,2,1,0:T(8,128)S(1)}, f32[1,3,64,128]{3,2,1,0:T(8,128)S(1)}, u32[]{:S(2)}, u32[]{:S(2)}) collective-permute-start(f32[1,3,64,128]{3,2,1,0:T(8,128)S(1)} %get-tuple-element.45), channel_id=1, source_target_pairs={{0,4},{4,0},{1,5},{5,1},{2,6},{6,2},{3,7},{7,3},{8,12},{12,8},{9,1... | collective-permute-start | bytes 294920 | tf_op jit(solution)/shard_map/ppermute | solution.py:373

commit v29 on v26

--- a/solution.py
+++ b/solution.py
@@ -282,8 +282,8 @@
     far_screens(0)
 
     waves = [(wave_ref[place, 0], wave_ref[place, 1]) for place in range(blocks)]
+    entering = wave_ref[own_place]
     for tick in range(count):
-        entering = (wave_ref if tick == 0 else kept_ref)[own_place]
         moved_ref[tick, 0], moved_ref[tick, 1] = turned(tick, own_place, screens, (entering[0], entering[1]))
         outer = (window_start, outer_high, outer_low) if tick + 1 == count else None
         waves = advance(tick, 0, waves, screens, row_matrix, col_ref, edges[tick % 2], outer)
@@ -293,7 +293,8 @@
         else:
             for place, wave in zip((1, 2, window_start * (blocks - 1)), waves):
                 kept_ref[place, 0], kept_ref[place, 1] = wave
-        left_ref[tick] = kept_ref[own_place]
+        entering = kept_ref[own_place]
+        left_ref[tick] = entering
 
     for edge_ref in edges:
         clear_edge(edge_ref, window - 1, True)

time: 32.2 us -> 32.2 us (level)
  no operation moved by 1% of the time
where the time goes in v29:
time: 32.2 us; the launch traced here: 31.9 us
  starting transfers between devices  16.1 us (50%)
  Pallas kernels  8.97 us (28%)
  waiting for transfers between devices  4.38 us (14%)
  local copies, waits for them, and re-layouts  1.5 us (5%)
  between operations  0.84 us (3%)
    ppermute x6, starting transfers between devices, spread(): pieces.append(lax.ppermute(shard, axis, pairs))  10.3 us
    pallas_call x1, Pallas kernels, whole_field_body(): pl.pallas_call(wave_kernel, out_shape=(array(1, 3, tile_r, tile_c),) * 2,...  7.06 us
    ppermute x2, starting transfers between devices, whole_field_body(): near_own.append(lax.ppermute(packet, 'col', close))  3.94 us
    ppermute x3, waiting for transfers between devices, swap_cores(): return lax.ppermute(value, 'row', [(0, 1), (1, 0)])  2.36 us
    ppermute x6, waiting for transfers between devices, spread(): pieces.append(lax.ppermute(shard, axis, pairs))  2.01 us
    ppermute x1, starting transfers between devices, whole_field_body(): lax.ppermute(slab, 'col', further)  1.52 us
    unnamed x13, local copies, waits for them, and re-layouts  1.46 us
    pallas_call x1, Pallas kernels, whole_field_body(): pl.pallas_call(load_kernel, out_shape=(jax.ShapeDtypeStruct(row_all.shape...  0.89 us
  transfers between devices with their start and end apart: 12, of which 3 were waited for; matrix products, arithmetic and copies ran while one was open for 3% of the time, Pallas kernels for 4%

profile of v29, /device:TPU:0, one launch (start us, length us, event | category | flops | bytes accessed | tf_op | source)
XLA Modules:
  0.0 31.9 jit_solution(5130901362741518428)
XLA Ops:
  0.6 0.0 copy-start.3
  0.6 3.1 %collective-permute-start = (f32[1,64,128]{2,1,0:T(8,128)}, f32[1,64,128]{2,1,0:T(8,128)S(1)}, u32[]{:S(2)}, u32[]{:S(2)}) collective-permute-start(f32[1,64,128]{2,1,0:T(8,128)} %param.5), channel_id=1, source_target_pairs={{0,8},{8,0},{16,24},{24,16},{1,9},{9,1},{17,25},{25,17},{2,10},{10... | collective-permute-start | bytes 98312 | tf_op jit(solution)/shard_map/ppermute | solution.py:368
  3.7 2.5 %collective-permute-start.1 = (f32[1,64,128]{2,1,0:T(8,128)}, f32[1,64,128]{2,1,0:T(8,128)S(1)}, u32[]{:S(2)}, u32[]{:S(2)}) collective-permute-start(f32[1,64,128]{2,1,0:T(8,128)} %param.5), channel_id=1, source_target_pairs={{0,24},{8,16},{16,8},{24,0},{1,25},{9,17},{17,9},{25,1},{2,26},{10... | collective-permute-start | bytes 98312 | tf_op jit(solution)/shard_map/ppermute | solution.py:368
  6.2 0.1 collective-permute-start.2
  6.3 0.0 collective-permute-done
  6.3 0.8 %constant_dynamic-update-slice_fusion.4 = f32[3,64,128]{2,1,0:T(8,128)S(1)} fusion(f32[1,64,128]{2,1,0:T(8,128)} %param.5), kind=kLoop, calls=%fused_computation.9 | loop fusion | bytes 65536
  7.1 1.5 %collective-permute-start.5 = (f32[1,64,128]{2,1,0:T(8,128)}, f32[1,64,128]{2,1,0:T(8,128)S(1)}, u32[]{:S(2)}, u32[]{:S(2)}) collective-permute-start(f32[1,64,128]{2,1,0:T(8,128)} %param.5), channel_id=1, source_target_pairs={{0,2},{1,3},{2,0},{3,1},{4,6},{5,7},{6,4},{7,5},{8,10},{9,11},{10,... | collective-permute-start | bytes 98312 | tf_op jit(solution)/shard_map/ppermute | solution.py:404
  8.6 0.0 copy-done.3
  8.6 0.7 %collective-permute-start.6 = (f32[3,64,128]{2,1,0:T(8,128)S(1)}, f32[3,64,128]{2,1,0:T(8,128)S(1)}, u32[]{:S(2)}, u32[]{:S(2)}) collective-permute-start(f32[3,64,128]{2,1,0:T(8,128)S(1)} %constant_dynamic-update-slice_fusion.3), channel_id=1, source_target_pairs={{1,2},{2,1},{5,6},{6,5},{9,10},{10,9},{13,14},{14,13},{17,18},{18,... | collective-permute-start | bytes 294920 | tf_op jit(solution)/shard_map/ppermute | solution.py:401
  9.3 3.3 %collective-permute-start.4 = (f32[3,64,128]{2,1,0:T(8,128)S(1)}, f32[3,64,128]{2,1,0:T(8,128)S(1)}, u32[]{:S(2)}, u32[]{:S(2)}) collective-permute-start(f32[3,64,128]{2,1,0:T(8,128)S(1)} %constant_dynamic-update-slice_fusion.3), channel_id=1, source_target_pairs={{0,1},{1,0},{2,3},{3,2},{4,5},{5,4},{6,7},{7,6},{8,9},{9,8},{10,11... | collective-permute-start | bytes 294920 | tf_op jit(solution)/shard_map/ppermute | solution.py:401
  12.6 0.0 collective-permute-done.1
  12.6 0.0 copy-start.1
  12.6 0.0 copy-start
  12.7 0.0 collective-permute-done.2
  12.7 0.8 %collective-permute-start.3 = (f32[3,64,128]{2,1,0:T(8,128)S(1)}, f32[3,64,128]{2,1,0:T(8,128)S(1)}, u32[]{:S(2)}, u32[]{:S(2)}) collective-permute-start(f32[3,64,128]{2,1,0:T(8,128)S(1)} %get-tuple-element.49), channel_id=1, source_target_pairs={{1,2},{2,1},{5,6},{6,5},{9,10},{10,9},{13,14},{14,13},{17,18},{18,... | collective-permute-start | bytes 294920 | tf_op jit(solution)/shard_map/ppermute | solution.py:368
  13.5 3.0 %collective-permute-start.8 = (f32[3,64,128]{2,1,0:T(8,128)S(1)}, f32[3,64,128]{2,1,0:T(8,128)S(1)}, u32[]{:S(2)}, u32[]{:S(2)}) collective-permute-start(f32[3,64,128]{2,1,0:T(8,128)S(1)} %get-tuple-element.49), channel_id=1, source_target_pairs={{0,2},{1,3},{2,0},{3,1},{4,6},{5,7},{6,4},{7,5},{8,10},{9,11},{10,... | collective-permute-start | bytes 294920 | tf_op jit(solution)/shard_map/ppermute | solution.py:368
  16.5 0.0 collective-permute-done.5
  16.5 0.8 %collective-permute-start.7 = (f32[3,64,128]{2,1,0:T(8,128)S(1)}, f32[3,64,128]{2,1,0:T(8,128)S(1)}, u32[]{:S(2)}, u32[]{:S(2)}) collective-permute-start(f32[3,64,128]{2,1,0:T(8,128)S(1)} %get-tuple-element.49), channel_id=1, source_target_pairs={{0,1},{1,0},{2,3},{3,2},{4,5},{5,4},{6,7},{7,6},{8,9},{9,8},{10,11... | collective-permute-start | bytes 294920 | tf_op jit(solution)/shard_map/ppermute | solution.py:368
  17.4 0.0 collective-permute-done.6
  17.4 0.0 collective-permute-done.4
  17.4 0.0 copy-start.2
  17.4 0.0 copy-done.1
  17.4 0.0 copy-done
  17.4 0.6 %copy-done.2 = s32[2,2]{1,0:T(2,128)S(1)} copy-done((s32[2,2]{1,0:T(2,128)S(1)}, s32[2,2]{1,0:T(2,128)}, u32[]{:S(2)}) %copy-start.2) | copy-done | bytes 40
  18.1 0.9 %shard_map.68 = (bf16[256,512]{1,0:T(8,128)(2,1)S(1)}, bf16[512,512]{1,0:T(8,128)(2,1)S(1)}, f32[4,2,128,128]{3,2,1,0:T(8,128)S(1)}, f32[4,64,128]{2,1,0:T(8,128)S(1)}, f32[4,64,128]{2,1,0:T(8,128)S(1)}) custom-call(s32[2,2]{1,0:T(2,128)S(1)} %copy-done.2, f32[4,3,64,128]{3,2,1,0:T(8,128)S(1)} %pad_maximum_fusion.near_own, bf16[2,256,512]{2,1,0:T(8,128)(2,1)S(1)} %copy-done, ...), custom_call_target="tpu_custom_call" | custom-call | flops 100000000 | bytes 1048576 | tf_op jit(solution)/shard_map/pallas_call | solution.py:412
  19.0 0.0 collective-permute-done.3
  19.1 0.1 collective-permute-start.9
  19.1 2.0 %collective-permute-done.7 = f32[3,64,128]{2,1,0:T(8,128)S(1)} collective-permute-done((f32[3,64,128]{2,1,0:T(8,128)S(1)}, f32[3,64,128]{2,1,0:T(8,128)S(1)}, u32[]{:S(2)}, u32[]{:S(2)}) %collective-permute-start.7) | collective-permute-done | bytes 98336 | tf_op jit(solution)/shard_map/ppermute | solution.py:368
  21.1 0.0 collective-permute-done.8
  21.2 0.1 collective-permute-start.10
  21.3 0.3 %shard_map.69 = (f32[4,4,64,128]{3,2,1,0:T(8,128)S(1)}, f32[4,4,64,128]{3,2,1,0:T(8,128)S(1)}) custom-call(f32[4,3,64,128]{3,2,1,0:T(8,128)S(1)} %pad_maximum_fusion.1.near_rest, f32[4,64,128]{2,1,0:T(8,128)S(1)} %get-tuple-element.37.own_cos, f32[4,64,128]{2,1,0:T(8,128)S(1)} %get-tuple-element.38.own_sin), custom_call_target="tpu_custom_call" | custom-call | flops 500000000 | bytes 1048576 | tf_op jit(solution)/shard_map/pallas_call | solution.py:436
  21.6 1.2 %collective-permute-done.10.far_second = f32[9,64,128]{2,1,0:T(8,128)S(1)} collective-permute-done((f32[9,64,128]{2,1,0:T(8,128)S(1)}, f32[9,64,128]{2,1,0:T(8,128)S(1)}, u32[]{:S(2)}, u32[]{:S(2)}) %collective-permute-start.10) | collective-permute-done | bytes 294944 | tf_op jit(solution)/shard_map/ppermute | solution.py:373
  22.8 0.0 collective-permute-done.9.far_first
  22.8 7.1 %shard_map.70 = (f32[1,3,64,128]{3,2,1,0:T(8,128)S(1)}, f32[1,3,64,128]{3,2,1,0:T(8,128)S(1)}) custom-call(f32[4,2,128,128]{3,2,1,0:T(8,128)S(1)} %get-tuple-element.35.wave_ref, f32[4,4,64,128]{3,2,1,0:T(8,128)S(1)} %get-tuple-element.39.near_cos, f32[4,4,64,128]{3,2,1,0:T(8,128)S(1)} %get-tuple-element.40.near_sin, ...), custom_call_target="tpu_custom_call" | custom-call | tf_op jit(solution)/shard_map/pallas_call | solution.py:444
  29.9 0.2 collective-permute-start.11
  30.1 1.2 %collective-permute-done.11.received_ref = f32[1,3,64,128]{3,2,1,0:T(8,128)S(1)} collective-permute-done((f32[1,3,64,128]{3,2,1,0:T(8,128)S(1)}, f32[1,3,64,128]{3,2,1,0:T(8,128)S(1)}, u32[]{:S(2)}, u32[]{:S(2)}) %collective-permute-start.11) | collective-permute-done | bytes 98336 | tf_op jit(solution)/shard_map/ppermute | solution.py:373
  31.2 0.7 %shard_map.71 = (f32[1,64,128]{2,1,0:T(8,128)}, f32[2,1,2,64,128]{4,3,2,1,0:T(8,128)}) custom-call(f32[1,3,64,128]{3,2,1,0:T(8,128)S(1)} %get-tuple-element.44.mine_ref, f32[1,3,64,128]{3,2,1,0:T(8,128)S(1)} %collective-permute-done.11.received_ref), custom_call_target="tpu_custom_call" | custom-call | tf_op jit(solution)/shard_map/pallas_call | solution.py:460
  (12 shorter events, 0.2 us)
Async XLA Ops:
  0.6 8.0 %copy-start.3 = (f32[2,64,128]{2,1,0:T(8,128)S(1)}, f32[2,64,128]{2,1,0:T(8,128)}, u32[]{:S(2)}) copy-start(f32[2,64,128]{2,1,0:T(8,128)} %param.7) | copy-start | bytes 196612
  0.6 5.7 %collective-permute-start = (f32[1,64,128]{2,1,0:T(8,128)}, f32[1,64,128]{2,1,0:T(8,128)S(1)}, u32[]{:S(2)}, u32[]{:S(2)}) collective-permute-start(f32[1,64,128]{2,1,0:T(8,128)} %param.5), channel_id=1, source_target_pairs={{0,8},{8,0},{16,24},{24,16},{1,9},{9,1},{17,25},{25,17},{2,10},{10... | collective-permute-start | bytes 98312 | tf_op jit(solution)/shard_map/ppermute | solution.py:368
  3.7 8.9 %collective-permute-start.1 = (f32[1,64,128]{2,1,0:T(8,128)}, f32[1,64,128]{2,1,0:T(8,128)S(1)}, u32[]{:S(2)}, u32[]{:S(2)}) collective-permute-start(f32[1,64,128]{2,1,0:T(8,128)} %param.5), channel_id=1, source_target_pairs={{0,24},{8,16},{16,8},{24,0},{1,25},{9,17},{17,9},{25,1},{2,26},{10... | collective-permute-start | bytes 98312 | tf_op jit(solution)/shard_map/ppermute | solution.py:368
  6.2 6.4 %collective-permute-start.2 = (f32[1,64,128]{2,1,0:T(8,128)}, f32[1,64,128]{2,1,0:T(8,128)S(1)}, u32[]{:S(2)}, u32[]{:S(2)}) collective-permute-start(f32[1,64,128]{2,1,0:T(8,128)} %param.5), channel_id=1, source_target_pairs={{0,16},{8,24},{16,0},{24,8},{1,17},{9,25},{17,1},{25,9},{2,18},{10... | collective-permute-start | bytes 98312 | tf_op jit(solution)/shard_map/ppermute | solution.py:368
  7.1 9.4 %collective-permute-start.5 = (f32[1,64,128]{2,1,0:T(8,128)}, f32[1,64,128]{2,1,0:T(8,128)S(1)}, u32[]{:S(2)}, u32[]{:S(2)}) collective-permute-start(f32[1,64,128]{2,1,0:T(8,128)} %param.5), channel_id=1, source_target_pairs={{0,2},{1,3},{2,0},{3,1},{4,6},{5,7},{6,4},{7,5},{8,10},{9,11},{10,... | collective-permute-start | bytes 98312 | tf_op jit(solution)/shard_map/ppermute | solution.py:404
  8.6 8.7 %collective-permute-start.6 = (f32[3,64,128]{2,1,0:T(8,128)S(1)}, f32[3,64,128]{2,1,0:T(8,128)S(1)}, u32[]{:S(2)}, u32[]{:S(2)}) collective-permute-start(f32[3,64,128]{2,1,0:T(8,128)S(1)} %constant_dynamic-update-slice_fusion.3), channel_id=1, source_target_pairs={{1,2},{2,1},{5,6},{6,5},{9,10},{10,9},{13,14},{14,13},{17,18},{18,... | collective-permute-start | bytes 294920 | tf_op jit(solution)/shard_map/ppermute | solution.py:401
  9.3 8.0 %collective-permute-start.4 = (f32[3,64,128]{2,1,0:T(8,128)S(1)}, f32[3,64,128]{2,1,0:T(8,128)S(1)}, u32[]{:S(2)}, u32[]{:S(2)}) collective-permute-start(f32[3,64,128]{2,1,0:T(8,128)S(1)} %constant_dynamic-update-slice_fusion.3), channel_id=1, source_target_pairs={{0,1},{1,0},{2,3},{3,2},{4,5},{5,4},{6,7},{7,6},{8,9},{9,8},{10,11... | collective-permute-start | bytes 294920 | tf_op jit(solution)/shard_map/ppermute | solution.py:401
  12.6 4.8 %copy-start.1 = (bf16[512,512]{1,0:T(8,128)(2,1)S(1)}, bf16[512,512]{1,0:T(8,128)(2,1)}, u32[]{:S(2)}) copy-start(bf16[512,512]{1,0:T(8,128)(2,1)} %constant.20.clone.col_from) | copy-start | bytes 1572868
  12.6 4.8 %copy-start = (bf16[2,256,512]{2,1,0:T(8,128)(2,1)S(1)}, bf16[2,256,512]{2,1,0:T(8,128)(2,1)}, u32[]{:S(2)}) copy-start(bf16[2,256,512]{2,1,0:T(8,128)(2,1)} %constant.19.clone.row_from) | copy-start | bytes 1572868
  12.7 6.3 %collective-permute-start.3 = (f32[3,64,128]{2,1,0:T(8,128)S(1)}, f32[3,64,128]{2,1,0:T(8,128)S(1)}, u32[]{:S(2)}, u32[]{:S(2)}) collective-permute-start(f32[3,64,128]{2,1,0:T(8,128)S(1)} %get-tuple-element.49), channel_id=1, source_target_pairs={{1,2},{2,1},{5,6},{6,5},{9,10},{10,9},{13,14},{14,13},{17,18},{18,... | collective-permute-start | bytes 294920 | tf_op jit(solution)/shard_map/ppermute | solution.py:368
  13.5 7.7 %collective-permute-start.8 = (f32[3,64,128]{2,1,0:T(8,128)S(1)}, f32[3,64,128]{2,1,0:T(8,128)S(1)}, u32[]{:S(2)}, u32[]{:S(2)}) collective-permute-start(f32[3,64,128]{2,1,0:T(8,128)S(1)} %get-tuple-element.49), channel_id=1, source_target_pairs={{0,2},{1,3},{2,0},{3,1},{4,6},{5,7},{6,4},{7,5},{8,10},{9,11},{10,... | collective-permute-start | bytes 294920 | tf_op jit(solution)/shard_map/ppermute | solution.py:368
  16.5 4.6 %collective-permute-start.7 = (f32[3,64,128]{2,1,0:T(8,128)S(1)}, f32[3,64,128]{2,1,0:T(8,128)S(1)}, u32[]{:S(2)}, u32[]{:S(2)}) collective-permute-start(f32[3,64,128]{2,1,0:T(8,128)S(1)} %get-tuple-element.49), channel_id=1, source_target_pairs={{0,1},{1,0},{2,3},{3,2},{4,5},{5,4},{6,7},{7,6},{8,9},{9,8},{10,11... | collective-permute-start | bytes 294920 | tf_op jit(solution)/shard_map/ppermute | solution.py:368
  17.4 0.7 %copy-start.2 = (s32[2,2]{1,0:T(2,128)S(1)}, s32[2,2]{1,0:T(2,128)}, u32[]{:S(2)}) copy-start(s32[2,2]{1,0:T(2,128)} %tilt_ref.1) | copy-start | bytes 52
  19.1 3.8 %collective-permute-start.9 = (f32[11,64,128]{2,1,0:T(8,128)S(1)}, f32[11,64,128]{2,1,0:T(8,128)S(1)}, u32[]{:S(2)}, u32[]{:S(2)}) collective-permute-start(f32[11,64,128]{2,1,0:T(8,128)S(1)} %pad_maximum_fusion.2), channel_id=1, source_target_pairs={{0,4},{4,0},{1,5},{5,1},{2,6},{6,2},{3,7},{7,3},{8,12},{12,8},{9,1... | collective-permute-start | bytes 1081352 | tf_op jit(solution)/shard_map/ppermute | solution.py:373
  21.2 1.6 %collective-permute-start.10 = (f32[9,64,128]{2,1,0:T(8,128)S(1)}, f32[9,64,128]{2,1,0:T(8,128)S(1)}, u32[]{:S(2)}, u32[]{:S(2)}) collective-permute-start(f32[9,64,128]{2,1,0:T(8,128)S(1)} %constant_dynamic-update-slice_fusion.5), channel_id=1, source_target_pairs={{0,4},{4,0},{1,5},{5,1},{2,6},{6,2},{3,7},{7,3},{8,12},{12,8},{9,1... | collective-permute-start | bytes 884744 | tf_op jit(solution)/shard_map/ppermute | solution.py:373
  29.9 1.4 %collective-permute-start.11 = (f32[1,3,64,128]{3,2,1,0:T(8,128)S(1)}, f32[1,3,64,128]{3,2,1,0:T(8,128)S(1)}, u32[]{:S(2)}, u32[]{:S(2)}) collective-permute-start(f32[1,3,64,128]{3,2,1,0:T(8,128)S(1)} %get-tuple-element.45), channel_id=1, source_target_pairs={{0,4},{4,0},{1,5},{5,1},{2,6},{6,2},{3,7},{7,3},{8,12},{12,8},{9,1... | collective-permute-start | bytes 294920 | tf_op jit(solution)/shard_map/ppermute | solution.py:373

commit v30 on v29

--- a/solution.py
+++ b/solution.py
@@ -285,10 +285,11 @@
     entering = wave_ref[own_place]
     for tick in range(count):
         moved_ref[tick, 0], moved_ref[tick, 1] = turned(tick, own_place, screens, (entering[0], entering[1]))
+        if tick + 1 < count:
+            far_screens(tick + 1)
         outer = (window_start, outer_high, outer_low) if tick + 1 == count else None
         waves = advance(tick, 0, waves, screens, row_matrix, col_ref, edges[tick % 2], outer)
         if tick + 1 < count:
-            far_screens(tick + 1)
             keep(kept_ref, waves)
         else:
             for place, wave in zip((1, 2, window_start * (blocks - 1)), waves):

time: 32.2 us -> 32.2 us (level)
  no operation moved by 1% of the time
where the time goes in v30:
time: 32.2 us; the launch traced here: 31.9 us
  starting transfers between devices  16.1 us (50%)
  Pallas kernels  8.97 us (28%)
  waiting for transfers between devices  4.38 us (14%)
  local copies, waits for them, and re-layouts  1.5 us (5%)
  between operations  0.84 us (3%)
    ppermute x6, starting transfers between devices, spread(): pieces.append(lax.ppermute(shard, axis, pairs))  10.3 us
    pallas_call x1, Pallas kernels, whole_field_body(): pl.pallas_call(wave_kernel, out_shape=(array(1, 3, tile_r, tile_c),) * 2,...  7.06 us
    ppermute x2, starting transfers between devices, whole_field_body(): near_own.append(lax.ppermute(packet, 'col', close))  3.94 us
    ppermute x3, waiting for transfers between devices, swap_cores(): return lax.ppermute(value, 'row', [(0, 1), (1, 0)])  2.36 us
    ppermute x6, waiting for transfers between devices, spread(): pieces.append(lax.ppermute(shard, axis, pairs))  2.01 us
    ppermute x1, starting transfers between devices, whole_field_body(): lax.ppermute(slab, 'col', further)  1.52 us
    unnamed x13, local copies, waits for them, and re-layouts  1.46 us
    pallas_call x1, Pallas kernels, whole_field_body(): pl.pallas_call(load_kernel, out_shape=(jax.ShapeDtypeStruct(row_all.shape...  0.89 us
  transfers between devices with their start and end apart: 12, of which 3 were waited for; matrix products, arithmetic and copies ran while one was open for 3% of the time, Pallas kernels for 4%

profile of v30, /device:TPU:0, one launch (start us, length us, event | category | flops | bytes accessed | tf_op | source)
XLA Modules:
  0.0 31.9 jit_solution(5130901362741518428)
XLA Ops:
  0.6 0.0 copy-start.3
  0.6 3.1 %collective-permute-start = (f32[1,64,128]{2,1,0:T(8,128)}, f32[1,64,128]{2,1,0:T(8,128)S(1)}, u32[]{:S(2)}, u32[]{:S(2)}) collective-permute-start(f32[1,64,128]{2,1,0:T(8,128)} %param.5), channel_id=1, source_target_pairs={{0,8},{8,0},{16,24},{24,16},{1,9},{9,1},{17,25},{25,17},{2,10},{10... | collective-permute-start | bytes 98312 | tf_op jit(solution)/shard_map/ppermute | solution.py:369
  3.7 2.5 %collective-permute-start.1 = (f32[1,64,128]{2,1,0:T(8,128)}, f32[1,64,128]{2,1,0:T(8,128)S(1)}, u32[]{:S(2)}, u32[]{:S(2)}) collective-permute-start(f32[1,64,128]{2,1,0:T(8,128)} %param.5), channel_id=1, source_target_pairs={{0,24},{8,16},{16,8},{24,0},{1,25},{9,17},{17,9},{25,1},{2,26},{10... | collective-permute-start | bytes 98312 | tf_op jit(solution)/shard_map/ppermute | solution.py:369
  6.2 0.1 collective-permute-start.2
  6.3 0.0 collective-permute-done
  6.3 0.8 %constant_dynamic-update-slice_fusion.4 = f32[3,64,128]{2,1,0:T(8,128)S(1)} fusion(f32[1,64,128]{2,1,0:T(8,128)} %param.5), kind=kLoop, calls=%fused_computation.9 | loop fusion | bytes 65536
  7.1 1.5 %collective-permute-start.5 = (f32[1,64,128]{2,1,0:T(8,128)}, f32[1,64,128]{2,1,0:T(8,128)S(1)}, u32[]{:S(2)}, u32[]{:S(2)}) collective-permute-start(f32[1,64,128]{2,1,0:T(8,128)} %param.5), channel_id=1, source_target_pairs={{0,2},{1,3},{2,0},{3,1},{4,6},{5,7},{6,4},{7,5},{8,10},{9,11},{10,... | collective-permute-start | bytes 98312 | tf_op jit(solution)/shard_map/ppermute | solution.py:405
  8.6 0.0 copy-done.3
  8.6 0.7 %collective-permute-start.6 = (f32[3,64,128]{2,1,0:T(8,128)S(1)}, f32[3,64,128]{2,1,0:T(8,128)S(1)}, u32[]{:S(2)}, u32[]{:S(2)}) collective-permute-start(f32[3,64,128]{2,1,0:T(8,128)S(1)} %constant_dynamic-update-slice_fusion.3), channel_id=1, source_target_pairs={{1,2},{2,1},{5,6},{6,5},{9,10},{10,9},{13,14},{14,13},{17,18},{18,... | collective-permute-start | bytes 294920 | tf_op jit(solution)/shard_map/ppermute | solution.py:402
  9.3 3.3 %collective-permute-start.4 = (f32[3,64,128]{2,1,0:T(8,128)S(1)}, f32[3,64,128]{2,1,0:T(8,128)S(1)}, u32[]{:S(2)}, u32[]{:S(2)}) collective-permute-start(f32[3,64,128]{2,1,0:T(8,128)S(1)} %constant_dynamic-update-slice_fusion.3), channel_id=1, source_target_pairs={{0,1},{1,0},{2,3},{3,2},{4,5},{5,4},{6,7},{7,6},{8,9},{9,8},{10,11... | collective-permute-start | bytes 294920 | tf_op jit(solution)/shard_map/ppermute | solution.py:402
  12.6 0.0 collective-permute-done.1
  12.6 0.0 copy-start.1
  12.6 0.0 copy-start
  12.7 0.0 collective-permute-done.2
  12.7 0.8 %collective-permute-start.3 = (f32[3,64,128]{2,1,0:T(8,128)S(1)}, f32[3,64,128]{2,1,0:T(8,128)S(1)}, u32[]{:S(2)}, u32[]{:S(2)}) collective-permute-start(f32[3,64,128]{2,1,0:T(8,128)S(1)} %get-tuple-element.49), channel_id=1, source_target_pairs={{1,2},{2,1},{5,6},{6,5},{9,10},{10,9},{13,14},{14,13},{17,18},{18,... | collective-permute-start | bytes 294920 | tf_op jit(solution)/shard_map/ppermute | solution.py:369
  13.5 3.0 %collective-permute-start.8 = (f32[3,64,128]{2,1,0:T(8,128)S(1)}, f32[3,64,128]{2,1,0:T(8,128)S(1)}, u32[]{:S(2)}, u32[]{:S(2)}) collective-permute-start(f32[3,64,128]{2,1,0:T(8,128)S(1)} %get-tuple-element.49), channel_id=1, source_target_pairs={{0,2},{1,3},{2,0},{3,1},{4,6},{5,7},{6,4},{7,5},{8,10},{9,11},{10,... | collective-permute-start | bytes 294920 | tf_op jit(solution)/shard_map/ppermute | solution.py:369
  16.5 0.0 collective-permute-done.5
  16.5 0.8 %collective-permute-start.7 = (f32[3,64,128]{2,1,0:T(8,128)S(1)}, f32[3,64,128]{2,1,0:T(8,128)S(1)}, u32[]{:S(2)}, u32[]{:S(2)}) collective-permute-start(f32[3,64,128]{2,1,0:T(8,128)S(1)} %get-tuple-element.49), channel_id=1, source_target_pairs={{0,1},{1,0},{2,3},{3,2},{4,5},{5,4},{6,7},{7,6},{8,9},{9,8},{10,11... | collective-permute-start | bytes 294920 | tf_op jit(solution)/shard_map/ppermute | solution.py:369
  17.4 0.0 collective-permute-done.6
  17.4 0.0 collective-permute-done.4
  17.4 0.0 copy-start.2
  17.4 0.0 copy-done.1
  17.4 0.0 copy-done
  17.4 0.6 %copy-done.2 = s32[2,2]{1,0:T(2,128)S(1)} copy-done((s32[2,2]{1,0:T(2,128)S(1)}, s32[2,2]{1,0:T(2,128)}, u32[]{:S(2)}) %copy-start.2) | copy-done | bytes 40
  18.1 0.9 %shard_map.68 = (bf16[256,512]{1,0:T(8,128)(2,1)S(1)}, bf16[512,512]{1,0:T(8,128)(2,1)S(1)}, f32[4,2,128,128]{3,2,1,0:T(8,128)S(1)}, f32[4,64,128]{2,1,0:T(8,128)S(1)}, f32[4,64,128]{2,1,0:T(8,128)S(1)}) custom-call(s32[2,2]{1,0:T(2,128)S(1)} %copy-done.2, f32[4,3,64,128]{3,2,1,0:T(8,128)S(1)} %pad_maximum_fusion.near_own, bf16[2,256,512]{2,1,0:T(8,128)(2,1)S(1)} %copy-done, ...), custom_call_target="tpu_custom_call" | custom-call | flops 100000000 | bytes 1048576 | tf_op jit(solution)/shard_map/pallas_call | solution.py:413
  19.0 0.0 collective-permute-done.3
  19.1 0.1 collective-permute-start.9
  19.1 2.0 %collective-permute-done.7 = f32[3,64,128]{2,1,0:T(8,128)S(1)} collective-permute-done((f32[3,64,128]{2,1,0:T(8,128)S(1)}, f32[3,64,128]{2,1,0:T(8,128)S(1)}, u32[]{:S(2)}, u32[]{:S(2)}) %collective-permute-start.7) | collective-permute-done | bytes 98336 | tf_op jit(solution)/shard_map/ppermute | solution.py:369
  21.1 0.0 collective-permute-done.8
  21.2 0.1 collective-permute-start.10
  21.3 0.3 %shard_map.69 = (f32[4,4,64,128]{3,2,1,0:T(8,128)S(1)}, f32[4,4,64,128]{3,2,1,0:T(8,128)S(1)}) custom-call(f32[4,3,64,128]{3,2,1,0:T(8,128)S(1)} %pad_maximum_fusion.1.near_rest, f32[4,64,128]{2,1,0:T(8,128)S(1)} %get-tuple-element.37.own_cos, f32[4,64,128]{2,1,0:T(8,128)S(1)} %get-tuple-element.38.own_sin), custom_call_target="tpu_custom_call" | custom-call | flops 500000000 | bytes 1048576 | tf_op jit(solution)/shard_map/pallas_call | solution.py:437
  21.6 1.2 %collective-permute-done.10.far_second = f32[9,64,128]{2,1,0:T(8,128)S(1)} collective-permute-done((f32[9,64,128]{2,1,0:T(8,128)S(1)}, f32[9,64,128]{2,1,0:T(8,128)S(1)}, u32[]{:S(2)}, u32[]{:S(2)}) %collective-permute-start.10) | collective-permute-done | bytes 294944 | tf_op jit(solution)/shard_map/ppermute | solution.py:374
  22.8 0.0 collective-permute-done.9.far_first
  22.8 7.1 %shard_map.70 = (f32[1,3,64,128]{3,2,1,0:T(8,128)S(1)}, f32[1,3,64,128]{3,2,1,0:T(8,128)S(1)}) custom-call(f32[4,2,128,128]{3,2,1,0:T(8,128)S(1)} %get-tuple-element.35.wave_ref, f32[4,4,64,128]{3,2,1,0:T(8,128)S(1)} %get-tuple-element.39.near_cos, f32[4,4,64,128]{3,2,1,0:T(8,128)S(1)} %get-tuple-element.40.near_sin, ...), custom_call_target="tpu_custom_call" | custom-call | tf_op jit(solution)/shard_map/pallas_call | solution.py:445
  29.9 0.2 collective-permute-start.11
  30.1 1.2 %collective-permute-done.11.received_ref = f32[1,3,64,128]{3,2,1,0:T(8,128)S(1)} collective-permute-done((f32[1,3,64,128]{3,2,1,0:T(8,128)S(1)}, f32[1,3,64,128]{3,2,1,0:T(8,128)S(1)}, u32[]{:S(2)}, u32[]{:S(2)}) %collective-permute-start.11) | collective-permute-done | bytes 98336 | tf_op jit(solution)/shard_map/ppermute | solution.py:374
  31.2 0.7 %shard_map.71 = (f32[1,64,128]{2,1,0:T(8,128)}, f32[2,1,2,64,128]{4,3,2,1,0:T(8,128)}) custom-call(f32[1,3,64,128]{3,2,1,0:T(8,128)S(1)} %get-tuple-element.44.mine_ref, f32[1,3,64,128]{3,2,1,0:T(8,128)S(1)} %collective-permute-done.11.received_ref), custom_call_target="tpu_custom_call" | custom-call | tf_op jit(solution)/shard_map/pallas_call | solution.py:461
  (12 shorter events, 0.2 us)
Async XLA Ops:
  0.6 8.0 %copy-start.3 = (f32[2,64,128]{2,1,0:T(8,128)S(1)}, f32[2,64,128]{2,1,0:T(8,128)}, u32[]{:S(2)}) copy-start(f32[2,64,128]{2,1,0:T(8,128)} %param.7) | copy-start | bytes 196612
  0.6 5.7 %collective-permute-start = (f32[1,64,128]{2,1,0:T(8,128)}, f32[1,64,128]{2,1,0:T(8,128)S(1)}, u32[]{:S(2)}, u32[]{:S(2)}) collective-permute-start(f32[1,64,128]{2,1,0:T(8,128)} %param.5), channel_id=1, source_target_pairs={{0,8},{8,0},{16,24},{24,16},{1,9},{9,1},{17,25},{25,17},{2,10},{10... | collective-permute-start | bytes 98312 | tf_op jit(solution)/shard_map/ppermute | solution.py:369
  3.7 8.9 %collective-permute-start.1 = (f32[1,64,128]{2,1,0:T(8,128)}, f32[1,64,128]{2,1,0:T(8,128)S(1)}, u32[]{:S(2)}, u32[]{:S(2)}) collective-permute-start(f32[1,64,128]{2,1,0:T(8,128)} %param.5), channel_id=1, source_target_pairs={{0,24},{8,16},{16,8},{24,0},{1,25},{9,17},{17,9},{25,1},{2,26},{10... | collective-permute-start | bytes 98312 | tf_op jit(solution)/shard_map/ppermute | solution.py:369
  6.2 6.4 %collective-permute-start.2 = (f32[1,64,128]{2,1,0:T(8,128)}, f32[1,64,128]{2,1,0:T(8,128)S(1)}, u32[]{:S(2)}, u32[]{:S(2)}) collective-permute-start(f32[1,64,128]{2,1,0:T(8,128)} %param.5), channel_id=1, source_target_pairs={{0,16},{8,24},{16,0},{24,8},{1,17},{9,25},{17,1},{25,9},{2,18},{10... | collective-permute-start | bytes 98312 | tf_op jit(solution)/shard_map/ppermute | solution.py:369
  7.1 9.4 %collective-permute-start.5 = (f32[1,64,128]{2,1,0:T(8,128)}, f32[1,64,128]{2,1,0:T(8,128)S(1)}, u32[]{:S(2)}, u32[]{:S(2)}) collective-permute-start(f32[1,64,128]{2,1,0:T(8,128)} %param.5), channel_id=1, source_target_pairs={{0,2},{1,3},{2,0},{3,1},{4,6},{5,7},{6,4},{7,5},{8,10},{9,11},{10,... | collective-permute-start | bytes 98312 | tf_op jit(solution)/shard_map/ppermute | solution.py:405
  8.6 8.7 %collective-permute-start.6 = (f32[3,64,128]{2,1,0:T(8,128)S(1)}, f32[3,64,128]{2,1,0:T(8,128)S(1)}, u32[]{:S(2)}, u32[]{:S(2)}) collective-permute-start(f32[3,64,128]{2,1,0:T(8,128)S(1)} %constant_dynamic-update-slice_fusion.3), channel_id=1, source_target_pairs={{1,2},{2,1},{5,6},{6,5},{9,10},{10,9},{13,14},{14,13},{17,18},{18,... | collective-permute-start | bytes 294920 | tf_op jit(solution)/shard_map/ppermute | solution.py:402
  9.3 8.0 %collective-permute-start.4 = (f32[3,64,128]{2,1,0:T(8,128)S(1)}, f32[3,64,128]{2,1,0:T(8,128)S(1)}, u32[]{:S(2)}, u32[]{:S(2)}) collective-permute-start(f32[3,64,128]{2,1,0:T(8,128)S(1)} %constant_dynamic-update-slice_fusion.3), channel_id=1, source_target_pairs={{0,1},{1,0},{2,3},{3,2},{4,5},{5,4},{6,7},{7,6},{8,9},{9,8},{10,11... | collective-permute-start | bytes 294920 | tf_op jit(solution)/shard_map/ppermute | solution.py:402
  12.6 4.8 %copy-start.1 = (bf16[512,512]{1,0:T(8,128)(2,1)S(1)}, bf16[512,512]{1,0:T(8,128)(2,1)}, u32[]{:S(2)}) copy-start(bf16[512,512]{1,0:T(8,128)(2,1)} %constant.20.clone.col_from) | copy-start | bytes 1572868
  12.6 4.8 %copy-start = (bf16[2,256,512]{2,1,0:T(8,128)(2,1)S(1)}, bf16[2,256,512]{2,1,0:T(8,128)(2,1)}, u32[]{:S(2)}) copy-start(bf16[2,256,512]{2,1,0:T(8,128)(2,1)} %constant.19.clone.row_from) | copy-start | bytes 1572868
  12.7 6.3 %collective-permute-start.3 = (f32[3,64,128]{2,1,0:T(8,128)S(1)}, f32[3,64,128]{2,1,0:T(8,128)S(1)}, u32[]{:S(2)}, u32[]{:S(2)}) collective-permute-start(f32[3,64,128]{2,1,0:T(8,128)S(1)} %get-tuple-element.49), channel_id=1, source_target_pairs={{1,2},{2,1},{5,6},{6,5},{9,10},{10,9},{13,14},{14,13},{17,18},{18,... | collective-permute-start | bytes 294920 | tf_op jit(solution)/shard_map/ppermute | solution.py:369
  13.5 7.7 %collective-permute-start.8 = (f32[3,64,128]{2,1,0:T(8,128)S(1)}, f32[3,64,128]{2,1,0:T(8,128)S(1)}, u32[]{:S(2)}, u32[]{:S(2)}) collective-permute-start(f32[3,64,128]{2,1,0:T(8,128)S(1)} %get-tuple-element.49), channel_id=1, source_target_pairs={{0,2},{1,3},{2,0},{3,1},{4,6},{5,7},{6,4},{7,5},{8,10},{9,11},{10,... | collective-permute-start | bytes 294920 | tf_op jit(solution)/shard_map/ppermute | solution.py:369
  16.5 4.6 %collective-permute-start.7 = (f32[3,64,128]{2,1,0:T(8,128)S(1)}, f32[3,64,128]{2,1,0:T(8,128)S(1)}, u32[]{:S(2)}, u32[]{:S(2)}) collective-permute-start(f32[3,64,128]{2,1,0:T(8,128)S(1)} %get-tuple-element.49), channel_id=1, source_target_pairs={{0,1},{1,0},{2,3},{3,2},{4,5},{5,4},{6,7},{7,6},{8,9},{9,8},{10,11... | collective-permute-start | bytes 294920 | tf_op jit(solution)/shard_map/ppermute | solution.py:369
  17.4 0.7 %copy-start.2 = (s32[2,2]{1,0:T(2,128)S(1)}, s32[2,2]{1,0:T(2,128)}, u32[]{:S(2)}) copy-start(s32[2,2]{1,0:T(2,128)} %tilt_ref.1) | copy-start | bytes 52
  19.1 3.8 %collective-permute-start.9 = (f32[11,64,128]{2,1,0:T(8,128)S(1)}, f32[11,64,128]{2,1,0:T(8,128)S(1)}, u32[]{:S(2)}, u32[]{:S(2)}) collective-permute-start(f32[11,64,128]{2,1,0:T(8,128)S(1)} %pad_maximum_fusion.2), channel_id=1, source_target_pairs={{0,4},{4,0},{1,5},{5,1},{2,6},{6,2},{3,7},{7,3},{8,12},{12,8},{9,1... | collective-permute-start | bytes 1081352 | tf_op jit(solution)/shard_map/ppermute | solution.py:374
  21.2 1.6 %collective-permute-start.10 = (f32[9,64,128]{2,1,0:T(8,128)S(1)}, f32[9,64,128]{2,1,0:T(8,128)S(1)}, u32[]{:S(2)}, u32[]{:S(2)}) collective-permute-start(f32[9,64,128]{2,1,0:T(8,128)S(1)} %constant_dynamic-update-slice_fusion.5), channel_id=1, source_target_pairs={{0,4},{4,0},{1,5},{5,1},{2,6},{6,2},{3,7},{7,3},{8,12},{12,8},{9,1... | collective-permute-start | bytes 884744 | tf_op jit(solution)/shard_map/ppermute | solution.py:374
  29.9 1.4 %collective-permute-start.11 = (f32[1,3,64,128]{3,2,1,0:T(8,128)S(1)}, f32[1,3,64,128]{3,2,1,0:T(8,128)S(1)}, u32[]{:S(2)}, u32[]{:S(2)}) collective-permute-start(f32[1,3,64,128]{3,2,1,0:T(8,128)S(1)} %get-tuple-element.45), channel_id=1, source_target_pairs={{0,4},{4,0},{1,5},{5,1},{2,6},{6,2},{3,7},{7,3},{8,12},{12,8},{9,1... | collective-permute-start | bytes 294920 | tf_op jit(solution)/shard_map/ppermute | solution.py:374
